TPU v7x, 32 devices: a whole 2x2x4 slice. The times are simulated.
32 devices in a mesh: rows: 2 (over x), samples: 4 (over y, core), chan: 4 (over z).
Axes of the slice: x: 2, y: 2, z: 4, core: 2. Of those that a mesh axis runs over, the one named last changes fastest.
Arguments:
- feature: bfloat16 [4, 256, 16, 512], P('samples', 'chan', 'rows'), may hold values from -6 to 6
- out_grad: bfloat16 [4, 256, 16, 512], P('samples', 'chan', 'rows'), may hold values from -6 to 6
- bank: float32 [4, 9, 256, 256], P(None, None, 'chan', 'rows'), may hold values from -0.125 to 0.125
- select: int32 [4, 4], P('samples'), may hold values from 1 to 8
- latent: float32 [4, 512], P('samples'), may hold values from -6 to 6
- affine_w: float32 [512, 256], P(None, 'rows'), may hold values from -0.25 to 0.25
- affine_b: float32 [256], P('rows'), may hold values from 0.5 to 1.5
Outputs:
- feature_grad: bfloat16 [4, 256, 16, 512], P('samples', 'chan', 'rows')
- bank_grad: float32 [4, 9, 256, 256], P(None, None, 'chan', 'rows')
- affine_w_grad: float32 [512, 256], P(None, 'rows')
- affine_b_grad: float32 [256], P('rows')
All inputs are finite; a program needn't handle non-finite values.
Results may differ from a plain program's by a relative error of at most 0.0049.
Values may be sent and summed in bfloat16 or wider, within the bound.
No kernel may reach another device: no remote copies, remote signals or barrier semaphores. Data moves between devices by JAX's collectives and lax.ppermute only.
A program may use at most 128 MiB of HBM per device.

v0:
```python
import jax
import jax.numpy as jnp
from jax import lax
from jax.sharding import PartitionSpec as P

EPS = 1e-08


def extended(x, sides, width):
    for axis, dim in sides:
        size, length = (lax.axis_size(axis), x.shape[dim])
        up = [(i, (i + 1) % size) for i in range(size - 1)]
        down = [(j, i) for i, j in up]
        last = lax.slice_in_dim(x, length - width, length, axis=dim)
        leading = lax.slice_in_dim(x, 0, width, axis=dim)
        before = lax.ppermute(last, axis, up)
        after = lax.ppermute(leading, axis, down)
        x = jnp.concatenate([before, x, after], axis=dim)
    return x


def tap_slice(padded, first_row, first_col, height, width):
    return padded[:, first_row : first_row + height, first_col : first_col + width].reshape(
        padded.shape[0], height * width
    )


def on_device(feature, out_grad, bank, select, latent, affine_w, affine_b):
    feat_own = feature[0]
    cotan_own = out_grad[0]
    local_ch = feat_own.shape[0]
    height = feat_own.shape[1]
    width = feat_own.shape[2]
    stacked = jnp.concatenate([feat_own, cotan_own], axis=0)
    rimmed = extended(stacked, (("rows", 1),), 1)
    feat_rim = rimmed[:local_ch]
    cotan_rim = rimmed[local_ch:]
    weights = select[0].astype(jnp.float32)
    kernel = jnp.einsum("k,ktoc->toc", weights, bank, precision=lax.Precision.HIGHEST)
    style = jnp.dot(latent, affine_w, precision=lax.Precision.HIGHEST)[0] + affine_b
    plain = kernel * style[None, None, :]
    energy = lax.psum(jnp.sum(plain * plain, axis=(0, 2)), "rows")
    scale = lax.rsqrt(energy + EPS)
    modulated = (plain * scale[None, :, None]).astype(jnp.bfloat16)
    mod_rows = lax.all_gather(modulated, "rows", axis=2, tiled=True)
    cotan_flat = cotan_own.reshape(local_ch, height * width)
    cotan_pad = jnp.pad(cotan_rim, ((0, 0), (0, 0), (1, 1)))
    piece_pad = jnp.pad(
        lax.all_gather(feat_rim, "chan", axis=0, tiled=True), ((0, 0), (0, 0), (1, 1))
    )
    grads = []
    for tap_tap_index in range(9):
        feat_tap = tap_slice(piece_pad, tap_tap_index // 3, tap_tap_index % 3, height, width)
        grads.append(
            lax.dot_general(
                cotan_flat, feat_tap, (((1,), (1,)), ((), ())), preferred_element_type=jnp.float32
            )
        )
    grad_part = jnp.stack(grads, 0)
    mod_grad = lax.psum_scatter(grad_part, "rows", scatter_dimension=2, tiled=True)
    cotan_taps = [
        tap_slice(cotan_pad, 2 - tap_index // 3, 2 - tap_index % 3, height, width)
        for tap_index in range(9)
    ]
    total = jnp.zeros((local_ch * lax.axis_size("chan"), height * width), jnp.float32)
    for tap_index in range(9):
        total = total + lax.dot_general(
            mod_rows[tap_index],
            cotan_taps[tap_index],
            (((0,), (0,)), ((), ())),
            preferred_element_type=jnp.float32,
        )
    input_total = lax.psum_scatter(total, "chan", scatter_dimension=0, tiled=True)
    feature_grad = input_total.reshape(1, local_ch, height, width).astype(jnp.bfloat16)
    slope = lax.psum(jnp.sum(mod_grad * plain, axis=(0, 2)), "rows")
    plain_grad = mod_grad * scale[None, :, None] - plain * (slope * scale**3)[None, :, None]
    kernel_grad = plain_grad * style[None, None, :]
    style_part = jnp.sum(plain_grad * kernel, axis=(0, 1))
    bank_part = weights[:, None, None, None] * kernel_grad[None]
    style_whole = lax.psum(style_part, "chan")
    affine_part = latent[0][:, None] * style_whole[None, :]
    bank_grad, affine_w_grad, affine_b_grad = lax.psum(
        (bank_part, affine_part, style_whole), "samples"
    )
    return (feature_grad, bank_grad, affine_w_grad, affine_b_grad)


def solution(mesh):
    return jax.shard_map(
        on_device,
        mesh=mesh,
        in_specs=(
            P("samples", "chan", "rows", None),
            P("samples", "chan", "rows", None),
            P(None, None, "chan", "rows"),
            P("samples", None),
            P("samples", None),
            P(None, "rows"),
            P("rows"),
        ),
        out_specs=(
            P("samples", "chan", "rows", None),
            P(None, None, "chan", "rows"),
            P(None, "rows"),
            P("rows"),
        ),
        check_vma=False,
    )
```

profile of v0, /device:TPU:0, one launch (start us, length us, event | category | flops | bytes accessed | tf_op | source)
XLA Modules:
  0.0 272.6 jit_solution(6505637847936007229)
XLA Ops:
  7.2 0.0 all-gather.2.cloned.1.call-start
  7.2 1.6 copy_bitcast_fusion
  8.9 4.8 %collective-permute-start = (bf16[128,1,512]{2,0,1:T(8,128)(2,1)S(1)}, bf16[128,1,512]{2,0,1:T(8,128)(2,1)S(1)}, u32[]{:S(2)}, u32[]{:S(2)}) collective-permute-start(bf16[128,1,512]{2,0,1:T(8,128)(2,1)S(1)} %get-tuple-element.23), channel_id=1, source_target_pairs={{0,16},{1,17},{2,18},{3,19},{4,20},{5,21},{6,22},{7,23},{8,24},{9,... | collective-permute-start | bytes 393224 | tf_op jit(solution)/shard_map/ppermute | solution.py:16
  13.7 1.3 collective-permute-start.1
  15.0 1.4 collective-permute-done
  16.5 4.1 %collective-permute-done.1 = bf16[128,1,512]{2,0,1:T(8,128)(2,1)S(1)} collective-permute-done((bf16[128,1,512]{2,0,1:T(8,128)(2,1)S(1)}, bf16[128,1,512]{2,0,1:T(8,128)(2,1)S(1)}, u32[]{:S(2)}, u32[]{:S(2)}) %collective-permute-start.1) | collective-permute-done | bytes 131104 | tf_op jit(solution)/shard_map/ppermute | solution.py:17
  20.6 0.1 pad_maximum_fusion
  20.7 1.2 fusion.26
  21.8 0.0 all-gather.2.cloned.1.call-update
  21.9 0.0 reduce-scatter.5.cloned.1.call-start
  21.9 0.2 copy.38
  22.1 55.0 %all-gather.2.cloned.1.call-done = bf16[256,10,512]{2,0,1:T(8,128)(2,1)} async-done(((bf16[64,10,512]{2,0,1:T(8,128)(2,1)}), bf16[256,10,512]{2,0,1:T(8,128)(2,1)}) %all-gather.2.cloned.1.call-update) | async-done | bytes 2621456 | tf_op jit(solution)/shard_map/all_gather | solution.py:49
  77.1 4.4 %copy.23 = bf16[256,10,512]{0,2,1:T(8,128)(2,1)} copy(bf16[256,10,512]{2,0,1:T(8,128)(2,1)} %all-gather.2.cloned.1.call-done) | data formatting | bytes 5242880 | tf_op jit(solution)/shard_map/all_gather | solution.py:49
  81.5 15.8 %pad_slice_fusion = (bf16[256,8,512]{0,2,1:T(8,128)(2,1)S(1)}, bf16[256,8,512]{0,2,1:T(8,128)(2,1)}, bf16[256,8,512]{0,2,1:T(8,128)(2,1)S(1)}, bf16[256,8,512]{0...) fusion(bf16[256,10,512]{0,2,1:T(8,128)(2,1)} %copy.23), kind=kLoop, calls=%fused_computation.9 | loop fusion | bytes 27787264 | tf_op jit(solution)/shard_map/slice | solution.py:23
  97.3 2.2 fusion.10
  99.5 0.5 fusion.9
  100.0 0.2 copy-done.2
  100.2 0.5 fusion.8
  100.6 0.5 fusion.7
  101.1 0.5 fusion.6
  101.6 0.5 fusion.5
  102.1 0.5 fusion.4
  102.5 0.5 fusion.3
  103.0 0.5 fusion.2
  103.5 0.8 copy-done.9
  104.4 0.2 reduce-scatter.3.cloned.1.call-start
  104.6 1.2 fusion.11
  105.8 2.6 fusion
  108.5 3.8 %fusion.17 = (bf16[8,8,8,512]{3,2,1,0:T(8,128)(2,1)S(1)}, bf16[8,8,8,512]{3,2,1,0:T(8,128)(2,1)S(1)}, bf16[8,8,8,512]{3,2,1,0:T(8,128)(2,1)S(1)}, bf16[8,8,8,512...) fusion(bf16[64,10,512]{2,0,1:T(8,128)(2,1)} %get-tuple-element.20), kind=kLoop, calls=%fused_computation.49 | loop fusion | bytes 3801088
  112.3 0.1 fusion.18
  112.4 0.8 copy.31
  113.3 0.8 copy.32
  114.1 0.8 copy.33
  114.9 0.9 copy.34
  116.0 2.7 reduce-scatter.5.cloned.1.call-done
  118.6 1.1 multiply_reduce_fusion.1
  119.7 4.9 %all-reduce.3 = (f32[64]{0:T(128)S(1)}, f32[64]{0:T(128)S(1)}) all-reduce(f32[64]{0:T(128)S(1)} %get-tuple-element.5, f32[64]{0:T(128)S(1)} %get-tuple-element.4), channel_id=1, replica_groups=mesh['rows'=2,'samples'=4,'chan'=4] {'rows'}, use_global_device_ids=true, to_apply=%region_1.0 | all-reduce | flops 128 | bytes 1024 | tf_op jit(solution)/shard_map/psum | solution.py:42
  124.7 1.2 multiply_reduce_fusion
  125.8 5.8 %all_gather.6 = bf16[9,64,256]{2,1,0:T(8,128)(2,1)S(1)} all-gather(bf16[9,64,128]{2,1,0:T(8,128)(2,1)S(1)} %get-tuple-element.33), channel_id=1, replica_groups=mesh['rows'=2,'samples'=4,'chan'=4] {'rows'}, dimensions={2}, use_global_device_ids=true | all-gather | bytes 442368 | tf_op jit(solution)/shard_map/all_gather | solution.py:45
  131.7 0.7 fusion.21
  132.4 0.3 copy-done.7
  132.7 0.7 convolution_add_fusion.7
  133.5 0.3 copy-done.6
  133.8 0.7 convolution_add_fusion.6
  134.5 0.3 copy-done.5
  134.8 0.7 convolution_add_fusion.5
  135.6 0.7 convolution_add_fusion.4
  136.3 0.3 copy-done.4
  136.6 0.7 convolution_add_fusion.3
  137.3 0.7 convolution_add_fusion.2
  138.1 0.7 convolution_add_fusion.1
  138.8 2.7 convolution_add_fusion
  141.5 0.0 reduce-scatter.3.cloned.1.call-update
  141.5 0.0 all-reduce.6.cloned.1.call-start
  141.6 11.8 %psum.45 = f32[128]{0:T(128)S(1)} all-reduce(f32[128]{0:T(128)S(1)} %get-tuple-element.31), channel_id=1, replica_groups=mesh['rows'=2,'samples'=4,'chan'=4] {'chan'}, use_global_device_ids=true, to_apply=%region_8.9 | all-reduce | flops 128 | bytes 1024 | tf_op jit(solution)/shard_map/psum | solution.py:80
  153.4 0.8 broadcast_multiply_fusion.1
  154.2 1.2 broadcast_multiply_fusion
  155.4 6.6 %psum.47 = f32[128]{0:T(128)} all-reduce(f32[128]{0:T(128)S(1)} %psum.45), channel_id=1, replica_groups=mesh['rows'=2,'samples'=4,'chan'=4] {'samples'}, use_global_device_ids=true, to_apply=%region_10.11 | all-reduce | flops 128 | bytes 1024 | tf_op jit(solution)/shard_map/psum | solution.py:82
  162.0 56.5 %reduce-scatter.3.cloned.1.call-done = f32[64,4096]{1,0:T(8,128)} async-done(((f32[256,4096]{1,0:T(8,128)}), f32[64,4096]{1,0:T(8,128)}) %reduce-scatter.3.cloned.1.call-update) | async-done | bytes 1048592 | tf_op jit(solution)/shard_map/reduce_scatter | solution.py:73
  218.5 1.4 convert_element_type.34
  219.9 1.0 copy.39
  220.8 42.1 %all-reduce.6.cloned.1.call-done = (f32[4,9,64,128]{3,2,1,0:T(8,128)}, f32[512,128]{1,0:T(8,128)}) async-done(((f32[4,9,64,128]{3,2,1,0:T(8,128)}, f32[512,128]{1,0:T(8,128)}), (f32[4,9,64,128]{3,2,1,0:T(8,128)}, f32[512,128]{1,0:T(8,128)})) %all-reduce.6.cloned.1.call-update) | async-done | bytes 1441808 | tf_op jit(solution)/shard_map/psum | solution.py:82
  262.9 2.5 copy.54
  265.4 0.7 copy.55
  (35 shorter events, 0.3 us)
Async XLA Ops:
  7.2 98.6 %copy-start = (f32[4,9,64,128]{3,2,1,0:T(8,128)S(1)}, f32[4,9,64,128]{3,2,1,0:T(8,128)}, u32[]{:S(2)}) copy-start(f32[4,9,64,128]{3,2,1,0:T(8,128)} %param.9) | copy-start | bytes 3538948
  7.2 69.9 %all-gather.2.cloned.1.call-start = ((), (), s32[]{:S(2)}) async-start(), calls=%async_computation.3 | async-start | bytes 3276800 | tf_op jit(solution)/shard_map/all_gather | solution.py:49
  8.9 7.6 %collective-permute-start = (bf16[128,1,512]{2,0,1:T(8,128)(2,1)S(1)}, bf16[128,1,512]{2,0,1:T(8,128)(2,1)S(1)}, u32[]{:S(2)}, u32[]{:S(2)}) collective-permute-start(bf16[128,1,512]{2,0,1:T(8,128)(2,1)S(1)} %get-tuple-element.23), channel_id=1, source_target_pairs={{0,16},{1,17},{2,18},{3,19},{4,20},{5,21},{6,22},{7,23},{8,24},{9,... | collective-permute-start | bytes 393224 | tf_op jit(solution)/shard_map/ppermute | solution.py:16
  13.7 6.9 %collective-permute-start.1 = (bf16[128,1,512]{2,0,1:T(8,128)(2,1)S(1)}, bf16[128,1,512]{2,0,1:T(8,128)(2,1)S(1)}, u32[]{:S(2)}, u32[]{:S(2)}) collective-permute-start(bf16[128,1,512]{2,0,1:T(8,128)(2,1)S(1)} %get-tuple-element.24), channel_id=1, source_target_pairs={{16,0},{17,1},{18,2},{19,3},{20,4},{21,5},{22,6},{23,7},{24,8},{25... | collective-permute-start | bytes 393224 | tf_op jit(solution)/shard_map/ppermute | solution.py:17
  20.6 1.3 copy-start.10
  20.7 1.2 copy-start.8
  21.9 96.7 %reduce-scatter.5.cloned.1.call-start = ((), (), s32[]{:S(2)}) async-start(), calls=%async_computation.4 | async-start | bytes 884736 | tf_op jit(solution)/shard_map/reduce_scatter | solution.py:60
  97.3 2.2 copy-start.3
  97.3 2.8 %copy-start.2 = (bf16[256,8,512]{0,2,1:T(8,128)(2,1)S(1)}, bf16[256,8,512]{0,2,1:T(8,128)(2,1)}, u32[]{:S(2)}) copy-start(bf16[256,8,512]{0,2,1:T(8,128)(2,1)} %get-tuple-element.11) | copy-start | bytes 6291460
  103.0 1.6 copy-start.13
  103.0 1.6 copy-start.14
  103.0 2.8 %copy-start.15 = (s32[1,4]{1,0:T(1,128)S(1)}, s32[1,4]{1,0:T(1,128)}, u32[]{:S(2)}) copy-start(s32[1,4]{1,0:T(1,128)} %param.10) | copy-start | bytes 52
  103.5 0.8 copy-start.9
  104.4 114.1 %reduce-scatter.3.cloned.1.call-start = ((), (), s32[]{:S(2)}) async-start(), calls=%async_computation.2 | async-start | bytes 5242880 | tf_op jit(solution)/shard_map/reduce_scatter | solution.py:73
  108.5 3.9 %copy-start.11 = (bf16[128,1,512]{2,0,1:T(8,128)(2,1)S(1)}, bf16[128,1,512]{2,0,1:T(8,128)(2,1)}, u32[]{:S(2)}) copy-start(bf16[128,1,512]{2,0,1:T(8,128)(2,1)} %copy-done.10) | copy-start | bytes 393220
  131.7 1.0 copy-start.7
  132.7 1.0 copy-start.6
  133.8 1.0 copy-start.5
  135.6 1.0 copy-start.4
  141.5 121.4 %all-reduce.6.cloned.1.call-start = ((), (), s32[]{:S(2)}) async-start(), calls=%async_computation.5 | async-start | bytes 2883584 | tf_op jit(solution)/shard_map/psum | solution.py:82
  218.5 47.6 %copy-start.1 = (f32[4,9,64,128]{3,2,1,0:T(8,128)S(1)}, f32[4,9,64,128]{3,2,1,0:T(8,128)}, u32[]{:S(2)}) copy-start(f32[4,9,64,128]{3,2,1,0:T(8,128)} %param.9) | copy-start | bytes 3538948
  262.9 2.5 copy-start.12
Sparse Core Ops, SparseCore 0:
  22.0 55.0 all-gather.1
  104.5 14.0 reduce-scatter.4
  141.6 76.8 reduce-scatter.2
  221.4 41.4 all-reduce.5
where the time goes:
time: 273 us
  waiting for transfers between devices  162 us (59%)
  local copies, waits for them, and re-layouts  36.9 us (14%)
  blocking collectives  29.1 us (11%)
  matrix products  18.3 us (7%)
  between operations  14.1 us (5%)
  starting transfers between devices  6.49 us (2%)
  other arithmetic  5.9 us (2%)
    reduce_scatter x1, waiting for transfers between devices, on_device(): lax.psum_scatter(total, 'chan', scatter_dimension=0, tiled=True)  56.5 us
    all_gather x1, waiting for transfers between devices, on_device(): lax.all_gather(feat_rim, 'chan', axis=0, tiled=True)  55 us
    psum x1, waiting for transfers between devices, on_device(): lax.psum((bank_part, affine_part, style_whole), 'samples')  42.1 us
    slice x1, local copies, waits for them, and re-layouts, tap_slice(): padded[:, first_row:first_row + height, first_col:first_col + width]  15.8 us
    psum x1, blocking collectives, on_device(): style_whole = lax.psum(style_part, 'chan')  11.8 us
    unnamed x37, local copies, waits for them, and re-layouts  10.4 us
    dot_general x9, matrix products, on_device(): lax.dot_general(mod_rows[tap_index], cotan_taps[tap_index], (((0,), (0,))...  8.5 us
    psum x1, blocking collectives, on_device(): lax.psum((bank_part, affine_part, style_whole), 'samples')  6.57 us
  transfers between devices with their start and end apart: 6, of which 6 were waited for; matrix products, arithmetic and copies ran while one was open for 6% of the time, Pallas kernels for 0%

commit v1 on v0

v1 whole, which is shorter than its diff:
```python
import functools

import jax
import jax.numpy as jnp
from jax import lax
from jax.experimental import pallas as pl
from jax.experimental.pallas import tpu as pltpu
from jax.sharding import PartitionSpec as P

EPS = 1e-08
TAPS = 9
F32 = jnp.float32
BF16 = jnp.bfloat16
VMEM_LIMIT = 48 * 2**20


def params():
    return pltpu.CompilerParams(vmem_limit_bytes=VMEM_LIMIT)


def vspec(n):
    return [pl.BlockSpec(memory_space=pltpu.VMEM)] * n


def sspec(n):
    return [pl.BlockSpec(memory_space=pltpu.SMEM)] * n


def cost(flops, moved):
    return pl.CostEstimate(flops=flops, bytes_accessed=moved, transcendentals=0)


def column(table, index):
    lane = lax.broadcasted_iota(jnp.int32, table.shape, 1)
    return jnp.sum(jnp.where(lane == index, table, 0.0), axis=1, keepdims=True)


def beside(pieces):
    return pieces[0] if len(pieces) == 1 else jnp.concatenate(pieces, axis=1)


def mixed(bank_ref, sel, sample, tap):
    total = sel[sample, 0] * bank_ref[0, tap]
    for k in range(1, bank_ref.shape[0]):
        total = total + sel[sample, k] * bank_ref[k, tap]
    return total


class Routes:
    def __init__(self, rows, size):
        self.rows, self.size = rows, size
        self.blocks, self.fold = max(1, size // rows), max(1, rows // size)
        self.steps = max(rows, size)

    def user_code(self, row, chan):
        return lax.rem(chan, self.blocks) + self.blocks * row

    def owner_code(self, row, chan):
        return chan + self.size * lax.rem(row, self.fold)

    def pairs(self, step):
        out = []
        for row in range(self.rows):
            for chan in range(self.size):
                code = (chan % self.blocks + self.blocks * row + step) % self.steps
                owner_row = chan // self.blocks * self.fold + code // self.size
                out.append((owner_row * self.size + code % self.size, row * self.size + chan))
        return out


def energy_kernel(sel, bank, latent, affine_w, affine_b, style_out, energy_out):
    samples = latent.shape[0]
    style = (
        jnp.dot(latent[...], affine_w[...], precision=lax.Precision.HIGHEST, preferred_element_type=F32)
        + affine_b[...]
    )
    style_out[...] = style
    out_ch, in_ch = bank.shape[2], bank.shape[3]
    totals = [jnp.zeros((out_ch, in_ch), F32) for _ in range(samples)]
    for tap in range(TAPS):
        for b in range(samples):
            plain = mixed(bank, sel, b, tap) * style[b : b + 1]
            totals[b] = totals[b] + plain * plain
    lane = lax.broadcasted_iota(jnp.int32, (out_ch, 128), 1)
    table = jnp.zeros((out_ch, 128), F32)
    for b in range(samples):
        table = jnp.where(lane == b, jnp.sum(totals[b], axis=1, keepdims=True), table)
    energy_out[...] = table


def modulated_kernel(routes, width, place, sel, bank, style, energy, *outs):
    sample, blocks = place[0], routes.blocks
    scale = lax.rsqrt(column(energy[...], sample) + EPS)
    own_style = style[pl.ds(sample, 1), :]
    mods = [mixed(bank, sel, sample, tap) * own_style * scale for tap in range(TAPS)]
    messages = [
        beside([m[:, j * width : (j + 1) * width] for m in mods]).astype(BF16)
        for j in range(blocks)
    ]
    code = routes.owner_code(place[2], place[1])
    for m in range(routes.steps):
        pick = lax.rem(lax.rem(code - m + routes.steps, routes.steps), blocks)
        value = messages[0]
        for j in range(1, blocks):
            value = jnp.where(pick == j, messages[j], value)
        outs[m][...] = value


def shifted(x, by):
    width = x.shape[1]
    lane = lax.broadcasted_iota(jnp.int32, x.shape, 1)
    moved = pltpu.roll(x, by % width, 1)
    return jnp.where(lane == (0 if by == 1 else width - 1), 0.0, moved)


def kernel_grad_kernel(routes, height, width, *refs):
    size, fold = routes.size, routes.fold
    cotan_own, left, right = refs[0], refs[1:size], refs[size : 2 * size - 1]
    feat, feat_before, feat_after = refs[2 * size - 1 : 2 * size + 2]
    outs = refs[2 * size + 2 : 2 * size + 2 + routes.steps]
    wide, gathered, total = refs[2 * size + 2 + routes.steps :]
    ch = feat.shape[0]
    gathered[0:ch] = cotan_own[...]
    for d in range(1, size):
        gathered[d * ch : (d + 1) * ch] = left[d - 1][...] + right[size - d - 1][...]
    for row in range(height + 2):
        if row == 0:
            x = feat_before[...]
        elif row == height + 1:
            x = feat_after[...]
        else:
            x = feat[:, (row - 1) * width : row * width]
        wide[ch : 2 * ch, row * width : (row + 1) * width] = x
        x = x.astype(F32)
        wide[0:ch, row * width : (row + 1) * width] = shifted(x, 1).astype(BF16)
        wide[2 * ch : 3 * ch, row * width : (row + 1) * width] = shifted(x, -1).astype(BF16)
    total[...] = jnp.zeros(total.shape, F32)

    def body(row, _):
        g = gathered[:, pl.ds(pl.multiple_of(row * width, width), width)]
        for kh in range(3):
            x = wide[:, pl.ds(pl.multiple_of((row + kh) * width, width), width)]
            total[kh] += lax.dot_general(g, x, (((1,), (1,)), ((), ())), preferred_element_type=F32)
        return 0

    lax.fori_loop(0, height, body, 0)
    whole = jnp.concatenate([total[kh] for kh in range(3)], axis=1)
    part = ch // fold
    for k in range(fold):
        value = whole
        if fold > 1:
            starts = [tap * ch + k * part for tap in range(TAPS)]
            value = jnp.concatenate([whole[:, at : at + part] for at in starts], axis=1)
        for d in range(size):
            outs[k * size + d][...] = value[d * ch : (d + 1) * ch].astype(BF16)


def input_grad_kernel(routes, height, width, place, *refs):
    size, fold, steps = routes.size, routes.fold, routes.steps
    cotan_own, left, right = refs[0], refs[1:size], refs[size : 2 * size - 1]
    mods = refs[2 * size - 1 : 2 * size - 1 + steps]
    main, before, after, gathered, taps, taps_t, total = refs[2 * size - 1 + steps :]
    ch = cotan_own.shape[0]
    chan = place[1]
    gathered[0:ch] = cotan_own[...]
    for d in range(1, size):
        gathered[d * ch : (d + 1) * ch] = left[d - 1][...] + right[size - d - 1][...]
    code = routes.user_code(place[2], chan)
    for m in range(steps):
        owner = lax.rem(code + m, steps)
        slot = lax.rem(chan - lax.rem(owner, size) + size, size)
        taps[lax.div(owner, size) * size + slot] = mods[m][...].astype(F32)
    part = ch // fold
    every = taps[0:size].reshape(size * ch, TAPS * part)
    if fold > 1:
        pieces = [taps[k * size : (k + 1) * size].reshape(size * ch, TAPS * part) for k in range(fold)]
        every = jnp.concatenate(
            [p[:, tap * part : (tap + 1) * part] for tap in range(TAPS) for p in pieces], axis=1
        )
    taps_t[...] = every.T.astype(BF16)
    total[...] = jnp.zeros(total.shape, F32)

    def body(row, _):
        g = gathered[:, pl.ds(pl.multiple_of(row * width, width), width)]
        for kh in range(3):
            y = jnp.dot(taps_t[kh * 3 * ch : (kh + 1) * 3 * ch], g, preferred_element_type=F32)
            total[row + kh] += y
        return 0

    lax.fori_loop(0, height, body, 0)
    for row in range(height + 2):
        value = total[row, ch : 2 * ch]
        value = value + shifted(total[row, 0:ch], -1) + shifted(total[row, 2 * ch : 3 * ch], 1)
        if row == 0:
            before[...] = value
        elif row == height + 1:
            after[...] = value
        else:
            main[:, (row - 1) * width : row * width] = value


def collect_kernel(routes, place, sel, bank, style, *refs):
    rows, blocks, steps = routes.rows, routes.blocks, routes.steps
    parts = refs[:steps]
    out, slope_out, held = refs[steps:]
    sample = place[0]
    code = routes.owner_code(place[2], place[1])
    for m in range(steps):
        held[lax.rem(code - m + steps, steps)] = parts[m][...].astype(F32)
    sums = []
    for j in range(blocks):
        value = held[j]
        for r in range(1, rows):
            value = value + held[r * blocks + j]
        sums.append(value)
    width = sums[0].shape[1] // TAPS
    own_style = style[pl.ds(sample, 1), :]
    product = jnp.zeros(bank.shape[2:], F32)
    for tap in range(TAPS):
        whole = beside([s[:, tap * width : (tap + 1) * width] for s in sums]).astype(BF16)
        out[tap] = whole
        product = product + whole.astype(F32) * (mixed(bank, sel, sample, tap) * own_style)
    slope = jnp.sum(product, axis=1, keepdims=True)
    lane = lax.broadcasted_iota(jnp.int32, slope_out.shape, 1)
    slope_out[...] = jnp.where(lane == sample, slope, 0.0)


def bank_grad_kernel(samples, place, sel, bank, style, energy, slope, *refs):
    parts = refs[:samples]
    bank_grad, style_grad, held = refs[samples:]
    sample = place[0]
    for s in range(samples):
        held[lax.rem(sample - s + samples, samples)] = parts[s][...]
    styles = style[...]
    energies, slopes = energy[...], slope[...]
    scales, falls = [], []
    for b in range(samples):
        scale = lax.rsqrt(energies[:, b : b + 1] + EPS)
        scales.append(scale)
        falls.append(slopes[:, b : b + 1] * (scale * scale * scale))
    sums = [jnp.zeros(bank.shape[2:], F32) for _ in range(samples)]
    for tap in range(TAPS):
        totals = [None] * bank.shape[0]
        for b in range(samples):
            kern = mixed(bank, sel, b, tap)
            own_style = styles[b : b + 1]
            plain_grad = held[b, tap].astype(F32) * scales[b] - kern * own_style * falls[b]
            sums[b] = sums[b] + plain_grad * kern
            kernel_grad = plain_grad * own_style
            for k in range(bank.shape[0]):
                term = sel[b, k] * kernel_grad
                totals[k] = term if totals[k] is None else totals[k] + term
        for k in range(bank.shape[0]):
            bank_grad[k, tap] = totals[k]
    for b in range(samples):
        style_grad[b : b + 1] = jnp.sum(sums[b], axis=0, keepdims=True)


def on_device(feature, out_grad, bank, select, latent, affine_w, affine_b):
    rows, samples, size = (lax.axis_size(a) for a in ("rows", "samples", "chan"))
    row_at, sample_at, chan_at = (lax.axis_index(a) for a in ("rows", "samples", "chan"))
    _, ch, height, width = feature.shape
    pixels = height * width
    in_ch = bank.shape[3]
    routes = Routes(rows, size)
    place = jnp.stack([sample_at, chan_at, row_at]).astype(jnp.int32)

    cotan = out_grad[0].reshape(ch, pixels)
    left, right = [], []
    from_left = from_right = cotan
    for step in range(1, size):
        from_left = lax.ppermute(from_left, "chan", [(i, i + 1) for i in range(step - 1, size - 1)])
        from_right = lax.ppermute(from_right, "chan", [(i + 1, i) for i in range(size - step)])
        left.append(from_left)
        right.append(from_right)

    feat = feature[0].reshape(ch, pixels)
    up = [(i, i + 1) for i in range(rows - 1)]
    down = [(i + 1, i) for i in range(rows - 1)]
    feat_before = lax.ppermute(feat[:, pixels - width :], "rows", up)
    feat_after = lax.ppermute(feat[:, :width], "rows", down)

    small = jnp.concatenate([latent[0], select[0].astype(F32)])
    small = lax.all_gather(small, "samples", axis=0)
    latents, sel = small[:, : latent.shape[1]], small[:, latent.shape[1] :]
    out_ch = bank.shape[2]
    style, energy = pl.pallas_call(
        energy_kernel,
        out_shape=(
            jax.ShapeDtypeStruct((samples, in_ch), F32),
            jax.ShapeDtypeStruct((out_ch, 128), F32),
        ),
        in_specs=sspec(1) + vspec(4),
        out_specs=tuple(vspec(2)),
        compiler_params=params(),
        cost_estimate=cost(10**7, bank.size * 4),
        name="energy",
    )(sel, bank, latents, affine_w, affine_b[None])
    energy = lax.psum(energy, "rows")
    message = jax.ShapeDtypeStruct((ch, TAPS * min(ch, in_ch)), BF16)
    to_send = pl.pallas_call(
        functools.partial(modulated_kernel, routes, min(ch, in_ch)),
        out_shape=(message,) * routes.steps,
        in_specs=sspec(2) + vspec(3),
        out_specs=tuple(vspec(routes.steps)),
        compiler_params=params(),
        cost_estimate=cost(10**7, bank.size * 4),
        name="modulated",
    )(place, sel, bank, style, energy)
    mods = [lax.ppermute(to_send[m], ("rows", "chan"), routes.pairs(m)) for m in range(routes.steps)]

    parts = pl.pallas_call(
        functools.partial(kernel_grad_kernel, routes, height, width),
        out_shape=(message,) * routes.steps,
        in_specs=vspec(2 * size + 2),
        out_specs=tuple(vspec(routes.steps)),
        scratch_shapes=[
            pltpu.VMEM((3 * ch, (height + 2) * width), BF16),
            pltpu.VMEM((size * ch, pixels), BF16),
            pltpu.VMEM((3, size * ch, 3 * ch), F32),
        ],
        compiler_params=params(),
        cost_estimate=cost(2 * TAPS * ch * ch * size * pixels, (2 * size + 1) * ch * pixels * 2),
        name="kernel_grad",
    )(cotan, *left, *right, feat, feat_before, feat_after)

    code = routes.user_code(row_at, chan_at)
    received = []
    for m in range(routes.steps):
        owner = lax.rem(code + m, routes.steps)
        slot = lax.rem(chan_at - lax.rem(owner, size) + size, size) + lax.div(owner, size) * size
        value = parts[0]
        for d in range(1, routes.steps):
            value = jnp.where(slot == d, parts[d], value)
        pairs = [(user, owner_at) for owner_at, user in routes.pairs(m)]
        received.append(lax.ppermute(value, ("rows", "chan"), pairs))

    main, before, after = pl.pallas_call(
        functools.partial(input_grad_kernel, routes, height, width),
        out_shape=(
            jax.ShapeDtypeStruct((ch, pixels), F32),
            jax.ShapeDtypeStruct((ch, width), F32),
            jax.ShapeDtypeStruct((ch, width), F32),
        ),
        in_specs=sspec(1) + vspec(2 * size - 1 + routes.steps),
        out_specs=tuple(vspec(3)),
        scratch_shapes=[
            pltpu.VMEM((size * ch, pixels), BF16),
            pltpu.VMEM((routes.steps, *message.shape), F32),
            pltpu.VMEM((TAPS * ch, size * ch), BF16),
            pltpu.VMEM((height + 2, 3 * ch, width), F32),
        ],
        compiler_params=params(),
        cost_estimate=cost(2 * TAPS * ch * ch * size * pixels, (2 * size + 1) * ch * pixels * 2),
        name="input_grad",
    )(place, cotan, *left, *right, *mods)
    from_below = lax.ppermute(before, "rows", down)
    from_above = lax.ppermute(after, "rows", up)
    edge = jnp.concatenate(
        [from_above[:, None], jnp.zeros((ch, height - 2, width), F32), from_below[:, None]], axis=1
    )
    feature_grad = (main.reshape(ch, height, width) + edge).astype(BF16)[None]

    mod_grad, slope = pl.pallas_call(
        functools.partial(collect_kernel, routes),
        out_shape=(
            jax.ShapeDtypeStruct((TAPS, out_ch, in_ch), BF16),
            jax.ShapeDtypeStruct((out_ch, 128), F32),
        ),
        in_specs=sspec(2) + vspec(2 + routes.steps),
        out_specs=tuple(vspec(2)),
        scratch_shapes=[pltpu.VMEM((routes.steps, *message.shape), F32)],
        compiler_params=params(),
        cost_estimate=cost(10**7, bank.size * 4),
        name="collect",
    )(place, sel, bank, style, *received)
    others = [
        lax.ppermute(mod_grad, "samples", [(i, (i + s) % samples) for i in range(samples)])
        for s in range(1, samples)
    ]
    slope = lax.psum(slope, ("rows", "samples"))
    bank_grad, style_part = pl.pallas_call(
        functools.partial(bank_grad_kernel, samples),
        out_shape=(
            jax.ShapeDtypeStruct(bank.shape, F32),
            jax.ShapeDtypeStruct((samples, in_ch), F32),
        ),
        in_specs=sspec(2) + vspec(4 + samples),
        out_specs=tuple(vspec(2)),
        scratch_shapes=[pltpu.VMEM((samples, TAPS, out_ch, in_ch), BF16)],
        compiler_params=params(),
        cost_estimate=cost(4 * 10**7, bank.size * 8),
        name="bank_grad",
    )(place, sel, bank, style, energy, slope, mod_grad, *others)
    style_grad = lax.psum(style_part, "chan")
    affine_w_grad = jnp.sum(latents[:, :, None] * style_grad[:, None, :], axis=0)
    affine_b_grad = jnp.sum(style_grad, axis=0)
    return (feature_grad, bank_grad, affine_w_grad, affine_b_grad)


def solution(mesh):
    return jax.shard_map(
        on_device,
        mesh=mesh,
        in_specs=(
            P("samples", "chan", "rows", None),
            P("samples", "chan", "rows", None),
            P(None, None, "chan", "rows"),
            P("samples", None),
            P("samples", None),
            P(None, "rows"),
            P("rows"),
        ),
        out_specs=(
            P("samples", "chan", "rows", None),
            P(None, None, "chan", "rows"),
            P(None, "rows"),
            P("rows"),
        ),
        check_vma=False,
    )
```

time: 273 us -> 151 us (0.55)
  waiting for transfers between devices: 162 us -> 25.7 us
  starting transfers between devices: 6.49 us -> 40.6 us
  local copies, waits for them, and re-layouts: 36.9 us -> 5.21 us
  blocking collectives: 29.1 us -> 57.5 us
  matrix products: 18.3 us -> 0 us
  Pallas kernels: 0 us -> 16.7 us
  between operations: 14.1 us -> 1.72 us
  other arithmetic: 5.9 us -> 2.97 us
    reduce_scatter x2 -> x0, waiting for transfers between devices: 59.1 us -> none  [the longest x1 56.5 us: on_device(): lax.psum_scatter(total, 'chan', scatter_dimension=0, tiled=True)]
    all_gather x1 -> x0, waiting for transfers between devices: 55 us -> none  [on_device(): lax.all_gather(feat_rim, 'chan', axis=0, tiled=True)]
    psum x1 -> x0, waiting for transfers between devices: 42.1 us -> none  [on_device(): lax.psum((bank_part, affine_part, style_whole), 'samples')]
    ppermute x2 -> x21, starting transfers between devices: 6.14 us -> 40.6 us  [the longest x4 9.33 us: on_device(): lax.ppermute(to_send[m], ('rows', 'chan'), routes.pairs(m))]
    psum x3, blocking collectives: 23.3 us -> 46.9 us  [the longest x1 30.7 us: on_device(): slope = lax.psum(slope, ('rows', 'samples'))]
    ppermute x2 -> x21, waiting for transfers between devices: 5.56 us -> 25.7 us  [the longest x3 22.1 us: on_device(): lax.ppermute(from_right, 'chan', [(i + 1, i) for i in range(size - step)])]
    dot_general x20 -> x0, matrix products: 18.3 us -> none  [the longest x9 8.5 us: on_device(): lax.dot_general(mod_rows[tap_index], cotan_taps[tap_index], (((0,), (0,))...]
    slice x2 -> x3, local copies, waits for them, and re-layouts: 16.9 us -> 0.01 us  [the longest x1 0.01 us: on_device(): feat_after = lax.ppermute(feat[:, :width], 'rows', down)]
  transfers between devices with their start and end apart: 6 -> 21, of which waited for: 6 -> 4; matrix products, arithmetic and copies ran while one was open for 6% -> 3% of each run, Pallas kernels for 0% -> 9%
where the time goes in v1:
time: 151 us; the launch traced here: 150 us
  blocking collectives  57.5 us (38%)
  starting transfers between devices  40.6 us (27%)
  waiting for transfers between devices  25.7 us (17%)
  Pallas kernels  16.7 us (11%)
  local copies, waits for them, and re-layouts  5.21 us (3%)
  other arithmetic  2.97 us (2%)
  between operations  1.72 us (1%)
    psum x1, blocking collectives, on_device(): slope = lax.psum(slope, ('rows', 'samples'))  30.7 us
    ppermute x3, waiting for transfers between devices, on_device(): lax.ppermute(from_right, 'chan', [(i + 1, i) for i in range(size - step)])  22.1 us
    unnamed x1, blocking collectives  10.5 us
    ppermute x4, starting transfers between devices, on_device(): lax.ppermute(to_send[m], ('rows', 'chan'), routes.pairs(m))  9.33 us
    psum x1, blocking collectives, on_device(): style_grad = lax.psum(style_part, 'chan')  9.32 us
    ppermute x3, starting transfers between devices, on_device(): lax.ppermute(from_left, 'chan', [(i, i + 1) for i in range(step - 1, size...  8.52 us
    ppermute x4, starting transfers between devices, on_device(): received.append(lax.ppermute(value, ('rows', 'chan'), pairs))  7.38 us
    psum x1, blocking collectives, on_device(): energy = lax.psum(energy, 'rows')  6.9 us
  transfers between devices with their start and end apart: 21, of which 4 were waited for; matrix products, arithmetic and copies ran while one was open for 3% of the time, Pallas kernels for 9%

profile of v1, /device:TPU:0, one launch (start us, length us, event | category | flops | bytes accessed | tf_op | source)
XLA Modules:
  0.0 150.4 jit_solution(13462156549929899722)
XLA Ops:
  0.6 0.0 copy-start.9
  0.7 1.3 copy.15
  2.1 1.3 collective-permute-start.3
  3.4 5.6 %collective-permute-start = (bf16[64,4096]{1,0:T(8,128)(2,1)S(1)}, bf16[64,4096]{1,0:T(8,128)(2,1)S(1)}, u32[]{:S(2)}, u32[]{:S(2)}) collective-permute-start(bf16[64,4096]{1,0:T(8,128)(2,1)S(1)} %bitcast.27), channel_id=1, source_target_pairs={{0,1},{1,2},{2,3},{4,5},{5,6},{6,7},{8,9},{9,10},{10,11},{12,13},{... | collective-permute-start | bytes 1572872 | tf_op jit(solution)/shard_map/ppermute | solution.py:272
  8.9 10.0 %collective-permute-done.3.refs_4_ = bf16[64,4096]{1,0:T(8,128)(2,1)S(1)} collective-permute-done((bf16[64,4096]{1,0:T(8,128)(2,1)S(1)}, bf16[64,4096]{1,0:T(8,128)(2,1)S(1)}, u32[]{:S(2)}, u32[]{:S(2)}) %collective-permute-start.3) | collective-permute-done | bytes 524320 | tf_op jit(solution)/shard_map/ppermute | solution.py:273
  18.9 1.3 collective-permute-start.4
  20.2 0.0 collective-permute-done.refs_1_
  20.2 0.0 copy-start.3
  20.2 1.5 collective-permute-start.1
  21.7 0.2 copy.17
  21.9 12.1 %collective-permute-done.4.refs_5_ = bf16[64,4096]{1,0:T(8,128)(2,1)} collective-permute-done((bf16[64,4096]{1,0:T(8,128)(2,1)S(1)}, bf16[64,4096]{1,0:T(8,128)(2,1)}, u32[]{:S(2)}, u32[]{:S(2)}) %collective-permute-start.4) | collective-permute-done | bytes 524320 | tf_op jit(solution)/shard_map/ppermute | solution.py:273
  34.0 1.3 collective-permute-start.5
  35.3 0.0 collective-permute-done.1.refs_2_
  35.3 1.5 collective-permute-start.2
  36.8 1.3 collective-permute-start.13
  38.1 4.5 %collective-permute-start.12 = (bf16[64,512]{1,0:T(8,128)(2,1)S(1)}, bf16[64,512]{1,0:T(8,128)(2,1)S(1)}, u32[]{:S(2)}, u32[]{:S(2)}) collective-permute-start(bf16[64,512]{1,0:T(8,128)(2,1)S(1)} %get-tuple-element.39), channel_id=1, source_target_pairs={{0,16},{1,17},{2,18},{3,19},{4,20},{5,21},{6,22},{7,23},{8,24},{9,... | collective-permute-start | bytes 196616 | tf_op jit(solution)/shard_map/ppermute | solution.py:280
  42.6 0.6 dynamic-slice
  44.0 0.1 maximum_dynamic-update-slice_fusion
  44.1 0.1 pad_add_fusion.place
  44.2 10.5 %all-reduce = f32[2064]{0:T(1024)S(1)} all-reduce(f32[2064]{0:T(1024)S(1)} %maximum_dynamic-update-slice_fusion), channel_id=2, replica_groups=mesh['rows'=2,'samples'=4,'chan'=4] {'samples'}, use_global_device_ids=true, to_apply=%add | all-reduce | flops 2064 | bytes 16512
  54.7 0.1 reshape.63
  54.8 1.2 energy.1
  56.0 6.9 %psum.21.energy = f32[64,128]{1,0:T(8,128)S(1)} all-reduce(f32[64,128]{1,0:T(8,128)S(1)} %get-tuple-element.22), channel_id=1, replica_groups=mesh['rows'=2,'samples'=4,'chan'=4] {'rows'}, use_global_device_ids=true, to_apply=%region_0.0 | all-reduce | flops 8192 | bytes 65536 | tf_op jit(solution)/shard_map/psum | solution.py:299
  62.9 0.8 modulated.1
  63.7 0.7 collective-permute-start.6
  64.5 0.0 collective-permute-done.13.refs_9_
  64.5 6.5 %collective-permute-start.7 = (bf16[64,576]{1,0:T(8,128)(2,1)S(1)}, bf16[64,576]{1,0:T(8,128)(2,1)S(1)}, u32[]{:S(2)}, u32[]{:S(2)}) collective-permute-start(bf16[64,576]{1,0:T(8,128)(2,1)S(1)} %get-tuple-element.24), channel_id=1, source_target_pairs={{1,0},{2,1},{17,2},{18,3},{3,16},{0,17},{19,18},{16,19},{5,4},{6,5... | collective-permute-start | bytes 221192 | tf_op jit(solution)/shard_map/ppermute | solution.py:310
  71.0 0.0 collective-permute-done.12.refs_8_
  71.0 1.6 %collective-permute-start.8 = (bf16[64,576]{1,0:T(8,128)(2,1)S(1)}, bf16[64,576]{1,0:T(8,128)(2,1)S(1)}, u32[]{:S(2)}, u32[]{:S(2)}) collective-permute-start(bf16[64,576]{1,0:T(8,128)(2,1)S(1)} %get-tuple-element.25), channel_id=1, source_target_pairs={{2,0},{3,1},{18,2},{19,3},{0,16},{1,17},{16,18},{17,19},{6,4},{7,5... | collective-permute-start | bytes 221192 | tf_op jit(solution)/shard_map/ppermute | solution.py:310
  72.7 0.0 collective-permute-done.5.refs_6_
  72.7 0.5 collective-permute-start.9
  73.2 0.0 collective-permute-done.2.refs_3_
  73.2 1.0 copy-done.4
  74.2 5.5 %kernel_grad.1 = (bf16[64,576]{1,0:T(8,128)(2,1)S(1)}, bf16[64,576]{1,0:T(8,128)(2,1)S(1)}, bf16[64,576]{1,0:T(8,128)(2,1)S(1)}, bf16[64,576]{1,0:T(8,128)(2,1)S(1)}) custom-call(bf16[64,4096]{1,0:T(8,128)(2,1)S(1)} %bitcast.28, bf16[64,4096]{1,0:T(8,128)(2,1)S(1)} %copy-done.4, bf16[64,4096]{1,0:T(8,128)(2,1)} %collective-permute-done.1.refs_2_, ...), custom_call_target="tpu_custom_call" | custom-call | flops 1207959552 | bytes 4718592 | tf_op jit(solution)/shard_map/kernel_grad/pallas_call | solution.py:312
  79.7 0.1 select_select_fusion
  79.8 3.4 %collective-permute-start.17 = (bf16[64,576]{1,0:T(8,128)(2,1)S(1)}, bf16[64,576]{1,0:T(8,128)(2,1)S(1)}, u32[]{:S(2)}, u32[]{:S(2)}) collective-permute-start(bf16[64,576]{1,0:T(8,128)(2,1)S(1)} %get-tuple-element.40), channel_id=1, source_target_pairs={{0,3},{1,0},{2,19},{3,16},{16,1},{17,2},{18,17},{19,18},{4,7},{5,4... | collective-permute-start | bytes 221192 | tf_op jit(solution)/shard_map/ppermute | solution.py:336
  83.1 0.0 collective-permute-done.6.refs_7_
  83.1 0.0 collective-permute-done.7.refs_8_
  83.1 0.0 collective-permute-done.8.refs_9_
  83.2 0.0 collective-permute-done.9.refs_10_
  83.2 5.6 %input_grad.1 = (f32[64,4096]{1,0:T(8,128)S(1)}, f32[64,512]{1,0:T(8,128)S(1)}, f32[64,512]{1,0:T(8,128)S(1)}) custom-call(s32[3]{0:T(128)S(1)} %pad_add_fusion.place, bf16[64,4096]{1,0:T(8,128)(2,1)S(1)} %bitcast.29, bf16[64,4096]{1,0:T(8,128)(2,1)S(1)} %copy-done.5, bf16[64,4096]{1,0:T(8,128)(2,1)} %collective-permute-done.1.refs_2_, ...), custom_call_target="tpu_custom_call" | custom-call | flops 1207959552 | bytes 4718592 | tf_op jit(solution)/shard_map/input_grad/pallas_call | solution.py:338
  88.8 3.6 %collective-permute-start.10 = (f32[64,512]{1,0:T(8,128)S(1)}, f32[64,512]{1,0:T(8,128)}, u32[]{:S(2)}, u32[]{:S(2)}) collective-permute-start(f32[64,512]{1,0:T(8,128)S(1)} %get-tuple-element.28), channel_id=1, source_target_pairs={{0,16},{1,17},{2,18},{3,19},{4,20},{5,21},{6,22},{7,23},{8,24},{9,... | collective-permute-start | bytes 393224 | tf_op jit(solution)/shard_map/ppermute | solution.py:358
  92.4 1.3 collective-permute-start.11
  93.7 2.8 %collective-permute-start.16 = (bf16[64,576]{1,0:T(8,128)(2,1)S(1)}, bf16[64,576]{1,0:T(8,128)(2,1)S(1)}, u32[]{:S(2)}, u32[]{:S(2)}) collective-permute-start(bf16[64,576]{1,0:T(8,128)(2,1)S(1)} %get-tuple-element.41), channel_id=1, source_target_pairs={{0,2},{1,3},{2,18},{3,19},{16,0},{17,1},{18,16},{19,17},{4,6},{5,7... | collective-permute-start | bytes 221192 | tf_op jit(solution)/shard_map/ppermute | solution.py:336
  96.4 0.6 collective-permute-start.15
  97.0 0.0 collective-permute-done.17.refs_3_
  97.0 0.7 collective-permute-start.14
  97.7 0.1 pad.1.clone
  97.8 0.6 copy.16
  98.4 1.7 %collective-permute-done.16.refs_2_ = bf16[64,576]{1,0:T(8,128)(2,1)S(1)} collective-permute-done((bf16[64,576]{1,0:T(8,128)(2,1)S(1)}, bf16[64,576]{1,0:T(8,128)(2,1)S(1)}, u32[]{:S(2)}, u32[]{:S(2)}) %collective-permute-start.16) | collective-permute-done | bytes 73760 | tf_op jit(solution)/shard_map/ppermute | solution.py:336
  100.1 1.9 %collective-permute-done.15.refs_1_ = bf16[64,576]{1,0:T(8,128)(2,1)S(1)} collective-permute-done((bf16[64,576]{1,0:T(8,128)(2,1)S(1)}, bf16[64,576]{1,0:T(8,128)(2,1)S(1)}, u32[]{:S(2)}, u32[]{:S(2)}) %collective-permute-start.15) | collective-permute-done | bytes 73760 | tf_op jit(solution)/shard_map/ppermute | solution.py:336
  102.0 0.0 collective-permute-done.14.refs_0_
  102.0 0.9 collect.1
  102.9 0.0 collective-permute-start.20
  102.9 0.6 collective-permute-start.19
  103.5 0.2 collective-permute-start.18
  103.7 30.7 %psum.22.slope = f32[64,128]{1,0:T(8,128)S(1)} all-reduce(f32[64,128]{1,0:T(8,128)S(1)} %get-tuple-element.34), channel_id=1, replica_groups=mesh['rows'=2,'samples'=4,'chan'=4] {'rows','samples'}, use_global_device_ids=true, to_apply=%region_1.2 | all-reduce | flops 8192 | bytes 65536 | tf_op jit(solution)/shard_map/psum | solution.py:381
  134.4 1.0 copy.13
  135.5 0.1 copy.14
  135.6 1.1 fusion
  136.8 2.8 %bank_grad.1 = (f32[4,9,64,128]{3,2,1,0:T(8,128)}, f32[4,128]{1,0:T(4,128)S(1)}) custom-call(s32[3]{0:T(128)S(1)} %pad_add_fusion.place, f32[4,4]{1,0:T(4,128)S(1)} %slice.16.sel, f32[4,9,64,128]{3,2,1,0:T(8,128)S(1)} %copy-done, f32[4,128]{1,0:T(4,128)S(1)} %get-tuple-element.21.style, f32[64,128]{1,0:T(8,128)S(1)} %psum.21.energy, ...), custom_call_target="tpu_custom_call" | custom-call | flops 40000000 | bytes 2359296 | tf_op jit(solution)/shard_map/bank_grad/pallas_call | solution.py:382
  139.5 9.3 %psum.23 = f32[4,128]{1,0:T(4,128)S(1)} all-reduce(f32[4,128]{1,0:T(4,128)S(1)} %get-tuple-element.37), channel_id=1, replica_groups=mesh['rows'=2,'samples'=4,'chan'=4] {'chan'}, use_global_device_ids=true, to_apply=%region_2.3 | all-reduce | flops 512 | bytes 4096 | tf_op jit(solution)/shard_map/psum | solution.py:395
  148.8 0.5 reduce_sum.19
  149.4 1.0 multiply_reduce_fusion
  (28 shorter events, 0.1 us)
Async XLA Ops:
  0.6 21.1 %copy-start.6 = (bf16[1,64,8,512]{3,2,1,0:T(8,128)(2,1)S(1)}, bf16[1,64,8,512]{3,2,1,0:T(8,128)(2,1)}, u32[]{:S(2)}) copy-start(bf16[1,64,8,512]{3,2,1,0:T(8,128)(2,1)} %param.7) | copy-start | bytes 1572868
  0.6 42.0 %copy-start.9 = (u32[32]{0:T(128)S(1)}, u32[32]{0:T(128)}, u32[]{:S(2)}) copy-start(u32[32]{0:T(128)} %constant.65) | copy-start | bytes 388
  0.7 43.3 %copy-start.8 = (s32[1,4]{1,0:T(1,128)S(1)}, s32[1,4]{1,0:T(1,128)}, u32[]{:S(2)}) copy-start(s32[1,4]{1,0:T(1,128)} %param.10) | copy-start | bytes 52
  0.7 43.3 %copy-start.7 = (f32[1,512]{1,0:T(1,128)S(1)}, f32[1,512]{1,0:T(1,128)}, u32[]{:S(2)}) copy-start(f32[1,512]{1,0:T(1,128)} %param.11) | copy-start | bytes 6148
  0.7 54.1 %copy-start = (f32[4,9,64,128]{3,2,1,0:T(8,128)S(1)}, f32[4,9,64,128]{3,2,1,0:T(8,128)}, u32[]{:S(2)}) copy-start(f32[4,9,64,128]{3,2,1,0:T(8,128)} %bank.7) | copy-start | bytes 3538948
  0.7 54.1 %copy-start.1 = (f32[512,128]{1,0:T(8,128)S(1)}, f32[512,128]{1,0:T(8,128)}, u32[]{:S(2)}) copy-start(f32[512,128]{1,0:T(8,128)} %affine_w.1) | copy-start | bytes 786436
  0.7 54.1 %copy-start.2 = (f32[128]{0:T(128)S(1)}, f32[128]{0:T(128)}, u32[]{:S(2)}) copy-start(f32[128]{0:T(128)} %param.13) | copy-start | bytes 1540
  2.1 16.8 %collective-permute-start.3 = (bf16[64,4096]{1,0:T(8,128)(2,1)S(1)}, bf16[64,4096]{1,0:T(8,128)(2,1)S(1)}, u32[]{:S(2)}, u32[]{:S(2)}) collective-permute-start(bf16[64,4096]{1,0:T(8,128)(2,1)S(1)} %bitcast.26), channel_id=1, source_target_pairs={{1,0},{2,1},{3,2},{5,4},{6,5},{7,6},{9,8},{10,9},{11,10},{13,12},{... | collective-permute-start | bytes 1572872 | tf_op jit(solution)/shard_map/ppermute | solution.py:273
  3.4 16.8 %collective-permute-start = (bf16[64,4096]{1,0:T(8,128)(2,1)S(1)}, bf16[64,4096]{1,0:T(8,128)(2,1)S(1)}, u32[]{:S(2)}, u32[]{:S(2)}) collective-permute-start(bf16[64,4096]{1,0:T(8,128)(2,1)S(1)} %bitcast.27), channel_id=1, source_target_pairs={{0,1},{1,2},{2,3},{4,5},{5,6},{6,7},{8,9},{9,10},{10,11},{12,13},{... | collective-permute-start | bytes 1572872 | tf_op jit(solution)/shard_map/ppermute | solution.py:272
  18.9 15.1 %collective-permute-start.4 = (bf16[64,4096]{1,0:T(8,128)(2,1)S(1)}, bf16[64,4096]{1,0:T(8,128)(2,1)}, u32[]{:S(2)}, u32[]{:S(2)}) collective-permute-start(bf16[64,4096]{1,0:T(8,128)(2,1)S(1)} %collective-permute-done.3.refs_4_), channel_id=1, source_target_pairs={{1,0},{2,1},{5,4},{6,5},{9,8},{10,9},{13,12},{14,13},{17,16},{18,1... | collective-permute-start | bytes 1572872 | tf_op jit(solution)/shard_map/ppermute | solution.py:273
  20.2 13.8 %copy-start.3 = (bf16[64,4096]{1,0:T(8,128)(2,1)}, bf16[64,4096]{1,0:T(8,128)(2,1)S(1)}, u32[]{:S(2)}) copy-start(bf16[64,4096]{1,0:T(8,128)(2,1)S(1)} %collective-permute-done.refs_1_) | copy-start | bytes 1572868
  20.2 15.1 %collective-permute-start.1 = (bf16[64,4096]{1,0:T(8,128)(2,1)S(1)}, bf16[64,4096]{1,0:T(8,128)(2,1)}, u32[]{:S(2)}, u32[]{:S(2)}) collective-permute-start(bf16[64,4096]{1,0:T(8,128)(2,1)S(1)} %collective-permute-done.refs_1_), channel_id=1, source_target_pairs={{1,2},{2,3},{5,6},{6,7},{9,10},{10,11},{13,14},{14,15},{17,18},{18... | collective-permute-start | bytes 1572872 | tf_op jit(solution)/shard_map/ppermute | solution.py:272
  34.0 38.7 %collective-permute-start.5 = (bf16[64,4096]{1,0:T(8,128)(2,1)}, bf16[64,4096]{1,0:T(8,128)(2,1)}, u32[]{:S(2)}, u32[]{:S(2)}) collective-permute-start(bf16[64,4096]{1,0:T(8,128)(2,1)} %collective-permute-done.4.refs_5_), channel_id=1, source_target_pairs={{1,0},{5,4},{9,8},{13,12},{17,16},{21,20},{25,24},{29,28}} | collective-permute-start | bytes 1572872 | tf_op jit(solution)/shard_map/ppermute | solution.py:273
  35.3 37.9 %collective-permute-start.2 = (bf16[64,4096]{1,0:T(8,128)(2,1)}, bf16[64,4096]{1,0:T(8,128)(2,1)}, u32[]{:S(2)}, u32[]{:S(2)}) collective-permute-start(bf16[64,4096]{1,0:T(8,128)(2,1)} %collective-permute-done.1.refs_2_), channel_id=1, source_target_pairs={{2,3},{6,7},{10,11},{14,15},{18,19},{22,23},{26,27},{30,31}} | collective-permute-start | bytes 1572872 | tf_op jit(solution)/shard_map/ppermute | solution.py:272
  36.8 27.7 %collective-permute-start.13 = (bf16[64,512]{1,0:T(8,128)(2,1)S(1)}, bf16[64,512]{1,0:T(8,128)(2,1)S(1)}, u32[]{:S(2)}, u32[]{:S(2)}) collective-permute-start(bf16[64,512]{1,0:T(8,128)(2,1)S(1)} %get-tuple-element.38), channel_id=1, source_target_pairs={{16,0},{17,1},{18,2},{19,3},{20,4},{21,5},{22,6},{23,7},{24,8},{25... | collective-permute-start | bytes 196616 | tf_op jit(solution)/shard_map/ppermute | solution.py:281
  38.1 33.0 %collective-permute-start.12 = (bf16[64,512]{1,0:T(8,128)(2,1)S(1)}, bf16[64,512]{1,0:T(8,128)(2,1)S(1)}, u32[]{:S(2)}, u32[]{:S(2)}) collective-permute-start(bf16[64,512]{1,0:T(8,128)(2,1)S(1)} %get-tuple-element.39), channel_id=1, source_target_pairs={{0,16},{1,17},{2,18},{3,19},{4,20},{5,21},{6,22},{7,23},{8,24},{9,... | collective-permute-start | bytes 196616 | tf_op jit(solution)/shard_map/ppermute | solution.py:280
  63.7 19.4 %collective-permute-start.6 = (bf16[64,576]{1,0:T(8,128)(2,1)S(1)}, bf16[64,576]{1,0:T(8,128)(2,1)S(1)}, u32[]{:S(2)}, u32[]{:S(2)}) collective-permute-start(bf16[64,576]{1,0:T(8,128)(2,1)S(1)} %get-tuple-element.23), channel_id=1, source_target_pairs={{0,0},{1,1},{16,2},{17,3},{2,16},{3,17},{18,18},{19,19},{4,4},{5,5... | collective-permute-start | bytes 221192 | tf_op jit(solution)/shard_map/ppermute | solution.py:310
  64.5 18.6 %collective-permute-start.7 = (bf16[64,576]{1,0:T(8,128)(2,1)S(1)}, bf16[64,576]{1,0:T(8,128)(2,1)S(1)}, u32[]{:S(2)}, u32[]{:S(2)}) collective-permute-start(bf16[64,576]{1,0:T(8,128)(2,1)S(1)} %get-tuple-element.24), channel_id=1, source_target_pairs={{1,0},{2,1},{17,2},{18,3},{3,16},{0,17},{19,18},{16,19},{5,4},{6,5... | collective-permute-start | bytes 221192 | tf_op jit(solution)/shard_map/ppermute | solution.py:310
  71.0 12.1 %collective-permute-start.8 = (bf16[64,576]{1,0:T(8,128)(2,1)S(1)}, bf16[64,576]{1,0:T(8,128)(2,1)S(1)}, u32[]{:S(2)}, u32[]{:S(2)}) collective-permute-start(bf16[64,576]{1,0:T(8,128)(2,1)S(1)} %get-tuple-element.25), channel_id=1, source_target_pairs={{2,0},{3,1},{18,2},{19,3},{0,16},{1,17},{16,18},{17,19},{6,4},{7,5... | collective-permute-start | bytes 221192 | tf_op jit(solution)/shard_map/ppermute | solution.py:310
  72.7 10.5 %collective-permute-start.9 = (bf16[64,576]{1,0:T(8,128)(2,1)S(1)}, bf16[64,576]{1,0:T(8,128)(2,1)S(1)}, u32[]{:S(2)}, u32[]{:S(2)}) collective-permute-start(bf16[64,576]{1,0:T(8,128)(2,1)S(1)} %get-tuple-element.26), channel_id=1, source_target_pairs={{3,0},{0,1},{19,2},{16,3},{1,16},{2,17},{17,18},{18,19},{7,4},{4,5... | collective-permute-start | bytes 221192 | tf_op jit(solution)/shard_map/ppermute | solution.py:310
  73.2 1.0 copy-start.4
  74.2 8.9 %copy-start.5 = (bf16[64,4096]{1,0:T(8,128)(2,1)S(1)}, bf16[64,4096]{1,0:T(8,128)(2,1)}, u32[]{:S(2)}) copy-start(bf16[64,4096]{1,0:T(8,128)(2,1)} %copy-done.3) | copy-start | bytes 1572868
  79.8 17.3 %collective-permute-start.17 = (bf16[64,576]{1,0:T(8,128)(2,1)S(1)}, bf16[64,576]{1,0:T(8,128)(2,1)S(1)}, u32[]{:S(2)}, u32[]{:S(2)}) collective-permute-start(bf16[64,576]{1,0:T(8,128)(2,1)S(1)} %get-tuple-element.40), channel_id=1, source_target_pairs={{0,3},{1,0},{2,19},{3,16},{16,1},{17,2},{18,17},{19,18},{4,7},{5,4... | collective-permute-start | bytes 221192 | tf_op jit(solution)/shard_map/ppermute | solution.py:336
  88.8 45.7 %collective-permute-start.10 = (f32[64,512]{1,0:T(8,128)S(1)}, f32[64,512]{1,0:T(8,128)}, u32[]{:S(2)}, u32[]{:S(2)}) collective-permute-start(f32[64,512]{1,0:T(8,128)S(1)} %get-tuple-element.28), channel_id=1, source_target_pairs={{0,16},{1,17},{2,18},{3,19},{4,20},{5,21},{6,22},{7,23},{8,24},{9,... | collective-permute-start | bytes 393224 | tf_op jit(solution)/shard_map/ppermute | solution.py:358
  92.4 43.1 %collective-permute-start.11 = (f32[64,512]{1,0:T(8,128)S(1)}, f32[64,512]{1,0:T(8,128)S(1)}, u32[]{:S(2)}, u32[]{:S(2)}) collective-permute-start(f32[64,512]{1,0:T(8,128)S(1)} %get-tuple-element.29), channel_id=1, source_target_pairs={{16,0},{17,1},{18,2},{19,3},{20,4},{21,5},{22,6},{23,7},{24,8},{25... | collective-permute-start | bytes 393224 | tf_op jit(solution)/shard_map/ppermute | solution.py:357
  93.7 6.4 %collective-permute-start.16 = (bf16[64,576]{1,0:T(8,128)(2,1)S(1)}, bf16[64,576]{1,0:T(8,128)(2,1)S(1)}, u32[]{:S(2)}, u32[]{:S(2)}) collective-permute-start(bf16[64,576]{1,0:T(8,128)(2,1)S(1)} %get-tuple-element.41), channel_id=1, source_target_pairs={{0,2},{1,3},{2,18},{3,19},{16,0},{17,1},{18,16},{19,17},{4,6},{5,7... | collective-permute-start | bytes 221192 | tf_op jit(solution)/shard_map/ppermute | solution.py:336
  96.4 5.5 %collective-permute-start.15 = (bf16[64,576]{1,0:T(8,128)(2,1)S(1)}, bf16[64,576]{1,0:T(8,128)(2,1)S(1)}, u32[]{:S(2)}, u32[]{:S(2)}) collective-permute-start(bf16[64,576]{1,0:T(8,128)(2,1)S(1)} %get-tuple-element.42), channel_id=1, source_target_pairs={{0,1},{1,2},{2,17},{3,18},{16,3},{17,0},{18,19},{19,16},{4,5},{5,6... | collective-permute-start | bytes 221192 | tf_op jit(solution)/shard_map/ppermute | solution.py:336
  97.0 5.0 %collective-permute-start.14 = (bf16[64,576]{1,0:T(8,128)(2,1)S(1)}, bf16[64,576]{1,0:T(8,128)(2,1)S(1)}, u32[]{:S(2)}, u32[]{:S(2)}) collective-permute-start(bf16[64,576]{1,0:T(8,128)(2,1)S(1)} %get-tuple-element.43), channel_id=1, source_target_pairs={{0,0},{1,1},{2,16},{3,17},{16,2},{17,3},{18,18},{19,19},{4,4},{5,5... | collective-permute-start | bytes 221192 | tf_op jit(solution)/shard_map/ppermute | solution.py:336
  102.9 33.9 %collective-permute-start.20 = (bf16[9,64,128]{2,1,0:T(8,128)(2,1)S(1)}, bf16[9,64,128]{2,1,0:T(8,128)(2,1)S(1)}, u32[]{:S(2)}, u32[]{:S(2)}) collective-permute-start(bf16[9,64,128]{2,1,0:T(8,128)(2,1)S(1)} %get-tuple-element.35.refs_0_), channel_id=1, source_target_pairs={{0,12},{4,0},{8,4},{12,8},{1,13},{5,1},{9,5},{13,9},{2,14},{6,2},{... | collective-permute-start | bytes 442376 | tf_op jit(solution)/shard_map/ppermute | solution.py:378
  102.9 33.8 %collective-permute-start.19 = (bf16[9,64,128]{2,1,0:T(8,128)(2,1)S(1)}, bf16[9,64,128]{2,1,0:T(8,128)(2,1)S(1)}, u32[]{:S(2)}, u32[]{:S(2)}) collective-permute-start(bf16[9,64,128]{2,1,0:T(8,128)(2,1)S(1)} %get-tuple-element.35.refs_0_), channel_id=1, source_target_pairs={{0,8},{4,12},{8,0},{12,4},{1,9},{5,13},{9,1},{13,5},{2,10},{6,14},... | collective-permute-start | bytes 442376 | tf_op jit(solution)/shard_map/ppermute | solution.py:378
  103.5 33.2 %collective-permute-start.18 = (bf16[9,64,128]{2,1,0:T(8,128)(2,1)S(1)}, bf16[9,64,128]{2,1,0:T(8,128)(2,1)S(1)}, u32[]{:S(2)}, u32[]{:S(2)}) collective-permute-start(bf16[9,64,128]{2,1,0:T(8,128)(2,1)S(1)} %get-tuple-element.35.refs_0_), channel_id=1, source_target_pairs={{0,4},{4,8},{8,12},{12,0},{1,5},{5,9},{9,13},{13,1},{2,6},{6,10},{... | collective-permute-start | bytes 442376 | tf_op jit(solution)/shard_map/ppermute | solution.py:378

commit v2 on v0

v2 whole, which is shorter than its diff:
```python
import functools

import jax
import jax.numpy as jnp
from jax import lax
from jax.experimental import pallas as pl
from jax.experimental.pallas import tpu as pltpu
from jax.sharding import PartitionSpec as P

EPS = 1e-08
TAPS = 9
F32 = jnp.float32
BF16 = jnp.bfloat16
VMEM_LIMIT = 48 * 2**20


def params():
    return pltpu.CompilerParams(vmem_limit_bytes=VMEM_LIMIT)


def vspec(n):
    return [pl.BlockSpec(memory_space=pltpu.VMEM)] * n


def sspec(n):
    return [pl.BlockSpec(memory_space=pltpu.SMEM)] * n


def cost(flops, moved):
    return pl.CostEstimate(flops=flops, bytes_accessed=moved, transcendentals=0)


def column(table, index):
    lane = lax.broadcasted_iota(jnp.int32, table.shape, 1)
    return jnp.sum(jnp.where(lane == index, table, 0.0), axis=1, keepdims=True)


def beside(pieces):
    return pieces[0] if len(pieces) == 1 else jnp.concatenate(pieces, axis=1)


def mixed(bank_ref, sel, sample, tap):
    total = sel[sample, 0] * bank_ref[0, tap]
    for k in range(1, bank_ref.shape[0]):
        total = total + sel[sample, k] * bank_ref[k, tap]
    return total


def energy_kernel(sel, bank, latent, affine_w, affine_b, style_out, energy_out):
    samples = latent.shape[0]
    style = (
        jnp.dot(latent[...], affine_w[...], precision=lax.Precision.HIGHEST, preferred_element_type=F32)
        + affine_b[...]
    )
    style_out[...] = style
    out_ch, in_ch = bank.shape[2], bank.shape[3]
    totals = [jnp.zeros((out_ch, in_ch), F32) for _ in range(samples)]
    for tap in range(TAPS):
        for b in range(samples):
            plain = mixed(bank, sel, b, tap) * style[b : b + 1]
            totals[b] = totals[b] + plain * plain
    lane = lax.broadcasted_iota(jnp.int32, (out_ch, 128), 1)
    table = jnp.zeros((out_ch, 128), F32)
    for b in range(samples):
        table = jnp.where(lane == b, jnp.sum(totals[b], axis=1, keepdims=True), table)
    energy_out[...] = table


def modulated_kernel(rows, place, sel, bank, style, *refs):
    energies, (mod_out, scale_out) = refs[:rows], refs[rows:]
    sample = place[0]
    energy = energies[0][...]
    for r in range(1, rows):
        energy = energy + energies[r][...]
    scales = lax.rsqrt(energy + EPS)
    scale_out[...] = scales
    scale = column(scales, sample)
    own_style = style[pl.ds(sample, 1), :]
    for tap in range(TAPS):
        mod_out[tap] = (mixed(bank, sel, sample, tap) * own_style * scale).astype(BF16)


def blocks_kernel(rows, size, place, *refs):
    parts, whole, outs = refs[:rows], refs[rows], refs[rows + 1 : rows + 1 + size]
    by_row, by_chan = refs[rows + 1 + size :]
    row_at, chan_at = place[2], place[1]
    for r in range(rows):
        by_row[lax.rem(row_at - r + rows, rows)] = parts[r][...]
    ch = whole.shape[2] // size
    taps = []
    for tap in range(TAPS):
        value = beside([by_row[r, tap].astype(F32) for r in range(rows)])
        whole[tap] = value.astype(BF16)
        taps.append(value)
    for z in range(size):
        by_chan[z] = beside([value[:, z * ch : (z + 1) * ch] for value in taps]).astype(BF16)
    for d in range(size):
        outs[d][...] = by_chan[lax.rem(chan_at + d, size)]


def shifted(x, by):
    width = x.shape[1]
    lane = lax.broadcasted_iota(jnp.int32, x.shape, 1)
    moved = pltpu.roll(x, by % width, 1)
    return jnp.where(lane == (0 if by == 1 else width - 1), 0.0, moved)


def tap_products(g_ref, wide, total, height, width):
    total[...] = jnp.zeros(total.shape, F32)

    def body(row, _):
        g = g_ref[:, pl.ds(pl.multiple_of(row * width, width), width)]
        for kh in range(3):
            x = wide[:, pl.ds(pl.multiple_of((row + kh) * width, width), width)]
            total[kh] += lax.dot_general(g, x, (((1,), (1,)), ((), ())), preferred_element_type=F32)
        return 0

    lax.fori_loop(0, height, body, 0)
    return jnp.concatenate([total[kh] for kh in range(3)], axis=1)


def near_grad_kernel(size, height, width, *refs):
    cotan_own, left, right = refs[0], refs[1 : size - 1], refs[size - 1 : 2 * size - 3]
    feat, feat_before, feat_after, out, wide, gathered, total = refs[2 * size - 3 :]
    ch = feat.shape[0]
    gathered[0:ch] = cotan_own[...]
    for d in range(1, size):
        found = []
        if d < size - 1:
            found.append(left[d - 1][...])
        if size - d < size - 1:
            found.append(right[size - d - 1][...])
        gathered[d * ch : (d + 1) * ch] = found[0] if len(found) == 1 else found[0] + found[1]
    for row in range(height + 2):
        if row == 0:
            x = feat_before[...]
        elif row == height + 1:
            x = feat_after[...]
        else:
            x = feat[:, (row - 1) * width : row * width]
        wide[ch : 2 * ch, row * width : (row + 1) * width] = x
        x = x.astype(F32)
        wide[0:ch, row * width : (row + 1) * width] = shifted(x, 1).astype(BF16)
        wide[2 * ch : 3 * ch, row * width : (row + 1) * width] = shifted(x, -1).astype(BF16)
    out[...] = tap_products(gathered, wide, total, height, width).astype(BF16)


def far_grad_kernel(rows, size, height, width, left, right, wide, *refs):
    nears, far_out, outs = refs[:rows], refs[rows], refs[rows + 1 : rows + 1 + size]
    cotan, total = refs[rows + 1 + size :]
    cotan[...] = left[...] + right[...]
    far_out[...] = tap_products(cotan, wide, total, height, width).astype(BF16)
    ch = cotan.shape[0]
    for d in range(size):
        value = nears[0][d * ch : (d + 1) * ch].astype(F32)
        for r in range(1, rows):
            value = value + nears[r][d * ch : (d + 1) * ch].astype(F32)
        outs[d][...] = value.astype(BF16)


def sum_kernel(*refs):
    value = refs[0][...].astype(F32)
    for ref in refs[1:-1]:
        value = value + ref[...].astype(F32)
    refs[-1][...] = value.astype(BF16)


def input_grad_kernel(size, height, width, *refs):
    cotan_own, left, right = refs[0], refs[1:size], refs[size : 2 * size - 1]
    mods = refs[2 * size - 1 : 3 * size - 1]
    main, before, after, gathered, taps_t, total = refs[3 * size - 1 :]
    ch = cotan_own.shape[0]
    gathered[0:ch] = cotan_own[...]
    for d in range(1, size):
        gathered[d * ch : (d + 1) * ch] = left[d - 1][...] + right[size - d - 1][...]
    every = jnp.concatenate([mod[...].astype(F32) for mod in mods], axis=0)
    taps_t[...] = every.T.astype(BF16)
    total[...] = jnp.zeros(total.shape, F32)

    def body(row, _):
        g = gathered[:, pl.ds(pl.multiple_of(row * width, width), width)]
        for kh in range(3):
            y = jnp.dot(taps_t[kh * 3 * ch : (kh + 1) * 3 * ch], g, preferred_element_type=F32)
            total[row + kh] += y
        return 0

    lax.fori_loop(0, height, body, 0)
    for row in range(height + 2):
        value = total[row, ch : 2 * ch]
        value = value + shifted(total[row, 0:ch], -1) + shifted(total[row, 2 * ch : 3 * ch], 1)
        if row == 0:
            before[...] = value
        elif row == height + 1:
            after[...] = value
        else:
            main[:, (row - 1) * width : row * width] = value


def split3(x):
    high = x.astype(BF16).astype(F32)
    mid = (x - high).astype(BF16).astype(F32)
    return high, mid, x - high - mid


def collect_kernel(rows, size, place, scales, whole_mod, far, *refs):
    nears, out, by_chan, by_row = refs[:size], refs[size], refs[size + 1], refs[size + 2]
    sample, chan_at, row_at = place[0], place[1], place[2]
    for d in range(size):
        by_chan[lax.rem(chan_at + d, size)] = nears[d][...].astype(F32)
    by_chan[jnp.where(chan_at == 0, size - 1, 0)] += far[...].astype(F32)
    ch = whole_mod.shape[2] // size
    in_ch = out.shape[2]
    product = jnp.zeros(whole_mod.shape[1:], F32)
    for tap in range(TAPS):
        value = beside([by_chan[z, :, tap * ch : (tap + 1) * ch] for z in range(size)])
        product = product + value * whole_mod[tap].astype(F32)
        for r in range(rows):
            by_row[r, tap] = value[:, r * in_ch : (r + 1) * in_ch].astype(BF16)
    out[0:TAPS] = by_row[row_at]
    scale = column(scales[...], sample)
    fall = jnp.sum(product, axis=1, keepdims=True) * (scale * scale)
    lane = lax.broadcasted_iota(jnp.int32, out.shape[1:], 1)
    last = jnp.zeros(out.shape[1:], F32)
    for at, piece in enumerate(split3(fall)):
        last = jnp.where(lane == at, piece, last)
    out[TAPS] = last.astype(BF16)


def bank_grad_kernel(samples, place, sel, bank, style, scales, *refs):
    parts = refs[:samples]
    bank_grad, style_grad, held = refs[samples:]
    sample = place[0]
    for s in range(samples):
        held[lax.rem(sample - s + samples, samples)] = parts[s][...]
    styles, every_scale = style[...], scales[...]
    falls = []
    for b in range(samples):
        last = held[b, TAPS].astype(F32)
        falls.append(last[:, 0:1] + last[:, 1:2] + last[:, 2:3])
    sums = [jnp.zeros(bank.shape[2:], F32) for _ in range(samples)]
    for tap in range(TAPS):
        totals = [None] * bank.shape[0]
        for b in range(samples):
            kern = mixed(bank, sel, b, tap)
            own_style = styles[b : b + 1]
            plain_grad = held[b, tap].astype(F32) * every_scale[:, b : b + 1] - kern * own_style * falls[b]
            sums[b] = sums[b] + plain_grad * kern
            kernel_grad = plain_grad * own_style
            for k in range(bank.shape[0]):
                term = sel[b, k] * kernel_grad
                totals[k] = term if totals[k] is None else totals[k] + term
        for k in range(bank.shape[0]):
            bank_grad[k, tap] = totals[k]
    for b in range(samples):
        style_grad[b : b + 1] = jnp.sum(sums[b], axis=0, keepdims=True)


def affine_kernel(size, place, latent_t, *refs):
    parts, w_grad, b_grad, held = refs[:size], refs[size], refs[size + 1], refs[size + 2]
    for d in range(size):
        held[lax.rem(place[1] - d + size, size)] = parts[d][...]
    style_grad = held[0]
    for z in range(1, size):
        style_grad = style_grad + held[z]
    columns = latent_t[...]
    samples = style_grad.shape[0]
    total, bias = None, None
    for b in range(samples):
        row = style_grad[b : b + 1]
        term = columns[:, b : b + 1] * row
        total = term if total is None else total + term
        bias = row if bias is None else bias + row
    w_grad[...] = total
    b_grad[...] = bias


def call(kernel, name, outs, *operands, scalars=0, scratch=(), flops=10**6):
    outs = tuple(jax.ShapeDtypeStruct(*o) for o in outs)
    moved = sum(o.size * o.dtype.itemsize for o in (*outs, *operands))
    return pl.pallas_call(
        kernel,
        out_shape=outs,
        in_specs=sspec(scalars) + vspec(len(operands) - scalars),
        out_specs=tuple(vspec(len(outs))),
        scratch_shapes=[pltpu.VMEM(*s) for s in scratch],
        compiler_params=params(),
        cost_estimate=cost(flops, moved),
        name=name,
    )(*operands)


def exchange(x, axis):
    size = lax.axis_size(axis)
    return [x] + [
        lax.ppermute(x, axis, [(i, (i + s) % size) for i in range(size)]) for s in range(1, size)
    ]


def from_sides(first, last, axis):
    size, at = lax.axis_size(axis), lax.axis_index(axis)
    if size == 2:
        got = lax.ppermute(jnp.where(at == 0, last, first), axis, [(0, 1), (1, 0)])
        nothing = jnp.zeros_like(got)
        return jnp.where(at == 1, got, nothing), jnp.where(at == 0, got, nothing)
    up = [(i, i + 1) for i in range(size - 1)]
    down = [(i + 1, i) for i in range(size - 1)]
    return lax.ppermute(last, axis, up), lax.ppermute(first, axis, down)


def on_device(feature, out_grad, bank, select, latent, affine_w, affine_b):
    rows, samples, size = (lax.axis_size(a) for a in ("rows", "samples", "chan"))
    row_at, sample_at, chan_at = (lax.axis_index(a) for a in ("rows", "samples", "chan"))
    _, ch, height, width = feature.shape
    out_ch, in_ch = bank.shape[2:]
    pixels, all_ch = height * width, ch * size
    place = jnp.stack([sample_at, chan_at, row_at]).astype(jnp.int32)
    flops = 2 * TAPS * ch * ch * size * pixels

    cotan = out_grad[0].reshape(ch, pixels)
    left, right = [], []

    def step(number, from_left, from_right):
        left.append(
            lax.ppermute(from_left, "chan", [(i, i + 1) for i in range(number - 1, size - 1)])
        )
        right.append(
            lax.ppermute(from_right, "chan", [(i + 1, i) for i in range(size - number)])
        )

    step(1, cotan, cotan)

    feat = feature[0].reshape(ch, pixels)
    feat_before, feat_after = from_sides(feat[:, :width], feat[:, pixels - width :], "rows")
    small = jnp.concatenate([latent[0], select[0].astype(F32)])[None]
    small = exchange(small, "samples")
    at = jnp.remainder(sample_at - jnp.arange(samples), samples)
    small = jnp.zeros((samples, small[0].shape[1]), F32).at[at].set(jnp.concatenate(small, axis=0))
    latents, sel = small[:, : latent.shape[1]], small[:, latent.shape[1] :]
    style, energy = call(
        energy_kernel,
        "energy",
        [((samples, in_ch), F32), ((out_ch, 128), F32)],
        sel,
        bank,
        latents,
        affine_w,
        affine_b[None],
        scalars=1,
    )
    energies = exchange(energy, "rows")
    left[0], right[0], energies, feat_before, feat_after = lax.optimization_barrier(
        (left[0], right[0], energies, feat_before, feat_after)
    )

    step(2, left[0], right[0])
    mod_own, scales = call(
        functools.partial(modulated_kernel, rows),
        "modulated",
        [((TAPS, out_ch, in_ch), BF16), ((out_ch, 128), F32)],
        place,
        sel,
        bank,
        style,
        *energies,
        scalars=2,
    )
    message = ((ch, TAPS * ch), BF16)
    whole_mod, *to_send = call(
        functools.partial(blocks_kernel, rows, size),
        "mod_blocks",
        [((TAPS, out_ch, all_ch), BF16)] + [message] * size,
        place,
        *exchange(mod_own, "rows"),
        scalars=1,
        scratch=[((rows, TAPS, out_ch, in_ch), BF16), ((size, *message[0]), BF16)],
    )
    left[1], right[1], to_send = lax.optimization_barrier((left[1], right[1], to_send))
    mods = [to_send[0]] + [
        lax.ppermute(to_send[d], "chan", [(i, (i + d) % size) for i in range(size)])
        for d in range(1, size)
    ]

    for number in range(3, size):
        step(number, left[number - 2], right[number - 2])
    near, wide = call(
        functools.partial(near_grad_kernel, size, height, width),
        "near_grad",
        [((all_ch, TAPS * ch), BF16), ((3 * ch, (height + 2) * width), BF16)],
        cotan,
        *left[: size - 2],
        *right[: size - 2],
        feat,
        feat_before,
        feat_after,
        scratch=[((all_ch, pixels), BF16), ((3, all_ch, 3 * ch), F32)],
        flops=flops,
    )
    nears = exchange(near, "rows")
    left[-1], right[-1], nears, mods = lax.optimization_barrier((left[-1], right[-1], nears, mods))
    far, *near_sums = call(
        functools.partial(far_grad_kernel, rows, size, height, width),
        "far_grad",
        [message] * (1 + size),
        left[-1],
        right[-1],
        wide,
        *nears,
        scratch=[((ch, pixels), BF16), ((3, ch, 3 * ch), F32)],
        flops=flops // size,
    )
    fars = exchange(far, "rows")
    got = [near_sums[0]]
    for d in range(1, size):
        pairs = [(i, i - d) for i in range(d, size) if d < size - 1]
        pairs += [(i, i - d + size) for i in range(d) if size - d < size - 1]
        got.append(lax.ppermute(near_sums[d], "chan", pairs))
    (far_sum,) = call(sum_kernel, "far_sum", [message], *fars)
    far_got = lax.ppermute(far_sum, "chan", [(0, size - 1), (size - 1, 0)])

    (own,) = call(
        functools.partial(collect_kernel, rows, size),
        "collect",
        [((TAPS + 1, out_ch, in_ch), BF16)],
        place,
        scales,
        whole_mod,
        far_got,
        *got,
        scalars=1,
        scratch=[((size, *message[0]), F32), ((rows, TAPS, out_ch, in_ch), BF16)],
    )
    every = exchange(own, "samples")

    own, mods = lax.optimization_barrier((own, mods))
    main, before, after = call(
        functools.partial(input_grad_kernel, size, height, width),
        "input_grad",
        [((ch, pixels), F32), ((ch, width), F32), ((ch, width), F32)],
        cotan,
        *left,
        *right,
        *mods,
        scratch=[
            ((all_ch, pixels), BF16),
            ((TAPS * ch, all_ch), BF16),
            ((height + 2, 3 * ch, width), F32),
        ],
        flops=flops,
    )
    every, main, before, after = lax.optimization_barrier((every, main, before, after))
    from_above, from_below = from_sides(before, after, "rows")
    edge = jnp.concatenate(
        [from_above[:, None], jnp.zeros((ch, height - 2, width), F32), from_below[:, None]], axis=1
    )
    feature_grad = (main.reshape(ch, height, width) + edge).astype(BF16)[None]

    bank_grad, style_part = call(
        functools.partial(bank_grad_kernel, samples),
        "bank_grad",
        [(bank.shape, F32), ((samples, in_ch), F32)],
        place,
        sel,
        bank,
        style,
        scales,
        *every,
        scalars=2,
        scratch=[((samples, TAPS + 1, out_ch, in_ch), BF16)],
    )
    affine_w_grad, affine_b_grad = call(
        functools.partial(affine_kernel, size),
        "affine",
        [(affine_w.shape, F32), ((1, in_ch), F32)],
        place,
        latents.T,
        *exchange(style_part, "chan"),
        scalars=1,
        scratch=[((size, samples, in_ch), F32)],
    )
    return (feature_grad, bank_grad, affine_w_grad, affine_b_grad[0])


def solution(mesh):
    return jax.shard_map(
        on_device,
        mesh=mesh,
        in_specs=(
            P("samples", "chan", "rows", None),
            P("samples", "chan", "rows", None),
            P(None, None, "chan", "rows"),
            P("samples", None),
            P("samples", None),
            P(None, "rows"),
            P("rows"),
        ),
        out_specs=(
            P("samples", "chan", "rows", None),
            P(None, None, "chan", "rows"),
            P(None, "rows"),
            P("rows"),
        ),
        check_vma=False,
    )
```

time: 273 us -> 109 us (0.40)
  waiting for transfers between devices: 162 us -> 38.7 us
  local copies, waits for them, and re-layouts: 36.9 us -> 3.67 us
  starting transfers between devices: 6.49 us -> 39.7 us
  blocking collectives: 29.1 us -> 0 us
  Pallas kernels: 0 us -> 21.3 us
  matrix products: 18.3 us -> 0 us
  between operations: 14.1 us -> 0.98 us
    reduce_scatter x2 -> x0, waiting for transfers between devices: 59.1 us -> none  [the longest x1 56.5 us: on_device(): lax.psum_scatter(total, 'chan', scatter_dimension=0, tiled=True)]
    all_gather x1 -> x0, waiting for transfers between devices: 55 us -> none  [on_device(): lax.all_gather(feat_rim, 'chan', axis=0, tiled=True)]
    psum x1 -> x0, waiting for transfers between devices: 42.1 us -> none  [on_device(): lax.psum((bank_part, affine_part, style_whole), 'samples')]
    ppermute x2 -> x28, starting transfers between devices: 6.14 us -> 39.7 us  [the longest x13 14.1 us: exchange(): lax.ppermute(x, axis, [(i, (i + s) % size) for i in range(size)])]
    ppermute x2 -> x28, waiting for transfers between devices: 5.56 us -> 38.7 us  [the longest x3 14.5 us: step(): lax.ppermute(from_right, 'chan', [(i + 1, i) for i in range(size - number)])]
    psum x3 -> x0, blocking collectives: 23.3 us -> none  [the longest x1 11.8 us: on_device(): style_whole = lax.psum(style_part, 'chan')]
    pallas_call x0 -> x10, Pallas kernels: none -> 21.3 us  [call(): pl.pallas_call(kernel, out_shape=outs, in_specs=sspec(scalars) + vspec(le...]
    dot_general x20 -> x0, matrix products: 18.3 us -> none  [the longest x9 8.5 us: on_device(): lax.dot_general(mod_rows[tap_index], cotan_taps[tap_index], (((0,), (0,))...]
  transfers between devices with their start and end apart: 6 -> 28, of which waited for: 6 -> 13; matrix products, arithmetic and copies ran while one was open for 6% -> 4% of each run, Pallas kernels for 0% -> 16%
where the time goes in v2:
time: 109 us; the launch traced here: 108 us
  starting transfers between devices  39.7 us (36%)
  waiting for transfers between devices  38.7 us (36%)
  Pallas kernels  21.3 us (20%)
  other arithmetic  3.92 us (4%)
  local copies, waits for them, and re-layouts  3.67 us (3%)
    pallas_call x10, Pallas kernels, call(): pl.pallas_call(kernel, out_shape=outs, in_specs=sspec(scalars) + vspec(le...  21.3 us
    ppermute x3, waiting for transfers between devices, step(): lax.ppermute(from_right, 'chan', [(i + 1, i) for i in range(size - number)])  14.5 us
    ppermute x13, starting transfers between devices, exchange(): lax.ppermute(x, axis, [(i, (i + s) % size) for i in range(size)])  14.1 us
    ppermute x13, waiting for transfers between devices, exchange(): lax.ppermute(x, axis, [(i, (i + s) % size) for i in range(size)])  8.87 us
    ppermute x3, waiting for transfers between devices, on_device(): lax.ppermute(to_send[d], 'chan', [(i, (i + d) % size) for i in range(size)])  7.46 us
    ppermute x3, starting transfers between devices, on_device(): got.append(lax.ppermute(near_sums[d], 'chan', pairs))  6.55 us
    ppermute x3, starting transfers between devices, step(): lax.ppermute(from_left, 'chan', [(i, i + 1) for i in range(number - 1, si...  5.64 us
    ppermute x1, waiting for transfers between devices, on_device(): far_got = lax.ppermute(far_sum, 'chan', [(0, size - 1), (size - 1, 0)])  5.11 us
  transfers between devices with their start and end apart: 28, of which 13 were waited for; matrix products, arithmetic and copies ran while one was open for 4% of the time, Pallas kernels for 16%

profile of v2, /device:TPU:0, one launch (start us, length us, event | category | flops | bytes accessed | tf_op | source)
XLA Modules:
  0.0 108.3 jit_solution(15056252821421522966)
XLA Ops:
  0.6 0.7 convert_bitcast_fusion
  1.3 0.7 pad_maximum_fusion
  2.0 2.4 %collective-permute-start.2 = (f32[1,516]{1,0:T(1,128)S(1)}, f32[1,516]{1,0:T(1,128)S(1)}, u32[]{:S(2)}, u32[]{:S(2)}) collective-permute-start(f32[1,516]{1,0:T(1,128)S(1)} %broadcast_in_dim.23), channel_id=1, source_target_pairs={{0,12},{4,0},{8,4},{12,8},{1,13},{5,1},{9,5},{13,9},{2,14},{6,2},{... | collective-permute-start | bytes 6200 | tf_op jit(solution)/shard_map/ppermute | solution.py:295
  4.4 0.6 collective-permute-start.1
  5.1 0.2 collective-permute-start
  5.2 1.3 %copy.22 = bf16[8,8,8,512]{3,1,2,0:T(8,128)(2,1)S(1)} copy(bf16[8,8,8,512]{3,2,1,0:T(8,128)(2,1)} %bitcast.38) | data formatting | bytes 1048576
  6.6 3.5 %collective-permute-start.3 = (bf16[64,4096]{1,0:T(8,128)(2,1)S(1)}, bf16[64,4096]{1,0:T(8,128)(2,1)S(1)}, u32[]{:S(2)}, u32[]{:S(2)}) collective-permute-start(bf16[64,4096]{1,0:T(8,128)(2,1)S(1)} %bitcast.32), channel_id=1, source_target_pairs={{0,1},{1,2},{2,3},{4,5},{5,6},{6,7},{8,9},{9,10},{10,11},{12,13},{... | collective-permute-start | bytes 1572872 | tf_op jit(solution)/shard_map/ppermute | solution.py:324
  10.1 1.3 %collective-permute-start.4 = (bf16[64,4096]{1,0:T(8,128)(2,1)S(1)}, bf16[64,4096]{1,0:T(8,128)(2,1)}, u32[]{:S(2)}, u32[]{:S(2)}) collective-permute-start(bf16[64,4096]{1,0:T(8,128)(2,1)S(1)} %bitcast.33), channel_id=1, source_target_pairs={{1,0},{2,1},{3,2},{5,4},{6,5},{7,6},{9,8},{10,9},{11,10},{13,12},{... | collective-permute-start | bytes 1572872 | tf_op jit(solution)/shard_map/ppermute | solution.py:327
  11.4 1.2 %copy.23 = bf16[8,8,8,512]{3,1,2,0:T(8,128)(2,1)S(1)} copy(bf16[8,8,8,512]{3,2,1,0:T(8,128)(2,1)} %bitcast.39) | data formatting | bytes 1048576
  12.6 0.0 collective-permute-done.2
  12.7 1.6 %collective-permute-start.6 = (bf16[64,512]{1,0:T(8,128)(2,1)S(1)}, bf16[64,512]{1,0:T(8,128)(2,1)S(1)}, u32[]{:S(2)}, u32[]{:S(2)}) collective-permute-start(bf16[64,512]{1,0:T(8,128)(2,1)S(1)} %slice_select_fusion), channel_id=1, source_target_pairs={{0,16},{16,0},{1,17},{17,1},{2,18},{18,2},{3,19},{19,3},{4,20},{20... | collective-permute-start | bytes 196616 | tf_op jit(solution)/shard_map/ppermute | solution.py:302
  14.2 0.0 collective-permute-done
  14.2 0.6 scatter_custom_fusion
  14.9 1.2 %energy.1 = (f32[4,128]{1,0:T(4,128)S(1)}, f32[64,128]{1,0:T(8,128)S(1)}) custom-call(f32[4,4]{1,0:T(4,128)S(1)} %slice.16.sel, f32[4,9,64,128]{3,2,1,0:T(8,128)S(1)} %copy-done, f32[4,512]{1,0:T(4,128)S(1)} %slice.17.latent, f32[512,128]{1,0:T(8,128)S(1)} %copy-done.1, f32[1,128]{1,0:T(1,128)S(1)} %bitcast.36), custom_call_target="tpu_custom_call" | custom-call | flops 1000000 | bytes 1485376 | tf_op jit(solution)/shard_map/energy/pallas_call | solution.py:280
  16.1 0.6 collective-permute-start.5
  16.7 0.9 collective-permute-done.6
  17.6 2.6 %collective-permute-done.5.refs_1_ = f32[64,128]{1,0:T(8,128)S(1)} collective-permute-done((f32[64,128]{1,0:T(8,128)S(1)}, f32[64,128]{1,0:T(8,128)S(1)}, u32[]{:S(2)}, u32[]{:S(2)}) %collective-permute-start.5) | collective-permute-done | bytes 32800 | tf_op jit(solution)/shard_map/ppermute | solution.py:295
  20.2 1.8 %collective-permute-done.3.refs_1_ = bf16[64,4096]{1,0:T(8,128)(2,1)S(1)} collective-permute-done((bf16[64,4096]{1,0:T(8,128)(2,1)S(1)}, bf16[64,4096]{1,0:T(8,128)(2,1)S(1)}, u32[]{:S(2)}, u32[]{:S(2)}) %collective-permute-start.3) | collective-permute-done | bytes 524320 | tf_op jit(solution)/shard_map/ppermute | solution.py:324
  22.1 4.7 %collective-permute-done.4.refs_3_.refs_4_ = bf16[64,4096]{1,0:T(8,128)(2,1)} collective-permute-done((bf16[64,4096]{1,0:T(8,128)(2,1)S(1)}, bf16[64,4096]{1,0:T(8,128)(2,1)}, u32[]{:S(2)}, u32[]{:S(2)}) %collective-permute-start.4) | collective-permute-done | bytes 524320 | tf_op jit(solution)/shard_map/ppermute | solution.py:327
  26.8 1.4 %collective-permute-start.8 = (bf16[64,4096]{1,0:T(8,128)(2,1)S(1)}, bf16[64,4096]{1,0:T(8,128)(2,1)}, u32[]{:S(2)}, u32[]{:S(2)}) collective-permute-start(bf16[64,4096]{1,0:T(8,128)(2,1)S(1)} %collective-permute-done.3.refs_1_), channel_id=1, source_target_pairs={{1,2},{2,3},{5,6},{6,7},{9,10},{10,11},{13,14},{14,15},{17,18},{18... | collective-permute-start | bytes 1572872 | tf_op jit(solution)/shard_map/ppermute | solution.py:324
  28.3 1.3 %collective-permute-start.9 = (bf16[64,4096]{1,0:T(8,128)(2,1)}, bf16[64,4096]{1,0:T(8,128)(2,1)}, u32[]{:S(2)}, u32[]{:S(2)}) collective-permute-start(bf16[64,4096]{1,0:T(8,128)(2,1)} %collective-permute-done.4.refs_3_.refs_4_), channel_id=1, source_target_pairs={{1,0},{2,1},{5,4},{6,5},{9,8},{10,9},{13,12},{14,13},{17,16},{18,1... | collective-permute-start | bytes 1572872 | tf_op jit(solution)/shard_map/ppermute | solution.py:327
  29.5 0.1 pad_add_fusion.place
  29.6 0.7 modulated.1
  30.3 1.6 %collective-permute-start.7 = (bf16[9,64,128]{2,1,0:T(8,128)(2,1)S(1)}, bf16[9,64,128]{2,1,0:T(8,128)(2,1)S(1)}, u32[]{:S(2)}, u32[]{:S(2)}) collective-permute-start(bf16[9,64,128]{2,1,0:T(8,128)(2,1)S(1)} %get-tuple-element.63.refs_0_), channel_id=1, source_target_pairs={{0,16},{16,0},{1,17},{17,1},{2,18},{18,2},{3,19},{19,3},{4,20},{20... | collective-permute-start | bytes 442376 | tf_op jit(solution)/shard_map/ppermute | solution.py:295
  31.9 4.4 %collective-permute-done.7.refs_1_ = bf16[9,64,128]{2,1,0:T(8,128)(2,1)S(1)} collective-permute-done((bf16[9,64,128]{2,1,0:T(8,128)(2,1)S(1)}, bf16[9,64,128]{2,1,0:T(8,128)(2,1)S(1)}, u32[]{:S(2)}, u32[]{:S(2)}) %collective-permute-start.7) | collective-permute-done | bytes 147488 | tf_op jit(solution)/shard_map/ppermute | solution.py:295
  36.2 0.8 mod_blocks.1
  37.0 9.7 %collective-permute-done.9.refs_4_.refs_5_ = bf16[64,4096]{1,0:T(8,128)(2,1)} collective-permute-done((bf16[64,4096]{1,0:T(8,128)(2,1)}, bf16[64,4096]{1,0:T(8,128)(2,1)}, u32[]{:S(2)}, u32[]{:S(2)}) %collective-permute-start.9) | collective-permute-done | bytes 524320 | tf_op jit(solution)/shard_map/ppermute | solution.py:327
  46.8 0.7 collective-permute-start.10
  47.4 1.3 %collective-permute-start.11 = (bf16[64,4096]{1,0:T(8,128)(2,1)}, bf16[64,4096]{1,0:T(8,128)(2,1)S(1)}, u32[]{:S(2)}, u32[]{:S(2)}) collective-permute-start(bf16[64,4096]{1,0:T(8,128)(2,1)} %collective-permute-done.9.refs_4_.refs_5_), channel_id=1, source_target_pairs={{1,0},{5,4},{9,8},{13,12},{17,16},{21,20},{25,24},{29,28}} | collective-permute-start | bytes 1572872 | tf_op jit(solution)/shard_map/ppermute | solution.py:327
  48.7 5.2 %near_grad.1 = (bf16[256,576]{1,0:T(8,128)(2,1)S(1)}, bf16[192,5120]{1,0:T(8,128)(2,1)S(1)}) custom-call(bf16[64,4096]{1,0:T(8,128)(2,1)S(1)} %bitcast.34, bf16[64,4096]{1,0:T(8,128)(2,1)S(1)} %collective-permute-done.3.refs_1_, bf16[64,4096]{1,0:T(8,128)(2,1)} %collective-permute-done.8.refs_2_, bf16[64,4096]{1,0:T(8,128)(2,1)} %collective-permute-done.4.refs_3_.refs_4_, ...), custom_call_target="tpu_custom_call" | custom-call | flops 1207959552 | bytes 5537792 | tf_op jit(solution)/shard_map/near_grad/pallas_call | solution.py:280
  53.9 1.6 %collective-permute-start.12 = (bf16[256,576]{1,0:T(8,128)(2,1)S(1)}, bf16[256,576]{1,0:T(8,128)(2,1)S(1)}, u32[]{:S(2)}, u32[]{:S(2)}) collective-permute-start(bf16[256,576]{1,0:T(8,128)(2,1)S(1)} %get-tuple-element.83.refs_0_), channel_id=1, source_target_pairs={{0,16},{16,0},{1,17},{17,1},{2,18},{18,2},{3,19},{19,3},{4,20},{20... | collective-permute-start | bytes 884744 | tf_op jit(solution)/shard_map/ppermute | solution.py:295
  55.5 2.7 %collective-permute-start.13 = (bf16[64,576]{1,0:T(8,128)(2,1)S(1)}, bf16[64,576]{1,0:T(8,128)(2,1)S(1)}, u32[]{:S(2)}, u32[]{:S(2)}) collective-permute-start(bf16[64,576]{1,0:T(8,128)(2,1)S(1)} %get-tuple-element.77), channel_id=1, source_target_pairs={{0,1},{1,2},{2,3},{3,0},{4,5},{5,6},{6,7},{7,4},{8,9},{9,10},{10,1... | collective-permute-start | bytes 221192 | tf_op jit(solution)/shard_map/ppermute | solution.py:379
  58.2 0.0 collective-permute-start.14
  58.2 3.6 %collective-permute-done.13.refs_8_ = bf16[64,576]{1,0:T(8,128)(2,1)S(1)} collective-permute-done((bf16[64,576]{1,0:T(8,128)(2,1)S(1)}, bf16[64,576]{1,0:T(8,128)(2,1)S(1)}, u32[]{:S(2)}, u32[]{:S(2)}) %collective-permute-start.13) | collective-permute-done | bytes 73760 | tf_op jit(solution)/shard_map/ppermute | solution.py:379
  61.8 2.3 %collective-permute-start.15 = (bf16[64,576]{1,0:T(8,128)(2,1)S(1)}, bf16[64,576]{1,0:T(8,128)(2,1)S(1)}, u32[]{:S(2)}, u32[]{:S(2)}) collective-permute-start(bf16[64,576]{1,0:T(8,128)(2,1)S(1)} %get-tuple-element.79), channel_id=1, source_target_pairs={{0,3},{1,0},{2,1},{3,2},{4,7},{5,4},{6,5},{7,6},{8,11},{9,8},{10,9... | collective-permute-start | bytes 221192 | tf_op jit(solution)/shard_map/ppermute | solution.py:379
  64.1 0.8 collective-permute-done.14.refs_9_
  64.9 3.0 %collective-permute-done.15.refs_10_ = bf16[64,576]{1,0:T(8,128)(2,1)S(1)} collective-permute-done((bf16[64,576]{1,0:T(8,128)(2,1)S(1)}, bf16[64,576]{1,0:T(8,128)(2,1)S(1)}, u32[]{:S(2)}, u32[]{:S(2)}) %collective-permute-start.15) | collective-permute-done | bytes 73760 | tf_op jit(solution)/shard_map/ppermute | solution.py:379
  67.9 2.7 %far_grad.1 = (bf16[64,576]{1,0:T(8,128)(2,1)S(1)}, bf16[64,576]{1,0:T(8,128)(2,1)S(1)}, bf16[64,576]{1,0:T(8,128)(2,1)S(1)}, bf16[64,576]{1,0:T(8,128)(2,1)S(1)}, bf16[64,576]{1,0:T(8,128)(2,1)S(1)}) custom-call(bf16[64,4096]{1,0:T(8,128)(2,1)S(1)} %collective-permute-done.10.left.refs_3_, bf16[64,4096]{1,0:T(8,128)(2,1)S(1)} %collective-permute-done.11.right.refs_6_, ...), custom_call_target="tpu_custom_call" | custom-call | flops 301989888 | bytes 3973120 | tf_op jit(solution)/shard_map/far_grad/pallas_call | solution.py:280
  70.6 1.6 %collective-permute-start.16 = (bf16[64,576]{1,0:T(8,128)(2,1)S(1)}, bf16[64,576]{1,0:T(8,128)(2,1)S(1)}, u32[]{:S(2)}, u32[]{:S(2)}) collective-permute-start(bf16[64,576]{1,0:T(8,128)(2,1)S(1)} %get-tuple-element.85.refs_0_), channel_id=1, source_target_pairs={{0,16},{16,0},{1,17},{17,1},{2,18},{18,2},{3,19},{19,3},{4,20},{20... | collective-permute-start | bytes 221192 | tf_op jit(solution)/shard_map/ppermute | solution.py:295
  72.2 1.3 %collective-permute-start.18 = (bf16[64,576]{1,0:T(8,128)(2,1)S(1)}, bf16[64,576]{1,0:T(8,128)(2,1)S(1)}, u32[]{:S(2)}, u32[]{:S(2)}) collective-permute-start(bf16[64,576]{1,0:T(8,128)(2,1)S(1)} %get-tuple-element.87), channel_id=1, source_target_pairs={{1,0},{2,1},{3,2},{5,4},{6,5},{7,6},{9,8},{10,9},{11,10},{13,12},{... | collective-permute-start | bytes 221192 | tf_op jit(solution)/shard_map/ppermute | solution.py:416
  73.5 1.7 %collective-permute-start.19 = (bf16[64,576]{1,0:T(8,128)(2,1)S(1)}, bf16[64,576]{1,0:T(8,128)(2,1)S(1)}, u32[]{:S(2)}, u32[]{:S(2)}) collective-permute-start(bf16[64,576]{1,0:T(8,128)(2,1)S(1)} %get-tuple-element.88), channel_id=1, source_target_pairs={{2,0},{3,1},{0,2},{1,3},{6,4},{7,5},{4,6},{5,7},{10,8},{11,9},{8,1... | collective-permute-start | bytes 221192 | tf_op jit(solution)/shard_map/ppermute | solution.py:416
  75.2 3.6 %collective-permute-start.20 = (bf16[64,576]{1,0:T(8,128)(2,1)S(1)}, bf16[64,576]{1,0:T(8,128)(2,1)S(1)}, u32[]{:S(2)}, u32[]{:S(2)}) collective-permute-start(bf16[64,576]{1,0:T(8,128)(2,1)S(1)} %get-tuple-element.89), channel_id=1, source_target_pairs={{0,1},{1,2},{2,3},{4,5},{5,6},{6,7},{8,9},{9,10},{10,11},{12,13},{... | collective-permute-start | bytes 221192 | tf_op jit(solution)/shard_map/ppermute | solution.py:416
  78.8 3.0 %collective-permute-start.17 = (bf16[64,576]{1,0:T(8,128)(2,1)S(1)}, bf16[64,576]{1,0:T(8,128)(2,1)S(1)}, u32[]{:S(2)}, u32[]{:S(2)}) collective-permute-start(bf16[64,576]{1,0:T(8,128)(2,1)S(1)} %far_sum.1), channel_id=1, source_target_pairs={{0,3},{3,0},{4,7},{7,4},{8,11},{11,8},{12,15},{15,12},{16,19},{19,... | collective-permute-start | bytes 221192 | tf_op jit(solution)/shard_map/ppermute | solution.py:418
  81.8 5.1 %collective-permute-done.17.far = bf16[64,576]{1,0:T(8,128)(2,1)S(1)} collective-permute-done((bf16[64,576]{1,0:T(8,128)(2,1)S(1)}, bf16[64,576]{1,0:T(8,128)(2,1)S(1)}, u32[]{:S(2)}, u32[]{:S(2)}) %collective-permute-start.17) | collective-permute-done | bytes 73760 | tf_op jit(solution)/shard_map/ppermute | solution.py:418
  86.9 0.9 collect.1.refs_0_
  87.9 0.1 collective-permute-start.21
  87.9 0.3 collective-permute-start.22
  88.3 1.5 %collective-permute-start.23 = (bf16[10,64,128]{2,1,0:T(8,128)(2,1)S(1)}, bf16[10,64,128]{2,1,0:T(8,128)(2,1)S(1)}, u32[]{:S(2)}, u32[]{:S(2)}) collective-permute-start(bf16[10,64,128]{2,1,0:T(8,128)(2,1)S(1)} %collect.1.refs_0_), channel_id=1, source_target_pairs={{0,12},{4,0},{8,4},{12,8},{1,13},{5,1},{9,5},{13,9},{2,14},{6,2},{... | collective-permute-start | bytes 491528 | tf_op jit(solution)/shard_map/ppermute | solution.py:295
  89.7 5.4 %input_grad.1 = (f32[64,4096]{1,0:T(8,128)S(1)}, f32[64,512]{1,0:T(8,128)S(1)}, f32[64,512]{1,0:T(8,128)S(1)}) custom-call(bf16[64,4096]{1,0:T(8,128)(2,1)S(1)} %bitcast.35, bf16[64,4096]{1,0:T(8,128)(2,1)S(1)} %collective-permute-done.3.refs_1_, bf16[64,4096]{1,0:T(8,128)(2,1)} %collective-permute-done.8.refs_2_, ...), custom_call_target="tpu_custom_call" | custom-call | flops 1207959552 | bytes 5275648 | tf_op jit(solution)/shard_map/input_grad/pallas_call | solution.py:280
  95.1 0.6 collective-permute-done.23.refs_3_
  95.7 0.7 broadcast_select_fusion
  96.4 0.0 collective-permute-start.24
  96.4 2.8 %bank_grad.1 = (f32[4,9,64,128]{3,2,1,0:T(8,128)}, f32[4,128]{1,0:T(4,128)S(1)}) custom-call(s32[3]{0:T(128)S(1)} %pad_add_fusion.place, f32[4,4]{1,0:T(4,128)S(1)} %slice.16.sel, f32[4,9,64,128]{3,2,1,0:T(8,128)S(1)} %copy-done, f32[4,128]{1,0:T(4,128)S(1)} %get-tuple-element.58.style, f32[64,128]{1,0:T(8,128)S(1)} %get-tuple-element.62.scales, ...), custom_call_target="tpu_custom_call" | custom-call | flops 1000000 | bytes 3051596 | tf_op jit(solution)/shard_map/bank_grad/pallas_call | solution.py:280
  99.3 1.8 %collective-permute-start.26 = (f32[4,128]{1,0:T(4,128)S(1)}, f32[4,128]{1,0:T(4,128)S(1)}, u32[]{:S(2)}, u32[]{:S(2)}) collective-permute-start(f32[4,128]{1,0:T(4,128)S(1)} %get-tuple-element.109.refs_0_), channel_id=1, source_target_pairs={{0,2},{1,3},{2,0},{3,1},{4,6},{5,7},{6,4},{7,5},{8,10},{9,11},{10,... | collective-permute-start | bytes 6152 | tf_op jit(solution)/shard_map/ppermute | solution.py:295
  101.0 2.1 %collective-permute-start.27 = (f32[4,128]{1,0:T(4,128)S(1)}, f32[4,128]{1,0:T(4,128)S(1)}, u32[]{:S(2)}, u32[]{:S(2)}) collective-permute-start(f32[4,128]{1,0:T(4,128)S(1)} %get-tuple-element.109.refs_0_), channel_id=1, source_target_pairs={{0,3},{1,0},{2,1},{3,2},{4,7},{5,4},{6,5},{7,6},{8,11},{9,8},{10,9... | collective-permute-start | bytes 6152 | tf_op jit(solution)/shard_map/ppermute | solution.py:295
  103.1 0.1 pad.1.clone
  103.2 0.1 copy.21
  103.3 0.6 copy.24
  103.9 0.7 collective-permute-done.25.refs_1_
  104.6 0.6 collective-permute-done.27.refs_3_
  105.2 1.6 %affine.1 = (f32[512,128]{1,0:T(8,128)}, f32[1,128]{1,0:T(1,128)}) custom-call(s32[3]{0:T(128)S(1)} %pad_add_fusion.place, f32[512,4]{1,0:T(8,128)S(1)} %bitcast.29, f32[4,128]{1,0:T(4,128)S(1)} %get-tuple-element.109.refs_0_, f32[4,128]{1,0:T(4,128)S(1)} %collective-permute-done.25.refs_1_, f32[4,128]{1,0:T(4,128)S(1)} %collective-permute-done.26.refs_2_, ...), custom_call_target="tpu_custom_call" | custom-call | flops 1000000 | bytes 279052 | tf_op jit(solution)/shard_map/affine/pallas_call | solution.py:280
  106.8 0.1 copy.20
  107.0 0.1 copy.19
  107.1 1.1 %fusion = bf16[1,64,8,512]{3,2,1,0:T(8,128)(2,1)} fusion(f32[1,64,1,512]{3,2,1,0:T(1,128)S(1)} %copy.20, f32[1,64,1,512]{3,2,1,0:T(1,128)S(1)} %copy.19, f32[8]{0:T(128)S(1)} %pad.1.clone, f32[1,64,8,512]{3,2,1,0:T(8,128)S(1)} %bitcast.37), kind=kLoop, calls=%fused_computation.2 | loop fusion | flops 1048576 | bytes 1835040 | tf_op jit(solution)/shard_map/convert_element_type | solution.py:455
  (29 shorter events, 0.1 us)
Async XLA Ops:
  2.0 10.7 %collective-permute-start.2 = (f32[1,516]{1,0:T(1,128)S(1)}, f32[1,516]{1,0:T(1,128)S(1)}, u32[]{:S(2)}, u32[]{:S(2)}) collective-permute-start(f32[1,516]{1,0:T(1,128)S(1)} %broadcast_in_dim.23), channel_id=1, source_target_pairs={{0,12},{4,0},{8,4},{12,8},{1,13},{5,1},{9,5},{13,9},{2,14},{6,2},{... | collective-permute-start | bytes 6200 | tf_op jit(solution)/shard_map/ppermute | solution.py:295
  4.4 9.8 %collective-permute-start.1 = (f32[1,516]{1,0:T(1,128)S(1)}, f32[1,516]{1,0:T(1,128)S(1)}, u32[]{:S(2)}, u32[]{:S(2)}) collective-permute-start(f32[1,516]{1,0:T(1,128)S(1)} %broadcast_in_dim.23), channel_id=1, source_target_pairs={{0,8},{4,12},{8,0},{12,4},{1,9},{5,13},{9,1},{13,5},{2,10},{6,14},... | collective-permute-start | bytes 6200 | tf_op jit(solution)/shard_map/ppermute | solution.py:295
  5.1 9.2 %collective-permute-start = (f32[1,516]{1,0:T(1,128)S(1)}, f32[1,516]{1,0:T(1,128)S(1)}, u32[]{:S(2)}, u32[]{:S(2)}) collective-permute-start(f32[1,516]{1,0:T(1,128)S(1)} %broadcast_in_dim.23), channel_id=1, source_target_pairs={{0,4},{4,8},{8,12},{12,0},{1,5},{5,9},{9,13},{13,1},{2,6},{6,10},{... | collective-permute-start | bytes 6200 | tf_op jit(solution)/shard_map/ppermute | solution.py:295
  5.2 9.7 %copy-start = (f32[4,9,64,128]{3,2,1,0:T(8,128)S(1)}, f32[4,9,64,128]{3,2,1,0:T(8,128)}, u32[]{:S(2)}) copy-start(f32[4,9,64,128]{3,2,1,0:T(8,128)} %bank.5) | copy-start | bytes 3538948
  5.2 9.7 %copy-start.1 = (f32[512,128]{1,0:T(8,128)S(1)}, f32[512,128]{1,0:T(8,128)}, u32[]{:S(2)}) copy-start(f32[512,128]{1,0:T(8,128)} %affine_w.1) | copy-start | bytes 786436
  5.2 9.7 %copy-start.2 = (f32[128]{0:T(128)S(1)}, f32[128]{0:T(128)}, u32[]{:S(2)}) copy-start(f32[128]{0:T(128)} %param.13) | copy-start | bytes 1540
  6.6 15.5 %collective-permute-start.3 = (bf16[64,4096]{1,0:T(8,128)(2,1)S(1)}, bf16[64,4096]{1,0:T(8,128)(2,1)S(1)}, u32[]{:S(2)}, u32[]{:S(2)}) collective-permute-start(bf16[64,4096]{1,0:T(8,128)(2,1)S(1)} %bitcast.32), channel_id=1, source_target_pairs={{0,1},{1,2},{2,3},{4,5},{5,6},{6,7},{8,9},{9,10},{10,11},{12,13},{... | collective-permute-start | bytes 1572872 | tf_op jit(solution)/shard_map/ppermute | solution.py:324
  10.1 16.7 %collective-permute-start.4 = (bf16[64,4096]{1,0:T(8,128)(2,1)S(1)}, bf16[64,4096]{1,0:T(8,128)(2,1)}, u32[]{:S(2)}, u32[]{:S(2)}) collective-permute-start(bf16[64,4096]{1,0:T(8,128)(2,1)S(1)} %bitcast.33), channel_id=1, source_target_pairs={{1,0},{2,1},{3,2},{5,4},{6,5},{7,6},{9,8},{10,9},{11,10},{13,12},{... | collective-permute-start | bytes 1572872 | tf_op jit(solution)/shard_map/ppermute | solution.py:327
  12.7 4.9 %collective-permute-start.6 = (bf16[64,512]{1,0:T(8,128)(2,1)S(1)}, bf16[64,512]{1,0:T(8,128)(2,1)S(1)}, u32[]{:S(2)}, u32[]{:S(2)}) collective-permute-start(bf16[64,512]{1,0:T(8,128)(2,1)S(1)} %slice_select_fusion), channel_id=1, source_target_pairs={{0,16},{16,0},{1,17},{17,1},{2,18},{18,2},{3,19},{19,3},{4,20},{20... | collective-permute-start | bytes 196616 | tf_op jit(solution)/shard_map/ppermute | solution.py:302
  16.1 4.1 %collective-permute-start.5 = (f32[64,128]{1,0:T(8,128)S(1)}, f32[64,128]{1,0:T(8,128)S(1)}, u32[]{:S(2)}, u32[]{:S(2)}) collective-permute-start(f32[64,128]{1,0:T(8,128)S(1)} %get-tuple-element.60.refs_0_), channel_id=1, source_target_pairs={{0,16},{16,0},{1,17},{17,1},{2,18},{18,2},{3,19},{19,3},{4,20},{20... | collective-permute-start | bytes 98312 | tf_op jit(solution)/shard_map/ppermute | solution.py:295
  26.8 10.2 %collective-permute-start.8 = (bf16[64,4096]{1,0:T(8,128)(2,1)S(1)}, bf16[64,4096]{1,0:T(8,128)(2,1)}, u32[]{:S(2)}, u32[]{:S(2)}) collective-permute-start(bf16[64,4096]{1,0:T(8,128)(2,1)S(1)} %collective-permute-done.3.refs_1_), channel_id=1, source_target_pairs={{1,2},{2,3},{5,6},{6,7},{9,10},{10,11},{13,14},{14,15},{17,18},{18... | collective-permute-start | bytes 1572872 | tf_op jit(solution)/shard_map/ppermute | solution.py:324
  28.3 18.5 %collective-permute-start.9 = (bf16[64,4096]{1,0:T(8,128)(2,1)}, bf16[64,4096]{1,0:T(8,128)(2,1)}, u32[]{:S(2)}, u32[]{:S(2)}) collective-permute-start(bf16[64,4096]{1,0:T(8,128)(2,1)} %collective-permute-done.4.refs_3_.refs_4_), channel_id=1, source_target_pairs={{1,0},{2,1},{5,4},{6,5},{9,8},{10,9},{13,12},{14,13},{17,16},{18,1... | collective-permute-start | bytes 1572872 | tf_op jit(solution)/shard_map/ppermute | solution.py:327
  30.3 5.9 %collective-permute-start.7 = (bf16[9,64,128]{2,1,0:T(8,128)(2,1)S(1)}, bf16[9,64,128]{2,1,0:T(8,128)(2,1)S(1)}, u32[]{:S(2)}, u32[]{:S(2)}) collective-permute-start(bf16[9,64,128]{2,1,0:T(8,128)(2,1)S(1)} %get-tuple-element.63.refs_0_), channel_id=1, source_target_pairs={{0,16},{16,0},{1,17},{17,1},{2,18},{18,2},{3,19},{19,3},{4,20},{20... | collective-permute-start | bytes 442376 | tf_op jit(solution)/shard_map/ppermute | solution.py:295
  46.8 21.2 %collective-permute-start.10 = (bf16[64,4096]{1,0:T(8,128)(2,1)}, bf16[64,4096]{1,0:T(8,128)(2,1)S(1)}, u32[]{:S(2)}, u32[]{:S(2)}) collective-permute-start(bf16[64,4096]{1,0:T(8,128)(2,1)} %collective-permute-done.8.refs_2_), channel_id=1, source_target_pairs={{2,3},{6,7},{10,11},{14,15},{18,19},{22,23},{26,27},{30,31}} | collective-permute-start | bytes 1572872 | tf_op jit(solution)/shard_map/ppermute | solution.py:324
  47.4 20.5 %collective-permute-start.11 = (bf16[64,4096]{1,0:T(8,128)(2,1)}, bf16[64,4096]{1,0:T(8,128)(2,1)S(1)}, u32[]{:S(2)}, u32[]{:S(2)}) collective-permute-start(bf16[64,4096]{1,0:T(8,128)(2,1)} %collective-permute-done.9.refs_4_.refs_5_), channel_id=1, source_target_pairs={{1,0},{5,4},{9,8},{13,12},{17,16},{21,20},{25,24},{29,28}} | collective-permute-start | bytes 1572872 | tf_op jit(solution)/shard_map/ppermute | solution.py:327
  53.9 14.0 %collective-permute-start.12 = (bf16[256,576]{1,0:T(8,128)(2,1)S(1)}, bf16[256,576]{1,0:T(8,128)(2,1)S(1)}, u32[]{:S(2)}, u32[]{:S(2)}) collective-permute-start(bf16[256,576]{1,0:T(8,128)(2,1)S(1)} %get-tuple-element.83.refs_0_), channel_id=1, source_target_pairs={{0,16},{16,0},{1,17},{17,1},{2,18},{18,2},{3,19},{19,3},{4,20},{20... | collective-permute-start | bytes 884744 | tf_op jit(solution)/shard_map/ppermute | solution.py:295
  55.5 6.3 %collective-permute-start.13 = (bf16[64,576]{1,0:T(8,128)(2,1)S(1)}, bf16[64,576]{1,0:T(8,128)(2,1)S(1)}, u32[]{:S(2)}, u32[]{:S(2)}) collective-permute-start(bf16[64,576]{1,0:T(8,128)(2,1)S(1)} %get-tuple-element.77), channel_id=1, source_target_pairs={{0,1},{1,2},{2,3},{3,0},{4,5},{5,6},{6,7},{7,4},{8,9},{9,10},{10,1... | collective-permute-start | bytes 221192 | tf_op jit(solution)/shard_map/ppermute | solution.py:379
  58.2 6.7 %collective-permute-start.14 = (bf16[64,576]{1,0:T(8,128)(2,1)S(1)}, bf16[64,576]{1,0:T(8,128)(2,1)S(1)}, u32[]{:S(2)}, u32[]{:S(2)}) collective-permute-start(bf16[64,576]{1,0:T(8,128)(2,1)S(1)} %get-tuple-element.78), channel_id=1, source_target_pairs={{0,2},{1,3},{2,0},{3,1},{4,6},{5,7},{6,4},{7,5},{8,10},{9,11},{10,... | collective-permute-start | bytes 221192 | tf_op jit(solution)/shard_map/ppermute | solution.py:379
  61.8 6.1 %collective-permute-start.15 = (bf16[64,576]{1,0:T(8,128)(2,1)S(1)}, bf16[64,576]{1,0:T(8,128)(2,1)S(1)}, u32[]{:S(2)}, u32[]{:S(2)}) collective-permute-start(bf16[64,576]{1,0:T(8,128)(2,1)S(1)} %get-tuple-element.79), channel_id=1, source_target_pairs={{0,3},{1,0},{2,1},{3,2},{4,7},{5,4},{6,5},{7,6},{8,11},{9,8},{10,9... | collective-permute-start | bytes 221192 | tf_op jit(solution)/shard_map/ppermute | solution.py:379
  70.6 8.1 %collective-permute-start.16 = (bf16[64,576]{1,0:T(8,128)(2,1)S(1)}, bf16[64,576]{1,0:T(8,128)(2,1)S(1)}, u32[]{:S(2)}, u32[]{:S(2)}) collective-permute-start(bf16[64,576]{1,0:T(8,128)(2,1)S(1)} %get-tuple-element.85.refs_0_), channel_id=1, source_target_pairs={{0,16},{16,0},{1,17},{17,1},{2,18},{18,2},{3,19},{19,3},{4,20},{20... | collective-permute-start | bytes 221192 | tf_op jit(solution)/shard_map/ppermute | solution.py:295
  72.2 9.6 %collective-permute-start.18 = (bf16[64,576]{1,0:T(8,128)(2,1)S(1)}, bf16[64,576]{1,0:T(8,128)(2,1)S(1)}, u32[]{:S(2)}, u32[]{:S(2)}) collective-permute-start(bf16[64,576]{1,0:T(8,128)(2,1)S(1)} %get-tuple-element.87), channel_id=1, source_target_pairs={{1,0},{2,1},{3,2},{5,4},{6,5},{7,6},{9,8},{10,9},{11,10},{13,12},{... | collective-permute-start | bytes 221192 | tf_op jit(solution)/shard_map/ppermute | solution.py:416
  73.5 8.3 %collective-permute-start.19 = (bf16[64,576]{1,0:T(8,128)(2,1)S(1)}, bf16[64,576]{1,0:T(8,128)(2,1)S(1)}, u32[]{:S(2)}, u32[]{:S(2)}) collective-permute-start(bf16[64,576]{1,0:T(8,128)(2,1)S(1)} %get-tuple-element.88), channel_id=1, source_target_pairs={{2,0},{3,1},{0,2},{1,3},{6,4},{7,5},{4,6},{5,7},{10,8},{11,9},{8,1... | collective-permute-start | bytes 221192 | tf_op jit(solution)/shard_map/ppermute | solution.py:416
  75.2 6.7 %collective-permute-start.20 = (bf16[64,576]{1,0:T(8,128)(2,1)S(1)}, bf16[64,576]{1,0:T(8,128)(2,1)S(1)}, u32[]{:S(2)}, u32[]{:S(2)}) collective-permute-start(bf16[64,576]{1,0:T(8,128)(2,1)S(1)} %get-tuple-element.89), channel_id=1, source_target_pairs={{0,1},{1,2},{2,3},{4,5},{5,6},{6,7},{8,9},{9,10},{10,11},{12,13},{... | collective-permute-start | bytes 221192 | tf_op jit(solution)/shard_map/ppermute | solution.py:416
  78.8 8.1 %collective-permute-start.17 = (bf16[64,576]{1,0:T(8,128)(2,1)S(1)}, bf16[64,576]{1,0:T(8,128)(2,1)S(1)}, u32[]{:S(2)}, u32[]{:S(2)}) collective-permute-start(bf16[64,576]{1,0:T(8,128)(2,1)S(1)} %far_sum.1), channel_id=1, source_target_pairs={{0,3},{3,0},{4,7},{7,4},{8,11},{11,8},{12,15},{15,12},{16,19},{19,... | collective-permute-start | bytes 221192 | tf_op jit(solution)/shard_map/ppermute | solution.py:418
  87.9 7.3 %collective-permute-start.21 = (bf16[10,64,128]{2,1,0:T(8,128)(2,1)S(1)}, bf16[10,64,128]{2,1,0:T(8,128)(2,1)S(1)}, u32[]{:S(2)}, u32[]{:S(2)}) collective-permute-start(bf16[10,64,128]{2,1,0:T(8,128)(2,1)S(1)} %collect.1.refs_0_), channel_id=1, source_target_pairs={{0,4},{4,8},{8,12},{12,0},{1,5},{5,9},{9,13},{13,1},{2,6},{6,10},{... | collective-permute-start | bytes 491528 | tf_op jit(solution)/shard_map/ppermute | solution.py:295
  87.9 7.2 %collective-permute-start.22 = (bf16[10,64,128]{2,1,0:T(8,128)(2,1)S(1)}, bf16[10,64,128]{2,1,0:T(8,128)(2,1)S(1)}, u32[]{:S(2)}, u32[]{:S(2)}) collective-permute-start(bf16[10,64,128]{2,1,0:T(8,128)(2,1)S(1)} %collect.1.refs_0_), channel_id=1, source_target_pairs={{0,8},{4,12},{8,0},{12,4},{1,9},{5,13},{9,1},{13,5},{2,10},{6,14},... | collective-permute-start | bytes 491528 | tf_op jit(solution)/shard_map/ppermute | solution.py:295
  88.3 7.5 %collective-permute-start.23 = (bf16[10,64,128]{2,1,0:T(8,128)(2,1)S(1)}, bf16[10,64,128]{2,1,0:T(8,128)(2,1)S(1)}, u32[]{:S(2)}, u32[]{:S(2)}) collective-permute-start(bf16[10,64,128]{2,1,0:T(8,128)(2,1)S(1)} %collect.1.refs_0_), channel_id=1, source_target_pairs={{0,12},{4,0},{8,4},{12,8},{1,13},{5,1},{9,5},{13,9},{2,14},{6,2},{... | collective-permute-start | bytes 491528 | tf_op jit(solution)/shard_map/ppermute | solution.py:295
  96.4 10.4 %collective-permute-start.24 = (f32[64,512]{1,0:T(8,128)}, f32[64,512]{1,0:T(8,128)S(1)}, u32[]{:S(2)}, u32[]{:S(2)}) collective-permute-start(f32[64,512]{1,0:T(8,128)} %broadcast_select_fusion), channel_id=1, source_target_pairs={{0,16},{16,0},{1,17},{17,1},{2,18},{18,2},{3,19},{19,3},{4,20},{20... | collective-permute-start | bytes 393224 | tf_op jit(solution)/shard_map/ppermute | solution.py:302
  99.2 5.4 %collective-permute-start.25 = (f32[4,128]{1,0:T(4,128)S(1)}, f32[4,128]{1,0:T(4,128)S(1)}, u32[]{:S(2)}, u32[]{:S(2)}) collective-permute-start(f32[4,128]{1,0:T(4,128)S(1)} %get-tuple-element.109.refs_0_), channel_id=1, source_target_pairs={{0,1},{1,2},{2,3},{3,0},{4,5},{5,6},{6,7},{7,4},{8,9},{9,10},{10,1... | collective-permute-start | bytes 6152 | tf_op jit(solution)/shard_map/ppermute | solution.py:295
  99.3 5.4 %collective-permute-start.26 = (f32[4,128]{1,0:T(4,128)S(1)}, f32[4,128]{1,0:T(4,128)S(1)}, u32[]{:S(2)}, u32[]{:S(2)}) collective-permute-start(f32[4,128]{1,0:T(4,128)S(1)} %get-tuple-element.109.refs_0_), channel_id=1, source_target_pairs={{0,2},{1,3},{2,0},{3,1},{4,6},{5,7},{6,4},{7,5},{8,10},{9,11},{10,... | collective-permute-start | bytes 6152 | tf_op jit(solution)/shard_map/ppermute | solution.py:295
  101.0 4.2 %collective-permute-start.27 = (f32[4,128]{1,0:T(4,128)S(1)}, f32[4,128]{1,0:T(4,128)S(1)}, u32[]{:S(2)}, u32[]{:S(2)}) collective-permute-start(f32[4,128]{1,0:T(4,128)S(1)} %get-tuple-element.109.refs_0_), channel_id=1, source_target_pairs={{0,3},{1,0},{2,1},{3,2},{4,7},{5,4},{6,5},{7,6},{8,11},{9,8},{10,9... | collective-permute-start | bytes 6152 | tf_op jit(solution)/shard_map/ppermute | solution.py:295

commit v3 on v2

--- a/solution.py
+++ b/solution.py
@@ -30,11 +30,6 @@
     return pl.CostEstimate(flops=flops, bytes_accessed=moved, transcendentals=0)
 
 
-def column(table, index):
-    lane = lax.broadcasted_iota(jnp.int32, table.shape, 1)
-    return jnp.sum(jnp.where(lane == index, table, 0.0), axis=1, keepdims=True)
-
-
 def beside(pieces):
     return pieces[0] if len(pieces) == 1 else jnp.concatenate(pieces, axis=1)
 
@@ -47,43 +42,35 @@
 
 
 def energy_kernel(sel, bank, latent, affine_w, affine_b, style_out, energy_out):
-    samples = latent.shape[0]
     style = (
         jnp.dot(latent[...], affine_w[...], precision=lax.Precision.HIGHEST, preferred_element_type=F32)
         + affine_b[...]
     )
     style_out[...] = style
-    out_ch, in_ch = bank.shape[2], bank.shape[3]
-    totals = [jnp.zeros((out_ch, in_ch), F32) for _ in range(samples)]
+    total = jnp.zeros(bank.shape[2:], F32)
     for tap in range(TAPS):
-        for b in range(samples):
-            plain = mixed(bank, sel, b, tap) * style[b : b + 1]
-            totals[b] = totals[b] + plain * plain
-    lane = lax.broadcasted_iota(jnp.int32, (out_ch, 128), 1)
-    table = jnp.zeros((out_ch, 128), F32)
-    for b in range(samples):
-        table = jnp.where(lane == b, jnp.sum(totals[b], axis=1, keepdims=True), table)
-    energy_out[...] = table
-
-
-def modulated_kernel(rows, place, sel, bank, style, *refs):
-    energies, (mod_out, scale_out) = refs[:rows], refs[rows:]
-    sample = place[0]
+        plain = mixed(bank, sel, 0, tap) * style
+        total = total + plain * plain
+    energy_out[...] = jnp.broadcast_to(jnp.sum(total, axis=1, keepdims=True), energy_out.shape)
+
+
+def modulated_kernel(sel, bank, style, *refs):
+    energies, (mod_out, scale_out, row_out) = refs[:-3], refs[-3:]
     energy = energies[0][...]
-    for r in range(1, rows):
-        energy = energy + energies[r][...]
+    for other in energies[1:]:
+        energy = energy + other[...]
     scales = lax.rsqrt(energy + EPS)
     scale_out[...] = scales
-    scale = column(scales, sample)
-    own_style = style[pl.ds(sample, 1), :]
+    row_out[...] = scales.T[0:1]
+    scale = scales[:, 0:1]
     for tap in range(TAPS):
-        mod_out[tap] = (mixed(bank, sel, sample, tap) * own_style * scale).astype(BF16)
+        mod_out[tap] = (mixed(bank, sel, 0, tap) * style[...] * scale).astype(BF16)
 
 
 def blocks_kernel(rows, size, place, *refs):
     parts, whole, outs = refs[:rows], refs[rows], refs[rows + 1 : rows + 1 + size]
     by_row, by_chan = refs[rows + 1 + size :]
-    row_at, chan_at = place[2], place[1]
+    row_at, chan_at, sign = place[2], place[1], place[3]
     for r in range(rows):
         by_row[lax.rem(row_at - r + rows, rows)] = parts[r][...]
     ch = whole.shape[2] // size
@@ -95,7 +82,7 @@
     for z in range(size):
         by_chan[z] = beside([value[:, z * ch : (z + 1) * ch] for value in taps]).astype(BF16)
     for d in range(size):
-        outs[d][...] = by_chan[lax.rem(chan_at + d, size)]
+        outs[d][...] = by_chan[lax.rem(chan_at + sign * d + size, size)]
 
 
 def shifted(x, by):
@@ -120,16 +107,16 @@
 
 
 def near_grad_kernel(size, height, width, *refs):
-    cotan_own, left, right = refs[0], refs[1 : size - 1], refs[size - 1 : 2 * size - 3]
+    cotan_own, first, second = refs[0], refs[1 : size - 1], refs[size - 1 : 2 * size - 3]
     feat, feat_before, feat_after, out, wide, gathered, total = refs[2 * size - 3 :]
     ch = feat.shape[0]
     gathered[0:ch] = cotan_own[...]
     for d in range(1, size):
         found = []
         if d < size - 1:
-            found.append(left[d - 1][...])
+            found.append(first[d - 1][...])
         if size - d < size - 1:
-            found.append(right[size - d - 1][...])
+            found.append(second[size - d - 1][...])
         gathered[d * ch : (d + 1) * ch] = found[0] if len(found) == 1 else found[0] + found[1]
     for row in range(height + 2):
         if row == 0:
@@ -145,12 +132,14 @@
     out[...] = tap_products(gathered, wide, total, height, width).astype(BF16)
 
 
-def far_grad_kernel(rows, size, height, width, left, right, wide, *refs):
-    nears, far_out, outs = refs[:rows], refs[rows], refs[rows + 1 : rows + 1 + size]
-    cotan, total = refs[rows + 1 + size :]
-    cotan[...] = left[...] + right[...]
-    far_out[...] = tap_products(cotan, wide, total, height, width).astype(BF16)
-    ch = cotan.shape[0]
+def far_grad_kernel(height, width, first, second, wide, out, cotan, total):
+    cotan[...] = first[...] + second[...]
+    out[...] = tap_products(cotan, wide, total, height, width).astype(BF16)
+
+
+def near_sum_kernel(rows, size, *refs):
+    nears, outs = refs[:rows], refs[rows:]
+    ch = outs[0].shape[0]
     for d in range(size):
         value = nears[0][d * ch : (d + 1) * ch].astype(F32)
         for r in range(1, rows):
@@ -166,13 +155,13 @@
 
 
 def input_grad_kernel(size, height, width, *refs):
-    cotan_own, left, right = refs[0], refs[1:size], refs[size : 2 * size - 1]
+    cotan_own, first, second = refs[0], refs[1:size], refs[size : 2 * size - 1]
     mods = refs[2 * size - 1 : 3 * size - 1]
     main, before, after, gathered, taps_t, total = refs[3 * size - 1 :]
     ch = cotan_own.shape[0]
     gathered[0:ch] = cotan_own[...]
     for d in range(1, size):
-        gathered[d * ch : (d + 1) * ch] = left[d - 1][...] + right[size - d - 1][...]
+        gathered[d * ch : (d + 1) * ch] = first[d - 1][...] + second[size - d - 1][...]
     every = jnp.concatenate([mod[...].astype(F32) for mod in mods], axis=0)
     taps_t[...] = every.T.astype(BF16)
     total[...] = jnp.zeros(total.shape, F32)
@@ -202,11 +191,11 @@
     return high, mid, x - high - mid
 
 
-def collect_kernel(rows, size, place, scales, whole_mod, far, *refs):
+def collect_kernel(rows, size, place, scale, whole_mod, far, *refs):
     nears, out, by_chan, by_row = refs[:size], refs[size], refs[size + 1], refs[size + 2]
-    sample, chan_at, row_at = place[0], place[1], place[2]
+    chan_at, row_at, sign = place[1], place[2], place[3]
     for d in range(size):
-        by_chan[lax.rem(chan_at + d, size)] = nears[d][...].astype(F32)
+        by_chan[lax.rem(chan_at + sign * d + size, size)] = nears[d][...].astype(F32)
     by_chan[jnp.where(chan_at == 0, size - 1, 0)] += far[...].astype(F32)
     ch = whole_mod.shape[2] // size
     in_ch = out.shape[2]
@@ -217,8 +206,7 @@
         for r in range(rows):
             by_row[r, tap] = value[:, r * in_ch : (r + 1) * in_ch].astype(BF16)
     out[0:TAPS] = by_row[row_at]
-    scale = column(scales[...], sample)
-    fall = jnp.sum(product, axis=1, keepdims=True) * (scale * scale)
+    fall = jnp.sum(product, axis=1, keepdims=True) * (scale[:, 0:1] * scale[:, 0:1])
     lane = lax.broadcasted_iota(jnp.int32, out.shape[1:], 1)
     last = jnp.zeros(out.shape[1:], F32)
     for at, piece in enumerate(split3(fall)):
@@ -313,56 +301,51 @@
     _, ch, height, width = feature.shape
     out_ch, in_ch = bank.shape[2:]
     pixels, all_ch = height * width, ch * size
-    place = jnp.stack([sample_at, chan_at, row_at]).astype(jnp.int32)
+    sign = 1 - 2 * jnp.remainder(sample_at, 2)
+    place = jnp.stack([sample_at, chan_at, row_at, sign]).astype(jnp.int32)
     flops = 2 * TAPS * ch * ch * size * pixels
 
+    def along(x, pairs):
+        whole = []
+        for b in range(samples):
+            for i, j in pairs:
+                if b % 2:
+                    i, j = size - 1 - i, size - 1 - j
+                whole.append((b * size + i, b * size + j))
+        return lax.ppermute(x, ("samples", "chan"), whole)
+
     cotan = out_grad[0].reshape(ch, pixels)
-    left, right = [], []
-
-    def step(number, from_left, from_right):
-        left.append(
-            lax.ppermute(from_left, "chan", [(i, i + 1) for i in range(number - 1, size - 1)])
-        )
-        right.append(
-            lax.ppermute(from_right, "chan", [(i + 1, i) for i in range(size - number)])
-        )
+    first, second = [], []
+
+    def step(number, x, y):
+        first.append(along(x, [(i, i + 1) for i in range(number - 1, size - 1)]))
+        second.append(along(y, [(i + 1, i) for i in range(size - number)]))
 
     step(1, cotan, cotan)
 
     feat = feature[0].reshape(ch, pixels)
     feat_before, feat_after = from_sides(feat[:, :width], feat[:, pixels - width :], "rows")
-    small = jnp.concatenate([latent[0], select[0].astype(F32)])[None]
-    small = exchange(small, "samples")
-    at = jnp.remainder(sample_at - jnp.arange(samples), samples)
-    small = jnp.zeros((samples, small[0].shape[1]), F32).at[at].set(jnp.concatenate(small, axis=0))
-    latents, sel = small[:, : latent.shape[1]], small[:, latent.shape[1] :]
+    own_sel = select.astype(F32)
     style, energy = call(
         energy_kernel,
         "energy",
-        [((samples, in_ch), F32), ((out_ch, 128), F32)],
-        sel,
+        [((1, in_ch), F32), ((out_ch, 128), F32)],
+        own_sel,
         bank,
-        latents,
+        latent,
         affine_w,
         affine_b[None],
         scalars=1,
     )
-    energies = exchange(energy, "rows")
-    left[0], right[0], energies, feat_before, feat_after = lax.optimization_barrier(
-        (left[0], right[0], energies, feat_before, feat_after)
-    )
-
-    step(2, left[0], right[0])
-    mod_own, scales = call(
-        functools.partial(modulated_kernel, rows),
+    mod_own, scale, scale_row = call(
+        modulated_kernel,
         "modulated",
-        [((TAPS, out_ch, in_ch), BF16), ((out_ch, 128), F32)],
-        place,
-        sel,
+        [((TAPS, out_ch, in_ch), BF16), ((out_ch, 128), F32), ((1, out_ch), F32)],
+        own_sel,
         bank,
         style,
-        *energies,
-        scalars=2,
+        *exchange(energy, "rows"),
+        scalars=1,
     )
     message = ((ch, TAPS * ch), BF16)
     whole_mod, *to_send = call(
@@ -374,47 +357,64 @@
         scalars=1,
         scratch=[((rows, TAPS, out_ch, in_ch), BF16), ((size, *message[0]), BF16)],
     )
-    left[1], right[1], to_send = lax.optimization_barrier((left[1], right[1], to_send))
+    first[0], second[0], to_send, feat_before, feat_after = lax.optimization_barrier(
+        (first[0], second[0], to_send, feat_before, feat_after)
+    )
+
+    step(2, first[0], second[0])
     mods = [to_send[0]] + [
-        lax.ppermute(to_send[d], "chan", [(i, (i + d) % size) for i in range(size)])
-        for d in range(1, size)
+        along(to_send[d], [(i, (i + d) % size) for i in range(size)]) for d in range(1, size)
     ]
+    small = jnp.concatenate([latent[0], own_sel[0], style[0], scale_row[0]])[None]
+    smalls = exchange(small, "samples")
+    first[1], second[1], mods, smalls = lax.optimization_barrier((first[1], second[1], mods, smalls))
+    at = jnp.remainder(sample_at - jnp.arange(samples), samples)
+    every = jnp.zeros((samples, small.shape[1]), F32).at[at].set(jnp.concatenate(smalls, axis=0))
+    ends = [latent.shape[1], latent.shape[1] + select.shape[1]]
+    latents, sel, styles, scales = jnp.split(every, ends + [ends[1] + in_ch], axis=1)
+    tables = latents.T, sel, styles, scales.T
 
     for number in range(3, size):
-        step(number, left[number - 2], right[number - 2])
+        step(number, first[number - 2], second[number - 2])
     near, wide = call(
         functools.partial(near_grad_kernel, size, height, width),
         "near_grad",
         [((all_ch, TAPS * ch), BF16), ((3 * ch, (height + 2) * width), BF16)],
         cotan,
-        *left[: size - 2],
-        *right[: size - 2],
+        *first[: size - 2],
+        *second[: size - 2],
         feat,
         feat_before,
         feat_after,
         scratch=[((all_ch, pixels), BF16), ((3, all_ch, 3 * ch), F32)],
         flops=flops,
     )
-    nears = exchange(near, "rows")
-    left[-1], right[-1], nears, mods = lax.optimization_barrier((left[-1], right[-1], nears, mods))
-    far, *near_sums = call(
-        functools.partial(far_grad_kernel, rows, size, height, width),
-        "far_grad",
-        [message] * (1 + size),
-        left[-1],
-        right[-1],
-        wide,
-        *nears,
-        scratch=[((ch, pixels), BF16), ((3, ch, 3 * ch), F32)],
-        flops=flops // size,
-    )
-    fars = exchange(far, "rows")
+    near_sums = call(
+        functools.partial(near_sum_kernel, rows, size),
+        "near_sum",
+        [message] * size,
+        *exchange(near, "rows"),
+    )
     got = [near_sums[0]]
     for d in range(1, size):
         pairs = [(i, i - d) for i in range(d, size) if d < size - 1]
         pairs += [(i, i - d + size) for i in range(d) if size - d < size - 1]
-        got.append(lax.ppermute(near_sums[d], "chan", pairs))
-    (far_sum,) = call(sum_kernel, "far_sum", [message], *fars)
+        got.append(along(near_sums[d], pairs))
+    first[-1], second[-1], near_sums, tables = lax.optimization_barrier(
+        (first[-1], second[-1], near_sums, tables)
+    )
+    latents, sel, styles, scales = tables
+    (far,) = call(
+        functools.partial(far_grad_kernel, height, width),
+        "far_grad",
+        [message],
+        first[-1],
+        second[-1],
+        wide,
+        scratch=[((ch, pixels), BF16), ((3, ch, 3 * ch), F32)],
+        flops=flops // size,
+    )
+    (far_sum,) = call(sum_kernel, "far_sum", [message], *exchange(far, "rows"))
     far_got = lax.ppermute(far_sum, "chan", [(0, size - 1), (size - 1, 0)])
 
     (own,) = call(
@@ -422,7 +422,7 @@
         "collect",
         [((TAPS + 1, out_ch, in_ch), BF16)],
         place,
-        scales,
+        scale,
         whole_mod,
         far_got,
         *got,
@@ -437,8 +437,8 @@
         "input_grad",
         [((ch, pixels), F32), ((ch, width), F32), ((ch, width), F32)],
         cotan,
-        *left,
-        *right,
+        *first,
+        *second,
         *mods,
         scratch=[
             ((all_ch, pixels), BF16),
@@ -461,7 +461,7 @@
         place,
         sel,
         bank,
-        style,
+        styles,
         scales,
         *every,
         scalars=2,
@@ -472,7 +472,7 @@
         "affine",
         [(affine_w.shape, F32), ((1, in_ch), F32)],
         place,
-        latents.T,
+        latents,
         *exchange(style_part, "chan"),
         scalars=1,
         scratch=[((size, samples, in_ch), F32)],

time: 109 us -> 120 us (1.10)
  waiting for transfers between devices: 38.7 us -> 23.2 us
  starting transfers between devices: 39.7 us -> 54.7 us
  local copies, waits for them, and re-layouts: 3.67 us -> 13.8 us
  Pallas kernels: 21.3 us -> 24.3 us
  other arithmetic: 3.92 us -> 2.66 us
    ppermute x12, waiting for transfers between devices: 23.8 us -> 5.71 us  [along(): return lax.ppermute(x, ('samples', 'chan'), whole)]
    ppermute x12, starting transfers between devices: 21 us -> 34.7 us  [along(): return lax.ppermute(x, ('samples', 'chan'), whole)]
    unnamed x10 -> x57, local copies, waits for them, and re-layouts: 3.31 us -> 13.1 us
    pallas_call x10 -> x11, Pallas kernels: 21.3 us -> 24.3 us  [call(): pl.pallas_call(kernel, out_shape=outs, in_specs=sspec(scalars) + vspec(le...]
    ppermute x13, starting transfers between devices: 14.1 us -> 16.6 us  [exchange(): lax.ppermute(x, axis, [(i, (i + s) % size) for i in range(size)])]
  transfers between devices with their start and end apart: 28 -> 28, of which waited for: 13 -> 9; matrix products, arithmetic and copies ran while one was open for 4% -> 3% of each run, Pallas kernels for 16% -> 16%
where the time goes in v3:
time: 120 us
  starting transfers between devices  54.7 us (46%)
  Pallas kernels  24.3 us (20%)
  waiting for transfers between devices  23.2 us (19%)
  local copies, waits for them, and re-layouts  13.8 us (12%)
  other arithmetic  2.66 us (2%)
    ppermute x12, starting transfers between devices, along(): return lax.ppermute(x, ('samples', 'chan'), whole)  34.7 us
    pallas_call x11, Pallas kernels, call(): pl.pallas_call(kernel, out_shape=outs, in_specs=sspec(scalars) + vspec(le...  24.3 us
    ppermute x13, starting transfers between devices, exchange(): lax.ppermute(x, axis, [(i, (i + s) % size) for i in range(size)])  16.6 us
    unnamed x57, local copies, waits for them, and re-layouts  13.1 us
    ppermute x13, waiting for transfers between devices, exchange(): lax.ppermute(x, axis, [(i, (i + s) % size) for i in range(size)])  9.92 us
    ppermute x1, waiting for transfers between devices, on_device(): far_got = lax.ppermute(far_sum, 'chan', [(0, size - 1), (size - 1, 0)])  6.14 us
    ppermute x12, waiting for transfers between devices, along(): return lax.ppermute(x, ('samples', 'chan'), whole)  5.71 us
  transfers between devices with their start and end apart: 28, of which 9 were waited for; matrix products, arithmetic and copies ran while one was open for 3% of the time, Pallas kernels for 16%

profile of v3, /device:TPU:0, one launch (start us, length us, event | category | flops | bytes accessed | tf_op | source)
XLA Modules:
  0.0 119.7 jit_solution(3699420211696883040)
XLA Ops:
  0.6 1.3 %copy.19 = bf16[8,8,8,512]{3,1,2,0:T(8,128)(2,1)S(1)} copy(bf16[8,8,8,512]{3,2,1,0:T(8,128)(2,1)} %bitcast.46) | data formatting | bytes 1048576
  1.9 5.0 %collective-permute-start.2 = (bf16[64,4096]{1,0:T(8,128)(2,1)S(1)}, bf16[64,4096]{1,0:T(8,128)(2,1)S(1)}, u32[]{:S(2)}, u32[]{:S(2)}) collective-permute-start(bf16[64,4096]{1,0:T(8,128)(2,1)S(1)} %bitcast.36), channel_id=1, source_target_pairs={{0,1},{1,2},{2,3},{7,6},{6,5},{5,4},{8,9},{9,10},{10,11},{15,14},{... | collective-permute-start | bytes 1572872 | tf_op jit(solution)/shard_map/ppermute | solution.py:315
  6.9 1.3 %collective-permute-start.3 = (bf16[64,4096]{1,0:T(8,128)(2,1)S(1)}, bf16[64,4096]{1,0:T(8,128)(2,1)S(1)}, u32[]{:S(2)}, u32[]{:S(2)}) collective-permute-start(bf16[64,4096]{1,0:T(8,128)(2,1)S(1)} %bitcast.37), channel_id=1, source_target_pairs={{1,0},{2,1},{3,2},{6,7},{5,6},{4,5},{9,8},{10,9},{11,10},{14,15},{... | collective-permute-start | bytes 1572872 | tf_op jit(solution)/shard_map/ppermute | solution.py:315
  8.2 0.7 convert_bitcast_fusion
  8.8 1.3 %copy-done = f32[4,9,64,128]{3,2,1,0:T(8,128)S(1)} copy-done((f32[4,9,64,128]{3,2,1,0:T(8,128)S(1)}, f32[4,9,64,128]{3,2,1,0:T(8,128)}, u32[]{:S(2)}) %copy-start) | copy-done | bytes 1179672
  10.1 0.7 copy-done.10
  10.8 0.7 copy-done.12
  11.5 0.9 energy.1
  12.3 1.5 %collective-permute-start = (f32[64,128]{1,0:T(8,128)S(1)}, f32[64,128]{1,0:T(8,128)S(1)}, u32[]{:S(2)}, u32[]{:S(2)}) collective-permute-start(f32[64,128]{1,0:T(8,128)S(1)} %get-tuple-element.63.refs_0_), channel_id=1, source_target_pairs={{0,16},{16,0},{1,17},{17,1},{2,18},{18,2},{3,19},{19,3},{4,20},{20... | collective-permute-start | bytes 98312 | tf_op jit(solution)/shard_map/ppermute | solution.py:283
  13.9 1.2 %copy.20 = bf16[8,8,8,512]{3,1,2,0:T(8,128)(2,1)S(1)} copy(bf16[8,8,8,512]{3,2,1,0:T(8,128)(2,1)} %bitcast.47) | data formatting | bytes 1048576
  15.1 0.6 collective-permute-start.4
  15.8 0.5 collective-permute-done.refs_1_
  16.3 0.7 modulated.1
  17.0 1.6 %collective-permute-start.1 = (bf16[9,64,128]{2,1,0:T(8,128)(2,1)S(1)}, bf16[9,64,128]{2,1,0:T(8,128)(2,1)S(1)}, u32[]{:S(2)}, u32[]{:S(2)}) collective-permute-start(bf16[9,64,128]{2,1,0:T(8,128)(2,1)S(1)} %get-tuple-element.65.refs_0_), channel_id=1, source_target_pairs={{0,16},{16,0},{1,17},{17,1},{2,18},{18,2},{3,19},{19,3},{4,20},{20... | collective-permute-start | bytes 442376 | tf_op jit(solution)/shard_map/ppermute | solution.py:283
  18.5 1.4 %collective-permute-done.4 = bf16[64,512]{1,0:T(8,128)(2,1)S(1)} collective-permute-done((bf16[64,512]{1,0:T(8,128)(2,1)S(1)}, bf16[64,512]{1,0:T(8,128)(2,1)S(1)}, u32[]{:S(2)}, u32[]{:S(2)}) %collective-permute-start.4) | collective-permute-done | bytes 65568 | tf_op jit(solution)/shard_map/ppermute | solution.py:290
  20.0 2.6 %collective-permute-done.1.refs_1_ = bf16[9,64,128]{2,1,0:T(8,128)(2,1)S(1)} collective-permute-done((bf16[9,64,128]{2,1,0:T(8,128)(2,1)S(1)}, bf16[9,64,128]{2,1,0:T(8,128)(2,1)S(1)}, u32[]{:S(2)}, u32[]{:S(2)}) %collective-permute-start.1) | collective-permute-done | bytes 147488 | tf_op jit(solution)/shard_map/ppermute | solution.py:283
  22.6 0.8 mod_blocks.1
  23.4 0.7 copy-done.7
  24.1 0.6 copy-done.19
  24.7 1.5 %collective-permute-start.5 = (bf16[64,4096]{1,0:T(8,128)(2,1)S(1)}, bf16[64,4096]{1,0:T(8,128)(2,1)}, u32[]{:S(2)}, u32[]{:S(2)}) collective-permute-start(bf16[64,4096]{1,0:T(8,128)(2,1)S(1)} %collective-permute-done.2.refs_1_), channel_id=1, source_target_pairs={{1,2},{2,3},{6,5},{5,4},{9,10},{10,11},{14,13},{13,12},{17,18},{18... | collective-permute-start | bytes 1572872 | tf_op jit(solution)/shard_map/ppermute | solution.py:315
  26.2 0.8 copy-done.13
  27.0 1.3 %collective-permute-start.6 = (bf16[64,4096]{1,0:T(8,128)(2,1)S(1)}, bf16[64,4096]{1,0:T(8,128)(2,1)}, u32[]{:S(2)}, u32[]{:S(2)}) collective-permute-start(bf16[64,4096]{1,0:T(8,128)(2,1)S(1)} %collective-permute-done.3.refs_3_.refs_4_), channel_id=1, source_target_pairs={{1,0},{2,1},{6,7},{5,6},{9,8},{10,9},{14,15},{13,14},{17,16},{18,1... | collective-permute-start | bytes 1572872 | tf_op jit(solution)/shard_map/ppermute | solution.py:315
  28.3 0.8 copy-done.16
  29.2 1.6 %collective-permute-start.11 = (f32[1,708]{1,0:T(1,128)S(1)}, f32[1,708]{1,0:T(1,128)S(1)}, u32[]{:S(2)}, u32[]{:S(2)}) collective-permute-start(f32[1,708]{1,0:T(1,128)S(1)} %broadcast_in_dim.24), channel_id=1, source_target_pairs={{0,8},{4,12},{8,0},{12,4},{1,9},{5,13},{9,1},{13,5},{2,10},{6,14},... | collective-permute-start | bytes 8504 | tf_op jit(solution)/shard_map/ppermute | solution.py:283
  30.8 1.4 %collective-permute-start.12 = (f32[1,708]{1,0:T(1,128)S(1)}, f32[1,708]{1,0:T(1,128)S(1)}, u32[]{:S(2)}, u32[]{:S(2)}) collective-permute-start(f32[1,708]{1,0:T(1,128)S(1)} %broadcast_in_dim.24), channel_id=1, source_target_pairs={{0,12},{4,0},{8,4},{12,8},{1,13},{5,1},{9,5},{13,9},{2,14},{6,2},{... | collective-permute-start | bytes 8504 | tf_op jit(solution)/shard_map/ppermute | solution.py:283
  32.2 5.6 %collective-permute-start.7 = (bf16[64,576]{1,0:T(8,128)(2,1)S(1)}, bf16[64,576]{1,0:T(8,128)(2,1)S(1)}, u32[]{:S(2)}, u32[]{:S(2)}) collective-permute-start(bf16[64,576]{1,0:T(8,128)(2,1)S(1)} %get-tuple-element.74), channel_id=1, source_target_pairs={{0,1},{1,2},{2,3},{3,0},{7,6},{6,5},{5,4},{4,7},{8,9},{9,10},{10,1... | collective-permute-start | bytes 221192 | tf_op jit(solution)/shard_map/ppermute | solution.py:315
  37.8 2.9 %collective-permute-start.8 = (bf16[64,576]{1,0:T(8,128)(2,1)S(1)}, bf16[64,576]{1,0:T(8,128)(2,1)S(1)}, u32[]{:S(2)}, u32[]{:S(2)}) collective-permute-start(bf16[64,576]{1,0:T(8,128)(2,1)S(1)} %get-tuple-element.75), channel_id=1, source_target_pairs={{0,2},{1,3},{2,0},{3,1},{7,5},{6,4},{5,7},{4,6},{8,10},{9,11},{10,... | collective-permute-start | bytes 221192 | tf_op jit(solution)/shard_map/ppermute | solution.py:315
  40.7 2.3 %collective-permute-start.9 = (bf16[64,576]{1,0:T(8,128)(2,1)S(1)}, bf16[64,576]{1,0:T(8,128)(2,1)S(1)}, u32[]{:S(2)}, u32[]{:S(2)}) collective-permute-start(bf16[64,576]{1,0:T(8,128)(2,1)S(1)} %get-tuple-element.76), channel_id=1, source_target_pairs={{0,3},{1,0},{2,1},{3,2},{7,4},{6,7},{5,6},{4,5},{8,11},{9,8},{10,9... | collective-permute-start | bytes 221192 | tf_op jit(solution)/shard_map/ppermute | solution.py:315
  43.0 5.6 %collective-permute-done.8.refs_9_ = bf16[64,576]{1,0:T(8,128)(2,1)S(1)} collective-permute-done((bf16[64,576]{1,0:T(8,128)(2,1)S(1)}, bf16[64,576]{1,0:T(8,128)(2,1)S(1)}, u32[]{:S(2)}, u32[]{:S(2)}) %collective-permute-start.8) | collective-permute-done | bytes 73760 | tf_op jit(solution)/shard_map/ppermute | solution.py:315
  48.6 0.6 copy-done.23
  49.3 0.6 copy-done.25
  49.9 1.5 %collective-permute-start.13 = (bf16[64,4096]{1,0:T(8,128)(2,1)}, bf16[64,4096]{1,0:T(8,128)(2,1)}, u32[]{:S(2)}, u32[]{:S(2)}) collective-permute-start(bf16[64,4096]{1,0:T(8,128)(2,1)} %collective-permute-done.5.refs_2_), channel_id=1, source_target_pairs={{2,3},{5,4},{10,11},{13,12},{18,19},{21,20},{26,27},{29,28}} | collective-permute-start | bytes 1572872 | tf_op jit(solution)/shard_map/ppermute | solution.py:315
  51.4 1.3 %collective-permute-start.14 = (bf16[64,4096]{1,0:T(8,128)(2,1)}, bf16[64,4096]{1,0:T(8,128)(2,1)}, u32[]{:S(2)}, u32[]{:S(2)}) collective-permute-start(bf16[64,4096]{1,0:T(8,128)(2,1)} %collective-permute-done.6.refs_4_.refs_5_), channel_id=1, source_target_pairs={{1,0},{6,7},{9,8},{14,15},{17,16},{22,23},{25,24},{30,31}} | collective-permute-start | bytes 1572872 | tf_op jit(solution)/shard_map/ppermute | solution.py:315
  52.7 1.0 copy-done.3
  53.7 1.0 copy-done.14
  54.8 1.0 copy-done.17
  55.8 5.7 %near_grad.1 = (bf16[256,576]{1,0:T(8,128)(2,1)}, bf16[192,5120]{1,0:T(8,128)(2,1)S(1)}) custom-call(bf16[64,4096]{1,0:T(8,128)(2,1)S(1)} %bitcast.38, bf16[64,4096]{1,0:T(8,128)(2,1)S(1)} %copy-done.14, bf16[64,4096]{1,0:T(8,128)(2,1)} %collective-permute-done.5.refs_2_, bf16[64,4096]{1,0:T(8,128)(2,1)S(1)} %copy-done.17, ...), custom_call_target="tpu_custom_call" | custom-call | flops 1207959552 | bytes 5537792 | tf_op jit(solution)/shard_map/near_grad/pallas_call | solution.py:268
  61.5 1.8 %collective-permute-start.15 = (bf16[256,576]{1,0:T(8,128)(2,1)}, bf16[256,576]{1,0:T(8,128)(2,1)}, u32[]{:S(2)}, u32[]{:S(2)}) collective-permute-start(bf16[256,576]{1,0:T(8,128)(2,1)} %get-tuple-element.82.refs_0_), channel_id=1, source_target_pairs={{0,16},{16,0},{1,17},{17,1},{2,18},{18,2},{3,19},{19,3},{4,20},{20... | collective-permute-start | bytes 884744 | tf_op jit(solution)/shard_map/ppermute | solution.py:283
  63.4 0.6 scatter_custom_fusion
  64.2 0.1 copy.15
  64.4 4.9 %collective-permute-done.15.refs_1_ = bf16[256,576]{1,0:T(8,128)(2,1)} collective-permute-done((bf16[256,576]{1,0:T(8,128)(2,1)}, bf16[256,576]{1,0:T(8,128)(2,1)}, u32[]{:S(2)}, u32[]{:S(2)}) %collective-permute-start.15) | collective-permute-done | bytes 294944 | tf_op jit(solution)/shard_map/ppermute | solution.py:283
  69.3 1.2 near_sum.1
  70.6 4.0 %far_grad.1.refs_0_ = bf16[64,576]{1,0:T(8,128)(2,1)S(1)} custom-call(bf16[64,4096]{1,0:T(8,128)(2,1)} %collective-permute-done.13.first.refs_3_, bf16[64,4096]{1,0:T(8,128)(2,1)} %collective-permute-done.14.second.refs_6_, bf16[192,5120]{1,0:T(8,128)(2,1)S(1)} %get-tuple-element.93.wide), custom_call_target="tpu_custom_call" | custom-call | flops 301989888 | bytes 3088384 | tf_op jit(solution)/shard_map/far_grad/pallas_call | solution.py:268
  74.6 1.8 %collective-permute-start.16 = (bf16[64,576]{1,0:T(8,128)(2,1)S(1)}, bf16[64,576]{1,0:T(8,128)(2,1)S(1)}, u32[]{:S(2)}, u32[]{:S(2)}) collective-permute-start(bf16[64,576]{1,0:T(8,128)(2,1)S(1)} %far_grad.1.refs_0_), channel_id=1, source_target_pairs={{0,16},{16,0},{1,17},{17,1},{2,18},{18,2},{3,19},{19,3},{4,20},{20... | collective-permute-start | bytes 221192 | tf_op jit(solution)/shard_map/ppermute | solution.py:283
  76.4 1.3 %collective-permute-start.18 = (bf16[64,576]{1,0:T(8,128)(2,1)S(1)}, bf16[64,576]{1,0:T(8,128)(2,1)S(1)}, u32[]{:S(2)}, u32[]{:S(2)}) collective-permute-start(bf16[64,576]{1,0:T(8,128)(2,1)S(1)} %get-tuple-element.84), channel_id=1, source_target_pairs={{1,0},{2,1},{3,2},{6,7},{5,6},{4,5},{9,8},{10,9},{11,10},{14,15},{... | collective-permute-start | bytes 221192 | tf_op jit(solution)/shard_map/ppermute | solution.py:315
  77.7 7.0 %collective-permute-start.19 = (bf16[64,576]{1,0:T(8,128)(2,1)S(1)}, bf16[64,576]{1,0:T(8,128)(2,1)S(1)}, u32[]{:S(2)}, u32[]{:S(2)}) collective-permute-start(bf16[64,576]{1,0:T(8,128)(2,1)S(1)} %get-tuple-element.85), channel_id=1, source_target_pairs={{2,0},{3,1},{0,2},{1,3},{5,7},{4,6},{7,5},{6,4},{10,8},{11,9},{8,1... | collective-permute-start | bytes 221192 | tf_op jit(solution)/shard_map/ppermute | solution.py:315
  84.7 3.9 %collective-permute-start.20 = (bf16[64,576]{1,0:T(8,128)(2,1)S(1)}, bf16[64,576]{1,0:T(8,128)(2,1)S(1)}, u32[]{:S(2)}, u32[]{:S(2)}) collective-permute-start(bf16[64,576]{1,0:T(8,128)(2,1)S(1)} %get-tuple-element.86), channel_id=1, source_target_pairs={{0,1},{1,2},{2,3},{7,6},{6,5},{5,4},{8,9},{9,10},{10,11},{15,14},{... | collective-permute-start | bytes 221192 | tf_op jit(solution)/shard_map/ppermute | solution.py:315
  88.7 1.9 %collective-permute-start.17 = (bf16[64,576]{1,0:T(8,128)(2,1)S(1)}, bf16[64,576]{1,0:T(8,128)(2,1)S(1)}, u32[]{:S(2)}, u32[]{:S(2)}) collective-permute-start(bf16[64,576]{1,0:T(8,128)(2,1)S(1)} %far_sum.1), channel_id=1, source_target_pairs={{0,3},{3,0},{4,7},{7,4},{8,11},{11,8},{12,15},{15,12},{16,19},{19,... | collective-permute-start | bytes 221192 | tf_op jit(solution)/shard_map/ppermute | solution.py:418
  90.7 6.1 %collective-permute-done.17.far = bf16[64,576]{1,0:T(8,128)(2,1)S(1)} collective-permute-done((bf16[64,576]{1,0:T(8,128)(2,1)S(1)}, bf16[64,576]{1,0:T(8,128)(2,1)S(1)}, u32[]{:S(2)}, u32[]{:S(2)}) %collective-permute-start.17) | collective-permute-done | bytes 73760 | tf_op jit(solution)/shard_map/ppermute | solution.py:418
  96.8 1.0 collect.1.refs_0_
  97.9 1.6 %collective-permute-start.22 = (bf16[10,64,128]{2,1,0:T(8,128)(2,1)S(1)}, bf16[10,64,128]{2,1,0:T(8,128)(2,1)S(1)}, u32[]{:S(2)}, u32[]{:S(2)}) collective-permute-start(bf16[10,64,128]{2,1,0:T(8,128)(2,1)S(1)} %collect.1.refs_0_), channel_id=1, source_target_pairs={{0,8},{4,12},{8,0},{12,4},{1,9},{5,13},{9,1},{13,5},{2,10},{6,14},... | collective-permute-start | bytes 491528 | tf_op jit(solution)/shard_map/ppermute | solution.py:283
  99.5 1.4 %collective-permute-start.23 = (bf16[10,64,128]{2,1,0:T(8,128)(2,1)S(1)}, bf16[10,64,128]{2,1,0:T(8,128)(2,1)S(1)}, u32[]{:S(2)}, u32[]{:S(2)}) collective-permute-start(bf16[10,64,128]{2,1,0:T(8,128)(2,1)S(1)} %collect.1.refs_0_), channel_id=1, source_target_pairs={{0,12},{4,0},{8,4},{12,8},{1,13},{5,1},{9,5},{13,9},{2,14},{6,2},{... | collective-permute-start | bytes 491528 | tf_op jit(solution)/shard_map/ppermute | solution.py:283
  100.9 5.6 %input_grad.1 = (f32[64,4096]{1,0:T(8,128)S(1)}, f32[64,512]{1,0:T(8,128)S(1)}, f32[64,512]{1,0:T(8,128)S(1)}) custom-call(bf16[64,4096]{1,0:T(8,128)(2,1)S(1)} %bitcast.39, bf16[64,4096]{1,0:T(8,128)(2,1)S(1)} %copy-done.15, bf16[64,4096]{1,0:T(8,128)(2,1)} %collective-permute-done.5.refs_2_, bf16[64,4096]{1,0:T(8,128)(2,1)} %collective-permute-done.13.first.refs_3_, ...), custom_call_target="tpu_custom_call" | custom-call | flops 1207959552 | bytes 5275648 | tf_op jit(solution)/shard_map/input_grad/pallas_call | solution.py:268
  106.5 0.4 collective-permute-done.23.refs_3_
  107.0 0.9 collective-permute-start.24
  107.9 2.8 %bank_grad.1 = (f32[4,9,64,128]{3,2,1,0:T(8,128)}, f32[4,128]{1,0:T(4,128)S(1)}) custom-call(s32[4]{0:T(128)S(1)} %pad_add_fusion.place, f32[4,4]{1,0:T(4,128)S(1)} %split.17.sel, f32[4,9,64,128]{3,2,1,0:T(8,128)S(1)} %copy-done.1, f32[4,128]{1,0:T(4,128)S(1)} %split.18.style, f32[64,4]{1,0:T(8,128)S(1)} %bitcast.40, ...), custom_call_target="tpu_custom_call" | custom-call | flops 1000000 | bytes 3019856 | tf_op jit(solution)/shard_map/bank_grad/pallas_call | solution.py:268
  110.7 0.6 collective-permute-start.26
  111.3 3.3 %collective-permute-start.27 = (f32[4,128]{1,0:T(4,128)S(1)}, f32[4,128]{1,0:T(4,128)S(1)}, u32[]{:S(2)}, u32[]{:S(2)}) collective-permute-start(f32[4,128]{1,0:T(4,128)S(1)} %get-tuple-element.117.refs_0_), channel_id=1, source_target_pairs={{0,3},{1,0},{2,1},{3,2},{4,7},{5,4},{6,5},{7,6},{8,11},{9,8},{10,9... | collective-permute-start | bytes 6152 | tf_op jit(solution)/shard_map/ppermute | solution.py:283
  114.6 0.6 copy.21
  115.2 0.9 collective-permute-done.25.refs_1_
  116.1 0.6 collective-permute-done.27.refs_3_
  116.7 1.6 %affine.1 = (f32[512,128]{1,0:T(8,128)}, f32[1,128]{1,0:T(1,128)}) custom-call(s32[4]{0:T(128)S(1)} %pad_add_fusion.place, f32[512,4]{1,0:T(8,128)S(1)} %bitcast.33, f32[4,128]{1,0:T(4,128)S(1)} %get-tuple-element.117.refs_0_, f32[4,128]{1,0:T(4,128)S(1)} %collective-permute-done.25.refs_1_, f32[4,128]{1,0:T(4,128)S(1)} %collective-permute-done.26.refs_2_, ...), custom_call_target="tpu_custom_call" | custom-call | flops 1000000 | bytes 279056 | tf_op jit(solution)/shard_map/affine/pallas_call | solution.py:268
  118.3 0.1 copy.17
  118.6 1.1 fusion
  (81 shorter events, 1.0 us)
Async XLA Ops:
  0.6 8.2 %copy-start.9 = (f32[512,128]{1,0:T(8,128)S(1)}, f32[512,128]{1,0:T(8,128)}, u32[]{:S(2)}) copy-start(f32[512,128]{1,0:T(8,128)} %affine_w.1) | copy-start | bytes 786436
  1.9 13.2 %copy-start.4 = (bf16[8,8,8,512]{3,1,2,0:T(8,128)(2,1)}, bf16[8,8,8,512]{3,1,2,0:T(8,128)(2,1)S(1)}, u32[]{:S(2)}) copy-start(bf16[8,8,8,512]{3,1,2,0:T(8,128)(2,1)S(1)} %copy.19) | copy-start | bytes 1572868
  1.9 22.8 %collective-permute-start.2 = (bf16[64,4096]{1,0:T(8,128)(2,1)S(1)}, bf16[64,4096]{1,0:T(8,128)(2,1)S(1)}, u32[]{:S(2)}, u32[]{:S(2)}) collective-permute-start(bf16[64,4096]{1,0:T(8,128)(2,1)S(1)} %bitcast.36), channel_id=1, source_target_pairs={{0,1},{1,2},{2,3},{7,6},{6,5},{5,4},{8,9},{9,10},{10,11},{15,14},{... | collective-permute-start | bytes 1572872 | tf_op jit(solution)/shard_map/ppermute | solution.py:315
  6.9 17.9 %collective-permute-start.3 = (bf16[64,4096]{1,0:T(8,128)(2,1)S(1)}, bf16[64,4096]{1,0:T(8,128)(2,1)S(1)}, u32[]{:S(2)}, u32[]{:S(2)}) collective-permute-start(bf16[64,4096]{1,0:T(8,128)(2,1)S(1)} %bitcast.37), channel_id=1, source_target_pairs={{1,0},{2,1},{3,2},{6,7},{5,6},{4,5},{9,8},{10,9},{11,10},{14,15},{... | collective-permute-start | bytes 1572872 | tf_op jit(solution)/shard_map/ppermute | solution.py:315
  8.8 1.3 %copy-start = (f32[4,9,64,128]{3,2,1,0:T(8,128)S(1)}, f32[4,9,64,128]{3,2,1,0:T(8,128)}, u32[]{:S(2)}) copy-start(f32[4,9,64,128]{3,2,1,0:T(8,128)} %bank.5) | copy-start | bytes 3538948
  10.1 0.7 copy-start.10
  10.8 0.7 copy-start.12
  11.5 4.8 %copy-start.1 = (f32[4,9,64,128]{3,2,1,0:T(8,128)S(1)}, f32[4,9,64,128]{3,2,1,0:T(8,128)}, u32[]{:S(2)}) copy-start(f32[4,9,64,128]{3,2,1,0:T(8,128)} %bank.5) | copy-start | bytes 3538948
  12.3 3.9 %collective-permute-start = (f32[64,128]{1,0:T(8,128)S(1)}, f32[64,128]{1,0:T(8,128)S(1)}, u32[]{:S(2)}, u32[]{:S(2)}) collective-permute-start(f32[64,128]{1,0:T(8,128)S(1)} %get-tuple-element.63.refs_0_), channel_id=1, source_target_pairs={{0,16},{16,0},{1,17},{17,1},{2,18},{18,2},{3,19},{19,3},{4,20},{20... | collective-permute-start | bytes 98312 | tf_op jit(solution)/shard_map/ppermute | solution.py:283
  15.1 36.3 %copy-start.2 = (bf16[8,8,8,512]{3,1,2,0:T(8,128)(2,1)}, bf16[8,8,8,512]{3,1,2,0:T(8,128)(2,1)S(1)}, u32[]{:S(2)}) copy-start(bf16[8,8,8,512]{3,1,2,0:T(8,128)(2,1)S(1)} %copy.20) | copy-start | bytes 1572868
  15.1 14.0 %copy-start.11 = (f32[1,512]{1,0:T(1,128)S(1)}, f32[1,512]{1,0:T(1,128)}, u32[]{:S(2)}) copy-start(f32[1,512]{1,0:T(1,128)} %latent.1) | copy-start | bytes 6148
  15.1 4.8 %collective-permute-start.4 = (bf16[64,512]{1,0:T(8,128)(2,1)S(1)}, bf16[64,512]{1,0:T(8,128)(2,1)S(1)}, u32[]{:S(2)}, u32[]{:S(2)}) collective-permute-start(bf16[64,512]{1,0:T(8,128)(2,1)S(1)} %slice_select_fusion), channel_id=1, source_target_pairs={{0,16},{16,0},{1,17},{17,1},{2,18},{18,2},{3,19},{19,3},{4,20},{20... | collective-permute-start | bytes 196616 | tf_op jit(solution)/shard_map/ppermute | solution.py:290
  15.8 36.9 %copy-start.5 = (bf16[8,8,8,512]{3,1,2,0:T(8,128)(2,1)S(1)}, bf16[8,8,8,512]{3,1,2,0:T(8,128)(2,1)}, u32[]{:S(2)}) copy-start(bf16[8,8,8,512]{3,1,2,0:T(8,128)(2,1)} %copy-done.4) | copy-start | bytes 1572868
  17.0 5.7 %collective-permute-start.1 = (bf16[9,64,128]{2,1,0:T(8,128)(2,1)S(1)}, bf16[9,64,128]{2,1,0:T(8,128)(2,1)S(1)}, u32[]{:S(2)}, u32[]{:S(2)}) collective-permute-start(bf16[9,64,128]{2,1,0:T(8,128)(2,1)S(1)} %get-tuple-element.65.refs_0_), channel_id=1, source_target_pairs={{0,16},{16,0},{1,17},{17,1},{2,18},{18,2},{3,19},{19,3},{4,20},{20... | collective-permute-start | bytes 442376 | tf_op jit(solution)/shard_map/ppermute | solution.py:283
  23.4 0.7 copy-start.7
  24.1 0.6 copy-start.19
  24.7 25.2 %collective-permute-start.5 = (bf16[64,4096]{1,0:T(8,128)(2,1)S(1)}, bf16[64,4096]{1,0:T(8,128)(2,1)}, u32[]{:S(2)}, u32[]{:S(2)}) collective-permute-start(bf16[64,4096]{1,0:T(8,128)(2,1)S(1)} %collective-permute-done.2.refs_1_), channel_id=1, source_target_pairs={{1,2},{2,3},{6,5},{5,4},{9,10},{10,11},{14,13},{13,12},{17,18},{18... | collective-permute-start | bytes 1572872 | tf_op jit(solution)/shard_map/ppermute | solution.py:315
  26.2 0.8 copy-start.13
  27.0 22.9 %collective-permute-start.6 = (bf16[64,4096]{1,0:T(8,128)(2,1)S(1)}, bf16[64,4096]{1,0:T(8,128)(2,1)}, u32[]{:S(2)}, u32[]{:S(2)}) collective-permute-start(bf16[64,4096]{1,0:T(8,128)(2,1)S(1)} %collective-permute-done.3.refs_3_.refs_4_), channel_id=1, source_target_pairs={{1,0},{2,1},{6,7},{5,6},{9,8},{10,9},{14,15},{13,14},{17,16},{18,1... | collective-permute-start | bytes 1572872 | tf_op jit(solution)/shard_map/ppermute | solution.py:315
  28.3 0.8 copy-start.16
  29.2 3.0 %collective-permute-start.10 = (f32[1,708]{1,0:T(1,128)S(1)}, f32[1,708]{1,0:T(1,128)S(1)}, u32[]{:S(2)}, u32[]{:S(2)}) collective-permute-start(f32[1,708]{1,0:T(1,128)S(1)} %broadcast_in_dim.24), channel_id=1, source_target_pairs={{0,4},{4,8},{8,12},{12,0},{1,5},{5,9},{9,13},{13,1},{2,6},{6,10},{... | collective-permute-start | bytes 8504 | tf_op jit(solution)/shard_map/ppermute | solution.py:283
  29.2 8.6 %collective-permute-start.11 = (f32[1,708]{1,0:T(1,128)S(1)}, f32[1,708]{1,0:T(1,128)S(1)}, u32[]{:S(2)}, u32[]{:S(2)}) collective-permute-start(f32[1,708]{1,0:T(1,128)S(1)} %broadcast_in_dim.24), channel_id=1, source_target_pairs={{0,8},{4,12},{8,0},{12,4},{1,9},{5,13},{9,1},{13,5},{2,10},{6,14},... | collective-permute-start | bytes 8504 | tf_op jit(solution)/shard_map/ppermute | solution.py:283
  30.8 9.9 %collective-permute-start.12 = (f32[1,708]{1,0:T(1,128)S(1)}, f32[1,708]{1,0:T(1,128)S(1)}, u32[]{:S(2)}, u32[]{:S(2)}) collective-permute-start(f32[1,708]{1,0:T(1,128)S(1)} %broadcast_in_dim.24), channel_id=1, source_target_pairs={{0,12},{4,0},{8,4},{12,8},{1,13},{5,1},{9,5},{13,9},{2,14},{6,2},{... | collective-permute-start | bytes 8504 | tf_op jit(solution)/shard_map/ppermute | solution.py:283
  32.2 10.8 %collective-permute-start.7 = (bf16[64,576]{1,0:T(8,128)(2,1)S(1)}, bf16[64,576]{1,0:T(8,128)(2,1)S(1)}, u32[]{:S(2)}, u32[]{:S(2)}) collective-permute-start(bf16[64,576]{1,0:T(8,128)(2,1)S(1)} %get-tuple-element.74), channel_id=1, source_target_pairs={{0,1},{1,2},{2,3},{3,0},{7,6},{6,5},{5,4},{4,7},{8,9},{9,10},{10,1... | collective-permute-start | bytes 221192 | tf_op jit(solution)/shard_map/ppermute | solution.py:315
  37.8 10.8 %collective-permute-start.8 = (bf16[64,576]{1,0:T(8,128)(2,1)S(1)}, bf16[64,576]{1,0:T(8,128)(2,1)S(1)}, u32[]{:S(2)}, u32[]{:S(2)}) collective-permute-start(bf16[64,576]{1,0:T(8,128)(2,1)S(1)} %get-tuple-element.75), channel_id=1, source_target_pairs={{0,2},{1,3},{2,0},{3,1},{7,5},{6,4},{5,7},{4,6},{8,10},{9,11},{10,... | collective-permute-start | bytes 221192 | tf_op jit(solution)/shard_map/ppermute | solution.py:315
  40.7 8.6 %collective-permute-start.9 = (bf16[64,576]{1,0:T(8,128)(2,1)S(1)}, bf16[64,576]{1,0:T(8,128)(2,1)S(1)}, u32[]{:S(2)}, u32[]{:S(2)}) collective-permute-start(bf16[64,576]{1,0:T(8,128)(2,1)S(1)} %get-tuple-element.76), channel_id=1, source_target_pairs={{0,3},{1,0},{2,1},{3,2},{7,4},{6,7},{5,6},{4,5},{8,11},{9,8},{10,9... | collective-permute-start | bytes 221192 | tf_op jit(solution)/shard_map/ppermute | solution.py:315
  43.0 18.5 %copy-start.21 = (bf16[64,576]{1,0:T(8,128)(2,1)}, bf16[64,576]{1,0:T(8,128)(2,1)S(1)}, u32[]{:S(2)}) copy-start(bf16[64,576]{1,0:T(8,128)(2,1)S(1)} %collective-permute-done.7.refs_8_) | copy-start | bytes 221188
  48.6 0.6 copy-start.23
  49.3 0.6 copy-start.25
  49.9 20.6 %collective-permute-start.13 = (bf16[64,4096]{1,0:T(8,128)(2,1)}, bf16[64,4096]{1,0:T(8,128)(2,1)}, u32[]{:S(2)}, u32[]{:S(2)}) collective-permute-start(bf16[64,4096]{1,0:T(8,128)(2,1)} %collective-permute-done.5.refs_2_), channel_id=1, source_target_pairs={{2,3},{5,4},{10,11},{13,12},{18,19},{21,20},{26,27},{29,28}} | collective-permute-start | bytes 1572872 | tf_op jit(solution)/shard_map/ppermute | solution.py:315
  51.4 19.1 %collective-permute-start.14 = (bf16[64,4096]{1,0:T(8,128)(2,1)}, bf16[64,4096]{1,0:T(8,128)(2,1)}, u32[]{:S(2)}, u32[]{:S(2)}) collective-permute-start(bf16[64,4096]{1,0:T(8,128)(2,1)} %collective-permute-done.6.refs_4_.refs_5_), channel_id=1, source_target_pairs={{1,0},{6,7},{9,8},{14,15},{17,16},{22,23},{25,24},{30,31}} | collective-permute-start | bytes 1572872 | tf_op jit(solution)/shard_map/ppermute | solution.py:315
  52.7 1.0 copy-start.3
  53.7 1.0 copy-start.14
  54.8 1.0 copy-start.17
  61.5 7.8 %collective-permute-start.15 = (bf16[256,576]{1,0:T(8,128)(2,1)}, bf16[256,576]{1,0:T(8,128)(2,1)}, u32[]{:S(2)}, u32[]{:S(2)}) collective-permute-start(bf16[256,576]{1,0:T(8,128)(2,1)} %get-tuple-element.82.refs_0_), channel_id=1, source_target_pairs={{0,16},{16,0},{1,17},{17,1},{2,18},{18,2},{3,19},{19,3},{4,20},{20... | collective-permute-start | bytes 884744 | tf_op jit(solution)/shard_map/ppermute | solution.py:283
  70.5 26.3 %copy-start.8 = (bf16[9,64,256]{2,1,0:T(8,128)(2,1)S(1)}, bf16[9,64,256]{2,1,0:T(8,128)(2,1)}, u32[]{:S(2)}) copy-start(bf16[9,64,256]{2,1,0:T(8,128)(2,1)} %copy-done.7) | copy-start | bytes 884740
  70.5 30.4 %copy-start.6 = (bf16[8,8,8,512]{3,1,2,0:T(8,128)(2,1)S(1)}, bf16[8,8,8,512]{3,1,2,0:T(8,128)(2,1)}, u32[]{:S(2)}) copy-start(bf16[8,8,8,512]{3,1,2,0:T(8,128)(2,1)} %copy-done.4) | copy-start | bytes 1572868
  70.5 30.3 %copy-start.15 = (bf16[64,4096]{1,0:T(8,128)(2,1)S(1)}, bf16[64,4096]{1,0:T(8,128)(2,1)}, u32[]{:S(2)}) copy-start(bf16[64,4096]{1,0:T(8,128)(2,1)} %copy-done.13) | copy-start | bytes 1572868
  70.5 30.3 %copy-start.18 = (bf16[64,4096]{1,0:T(8,128)(2,1)S(1)}, bf16[64,4096]{1,0:T(8,128)(2,1)}, u32[]{:S(2)}) copy-start(bf16[64,4096]{1,0:T(8,128)(2,1)} %copy-done.16) | copy-start | bytes 1572868
  70.6 30.3 %copy-start.20 = (bf16[64,576]{1,0:T(8,128)(2,1)S(1)}, bf16[64,576]{1,0:T(8,128)(2,1)}, u32[]{:S(2)}) copy-start(bf16[64,576]{1,0:T(8,128)(2,1)} %copy-done.19) | copy-start | bytes 221188
  70.6 30.3 %copy-start.22 = (bf16[64,576]{1,0:T(8,128)(2,1)S(1)}, bf16[64,576]{1,0:T(8,128)(2,1)}, u32[]{:S(2)}) copy-start(bf16[64,576]{1,0:T(8,128)(2,1)} %copy-done.21) | copy-start | bytes 221188
  70.6 30.3 %copy-start.24 = (bf16[64,576]{1,0:T(8,128)(2,1)S(1)}, bf16[64,576]{1,0:T(8,128)(2,1)}, u32[]{:S(2)}) copy-start(bf16[64,576]{1,0:T(8,128)(2,1)} %copy-done.23) | copy-start | bytes 221188
  70.6 30.3 %copy-start.26 = (bf16[64,576]{1,0:T(8,128)(2,1)S(1)}, bf16[64,576]{1,0:T(8,128)(2,1)}, u32[]{:S(2)}) copy-start(bf16[64,576]{1,0:T(8,128)(2,1)} %copy-done.25) | copy-start | bytes 221188
  74.6 14.0 %collective-permute-start.16 = (bf16[64,576]{1,0:T(8,128)(2,1)S(1)}, bf16[64,576]{1,0:T(8,128)(2,1)S(1)}, u32[]{:S(2)}, u32[]{:S(2)}) collective-permute-start(bf16[64,576]{1,0:T(8,128)(2,1)S(1)} %far_grad.1.refs_0_), channel_id=1, source_target_pairs={{0,16},{16,0},{1,17},{17,1},{2,18},{18,2},{3,19},{19,3},{4,20},{20... | collective-permute-start | bytes 221192 | tf_op jit(solution)/shard_map/ppermute | solution.py:283
  76.4 14.2 %collective-permute-start.18 = (bf16[64,576]{1,0:T(8,128)(2,1)S(1)}, bf16[64,576]{1,0:T(8,128)(2,1)S(1)}, u32[]{:S(2)}, u32[]{:S(2)}) collective-permute-start(bf16[64,576]{1,0:T(8,128)(2,1)S(1)} %get-tuple-element.84), channel_id=1, source_target_pairs={{1,0},{2,1},{3,2},{6,7},{5,6},{4,5},{9,8},{10,9},{11,10},{14,15},{... | collective-permute-start | bytes 221192 | tf_op jit(solution)/shard_map/ppermute | solution.py:315
  77.7 12.9 %collective-permute-start.19 = (bf16[64,576]{1,0:T(8,128)(2,1)S(1)}, bf16[64,576]{1,0:T(8,128)(2,1)S(1)}, u32[]{:S(2)}, u32[]{:S(2)}) collective-permute-start(bf16[64,576]{1,0:T(8,128)(2,1)S(1)} %get-tuple-element.85), channel_id=1, source_target_pairs={{2,0},{3,1},{0,2},{1,3},{5,7},{4,6},{7,5},{6,4},{10,8},{11,9},{8,1... | collective-permute-start | bytes 221192 | tf_op jit(solution)/shard_map/ppermute | solution.py:315
  84.7 6.0 %collective-permute-start.20 = (bf16[64,576]{1,0:T(8,128)(2,1)S(1)}, bf16[64,576]{1,0:T(8,128)(2,1)S(1)}, u32[]{:S(2)}, u32[]{:S(2)}) collective-permute-start(bf16[64,576]{1,0:T(8,128)(2,1)S(1)} %get-tuple-element.86), channel_id=1, source_target_pairs={{0,1},{1,2},{2,3},{7,6},{6,5},{5,4},{8,9},{9,10},{10,11},{15,14},{... | collective-permute-start | bytes 221192 | tf_op jit(solution)/shard_map/ppermute | solution.py:315
  88.7 8.1 %collective-permute-start.17 = (bf16[64,576]{1,0:T(8,128)(2,1)S(1)}, bf16[64,576]{1,0:T(8,128)(2,1)S(1)}, u32[]{:S(2)}, u32[]{:S(2)}) collective-permute-start(bf16[64,576]{1,0:T(8,128)(2,1)S(1)} %far_sum.1), channel_id=1, source_target_pairs={{0,3},{3,0},{4,7},{7,4},{8,11},{11,8},{12,15},{15,12},{16,19},{19,... | collective-permute-start | bytes 221192 | tf_op jit(solution)/shard_map/ppermute | solution.py:418
  97.8 8.6 %collective-permute-start.21 = (bf16[10,64,128]{2,1,0:T(8,128)(2,1)S(1)}, bf16[10,64,128]{2,1,0:T(8,128)(2,1)S(1)}, u32[]{:S(2)}, u32[]{:S(2)}) collective-permute-start(bf16[10,64,128]{2,1,0:T(8,128)(2,1)S(1)} %collect.1.refs_0_), channel_id=1, source_target_pairs={{0,4},{4,8},{8,12},{12,0},{1,5},{5,9},{9,13},{13,1},{2,6},{6,10},{... | collective-permute-start | bytes 491528 | tf_op jit(solution)/shard_map/ppermute | solution.py:283
  97.9 8.6 %collective-permute-start.22 = (bf16[10,64,128]{2,1,0:T(8,128)(2,1)S(1)}, bf16[10,64,128]{2,1,0:T(8,128)(2,1)S(1)}, u32[]{:S(2)}, u32[]{:S(2)}) collective-permute-start(bf16[10,64,128]{2,1,0:T(8,128)(2,1)S(1)} %collect.1.refs_0_), channel_id=1, source_target_pairs={{0,8},{4,12},{8,0},{12,4},{1,9},{5,13},{9,1},{13,5},{2,10},{6,14},... | collective-permute-start | bytes 491528 | tf_op jit(solution)/shard_map/ppermute | solution.py:283
  99.5 7.5 %collective-permute-start.23 = (bf16[10,64,128]{2,1,0:T(8,128)(2,1)S(1)}, bf16[10,64,128]{2,1,0:T(8,128)(2,1)S(1)}, u32[]{:S(2)}, u32[]{:S(2)}) collective-permute-start(bf16[10,64,128]{2,1,0:T(8,128)(2,1)S(1)} %collect.1.refs_0_), channel_id=1, source_target_pairs={{0,12},{4,0},{8,4},{12,8},{1,13},{5,1},{9,5},{13,9},{2,14},{6,2},{... | collective-permute-start | bytes 491528 | tf_op jit(solution)/shard_map/ppermute | solution.py:283
  107.0 11.3 %collective-permute-start.24 = (f32[64,512]{1,0:T(8,128)S(1)}, f32[64,512]{1,0:T(8,128)S(1)}, u32[]{:S(2)}, u32[]{:S(2)}) collective-permute-start(f32[64,512]{1,0:T(8,128)S(1)} %broadcast_select_fusion), channel_id=1, source_target_pairs={{0,16},{16,0},{1,17},{17,1},{2,18},{18,2},{3,19},{19,3},{4,20},{20... | collective-permute-start | bytes 393224 | tf_op jit(solution)/shard_map/ppermute | solution.py:290
  110.7 5.4 %collective-permute-start.25 = (f32[4,128]{1,0:T(4,128)S(1)}, f32[4,128]{1,0:T(4,128)S(1)}, u32[]{:S(2)}, u32[]{:S(2)}) collective-permute-start(f32[4,128]{1,0:T(4,128)S(1)} %get-tuple-element.117.refs_0_), channel_id=1, source_target_pairs={{0,1},{1,2},{2,3},{3,0},{4,5},{5,6},{6,7},{7,4},{8,9},{9,10},{10,1... | collective-permute-start | bytes 6152 | tf_op jit(solution)/shard_map/ppermute | solution.py:283
  110.7 5.4 %collective-permute-start.26 = (f32[4,128]{1,0:T(4,128)S(1)}, f32[4,128]{1,0:T(4,128)S(1)}, u32[]{:S(2)}, u32[]{:S(2)}) collective-permute-start(f32[4,128]{1,0:T(4,128)S(1)} %get-tuple-element.117.refs_0_), channel_id=1, source_target_pairs={{0,2},{1,3},{2,0},{3,1},{4,6},{5,7},{6,4},{7,5},{8,10},{9,11},{10,... | collective-permute-start | bytes 6152 | tf_op jit(solution)/shard_map/ppermute | solution.py:283
  111.3 5.4 %collective-permute-start.27 = (f32[4,128]{1,0:T(4,128)S(1)}, f32[4,128]{1,0:T(4,128)S(1)}, u32[]{:S(2)}, u32[]{:S(2)}) collective-permute-start(f32[4,128]{1,0:T(4,128)S(1)} %get-tuple-element.117.refs_0_), channel_id=1, source_target_pairs={{0,3},{1,0},{2,1},{3,2},{4,7},{5,4},{6,5},{7,6},{8,11},{9,8},{10,9... | collective-permute-start | bytes 6152 | tf_op jit(solution)/shard_map/ppermute | solution.py:283

commit v4 on v3

--- a/solution.py
+++ b/solution.py
@@ -11,7 +11,7 @@
 TAPS = 9
 F32 = jnp.float32
 BF16 = jnp.bfloat16
-VMEM_LIMIT = 48 * 2**20
+VMEM_LIMIT = 16 * 2**20
 
 
 def params():
@@ -67,22 +67,23 @@
         mod_out[tap] = (mixed(bank, sel, 0, tap) * style[...] * scale).astype(BF16)
 
 
-def blocks_kernel(rows, size, place, *refs):
-    parts, whole, outs = refs[:rows], refs[rows], refs[rows + 1 : rows + 1 + size]
-    by_row, by_chan = refs[rows + 1 + size :]
-    row_at, chan_at, sign = place[2], place[1], place[3]
+def blocks_kernel(rows, size, shares, place, *refs):
+    parts, whole, out, by_row, by_share = refs[:rows], *refs[rows:]
+    row_at = place[2]
     for r in range(rows):
         by_row[lax.rem(row_at - r + rows, rows)] = parts[r][...]
     ch = whole.shape[2] // size
+    share = out.shape[1]
     taps = []
     for tap in range(TAPS):
         value = beside([by_row[r, tap].astype(F32) for r in range(rows)])
         whole[tap] = value.astype(BF16)
         taps.append(value)
     for z in range(size):
-        by_chan[z] = beside([value[:, z * ch : (z + 1) * ch] for value in taps]).astype(BF16)
-    for d in range(size):
-        outs[d][...] = by_chan[lax.rem(chan_at + sign * d + size, size)]
+        value = beside([value[:, z * ch : (z + 1) * ch] for value in taps]).astype(BF16)
+        for k in range(shares):
+            by_share[k, z] = value[k * share : (k + 1) * share]
+    out[...] = by_share[row_at if shares > 1 else 0]
 
 
 def shifted(x, by):
@@ -107,17 +108,11 @@
 
 
 def near_grad_kernel(size, height, width, *refs):
-    cotan_own, first, second = refs[0], refs[1 : size - 1], refs[size - 1 : 2 * size - 3]
-    feat, feat_before, feat_after, out, wide, gathered, total = refs[2 * size - 3 :]
+    cotans, (feat, feat_before, feat_after) = refs[:3], refs[3:6]
+    outs, (wide, gathered, total) = refs[6:9], refs[9:]
     ch = feat.shape[0]
-    gathered[0:ch] = cotan_own[...]
-    for d in range(1, size):
-        found = []
-        if d < size - 1:
-            found.append(first[d - 1][...])
-        if size - d < size - 1:
-            found.append(second[size - d - 1][...])
-        gathered[d * ch : (d + 1) * ch] = found[0] if len(found) == 1 else found[0] + found[1]
+    for at, cotan in enumerate(cotans):
+        gathered[at * ch : (at + 1) * ch] = cotan[...]
     for row in range(height + 2):
         if row == 0:
             x = feat_before[...]
@@ -129,41 +124,35 @@
         x = x.astype(F32)
         wide[0:ch, row * width : (row + 1) * width] = shifted(x, 1).astype(BF16)
         wide[2 * ch : 3 * ch, row * width : (row + 1) * width] = shifted(x, -1).astype(BF16)
-    out[...] = tap_products(gathered, wide, total, height, width).astype(BF16)
-
-
-def far_grad_kernel(height, width, first, second, wide, out, cotan, total):
-    cotan[...] = first[...] + second[...]
-    out[...] = tap_products(cotan, wide, total, height, width).astype(BF16)
-
-
-def near_sum_kernel(rows, size, *refs):
-    nears, outs = refs[:rows], refs[rows:]
+    whole = tap_products(gathered, wide, total, height, width).astype(BF16)
+    for at, out in enumerate(outs):
+        out[...] = whole[at * ch : (at + 1) * ch]
+
+
+def far_grad_kernel(count, height, width, *refs):
+    first, second, wide = refs[:count], refs[count : 2 * count], refs[2 * count]
+    outs, (gathered, total) = refs[2 * count + 1 : 3 * count + 1], refs[3 * count + 1 :]
     ch = outs[0].shape[0]
-    for d in range(size):
-        value = nears[0][d * ch : (d + 1) * ch].astype(F32)
-        for r in range(1, rows):
-            value = value + nears[r][d * ch : (d + 1) * ch].astype(F32)
-        outs[d][...] = value.astype(BF16)
-
-
-def sum_kernel(*refs):
-    value = refs[0][...].astype(F32)
-    for ref in refs[1:-1]:
-        value = value + ref[...].astype(F32)
-    refs[-1][...] = value.astype(BF16)
-
-
-def input_grad_kernel(size, height, width, *refs):
+    for at in range(count):
+        gathered[at * ch : (at + 1) * ch] = first[at][...] + second[at][...]
+    whole = tap_products(gathered, wide, total, height, width).astype(BF16)
+    for at, out in enumerate(outs):
+        out[...] = whole[at * ch : (at + 1) * ch]
+
+
+def input_grad_kernel(rows, size, shares, height, width, place, *refs):
     cotan_own, first, second = refs[0], refs[1:size], refs[size : 2 * size - 1]
-    mods = refs[2 * size - 1 : 3 * size - 1]
-    main, before, after, gathered, taps_t, total = refs[3 * size - 1 :]
+    mods = refs[2 * size - 1 : 2 * size - 1 + shares]
+    main, before, after, gathered, taps, taps_t, total = refs[2 * size - 1 + shares :]
     ch = cotan_own.shape[0]
     gathered[0:ch] = cotan_own[...]
     for d in range(1, size):
         gathered[d * ch : (d + 1) * ch] = first[d - 1][...] + second[size - d - 1][...]
-    every = jnp.concatenate([mod[...].astype(F32) for mod in mods], axis=0)
-    taps_t[...] = every.T.astype(BF16)
+    for k in range(shares):
+        share = lax.rem(place[2] - k + rows, rows) if shares > 1 else 0
+        for d in range(size):
+            taps[d, share] = mods[k][lax.rem(place[1] - place[3] * d + size, size)].astype(F32)
+    taps_t[...] = taps[...].reshape(size * ch, taps.shape[3]).T.astype(BF16)
     total[...] = jnp.zeros(total.shape, F32)
 
     def body(row, _):
@@ -191,27 +180,51 @@
     return high, mid, x - high - mid
 
 
+def put_fall(out, fall):
+    lane = lax.broadcasted_iota(jnp.int32, out.shape[1:], 1)
+    last = jnp.zeros(out.shape[1:], F32)
+    for at, piece in enumerate(split3(fall)):
+        last = jnp.where(lane == at, piece, last)
+    out[TAPS] = last.astype(BF16)
+
+
+def get_fall(last):
+    last = last.astype(F32)
+    return last[:, 0:1] + last[:, 1:2] + last[:, 2:3]
+
+
 def collect_kernel(rows, size, place, scale, whole_mod, far, *refs):
-    nears, out, by_chan, by_row = refs[:size], refs[size], refs[size + 1], refs[size + 2]
+    nears, outs = refs[:size], refs[size : size + rows]
+    by_chan, by_row = refs[size + rows :]
     chan_at, row_at, sign = place[1], place[2], place[3]
     for d in range(size):
         by_chan[lax.rem(chan_at + sign * d + size, size)] = nears[d][...].astype(F32)
     by_chan[jnp.where(chan_at == 0, size - 1, 0)] += far[...].astype(F32)
     ch = whole_mod.shape[2] // size
-    in_ch = out.shape[2]
+    in_ch = outs[0].shape[2]
     product = jnp.zeros(whole_mod.shape[1:], F32)
     for tap in range(TAPS):
         value = beside([by_chan[z, :, tap * ch : (tap + 1) * ch] for z in range(size)])
         product = product + value * whole_mod[tap].astype(F32)
         for r in range(rows):
             by_row[r, tap] = value[:, r * in_ch : (r + 1) * in_ch].astype(BF16)
-    out[0:TAPS] = by_row[row_at]
     fall = jnp.sum(product, axis=1, keepdims=True) * (scale[:, 0:1] * scale[:, 0:1])
-    lane = lax.broadcasted_iota(jnp.int32, out.shape[1:], 1)
-    last = jnp.zeros(out.shape[1:], F32)
-    for at, piece in enumerate(split3(fall)):
-        last = jnp.where(lane == at, piece, last)
-    out[TAPS] = last.astype(BF16)
+    for r in range(rows):
+        outs[r][0:TAPS] = by_row[lax.rem(row_at + r, rows)]
+        put_fall(outs[r], fall)
+
+
+def row_sum_kernel(*refs):
+    parts, out = refs[:-1], refs[-1]
+    fall = get_fall(parts[0][TAPS])
+    for part in parts[1:]:
+        fall = fall + get_fall(part[TAPS])
+    for tap in range(TAPS):
+        value = parts[0][tap].astype(F32)
+        for part in parts[1:]:
+            value = value + part[tap].astype(F32)
+        out[tap] = value.astype(BF16)
+    put_fall(out, fall)
 
 
 def bank_grad_kernel(samples, place, sel, bank, style, scales, *refs):
@@ -223,8 +236,7 @@
     styles, every_scale = style[...], scales[...]
     falls = []
     for b in range(samples):
-        last = held[b, TAPS].astype(F32)
-        falls.append(last[:, 0:1] + last[:, 1:2] + last[:, 2:3])
+        falls.append(get_fall(held[b, TAPS]))
     sums = [jnp.zeros(bank.shape[2:], F32) for _ in range(samples)]
     for tap in range(TAPS):
         totals = [None] * bank.shape[0]
@@ -348,26 +360,46 @@
         scalars=1,
     )
     message = ((ch, TAPS * ch), BF16)
-    whole_mod, *to_send = call(
-        functools.partial(blocks_kernel, rows, size),
+    shares = rows if ch % (16 * rows) == 0 else 1
+    share = (ch // shares, TAPS * ch)
+    whole_mod, to_send = call(
+        functools.partial(blocks_kernel, rows, size, shares),
         "mod_blocks",
-        [((TAPS, out_ch, all_ch), BF16)] + [message] * size,
+        [((TAPS, out_ch, all_ch), BF16), ((size, *share), BF16)],
         place,
         *exchange(mod_own, "rows"),
         scalars=1,
-        scratch=[((rows, TAPS, out_ch, in_ch), BF16), ((size, *message[0]), BF16)],
+        scratch=[((rows, TAPS, out_ch, in_ch), BF16), ((shares, size, *share), BF16)],
     )
     first[0], second[0], to_send, feat_before, feat_after = lax.optimization_barrier(
         (first[0], second[0], to_send, feat_before, feat_after)
     )
 
     step(2, first[0], second[0])
-    mods = [to_send[0]] + [
-        along(to_send[d], [(i, (i + d) % size) for i in range(size)]) for d in range(1, size)
-    ]
+    *near, wide = call(
+        functools.partial(near_grad_kernel, size, height, width),
+        "near_grad",
+        [message] * 3 + [((3 * ch, (height + 2) * width), BF16)],
+        cotan,
+        first[0],
+        second[0],
+        feat,
+        feat_before,
+        feat_after,
+        scratch=[((3 * ch, pixels), BF16), ((3, 3 * ch, 3 * ch), F32)],
+        flops=flops * 3 // size,
+    )
+    near, to_send = lax.optimization_barrier((near, to_send))
+    got = [None] * size
+    got[0] = near[0]
+    got[1] = along(near[1], [(i, i - 1) for i in range(1, size)])
+    got[size - 1] = along(near[2], [(i, i + 1) for i in range(size - 1)])
+    mods = lax.all_to_all(to_send, "chan", 0, 0)
     small = jnp.concatenate([latent[0], own_sel[0], style[0], scale_row[0]])[None]
     smalls = exchange(small, "samples")
-    first[1], second[1], mods, smalls = lax.optimization_barrier((first[1], second[1], mods, smalls))
+    first[1], second[1], mods, smalls, got[1], got[size - 1] = lax.optimization_barrier(
+        (first[1], second[1], mods, smalls, got[1], got[size - 1])
+    )
     at = jnp.remainder(sample_at - jnp.arange(samples), samples)
     every = jnp.zeros((samples, small.shape[1]), F32).at[at].set(jnp.concatenate(smalls, axis=0))
     ends = [latent.shape[1], latent.shape[1] + select.shape[1]]
@@ -376,36 +408,30 @@
 
     for number in range(3, size):
         step(number, first[number - 2], second[number - 2])
-    near, wide = call(
-        functools.partial(near_grad_kernel, size, height, width),
-        "near_grad",
-        [((all_ch, TAPS * ch), BF16), ((3 * ch, (height + 2) * width), BF16)],
-        cotan,
-        *first[: size - 2],
-        *second[: size - 2],
-        feat,
-        feat_before,
-        feat_after,
-        scratch=[((all_ch, pixels), BF16), ((3, all_ch, 3 * ch), F32)],
-        flops=flops,
-    )
-    near_sums = call(
-        functools.partial(near_sum_kernel, rows, size),
-        "near_sum",
-        [message] * size,
-        *exchange(near, "rows"),
-    )
-    got = [near_sums[0]]
-    for d in range(1, size):
-        pairs = [(i, i - d) for i in range(d, size) if d < size - 1]
-        pairs += [(i, i - d + size) for i in range(d) if size - d < size - 1]
-        got.append(along(near_sums[d], pairs))
-    first[-1], second[-1], near_sums, tables = lax.optimization_barrier(
-        (first[-1], second[-1], near_sums, tables)
+    mods = exchange(mods, "rows") if shares > 1 else [mods]
+
+    def far_grad(slots, name):
+        return call(
+            functools.partial(far_grad_kernel, len(slots), height, width),
+            name,
+            [message] * len(slots),
+            *[first[d - 1] for d in slots],
+            *[second[size - d - 1] for d in slots],
+            wide,
+            scratch=[((len(slots) * ch, pixels), BF16), ((3, len(slots) * ch, 3 * ch), F32)],
+            flops=flops * len(slots) // size,
+        )
+
+    between = list(range(2, size - 1))
+    middle = far_grad(between, "middle_grad")
+    for d, part in zip(between, middle):
+        got[d] = along(part, [(i, (i - d) % size) for i in range(size)])
+    first[-1], second[-1], middle, tables, mods = lax.optimization_barrier(
+        (first[-1], second[-1], middle, tables, mods)
     )
     latents, sel, styles, scales = tables
     (far,) = call(
-        functools.partial(far_grad_kernel, height, width),
+        functools.partial(far_grad_kernel, 1, height, width),
         "far_grad",
         [message],
         first[-1],
@@ -414,13 +440,12 @@
         scratch=[((ch, pixels), BF16), ((3, ch, 3 * ch), F32)],
         flops=flops // size,
     )
-    (far_sum,) = call(sum_kernel, "far_sum", [message], *exchange(far, "rows"))
-    far_got = lax.ppermute(far_sum, "chan", [(0, size - 1), (size - 1, 0)])
-
-    (own,) = call(
+    far_got = lax.ppermute(far, "chan", [(0, size - 1), (size - 1, 0)])
+
+    parts = call(
         functools.partial(collect_kernel, rows, size),
         "collect",
-        [((TAPS + 1, out_ch, in_ch), BF16)],
+        [((TAPS + 1, out_ch, in_ch), BF16)] * rows,
         place,
         scale,
         whole_mod,
@@ -429,19 +454,27 @@
         scalars=1,
         scratch=[((size, *message[0]), F32), ((rows, TAPS, out_ch, in_ch), BF16)],
     )
+    parts = [parts[0]] + [
+        lax.ppermute(parts[r], "rows", [(i, (i + r) % rows) for i in range(rows)])
+        for r in range(1, rows)
+    ]
+    (own,) = call(row_sum_kernel, "row_sum", [((TAPS + 1, out_ch, in_ch), BF16)], *parts)
     every = exchange(own, "samples")
 
     own, mods = lax.optimization_barrier((own, mods))
     main, before, after = call(
-        functools.partial(input_grad_kernel, size, height, width),
+        functools.partial(input_grad_kernel, rows, size, shares, height, width),
         "input_grad",
         [((ch, pixels), F32), ((ch, width), F32), ((ch, width), F32)],
+        place,
         cotan,
         *first,
         *second,
         *mods,
+        scalars=1,
         scratch=[
             ((all_ch, pixels), BF16),
+            ((size, shares, *share), F32),
             ((TAPS * ch, all_ch), BF16),
             ((height + 2, 3 * ch, width), F32),
         ],

time: 120 us -> 120 us (level)
  starting transfers between devices: 54.7 us -> 49.6 us
  waiting for transfers between devices: 23.2 us -> 26.9 us
  Pallas kernels: 24.3 us -> 27.5 us
  local copies, waits for them, and re-layouts: 13.8 us -> 10.9 us
    ppermute x12 -> x9, starting transfers between devices: 34.7 us -> 22.1 us  [along(): return lax.ppermute(x, ('samples', 'chan'), whole)]
    all_to_all x0 -> x1, starting transfers between devices: none -> 8.77 us  [on_device(): mods = lax.all_to_all(to_send, 'chan', 0, 0)]
    unnamed x57 -> x49, local copies, waits for them, and re-layouts: 13.1 us -> 7.74 us
    ppermute x13 -> x12, starting transfers between devices: 16.6 us -> 12.4 us  [exchange(): lax.ppermute(x, axis, [(i, (i + s) % size) for i in range(size)])]
    ppermute x1 -> x2, waiting for transfers between devices: 6.14 us -> 9.76 us  [the longest x1 6.19 us: on_device(): far_got = lax.ppermute(far, 'chan', [(0, size - 1), (size - 1, 0)])]
    ppermute x13 -> x12, waiting for transfers between devices: 9.92 us -> 13.4 us  [exchange(): lax.ppermute(x, axis, [(i, (i + s) % size) for i in range(size)])]
    pallas_call x11, Pallas kernels: 24.3 us -> 27.5 us  [call(): pl.pallas_call(kernel, out_shape=outs, in_specs=sspec(scalars) + vspec(le...]
    split x6, local copies, waits for them, and re-layouts: 0.39 us -> 2.82 us  [on_device(): jnp.split(every, ends + [ends[1] + in_ch], axis=1)]
  transfers between devices with their start and end apart: 28 -> 26, of which waited for: 9 -> 10; matrix products, arithmetic and copies ran while one was open for 3% -> 5% of each run, Pallas kernels for 16% -> 22%
where the time goes in v4:
time: 120 us; the launch traced here: 119 us
  starting transfers between devices  49.6 us (41%)
  Pallas kernels  27.5 us (23%)
  waiting for transfers between devices  26.9 us (22%)
  local copies, waits for them, and re-layouts  10.9 us (9%)
  other arithmetic  3.13 us (3%)
    pallas_call x11, Pallas kernels, call(): pl.pallas_call(kernel, out_shape=outs, in_specs=sspec(scalars) + vspec(le...  27.5 us
    ppermute x9, starting transfers between devices, along(): return lax.ppermute(x, ('samples', 'chan'), whole)  22.1 us
    ppermute x12, waiting for transfers between devices, exchange(): lax.ppermute(x, axis, [(i, (i + s) % size) for i in range(size)])  13.4 us
    ppermute x12, starting transfers between devices, exchange(): lax.ppermute(x, axis, [(i, (i + s) % size) for i in range(size)])  12.4 us
    all_to_all x1, starting transfers between devices, on_device(): mods = lax.all_to_all(to_send, 'chan', 0, 0)  8.77 us
    unnamed x49, local copies, waits for them, and re-layouts  7.74 us
    ppermute x1, waiting for transfers between devices, on_device(): far_got = lax.ppermute(far, 'chan', [(0, size - 1), (size - 1, 0)])  6.19 us
    ppermute x9, waiting for transfers between devices, along(): return lax.ppermute(x, ('samples', 'chan'), whole)  3.78 us
  transfers between devices with their start and end apart: 26, of which 10 were waited for; matrix products, arithmetic and copies ran while one was open for 5% of the time, Pallas kernels for 22%

profile of v4, /device:TPU:0, one launch (start us, length us, event | category | flops | bytes accessed | tf_op | source)
XLA Modules:
  0.0 119.1 jit_solution(741249130799280950)
XLA Ops:
  0.7 1.3 %copy.19 = bf16[8,8,8,512]{3,1,2,0:T(8,128)(2,1)S(1)} copy(bf16[8,8,8,512]{3,2,1,0:T(8,128)(2,1)} %bitcast.46) | data formatting | bytes 1048576
  1.9 5.7 %collective-permute-start.2 = (bf16[64,4096]{1,0:T(8,128)(2,1)S(1)}, bf16[64,4096]{1,0:T(8,128)(2,1)}, u32[]{:S(2)}, u32[]{:S(2)}) collective-permute-start(bf16[64,4096]{1,0:T(8,128)(2,1)S(1)} %bitcast.36), channel_id=1, source_target_pairs={{0,1},{1,2},{2,3},{7,6},{6,5},{5,4},{8,9},{9,10},{10,11},{15,14},{... | collective-permute-start | bytes 1572872 | tf_op jit(solution)/shard_map/ppermute | solution.py:327
  7.7 1.3 %collective-permute-start.3 = (bf16[64,4096]{1,0:T(8,128)(2,1)S(1)}, bf16[64,4096]{1,0:T(8,128)(2,1)}, u32[]{:S(2)}, u32[]{:S(2)}) collective-permute-start(bf16[64,4096]{1,0:T(8,128)(2,1)S(1)} %bitcast.37), channel_id=1, source_target_pairs={{1,0},{2,1},{3,2},{6,7},{5,6},{4,5},{9,8},{10,9},{11,10},{14,15},{... | collective-permute-start | bytes 1572872 | tf_op jit(solution)/shard_map/ppermute | solution.py:327
  9.0 1.2 convert_bitcast_fusion
  10.2 1.3 %copy-done = f32[4,9,64,128]{3,2,1,0:T(8,128)S(1)} copy-done((f32[4,9,64,128]{3,2,1,0:T(8,128)S(1)}, f32[4,9,64,128]{3,2,1,0:T(8,128)}, u32[]{:S(2)}) %copy-start) | copy-done | bytes 1179672
  11.4 0.7 copy-done.16
  12.1 0.7 copy-done.20
  12.8 0.9 energy.1
  13.7 1.5 %collective-permute-start = (f32[64,128]{1,0:T(8,128)S(1)}, f32[64,128]{1,0:T(8,128)S(1)}, u32[]{:S(2)}, u32[]{:S(2)}) collective-permute-start(f32[64,128]{1,0:T(8,128)S(1)} %get-tuple-element.60.refs_0_), channel_id=1, source_target_pairs={{0,16},{16,0},{1,17},{17,1},{2,18},{18,2},{3,19},{19,3},{4,20},{20... | collective-permute-start | bytes 98312 | tf_op jit(solution)/shard_map/ppermute | solution.py:295
  15.2 0.2 copy.20
  15.4 0.6 collective-permute-start.4
  16.1 1.5 %collective-permute-done.refs_1_ = f32[64,128]{1,0:T(8,128)S(1)} collective-permute-done((f32[64,128]{1,0:T(8,128)S(1)}, f32[64,128]{1,0:T(8,128)S(1)}, u32[]{:S(2)}, u32[]{:S(2)}) %collective-permute-start) | collective-permute-done | bytes 32800 | tf_op jit(solution)/shard_map/ppermute | solution.py:295
  17.6 0.7 modulated.1
  18.3 1.9 %collective-permute-start.1 = (bf16[9,64,128]{2,1,0:T(8,128)(2,1)S(1)}, bf16[9,64,128]{2,1,0:T(8,128)(2,1)S(1)}, u32[]{:S(2)}, u32[]{:S(2)}) collective-permute-start(bf16[9,64,128]{2,1,0:T(8,128)(2,1)S(1)} %get-tuple-element.62.refs_0_), channel_id=1, source_target_pairs={{0,16},{16,0},{1,17},{17,1},{2,18},{18,2},{3,19},{19,3},{4,20},{20... | collective-permute-start | bytes 442376 | tf_op jit(solution)/shard_map/ppermute | solution.py:295
  20.2 3.3 %collective-permute-done.1.refs_1_ = bf16[9,64,128]{2,1,0:T(8,128)(2,1)S(1)} collective-permute-done((bf16[9,64,128]{2,1,0:T(8,128)(2,1)S(1)}, bf16[9,64,128]{2,1,0:T(8,128)(2,1)S(1)}, u32[]{:S(2)}, u32[]{:S(2)}) %collective-permute-start.1) | collective-permute-done | bytes 147488 | tf_op jit(solution)/shard_map/ppermute | solution.py:295
  23.5 1.4 %mod_blocks.1 = (bf16[9,64,256]{2,1,0:T(8,128)(2,1)S(1)}, bf16[4,32,576]{2,1,0:T(8,128)(2,1)}) custom-call(s32[4]{0:T(128)S(1)} %pad_add_fusion.place, bf16[9,64,128]{2,1,0:T(8,128)(2,1)S(1)} %get-tuple-element.62.refs_0_, bf16[9,64,128]{2,1,0:T(8,128)(2,1)S(1)} %collective-permute-done.1.refs_1_), custom_call_target="tpu_custom_call" | custom-call | flops 1000000 | bytes 737296 | tf_op jit(solution)/shard_map/mod_blocks/pallas_call | solution.py:280
  24.9 0.7 copy-done.7
  25.6 1.5 %collective-permute-start.5 = (bf16[64,4096]{1,0:T(8,128)(2,1)}, bf16[64,4096]{1,0:T(8,128)(2,1)}, u32[]{:S(2)}, u32[]{:S(2)}) collective-permute-start(bf16[64,4096]{1,0:T(8,128)(2,1)} %collective-permute-done.2.refs_1_), channel_id=1, source_target_pairs={{1,2},{2,3},{6,5},{5,4},{9,10},{10,11},{14,13},{13,12},{17,18},{18... | collective-permute-start | bytes 1572872 | tf_op jit(solution)/shard_map/ppermute | solution.py:327
  27.1 1.3 %collective-permute-start.6 = (bf16[64,4096]{1,0:T(8,128)(2,1)}, bf16[64,4096]{1,0:T(8,128)(2,1)}, u32[]{:S(2)}, u32[]{:S(2)}) collective-permute-start(bf16[64,4096]{1,0:T(8,128)(2,1)} %collective-permute-done.3.refs_2_.refs_4_), channel_id=1, source_target_pairs={{1,0},{2,1},{6,7},{5,6},{9,8},{10,9},{14,15},{13,14},{17,16},{18,1... | collective-permute-start | bytes 1572872 | tf_op jit(solution)/shard_map/ppermute | solution.py:327
  28.4 1.0 copy-done.3
  29.5 5.2 %near_grad.1 = (bf16[64,576]{1,0:T(8,128)(2,1)S(1)}, bf16[64,576]{1,0:T(8,128)(2,1)}, bf16[64,576]{1,0:T(8,128)(2,1)S(1)}, bf16[192,5120]{1,0:T(8,128)(2,1)S(1)}) custom-call(bf16[64,4096]{1,0:T(8,128)(2,1)S(1)} %bitcast.38, bf16[64,4096]{1,0:T(8,128)(2,1)} %collective-permute-done.2.refs_1_, bf16[64,4096]{1,0:T(8,128)(2,1)} %collective-permute-done.3.refs_2_.refs_4_, ...), custom_call_target="tpu_custom_call" | custom-call | flops 905969664 | bytes 4415488 | tf_op jit(solution)/shard_map/near_grad/pallas_call | solution.py:280
  34.6 8.8 %all-to-all-start = ((bf16[4,32,576]{2,1,0:T(8,128)(2,1)}), bf16[4,32,576]{2,1,0:T(8,128)(2,1)}, u32[]{:S(2)}, u32[]{:S(2)}) async-start(bf16[4,32,576]{2,1,0:T(8,128)(2,1)} %get-tuple-element.73), calls=%async_computation | async-start | bytes 327680 | tf_op jit(solution)/shard_map/all_to_all | solution.py:397
  43.4 1.3 %collective-permute-start.10 = (bf16[64,576]{1,0:T(8,128)(2,1)}, bf16[64,576]{1,0:T(8,128)(2,1)S(1)}, u32[]{:S(2)}, u32[]{:S(2)}) collective-permute-start(bf16[64,576]{1,0:T(8,128)(2,1)} %get-tuple-element.75), channel_id=1, source_target_pairs={{1,0},{2,1},{3,2},{6,7},{5,6},{4,5},{9,8},{10,9},{11,10},{14,15},{... | collective-permute-start | bytes 221192 | tf_op jit(solution)/shard_map/ppermute | solution.py:327
  44.7 4.6 %collective-permute-start.11 = (bf16[64,576]{1,0:T(8,128)(2,1)S(1)}, bf16[64,576]{1,0:T(8,128)(2,1)S(1)}, u32[]{:S(2)}, u32[]{:S(2)}) collective-permute-start(bf16[64,576]{1,0:T(8,128)(2,1)S(1)} %get-tuple-element.76), channel_id=1, source_target_pairs={{0,1},{1,2},{2,3},{7,6},{6,5},{5,4},{8,9},{9,10},{10,11},{15,14},{... | collective-permute-start | bytes 221192 | tf_op jit(solution)/shard_map/ppermute | solution.py:327
  49.3 0.1 pad_maximum_fusion
  49.4 3.0 %collective-permute-done.7 = f32[1,708]{1,0:T(1,128)S(1)} collective-permute-done((f32[1,708]{1,0:T(1,128)S(1)}, f32[1,708]{1,0:T(1,128)S(1)}, u32[]{:S(2)}, u32[]{:S(2)}) %collective-permute-start.7) | collective-permute-done | bytes 2864 | tf_op jit(solution)/shard_map/ppermute | solution.py:295
  52.4 1.5 %collective-permute-start.8 = (f32[1,708]{1,0:T(1,128)S(1)}, f32[1,708]{1,0:T(1,128)S(1)}, u32[]{:S(2)}, u32[]{:S(2)}) collective-permute-start(f32[1,708]{1,0:T(1,128)S(1)} %broadcast_in_dim.24), channel_id=1, source_target_pairs={{0,8},{4,12},{8,0},{12,4},{1,9},{5,13},{9,1},{13,5},{2,10},{6,14},... | collective-permute-start | bytes 8504 | tf_op jit(solution)/shard_map/ppermute | solution.py:295
  53.9 2.1 %collective-permute-done.8 = f32[1,708]{1,0:T(1,128)S(1)} collective-permute-done((f32[1,708]{1,0:T(1,128)S(1)}, f32[1,708]{1,0:T(1,128)S(1)}, u32[]{:S(2)}, u32[]{:S(2)}) %collective-permute-start.8) | collective-permute-done | bytes 2864 | tf_op jit(solution)/shard_map/ppermute | solution.py:295
  56.0 1.3 %collective-permute-done.9 = f32[1,708]{1,0:T(1,128)S(1)} collective-permute-done((f32[1,708]{1,0:T(1,128)S(1)}, f32[1,708]{1,0:T(1,128)S(1)}, u32[]{:S(2)}, u32[]{:S(2)}) %collective-permute-start.9) | collective-permute-done | bytes 2864 | tf_op jit(solution)/shard_map/ppermute | solution.py:295
  57.3 0.6 copy-done.10
  57.9 0.6 copy-done.12
  58.6 1.5 %collective-permute-start.12 = (bf16[64,4096]{1,0:T(8,128)(2,1)}, bf16[64,4096]{1,0:T(8,128)(2,1)}, u32[]{:S(2)}, u32[]{:S(2)}) collective-permute-start(bf16[64,4096]{1,0:T(8,128)(2,1)} %collective-permute-done.5.refs_0_.refs_2_), channel_id=1, source_target_pairs={{2,3},{5,4},{10,11},{13,12},{18,19},{21,20},{26,27},{29,28}} | collective-permute-start | bytes 1572872 | tf_op jit(solution)/shard_map/ppermute | solution.py:327
  60.0 1.3 %collective-permute-start.13 = (bf16[64,4096]{1,0:T(8,128)(2,1)}, bf16[64,4096]{1,0:T(8,128)(2,1)}, u32[]{:S(2)}, u32[]{:S(2)}) collective-permute-start(bf16[64,4096]{1,0:T(8,128)(2,1)} %collective-permute-done.6.refs_1_.refs_5_), channel_id=1, source_target_pairs={{1,0},{6,7},{9,8},{14,15},{17,16},{22,23},{25,24},{30,31}} | collective-permute-start | bytes 1572872 | tf_op jit(solution)/shard_map/ppermute | solution.py:327
  61.3 1.8 %collective-permute-start.14 = (bf16[4,32,576]{2,1,0:T(8,128)(2,1)}, bf16[4,32,576]{2,1,0:T(8,128)(2,1)}, u32[]{:S(2)}, u32[]{:S(2)}) collective-permute-start(bf16[4,32,576]{2,1,0:T(8,128)(2,1)} %all-to-all-done.refs_7_), channel_id=1, source_target_pairs={{0,16},{16,0},{1,17},{17,1},{2,18},{18,2},{3,19},{19,3},{4,20},{20... | collective-permute-start | bytes 442376 | tf_op jit(solution)/shard_map/ppermute | solution.py:295
  63.1 0.6 scatter_custom_fusion
  63.8 0.6 split.17.sel
  64.4 0.6 split.18.style
  65.0 0.7 split.19
  65.7 0.1 copy.15
  65.8 0.8 copy.16
  66.6 3.9 %middle_grad.1 = bf16[64,576]{1,0:T(8,128)(2,1)S(1)} custom-call(bf16[64,4096]{1,0:T(8,128)(2,1)} %collective-permute-done.5.refs_0_.refs_2_, bf16[64,4096]{1,0:T(8,128)(2,1)} %collective-permute-done.6.refs_1_.refs_5_, bf16[192,5120]{1,0:T(8,128)(2,1)S(1)} %get-tuple-element.79.refs_2_), custom_call_target="tpu_custom_call" | custom-call | flops 301989888 | bytes 3088384 | tf_op jit(solution)/shard_map/middle_grad/pallas_call | solution.py:280
  70.5 3.7 %collective-permute-start.16 = (bf16[64,576]{1,0:T(8,128)(2,1)S(1)}, bf16[64,576]{1,0:T(8,128)(2,1)S(1)}, u32[]{:S(2)}, u32[]{:S(2)}) collective-permute-start(bf16[64,576]{1,0:T(8,128)(2,1)S(1)} %middle_grad.1), channel_id=1, source_target_pairs={{0,2},{1,3},{2,0},{3,1},{7,5},{6,4},{5,7},{4,6},{8,10},{9,11},{10,... | collective-permute-start | bytes 221192 | tf_op jit(solution)/shard_map/ppermute | solution.py:327
  74.2 3.8 %collective-permute-done.13.refs_1_.refs_6_ = bf16[64,4096]{1,0:T(8,128)(2,1)} collective-permute-done((bf16[64,4096]{1,0:T(8,128)(2,1)}, bf16[64,4096]{1,0:T(8,128)(2,1)}, u32[]{:S(2)}, u32[]{:S(2)}) %collective-permute-start.13) | collective-permute-done | bytes 524320 | tf_op jit(solution)/shard_map/ppermute | solution.py:327
  78.0 3.9 %far_grad.1 = bf16[64,576]{1,0:T(8,128)(2,1)S(1)} custom-call(bf16[64,4096]{1,0:T(8,128)(2,1)} %collective-permute-done.12.refs_0_.refs_3_, bf16[64,4096]{1,0:T(8,128)(2,1)} %collective-permute-done.13.refs_1_.refs_6_, bf16[192,5120]{1,0:T(8,128)(2,1)S(1)} %get-tuple-element.79.refs_2_), custom_call_target="tpu_custom_call" | custom-call | flops 301989888 | bytes 3088384 | tf_op jit(solution)/shard_map/far_grad/pallas_call | solution.py:280
  81.9 2.1 %collective-permute-start.15 = (bf16[64,576]{1,0:T(8,128)(2,1)S(1)}, bf16[64,576]{1,0:T(8,128)(2,1)S(1)}, u32[]{:S(2)}, u32[]{:S(2)}) collective-permute-start(bf16[64,576]{1,0:T(8,128)(2,1)S(1)} %far_grad.1), channel_id=1, source_target_pairs={{0,3},{3,0},{4,7},{7,4},{8,11},{11,8},{12,15},{15,12},{16,19},{19,... | collective-permute-start | bytes 221192 | tf_op jit(solution)/shard_map/ppermute | solution.py:443
  84.0 6.2 %collective-permute-done.15.far = bf16[64,576]{1,0:T(8,128)(2,1)S(1)} collective-permute-done((bf16[64,576]{1,0:T(8,128)(2,1)S(1)}, bf16[64,576]{1,0:T(8,128)(2,1)S(1)}, u32[]{:S(2)}, u32[]{:S(2)}) %collective-permute-start.15) | collective-permute-done | bytes 73760 | tf_op jit(solution)/shard_map/ppermute | solution.py:443
  90.2 1.0 collect.1
  91.2 1.8 %collective-permute-start.17 = (bf16[10,64,128]{2,1,0:T(8,128)(2,1)S(1)}, bf16[10,64,128]{2,1,0:T(8,128)(2,1)S(1)}, u32[]{:S(2)}, u32[]{:S(2)}) collective-permute-start(bf16[10,64,128]{2,1,0:T(8,128)(2,1)S(1)} %get-tuple-element.91), channel_id=1, source_target_pairs={{0,16},{16,0},{1,17},{17,1},{2,18},{18,2},{3,19},{19,3},{4,20},{20... | collective-permute-start | bytes 491528 | tf_op jit(solution)/shard_map/ppermute | solution.py:458
  93.1 3.6 %collective-permute-done.17.refs_1_ = bf16[10,64,128]{2,1,0:T(8,128)(2,1)S(1)} collective-permute-done((bf16[10,64,128]{2,1,0:T(8,128)(2,1)S(1)}, bf16[10,64,128]{2,1,0:T(8,128)(2,1)S(1)}, u32[]{:S(2)}, u32[]{:S(2)}) %collective-permute-start.17) | collective-permute-done | bytes 163872 | tf_op jit(solution)/shard_map/ppermute | solution.py:458
  96.6 0.2 row_sum.1.refs_0_
  96.9 0.1 collective-permute-start.19
  97.1 1.6 %collective-permute-start.20 = (bf16[10,64,128]{2,1,0:T(8,128)(2,1)S(1)}, bf16[10,64,128]{2,1,0:T(8,128)(2,1)S(1)}, u32[]{:S(2)}, u32[]{:S(2)}) collective-permute-start(bf16[10,64,128]{2,1,0:T(8,128)(2,1)S(1)} %row_sum.1.refs_0_), channel_id=1, source_target_pairs={{0,12},{4,0},{8,4},{12,8},{1,13},{5,1},{9,5},{13,9},{2,14},{6,2},{... | collective-permute-start | bytes 491528 | tf_op jit(solution)/shard_map/ppermute | solution.py:295
  98.7 5.9 %input_grad.1 = (f32[64,4096]{1,0:T(8,128)S(1)}, f32[64,512]{1,0:T(8,128)S(1)}, f32[64,512]{1,0:T(8,128)S(1)}) custom-call(s32[4]{0:T(128)S(1)} %copy-done.15, bf16[64,4096]{1,0:T(8,128)(2,1)S(1)} %bitcast.39, bf16[64,4096]{1,0:T(8,128)(2,1)} %collective-permute-done.2.refs_1_, bf16[64,4096]{1,0:T(8,128)(2,1)} %collective-permute-done.5.refs_0_.refs_2_, ...), custom_call_target="tpu_custom_call" | custom-call | flops 1207959552 | bytes 5275664 | tf_op jit(solution)/shard_map/input_grad/pallas_call | solution.py:280
  104.7 1.9 %collective-permute-start.21 = (f32[64,512]{1,0:T(8,128)S(1)}, f32[64,512]{1,0:T(8,128)S(1)}, u32[]{:S(2)}, u32[]{:S(2)}) collective-permute-start(f32[64,512]{1,0:T(8,128)S(1)} %broadcast_select_fusion), channel_id=1, source_target_pairs={{0,16},{16,0},{1,17},{17,1},{2,18},{18,2},{3,19},{19,3},{4,20},{20... | collective-permute-start | bytes 393224 | tf_op jit(solution)/shard_map/ppermute | solution.py:302
  106.6 2.8 %bank_grad.1 = (f32[4,9,64,128]{3,2,1,0:T(8,128)}, f32[4,128]{1,0:T(4,128)S(1)}) custom-call(s32[4]{0:T(128)S(1)} %copy-done.15, f32[4,4]{1,0:T(4,128)S(1)} %copy-done.18, f32[4,9,64,128]{3,2,1,0:T(8,128)S(1)} %copy-done.1, f32[4,128]{1,0:T(4,128)S(1)} %copy-done.19, f32[64,4]{1,0:T(8,128)S(1)} %bitcast.40, bf16[10,64,128]{2,1,0:T(8,128)(2,1)S(1)} %row_sum.1.refs_0_, ...), custom_call_target="tpu_custom_call" | custom-call | flops 1000000 | bytes 3019856 | tf_op jit(solution)/shard_map/bank_grad/pallas_call | solution.py:280
  109.5 3.0 %collective-permute-start.23 = (f32[4,128]{1,0:T(4,128)S(1)}, f32[4,128]{1,0:T(4,128)S(1)}, u32[]{:S(2)}, u32[]{:S(2)}) collective-permute-start(f32[4,128]{1,0:T(4,128)S(1)} %get-tuple-element.111.refs_0_), channel_id=1, source_target_pairs={{0,2},{1,3},{2,0},{3,1},{4,6},{5,7},{6,4},{7,5},{8,10},{9,11},{10,... | collective-permute-start | bytes 6152 | tf_op jit(solution)/shard_map/ppermute | solution.py:295
  112.5 0.8 collective-permute-start.24
  113.4 0.6 copy.21
  114.0 0.9 collective-permute-done.22.refs_1_
  114.8 1.3 %collective-permute-done.24.refs_3_ = f32[4,128]{1,0:T(4,128)S(1)} collective-permute-done((f32[4,128]{1,0:T(4,128)S(1)}, f32[4,128]{1,0:T(4,128)S(1)}, u32[]{:S(2)}, u32[]{:S(2)}) %collective-permute-start.24) | collective-permute-done | bytes 2080 | tf_op jit(solution)/shard_map/ppermute | solution.py:295
  116.1 1.6 %affine.1 = (f32[512,128]{1,0:T(8,128)}, f32[1,128]{1,0:T(1,128)}) custom-call(s32[4]{0:T(128)S(1)} %copy-done.15, f32[512,4]{1,0:T(8,128)S(1)} %bitcast.33, f32[4,128]{1,0:T(4,128)S(1)} %get-tuple-element.111.refs_0_, f32[4,128]{1,0:T(4,128)S(1)} %collective-permute-done.22.refs_1_, f32[4,128]{1,0:T(4,128)S(1)} %collective-permute-done.23.refs_2_, ...), custom_call_target="tpu_custom_call" | custom-call | flops 1000000 | bytes 279056 | tf_op jit(solution)/shard_map/affine/pallas_call | solution.py:280
  117.7 0.1 copy.18
  117.9 0.1 copy.17
  118.0 1.1 fusion
  (69 shorter events, 0.4 us)
Async XLA Ops:
  0.6 9.5 %copy-start.9 = (f32[512,128]{1,0:T(8,128)S(1)}, f32[512,128]{1,0:T(8,128)}, u32[]{:S(2)}) copy-start(f32[512,128]{1,0:T(8,128)} %affine_w.1) | copy-start | bytes 786436
  0.6 14.5 %copy-start.21 = (bf16[1,64,8,512]{3,2,1,0:T(8,128)(2,1)S(1)}, bf16[1,64,8,512]{3,2,1,0:T(8,128)(2,1)}, u32[]{:S(2)}) copy-start(bf16[1,64,8,512]{3,2,1,0:T(8,128)(2,1)} %param.7) | copy-start | bytes 1572868
  1.9 13.4 %copy-start.4 = (bf16[8,8,8,512]{3,1,2,0:T(8,128)(2,1)}, bf16[8,8,8,512]{3,1,2,0:T(8,128)(2,1)S(1)}, u32[]{:S(2)}) copy-start(bf16[8,8,8,512]{3,1,2,0:T(8,128)(2,1)S(1)} %copy.19) | copy-start | bytes 1572868
  1.9 23.7 %collective-permute-start.2 = (bf16[64,4096]{1,0:T(8,128)(2,1)S(1)}, bf16[64,4096]{1,0:T(8,128)(2,1)}, u32[]{:S(2)}, u32[]{:S(2)}) collective-permute-start(bf16[64,4096]{1,0:T(8,128)(2,1)S(1)} %bitcast.36), channel_id=1, source_target_pairs={{0,1},{1,2},{2,3},{7,6},{6,5},{5,4},{8,9},{9,10},{10,11},{15,14},{... | collective-permute-start | bytes 1572872 | tf_op jit(solution)/shard_map/ppermute | solution.py:327
  7.7 17.9 %collective-permute-start.3 = (bf16[64,4096]{1,0:T(8,128)(2,1)S(1)}, bf16[64,4096]{1,0:T(8,128)(2,1)}, u32[]{:S(2)}, u32[]{:S(2)}) collective-permute-start(bf16[64,4096]{1,0:T(8,128)(2,1)S(1)} %bitcast.37), channel_id=1, source_target_pairs={{1,0},{2,1},{3,2},{6,7},{5,6},{4,5},{9,8},{10,9},{11,10},{14,15},{... | collective-permute-start | bytes 1572872 | tf_op jit(solution)/shard_map/ppermute | solution.py:327
  10.2 1.3 %copy-start = (f32[4,9,64,128]{3,2,1,0:T(8,128)S(1)}, f32[4,9,64,128]{3,2,1,0:T(8,128)}, u32[]{:S(2)}) copy-start(f32[4,9,64,128]{3,2,1,0:T(8,128)} %bank.5) | copy-start | bytes 3538948
  11.4 0.7 copy-start.16
  12.1 0.7 copy-start.20
  12.8 4.8 %copy-start.1 = (f32[4,9,64,128]{3,2,1,0:T(8,128)S(1)}, f32[4,9,64,128]{3,2,1,0:T(8,128)}, u32[]{:S(2)}) copy-start(f32[4,9,64,128]{3,2,1,0:T(8,128)} %bank.5) | copy-start | bytes 3538948
  13.7 3.9 %collective-permute-start = (f32[64,128]{1,0:T(8,128)S(1)}, f32[64,128]{1,0:T(8,128)S(1)}, u32[]{:S(2)}, u32[]{:S(2)}) collective-permute-start(f32[64,128]{1,0:T(8,128)S(1)} %get-tuple-element.60.refs_0_), channel_id=1, source_target_pairs={{0,16},{16,0},{1,17},{17,1},{2,18},{18,2},{3,19},{19,3},{4,20},{20... | collective-permute-start | bytes 98312 | tf_op jit(solution)/shard_map/ppermute | solution.py:295
  15.4 11.7 %copy-start.2 = (bf16[8,8,8,512]{3,1,2,0:T(8,128)(2,1)}, bf16[8,8,8,512]{3,1,2,0:T(8,128)(2,1)S(1)}, u32[]{:S(2)}) copy-start(bf16[8,8,8,512]{3,1,2,0:T(8,128)(2,1)S(1)} %copy.20) | copy-start | bytes 1572868
  15.4 4.8 %collective-permute-start.4 = (bf16[64,512]{1,0:T(8,128)(2,1)S(1)}, bf16[64,512]{1,0:T(8,128)(2,1)S(1)}, u32[]{:S(2)}, u32[]{:S(2)}) collective-permute-start(bf16[64,512]{1,0:T(8,128)(2,1)S(1)} %slice_select_fusion), channel_id=1, source_target_pairs={{0,16},{16,0},{1,17},{17,1},{2,18},{18,2},{3,19},{19,3},{4,20},{20... | collective-permute-start | bytes 196616 | tf_op jit(solution)/shard_map/ppermute | solution.py:302
  16.1 11.0 %copy-start.14 = (s32[4]{0:T(128)}, s32[4]{0:T(128)S(1)}, u32[]{:S(2)}) copy-start(s32[4]{0:T(128)S(1)} %pad_add_fusion.place) | copy-start | bytes 52
  16.1 12.3 %copy-start.5 = (bf16[8,8,8,512]{3,1,2,0:T(8,128)(2,1)S(1)}, bf16[8,8,8,512]{3,1,2,0:T(8,128)(2,1)}, u32[]{:S(2)}) copy-start(bf16[8,8,8,512]{3,1,2,0:T(8,128)(2,1)} %copy-done.4) | copy-start | bytes 1572868
  18.3 5.3 %collective-permute-start.1 = (bf16[9,64,128]{2,1,0:T(8,128)(2,1)S(1)}, bf16[9,64,128]{2,1,0:T(8,128)(2,1)S(1)}, u32[]{:S(2)}, u32[]{:S(2)}) collective-permute-start(bf16[9,64,128]{2,1,0:T(8,128)(2,1)S(1)} %get-tuple-element.62.refs_0_), channel_id=1, source_target_pairs={{0,16},{16,0},{1,17},{17,1},{2,18},{18,2},{3,19},{19,3},{4,20},{20... | collective-permute-start | bytes 442376 | tf_op jit(solution)/shard_map/ppermute | solution.py:295
  24.9 0.7 copy-start.7
  25.6 23.6 %copy-start.22 = (f32[4]{0:T(128)S(1)}, f32[4]{0:T(128)}, u32[]{:S(2)}) copy-start(f32[4]{0:T(128)} %get-tuple-element.118) | copy-start | bytes 52
  25.6 32.9 %collective-permute-start.5 = (bf16[64,4096]{1,0:T(8,128)(2,1)}, bf16[64,4096]{1,0:T(8,128)(2,1)}, u32[]{:S(2)}, u32[]{:S(2)}) collective-permute-start(bf16[64,4096]{1,0:T(8,128)(2,1)} %collective-permute-done.2.refs_1_), channel_id=1, source_target_pairs={{1,2},{2,3},{6,5},{5,4},{9,10},{10,11},{14,13},{13,12},{17,18},{18... | collective-permute-start | bytes 1572872 | tf_op jit(solution)/shard_map/ppermute | solution.py:327
  27.1 31.5 %collective-permute-start.6 = (bf16[64,4096]{1,0:T(8,128)(2,1)}, bf16[64,4096]{1,0:T(8,128)(2,1)}, u32[]{:S(2)}, u32[]{:S(2)}) collective-permute-start(bf16[64,4096]{1,0:T(8,128)(2,1)} %collective-permute-done.3.refs_2_.refs_4_), channel_id=1, source_target_pairs={{1,0},{2,1},{6,7},{5,6},{9,8},{10,9},{14,15},{13,14},{17,16},{18,1... | collective-permute-start | bytes 1572872 | tf_op jit(solution)/shard_map/ppermute | solution.py:327
  28.4 1.0 copy-start.3
  29.5 19.8 %copy-start.17 = (f32[1,512]{1,0:T(1,128)S(1)}, f32[1,512]{1,0:T(1,128)}, u32[]{:S(2)}) copy-start(f32[1,512]{1,0:T(1,128)} %latent.1) | copy-start | bytes 6148
  34.6 23.9 %all-to-all-start = ((bf16[4,32,576]{2,1,0:T(8,128)(2,1)}), bf16[4,32,576]{2,1,0:T(8,128)(2,1)}, u32[]{:S(2)}, u32[]{:S(2)}) async-start(bf16[4,32,576]{2,1,0:T(8,128)(2,1)} %get-tuple-element.73), calls=%async_computation | async-start | bytes 327680 | tf_op jit(solution)/shard_map/all_to_all | solution.py:397
  43.4 13.9 %collective-permute-start.10 = (bf16[64,576]{1,0:T(8,128)(2,1)}, bf16[64,576]{1,0:T(8,128)(2,1)S(1)}, u32[]{:S(2)}, u32[]{:S(2)}) collective-permute-start(bf16[64,576]{1,0:T(8,128)(2,1)} %get-tuple-element.75), channel_id=1, source_target_pairs={{1,0},{2,1},{3,2},{6,7},{5,6},{4,5},{9,8},{10,9},{11,10},{14,15},{... | collective-permute-start | bytes 221192 | tf_op jit(solution)/shard_map/ppermute | solution.py:327
  44.7 13.3 %collective-permute-start.11 = (bf16[64,576]{1,0:T(8,128)(2,1)S(1)}, bf16[64,576]{1,0:T(8,128)(2,1)S(1)}, u32[]{:S(2)}, u32[]{:S(2)}) collective-permute-start(bf16[64,576]{1,0:T(8,128)(2,1)S(1)} %get-tuple-element.76), channel_id=1, source_target_pairs={{0,1},{1,2},{2,3},{7,6},{6,5},{5,4},{8,9},{9,10},{10,11},{15,14},{... | collective-permute-start | bytes 221192 | tf_op jit(solution)/shard_map/ppermute | solution.py:327
  49.3 3.0 %collective-permute-start.7 = (f32[1,708]{1,0:T(1,128)S(1)}, f32[1,708]{1,0:T(1,128)S(1)}, u32[]{:S(2)}, u32[]{:S(2)}) collective-permute-start(f32[1,708]{1,0:T(1,128)S(1)} %broadcast_in_dim.24), channel_id=1, source_target_pairs={{0,4},{4,8},{8,12},{12,0},{1,5},{5,9},{9,13},{13,1},{2,6},{6,10},{... | collective-permute-start | bytes 8504 | tf_op jit(solution)/shard_map/ppermute | solution.py:295
  52.4 3.6 %collective-permute-start.8 = (f32[1,708]{1,0:T(1,128)S(1)}, f32[1,708]{1,0:T(1,128)S(1)}, u32[]{:S(2)}, u32[]{:S(2)}) collective-permute-start(f32[1,708]{1,0:T(1,128)S(1)} %broadcast_in_dim.24), channel_id=1, source_target_pairs={{0,8},{4,12},{8,0},{12,4},{1,9},{5,13},{9,1},{13,5},{2,10},{6,14},... | collective-permute-start | bytes 8504 | tf_op jit(solution)/shard_map/ppermute | solution.py:295
  56.0 1.3 %collective-permute-start.9 = (f32[1,708]{1,0:T(1,128)S(1)}, f32[1,708]{1,0:T(1,128)S(1)}, u32[]{:S(2)}, u32[]{:S(2)}) collective-permute-start(f32[1,708]{1,0:T(1,128)S(1)} %broadcast_in_dim.24), channel_id=1, source_target_pairs={{0,12},{4,0},{8,4},{12,8},{1,13},{5,1},{9,5},{13,9},{2,14},{6,2},{... | collective-permute-start | bytes 8504 | tf_op jit(solution)/shard_map/ppermute | solution.py:295
  57.3 0.6 copy-start.10
  57.9 0.6 copy-start.12
  58.6 15.6 %collective-permute-start.12 = (bf16[64,4096]{1,0:T(8,128)(2,1)}, bf16[64,4096]{1,0:T(8,128)(2,1)}, u32[]{:S(2)}, u32[]{:S(2)}) collective-permute-start(bf16[64,4096]{1,0:T(8,128)(2,1)} %collective-permute-done.5.refs_0_.refs_2_), channel_id=1, source_target_pairs={{2,3},{5,4},{10,11},{13,12},{18,19},{21,20},{26,27},{29,28}} | collective-permute-start | bytes 1572872 | tf_op jit(solution)/shard_map/ppermute | solution.py:327
  60.0 17.9 %collective-permute-start.13 = (bf16[64,4096]{1,0:T(8,128)(2,1)}, bf16[64,4096]{1,0:T(8,128)(2,1)}, u32[]{:S(2)}, u32[]{:S(2)}) collective-permute-start(bf16[64,4096]{1,0:T(8,128)(2,1)} %collective-permute-done.6.refs_1_.refs_5_), channel_id=1, source_target_pairs={{1,0},{6,7},{9,8},{14,15},{17,16},{22,23},{25,24},{30,31}} | collective-permute-start | bytes 1572872 | tf_op jit(solution)/shard_map/ppermute | solution.py:327
  61.3 12.9 %collective-permute-start.14 = (bf16[4,32,576]{2,1,0:T(8,128)(2,1)}, bf16[4,32,576]{2,1,0:T(8,128)(2,1)}, u32[]{:S(2)}, u32[]{:S(2)}) collective-permute-start(bf16[4,32,576]{2,1,0:T(8,128)(2,1)} %all-to-all-done.refs_7_), channel_id=1, source_target_pairs={{0,16},{16,0},{1,17},{17,1},{2,18},{18,2},{3,19},{19,3},{4,20},{20... | collective-permute-start | bytes 442376 | tf_op jit(solution)/shard_map/ppermute | solution.py:295
  70.5 13.5 %collective-permute-start.16 = (bf16[64,576]{1,0:T(8,128)(2,1)S(1)}, bf16[64,576]{1,0:T(8,128)(2,1)S(1)}, u32[]{:S(2)}, u32[]{:S(2)}) collective-permute-start(bf16[64,576]{1,0:T(8,128)(2,1)S(1)} %middle_grad.1), channel_id=1, source_target_pairs={{0,2},{1,3},{2,0},{3,1},{7,5},{6,4},{5,7},{4,6},{8,10},{9,11},{10,... | collective-permute-start | bytes 221192 | tf_op jit(solution)/shard_map/ppermute | solution.py:327
  78.0 12.2 %copy-start.8 = (bf16[9,64,256]{2,1,0:T(8,128)(2,1)S(1)}, bf16[9,64,256]{2,1,0:T(8,128)(2,1)}, u32[]{:S(2)}) copy-start(bf16[9,64,256]{2,1,0:T(8,128)(2,1)} %copy-done.7) | copy-start | bytes 884740
  78.0 12.2 %copy-start.11 = (bf16[64,576]{1,0:T(8,128)(2,1)S(1)}, bf16[64,576]{1,0:T(8,128)(2,1)}, u32[]{:S(2)}) copy-start(bf16[64,576]{1,0:T(8,128)(2,1)} %copy-done.10) | copy-start | bytes 221188
  78.0 12.2 %copy-start.13 = (bf16[64,576]{1,0:T(8,128)(2,1)S(1)}, bf16[64,576]{1,0:T(8,128)(2,1)}, u32[]{:S(2)}) copy-start(bf16[64,576]{1,0:T(8,128)(2,1)} %copy-done.12) | copy-start | bytes 221188
  78.0 12.2 %copy-start.15 = (s32[4]{0:T(128)S(1)}, s32[4]{0:T(128)}, u32[]{:S(2)}) copy-start(s32[4]{0:T(128)} %copy-done.14) | copy-start | bytes 52
  81.9 16.8 %copy-start.6 = (bf16[8,8,8,512]{3,1,2,0:T(8,128)(2,1)S(1)}, bf16[8,8,8,512]{3,1,2,0:T(8,128)(2,1)}, u32[]{:S(2)}) copy-start(bf16[8,8,8,512]{3,1,2,0:T(8,128)(2,1)} %copy-done.4) | copy-start | bytes 1572868
  81.9 8.3 %collective-permute-start.15 = (bf16[64,576]{1,0:T(8,128)(2,1)S(1)}, bf16[64,576]{1,0:T(8,128)(2,1)S(1)}, u32[]{:S(2)}, u32[]{:S(2)}) collective-permute-start(bf16[64,576]{1,0:T(8,128)(2,1)S(1)} %far_grad.1), channel_id=1, source_target_pairs={{0,3},{3,0},{4,7},{7,4},{8,11},{11,8},{12,15},{15,12},{16,19},{19,... | collective-permute-start | bytes 221192 | tf_op jit(solution)/shard_map/ppermute | solution.py:443
  91.2 5.4 %collective-permute-start.17 = (bf16[10,64,128]{2,1,0:T(8,128)(2,1)S(1)}, bf16[10,64,128]{2,1,0:T(8,128)(2,1)S(1)}, u32[]{:S(2)}, u32[]{:S(2)}) collective-permute-start(bf16[10,64,128]{2,1,0:T(8,128)(2,1)S(1)} %get-tuple-element.91), channel_id=1, source_target_pairs={{0,16},{16,0},{1,17},{17,1},{2,18},{18,2},{3,19},{19,3},{4,20},{20... | collective-permute-start | bytes 491528 | tf_op jit(solution)/shard_map/ppermute | solution.py:458
  96.8 9.8 %copy-start.18 = (f32[4,4]{1,0:T(4,128)S(1)}, f32[4,4]{1,0:T(4,128)}, u32[]{:S(2)}) copy-start(f32[4,4]{1,0:T(4,128)} %split.17.sel) | copy-start | bytes 196
  96.8 9.8 %copy-start.19 = (f32[4,128]{1,0:T(4,128)S(1)}, f32[4,128]{1,0:T(4,128)}, u32[]{:S(2)}) copy-start(f32[4,128]{1,0:T(4,128)} %split.18.style) | copy-start | bytes 6148
  96.9 7.8 %collective-permute-start.18 = (bf16[10,64,128]{2,1,0:T(8,128)(2,1)S(1)}, bf16[10,64,128]{2,1,0:T(8,128)(2,1)S(1)}, u32[]{:S(2)}, u32[]{:S(2)}) collective-permute-start(bf16[10,64,128]{2,1,0:T(8,128)(2,1)S(1)} %row_sum.1.refs_0_), channel_id=1, source_target_pairs={{0,4},{4,8},{8,12},{12,0},{1,5},{5,9},{9,13},{13,1},{2,6},{6,10},{... | collective-permute-start | bytes 491528 | tf_op jit(solution)/shard_map/ppermute | solution.py:295
  96.9 7.7 %collective-permute-start.19 = (bf16[10,64,128]{2,1,0:T(8,128)(2,1)S(1)}, bf16[10,64,128]{2,1,0:T(8,128)(2,1)S(1)}, u32[]{:S(2)}, u32[]{:S(2)}) collective-permute-start(bf16[10,64,128]{2,1,0:T(8,128)(2,1)S(1)} %row_sum.1.refs_0_), channel_id=1, source_target_pairs={{0,8},{4,12},{8,0},{12,4},{1,9},{5,13},{9,1},{13,5},{2,10},{6,14},... | collective-permute-start | bytes 491528 | tf_op jit(solution)/shard_map/ppermute | solution.py:295
  97.1 7.6 %collective-permute-start.20 = (bf16[10,64,128]{2,1,0:T(8,128)(2,1)S(1)}, bf16[10,64,128]{2,1,0:T(8,128)(2,1)S(1)}, u32[]{:S(2)}, u32[]{:S(2)}) collective-permute-start(bf16[10,64,128]{2,1,0:T(8,128)(2,1)S(1)} %row_sum.1.refs_0_), channel_id=1, source_target_pairs={{0,12},{4,0},{8,4},{12,8},{1,13},{5,1},{9,5},{13,9},{2,14},{6,2},{... | collective-permute-start | bytes 491528 | tf_op jit(solution)/shard_map/ppermute | solution.py:295
  104.7 13.0 %collective-permute-start.21 = (f32[64,512]{1,0:T(8,128)S(1)}, f32[64,512]{1,0:T(8,128)S(1)}, u32[]{:S(2)}, u32[]{:S(2)}) collective-permute-start(f32[64,512]{1,0:T(8,128)S(1)} %broadcast_select_fusion), channel_id=1, source_target_pairs={{0,16},{16,0},{1,17},{17,1},{2,18},{18,2},{3,19},{19,3},{4,20},{20... | collective-permute-start | bytes 393224 | tf_op jit(solution)/shard_map/ppermute | solution.py:302
  109.5 5.4 %collective-permute-start.22 = (f32[4,128]{1,0:T(4,128)S(1)}, f32[4,128]{1,0:T(4,128)S(1)}, u32[]{:S(2)}, u32[]{:S(2)}) collective-permute-start(f32[4,128]{1,0:T(4,128)S(1)} %get-tuple-element.111.refs_0_), channel_id=1, source_target_pairs={{0,1},{1,2},{2,3},{3,0},{4,5},{5,6},{6,7},{7,4},{8,9},{9,10},{10,1... | collective-permute-start | bytes 6152 | tf_op jit(solution)/shard_map/ppermute | solution.py:295
  109.5 5.4 %collective-permute-start.23 = (f32[4,128]{1,0:T(4,128)S(1)}, f32[4,128]{1,0:T(4,128)S(1)}, u32[]{:S(2)}, u32[]{:S(2)}) collective-permute-start(f32[4,128]{1,0:T(4,128)S(1)} %get-tuple-element.111.refs_0_), channel_id=1, source_target_pairs={{0,2},{1,3},{2,0},{3,1},{4,6},{5,7},{6,4},{7,5},{8,10},{9,11},{10,... | collective-permute-start | bytes 6152 | tf_op jit(solution)/shard_map/ppermute | solution.py:295
  112.5 3.6 %collective-permute-start.24 = (f32[4,128]{1,0:T(4,128)S(1)}, f32[4,128]{1,0:T(4,128)S(1)}, u32[]{:S(2)}, u32[]{:S(2)}) collective-permute-start(f32[4,128]{1,0:T(4,128)S(1)} %get-tuple-element.111.refs_0_), channel_id=1, source_target_pairs={{0,3},{1,0},{2,1},{3,2},{4,7},{5,4},{6,5},{7,6},{8,11},{9,8},{10,9... | collective-permute-start | bytes 6152 | tf_op jit(solution)/shard_map/ppermute | solution.py:295

commit v5 on v4

--- a/solution.py
+++ b/solution.py
@@ -35,10 +35,14 @@
 
 
 def mixed(bank_ref, sel, sample, tap):
-    total = sel[sample, 0] * bank_ref[0, tap]
+    total = sel[sample][0] * bank_ref[0, tap]
     for k in range(1, bank_ref.shape[0]):
-        total = total + sel[sample, k] * bank_ref[k, tap]
+        total = total + sel[sample][k] * bank_ref[k, tap]
     return total
+
+
+def own_select(sel_ref):
+    return [[sel_ref[0, k].astype(F32) for k in range(sel_ref.shape[1])]]
 
 
 def energy_kernel(sel, bank, latent, affine_w, affine_b, style_out, energy_out):
@@ -48,6 +52,7 @@
     )
     style_out[...] = style
     total = jnp.zeros(bank.shape[2:], F32)
+    sel = own_select(sel)
     for tap in range(TAPS):
         plain = mixed(bank, sel, 0, tap) * style
         total = total + plain * plain
@@ -63,6 +68,7 @@
     scale_out[...] = scales
     row_out[...] = scales.T[0:1]
     scale = scales[:, 0:1]
+    sel = own_select(sel)
     for tap in range(TAPS):
         mod_out[tap] = (mixed(bank, sel, 0, tap) * style[...] * scale).astype(BF16)
 
@@ -129,15 +135,9 @@
         out[...] = whole[at * ch : (at + 1) * ch]
 
 
-def far_grad_kernel(count, height, width, *refs):
-    first, second, wide = refs[:count], refs[count : 2 * count], refs[2 * count]
-    outs, (gathered, total) = refs[2 * count + 1 : 3 * count + 1], refs[3 * count + 1 :]
-    ch = outs[0].shape[0]
-    for at in range(count):
-        gathered[at * ch : (at + 1) * ch] = first[at][...] + second[at][...]
-    whole = tap_products(gathered, wide, total, height, width).astype(BF16)
-    for at, out in enumerate(outs):
-        out[...] = whole[at * ch : (at + 1) * ch]
+def far_grad_kernel(height, width, first, second, wide, out, gathered, total):
+    gathered[...] = first[...] + second[...]
+    out[...] = tap_products(gathered, wide, total, height, width).astype(BF16)
 
 
 def input_grad_kernel(rows, size, shares, height, width, place, *refs):
@@ -180,6 +180,19 @@
     return high, mid, x - high - mid
 
 
+def middle_grad_kernel(size, height, width, place, *refs):
+    count = size - 3
+    first, second, (wide, own, before, after) = refs[:count], refs[count : 2 * count], refs[2 * count : 2 * count + 4]
+    out, gathered, total = refs[2 * count + 4 :]
+    ch = own.shape[0]
+    for at in range(count):
+        gathered[at * ch : (at + 1) * ch] = first[at][...] + second[at][...]
+    whole = tap_products(gathered, wide, total, height, width).astype(BF16)
+    slots = [own[...], before[...]] + [whole[at * ch : (at + 1) * ch] for at in range(count)] + [after[...]]
+    for d, value in enumerate(slots):
+        out[lax.rem(place[1] - place[3] * d + size, size)] = value
+
+
 def put_fall(out, fall):
     lane = lax.broadcasted_iota(jnp.int32, out.shape[1:], 1)
     last = jnp.zeros(out.shape[1:], F32)
@@ -193,12 +206,10 @@
     return last[:, 0:1] + last[:, 1:2] + last[:, 2:3]
 
 
-def collect_kernel(rows, size, place, scale, whole_mod, far, *refs):
-    nears, outs = refs[:size], refs[size : size + rows]
-    by_chan, by_row = refs[size + rows :]
-    chan_at, row_at, sign = place[1], place[2], place[3]
-    for d in range(size):
-        by_chan[lax.rem(chan_at + sign * d + size, size)] = nears[d][...].astype(F32)
+def collect_kernel(rows, size, place, scale, whole_mod, far, near, *refs):
+    outs, (by_chan, by_row) = refs[:rows], refs[rows:]
+    chan_at, row_at = place[1], place[2]
+    by_chan[...] = near[...].astype(F32)
     by_chan[jnp.where(chan_at == 0, size - 1, 0)] += far[...].astype(F32)
     ch = whole_mod.shape[2] // size
     in_ch = outs[0].shape[2]
@@ -227,60 +238,70 @@
     put_fall(out, fall)
 
 
-def bank_grad_kernel(samples, place, sel, bank, style, scales, *refs):
-    parts = refs[:samples]
-    bank_grad, style_grad, held = refs[samples:]
+def bank_grad_kernel(samples, starts, place, bank, *refs):
+    parts, smalls = refs[:samples], refs[samples : 2 * samples]
+    bank_grad, style_grad, held, small = refs[2 * samples :]
     sample = place[0]
     for s in range(samples):
         held[lax.rem(sample - s + samples, samples)] = parts[s][...]
-    styles, every_scale = style[...], scales[...]
-    falls = []
+        small[lax.rem(sample - s + samples, samples)] = smalls[s][...]
+    filters, out_ch, in_ch = bank.shape[0], bank.shape[2], bank.shape[3]
+    at_style, at_scale, at_sel = starts
+    sel, styles, scales, falls = [], [], [], []
     for b in range(samples):
+        row = small[b]
+        sel.append([row[:, at_sel + k : at_sel + k + 1] for k in range(filters)])
+        styles.append(row[:, at_style : at_style + in_ch])
+        across = jnp.broadcast_to(row[:, at_scale : at_scale + 128], (128, 128))
+        scales.append(across.T[:out_ch, 0:1])
         falls.append(get_fall(held[b, TAPS]))
     sums = [jnp.zeros(bank.shape[2:], F32) for _ in range(samples)]
     for tap in range(TAPS):
-        totals = [None] * bank.shape[0]
+        totals = [None] * filters
         for b in range(samples):
             kern = mixed(bank, sel, b, tap)
-            own_style = styles[b : b + 1]
-            plain_grad = held[b, tap].astype(F32) * every_scale[:, b : b + 1] - kern * own_style * falls[b]
+            plain_grad = held[b, tap].astype(F32) * scales[b] - kern * styles[b] * falls[b]
             sums[b] = sums[b] + plain_grad * kern
-            kernel_grad = plain_grad * own_style
-            for k in range(bank.shape[0]):
-                term = sel[b, k] * kernel_grad
+            kernel_grad = plain_grad * styles[b]
+            for k in range(filters):
+                term = sel[b][k] * kernel_grad
                 totals[k] = term if totals[k] is None else totals[k] + term
-        for k in range(bank.shape[0]):
+        for k in range(filters):
             bank_grad[k, tap] = totals[k]
     for b in range(samples):
-        style_grad[b : b + 1] = jnp.sum(sums[b], axis=0, keepdims=True)
-
-
-def affine_kernel(size, place, latent_t, *refs):
-    parts, w_grad, b_grad, held = refs[:size], refs[size], refs[size + 1], refs[size + 2]
-    for d in range(size):
-        held[lax.rem(place[1] - d + size, size)] = parts[d][...]
-    style_grad = held[0]
-    for z in range(1, size):
-        style_grad = style_grad + held[z]
-    columns = latent_t[...]
-    samples = style_grad.shape[0]
-    total, bias = None, None
-    for b in range(samples):
-        row = style_grad[b : b + 1]
-        term = columns[:, b : b + 1] * row
-        total = term if total is None else total + term
-        bias = row if bias is None else bias + row
-    w_grad[...] = total
+        value = jnp.sum(sums[b], axis=0, keepdims=True)
+        for z in range(style_grad.shape[0]):
+            style_grad[z, b : b + 1] = value
+
+
+def affine_kernel(samples, place, parts, *refs):
+    smalls, w_grad, b_grad, latents = refs[:samples], *refs[samples:]
+    for s in range(samples):
+        at = lax.rem(place[0] - s + samples, samples)
+        latents[pl.ds(at, 1)] = smalls[s][:, : latents.shape[1]]
+    style_grad = parts[0]
+    for z in range(1, parts.shape[0]):
+        style_grad = style_grad + parts[z]
+    w_grad[...] = lax.dot_general(
+        latents[...],
+        style_grad,
+        (((0,), (0,)), ((), ())),
+        precision=lax.Precision.HIGHEST,
+        preferred_element_type=F32,
+    )
+    bias = style_grad[0:1]
+    for b in range(1, samples):
+        bias = bias + style_grad[b : b + 1]
     b_grad[...] = bias
 
 
-def call(kernel, name, outs, *operands, scalars=0, scratch=(), flops=10**6):
+def call(kernel, name, outs, *operands, scalars=0, fetched=0, scratch=(), flops=10**6):
     outs = tuple(jax.ShapeDtypeStruct(*o) for o in outs)
     moved = sum(o.size * o.dtype.itemsize for o in (*outs, *operands))
     return pl.pallas_call(
         kernel,
         out_shape=outs,
-        in_specs=sspec(scalars) + vspec(len(operands) - scalars),
+        in_specs=sspec(scalars) + [pl.BlockSpec()] * fetched + vspec(len(operands) - scalars - fetched),
         out_specs=tuple(vspec(len(outs))),
         scratch_shapes=[pltpu.VMEM(*s) for s in scratch],
         compiler_params=params(),
@@ -337,45 +358,51 @@
 
     feat = feature[0].reshape(ch, pixels)
     feat_before, feat_after = from_sides(feat[:, :width], feat[:, pixels - width :], "rows")
-    own_sel = select.astype(F32)
     style, energy = call(
         energy_kernel,
         "energy",
         [((1, in_ch), F32), ((out_ch, 128), F32)],
-        own_sel,
+        select,
         bank,
         latent,
         affine_w,
         affine_b[None],
         scalars=1,
+        fetched=4,
     )
     mod_own, scale, scale_row = call(
         modulated_kernel,
         "modulated",
         [((TAPS, out_ch, in_ch), BF16), ((out_ch, 128), F32), ((1, out_ch), F32)],
-        own_sel,
+        select,
         bank,
         style,
         *exchange(energy, "rows"),
         scalars=1,
-    )
+        fetched=1,
+    )
+    pieces, starts, at = [], [], 0
+    for piece in (latent, style, scale_row, select.astype(F32)):
+        length = -(-piece.shape[1] // 128) * 128
+        pieces.append(jnp.pad(piece, ((0, 0), (0, length - piece.shape[1]))))
+        starts.append(at)
+        at += length
+    smalls = exchange(jnp.concatenate(pieces, axis=1), "samples")
+    first[0], second[0], smalls, feat_before, feat_after = lax.optimization_barrier(
+        (first[0], second[0], smalls, feat_before, feat_after)
+    )
+
+    step(2, first[0], second[0])
     message = ((ch, TAPS * ch), BF16)
-    shares = rows if ch % (16 * rows) == 0 else 1
-    share = (ch // shares, TAPS * ch)
     whole_mod, to_send = call(
-        functools.partial(blocks_kernel, rows, size, shares),
+        functools.partial(blocks_kernel, rows, size, 1),
         "mod_blocks",
-        [((TAPS, out_ch, all_ch), BF16), ((size, *share), BF16)],
+        [((TAPS, out_ch, all_ch), BF16), ((size, *message[0]), BF16)],
         place,
         *exchange(mod_own, "rows"),
         scalars=1,
-        scratch=[((rows, TAPS, out_ch, in_ch), BF16), ((shares, size, *share), BF16)],
-    )
-    first[0], second[0], to_send, feat_before, feat_after = lax.optimization_barrier(
-        (first[0], second[0], to_send, feat_before, feat_after)
-    )
-
-    step(2, first[0], second[0])
+        scratch=[((rows, TAPS, out_ch, in_ch), BF16), ((1, size, *message[0]), BF16)],
+    )
     *near, wide = call(
         functools.partial(near_grad_kernel, size, height, width),
         "near_grad",
@@ -389,49 +416,30 @@
         scratch=[((3 * ch, pixels), BF16), ((3, 3 * ch, 3 * ch), F32)],
         flops=flops * 3 // size,
     )
-    near, to_send = lax.optimization_barrier((near, to_send))
-    got = [None] * size
-    got[0] = near[0]
-    got[1] = along(near[1], [(i, i - 1) for i in range(1, size)])
-    got[size - 1] = along(near[2], [(i, i + 1) for i in range(size - 1)])
-    mods = lax.all_to_all(to_send, "chan", 0, 0)
-    small = jnp.concatenate([latent[0], own_sel[0], style[0], scale_row[0]])[None]
-    smalls = exchange(small, "samples")
-    first[1], second[1], mods, smalls, got[1], got[size - 1] = lax.optimization_barrier(
-        (first[1], second[1], mods, smalls, got[1], got[size - 1])
-    )
-    at = jnp.remainder(sample_at - jnp.arange(samples), samples)
-    every = jnp.zeros((samples, small.shape[1]), F32).at[at].set(jnp.concatenate(smalls, axis=0))
-    ends = [latent.shape[1], latent.shape[1] + select.shape[1]]
-    latents, sel, styles, scales = jnp.split(every, ends + [ends[1] + in_ch], axis=1)
-    tables = latents.T, sel, styles, scales.T
+    first[1], second[1], near, to_send, whole_mod = lax.optimization_barrier(
+        (first[1], second[1], near, to_send, whole_mod)
+    )
 
     for number in range(3, size):
         step(number, first[number - 2], second[number - 2])
-    mods = exchange(mods, "rows") if shares > 1 else [mods]
-
-    def far_grad(slots, name):
-        return call(
-            functools.partial(far_grad_kernel, len(slots), height, width),
-            name,
-            [message] * len(slots),
-            *[first[d - 1] for d in slots],
-            *[second[size - d - 1] for d in slots],
-            wide,
-            scratch=[((len(slots) * ch, pixels), BF16), ((3, len(slots) * ch, 3 * ch), F32)],
-            flops=flops * len(slots) // size,
-        )
-
-    between = list(range(2, size - 1))
-    middle = far_grad(between, "middle_grad")
-    for d, part in zip(between, middle):
-        got[d] = along(part, [(i, (i - d) % size) for i in range(size)])
-    first[-1], second[-1], middle, tables, mods = lax.optimization_barrier(
-        (first[-1], second[-1], middle, tables, mods)
-    )
-    latents, sel, styles, scales = tables
+    between = range(2, size - 1)
+    (near,) = call(
+        functools.partial(middle_grad_kernel, size, height, width),
+        "middle_grad",
+        [((size, *message[0]), BF16)],
+        place,
+        *[first[d - 1] for d in between],
+        *[second[size - d - 1] for d in between],
+        wide,
+        *near,
+        scalars=1,
+        scratch=[((len(between) * ch, pixels), BF16), ((3, len(between) * ch, 3 * ch), F32)],
+        flops=flops * len(between) // size,
+    )
+    near_got = lax.all_to_all(near, "chan", 0, 0)
+    first[-1], second[-1], near = lax.optimization_barrier((first[-1], second[-1], near))
     (far,) = call(
-        functools.partial(far_grad_kernel, 1, height, width),
+        functools.partial(far_grad_kernel, height, width),
         "far_grad",
         [message],
         first[-1],
@@ -442,6 +450,8 @@
     )
     far_got = lax.ppermute(far, "chan", [(0, size - 1), (size - 1, 0)])
 
+    far_got, to_send = lax.optimization_barrier((far_got, to_send))
+    mods = lax.all_to_all(to_send, "chan", 0, 0)
     parts = call(
         functools.partial(collect_kernel, rows, size),
         "collect",
@@ -450,7 +460,7 @@
         scale,
         whole_mod,
         far_got,
-        *got,
+        near_got,
         scalars=1,
         scratch=[((size, *message[0]), F32), ((rows, TAPS, out_ch, in_ch), BF16)],
     )
@@ -463,52 +473,52 @@
 
     own, mods = lax.optimization_barrier((own, mods))
     main, before, after = call(
-        functools.partial(input_grad_kernel, rows, size, shares, height, width),
+        functools.partial(input_grad_kernel, rows, size, 1, height, width),
         "input_grad",
         [((ch, pixels), F32), ((ch, width), F32), ((ch, width), F32)],
         place,
         cotan,
         *first,
         *second,
-        *mods,
+        mods,
         scalars=1,
         scratch=[
             ((all_ch, pixels), BF16),
-            ((size, shares, *share), F32),
+            ((size, 1, *message[0]), F32),
             ((TAPS * ch, all_ch), BF16),
             ((height + 2, 3 * ch, width), F32),
         ],
         flops=flops,
     )
     every, main, before, after = lax.optimization_barrier((every, main, before, after))
+    bank_grad, style_parts = call(
+        functools.partial(bank_grad_kernel, samples, starts[1:]),
+        "bank_grad",
+        [(bank.shape, F32), ((size, samples, in_ch), F32)],
+        place,
+        bank,
+        *every,
+        *smalls,
+        scalars=1,
+        fetched=1,
+        scratch=[((samples, TAPS + 1, out_ch, in_ch), BF16), ((samples, *smalls[0].shape), F32)],
+    )
+    style_parts, before, after = lax.optimization_barrier((style_parts, before, after))
+    style_parts = lax.all_to_all(style_parts, "chan", 0, 0)
     from_above, from_below = from_sides(before, after, "rows")
     edge = jnp.concatenate(
         [from_above[:, None], jnp.zeros((ch, height - 2, width), F32), from_below[:, None]], axis=1
     )
     feature_grad = (main.reshape(ch, height, width) + edge).astype(BF16)[None]
-
-    bank_grad, style_part = call(
-        functools.partial(bank_grad_kernel, samples),
-        "bank_grad",
-        [(bank.shape, F32), ((samples, in_ch), F32)],
-        place,
-        sel,
-        bank,
-        styles,
-        scales,
-        *every,
-        scalars=2,
-        scratch=[((samples, TAPS + 1, out_ch, in_ch), BF16)],
-    )
     affine_w_grad, affine_b_grad = call(
-        functools.partial(affine_kernel, size),
+        functools.partial(affine_kernel, samples),
         "affine",
         [(affine_w.shape, F32), ((1, in_ch), F32)],
         place,
-        latents,
-        *exchange(style_part, "chan"),
-        scalars=1,
-        scratch=[((size, samples, in_ch), F32)],
+        style_parts,
+        *smalls,
+        scalars=1,
+        scratch=[((samples, latent.shape[1]), F32)],
     )
     return (feature_grad, bank_grad, affine_w_grad, affine_b_grad[0])
 

time: 120 us -> 114 us (0.950)
  starting transfers between devices: 49.6 us -> 44.7 us
  other arithmetic: 3.13 us -> 1.3 us
  local copies, waits for them, and re-layouts: 10.9 us -> 12.6 us
  Pallas kernels: 27.5 us -> 26.2 us
    all_to_all x0 -> x2, starting transfers between devices: none -> 13.4 us  [the longest x1 8.32 us: on_device(): near_got = lax.all_to_all(near, 'chan', 0, 0)]
    ppermute x9 -> x6, starting transfers between devices: 22.1 us -> 12.5 us  [along(): return lax.ppermute(x, ('samples', 'chan'), whole)]
    ppermute x12 -> x8, waiting for transfers between devices: 13.4 us -> 7.33 us  [exchange(): lax.ppermute(x, axis, [(i, (i + s) % size) for i in range(size)])]
    all_to_all x1, starting transfers between devices: 8.77 us -> 3.45 us  [on_device(): mods = lax.all_to_all(to_send, 'chan', 0, 0)]
    all_to_all x0 -> x2, waiting for transfers between devices: none -> 4.91 us  [the longest x1 4.9 us: on_device(): style_parts = lax.all_to_all(style_parts, 'chan', 0, 0)]
    unnamed x49 -> x43, local copies, waits for them, and re-layouts: 7.74 us -> 12.2 us
    ppermute x12 -> x8, starting transfers between devices: 12.4 us -> 8.3 us  [exchange(): lax.ppermute(x, axis, [(i, (i + s) % size) for i in range(size)])]
    split x6 -> x0, local copies, waits for them, and re-layouts: 2.82 us -> none  [on_device(): jnp.split(every, ends + [ends[1] + in_ch], axis=1)]
  transfers between devices with their start and end apart: 26 -> 21, of which waited for: 10 -> 8; matrix products, arithmetic and copies ran while one was open for 5% -> 1% of each run, Pallas kernels for 22% -> 21%
where the time goes in v5:
time: 114 us
  starting transfers between devices  44.7 us (39%)
  waiting for transfers between devices  27.9 us (24%)
  Pallas kernels  26.2 us (23%)
  local copies, waits for them, and re-layouts  12.6 us (11%)
  other arithmetic  1.3 us (1%)
    pallas_call x11, Pallas kernels, call(): pl.pallas_call(kernel, out_shape=outs, in_specs=sspec(scalars) + [pl.Bloc...  26.2 us
    ppermute x6, starting transfers between devices, along(): return lax.ppermute(x, ('samples', 'chan'), whole)  12.5 us
    unnamed x43, local copies, waits for them, and re-layouts  12.2 us
    all_to_all x1, starting transfers between devices, on_device(): near_got = lax.all_to_all(near, 'chan', 0, 0)  8.32 us
    ppermute x8, starting transfers between devices, exchange(): lax.ppermute(x, axis, [(i, (i + s) % size) for i in range(size)])  8.3 us
    ppermute x8, waiting for transfers between devices, exchange(): lax.ppermute(x, axis, [(i, (i + s) % size) for i in range(size)])  7.33 us
    ppermute x6, waiting for transfers between devices, along(): return lax.ppermute(x, ('samples', 'chan'), whole)  6.58 us
    ppermute x1, waiting for transfers between devices, on_device(): far_got = lax.ppermute(far, 'chan', [(0, size - 1), (size - 1, 0)])  5.49 us
  transfers between devices with their start and end apart: 21, of which 8 were waited for; matrix products, arithmetic and copies ran while one was open for 1% of the time, Pallas kernels for 21%

profile of v5, /device:TPU:0, one launch (start us, length us, event | category | flops | bytes accessed | tf_op | source)
XLA Modules:
  0.0 113.6 jit_solution(2462037568040419503)
XLA Ops:
  0.7 1.3 %copy.13 = bf16[8,8,8,512]{3,1,2,0:T(8,128)(2,1)S(1)} copy(bf16[8,8,8,512]{3,2,1,0:T(8,128)(2,1)} %bitcast.32) | data formatting | bytes 1048576
  1.9 0.0 copy-start.5
  1.9 5.7 %collective-permute-start.1 = (bf16[64,4096]{1,0:T(8,128)(2,1)S(1)}, bf16[64,4096]{1,0:T(8,128)(2,1)}, u32[]{:S(2)}, u32[]{:S(2)}) collective-permute-start(bf16[64,4096]{1,0:T(8,128)(2,1)S(1)} %bitcast.26), channel_id=1, source_target_pairs={{0,1},{1,2},{2,3},{7,6},{6,5},{5,4},{8,9},{9,10},{10,11},{15,14},{... | collective-permute-start | bytes 1572872 | tf_op jit(solution)/shard_map/ppermute | solution.py:348
  7.7 1.3 %collective-permute-start.2 = (bf16[64,4096]{1,0:T(8,128)(2,1)S(1)}, bf16[64,4096]{1,0:T(8,128)(2,1)}, u32[]{:S(2)}, u32[]{:S(2)}) collective-permute-start(bf16[64,4096]{1,0:T(8,128)(2,1)S(1)} %bitcast.27), channel_id=1, source_target_pairs={{1,0},{2,1},{3,2},{6,7},{5,6},{4,5},{9,8},{10,9},{11,10},{14,15},{... | collective-permute-start | bytes 1572872 | tf_op jit(solution)/shard_map/ppermute | solution.py:348
  9.0 0.0 copy-start
  9.0 1.3 %copy-done = f32[4,9,64,128]{3,2,1,0:T(8,128)S(1)} copy-done((f32[4,9,64,128]{3,2,1,0:T(8,128)S(1)}, f32[4,9,64,128]{3,2,1,0:T(8,128)}, u32[]{:S(2)}) %copy-start) | copy-done | bytes 1179672
  10.2 0.7 copy-done.14
  10.9 0.7 copy-done.16
  11.6 0.7 copy-done.18
  12.2 0.9 energy.1
  13.1 1.5 %collective-permute-start = (f32[64,128]{1,0:T(8,128)S(1)}, f32[64,128]{1,0:T(8,128)S(1)}, u32[]{:S(2)}, u32[]{:S(2)}) collective-permute-start(f32[64,128]{1,0:T(8,128)S(1)} %get-tuple-element.55.refs_0_), channel_id=1, source_target_pairs={{0,16},{16,0},{1,17},{17,1},{2,18},{18,2},{3,19},{19,3},{4,20},{20... | collective-permute-start | bytes 98312 | tf_op jit(solution)/shard_map/ppermute | solution.py:316
  14.7 0.2 copy.14
  14.9 0.0 copy-start.3
  14.9 0.6 collective-permute-start.6
  15.5 1.6 %collective-permute-done.refs_1_ = f32[64,128]{1,0:T(8,128)S(1)} collective-permute-done((f32[64,128]{1,0:T(8,128)S(1)}, f32[64,128]{1,0:T(8,128)S(1)}, u32[]{:S(2)}, u32[]{:S(2)}) %collective-permute-start) | collective-permute-done | bytes 32800 | tf_op jit(solution)/shard_map/ppermute | solution.py:316
  17.1 0.7 modulated.1
  17.8 0.1 collective-permute-start.3
  17.8 1.6 %collective-permute-start.4 = (f32[1,896]{1,0:T(1,128)S(1)}, f32[1,896]{1,0:T(1,128)S(1)}, u32[]{:S(2)}, u32[]{:S(2)}) collective-permute-start(f32[1,896]{1,0:T(1,128)S(1)} %fusion.2.refs_4_.refs_0_), channel_id=1, source_target_pairs={{0,8},{4,12},{8,0},{12,4},{1,9},{5,13},{9,1},{13,5},{2,10},{6,14},... | collective-permute-start | bytes 10760 | tf_op jit(solution)/shard_map/ppermute | solution.py:316
  19.5 1.4 %collective-permute-start.5 = (f32[1,896]{1,0:T(1,128)S(1)}, f32[1,896]{1,0:T(1,128)S(1)}, u32[]{:S(2)}, u32[]{:S(2)}) collective-permute-start(f32[1,896]{1,0:T(1,128)S(1)} %fusion.2.refs_4_.refs_0_), channel_id=1, source_target_pairs={{0,12},{4,0},{8,4},{12,8},{1,13},{5,1},{9,5},{13,9},{2,14},{6,2},{... | collective-permute-start | bytes 10760 | tf_op jit(solution)/shard_map/ppermute | solution.py:316
  20.9 0.0 collective-permute-done.3.refs_5_.refs_1_
  20.9 0.6 collective-permute-done.4.refs_6_.refs_2_
  21.5 0.6 collective-permute-done.5.refs_7_.refs_3_
  22.2 1.5 %collective-permute-start.7 = (bf16[64,4096]{1,0:T(8,128)(2,1)}, bf16[64,4096]{1,0:T(8,128)(2,1)}, u32[]{:S(2)}, u32[]{:S(2)}) collective-permute-start(bf16[64,4096]{1,0:T(8,128)(2,1)} %collective-permute-done.1.refs_1_), channel_id=1, source_target_pairs={{1,2},{2,3},{6,5},{5,4},{9,10},{10,11},{14,13},{13,12},{17,18},{18... | collective-permute-start | bytes 1572872 | tf_op jit(solution)/shard_map/ppermute | solution.py:348
  23.6 1.3 %collective-permute-start.8 = (bf16[64,4096]{1,0:T(8,128)(2,1)}, bf16[64,4096]{1,0:T(8,128)(2,1)}, u32[]{:S(2)}, u32[]{:S(2)}) collective-permute-start(bf16[64,4096]{1,0:T(8,128)(2,1)} %collective-permute-done.2.refs_2_.refs_4_), channel_id=1, source_target_pairs={{1,0},{2,1},{6,7},{5,6},{9,8},{10,9},{14,15},{13,14},{17,16},{18,1... | collective-permute-start | bytes 1572872 | tf_op jit(solution)/shard_map/ppermute | solution.py:348
  24.9 1.9 %collective-permute-start.9 = (bf16[9,64,128]{2,1,0:T(8,128)(2,1)S(1)}, bf16[9,64,128]{2,1,0:T(8,128)(2,1)S(1)}, u32[]{:S(2)}, u32[]{:S(2)}) collective-permute-start(bf16[9,64,128]{2,1,0:T(8,128)(2,1)S(1)} %get-tuple-element.65.refs_0_), channel_id=1, source_target_pairs={{0,16},{16,0},{1,17},{17,1},{2,18},{18,2},{3,19},{19,3},{4,20},{20... | collective-permute-start | bytes 442376 | tf_op jit(solution)/shard_map/ppermute | solution.py:316
  26.8 0.1 pad_add_fusion.place
  26.9 4.4 %collective-permute-done.9.refs_1_ = bf16[9,64,128]{2,1,0:T(8,128)(2,1)S(1)} collective-permute-done((bf16[9,64,128]{2,1,0:T(8,128)(2,1)S(1)}, bf16[9,64,128]{2,1,0:T(8,128)(2,1)S(1)}, u32[]{:S(2)}, u32[]{:S(2)}) %collective-permute-start.9) | collective-permute-done | bytes 147488 | tf_op jit(solution)/shard_map/ppermute | solution.py:316
  31.4 0.7 mod_blocks.1
  32.1 0.7 copy-done.8
  32.8 0.7 copy-done.11
  33.5 1.0 copy-done.4
  34.6 1.0 copy-done.6
  35.6 4.5 %near_grad.1 = (bf16[64,576]{1,0:T(8,128)(2,1)S(1)}, bf16[64,576]{1,0:T(8,128)(2,1)S(1)}, bf16[64,576]{1,0:T(8,128)(2,1)S(1)}, bf16[192,5120]{1,0:T(8,128)(2,1)S(1)}) custom-call(bf16[64,4096]{1,0:T(8,128)(2,1)S(1)} %bitcast.28, bf16[64,4096]{1,0:T(8,128)(2,1)} %collective-permute-done.1.refs_1_, bf16[64,4096]{1,0:T(8,128)(2,1)} %collective-permute-done.2.refs_2_.refs_4_, ...), custom_call_target="tpu_custom_call" | custom-call | flops 905969664 | bytes 4415488 | tf_op jit(solution)/shard_map/near_grad/pallas_call | solution.py:301
  40.2 1.5 %collective-permute-start.10 = (bf16[64,4096]{1,0:T(8,128)(2,1)}, bf16[64,4096]{1,0:T(8,128)(2,1)}, u32[]{:S(2)}, u32[]{:S(2)}) collective-permute-start(bf16[64,4096]{1,0:T(8,128)(2,1)} %collective-permute-done.7.refs_0_.refs_2_), channel_id=1, source_target_pairs={{2,3},{5,4},{10,11},{13,12},{18,19},{21,20},{26,27},{29,28}} | collective-permute-start | bytes 1572872 | tf_op jit(solution)/shard_map/ppermute | solution.py:348
  41.6 1.3 %collective-permute-start.11 = (bf16[64,4096]{1,0:T(8,128)(2,1)}, bf16[64,4096]{1,0:T(8,128)(2,1)}, u32[]{:S(2)}, u32[]{:S(2)}) collective-permute-start(bf16[64,4096]{1,0:T(8,128)(2,1)} %collective-permute-done.8.refs_1_.refs_5_), channel_id=1, source_target_pairs={{1,0},{6,7},{9,8},{14,15},{17,16},{22,23},{25,24},{30,31}} | collective-permute-start | bytes 1572872 | tf_op jit(solution)/shard_map/ppermute | solution.py:348
  42.9 3.9 %middle_grad.1 = bf16[4,64,576]{2,1,0:T(8,128)(2,1)S(1)} custom-call(s32[4]{0:T(128)S(1)} %pad_add_fusion.place, bf16[64,4096]{1,0:T(8,128)(2,1)} %collective-permute-done.7.refs_0_.refs_2_, bf16[64,4096]{1,0:T(8,128)(2,1)} %collective-permute-done.8.refs_1_.refs_5_, bf16[192,5120]{1,0:T(8,128)(2,1)S(1)} %get-tuple-element.71.refs_2_.wide, ...), custom_call_target="tpu_custom_call" | custom-call | flops 301989888 | bytes 3530768 | tf_op jit(solution)/shard_map/middle_grad/pallas_call | solution.py:301
  46.8 0.7 copy-done.2
  47.5 8.3 %all-to-all-start = ((bf16[4,64,576]{2,1,0:T(8,128)(2,1)}), bf16[4,64,576]{2,1,0:T(8,128)(2,1)S(1)}, u32[]{:S(2)}, u32[]{:S(2)}) async-start(bf16[4,64,576]{2,1,0:T(8,128)(2,1)} %copy-done.2), calls=%async_computation | async-start | bytes 655360 | tf_op jit(solution)/shard_map/all_to_all | solution.py:439
  55.9 6.6 %collective-permute-done.11.second.refs_6_ = bf16[64,4096]{1,0:T(8,128)(2,1)} collective-permute-done((bf16[64,4096]{1,0:T(8,128)(2,1)}, bf16[64,4096]{1,0:T(8,128)(2,1)}, u32[]{:S(2)}, u32[]{:S(2)}) %collective-permute-start.11) | collective-permute-done | bytes 524320 | tf_op jit(solution)/shard_map/ppermute | solution.py:348
  62.4 3.9 %far_grad.1 = bf16[64,576]{1,0:T(8,128)(2,1)S(1)} custom-call(bf16[64,4096]{1,0:T(8,128)(2,1)} %collective-permute-done.10.first.refs_3_, bf16[64,4096]{1,0:T(8,128)(2,1)} %collective-permute-done.11.second.refs_6_, bf16[192,5120]{1,0:T(8,128)(2,1)S(1)} %get-tuple-element.71.refs_2_.wide), custom_call_target="tpu_custom_call" | custom-call | flops 301989888 | bytes 3088384 | tf_op jit(solution)/shard_map/far_grad/pallas_call | solution.py:301
  66.3 2.8 %collective-permute-start.12 = (bf16[64,576]{1,0:T(8,128)(2,1)S(1)}, bf16[64,576]{1,0:T(8,128)(2,1)S(1)}, u32[]{:S(2)}, u32[]{:S(2)}) collective-permute-start(bf16[64,576]{1,0:T(8,128)(2,1)S(1)} %far_grad.1), channel_id=1, source_target_pairs={{0,3},{3,0},{4,7},{7,4},{8,11},{11,8},{12,15},{15,12},{16,19},{19,... | collective-permute-start | bytes 221192 | tf_op jit(solution)/shard_map/ppermute | solution.py:451
  69.1 5.5 %collective-permute-done.12.far = bf16[64,576]{1,0:T(8,128)(2,1)S(1)} collective-permute-done((bf16[64,576]{1,0:T(8,128)(2,1)S(1)}, bf16[64,576]{1,0:T(8,128)(2,1)S(1)}, u32[]{:S(2)}, u32[]{:S(2)}) %collective-permute-start.12) | collective-permute-done | bytes 73760 | tf_op jit(solution)/shard_map/ppermute | solution.py:451
  74.6 3.5 %all-to-all-start.1 = ((bf16[4,64,576]{2,1,0:T(8,128)(2,1)}), bf16[4,64,576]{2,1,0:T(8,128)(2,1)S(1)}, u32[]{:S(2)}, u32[]{:S(2)}) async-start(bf16[4,64,576]{2,1,0:T(8,128)(2,1)} %copy-done.8), calls=%async_computation.1 | async-start | bytes 655360 | tf_op jit(solution)/shard_map/all_to_all | solution.py:454
  78.1 1.0 copy-done.12
  79.0 1.0 collect.1
  80.0 1.8 %collective-permute-start.13 = (bf16[10,64,128]{2,1,0:T(8,128)(2,1)S(1)}, bf16[10,64,128]{2,1,0:T(8,128)(2,1)S(1)}, u32[]{:S(2)}, u32[]{:S(2)}) collective-permute-start(bf16[10,64,128]{2,1,0:T(8,128)(2,1)S(1)} %get-tuple-element.80), channel_id=1, source_target_pairs={{0,16},{16,0},{1,17},{17,1},{2,18},{18,2},{3,19},{19,3},{4,20},{20... | collective-permute-start | bytes 491528 | tf_op jit(solution)/shard_map/ppermute | solution.py:468
  81.9 3.6 %collective-permute-done.13.refs_1_ = bf16[10,64,128]{2,1,0:T(8,128)(2,1)S(1)} collective-permute-done((bf16[10,64,128]{2,1,0:T(8,128)(2,1)S(1)}, bf16[10,64,128]{2,1,0:T(8,128)(2,1)S(1)}, u32[]{:S(2)}, u32[]{:S(2)}) %collective-permute-start.13) | collective-permute-done | bytes 163872 | tf_op jit(solution)/shard_map/ppermute | solution.py:468
  85.4 0.2 row_sum.1.refs_0_
  85.6 0.1 collective-permute-start.14
  85.7 0.2 collective-permute-start.15
  86.0 1.5 %collective-permute-start.16 = (bf16[10,64,128]{2,1,0:T(8,128)(2,1)S(1)}, bf16[10,64,128]{2,1,0:T(8,128)(2,1)S(1)}, u32[]{:S(2)}, u32[]{:S(2)}) collective-permute-start(bf16[10,64,128]{2,1,0:T(8,128)(2,1)S(1)} %row_sum.1.refs_0_), channel_id=1, source_target_pairs={{0,12},{4,0},{8,4},{12,8},{1,13},{5,1},{9,5},{13,9},{2,14},{6,2},{... | collective-permute-start | bytes 491528 | tf_op jit(solution)/shard_map/ppermute | solution.py:316
  87.5 0.7 copy-done.9
  88.2 1.0 copy-done.10
  89.2 5.8 %input_grad.1 = (f32[64,4096]{1,0:T(8,128)S(1)}, f32[64,512]{1,0:T(8,128)S(1)}, f32[64,512]{1,0:T(8,128)S(1)}) custom-call(s32[4]{0:T(128)S(1)} %pad_add_fusion.place, bf16[64,4096]{1,0:T(8,128)(2,1)S(1)} %bitcast.29, bf16[64,4096]{1,0:T(8,128)(2,1)} %collective-permute-done.1.refs_1_, bf16[64,4096]{1,0:T(8,128)(2,1)} %collective-permute-done.7.refs_0_.refs_2_, ...), custom_call_target="tpu_custom_call" | custom-call | flops 1207959552 | bytes 5275664 | tf_op jit(solution)/shard_map/input_grad/pallas_call | solution.py:301
  95.0 2.9 %bank_grad.1 = (f32[4,9,64,128]{3,2,1,0:T(8,128)}, f32[4,4,128]{2,1,0:T(4,128)}) custom-call(s32[4]{0:T(128)S(1)} %pad_add_fusion.place, f32[4,9,64,128]{3,2,1,0:T(8,128)S(1)} %copy-done.1, bf16[10,64,128]{2,1,0:T(8,128)(2,1)S(1)} %row_sum.1.refs_0_, bf16[10,64,128]{2,1,0:T(8,128)(2,1)S(1)} %collective-permute-done.14.refs_1_, ...), custom_call_target="tpu_custom_call" | custom-call | flops 1000000 | bytes 3037200 | tf_op jit(solution)/shard_map/bank_grad/pallas_call | solution.py:301
  98.0 1.8 %collective-permute-start.17 = (f32[64,512]{1,0:T(8,128)S(1)}, f32[64,512]{1,0:T(8,128)S(1)}, u32[]{:S(2)}, u32[]{:S(2)}) collective-permute-start(f32[64,512]{1,0:T(8,128)S(1)} %broadcast_select_fusion), channel_id=1, source_target_pairs={{0,16},{16,0},{1,17},{17,1},{2,18},{18,2},{3,19},{19,3},{4,20},{20... | collective-permute-start | bytes 393224 | tf_op jit(solution)/shard_map/ppermute | solution.py:323
  99.8 5.1 %all-to-all-start.2 = ((f32[4,4,128]{2,1,0:T(4,128)}), f32[4,4,128]{2,1,0:T(4,128)S(1)}, u32[]{:S(2)}, u32[]{:S(2)}) async-start(f32[4,4,128]{2,1,0:T(4,128)} %get-tuple-element.101), calls=%async_computation.2 | async-start | bytes 16384 | tf_op jit(solution)/shard_map/all_to_all | solution.py:507
  104.9 0.1 pad.11.clone
  104.9 0.6 copy.15
  105.6 4.9 %all-to-all-done.2.parts = f32[4,4,128]{2,1,0:T(4,128)S(1)} async-done(((f32[4,4,128]{2,1,0:T(4,128)}), f32[4,4,128]{2,1,0:T(4,128)S(1)}, u32[]{:S(2)}, u32[]{:S(2)}) %all-to-all-start.2) | async-done | bytes 8224 | tf_op jit(solution)/shard_map/all_to_all | solution.py:507
  110.5 1.7 %affine.1 = (f32[512,128]{1,0:T(8,128)}, f32[1,128]{1,0:T(1,128)}) custom-call(s32[4]{0:T(128)S(1)} %pad_add_fusion.place, f32[4,4,128]{2,1,0:T(4,128)S(1)} %all-to-all-done.2.parts, f32[1,896]{1,0:T(1,128)S(1)} %fusion.2.refs_4_.refs_0_, f32[1,896]{1,0:T(1,128)S(1)} %collective-permute-done.3.refs_5_.refs_1_, ...), custom_call_target="tpu_custom_call" | custom-call | flops 1000000 | bytes 285200 | tf_op jit(solution)/shard_map/affine/pallas_call | solution.py:301
  112.2 0.1 copy.11
  112.3 0.1 copy.12
  112.5 1.1 %fusion = bf16[1,64,8,512]{3,2,1,0:T(8,128)(2,1)} fusion(f32[1,64,1,512]{3,2,1,0:T(1,128)S(1)} %copy.12, f32[1,64,1,512]{3,2,1,0:T(1,128)S(1)} %copy.11, f32[8]{0:T(128)S(1)} %pad.11.clone, f32[1,64,8,512]{3,2,1,0:T(8,128)S(1)} %bitcast.31), kind=kLoop, calls=%fused_computation.1 | loop fusion | flops 1048576 | bytes 1835040 | tf_op jit(solution)/shard_map/convert_element_type | solution.py:512
  (44 shorter events, 0.2 us)
Async XLA Ops:
  0.6 8.3 %copy-start.13 = (f32[512,128]{1,0:T(8,128)S(1)}, f32[512,128]{1,0:T(8,128)}, u32[]{:S(2)}) copy-start(f32[512,128]{1,0:T(8,128)} %affine_w.1) | copy-start | bytes 786436
  0.6 14.0 %copy-start.19 = (bf16[1,64,8,512]{3,2,1,0:T(8,128)(2,1)S(1)}, bf16[1,64,8,512]{3,2,1,0:T(8,128)(2,1)}, u32[]{:S(2)}) copy-start(bf16[1,64,8,512]{3,2,1,0:T(8,128)(2,1)} %param.7) | copy-start | bytes 1572868
  1.9 12.9 %copy-start.5 = (bf16[8,8,8,512]{3,1,2,0:T(8,128)(2,1)}, bf16[8,8,8,512]{3,1,2,0:T(8,128)(2,1)S(1)}, u32[]{:S(2)}) copy-start(bf16[8,8,8,512]{3,1,2,0:T(8,128)(2,1)S(1)} %copy.13) | copy-start | bytes 1572868
  1.9 20.2 %collective-permute-start.1 = (bf16[64,4096]{1,0:T(8,128)(2,1)S(1)}, bf16[64,4096]{1,0:T(8,128)(2,1)}, u32[]{:S(2)}, u32[]{:S(2)}) collective-permute-start(bf16[64,4096]{1,0:T(8,128)(2,1)S(1)} %bitcast.26), channel_id=1, source_target_pairs={{0,1},{1,2},{2,3},{7,6},{6,5},{5,4},{8,9},{9,10},{10,11},{15,14},{... | collective-permute-start | bytes 1572872 | tf_op jit(solution)/shard_map/ppermute | solution.py:348
  7.7 14.5 %collective-permute-start.2 = (bf16[64,4096]{1,0:T(8,128)(2,1)S(1)}, bf16[64,4096]{1,0:T(8,128)(2,1)}, u32[]{:S(2)}, u32[]{:S(2)}) collective-permute-start(bf16[64,4096]{1,0:T(8,128)(2,1)S(1)} %bitcast.27), channel_id=1, source_target_pairs={{1,0},{2,1},{3,2},{6,7},{5,6},{4,5},{9,8},{10,9},{11,10},{14,15},{... | collective-permute-start | bytes 1572872 | tf_op jit(solution)/shard_map/ppermute | solution.py:348
  9.0 1.3 %copy-start = (f32[4,9,64,128]{3,2,1,0:T(8,128)S(1)}, f32[4,9,64,128]{3,2,1,0:T(8,128)}, u32[]{:S(2)}) copy-start(f32[4,9,64,128]{3,2,1,0:T(8,128)} %bank.5) | copy-start | bytes 3538948
  10.2 0.7 copy-start.14
  10.9 0.7 copy-start.16
  11.6 0.7 copy-start.18
  12.2 3.2 %copy-start.17 = (s32[1,4]{1,0:T(1,128)S(1)}, s32[1,4]{1,0:T(1,128)}, u32[]{:S(2)}) copy-start(s32[1,4]{1,0:T(1,128)} %sel.3) | copy-start | bytes 52
  12.2 4.8 %copy-start.1 = (f32[4,9,64,128]{3,2,1,0:T(8,128)S(1)}, f32[4,9,64,128]{3,2,1,0:T(8,128)}, u32[]{:S(2)}) copy-start(f32[4,9,64,128]{3,2,1,0:T(8,128)} %bank.5) | copy-start | bytes 3538948
  13.1 3.9 %collective-permute-start = (f32[64,128]{1,0:T(8,128)S(1)}, f32[64,128]{1,0:T(8,128)S(1)}, u32[]{:S(2)}, u32[]{:S(2)}) collective-permute-start(f32[64,128]{1,0:T(8,128)S(1)} %get-tuple-element.55.refs_0_), channel_id=1, source_target_pairs={{0,16},{16,0},{1,17},{17,1},{2,18},{18,2},{3,19},{19,3},{4,20},{20... | collective-permute-start | bytes 98312 | tf_op jit(solution)/shard_map/ppermute | solution.py:316
  14.7 3.1 %copy-start.15 = (f32[1,512]{1,0:T(1,128)S(1)}, f32[1,512]{1,0:T(1,128)}, u32[]{:S(2)}) copy-start(f32[1,512]{1,0:T(1,128)} %latent.1) | copy-start | bytes 6148
  14.9 16.5 %copy-start.3 = (bf16[8,8,8,512]{3,1,2,0:T(8,128)(2,1)}, bf16[8,8,8,512]{3,1,2,0:T(8,128)(2,1)S(1)}, u32[]{:S(2)}) copy-start(bf16[8,8,8,512]{3,1,2,0:T(8,128)(2,1)S(1)} %copy.14) | copy-start | bytes 1572868
  14.9 4.6 %collective-permute-start.6 = (bf16[64,512]{1,0:T(8,128)(2,1)S(1)}, bf16[64,512]{1,0:T(8,128)(2,1)S(1)}, u32[]{:S(2)}, u32[]{:S(2)}) collective-permute-start(bf16[64,512]{1,0:T(8,128)(2,1)S(1)} %slice_select_fusion), channel_id=1, source_target_pairs={{0,16},{16,0},{1,17},{17,1},{2,18},{18,2},{3,19},{19,3},{4,20},{20... | collective-permute-start | bytes 196616 | tf_op jit(solution)/shard_map/ppermute | solution.py:323
  17.8 3.1 %collective-permute-start.3 = (f32[1,896]{1,0:T(1,128)S(1)}, f32[1,896]{1,0:T(1,128)S(1)}, u32[]{:S(2)}, u32[]{:S(2)}) collective-permute-start(f32[1,896]{1,0:T(1,128)S(1)} %fusion.2.refs_4_.refs_0_), channel_id=1, source_target_pairs={{0,4},{4,8},{8,12},{12,0},{1,5},{5,9},{9,13},{13,1},{2,6},{6,10},{... | collective-permute-start | bytes 10760 | tf_op jit(solution)/shard_map/ppermute | solution.py:316
  17.8 3.7 %collective-permute-start.4 = (f32[1,896]{1,0:T(1,128)S(1)}, f32[1,896]{1,0:T(1,128)S(1)}, u32[]{:S(2)}, u32[]{:S(2)}) collective-permute-start(f32[1,896]{1,0:T(1,128)S(1)} %fusion.2.refs_4_.refs_0_), channel_id=1, source_target_pairs={{0,8},{4,12},{8,0},{12,4},{1,9},{5,13},{9,1},{13,5},{2,10},{6,14},... | collective-permute-start | bytes 10760 | tf_op jit(solution)/shard_map/ppermute | solution.py:316
  19.5 2.7 %collective-permute-start.5 = (f32[1,896]{1,0:T(1,128)S(1)}, f32[1,896]{1,0:T(1,128)S(1)}, u32[]{:S(2)}, u32[]{:S(2)}) collective-permute-start(f32[1,896]{1,0:T(1,128)S(1)} %fusion.2.refs_4_.refs_0_), channel_id=1, source_target_pairs={{0,12},{4,0},{8,4},{12,8},{1,13},{5,1},{9,5},{13,9},{2,14},{6,2},{... | collective-permute-start | bytes 10760 | tf_op jit(solution)/shard_map/ppermute | solution.py:316
  22.2 18.0 %collective-permute-start.7 = (bf16[64,4096]{1,0:T(8,128)(2,1)}, bf16[64,4096]{1,0:T(8,128)(2,1)}, u32[]{:S(2)}, u32[]{:S(2)}) collective-permute-start(bf16[64,4096]{1,0:T(8,128)(2,1)} %collective-permute-done.1.refs_1_), channel_id=1, source_target_pairs={{1,2},{2,3},{6,5},{5,4},{9,10},{10,11},{14,13},{13,12},{17,18},{18... | collective-permute-start | bytes 1572872 | tf_op jit(solution)/shard_map/ppermute | solution.py:348
  23.6 16.5 %collective-permute-start.8 = (bf16[64,4096]{1,0:T(8,128)(2,1)}, bf16[64,4096]{1,0:T(8,128)(2,1)}, u32[]{:S(2)}, u32[]{:S(2)}) collective-permute-start(bf16[64,4096]{1,0:T(8,128)(2,1)} %collective-permute-done.2.refs_2_.refs_4_), channel_id=1, source_target_pairs={{1,0},{2,1},{6,7},{5,6},{9,8},{10,9},{14,15},{13,14},{17,16},{18,1... | collective-permute-start | bytes 1572872 | tf_op jit(solution)/shard_map/ppermute | solution.py:348
  24.9 6.4 %collective-permute-start.9 = (bf16[9,64,128]{2,1,0:T(8,128)(2,1)S(1)}, bf16[9,64,128]{2,1,0:T(8,128)(2,1)S(1)}, u32[]{:S(2)}, u32[]{:S(2)}) collective-permute-start(bf16[9,64,128]{2,1,0:T(8,128)(2,1)S(1)} %get-tuple-element.65.refs_0_), channel_id=1, source_target_pairs={{0,16},{16,0},{1,17},{17,1},{2,18},{18,2},{3,19},{19,3},{4,20},{20... | collective-permute-start | bytes 442376 | tf_op jit(solution)/shard_map/ppermute | solution.py:316
  32.1 0.7 copy-start.8
  32.8 0.7 copy-start.11
  33.5 1.0 copy-start.4
  34.6 1.0 copy-start.6
  40.2 15.7 %collective-permute-start.10 = (bf16[64,4096]{1,0:T(8,128)(2,1)}, bf16[64,4096]{1,0:T(8,128)(2,1)}, u32[]{:S(2)}, u32[]{:S(2)}) collective-permute-start(bf16[64,4096]{1,0:T(8,128)(2,1)} %collective-permute-done.7.refs_0_.refs_2_), channel_id=1, source_target_pairs={{2,3},{5,4},{10,11},{13,12},{18,19},{21,20},{26,27},{29,28}} | collective-permute-start | bytes 1572872 | tf_op jit(solution)/shard_map/ppermute | solution.py:348
  41.6 20.8 %collective-permute-start.11 = (bf16[64,4096]{1,0:T(8,128)(2,1)}, bf16[64,4096]{1,0:T(8,128)(2,1)}, u32[]{:S(2)}, u32[]{:S(2)}) collective-permute-start(bf16[64,4096]{1,0:T(8,128)(2,1)} %collective-permute-done.8.refs_1_.refs_5_), channel_id=1, source_target_pairs={{1,0},{6,7},{9,8},{14,15},{17,16},{22,23},{25,24},{30,31}} | collective-permute-start | bytes 1572872 | tf_op jit(solution)/shard_map/ppermute | solution.py:348
  46.8 0.7 copy-start.2
  47.5 27.0 %all-to-all-start = ((bf16[4,64,576]{2,1,0:T(8,128)(2,1)}), bf16[4,64,576]{2,1,0:T(8,128)(2,1)S(1)}, u32[]{:S(2)}, u32[]{:S(2)}) async-start(bf16[4,64,576]{2,1,0:T(8,128)(2,1)} %copy-done.2), calls=%async_computation | async-start | bytes 655360 | tf_op jit(solution)/shard_map/all_to_all | solution.py:439
  66.3 21.9 %copy-start.7 = (bf16[8,8,8,512]{3,1,2,0:T(8,128)(2,1)S(1)}, bf16[8,8,8,512]{3,1,2,0:T(8,128)(2,1)}, u32[]{:S(2)}) copy-start(bf16[8,8,8,512]{3,1,2,0:T(8,128)(2,1)} %copy-done.5) | copy-start | bytes 1572868
  66.3 8.3 %collective-permute-start.12 = (bf16[64,576]{1,0:T(8,128)(2,1)S(1)}, bf16[64,576]{1,0:T(8,128)(2,1)S(1)}, u32[]{:S(2)}, u32[]{:S(2)}) collective-permute-start(bf16[64,576]{1,0:T(8,128)(2,1)S(1)} %far_grad.1), channel_id=1, source_target_pairs={{0,3},{3,0},{4,7},{7,4},{8,11},{11,8},{12,15},{15,12},{16,19},{19,... | collective-permute-start | bytes 221192 | tf_op jit(solution)/shard_map/ppermute | solution.py:451
  74.6 12.9 %all-to-all-start.1 = ((bf16[4,64,576]{2,1,0:T(8,128)(2,1)}), bf16[4,64,576]{2,1,0:T(8,128)(2,1)S(1)}, u32[]{:S(2)}, u32[]{:S(2)}) async-start(bf16[4,64,576]{2,1,0:T(8,128)(2,1)} %copy-done.8), calls=%async_computation.1 | async-start | bytes 655360 | tf_op jit(solution)/shard_map/all_to_all | solution.py:454
  78.0 1.0 copy-start.12
  80.0 5.4 %collective-permute-start.13 = (bf16[10,64,128]{2,1,0:T(8,128)(2,1)S(1)}, bf16[10,64,128]{2,1,0:T(8,128)(2,1)S(1)}, u32[]{:S(2)}, u32[]{:S(2)}) collective-permute-start(bf16[10,64,128]{2,1,0:T(8,128)(2,1)S(1)} %get-tuple-element.80), channel_id=1, source_target_pairs={{0,16},{16,0},{1,17},{17,1},{2,18},{18,2},{3,19},{19,3},{4,20},{20... | collective-permute-start | bytes 491528 | tf_op jit(solution)/shard_map/ppermute | solution.py:468
  85.6 9.3 %collective-permute-start.14 = (bf16[10,64,128]{2,1,0:T(8,128)(2,1)S(1)}, bf16[10,64,128]{2,1,0:T(8,128)(2,1)S(1)}, u32[]{:S(2)}, u32[]{:S(2)}) collective-permute-start(bf16[10,64,128]{2,1,0:T(8,128)(2,1)S(1)} %row_sum.1.refs_0_), channel_id=1, source_target_pairs={{0,4},{4,8},{8,12},{12,0},{1,5},{5,9},{9,13},{13,1},{2,6},{6,10},{... | collective-permute-start | bytes 491528 | tf_op jit(solution)/shard_map/ppermute | solution.py:316
  85.7 9.3 %collective-permute-start.15 = (bf16[10,64,128]{2,1,0:T(8,128)(2,1)S(1)}, bf16[10,64,128]{2,1,0:T(8,128)(2,1)S(1)}, u32[]{:S(2)}, u32[]{:S(2)}) collective-permute-start(bf16[10,64,128]{2,1,0:T(8,128)(2,1)S(1)} %row_sum.1.refs_0_), channel_id=1, source_target_pairs={{0,8},{4,12},{8,0},{12,4},{1,9},{5,13},{9,1},{13,5},{2,10},{6,14},... | collective-permute-start | bytes 491528 | tf_op jit(solution)/shard_map/ppermute | solution.py:316
  86.0 9.1 %collective-permute-start.16 = (bf16[10,64,128]{2,1,0:T(8,128)(2,1)S(1)}, bf16[10,64,128]{2,1,0:T(8,128)(2,1)S(1)}, u32[]{:S(2)}, u32[]{:S(2)}) collective-permute-start(bf16[10,64,128]{2,1,0:T(8,128)(2,1)S(1)} %row_sum.1.refs_0_), channel_id=1, source_target_pairs={{0,12},{4,0},{8,4},{12,8},{1,13},{5,1},{9,5},{13,9},{2,14},{6,2},{... | collective-permute-start | bytes 491528 | tf_op jit(solution)/shard_map/ppermute | solution.py:316
  87.5 0.7 copy-start.9
  88.2 1.0 copy-start.10
  98.0 14.2 %collective-permute-start.17 = (f32[64,512]{1,0:T(8,128)S(1)}, f32[64,512]{1,0:T(8,128)S(1)}, u32[]{:S(2)}, u32[]{:S(2)}) collective-permute-start(f32[64,512]{1,0:T(8,128)S(1)} %broadcast_select_fusion), channel_id=1, source_target_pairs={{0,16},{16,0},{1,17},{17,1},{2,18},{18,2},{3,19},{19,3},{4,20},{20... | collective-permute-start | bytes 393224 | tf_op jit(solution)/shard_map/ppermute | solution.py:323
  99.8 10.7 %all-to-all-start.2 = ((f32[4,4,128]{2,1,0:T(4,128)}), f32[4,4,128]{2,1,0:T(4,128)S(1)}, u32[]{:S(2)}, u32[]{:S(2)}) async-start(f32[4,4,128]{2,1,0:T(4,128)} %get-tuple-element.101), calls=%async_computation.2 | async-start | bytes 16384 | tf_op jit(solution)/shard_map/all_to_all | solution.py:507

commit v6 on v5

v6 whole, which is shorter than its diff:
```python
import functools

import jax
import jax.numpy as jnp
from jax import lax
from jax.experimental import pallas as pl
from jax.experimental.pallas import tpu as pltpu
from jax.sharding import PartitionSpec as P

EPS = 1e-08
TAPS = 9
F32 = jnp.float32
BF16 = jnp.bfloat16
VMEM_LIMIT = 16 * 2**20


def params():
    return pltpu.CompilerParams(vmem_limit_bytes=VMEM_LIMIT)


def vspec(n):
    return [pl.BlockSpec(memory_space=pltpu.VMEM)] * n


def sspec(n):
    return [pl.BlockSpec(memory_space=pltpu.SMEM)] * n


def cost(flops, moved):
    return pl.CostEstimate(flops=flops, bytes_accessed=moved, transcendentals=0)


def beside(pieces):
    return pieces[0] if len(pieces) == 1 else jnp.concatenate(pieces, axis=1)


def mixed(bank_ref, sel, sample, tap):
    total = sel[sample][0] * bank_ref[0, tap]
    for k in range(1, bank_ref.shape[0]):
        total = total + sel[sample][k] * bank_ref[k, tap]
    return total


def own_select(sel_ref):
    return [[sel_ref[0, k].astype(F32) for k in range(sel_ref.shape[1])]]


def energy_kernel(sel, latent, affine_b, bank_hbm, w_hbm, style_out, kernel_out, energy_out, bank, affine_w, sems):
    copies = [
        pltpu.make_async_copy(w_hbm, affine_w, sems.at[0]),
        pltpu.make_async_copy(bank_hbm, bank, sems.at[1]),
    ]
    for copy in copies:
        copy.start()
    copies[0].wait()
    style = (
        jnp.dot(latent[...], affine_w[...], precision=lax.Precision.HIGHEST, preferred_element_type=F32)
        + affine_b[...]
    )
    style_out[...] = style
    total = jnp.zeros(bank.shape[2:], F32)
    sel = own_select(sel)
    copies[1].wait()
    for tap in range(TAPS):
        kernel = mixed(bank, sel, 0, tap)
        kernel_out[tap] = kernel
        plain = kernel * style
        total = total + plain * plain
    energy_out[...] = jnp.broadcast_to(jnp.sum(total, axis=1, keepdims=True), energy_out.shape)


def modulated_kernel(kernel, style, *refs):
    energies, (mod_out, scale_out, row_out) = refs[:-3], refs[-3:]
    energy = energies[0][...]
    for other in energies[1:]:
        energy = energy + other[...]
    scales = lax.rsqrt(energy + EPS)
    scale_out[...] = scales
    row_out[...] = scales.T[0:1]
    scale = scales[:, 0:1]
    for tap in range(TAPS):
        mod_out[tap] = (kernel[tap] * style[...] * scale).astype(BF16)


def blocks_kernel(rows, size, shares, place, *refs):
    parts, whole, own, ahead, behind, others, by_row, by_share = refs[:rows], *refs[rows:]
    chan_at, row_at, sign = place[1], place[2], place[3]
    for r in range(rows):
        by_row[lax.rem(row_at - r + rows, rows)] = parts[r][...]
    ch = whole.shape[2] // size
    share = ch // shares
    taps = []
    for tap in range(TAPS):
        value = beside([by_row[r, tap].astype(F32) for r in range(rows)])
        whole[tap] = value.astype(BF16)
        taps.append(value)
    for z in range(size):
        value = beside([value[:, z * ch : (z + 1) * ch] for value in taps]).astype(BF16)
        for k in range(shares):
            by_share[k, z] = value[k * share : (k + 1) * share]
    for k in range(shares):
        own[k * share : (k + 1) * share] = by_share[k, chan_at]
    k = row_at if shares > 1 else 0
    ahead[...] = by_share[k, lax.rem(chan_at + sign + size, size)]
    behind[...] = by_share[k, lax.rem(chan_at - sign + size, size)]
    for d in range(2, size - 1):
        others[(d - 2) * share : (d - 1) * share] = by_share[k, lax.rem(chan_at + sign * d + size, size)]
    others[(size - 3) * share :] = by_share[k, size - 1 - chan_at]


def shifted(x, by):
    width = x.shape[1]
    lane = lax.broadcasted_iota(jnp.int32, x.shape, 1)
    moved = pltpu.roll(x, by % width, 1)
    return jnp.where(lane == (0 if by == 1 else width - 1), 0.0, moved)


def spread(wide, row, x):
    ch, width = x.shape
    wide[ch : 2 * ch, row * width : (row + 1) * width] = x
    x = x.astype(F32)
    wide[0:ch, row * width : (row + 1) * width] = shifted(x, 1).astype(BF16)
    wide[2 * ch : 3 * ch, row * width : (row + 1) * width] = shifted(x, -1).astype(BF16)


def rows_kernel(height, width, feat, feat_before, feat_after, out):
    out[:, 0:width] = feat_before[...]
    out[:, width : (height + 1) * width] = feat[...]
    out[:, (height + 1) * width :] = feat_after[...]


def tap_products(g_ref, wides, totals, height, width):
    for total in totals:
        total[...] = jnp.zeros(total.shape, F32)

    def body(row, _):
        g = g_ref[:, pl.ds(pl.multiple_of(row * width, width), width)]
        for wide, total in zip(wides, totals):
            for kh in range(3):
                x = wide[:, pl.ds(pl.multiple_of((row + kh) * width, width), width)]
                total[kh] += lax.dot_general(g, x, (((1,), (1,)), ((), ())), preferred_element_type=F32)
        return 0

    lax.fori_loop(0, height, body, 0)
    return [jnp.concatenate([total[kh] for kh in range(3)], axis=1).astype(BF16) for total in totals]


def near_grad_kernel(height, width, *refs):
    cotans, feat, outs, (wide, gathered, total) = refs[:3], refs[3], refs[4:7], refs[7:]
    ch = feat.shape[0]
    for at, cotan in enumerate(cotans):
        gathered[at * ch : (at + 1) * ch] = cotan[...]
    for row in range(height + 2):
        spread(wide, row, feat[:, row * width : (row + 1) * width])
    (whole,) = tap_products(gathered, [wide], [total], height, width)
    for at, out in enumerate(outs):
        out[...] = whole[at * ch : (at + 1) * ch]


def far_grad_kernel(count, height, width, *refs):
    first, second, (wide, feat) = refs[:count], refs[count : 2 * count], refs[2 * count : 2 * count + 2]
    outs, (wide_end, gathered, end_block, total, end_total) = refs[2 * count + 2 : -5], refs[-5:]
    ch = feat.shape[0]
    for at in range(count):
        gathered[at * ch : (at + 1) * ch] = first[at][...] + second[count - 1 - at][...]
    for row in range(height + 2):
        spread(wide_end, row, feat[:, row * width : (row + 1) * width])
    if count == 1:
        whole, end = tap_products(gathered, [wide, wide_end], [total, end_total], height, width)
    else:
        end_block[...] = first[-1][...] + second[-1][...]
        (whole,) = tap_products(gathered, [wide], [total], height, width)
        (end,) = tap_products(end_block, [wide_end], [end_total], height, width)
    out = outs[0]
    out[0 : count * ch] = whole
    out[count * ch :] = end


def input_products(cotan, taps_t, total, outs, height, width):
    main, before, after = outs
    ch = main.shape[0]
    total[...] = jnp.zeros(total.shape, F32)

    def body(row, _):
        g = cotan[:, pl.ds(pl.multiple_of(row * width, width), width)]
        for kh in range(3):
            y = jnp.dot(taps_t[kh * 3 * ch : (kh + 1) * 3 * ch], g, preferred_element_type=F32)
            total[row + kh] += y
        return 0

    lax.fori_loop(0, height, body, 0)
    for row in range(height + 2):
        value = total[row, ch : 2 * ch]
        value = value + shifted(total[row, 0:ch], -1) + shifted(total[row, 2 * ch : 3 * ch], 1)
        value = value.astype(main.dtype)
        if row == 0:
            before[...] = value
        elif row == height + 1:
            after[...] = value
        else:
            main[:, (row - 1) * width : row * width] = value


def input_grad_kernel(rows, count, height, width, place, *refs):
    cotans, first, second = refs[:3], refs[3 : 3 + count], refs[3 + count : 3 + 2 * count]
    own_mod, mods, outs = refs[3 + 2 * count], refs[4 + 2 * count : -7], refs[-7:-4]
    gathered, taps, taps_t, total = refs[-4:]
    ch = own_mod.shape[0]
    shares, share = len(mods), ch // len(mods)
    for at, cotan in enumerate(cotans):
        gathered[at * ch : (at + 1) * ch] = cotan[...]
    for at in range(count):
        gathered[(3 + at) * ch : (4 + at) * ch] = first[at][...] + second[count - 1 - at][...]
    for k in range(shares):
        taps[0, k] = own_mod[k * share : (k + 1) * share].astype(F32)
        owner = lax.rem(place[2] - k + rows, rows) if shares > 1 else 0
        for at in range(2 + count):
            taps[1 + at, owner] = mods[k][at * share : (at + 1) * share].astype(F32)
    taps_t[...] = taps[...].reshape((3 + count) * ch, taps.shape[3]).T.astype(BF16)
    input_products(gathered, taps_t, total, outs, height, width)


def end_input_kernel(rows, count, height, width, place, first, second, *refs):
    mods, outs, (gathered, taps, taps_t, total) = refs[:-7], refs[-7:-4], refs[-4:]
    ch = outs[0].shape[0]
    shares, share = len(mods), ch // len(mods)
    gathered[...] = first[...] + second[...]
    for k in range(shares):
        owner = lax.rem(place[2] - k + rows, rows) if shares > 1 else 0
        taps[owner] = mods[k][(2 + count) * share :].astype(F32)
    taps_t[...] = taps[...].reshape(ch, taps.shape[2]).T.astype(BF16)
    input_products(gathered, taps_t, total, outs, height, width)


def split3(x):
    high = x.astype(BF16).astype(F32)
    mid = (x - high).astype(BF16).astype(F32)
    return high, mid, x - high - mid


def put_fall(out, fall):
    lane = lax.broadcasted_iota(jnp.int32, out.shape[1:], 1)
    last = jnp.zeros(out.shape[1:], F32)
    for at, piece in enumerate(split3(fall)):
        last = jnp.where(lane == at, piece, last)
    out[TAPS] = last.astype(BF16)


def get_fall(last):
    last = last.astype(F32)
    return last[:, 0:1] + last[:, 1:2] + last[:, 2:3]


def collect_kernel(rows, size, place, scale, whole_mod, own, ahead, behind, others, *refs):
    outs, (by_chan, by_row) = refs[:rows], refs[rows:]
    chan_at, row_at, sign = place[1], place[2], place[3]
    ch = own.shape[0]
    by_chan[chan_at] = own[...].astype(F32)
    by_chan[lax.rem(chan_at + sign + size, size)] = ahead[...].astype(F32)
    by_chan[lax.rem(chan_at - sign + size, size)] = behind[...].astype(F32)
    for d in range(2, size - 1):
        value = others[(d - 2) * ch : (d - 1) * ch].astype(F32)
        by_chan[lax.rem(chan_at + sign * d + size, size)] = value
    by_chan[jnp.where(chan_at == 0, size - 1, 0)] += others[(size - 3) * ch :].astype(F32)
    in_ch = outs[0].shape[2]
    product = jnp.zeros(whole_mod.shape[1:], F32)
    for tap in range(TAPS):
        value = beside([by_chan[z, :, tap * ch : (tap + 1) * ch] for z in range(size)])
        product = product + value * whole_mod[tap].astype(F32)
        for r in range(rows):
            by_row[r, tap] = value[:, r * in_ch : (r + 1) * in_ch].astype(BF16)
    fall = jnp.sum(product, axis=1, keepdims=True) * (scale[:, 0:1] * scale[:, 0:1])
    for r in range(rows):
        outs[r][0:TAPS] = by_row[lax.rem(row_at + r, rows)]
        put_fall(outs[r], fall)


def row_sum_kernel(*refs):
    parts, out = refs[:-1], refs[-1]
    fall = get_fall(parts[0][TAPS])
    for part in parts[1:]:
        fall = fall + get_fall(part[TAPS])
    for tap in range(TAPS):
        value = parts[0][tap].astype(F32)
        for part in parts[1:]:
            value = value + part[tap].astype(F32)
        out[tap] = value.astype(BF16)
    put_fall(out, fall)


def bank_grad_kernel(samples, starts, place, bank, *refs):
    parts, smalls = refs[:samples], refs[samples : 2 * samples]
    bank_grad, style_grad, held, small = refs[2 * samples :]
    sample = place[0]
    for s in range(samples):
        held[lax.rem(sample - s + samples, samples)] = parts[s][...]
        small[lax.rem(sample - s + samples, samples)] = smalls[s][...]
    filters, out_ch, in_ch = bank.shape[0], bank.shape[2], bank.shape[3]
    at_style, at_scale, at_sel = starts
    sel, styles, scales, falls = [], [], [], []
    for b in range(samples):
        row = small[b]
        sel.append([row[:, at_sel + k : at_sel + k + 1] for k in range(filters)])
        styles.append(row[:, at_style : at_style + in_ch])
        across = jnp.broadcast_to(row[:, at_scale : at_scale + 128], (128, 128))
        scales.append(across.T[:out_ch, 0:1])
        falls.append(get_fall(held[b, TAPS]))
    sums = [jnp.zeros(bank.shape[2:], F32) for _ in range(samples)]
    for tap in range(TAPS):
        totals = [None] * filters
        for b in range(samples):
            kern = mixed(bank, sel, b, tap)
            plain_grad = held[b, tap].astype(F32) * scales[b] - kern * styles[b] * falls[b]
            sums[b] = sums[b] + plain_grad * kern
            kernel_grad = plain_grad * styles[b]
            for k in range(filters):
                term = sel[b][k] * kernel_grad
                totals[k] = term if totals[k] is None else totals[k] + term
        for k in range(filters):
            bank_grad[k, tap] = totals[k]
    for b in range(samples):
        value = jnp.sum(sums[b], axis=0, keepdims=True)
        style_grad[b : b + 1] = value


def affine_kernel(samples, size, place, *refs):
    parts, smalls = refs[:size], refs[size : size + samples]
    w_grad, b_grad, latents, held = refs[size + samples :]
    for s in range(samples):
        at = lax.rem(place[0] - s + samples, samples)
        latents[pl.ds(at, 1)] = smalls[s][:, : latents.shape[1]]
    for d in range(size):
        held[lax.rem(place[1] - d + size, size)] = parts[d][...]
    style_grad = held[0]
    for z in range(1, size):
        style_grad = style_grad + held[z]
    w_grad[...] = lax.dot_general(
        latents[...],
        style_grad,
        (((0,), (0,)), ((), ())),
        precision=lax.Precision.HIGHEST,
        preferred_element_type=F32,
    )
    bias = style_grad[0:1]
    for b in range(1, samples):
        bias = bias + style_grad[b : b + 1]
    b_grad[...] = bias


def call(kernel, name, outs, *operands, scalars=0, fetched=0, scratch=(), copies=0, flops=10**6):
    outs = tuple(jax.ShapeDtypeStruct(*o) for o in outs)
    moved = sum(o.size * o.dtype.itemsize for o in (*outs, *operands))
    return pl.pallas_call(
        kernel,
        out_shape=outs,
        in_specs=sspec(scalars)
        + vspec(len(operands) - scalars - fetched)
        + [pl.BlockSpec(memory_space=pltpu.HBM)] * fetched,
        out_specs=tuple(vspec(len(outs))),
        scratch_shapes=[pltpu.VMEM(*s) for s in scratch] + [pltpu.SemaphoreType.DMA((copies,))] * (copies > 0),
        compiler_params=params(),
        cost_estimate=cost(flops, moved),
        name=name,
    )(*operands)


def exchange(x, axis):
    size = lax.axis_size(axis)
    return [x] + [
        lax.ppermute(x, axis, [(i, (i + s) % size) for i in range(size)]) for s in range(1, size)
    ]


def from_sides(first, last, lines):
    size, chans, at = lax.axis_size("rows"), lax.axis_size("chan"), lax.axis_index("rows")

    def send(x, pairs):
        return lax.ppermute(
            x, ("rows", "chan"), [(r * chans + i, q * chans + j) for r, q in pairs for i, j in lines]
        )

    if size == 2:
        got = send(jnp.where(at == 0, last, first), [(0, 1), (1, 0)])
        nothing = jnp.zeros_like(got)
        return jnp.where(at == 1, got, nothing), jnp.where(at == 0, got, nothing)
    up = [(i, i + 1) for i in range(size - 1)]
    down = [(i + 1, i) for i in range(size - 1)]
    return send(last, up), send(first, down)


def on_device(feature, out_grad, bank, select, latent, affine_w, affine_b):
    rows, samples, size = (lax.axis_size(a) for a in ("rows", "samples", "chan"))
    row_at, sample_at, chan_at = (lax.axis_index(a) for a in ("rows", "samples", "chan"))
    _, ch, height, width = feature.shape
    out_ch, in_ch = bank.shape[2:]
    pixels, all_ch = height * width, ch * size
    sign = 1 - 2 * jnp.remainder(sample_at, 2)
    place = jnp.stack([sample_at, chan_at, row_at, sign]).astype(jnp.int32)
    flops = 2 * TAPS * ch * ch * size * pixels

    def along(x, pairs):
        whole = []
        for b in range(samples):
            for i, j in pairs:
                if b % 2:
                    i, j = size - 1 - i, size - 1 - j
                whole.append((b * size + i, b * size + j))
        return lax.ppermute(x, ("samples", "chan"), whole)

    cotan = out_grad[0].reshape(ch, pixels)
    first, second = [], []

    def step(number, x, y):
        first.append(along(x, [(i, i + 1) for i in range(number - 1, size - 1)]))
        second.append(along(y, [(i + 1, i) for i in range(size - number)]))

    step(1, cotan, cotan)

    same = [(i, i) for i in range(size)]
    feat = feature[0].reshape(ch, pixels)
    feat_before, feat_after = from_sides(feat[:, :width], feat[:, pixels - width :], same)
    style, kernel, energy = call(
        energy_kernel,
        "energy",
        [((1, in_ch), F32), ((TAPS, out_ch, in_ch), F32), ((out_ch, 128), F32)],
        select,
        latent,
        affine_b[None],
        bank,
        affine_w,
        scalars=1,
        fetched=2,
        scratch=[(bank.shape, F32), (affine_w.shape, F32)],
        copies=2,
    )
    mod_own, scale, scale_row = call(
        modulated_kernel,
        "modulated",
        [((TAPS, out_ch, in_ch), BF16), ((out_ch, 128), F32), ((1, out_ch), F32)],
        kernel,
        style,
        *exchange(energy, "rows"),
    )
    extended = ((ch, (height + 2) * width), BF16)
    (feat,) = call(
        functools.partial(rows_kernel, height, width), "feat_rows", [extended], feat, feat_before, feat_after
    )
    message = ((ch, TAPS * ch), BF16)
    shares = rows if ch % (16 * rows) == 0 else 1
    share = ((ch // shares, TAPS * ch), BF16)
    count = size - 3
    whole_mod, own_mod, mod_ahead, mod_behind, mod_others = call(
        functools.partial(blocks_kernel, rows, size, shares),
        "mod_blocks",
        [
            ((TAPS, out_ch, all_ch), BF16),
            message,
            share,
            share,
            (((count + 1) * share[0][0], share[0][1]), BF16),
        ],
        place,
        *exchange(mod_own, "rows"),
        scalars=1,
        scratch=[((rows, TAPS, out_ch, in_ch), BF16), ((shares, size, *share[0]), BF16)],
    )
    first[0], second[0], feat, mod_ahead, mod_behind, mod_others = lax.optimization_barrier(
        (first[0], second[0], feat, mod_ahead, mod_behind, mod_others)
    )

    step(2, first[0], second[0])
    feat_end = lax.ppermute(feat, "chan", [(0, 1), (size - 1, size - 2)])
    forth = [(i, i + 1) for i in range(size - 1)]
    back = [(i + 1, i) for i in range(size - 1)]
    ring = [(i, (i + 2) % size) for i in range(size)]
    mods = [along(mod_ahead, forth), along(mod_behind, back), along(mod_others, ring)]
    pieces, starts, at = [], [], 0
    for piece in (latent, style, scale_row, select.astype(F32)):
        length = -(-piece.shape[1] // 128) * 128
        pieces.append(jnp.pad(piece, ((0, 0), (0, length - piece.shape[1]))))
        starts.append(at)
        at += length
    smalls = exchange(jnp.concatenate(pieces, axis=1), "samples")
    own_grad, grad_behind, grad_ahead, wide = call(
        functools.partial(near_grad_kernel, height, width),
        "near_grad",
        [message] * 3 + [((3 * ch, (height + 2) * width), BF16)],
        cotan,
        first[0],
        second[0],
        feat,
        scratch=[((3 * ch, pixels), BF16), ((3, 3 * ch, 3 * ch), F32)],
        flops=flops * 3 // size,
    )
    from_ahead, from_behind = along(grad_behind, back), along(grad_ahead, forth)
    first[1], second[1], feat_end, mods, smalls, wide = lax.optimization_barrier(
        (first[1], second[1], feat_end, mods, smalls, wide)
    )

    (grad_others,) = call(
        functools.partial(far_grad_kernel, count, height, width),
        "far_grad",
        [(((count + 1) * ch, TAPS * ch), BF16)],
        *first[1:],
        *second[1:],
        wide,
        feat_end,
        scratch=[
            ((3 * ch, (height + 2) * width), BF16),
            ((count * ch, pixels), BF16),
            ((ch, pixels), BF16),
            ((3, count * ch, 3 * ch), F32),
            ((3, ch, 3 * ch), F32),
        ],
        flops=flops * 2 // size,
    )
    from_others = along(grad_others, ring)
    mods = jnp.concatenate(mods, axis=0)
    mods = exchange(mods, "rows") if shares > 1 else [mods]
    parts = call(
        functools.partial(collect_kernel, rows, size),
        "collect",
        [((TAPS + 1, out_ch, in_ch), BF16)] * rows,
        place,
        scale,
        whole_mod,
        own_grad,
        from_ahead,
        from_behind,
        from_others,
        scalars=1,
        scratch=[((size, *message[0]), F32), ((rows, TAPS, out_ch, in_ch), BF16)],
    )
    parts, mods = lax.optimization_barrier((parts, mods))
    parts = [parts[0]] + [
        lax.ppermute(parts[r], "rows", [(i, (i + r) % rows) for i in range(rows)])
        for r in range(1, rows)
    ]
    end_main, end_before, end_after = call(
        functools.partial(end_input_kernel, rows, count, height, width),
        "end_input_grad",
        [((ch, pixels), BF16), ((ch, width), BF16), ((ch, width), BF16)],
        place,
        first[-1],
        second[-1],
        *mods,
        scalars=1,
        scratch=[
            ((ch, pixels), BF16),
            ((shares, *share[0]), F32),
            ((TAPS * ch, ch), BF16),
            ((height + 2, 3 * ch, width), F32),
        ],
        flops=flops // size,
    )
    (own,) = call(row_sum_kernel, "row_sum", [((TAPS + 1, out_ch, in_ch), BF16)], *parts)
    every = exchange(own, "samples")
    outward = [(1, 0), (size - 2, size - 1)]
    far_main = lax.ppermute(end_main, "chan", outward)

    own, mods = lax.optimization_barrier((own, mods))
    main, before, after = call(
        functools.partial(input_grad_kernel, rows, count, height, width),
        "input_grad",
        [((ch, pixels), F32), ((ch, width), F32), ((ch, width), F32)],
        place,
        cotan,
        first[0],
        second[0],
        *first[1:],
        *second[1:],
        own_mod,
        *mods,
        scalars=1,
        scratch=[
            (((3 + count) * ch, pixels), BF16),
            ((3 + count, shares, *share[0]), F32),
            ((TAPS * ch, (3 + count) * ch), BF16),
            ((height + 2, 3 * ch, width), F32),
        ],
        flops=flops,
    )
    every, main, before, after = lax.optimization_barrier((every, main, before, after))
    bank_grad, style_part = call(
        functools.partial(bank_grad_kernel, samples, starts[1:]),
        "bank_grad",
        [(bank.shape, F32), ((samples, in_ch), F32)],
        place,
        bank,
        *every,
        *smalls,
        scalars=1,
        scratch=[((samples, TAPS + 1, out_ch, in_ch), BF16), ((samples, *smalls[0].shape), F32)],
    )
    style_part, sides = lax.optimization_barrier((style_part, (before, after, end_before, end_after)))
    style_parts = exchange(style_part, "chan")
    above, below = from_sides(*sides[:2], same)
    end_above, end_below = from_sides(*sides[2:], outward)
    from_above, from_below = above + end_above.astype(F32), below + end_below.astype(F32)
    edge = jnp.concatenate(
        [from_above[:, None], jnp.zeros((ch, height - 2, width), F32), from_below[:, None]], axis=1
    )
    total = (main + far_main.astype(F32)).reshape(ch, height, width) + edge
    feature_grad = total.astype(BF16)[None]
    affine_w_grad, affine_b_grad = call(
        functools.partial(affine_kernel, samples, size),
        "affine",
        [(affine_w.shape, F32), ((1, in_ch), F32)],
        place,
        *style_parts,
        *smalls,
        scalars=1,
        scratch=[((samples, latent.shape[1]), F32), ((size, samples, in_ch), F32)],
    )
    return (feature_grad, bank_grad, affine_w_grad, affine_b_grad[0])


def solution(mesh):
    return jax.shard_map(
        on_device,
        mesh=mesh,
        in_specs=(
            P("samples", "chan", "rows", None),
            P("samples", "chan", "rows", None),
            P(None, None, "chan", "rows"),
            P("samples", None),
            P("samples", None),
            P(None, "rows"),
            P("rows"),
        ),
        out_specs=(
            P("samples", "chan", "rows", None),
            P(None, None, "chan", "rows"),
            P(None, "rows"),
            P("rows"),
        ),
        check_vma=False,
    )
```

time: 114 us -> 106 us (0.930)
  local copies, waits for them, and re-layouts: 12.6 us -> 5.73 us
  starting transfers between devices: 44.7 us -> 47.1 us
  Pallas kernels: 26.2 us -> 24.3 us
  waiting for transfers between devices: 27.9 us -> 26.1 us
    all_to_all x3 -> x0, starting transfers between devices: 16.9 us -> none  [the longest x1 8.32 us: on_device(): near_got = lax.all_to_all(near, 'chan', 0, 0)]
    ppermute x6 -> x10, starting transfers between devices: 12.5 us -> 23 us  [along(): return lax.ppermute(x, ('samples', 'chan'), whole)]
    ppermute x8 -> x12, waiting for transfers between devices: 7.33 us -> 15.8 us  [exchange(): lax.ppermute(x, axis, [(i, (i + s) % size) for i in range(size)])]
    unnamed x43 -> x23, local copies, waits for them, and re-layouts: 12.2 us -> 5.37 us
    ppermute x8 -> x12, starting transfers between devices: 8.3 us -> 13.6 us  [exchange(): lax.ppermute(x, axis, [(i, (i + s) % size) for i in range(size)])]
    ppermute x3 -> x5, waiting for transfers between devices: 5.5 us -> 0.23 us  [the longest x3 0.23 us: send(): lax.ppermute(x, ('rows', 'chan'), [(r * chans + i, q * chans + j) for r,...]
    all_to_all x3 -> x0, waiting for transfers between devices: 4.91 us -> none  [the longest x1 4.9 us: on_device(): style_parts = lax.all_to_all(style_parts, 'chan', 0, 0)]
    ppermute x3 -> x5, starting transfers between devices: 5.17 us -> 9.31 us  [the longest x1 4.94 us: on_device(): feat_end = lax.ppermute(feat, 'chan', [(0, 1), (size - 1, size - 2)])]
  transfers between devices with their start and end apart: 21 -> 28, of which waited for: 8 -> 14; matrix products, arithmetic and copies ran while one was open for 1% -> 1% of each run, Pallas kernels for 21% -> 18%
where the time goes in v6:
time: 106 us
  starting transfers between devices  47.1 us (44%)
  waiting for transfers between devices  26.1 us (25%)
  Pallas kernels  24.3 us (23%)
  local copies, waits for them, and re-layouts  5.73 us (5%)
  other arithmetic  1.37 us (1%)
    pallas_call x12, Pallas kernels, call(): pl.pallas_call(kernel, out_shape=outs, in_specs=sspec(scalars) + vspec(le...  24.3 us
    ppermute x10, starting transfers between devices, along(): return lax.ppermute(x, ('samples', 'chan'), whole)  23 us
    ppermute x12, waiting for transfers between devices, exchange(): lax.ppermute(x, axis, [(i, (i + s) % size) for i in range(size)])  15.8 us
    ppermute x12, starting transfers between devices, exchange(): lax.ppermute(x, axis, [(i, (i + s) % size) for i in range(size)])  13.6 us
    ppermute x1, waiting for transfers between devices, on_device(): lax.ppermute(parts[r], 'rows', [(i, (i + r) % rows) for i in range(rows)])  5.89 us
    unnamed x23, local copies, waits for them, and re-layouts  5.37 us
    ppermute x1, starting transfers between devices, on_device(): feat_end = lax.ppermute(feat, 'chan', [(0, 1), (size - 1, size - 2)])  4.94 us
    ppermute x10, waiting for transfers between devices, along(): return lax.ppermute(x, ('samples', 'chan'), whole)  4.19 us
  transfers between devices with their start and end apart: 28, of which 14 were waited for; matrix products, arithmetic and copies ran while one was open for 1% of the time, Pallas kernels for 18%

profile of v6, /device:TPU:0, one launch (start us, length us, event | category | flops | bytes accessed | tf_op | source)
XLA Modules:
  0.0 105.7 jit_solution(17315055882067879809)
XLA Ops:
  0.7 1.3 %copy.13 = bf16[8,8,8,512]{3,1,2,0:T(8,128)(2,1)S(1)} copy(bf16[8,8,8,512]{3,2,1,0:T(8,128)(2,1)} %bitcast.32) | data formatting | bytes 1048576
  1.9 5.0 %collective-permute-start.2 = (bf16[64,4096]{1,0:T(8,128)(2,1)S(1)}, bf16[64,4096]{1,0:T(8,128)(2,1)S(1)}, u32[]{:S(2)}, u32[]{:S(2)}) collective-permute-start(bf16[64,4096]{1,0:T(8,128)(2,1)S(1)} %bitcast.25), channel_id=1, source_target_pairs={{0,1},{1,2},{2,3},{7,6},{6,5},{5,4},{8,9},{9,10},{10,11},{15,14},{... | collective-permute-start | bytes 1572872 | tf_op jit(solution)/shard_map/ppermute | solution.py:408
  6.9 1.3 %collective-permute-start.3 = (bf16[64,4096]{1,0:T(8,128)(2,1)S(1)}, bf16[64,4096]{1,0:T(8,128)(2,1)S(1)}, u32[]{:S(2)}, u32[]{:S(2)}) collective-permute-start(bf16[64,4096]{1,0:T(8,128)(2,1)S(1)} %bitcast.26), channel_id=1, source_target_pairs={{1,0},{2,1},{3,2},{6,7},{5,6},{4,5},{9,8},{10,9},{11,10},{14,15},{... | collective-permute-start | bytes 1572872 | tf_op jit(solution)/shard_map/ppermute | solution.py:408
  8.2 1.3 %copy-done = f32[4,9,64,128]{3,2,1,0:T(8,128)S(1)} copy-done((f32[4,9,64,128]{3,2,1,0:T(8,128)S(1)}, f32[4,9,64,128]{3,2,1,0:T(8,128)}, u32[]{:S(2)}) %copy-start) | copy-done | bytes 1179672
  9.5 0.7 copy-done.3
  10.2 0.7 copy-done.5
  10.8 0.7 copy-done.6
  11.5 1.2 %energy.1 = (f32[1,128]{1,0:T(1,128)S(1)}, f32[9,64,128]{2,1,0:T(8,128)S(1)}, f32[64,128]{1,0:T(8,128)S(1)}) custom-call(s32[1,4]{1,0:T(1,128)S(1)} %copy-done.6, f32[1,512]{1,0:T(1,128)S(1)} %copy-done.3, f32[1,128]{1,0:T(1,128)S(1)} %bitcast.29, f32[4,9,64,128]{3,2,1,0:T(8,128)S(1)} %copy-done, f32[512,128]{1,0:T(8,128)S(1)} %copy-done.2), custom_call_target="tpu_custom_call" | custom-call | flops 1000000 | bytes 1772560 | tf_op jit(solution)/shard_map/energy/pallas_call | solution.py:353
  12.7 1.6 %collective-permute-start = (f32[64,128]{1,0:T(8,128)S(1)}, f32[64,128]{1,0:T(8,128)S(1)}, u32[]{:S(2)}, u32[]{:S(2)}) collective-permute-start(f32[64,128]{1,0:T(8,128)S(1)} %get-tuple-element.68.refs_0_), channel_id=1, source_target_pairs={{0,16},{16,0},{1,17},{17,1},{2,18},{18,2},{3,19},{19,3},{4,20},{20... | collective-permute-start | bytes 98312 | tf_op jit(solution)/shard_map/ppermute | solution.py:370
  14.3 0.2 copy.14
  14.5 0.6 collective-permute-start.4
  15.1 0.1 pad_add_fusion.place
  15.2 1.5 %collective-permute-done.refs_1_ = f32[64,128]{1,0:T(8,128)S(1)} collective-permute-done((f32[64,128]{1,0:T(8,128)S(1)}, f32[64,128]{1,0:T(8,128)S(1)}, u32[]{:S(2)}, u32[]{:S(2)}) %collective-permute-start) | collective-permute-done | bytes 32800 | tf_op jit(solution)/shard_map/ppermute | solution.py:370
  16.7 0.1 modulated.1
  16.8 1.9 %collective-permute-start.1 = (bf16[9,64,128]{2,1,0:T(8,128)(2,1)S(1)}, bf16[9,64,128]{2,1,0:T(8,128)(2,1)S(1)}, u32[]{:S(2)}, u32[]{:S(2)}) collective-permute-start(bf16[9,64,128]{2,1,0:T(8,128)(2,1)S(1)} %get-tuple-element.70.refs_0_), channel_id=1, source_target_pairs={{0,16},{16,0},{1,17},{17,1},{2,18},{18,2},{3,19},{19,3},{4,20},{20... | collective-permute-start | bytes 442376 | tf_op jit(solution)/shard_map/ppermute | solution.py:370
  18.7 0.2 collective-permute-done.4
  19.0 3.0 %collective-permute-done.1.refs_1_ = bf16[9,64,128]{2,1,0:T(8,128)(2,1)S(1)} collective-permute-done((bf16[9,64,128]{2,1,0:T(8,128)(2,1)S(1)}, bf16[9,64,128]{2,1,0:T(8,128)(2,1)S(1)}, u32[]{:S(2)}, u32[]{:S(2)}) %collective-permute-start.1) | collective-permute-done | bytes 147488 | tf_op jit(solution)/shard_map/ppermute | solution.py:370
  22.0 0.7 mod_blocks.1
  22.8 4.9 %collective-permute-start.9 = (bf16[64,5120]{1,0:T(8,128)(2,1)S(1)}, bf16[64,5120]{1,0:T(8,128)(2,1)S(1)}, u32[]{:S(2)}, u32[]{:S(2)}) collective-permute-start(bf16[64,5120]{1,0:T(8,128)(2,1)S(1)} %feat_rows.1.refs_3_), channel_id=1, source_target_pairs={{0,1},{3,2},{4,5},{7,6},{8,9},{11,10},{12,13},{15,14},{16,17},{19,... | collective-permute-start | bytes 1966088 | tf_op jit(solution)/shard_map/ppermute | solution.py:472
  27.7 0.7 collective-permute-start.7
  28.4 1.3 %collective-permute-start.8 = (bf16[64,4096]{1,0:T(8,128)(2,1)S(1)}, bf16[64,4096]{1,0:T(8,128)(2,1)S(1)}, u32[]{:S(2)}, u32[]{:S(2)}) collective-permute-start(bf16[64,4096]{1,0:T(8,128)(2,1)S(1)} %collective-permute-done.3.refs_2_), channel_id=1, source_target_pairs={{1,0},{2,1},{6,7},{5,6},{9,8},{10,9},{14,15},{13,14},{17,16},{18,1... | collective-permute-start | bytes 1572872 | tf_op jit(solution)/shard_map/ppermute | solution.py:408
  29.8 4.7 %collective-permute-start.10 = (bf16[32,576]{1,0:T(8,128)(2,1)S(1)}, bf16[32,576]{1,0:T(8,128)(2,1)S(1)}, u32[]{:S(2)}, u32[]{:S(2)}) collective-permute-start(bf16[32,576]{1,0:T(8,128)(2,1)S(1)} %get-tuple-element.81), channel_id=1, source_target_pairs={{0,1},{1,2},{2,3},{7,6},{6,5},{5,4},{8,9},{9,10},{10,11},{15,14},{... | collective-permute-start | bytes 110600 | tf_op jit(solution)/shard_map/ppermute | solution.py:408
  34.5 0.1 collective-permute-start.13
  34.5 3.0 %collective-permute-done.13.refs_5_ = f32[1,896]{1,0:T(1,128)S(1)} collective-permute-done((f32[1,896]{1,0:T(1,128)S(1)}, f32[1,896]{1,0:T(1,128)S(1)}, u32[]{:S(2)}, u32[]{:S(2)}) %collective-permute-start.13) | collective-permute-done | bytes 3616 | tf_op jit(solution)/shard_map/ppermute | solution.py:370
  37.5 1.5 %collective-permute-start.14 = (f32[1,896]{1,0:T(1,128)S(1)}, f32[1,896]{1,0:T(1,128)S(1)}, u32[]{:S(2)}, u32[]{:S(2)}) collective-permute-start(f32[1,896]{1,0:T(1,128)S(1)} %fusion.2.refs_4_), channel_id=1, source_target_pairs={{0,8},{4,12},{8,0},{12,4},{1,9},{5,13},{9,1},{13,5},{2,10},{6,14},... | collective-permute-start | bytes 10760 | tf_op jit(solution)/shard_map/ppermute | solution.py:370
  39.1 2.1 %collective-permute-done.14.refs_6_ = f32[1,896]{1,0:T(1,128)S(1)} collective-permute-done((f32[1,896]{1,0:T(1,128)S(1)}, f32[1,896]{1,0:T(1,128)S(1)}, u32[]{:S(2)}, u32[]{:S(2)}) %collective-permute-start.14) | collective-permute-done | bytes 3616 | tf_op jit(solution)/shard_map/ppermute | solution.py:370
  41.1 1.3 %collective-permute-done.15.refs_7_ = f32[1,896]{1,0:T(1,128)S(1)} collective-permute-done((f32[1,896]{1,0:T(1,128)S(1)}, f32[1,896]{1,0:T(1,128)S(1)}, u32[]{:S(2)}, u32[]{:S(2)}) %collective-permute-start.15) | collective-permute-done | bytes 3616 | tf_op jit(solution)/shard_map/ppermute | solution.py:370
  42.5 1.5 %collective-permute-start.12 = (bf16[64,576]{1,0:T(8,128)(2,1)S(1)}, bf16[64,576]{1,0:T(8,128)(2,1)S(1)}, u32[]{:S(2)}, u32[]{:S(2)}) collective-permute-start(bf16[64,576]{1,0:T(8,128)(2,1)S(1)} %get-tuple-element.83), channel_id=1, source_target_pairs={{0,2},{1,3},{2,0},{3,1},{7,5},{6,4},{5,7},{4,6},{8,10},{9,11},{10,... | collective-permute-start | bytes 221192 | tf_op jit(solution)/shard_map/ppermute | solution.py:408
  44.0 1.3 %collective-permute-start.11 = (bf16[32,576]{1,0:T(8,128)(2,1)S(1)}, bf16[32,576]{1,0:T(8,128)(2,1)S(1)}, u32[]{:S(2)}, u32[]{:S(2)}) collective-permute-start(bf16[32,576]{1,0:T(8,128)(2,1)S(1)} %get-tuple-element.82), channel_id=1, source_target_pairs={{1,0},{2,1},{3,2},{6,7},{5,6},{4,5},{9,8},{10,9},{11,10},{14,15},{... | collective-permute-start | bytes 110600 | tf_op jit(solution)/shard_map/ppermute | solution.py:408
  45.3 3.3 %near_grad.1 = (bf16[64,576]{1,0:T(8,128)(2,1)S(1)}, bf16[64,576]{1,0:T(8,128)(2,1)S(1)}, bf16[64,576]{1,0:T(8,128)(2,1)S(1)}, bf16[192,5120]{1,0:T(8,128)(2,1)S(1)}) custom-call(bf16[64,4096]{1,0:T(8,128)(2,1)S(1)} %bitcast.27, bf16[64,4096]{1,0:T(8,128)(2,1)S(1)} %collective-permute-done.2.refs_1_, bf16[64,4096]{1,0:T(8,128)(2,1)S(1)} %collective-permute-done.3.refs_2_, ...), custom_call_target="tpu_custom_call" | custom-call | flops 905969664 | bytes 4415488 | tf_op jit(solution)/shard_map/near_grad/pallas_call | solution.py:353
  48.5 1.3 %collective-permute-done.11 = bf16[32,576]{1,0:T(8,128)(2,1)S(1)} collective-permute-done((bf16[32,576]{1,0:T(8,128)(2,1)S(1)}, bf16[32,576]{1,0:T(8,128)(2,1)S(1)}, u32[]{:S(2)}, u32[]{:S(2)}) %collective-permute-start.11) | collective-permute-done | bytes 36896 | tf_op jit(solution)/shard_map/ppermute | solution.py:408
  49.9 4.6 %far_grad.1 = bf16[128,576]{1,0:T(8,128)(2,1)S(1)} custom-call(bf16[64,4096]{1,0:T(8,128)(2,1)S(1)} %collective-permute-done.7.refs_0_.refs_3_.first, bf16[64,4096]{1,0:T(8,128)(2,1)S(1)} %collective-permute-done.8.refs_1_.refs_4_.second, bf16[192,5120]{1,0:T(8,128)(2,1)S(1)} %get-tuple-element.88.refs_2_, bf16[64,5120]{1,0:T(8,128)(2,1)S(1)} %collective-permute-done.9.refs_3_), custom_call_target="tpu_custom_call" | custom-call | flops 603979776 | bytes 3817472 | tf_op jit(solution)/shard_map/far_grad/pallas_call | solution.py:353
  54.5 1.5 %collective-permute-start.16 = (bf16[128,576]{1,0:T(8,128)(2,1)S(1)}, bf16[128,576]{1,0:T(8,128)(2,1)S(1)}, u32[]{:S(2)}, u32[]{:S(2)}) collective-permute-start(bf16[128,576]{1,0:T(8,128)(2,1)S(1)} %far_grad.1), channel_id=1, source_target_pairs={{0,2},{1,3},{2,0},{3,1},{7,5},{6,4},{5,7},{4,6},{8,10},{9,11},{10,... | collective-permute-start | bytes 442376 | tf_op jit(solution)/shard_map/ppermute | solution.py:408
  56.0 1.2 %collective-permute-start.17 = (bf16[128,576]{1,0:T(8,128)(2,1)S(1)}, bf16[128,576]{1,0:T(8,128)(2,1)S(1)}, u32[]{:S(2)}, u32[]{:S(2)}) collective-permute-start(bf16[128,576]{1,0:T(8,128)(2,1)S(1)} %constant_dynamic-update-slice_fusion.refs_6_.refs_0_), channel_id=1, source_target_pairs={{0,16},{16,0},{1,17},{17,1},{2,18},{18,2},{3,19},{19,3},{4,20},{20... | collective-permute-start | bytes 442376 | tf_op jit(solution)/shard_map/ppermute | solution.py:370
  57.2 1.3 %collective-permute-start.5 = (bf16[64,576]{1,0:T(8,128)(2,1)S(1)}, bf16[64,576]{1,0:T(8,128)(2,1)S(1)}, u32[]{:S(2)}, u32[]{:S(2)}) collective-permute-start(bf16[64,576]{1,0:T(8,128)(2,1)S(1)} %get-tuple-element.79), channel_id=1, source_target_pairs={{1,0},{2,1},{3,2},{6,7},{5,6},{4,5},{9,8},{10,9},{11,10},{14,15},{... | collective-permute-start | bytes 221192 | tf_op jit(solution)/shard_map/ppermute | solution.py:408
  58.5 4.6 %collective-permute-start.6 = (bf16[64,576]{1,0:T(8,128)(2,1)S(1)}, bf16[64,576]{1,0:T(8,128)(2,1)S(1)}, u32[]{:S(2)}, u32[]{:S(2)}) collective-permute-start(bf16[64,576]{1,0:T(8,128)(2,1)S(1)} %get-tuple-element.80), channel_id=1, source_target_pairs={{0,1},{1,2},{2,3},{7,6},{6,5},{5,4},{8,9},{9,10},{10,11},{15,14},{... | collective-permute-start | bytes 221192 | tf_op jit(solution)/shard_map/ppermute | solution.py:408
  63.1 0.5 collective-permute-done.5.ahead
  63.5 1.5 %collective-permute-done.6.behind = bf16[64,576]{1,0:T(8,128)(2,1)S(1)} collective-permute-done((bf16[64,576]{1,0:T(8,128)(2,1)S(1)}, bf16[64,576]{1,0:T(8,128)(2,1)S(1)}, u32[]{:S(2)}, u32[]{:S(2)}) %collective-permute-start.6) | collective-permute-done | bytes 73760 | tf_op jit(solution)/shard_map/ppermute | solution.py:408
  65.1 0.8 collective-permute-done.16.others
  65.9 1.1 collect.1
  67.0 1.2 %collective-permute-start.18 = (bf16[10,64,128]{2,1,0:T(8,128)(2,1)S(1)}, bf16[10,64,128]{2,1,0:T(8,128)(2,1)S(1)}, u32[]{:S(2)}, u32[]{:S(2)}) collective-permute-start(bf16[10,64,128]{2,1,0:T(8,128)(2,1)S(1)} %get-tuple-element.96), channel_id=1, source_target_pairs={{0,16},{16,0},{1,17},{17,1},{2,18},{18,2},{3,19},{19,3},{4,20},{20... | collective-permute-start | bytes 491528 | tf_op jit(solution)/shard_map/ppermute | solution.py:536
  68.2 5.9 %collective-permute-done.18.refs_1_ = bf16[10,64,128]{2,1,0:T(8,128)(2,1)S(1)} collective-permute-done((bf16[10,64,128]{2,1,0:T(8,128)(2,1)S(1)}, bf16[10,64,128]{2,1,0:T(8,128)(2,1)S(1)}, u32[]{:S(2)}, u32[]{:S(2)}) %collective-permute-start.18) | collective-permute-done | bytes 163872 | tf_op jit(solution)/shard_map/ppermute | solution.py:536
  74.1 0.2 row_sum.1.refs_0_
  74.3 0.1 collective-permute-start.19
  74.4 1.7 %collective-permute-start.20 = (bf16[10,64,128]{2,1,0:T(8,128)(2,1)S(1)}, bf16[10,64,128]{2,1,0:T(8,128)(2,1)S(1)}, u32[]{:S(2)}, u32[]{:S(2)}) collective-permute-start(bf16[10,64,128]{2,1,0:T(8,128)(2,1)S(1)} %row_sum.1.refs_0_), channel_id=1, source_target_pairs={{0,8},{4,12},{8,0},{12,4},{1,9},{5,13},{9,1},{13,5},{2,10},{6,14},... | collective-permute-start | bytes 491528 | tf_op jit(solution)/shard_map/ppermute | solution.py:370
  76.1 1.4 %collective-permute-start.21 = (bf16[10,64,128]{2,1,0:T(8,128)(2,1)S(1)}, bf16[10,64,128]{2,1,0:T(8,128)(2,1)S(1)}, u32[]{:S(2)}, u32[]{:S(2)}) collective-permute-start(bf16[10,64,128]{2,1,0:T(8,128)(2,1)S(1)} %row_sum.1.refs_0_), channel_id=1, source_target_pairs={{0,12},{4,0},{8,4},{12,8},{1,13},{5,1},{9,5},{13,9},{2,14},{6,2},{... | collective-permute-start | bytes 491528 | tf_op jit(solution)/shard_map/ppermute | solution.py:370
  77.5 4.0 %end_input_grad.1 = (bf16[64,4096]{1,0:T(8,128)(2,1)S(1)}, bf16[64,512]{1,0:T(8,128)(2,1)S(1)}, bf16[64,512]{1,0:T(8,128)(2,1)S(1)}) custom-call(s32[4]{0:T(128)S(1)} %pad_add_fusion.place, bf16[64,4096]{1,0:T(8,128)(2,1)S(1)} %collective-permute-done.7.refs_0_.refs_3_.first, bf16[64,4096]{1,0:T(8,128)(2,1)S(1)} %collective-permute-done.8.refs_1_.refs_4_.second, ...), custom_call_target="tpu_custom_call" | custom-call | flops 301989888 | bytes 1998864 | tf_op jit(solution)/shard_map/end_input_grad/pallas_call | solution.py:353
  81.5 1.3 %collective-permute-start.22 = (bf16[64,4096]{1,0:T(8,128)(2,1)S(1)}, bf16[64,4096]{1,0:T(8,128)(2,1)S(1)}, u32[]{:S(2)}, u32[]{:S(2)}) collective-permute-start(bf16[64,4096]{1,0:T(8,128)(2,1)S(1)} %get-tuple-element.106), channel_id=1, source_target_pairs={{1,0},{2,3},{5,4},{6,7},{9,8},{10,11},{13,12},{14,15},{17,16},{18,... | collective-permute-start | bytes 1572872 | tf_op jit(solution)/shard_map/ppermute | solution.py:559
  82.8 4.5 %input_grad.1 = (f32[64,4096]{1,0:T(8,128)S(1)}, f32[64,512]{1,0:T(8,128)S(1)}, f32[64,512]{1,0:T(8,128)S(1)}) custom-call(s32[4]{0:T(128)S(1)} %pad_add_fusion.place, bf16[64,4096]{1,0:T(8,128)(2,1)S(1)} %bitcast.28, bf16[64,4096]{1,0:T(8,128)(2,1)S(1)} %collective-permute-done.2.refs_1_, bf16[64,4096]{1,0:T(8,128)(2,1)S(1)} %collective-permute-done.3.refs_2_, ...), custom_call_target="tpu_custom_call" | custom-call | flops 1207959552 | bytes 4300816 | tf_op jit(solution)/shard_map/input_grad/pallas_call | solution.py:353
  87.4 2.9 %bank_grad.1 = (f32[4,9,64,128]{3,2,1,0:T(8,128)}, f32[4,128]{1,0:T(4,128)S(1)}) custom-call(s32[4]{0:T(128)S(1)} %pad_add_fusion.place, f32[4,9,64,128]{3,2,1,0:T(8,128)S(1)} %copy-done.1, bf16[10,64,128]{2,1,0:T(8,128)(2,1)S(1)} %row_sum.1.refs_0_, bf16[10,64,128]{2,1,0:T(8,128)(2,1)S(1)} %collective-permute-done.19.refs_1_, ...), custom_call_target="tpu_custom_call" | custom-call | flops 1000000 | bytes 3031056 | tf_op jit(solution)/shard_map/bank_grad/pallas_call | solution.py:353
  90.3 1.2 %collective-permute-start.23 = (f32[64,512]{1,0:T(8,128)S(1)}, f32[64,512]{1,0:T(8,128)S(1)}, u32[]{:S(2)}, u32[]{:S(2)}) collective-permute-start(f32[64,512]{1,0:T(8,128)S(1)} %broadcast_select_fusion.1), channel_id=1, source_target_pairs={{0,16},{1,17},{2,18},{3,19},{16,0},{17,1},{18,2},{19,3},{4,20},{5,... | collective-permute-start | bytes 393224 | tf_op jit(solution)/shard_map/ppermute | solution.py:378
  91.5 1.3 %collective-permute-start.24 = (bf16[64,512]{1,0:T(8,128)(2,1)S(1)}, bf16[64,512]{1,0:T(8,128)(2,1)S(1)}, u32[]{:S(2)}, u32[]{:S(2)}) collective-permute-start(bf16[64,512]{1,0:T(8,128)(2,1)S(1)} %broadcast_select_fusion), channel_id=1, source_target_pairs={{1,16},{2,19},{17,0},{18,3},{5,20},{6,23},{21,4},{22,7},{9,24},{10... | collective-permute-start | bytes 196616 | tf_op jit(solution)/shard_map/ppermute | solution.py:378
  92.8 3.0 %collective-permute-start.25 = (f32[4,128]{1,0:T(4,128)S(1)}, f32[4,128]{1,0:T(4,128)S(1)}, u32[]{:S(2)}, u32[]{:S(2)}) collective-permute-start(f32[4,128]{1,0:T(4,128)S(1)} %get-tuple-element.125.refs_0_), channel_id=1, source_target_pairs={{0,1},{1,2},{2,3},{3,0},{4,5},{5,6},{6,7},{7,4},{8,9},{9,10},{10,1... | collective-permute-start | bytes 6152 | tf_op jit(solution)/shard_map/ppermute | solution.py:370
  95.8 2.4 %collective-permute-done.25.refs_1_ = f32[4,128]{1,0:T(4,128)S(1)} collective-permute-done((f32[4,128]{1,0:T(4,128)S(1)}, f32[4,128]{1,0:T(4,128)S(1)}, u32[]{:S(2)}, u32[]{:S(2)}) %collective-permute-start.25) | collective-permute-done | bytes 2080 | tf_op jit(solution)/shard_map/ppermute | solution.py:370
  98.2 1.1 %collective-permute-start.27 = (f32[4,128]{1,0:T(4,128)S(1)}, f32[4,128]{1,0:T(4,128)S(1)}, u32[]{:S(2)}, u32[]{:S(2)}) collective-permute-start(f32[4,128]{1,0:T(4,128)S(1)} %get-tuple-element.125.refs_0_), channel_id=1, source_target_pairs={{0,3},{1,0},{2,1},{3,2},{4,7},{5,4},{6,5},{7,6},{8,11},{9,8},{10,9... | collective-permute-start | bytes 6152 | tf_op jit(solution)/shard_map/ppermute | solution.py:370
  99.3 0.1 pad.11.clone
  99.4 0.9 collective-permute-done.26.refs_2_
  100.3 1.5 %collective-permute-done.27.refs_3_ = f32[4,128]{1,0:T(4,128)S(1)} collective-permute-done((f32[4,128]{1,0:T(4,128)S(1)}, f32[4,128]{1,0:T(4,128)S(1)}, u32[]{:S(2)}, u32[]{:S(2)}) %collective-permute-start.27) | collective-permute-done | bytes 2080 | tf_op jit(solution)/shard_map/ppermute | solution.py:370
  101.8 1.7 %affine.1 = (f32[512,128]{1,0:T(8,128)}, f32[1,128]{1,0:T(1,128)}) custom-call(s32[4]{0:T(128)S(1)} %pad_add_fusion.place, f32[4,128]{1,0:T(4,128)S(1)} %get-tuple-element.125.refs_0_, f32[4,128]{1,0:T(4,128)S(1)} %collective-permute-done.25.refs_1_, f32[4,128]{1,0:T(4,128)S(1)} %collective-permute-done.26.refs_2_, ...), custom_call_target="tpu_custom_call" | custom-call | flops 1000000 | bytes 285200 | tf_op jit(solution)/shard_map/affine/pallas_call | solution.py:353
  103.6 0.1 copy.11
  103.7 0.1 copy.12
  103.9 0.1 convert_add_fusion
  104.0 0.6 copy.15
  104.6 1.1 %fusion = bf16[1,64,8,512]{3,2,1,0:T(8,128)(2,1)} fusion(f32[1,64,1,512]{3,2,1,0:T(1,128)S(1)} %copy.12, f32[1,64,1,512]{3,2,1,0:T(1,128)S(1)} %copy.11, f32[8]{0:T(128)S(1)} %pad.11.clone, f32[1,64,8,512]{3,2,1,0:T(8,128)S(1)} %bitcast.30), kind=kLoop, calls=%fused_computation.1 | loop fusion | flops 1048576 | bytes 1835040 | tf_op jit(solution)/shard_map/convert_element_type | solution.py:604
  (42 shorter events, 0.3 us)
Async XLA Ops:
  0.6 7.6 %copy-start.2 = (f32[512,128]{1,0:T(8,128)S(1)}, f32[512,128]{1,0:T(8,128)}, u32[]{:S(2)}) copy-start(f32[512,128]{1,0:T(8,128)} %w_hbm.1) | copy-start | bytes 786436
  0.6 13.7 %copy-start.8 = (bf16[1,64,8,512]{3,2,1,0:T(8,128)(2,1)S(1)}, bf16[1,64,8,512]{3,2,1,0:T(8,128)(2,1)}, u32[]{:S(2)}) copy-start(bf16[1,64,8,512]{3,2,1,0:T(8,128)(2,1)} %param.7) | copy-start | bytes 1572868
  1.9 20.8 %collective-permute-start.2 = (bf16[64,4096]{1,0:T(8,128)(2,1)S(1)}, bf16[64,4096]{1,0:T(8,128)(2,1)S(1)}, u32[]{:S(2)}, u32[]{:S(2)}) collective-permute-start(bf16[64,4096]{1,0:T(8,128)(2,1)S(1)} %bitcast.25), channel_id=1, source_target_pairs={{0,1},{1,2},{2,3},{7,6},{6,5},{5,4},{8,9},{9,10},{10,11},{15,14},{... | collective-permute-start | bytes 1572872 | tf_op jit(solution)/shard_map/ppermute | solution.py:408
  6.9 15.9 %collective-permute-start.3 = (bf16[64,4096]{1,0:T(8,128)(2,1)S(1)}, bf16[64,4096]{1,0:T(8,128)(2,1)S(1)}, u32[]{:S(2)}, u32[]{:S(2)}) collective-permute-start(bf16[64,4096]{1,0:T(8,128)(2,1)S(1)} %bitcast.26), channel_id=1, source_target_pairs={{1,0},{2,1},{3,2},{6,7},{5,6},{4,5},{9,8},{10,9},{11,10},{14,15},{... | collective-permute-start | bytes 1572872 | tf_op jit(solution)/shard_map/ppermute | solution.py:408
  8.2 1.3 %copy-start = (f32[4,9,64,128]{3,2,1,0:T(8,128)S(1)}, f32[4,9,64,128]{3,2,1,0:T(8,128)}, u32[]{:S(2)}) copy-start(f32[4,9,64,128]{3,2,1,0:T(8,128)} %bank.1) | copy-start | bytes 3538948
  9.5 0.7 copy-start.3
  10.2 0.7 copy-start.5
  10.8 0.7 copy-start.6
  12.7 4.0 %collective-permute-start = (f32[64,128]{1,0:T(8,128)S(1)}, f32[64,128]{1,0:T(8,128)S(1)}, u32[]{:S(2)}, u32[]{:S(2)}) collective-permute-start(f32[64,128]{1,0:T(8,128)S(1)} %get-tuple-element.68.refs_0_), channel_id=1, source_target_pairs={{0,16},{16,0},{1,17},{17,1},{2,18},{18,2},{3,19},{19,3},{4,20},{20... | collective-permute-start | bytes 98312 | tf_op jit(solution)/shard_map/ppermute | solution.py:370
  14.5 15.3 %copy-start.7 = (s32[1,4]{1,0:T(1,128)S(1)}, s32[1,4]{1,0:T(1,128)}, u32[]{:S(2)}) copy-start(s32[1,4]{1,0:T(1,128)} %sel.1) | copy-start | bytes 52
  14.5 20.0 %copy-start.4 = (f32[1,512]{1,0:T(1,128)S(1)}, f32[1,512]{1,0:T(1,128)}, u32[]{:S(2)}) copy-start(f32[1,512]{1,0:T(1,128)} %latent.1) | copy-start | bytes 6148
  14.5 4.4 %collective-permute-start.4 = (bf16[64,512]{1,0:T(8,128)(2,1)S(1)}, bf16[64,512]{1,0:T(8,128)(2,1)S(1)}, u32[]{:S(2)}, u32[]{:S(2)}) collective-permute-start(bf16[64,512]{1,0:T(8,128)(2,1)S(1)} %slice_select_fusion), channel_id=1, source_target_pairs={{0,16},{1,17},{2,18},{3,19},{16,0},{17,1},{18,2},{19,3},{4,20},{5,... | collective-permute-start | bytes 196616 | tf_op jit(solution)/shard_map/ppermute | solution.py:378
  16.8 5.2 %collective-permute-start.1 = (bf16[9,64,128]{2,1,0:T(8,128)(2,1)S(1)}, bf16[9,64,128]{2,1,0:T(8,128)(2,1)S(1)}, u32[]{:S(2)}, u32[]{:S(2)}) collective-permute-start(bf16[9,64,128]{2,1,0:T(8,128)(2,1)S(1)} %get-tuple-element.70.refs_0_), channel_id=1, source_target_pairs={{0,16},{16,0},{1,17},{17,1},{2,18},{18,2},{3,19},{19,3},{4,20},{20... | collective-permute-start | bytes 442376 | tf_op jit(solution)/shard_map/ppermute | solution.py:370
  22.8 27.1 %collective-permute-start.9 = (bf16[64,5120]{1,0:T(8,128)(2,1)S(1)}, bf16[64,5120]{1,0:T(8,128)(2,1)S(1)}, u32[]{:S(2)}, u32[]{:S(2)}) collective-permute-start(bf16[64,5120]{1,0:T(8,128)(2,1)S(1)} %feat_rows.1.refs_3_), channel_id=1, source_target_pairs={{0,1},{3,2},{4,5},{7,6},{8,9},{11,10},{12,13},{15,14},{16,17},{19,... | collective-permute-start | bytes 1966088 | tf_op jit(solution)/shard_map/ppermute | solution.py:472
  27.7 22.1 %collective-permute-start.7 = (bf16[64,4096]{1,0:T(8,128)(2,1)S(1)}, bf16[64,4096]{1,0:T(8,128)(2,1)S(1)}, u32[]{:S(2)}, u32[]{:S(2)}) collective-permute-start(bf16[64,4096]{1,0:T(8,128)(2,1)S(1)} %collective-permute-done.2.refs_1_), channel_id=1, source_target_pairs={{1,2},{2,3},{6,5},{5,4},{9,10},{10,11},{14,13},{13,12},{17,18},{18... | collective-permute-start | bytes 1572872 | tf_op jit(solution)/shard_map/ppermute | solution.py:408
  28.4 21.4 %collective-permute-start.8 = (bf16[64,4096]{1,0:T(8,128)(2,1)S(1)}, bf16[64,4096]{1,0:T(8,128)(2,1)S(1)}, u32[]{:S(2)}, u32[]{:S(2)}) collective-permute-start(bf16[64,4096]{1,0:T(8,128)(2,1)S(1)} %collective-permute-done.3.refs_2_), channel_id=1, source_target_pairs={{1,0},{2,1},{6,7},{5,6},{9,8},{10,9},{14,15},{13,14},{17,16},{18,1... | collective-permute-start | bytes 1572872 | tf_op jit(solution)/shard_map/ppermute | solution.py:408
  29.8 14.2 %collective-permute-start.10 = (bf16[32,576]{1,0:T(8,128)(2,1)S(1)}, bf16[32,576]{1,0:T(8,128)(2,1)S(1)}, u32[]{:S(2)}, u32[]{:S(2)}) collective-permute-start(bf16[32,576]{1,0:T(8,128)(2,1)S(1)} %get-tuple-element.81), channel_id=1, source_target_pairs={{0,1},{1,2},{2,3},{7,6},{6,5},{5,4},{8,9},{9,10},{10,11},{15,14},{... | collective-permute-start | bytes 110600 | tf_op jit(solution)/shard_map/ppermute | solution.py:408
  34.5 3.1 %collective-permute-start.13 = (f32[1,896]{1,0:T(1,128)S(1)}, f32[1,896]{1,0:T(1,128)S(1)}, u32[]{:S(2)}, u32[]{:S(2)}) collective-permute-start(f32[1,896]{1,0:T(1,128)S(1)} %fusion.2.refs_4_), channel_id=1, source_target_pairs={{0,4},{4,8},{8,12},{12,0},{1,5},{5,9},{9,13},{13,1},{2,6},{6,10},{... | collective-permute-start | bytes 10760 | tf_op jit(solution)/shard_map/ppermute | solution.py:370
  37.5 3.6 %collective-permute-start.14 = (f32[1,896]{1,0:T(1,128)S(1)}, f32[1,896]{1,0:T(1,128)S(1)}, u32[]{:S(2)}, u32[]{:S(2)}) collective-permute-start(f32[1,896]{1,0:T(1,128)S(1)} %fusion.2.refs_4_), channel_id=1, source_target_pairs={{0,8},{4,12},{8,0},{12,4},{1,9},{5,13},{9,1},{13,5},{2,10},{6,14},... | collective-permute-start | bytes 10760 | tf_op jit(solution)/shard_map/ppermute | solution.py:370
  41.1 1.3 %collective-permute-start.15 = (f32[1,896]{1,0:T(1,128)S(1)}, f32[1,896]{1,0:T(1,128)S(1)}, u32[]{:S(2)}, u32[]{:S(2)}) collective-permute-start(f32[1,896]{1,0:T(1,128)S(1)} %fusion.2.refs_4_), channel_id=1, source_target_pairs={{0,12},{4,0},{8,4},{12,8},{1,13},{5,1},{9,5},{13,9},{2,14},{6,2},{... | collective-permute-start | bytes 10760 | tf_op jit(solution)/shard_map/ppermute | solution.py:370
  42.5 7.4 %collective-permute-start.12 = (bf16[64,576]{1,0:T(8,128)(2,1)S(1)}, bf16[64,576]{1,0:T(8,128)(2,1)S(1)}, u32[]{:S(2)}, u32[]{:S(2)}) collective-permute-start(bf16[64,576]{1,0:T(8,128)(2,1)S(1)} %get-tuple-element.83), channel_id=1, source_target_pairs={{0,2},{1,3},{2,0},{3,1},{7,5},{6,4},{5,7},{4,6},{8,10},{9,11},{10,... | collective-permute-start | bytes 221192 | tf_op jit(solution)/shard_map/ppermute | solution.py:408
  44.0 5.9 %collective-permute-start.11 = (bf16[32,576]{1,0:T(8,128)(2,1)S(1)}, bf16[32,576]{1,0:T(8,128)(2,1)S(1)}, u32[]{:S(2)}, u32[]{:S(2)}) collective-permute-start(bf16[32,576]{1,0:T(8,128)(2,1)S(1)} %get-tuple-element.82), channel_id=1, source_target_pairs={{1,0},{2,1},{3,2},{6,7},{5,6},{4,5},{9,8},{10,9},{11,10},{14,15},{... | collective-permute-start | bytes 110600 | tf_op jit(solution)/shard_map/ppermute | solution.py:408
  54.5 11.4 %collective-permute-start.16 = (bf16[128,576]{1,0:T(8,128)(2,1)S(1)}, bf16[128,576]{1,0:T(8,128)(2,1)S(1)}, u32[]{:S(2)}, u32[]{:S(2)}) collective-permute-start(bf16[128,576]{1,0:T(8,128)(2,1)S(1)} %far_grad.1), channel_id=1, source_target_pairs={{0,2},{1,3},{2,0},{3,1},{7,5},{6,4},{5,7},{4,6},{8,10},{9,11},{10,... | collective-permute-start | bytes 442376 | tf_op jit(solution)/shard_map/ppermute | solution.py:408
  56.0 11.0 %collective-permute-start.17 = (bf16[128,576]{1,0:T(8,128)(2,1)S(1)}, bf16[128,576]{1,0:T(8,128)(2,1)S(1)}, u32[]{:S(2)}, u32[]{:S(2)}) collective-permute-start(bf16[128,576]{1,0:T(8,128)(2,1)S(1)} %constant_dynamic-update-slice_fusion.refs_6_.refs_0_), channel_id=1, source_target_pairs={{0,16},{16,0},{1,17},{17,1},{2,18},{18,2},{3,19},{19,3},{4,20},{20... | collective-permute-start | bytes 442376 | tf_op jit(solution)/shard_map/ppermute | solution.py:370
  57.2 6.3 %collective-permute-start.5 = (bf16[64,576]{1,0:T(8,128)(2,1)S(1)}, bf16[64,576]{1,0:T(8,128)(2,1)S(1)}, u32[]{:S(2)}, u32[]{:S(2)}) collective-permute-start(bf16[64,576]{1,0:T(8,128)(2,1)S(1)} %get-tuple-element.79), channel_id=1, source_target_pairs={{1,0},{2,1},{3,2},{6,7},{5,6},{4,5},{9,8},{10,9},{11,10},{14,15},{... | collective-permute-start | bytes 221192 | tf_op jit(solution)/shard_map/ppermute | solution.py:408
  58.5 6.6 %collective-permute-start.6 = (bf16[64,576]{1,0:T(8,128)(2,1)S(1)}, bf16[64,576]{1,0:T(8,128)(2,1)S(1)}, u32[]{:S(2)}, u32[]{:S(2)}) collective-permute-start(bf16[64,576]{1,0:T(8,128)(2,1)S(1)} %get-tuple-element.80), channel_id=1, source_target_pairs={{0,1},{1,2},{2,3},{7,6},{6,5},{5,4},{8,9},{9,10},{10,11},{15,14},{... | collective-permute-start | bytes 221192 | tf_op jit(solution)/shard_map/ppermute | solution.py:408
  67.0 7.1 %collective-permute-start.18 = (bf16[10,64,128]{2,1,0:T(8,128)(2,1)S(1)}, bf16[10,64,128]{2,1,0:T(8,128)(2,1)S(1)}, u32[]{:S(2)}, u32[]{:S(2)}) collective-permute-start(bf16[10,64,128]{2,1,0:T(8,128)(2,1)S(1)} %get-tuple-element.96), channel_id=1, source_target_pairs={{0,16},{16,0},{1,17},{17,1},{2,18},{18,2},{3,19},{19,3},{4,20},{20... | collective-permute-start | bytes 491528 | tf_op jit(solution)/shard_map/ppermute | solution.py:536
  74.3 13.0 %collective-permute-start.19 = (bf16[10,64,128]{2,1,0:T(8,128)(2,1)S(1)}, bf16[10,64,128]{2,1,0:T(8,128)(2,1)S(1)}, u32[]{:S(2)}, u32[]{:S(2)}) collective-permute-start(bf16[10,64,128]{2,1,0:T(8,128)(2,1)S(1)} %row_sum.1.refs_0_), channel_id=1, source_target_pairs={{0,4},{4,8},{8,12},{12,0},{1,5},{5,9},{9,13},{13,1},{2,6},{6,10},{... | collective-permute-start | bytes 491528 | tf_op jit(solution)/shard_map/ppermute | solution.py:370
  74.4 12.9 %collective-permute-start.20 = (bf16[10,64,128]{2,1,0:T(8,128)(2,1)S(1)}, bf16[10,64,128]{2,1,0:T(8,128)(2,1)S(1)}, u32[]{:S(2)}, u32[]{:S(2)}) collective-permute-start(bf16[10,64,128]{2,1,0:T(8,128)(2,1)S(1)} %row_sum.1.refs_0_), channel_id=1, source_target_pairs={{0,8},{4,12},{8,0},{12,4},{1,9},{5,13},{9,1},{13,5},{2,10},{6,14},... | collective-permute-start | bytes 491528 | tf_op jit(solution)/shard_map/ppermute | solution.py:370
  76.1 11.2 %collective-permute-start.21 = (bf16[10,64,128]{2,1,0:T(8,128)(2,1)S(1)}, bf16[10,64,128]{2,1,0:T(8,128)(2,1)S(1)}, u32[]{:S(2)}, u32[]{:S(2)}) collective-permute-start(bf16[10,64,128]{2,1,0:T(8,128)(2,1)S(1)} %row_sum.1.refs_0_), channel_id=1, source_target_pairs={{0,12},{4,0},{8,4},{12,8},{1,13},{5,1},{9,5},{13,9},{2,14},{6,2},{... | collective-permute-start | bytes 491528 | tf_op jit(solution)/shard_map/ppermute | solution.py:370
  81.5 22.4 %collective-permute-start.22 = (bf16[64,4096]{1,0:T(8,128)(2,1)S(1)}, bf16[64,4096]{1,0:T(8,128)(2,1)S(1)}, u32[]{:S(2)}, u32[]{:S(2)}) collective-permute-start(bf16[64,4096]{1,0:T(8,128)(2,1)S(1)} %get-tuple-element.106), channel_id=1, source_target_pairs={{1,0},{2,3},{5,4},{6,7},{9,8},{10,11},{13,12},{14,15},{17,16},{18,... | collective-permute-start | bytes 1572872 | tf_op jit(solution)/shard_map/ppermute | solution.py:559
  82.8 4.5 %copy-start.1 = (f32[4,9,64,128]{3,2,1,0:T(8,128)S(1)}, f32[4,9,64,128]{3,2,1,0:T(8,128)}, u32[]{:S(2)}) copy-start(f32[4,9,64,128]{3,2,1,0:T(8,128)} %bank.1) | copy-start | bytes 3538948
  90.3 13.2 %collective-permute-start.23 = (f32[64,512]{1,0:T(8,128)S(1)}, f32[64,512]{1,0:T(8,128)S(1)}, u32[]{:S(2)}, u32[]{:S(2)}) collective-permute-start(f32[64,512]{1,0:T(8,128)S(1)} %broadcast_select_fusion.1), channel_id=1, source_target_pairs={{0,16},{1,17},{2,18},{3,19},{16,0},{17,1},{18,2},{19,3},{4,20},{5,... | collective-permute-start | bytes 393224 | tf_op jit(solution)/shard_map/ppermute | solution.py:378
  91.5 12.0 %collective-permute-start.24 = (bf16[64,512]{1,0:T(8,128)(2,1)S(1)}, bf16[64,512]{1,0:T(8,128)(2,1)S(1)}, u32[]{:S(2)}, u32[]{:S(2)}) collective-permute-start(bf16[64,512]{1,0:T(8,128)(2,1)S(1)} %broadcast_select_fusion), channel_id=1, source_target_pairs={{1,16},{2,19},{17,0},{18,3},{5,20},{6,23},{21,4},{22,7},{9,24},{10... | collective-permute-start | bytes 196616 | tf_op jit(solution)/shard_map/ppermute | solution.py:378
  92.8 5.4 %collective-permute-start.25 = (f32[4,128]{1,0:T(4,128)S(1)}, f32[4,128]{1,0:T(4,128)S(1)}, u32[]{:S(2)}, u32[]{:S(2)}) collective-permute-start(f32[4,128]{1,0:T(4,128)S(1)} %get-tuple-element.125.refs_0_), channel_id=1, source_target_pairs={{0,1},{1,2},{2,3},{3,0},{4,5},{5,6},{6,7},{7,4},{8,9},{9,10},{10,1... | collective-permute-start | bytes 6152 | tf_op jit(solution)/shard_map/ppermute | solution.py:370
  95.8 4.5 %collective-permute-start.26 = (f32[4,128]{1,0:T(4,128)S(1)}, f32[4,128]{1,0:T(4,128)S(1)}, u32[]{:S(2)}, u32[]{:S(2)}) collective-permute-start(f32[4,128]{1,0:T(4,128)S(1)} %get-tuple-element.125.refs_0_), channel_id=1, source_target_pairs={{0,2},{1,3},{2,0},{3,1},{4,6},{5,7},{6,4},{7,5},{8,10},{9,11},{10,... | collective-permute-start | bytes 6152 | tf_op jit(solution)/shard_map/ppermute | solution.py:370
  98.2 3.6 %collective-permute-start.27 = (f32[4,128]{1,0:T(4,128)S(1)}, f32[4,128]{1,0:T(4,128)S(1)}, u32[]{:S(2)}, u32[]{:S(2)}) collective-permute-start(f32[4,128]{1,0:T(4,128)S(1)} %get-tuple-element.125.refs_0_), channel_id=1, source_target_pairs={{0,3},{1,0},{2,1},{3,2},{4,7},{5,4},{6,5},{7,6},{8,11},{9,8},{10,9... | collective-permute-start | bytes 6152 | tf_op jit(solution)/shard_map/ppermute | solution.py:370

commit v7 on v6

v7 whole, which is shorter than its diff:
```python
import functools

import jax
import jax.numpy as jnp
from jax import lax
from jax.experimental import pallas as pl
from jax.experimental.pallas import tpu as pltpu
from jax.sharding import PartitionSpec as P

EPS = 1e-08
TAPS = 9
F32 = jnp.float32
BF16 = jnp.bfloat16
VMEM_LIMIT = 16 * 2**20


def params():
    return pltpu.CompilerParams(vmem_limit_bytes=VMEM_LIMIT)


def vspec(n):
    return [pl.BlockSpec(memory_space=pltpu.VMEM)] * n


def sspec(n):
    return [pl.BlockSpec(memory_space=pltpu.SMEM)] * n


def cost(flops, moved):
    return pl.CostEstimate(flops=flops, bytes_accessed=moved, transcendentals=0)


def beside(pieces):
    return pieces[0] if len(pieces) == 1 else jnp.concatenate(pieces, axis=1)


def mixed(bank_ref, weights, tap):
    total = weights[0] * bank_ref[0, tap]
    for k in range(1, bank_ref.shape[0]):
        total = total + weights[k] * bank_ref[k, tap]
    return total


def energy_kernel(*refs):
    given, (style_out, kernel_out, energy_out, small), held, sems = refs[:5], refs[5:9], refs[9:14], refs[14]
    copies = [pltpu.make_async_copy(x, y, sems.at[n]) for n, (x, y) in enumerate(zip(given, held))]
    for copy in copies:
        copy.start()
    for copy in copies:
        copy.wait()
    select, latent, affine_b, affine_w, bank = held
    style = (
        jnp.dot(latent[...], affine_w[...], precision=lax.Precision.HIGHEST, preferred_element_type=F32)
        + affine_b[...]
    )
    style_out[...] = style
    filters, in_ch = bank.shape[0], bank.shape[3]
    weights = [select[0, k].astype(F32) for k in range(filters)]
    total = jnp.zeros(bank.shape[2:], F32)
    for tap in range(TAPS):
        kernel = mixed(bank, weights, tap)
        kernel_out[tap] = kernel
        plain = kernel * style
        total = total + plain * plain
    energy_out[...] = jnp.broadcast_to(jnp.sum(total, axis=1, keepdims=True), energy_out.shape)
    small[...] = jnp.zeros(small.shape, F32)
    last = latent.shape[1] // in_ch
    for n in range(last):
        small[n : n + 1] = latent[:, n * in_ch : (n + 1) * in_ch]
    small[last : last + 1] = style
    lane = lax.broadcasted_iota(jnp.int32, (1, in_ch), 1)
    row = jnp.zeros((1, in_ch), F32)
    for k in range(filters):
        row = jnp.where(lane == k, weights[k], row)
    small[last + 1 : last + 2] = row


def modulated_kernel(kernel, style, *refs):
    energies, (mod_out, scale_out) = refs[:-2], refs[-2:]
    energy = energies[0][...]
    for other in energies[1:]:
        energy = energy + other[...]
    scales = lax.rsqrt(energy + EPS)
    scale_out[...] = scales
    scale = scales[:, 0:1]
    for tap in range(TAPS):
        mod_out[tap] = (kernel[tap] * style[...] * scale).astype(BF16)


def blocks_kernel(rows, size, place, *refs):
    parts, whole, outs, (by_row, by_chan) = refs[:rows], refs[rows], refs[rows + 1 : rows + 1 + size], refs[-2:]
    row_at, chan_at, sign = place[2], place[1], place[3]
    for r in range(rows):
        by_row[lax.rem(row_at - r + rows, rows)] = parts[r][...]
    ch = whole.shape[2] // size
    taps = []
    for tap in range(TAPS):
        value = beside([by_row[r, tap].astype(F32) for r in range(rows)])
        whole[tap] = value.astype(BF16)
        taps.append(value)
    for z in range(size):
        by_chan[z] = beside([value[:, z * ch : (z + 1) * ch] for value in taps]).astype(BF16)
    for d in range(size):
        outs[d][...] = by_chan[lax.rem(chan_at + sign * d + size, size)]


def shifted(x, by):
    width = x.shape[1]
    lane = lax.broadcasted_iota(jnp.int32, x.shape, 1)
    moved = pltpu.roll(x, by % width, 1)
    return jnp.where(lane == (0 if by == 1 else width - 1), 0.0, moved)


def spread(wide, row, x):
    ch, width = x.shape
    wide[ch : 2 * ch, row * width : (row + 1) * width] = x
    x = x.astype(F32)
    wide[0:ch, row * width : (row + 1) * width] = shifted(x, 1).astype(BF16)
    wide[2 * ch : 3 * ch, row * width : (row + 1) * width] = shifted(x, -1).astype(BF16)


def rows_kernel(height, width, feat, feat_before, feat_after, out):
    out[:, 0:width] = feat_before[...]
    out[:, width : (height + 1) * width] = feat[...]
    out[:, (height + 1) * width :] = feat_after[...]


def tap_products(g_ref, wides, totals, height, width):
    for total in totals:
        total[...] = jnp.zeros(total.shape, F32)

    def body(row, _):
        g = g_ref[:, pl.ds(pl.multiple_of(row * width, width), width)]
        for wide, total in zip(wides, totals):
            for kh in range(3):
                x = wide[:, pl.ds(pl.multiple_of((row + kh) * width, width), width)]
                total[kh] += lax.dot_general(g, x, (((1,), (1,)), ((), ())), preferred_element_type=F32)
        return 0

    lax.fori_loop(0, height, body, 0)
    return [jnp.concatenate([total[kh] for kh in range(3)], axis=1).astype(BF16) for total in totals]


def near_grad_kernel(height, width, *refs):
    cotans, feat, outs, (wide, gathered, total) = refs[:3], refs[3], refs[4:7], refs[7:]
    ch = feat.shape[0]
    for at, cotan in enumerate(cotans):
        gathered[at * ch : (at + 1) * ch] = cotan[...]
    for row in range(height + 2):
        spread(wide, row, feat[:, row * width : (row + 1) * width])
    (whole,) = tap_products(gathered, [wide], [total], height, width)
    for at, out in enumerate(outs):
        out[...] = whole[at * ch : (at + 1) * ch]


def far_grad_kernel(count, height, width, *refs):
    first, second, (wide, feat) = refs[:count], refs[count : 2 * count], refs[2 * count : 2 * count + 2]
    (out, middle, end_block), (wide_end, total, end_total) = refs[2 * count + 2 : -3], refs[-3:]
    ch = feat.shape[0]
    for at in range(count):
        middle[at * ch : (at + 1) * ch] = first[at][...] + second[count - 1 - at][...]
    end_block[...] = first[-1][...] + second[-1][...]
    for row in range(height + 2):
        spread(wide_end, row, feat[:, row * width : (row + 1) * width])
    if count == 1:
        whole, end = tap_products(end_block, [wide, wide_end], [total, end_total], height, width)
    else:
        (whole,) = tap_products(middle, [wide], [total], height, width)
        (end,) = tap_products(end_block, [wide_end], [end_total], height, width)
    out[0 : count * ch] = whole
    out[count * ch :] = end


def input_grad_kernel(size, height, width, place, cotan, first, second, middle, far, *refs):
    mods, (main, before, after, gathered, taps_t, total) = refs[:size], refs[size:]
    ch = main.shape[0]
    spot = jnp.where(place[3] > 0, place[1], size - 1 - place[1])
    gathered[0:ch] = cotan[...]
    gathered[ch : 2 * ch] = jnp.where(spot == 0, far[...], first[...])
    gathered[2 * ch : (size - 1) * ch] = middle[...]
    gathered[(size - 1) * ch :] = jnp.where(spot == size - 1, far[...], second[...])
    every = jnp.concatenate([mod[...].astype(F32) for mod in mods], axis=0)
    taps_t[...] = every.T.astype(BF16)
    total[...] = jnp.zeros(total.shape, F32)

    def body(row, _):
        g = gathered[:, pl.ds(pl.multiple_of(row * width, width), width)]
        for kh in range(3):
            y = jnp.dot(taps_t[kh * 3 * ch : (kh + 1) * 3 * ch], g, preferred_element_type=F32)
            total[row + kh] += y
        return 0

    lax.fori_loop(0, height, body, 0)
    for row in range(height + 2):
        value = total[row, ch : 2 * ch]
        value = value + shifted(total[row, 0:ch], -1) + shifted(total[row, 2 * ch : 3 * ch], 1)
        if row == 0:
            before[...] = value
        elif row == height + 1:
            after[...] = value
        else:
            main[:, (row - 1) * width : row * width] = value


def split3(x):
    high = x.astype(BF16).astype(F32)
    mid = (x - high).astype(BF16).astype(F32)
    return high, mid, x - high - mid


def put_columns(out, columns):
    lane = lax.broadcasted_iota(jnp.int32, out.shape[1:], 1)
    last = jnp.zeros(out.shape[1:], F32)
    for n, column in enumerate(columns):
        for at, piece in enumerate(split3(column)):
            last = jnp.where(lane == 3 * n + at, piece, last)
    out[TAPS] = last.astype(BF16)


def get_column(last, n=0):
    last = last.astype(F32)
    return last[:, 3 * n : 3 * n + 1] + last[:, 3 * n + 1 : 3 * n + 2] + last[:, 3 * n + 2 : 3 * n + 3]


def collect_kernel(rows, size, place, scale, whole_mod, own, ahead, behind, others, *refs):
    outs, (by_chan, by_row) = refs[:rows], refs[rows:]
    chan_at, row_at, sign = place[1], place[2], place[3]
    ch = own.shape[0]
    by_chan[chan_at] = own[...].astype(F32)
    by_chan[lax.rem(chan_at + sign + size, size)] = ahead[...].astype(F32)
    by_chan[lax.rem(chan_at - sign + size, size)] = behind[...].astype(F32)
    for d in range(2, size - 1):
        value = others[(d - 2) * ch : (d - 1) * ch].astype(F32)
        by_chan[lax.rem(chan_at + sign * d + size, size)] = value
    by_chan[jnp.where(chan_at == 0, size - 1, 0)] += others[(size - 3) * ch :].astype(F32)
    in_ch = outs[0].shape[2]
    product = jnp.zeros(whole_mod.shape[1:], F32)
    for tap in range(TAPS):
        value = beside([by_chan[z, :, tap * ch : (tap + 1) * ch] for z in range(size)])
        product = product + value * whole_mod[tap].astype(F32)
        for r in range(rows):
            by_row[r, tap] = value[:, r * in_ch : (r + 1) * in_ch].astype(BF16)
    fall = jnp.sum(product, axis=1, keepdims=True) * (scale[:, 0:1] * scale[:, 0:1])
    for r in range(rows):
        outs[r][0:TAPS] = by_row[lax.rem(row_at + r, rows)]
        put_columns(outs[r], [fall])


def row_sum_kernel(scale, small, *refs):
    parts, out = refs[:-1], refs[-1]
    fall = get_column(parts[0][TAPS])
    for part in parts[1:]:
        fall = fall + get_column(part[TAPS])
    for tap in range(TAPS):
        value = parts[0][tap].astype(F32)
        for part in parts[1:]:
            value = value + part[tap].astype(F32)
        out[tap] = value.astype(BF16)
    put_columns(out, [fall, scale[:, 0:1]])
    out_ch, in_ch = out.shape[1:]
    pieces = list(split3(small[...]))
    spare = (out.shape[0] - TAPS - 1) * out_ch - 3 * small.shape[0]
    if spare:
        pieces.append(jnp.zeros((spare, in_ch), F32))
    pieces = jnp.concatenate(pieces, axis=0).astype(BF16)
    for n in range(out.shape[0] - TAPS - 1):
        out[TAPS + 1 + n] = pieces[n * out_ch : (n + 1) * out_ch]


def bank_grad_kernel(samples, small_rows, place, bank, *refs):
    parts, (bank_grad, style_grad, latents, held) = refs[:samples], refs[samples:]
    for s in range(samples):
        held[lax.rem(place[0] - s + samples, samples)] = parts[s][...]
    filters, in_ch = bank.shape[0], bank.shape[3]
    last = latents.shape[1] // in_ch
    sel, styles, scales, falls = [], [], [], []
    for b in range(samples):
        rows = jnp.concatenate([held[b, n].astype(F32) for n in range(TAPS + 1, held.shape[1])], axis=0)
        small = rows[:small_rows] + rows[small_rows : 2 * small_rows] + rows[2 * small_rows : 3 * small_rows]
        latents[b : b + 1] = beside([small[n : n + 1] for n in range(last)])
        styles.append(small[last : last + 1])
        sel.append([small[last + 1 : last + 2, k : k + 1] for k in range(filters)])
        falls.append(get_column(held[b, TAPS]))
        scales.append(get_column(held[b, TAPS], 1))
    sums = [jnp.zeros(bank.shape[2:], F32) for _ in range(samples)]
    for tap in range(TAPS):
        totals = [None] * filters
        for b in range(samples):
            kern = mixed(bank, sel[b], tap)
            plain_grad = held[b, tap].astype(F32) * scales[b] - kern * styles[b] * falls[b]
            sums[b] = sums[b] + plain_grad * kern
            kernel_grad = plain_grad * styles[b]
            for k in range(filters):
                term = sel[b][k] * kernel_grad
                totals[k] = term if totals[k] is None else totals[k] + term
        for k in range(filters):
            bank_grad[k, tap] = totals[k]
    for b in range(samples):
        value = jnp.sum(sums[b], axis=0, keepdims=True)
        style_grad[b : b + 1] = value


def affine_kernel(samples, size, place, latents, *refs):
    parts, (w_grad, b_grad, held) = refs[:size], refs[size:]
    for d in range(size):
        held[lax.rem(place[1] - d + size, size)] = parts[d][...]
    style_grad = held[0]
    for z in range(1, size):
        style_grad = style_grad + held[z]
    w_grad[...] = lax.dot_general(
        latents[...],
        style_grad,
        (((0,), (0,)), ((), ())),
        precision=lax.Precision.HIGHEST,
        preferred_element_type=F32,
    )
    bias = style_grad[0:1]
    for b in range(1, samples):
        bias = bias + style_grad[b : b + 1]
    b_grad[...] = bias


def call(kernel, name, outs, *operands, scalars=0, fetched=0, scratch=(), flops=10**6):
    outs = tuple(jax.ShapeDtypeStruct(*o) for o in outs)
    moved = sum(o.size * o.dtype.itemsize for o in (*outs, *operands))
    return pl.pallas_call(
        kernel,
        out_shape=outs,
        in_specs=sspec(scalars)
        + vspec(len(operands) - scalars - fetched)
        + [pl.BlockSpec(memory_space=pltpu.HBM)] * fetched,
        out_specs=tuple(vspec(len(outs))),
        scratch_shapes=[pltpu.VMEM(*s) if isinstance(s, tuple) else s for s in scratch],
        compiler_params=params(),
        cost_estimate=cost(flops, moved),
        name=name,
    )(*operands)


def exchange(x, axis):
    size = lax.axis_size(axis)
    return [x] + [
        lax.ppermute(x, axis, [(i, (i + s) % size) for i in range(size)]) for s in range(1, size)
    ]


def from_sides(first, last, axis):
    size, at = lax.axis_size(axis), lax.axis_index(axis)
    if size == 2:
        got = lax.ppermute(jnp.where(at == 0, last, first), axis, [(0, 1), (1, 0)])
        nothing = jnp.zeros_like(got)
        return jnp.where(at == 1, got, nothing), jnp.where(at == 0, got, nothing)
    up = [(i, i + 1) for i in range(size - 1)]
    down = [(i + 1, i) for i in range(size - 1)]
    return lax.ppermute(last, axis, up), lax.ppermute(first, axis, down)


def on_device(feature, out_grad, bank, select, latent, affine_w, affine_b):
    rows, samples, size = (lax.axis_size(a) for a in ("rows", "samples", "chan"))
    row_at, sample_at, chan_at = (lax.axis_index(a) for a in ("rows", "samples", "chan"))
    _, ch, height, width = feature.shape
    out_ch, in_ch = bank.shape[2:]
    pixels, all_ch = height * width, ch * size
    sign = 1 - 2 * jnp.remainder(sample_at, 2)
    place = jnp.stack([sample_at, chan_at, row_at, sign]).astype(jnp.int32)
    flops = 2 * TAPS * ch * ch * size * pixels

    def along(x, pairs):
        whole = []
        for b in range(samples):
            for i, j in pairs:
                if b % 2:
                    i, j = size - 1 - i, size - 1 - j
                whole.append((b * size + i, b * size + j))
        return lax.ppermute(x, ("samples", "chan"), whole)

    cotan = out_grad[0].reshape(ch, pixels)
    first, second = [], []

    def step(number, x, y):
        first.append(along(x, [(i, i + 1) for i in range(number - 1, size - 1)]))
        second.append(along(y, [(i + 1, i) for i in range(size - number)]))

    step(1, cotan, cotan)

    feat = feature[0].reshape(ch, pixels)
    feat_before, feat_after = from_sides(feat[:, :width], feat[:, pixels - width :], "rows")
    small_rows = -(-(latent.shape[1] // in_ch + 2) // 8) * 8
    style, kernel, energy, small = call(
        energy_kernel,
        "energy",
        [((1, in_ch), F32), ((TAPS, out_ch, in_ch), F32), ((out_ch, 128), F32), ((small_rows, in_ch), F32)],
        select,
        latent,
        affine_b[None],
        affine_w,
        bank,
        fetched=5,
        scratch=[
            pltpu.SMEM(select.shape, jnp.int32),
            (latent.shape, F32),
            ((1, in_ch), F32),
            (affine_w.shape, F32),
            (bank.shape, F32),
            pltpu.SemaphoreType.DMA((5,)),
        ],
    )
    extended = ((ch, (height + 2) * width), BF16)
    (feat,) = call(
        functools.partial(rows_kernel, height, width), "feat_rows", [extended], feat, feat_before, feat_after
    )
    feat_end = lax.ppermute(feat, "chan", [(0, 1), (size - 1, size - 2)])
    mod_own, scale = call(
        modulated_kernel,
        "modulated",
        [((TAPS, out_ch, in_ch), BF16), ((out_ch, 128), F32)],
        kernel,
        style,
        *exchange(energy, "rows"),
    )
    message = ((ch, TAPS * ch), BF16)
    whole_mod, *mods = call(
        functools.partial(blocks_kernel, rows, size),
        "mod_blocks",
        [((TAPS, out_ch, all_ch), BF16)] + [message] * size,
        place,
        *exchange(mod_own, "rows"),
        scalars=1,
        scratch=[((rows, TAPS, out_ch, in_ch), BF16), ((size, *message[0]), BF16)],
    )
    first[0], second[0], energy, mod_own = lax.optimization_barrier((first[0], second[0], energy, mod_own))

    step(2, first[0], second[0])
    own_grad, grad_behind, grad_ahead, wide = call(
        functools.partial(near_grad_kernel, height, width),
        "near_grad",
        [message] * 3 + [((3 * ch, (height + 2) * width), BF16)],
        cotan,
        first[0],
        second[0],
        feat,
        scratch=[((3 * ch, pixels), BF16), ((3, 3 * ch, 3 * ch), F32)],
        flops=flops * 3 // size,
    )
    forth = [(i, i + 1) for i in range(size - 1)]
    back = [(i + 1, i) for i in range(size - 1)]
    from_ahead, from_behind = along(grad_behind, back), along(grad_ahead, forth)
    first[1], second[1], feat_end, wide, mods, whole_mod, from_ahead, from_behind = lax.optimization_barrier(
        (first[1], second[1], feat_end, wide, mods, whole_mod, from_ahead, from_behind)
    )

    count = size - 3
    grad_others, middle, end_block = call(
        functools.partial(far_grad_kernel, count, height, width),
        "far_grad",
        [(((count + 1) * ch, TAPS * ch), BF16), ((count * ch, pixels), BF16), ((ch, pixels), BF16)],
        *first[1:],
        *second[1:],
        wide,
        feat_end,
        scratch=[
            ((3 * ch, (height + 2) * width), BF16),
            ((3, count * ch, 3 * ch), F32),
            ((3, ch, 3 * ch), F32),
        ],
        flops=flops * 2 // size,
    )
    from_others = along(grad_others, [(i, (i + 2) % size) for i in range(size)])
    far = lax.ppermute(end_block, "chan", [(1, 0), (size - 2, size - 1)])
    parts = call(
        functools.partial(collect_kernel, rows, size),
        "collect",
        [((TAPS + 1, out_ch, in_ch), BF16)] * rows,
        place,
        scale,
        whole_mod,
        own_grad,
        from_ahead,
        from_behind,
        from_others,
        scalars=1,
        scratch=[((size, *message[0]), F32), ((rows, TAPS, out_ch, in_ch), BF16)],
    )
    parts, mods = lax.optimization_barrier((parts, mods))
    mods = [mods[0]] + [along(mods[d], [(i, (i + d) % size) for i in range(size)]) for d in range(1, size)]
    parts = [parts[0]] + [
        lax.ppermute(parts[r], "rows", [(i, (i + r) % rows) for i in range(rows)])
        for r in range(1, rows)
    ]
    slots = TAPS + 1 - (-3 * small_rows // out_ch)
    (own,) = call(row_sum_kernel, "row_sum", [((slots, out_ch, in_ch), BF16)], scale, small, *parts)
    every = exchange(own, "samples")

    own, mods, far = lax.optimization_barrier((own, mods, far))
    main, before, after = call(
        functools.partial(input_grad_kernel, size, height, width),
        "input_grad",
        [((ch, pixels), F32), ((ch, width), F32), ((ch, width), F32)],
        place,
        cotan,
        first[0],
        second[0],
        middle,
        far,
        *mods,
        scalars=1,
        scratch=[
            ((all_ch, pixels), BF16),
            ((TAPS * ch, all_ch), BF16),
            ((height + 2, 3 * ch, width), F32),
        ],
        flops=flops,
    )
    every, main, before, after = lax.optimization_barrier((every, main, before, after))
    from_above, from_below = from_sides(before, after, "rows")
    bank_grad, style_part, latents = call(
        functools.partial(bank_grad_kernel, samples, small_rows),
        "bank_grad",
        [(bank.shape, F32), ((samples, in_ch), F32), ((samples, latent.shape[1]), F32)],
        place,
        bank,
        *every,
        scalars=1,
        scratch=[((samples, slots, out_ch, in_ch), BF16)],
    )
    style_parts = exchange(style_part, "chan")
    edge = jnp.concatenate(
        [from_above[:, None], jnp.zeros((ch, height - 2, width), F32), from_below[:, None]], axis=1
    )
    feature_grad = (main.reshape(ch, height, width) + edge).astype(BF16)[None]
    affine_w_grad, affine_b_grad = call(
        functools.partial(affine_kernel, samples, size),
        "affine",
        [(affine_w.shape, F32), ((1, in_ch), F32)],
        place,
        latents,
        *style_parts,
        scalars=1,
        scratch=[((size, samples, in_ch), F32)],
    )
    return (feature_grad, bank_grad, affine_w_grad, affine_b_grad[0])


def solution(mesh):
    return jax.shard_map(
        on_device,
        mesh=mesh,
        in_specs=(
            P("samples", "chan", "rows", None),
            P("samples", "chan", "rows", None),
            P(None, None, "chan", "rows"),
            P("samples", None),
            P("samples", None),
            P(None, "rows"),
            P("rows"),
        ),
        out_specs=(
            P("samples", "chan", "rows", None),
            P(None, None, "chan", "rows"),
            P(None, "rows"),
            P("rows"),
        ),
        check_vma=False,
    )
```

time: 106 us -> 89.9 us (0.85)
  waiting for transfers between devices: 26.1 us -> 12.9 us
  local copies, waits for them, and re-layouts: 5.73 us -> 4.12 us
  Pallas kernels: 24.3 us -> 22.9 us
    ppermute x12 -> x8, waiting for transfers between devices: 15.8 us -> 3.87 us  [exchange(): lax.ppermute(x, axis, [(i, (i + s) % size) for i in range(size)])]
    ppermute x1, waiting for transfers between devices: 5.89 us -> 0.01 us  [on_device(): lax.ppermute(parts[r], 'rows', [(i, (i + r) % rows) for i in range(rows)])]
    ppermute x10, starting transfers between devices: 23 us -> 26.3 us  [along(): return lax.ppermute(x, ('samples', 'chan'), whole)]
    ppermute x4 -> x3, waiting for transfers between devices: 0.23 us -> 2.78 us  [the longest x2 2.78 us: from_sides(): got = lax.ppermute(jnp.where(at == 0, last, first), axis, [(0, 1), (1, 0)])]
    ppermute x10, waiting for transfers between devices: 4.19 us -> 6.23 us  [along(): return lax.ppermute(x, ('samples', 'chan'), whole)]
    unnamed x23 -> x25, local copies, waits for them, and re-layouts: 5.37 us -> 3.76 us
    pallas_call x12 -> x11, Pallas kernels: 24.3 us -> 22.9 us  [call(): pl.pallas_call(kernel, out_shape=outs, in_specs=sspec(scalars) + vspec(le...]
    ppermute x12 -> x8, starting transfers between devices: 13.6 us -> 12.2 us  [exchange(): lax.ppermute(x, axis, [(i, (i + s) % size) for i in range(size)])]
  transfers between devices with their start and end apart: 28 -> 23, of which waited for: 14 -> 7; matrix products, arithmetic and copies ran while one was open for 1% -> 1% of each run, Pallas kernels for 18% -> 21%
where the time goes in v7:
time: 89.9 us; the launch traced here: 89.5 us
  starting transfers between devices  47.3 us (53%)
  Pallas kernels  22.9 us (25%)
  waiting for transfers between devices  12.9 us (14%)
  local copies, waits for them, and re-layouts  4.12 us (5%)
  other arithmetic  1.29 us (1%)
  between operations  1.01 us (1%)
    ppermute x10, starting transfers between devices, along(): return lax.ppermute(x, ('samples', 'chan'), whole)  26.3 us
    pallas_call x11, Pallas kernels, call(): pl.pallas_call(kernel, out_shape=outs, in_specs=sspec(scalars) + vspec(le...  22.9 us
    ppermute x8, starting transfers between devices, exchange(): lax.ppermute(x, axis, [(i, (i + s) % size) for i in range(size)])  12.2 us
    ppermute x10, waiting for transfers between devices, along(): return lax.ppermute(x, ('samples', 'chan'), whole)  6.23 us
    ppermute x1, starting transfers between devices, on_device(): feat_end = lax.ppermute(feat, 'chan', [(0, 1), (size - 1, size - 2)])  4.59 us
    ppermute x8, waiting for transfers between devices, exchange(): lax.ppermute(x, axis, [(i, (i + s) % size) for i in range(size)])  3.87 us
    unnamed x25, local copies, waits for them, and re-layouts  3.76 us
    ppermute x2, waiting for transfers between devices, from_sides(): got = lax.ppermute(jnp.where(at == 0, last, first), axis, [(0, 1), (1, 0)])  2.78 us
  transfers between devices with their start and end apart: 23, of which 7 were waited for; matrix products, arithmetic and copies ran while one was open for 1% of the time, Pallas kernels for 21%

profile of v7, /device:TPU:0, one launch (start us, length us, event | category | flops | bytes accessed | tf_op | source)
XLA Modules:
  0.0 89.5 jit_solution(8674901431753686663)
XLA Ops:
  0.6 1.3 %copy.13 = bf16[8,8,8,512]{3,1,2,0:T(8,128)(2,1)S(1)} copy(bf16[8,8,8,512]{3,2,1,0:T(8,128)(2,1)} %bitcast.32) | data formatting | bytes 1048576
  1.9 0.0 copy-start.1
  1.9 5.7 %collective-permute-start.1 = (bf16[64,4096]{1,0:T(8,128)(2,1)S(1)}, bf16[64,4096]{1,0:T(8,128)(2,1)}, u32[]{:S(2)}, u32[]{:S(2)}) collective-permute-start(bf16[64,4096]{1,0:T(8,128)(2,1)S(1)} %bitcast.26), channel_id=1, source_target_pairs={{0,1},{1,2},{2,3},{7,6},{6,5},{5,4},{8,9},{9,10},{10,11},{15,14},{... | collective-permute-start | bytes 1572872 | tf_op jit(solution)/shard_map/ppermute | solution.py:375
  7.7 1.3 %collective-permute-start.2 = (bf16[64,4096]{1,0:T(8,128)(2,1)S(1)}, bf16[64,4096]{1,0:T(8,128)(2,1)}, u32[]{:S(2)}, u32[]{:S(2)}) collective-permute-start(bf16[64,4096]{1,0:T(8,128)(2,1)S(1)} %bitcast.27), channel_id=1, source_target_pairs={{1,0},{2,1},{3,2},{6,7},{5,6},{4,5},{9,8},{10,9},{11,10},{14,15},{... | collective-permute-start | bytes 1572872 | tf_op jit(solution)/shard_map/ppermute | solution.py:375
  9.0 0.0 copy-start
  9.0 0.0 copy-start.4
  9.0 0.0 copy-start.7
  9.0 0.0 copy-start.8
  9.0 0.0 copy-start.9
  9.0 0.2 copy.14
  9.2 1.6 %collective-permute-start.5 = (bf16[64,512]{1,0:T(8,128)(2,1)S(1)}, bf16[64,512]{1,0:T(8,128)(2,1)S(1)}, u32[]{:S(2)}, u32[]{:S(2)}) collective-permute-start(bf16[64,512]{1,0:T(8,128)(2,1)S(1)} %slice_select_fusion), channel_id=1, source_target_pairs={{0,16},{16,0},{1,17},{17,1},{2,18},{18,2},{3,19},{19,3},{4,20},{20... | collective-permute-start | bytes 196616 | tf_op jit(solution)/shard_map/ppermute | solution.py:350
  10.8 2.8 %collective-permute-done.5 = bf16[64,512]{1,0:T(8,128)(2,1)S(1)} collective-permute-done((bf16[64,512]{1,0:T(8,128)(2,1)S(1)}, bf16[64,512]{1,0:T(8,128)(2,1)S(1)}, u32[]{:S(2)}, u32[]{:S(2)}) %collective-permute-start.5) | collective-permute-done | bytes 65568 | tf_op jit(solution)/shard_map/ppermute | solution.py:350
  13.6 4.6 %collective-permute-start.6 = (bf16[64,5120]{1,0:T(8,128)(2,1)S(1)}, bf16[64,5120]{1,0:T(8,128)(2,1)S(1)}, u32[]{:S(2)}, u32[]{:S(2)}) collective-permute-start(bf16[64,5120]{1,0:T(8,128)(2,1)S(1)} %feat_rows.1.refs_3_), channel_id=1, source_target_pairs={{0,1},{3,2},{4,5},{7,6},{8,9},{11,10},{12,13},{15,14},{16,17},{19,... | collective-permute-start | bytes 1966088 | tf_op jit(solution)/shard_map/ppermute | solution.py:412
  18.3 1.0 %energy.1 = (f32[1,128]{1,0:T(1,128)S(1)}, f32[9,64,128]{2,1,0:T(8,128)S(1)}, f32[64,128]{1,0:T(8,128)S(1)}, f32[8,128]{1,0:T(8,128)S(1)}) custom-call(s32[1,4]{1,0:T(1,128)S(1)} %copy-done.8, f32[1,512]{1,0:T(1,128)S(1)} %copy-done.7, f32[1,128]{1,0:T(1,128)S(1)} %bitcast.30, f32[512,128]{1,0:T(8,128)S(1)} %copy-done.4, f32[4,9,64,128]{3,2,1,0:T(8,128)S(1)} %copy-done), custom_call_target="tpu_custom_call" | custom-call | flops 1000000 | bytes 1776656 | tf_op jit(solution)/shard_map/energy/pallas_call | solution.py:326
  19.2 1.6 %collective-permute-start = (f32[64,128]{1,0:T(8,128)S(1)}, f32[64,128]{1,0:T(8,128)S(1)}, u32[]{:S(2)}, u32[]{:S(2)}) collective-permute-start(f32[64,128]{1,0:T(8,128)S(1)} %get-tuple-element.65.refs_0_), channel_id=1, source_target_pairs={{0,16},{16,0},{1,17},{17,1},{2,18},{18,2},{3,19},{19,3},{4,20},{20... | collective-permute-start | bytes 98312 | tf_op jit(solution)/shard_map/ppermute | solution.py:343
  20.8 2.4 %collective-permute-done.refs_1_ = f32[64,128]{1,0:T(8,128)S(1)} collective-permute-done((f32[64,128]{1,0:T(8,128)S(1)}, f32[64,128]{1,0:T(8,128)S(1)}, u32[]{:S(2)}, u32[]{:S(2)}) %collective-permute-start) | collective-permute-done | bytes 32800 | tf_op jit(solution)/shard_map/ppermute | solution.py:343
  23.2 0.8 modulated.1
  24.0 0.6 copy-done.5
  24.6 0.0 collective-permute-done.1.refs_1_.first
  24.6 0.0 collective-permute-done.2.refs_2_.second
  24.6 0.7 collective-permute-start.3
  25.3 1.3 %collective-permute-start.4 = (bf16[64,4096]{1,0:T(8,128)(2,1)}, bf16[64,4096]{1,0:T(8,128)(2,1)S(1)}, u32[]{:S(2)}, u32[]{:S(2)}) collective-permute-start(bf16[64,4096]{1,0:T(8,128)(2,1)} %collective-permute-done.2.refs_2_.second), channel_id=1, source_target_pairs={{1,0},{2,1},{6,7},{5,6},{9,8},{10,9},{14,15},{13,14},{17,16},{18,1... | collective-permute-start | bytes 1572872 | tf_op jit(solution)/shard_map/ppermute | solution.py:375
  26.6 1.6 %collective-permute-start.7 = (bf16[9,64,128]{2,1,0:T(8,128)(2,1)}, bf16[9,64,128]{2,1,0:T(8,128)(2,1)}, u32[]{:S(2)}, u32[]{:S(2)}) collective-permute-start(bf16[9,64,128]{2,1,0:T(8,128)(2,1)} %get-tuple-element.68.refs_0_), channel_id=1, source_target_pairs={{0,16},{16,0},{1,17},{17,1},{2,18},{18,2},{3,19},{19,3},{4,20},{20... | collective-permute-start | bytes 442376 | tf_op jit(solution)/shard_map/ppermute | solution.py:343
  28.2 1.0 %copy-done.2 = bf16[8,8,8,512]{3,1,2,0:T(8,128)(2,1)S(1)} copy-done((bf16[8,8,8,512]{3,1,2,0:T(8,128)(2,1)S(1)}, bf16[8,8,8,512]{3,1,2,0:T(8,128)(2,1)}, u32[]{:S(2)}) %copy-start.2) | copy-done | bytes 524312
  29.2 4.5 %near_grad.1 = (bf16[64,576]{1,0:T(8,128)(2,1)S(1)}, bf16[64,576]{1,0:T(8,128)(2,1)S(1)}, bf16[64,576]{1,0:T(8,128)(2,1)S(1)}, bf16[192,5120]{1,0:T(8,128)(2,1)S(1)}) custom-call(bf16[64,4096]{1,0:T(8,128)(2,1)S(1)} %bitcast.28, bf16[64,4096]{1,0:T(8,128)(2,1)} %collective-permute-done.1.refs_1_.first, ...), custom_call_target="tpu_custom_call" | custom-call | flops 905969664 | bytes 4415488 | tf_op jit(solution)/shard_map/near_grad/pallas_call | solution.py:326
  33.7 1.3 %collective-permute-start.8 = (bf16[64,576]{1,0:T(8,128)(2,1)S(1)}, bf16[64,576]{1,0:T(8,128)(2,1)S(1)}, u32[]{:S(2)}, u32[]{:S(2)}) collective-permute-start(bf16[64,576]{1,0:T(8,128)(2,1)S(1)} %get-tuple-element.77), channel_id=1, source_target_pairs={{1,0},{2,1},{3,2},{6,7},{5,6},{4,5},{9,8},{10,9},{11,10},{14,15},{... | collective-permute-start | bytes 221192 | tf_op jit(solution)/shard_map/ppermute | solution.py:375
  35.0 0.0 collective-permute-done.7.refs_1_
  35.0 5.2 %collective-permute-start.9 = (bf16[64,576]{1,0:T(8,128)(2,1)S(1)}, bf16[64,576]{1,0:T(8,128)(2,1)S(1)}, u32[]{:S(2)}, u32[]{:S(2)}) collective-permute-start(bf16[64,576]{1,0:T(8,128)(2,1)S(1)} %get-tuple-element.78), channel_id=1, source_target_pairs={{0,1},{1,2},{2,3},{7,6},{6,5},{5,4},{8,9},{9,10},{10,11},{15,14},{... | collective-permute-start | bytes 221192 | tf_op jit(solution)/shard_map/ppermute | solution.py:375
  40.2 0.1 pad_add_fusion.place
  40.3 1.2 %mod_blocks.1 = (bf16[9,64,256]{2,1,0:T(8,128)(2,1)S(1)}, bf16[64,576]{1,0:T(8,128)(2,1)S(1)}, bf16[64,576]{1,0:T(8,128)(2,1)S(1)}, bf16[64,576]{1,0:T(8,128)(2,1)S(1)}, bf16[64,576]{1,0:T(8,128)(2,1)S(1)}) custom-call(s32[4]{0:T(128)S(1)} %pad_add_fusion.place, bf16[9,64,128]{2,1,0:T(8,128)(2,1)} %get-tuple-element.68.refs_0_, ...), custom_call_target="tpu_custom_call" | custom-call | flops 1000000 | bytes 884752 | tf_op jit(solution)/shard_map/mod_blocks/pallas_call | solution.py:326
  41.5 0.0 collective-permute-done.8.ahead
  41.5 0.7 collective-permute-done.9.behind
  42.3 0.0 copy-start.6
  42.3 4.6 %far_grad.1 = (bf16[128,576]{1,0:T(8,128)(2,1)S(1)}, bf16[64,4096]{1,0:T(8,128)(2,1)S(1)}, bf16[64,4096]{1,0:T(8,128)(2,1)S(1)}) custom-call(bf16[64,4096]{1,0:T(8,128)(2,1)S(1)} %collective-permute-done.3.refs_0_, bf16[64,4096]{1,0:T(8,128)(2,1)S(1)} %collective-permute-done.4.refs_1_, bf16[192,5120]{1,0:T(8,128)(2,1)S(1)} %get-tuple-element.85.refs_2_, ...), custom_call_target="tpu_custom_call" | custom-call | flops 603979776 | bytes 4866048 | tf_op jit(solution)/shard_map/far_grad/pallas_call | solution.py:326
  46.9 0.0 copy-start.3
  46.9 1.4 %collective-permute-start.18 = (bf16[64,4096]{1,0:T(8,128)(2,1)S(1)}, bf16[64,4096]{1,0:T(8,128)(2,1)S(1)}, u32[]{:S(2)}, u32[]{:S(2)}) collective-permute-start(bf16[64,4096]{1,0:T(8,128)(2,1)S(1)} %get-tuple-element.101), channel_id=1, source_target_pairs={{1,0},{2,3},{5,4},{6,7},{9,8},{10,11},{13,12},{14,15},{17,16},{18,... | collective-permute-start | bytes 1572872 | tf_op jit(solution)/shard_map/ppermute | solution.py:469
  48.3 6.0 %collective-permute-start.10 = (bf16[128,576]{1,0:T(8,128)(2,1)S(1)}, bf16[128,576]{1,0:T(8,128)(2,1)S(1)}, u32[]{:S(2)}, u32[]{:S(2)}) collective-permute-start(bf16[128,576]{1,0:T(8,128)(2,1)S(1)} %get-tuple-element.87), channel_id=1, source_target_pairs={{0,2},{1,3},{2,0},{3,1},{7,5},{6,4},{5,7},{4,6},{8,10},{9,11},{10,... | collective-permute-start | bytes 442376 | tf_op jit(solution)/shard_map/ppermute | solution.py:375
  54.3 4.3 %collective-permute-done.10.others = bf16[128,576]{1,0:T(8,128)(2,1)S(1)} collective-permute-done((bf16[128,576]{1,0:T(8,128)(2,1)S(1)}, bf16[128,576]{1,0:T(8,128)(2,1)S(1)}, u32[]{:S(2)}, u32[]{:S(2)}) %collective-permute-start.10) | collective-permute-done | bytes 147488 | tf_op jit(solution)/shard_map/ppermute | solution.py:375
  58.6 1.1 %collect.1 = (bf16[10,64,128]{2,1,0:T(8,128)(2,1)S(1)}, bf16[10,64,128]{2,1,0:T(8,128)(2,1)S(1)}) custom-call(s32[4]{0:T(128)S(1)} %pad_add_fusion.place, f32[64,128]{1,0:T(8,128)S(1)} %copy-done.6, bf16[9,64,256]{2,1,0:T(8,128)(2,1)S(1)} %get-tuple-element.79.whole_mod, bf16[64,576]{1,0:T(8,128)(2,1)S(1)} %get-tuple-element.80.own, ...), custom_call_target="tpu_custom_call" | custom-call | flops 1000000 | bytes 1024016 | tf_op jit(solution)/shard_map/collect/pallas_call | solution.py:326
  59.6 0.6 collective-permute-start.11
  60.2 1.9 %collective-permute-start.16 = (bf16[64,576]{1,0:T(8,128)(2,1)S(1)}, bf16[64,576]{1,0:T(8,128)(2,1)S(1)}, u32[]{:S(2)}, u32[]{:S(2)}) collective-permute-start(bf16[64,576]{1,0:T(8,128)(2,1)S(1)} %get-tuple-element.99), channel_id=1, source_target_pairs={{0,2},{1,3},{2,0},{3,1},{7,5},{6,4},{5,7},{4,6},{8,10},{9,11},{10,... | collective-permute-start | bytes 221192 | tf_op jit(solution)/shard_map/ppermute | solution.py:375
  62.2 2.9 %collective-permute-start.17 = (bf16[64,576]{1,0:T(8,128)(2,1)S(1)}, bf16[64,576]{1,0:T(8,128)(2,1)S(1)}, u32[]{:S(2)}, u32[]{:S(2)}) collective-permute-start(bf16[64,576]{1,0:T(8,128)(2,1)S(1)} %get-tuple-element.100), channel_id=1, source_target_pairs={{0,3},{1,0},{2,1},{3,2},{7,4},{6,7},{5,6},{4,5},{8,11},{9,8},{10,9... | collective-permute-start | bytes 221192 | tf_op jit(solution)/shard_map/ppermute | solution.py:375
  65.1 0.2 row_sum.1.refs_0_
  65.3 0.1 collective-permute-start.12
  65.4 1.2 %collective-permute-done.15.refs_1_ = bf16[64,576]{1,0:T(8,128)(2,1)S(1)} collective-permute-done((bf16[64,576]{1,0:T(8,128)(2,1)S(1)}, bf16[64,576]{1,0:T(8,128)(2,1)S(1)}, u32[]{:S(2)}, u32[]{:S(2)}) %collective-permute-start.15) | collective-permute-done | bytes 73760 | tf_op jit(solution)/shard_map/ppermute | solution.py:375
  66.6 1.5 %collective-permute-start.13 = (bf16[11,64,128]{2,1,0:T(8,128)(2,1)S(1)}, bf16[11,64,128]{2,1,0:T(8,128)(2,1)S(1)}, u32[]{:S(2)}, u32[]{:S(2)}) collective-permute-start(bf16[11,64,128]{2,1,0:T(8,128)(2,1)S(1)} %row_sum.1.refs_0_), channel_id=1, source_target_pairs={{0,8},{4,12},{8,0},{12,4},{1,9},{5,13},{9,1},{13,5},{2,10},{6,14},... | collective-permute-start | bytes 540680 | tf_op jit(solution)/shard_map/ppermute | solution.py:343
  68.1 3.7 %collective-permute-start.14 = (bf16[11,64,128]{2,1,0:T(8,128)(2,1)S(1)}, bf16[11,64,128]{2,1,0:T(8,128)(2,1)S(1)}, u32[]{:S(2)}, u32[]{:S(2)}) collective-permute-start(bf16[11,64,128]{2,1,0:T(8,128)(2,1)S(1)} %row_sum.1.refs_0_), channel_id=1, source_target_pairs={{0,12},{4,0},{8,4},{12,8},{1,13},{5,1},{9,5},{13,9},{2,14},{6,2},{... | collective-permute-start | bytes 540680 | tf_op jit(solution)/shard_map/ppermute | solution.py:343
  71.8 5.1 %input_grad.1 = (f32[64,4096]{1,0:T(8,128)S(1)}, f32[64,512]{1,0:T(8,128)S(1)}, f32[64,512]{1,0:T(8,128)S(1)}) custom-call(s32[4]{0:T(128)S(1)} %pad_add_fusion.place, bf16[64,4096]{1,0:T(8,128)(2,1)S(1)} %bitcast.29, bf16[64,4096]{1,0:T(8,128)(2,1)} %collective-permute-done.1.refs_1_.first, bf16[64,4096]{1,0:T(8,128)(2,1)} %collective-permute-done.2.refs_2_.second, ...), custom_call_target="tpu_custom_call" | custom-call | flops 1207959552 | bytes 4227088 | tf_op jit(solution)/shard_map/input_grad/pallas_call | solution.py:326
  77.0 0.0 collective-permute-done.13.refs_2_
  77.0 0.0 collective-permute-done.14.refs_3_
  77.0 0.6 collective-permute-start.19
  77.6 2.8 %bank_grad.1 = (f32[4,9,64,128]{3,2,1,0:T(8,128)}, f32[4,128]{1,0:T(4,128)S(1)}, f32[4,512]{1,0:T(4,128)S(1)}) custom-call(s32[4]{0:T(128)S(1)} %pad_add_fusion.place, f32[4,9,64,128]{3,2,1,0:T(8,128)S(1)} %copy-done, bf16[11,64,128]{2,1,0:T(8,128)(2,1)S(1)} %row_sum.1.refs_0_, bf16[11,64,128]{2,1,0:T(8,128)(2,1)S(1)} %collective-permute-done.12.refs_1_, ...), custom_call_target="tpu_custom_call" | custom-call | flops 1000000 | bytes 3090448 | tf_op jit(solution)/shard_map/bank_grad/pallas_call | solution.py:326
  80.4 0.0 collective-permute-start.20
  80.4 1.1 %collective-permute-start.21 = (f32[4,128]{1,0:T(4,128)S(1)}, f32[4,128]{1,0:T(4,128)S(1)}, u32[]{:S(2)}, u32[]{:S(2)}) collective-permute-start(f32[4,128]{1,0:T(4,128)S(1)} %get-tuple-element.119.refs_0_), channel_id=1, source_target_pairs={{0,2},{1,3},{2,0},{3,1},{4,6},{5,7},{6,4},{7,5},{8,10},{9,11},{10,... | collective-permute-start | bytes 6152 | tf_op jit(solution)/shard_map/ppermute | solution.py:343
  81.5 2.8 %collective-permute-start.22 = (f32[4,128]{1,0:T(4,128)S(1)}, f32[4,128]{1,0:T(4,128)S(1)}, u32[]{:S(2)}, u32[]{:S(2)}) collective-permute-start(f32[4,128]{1,0:T(4,128)S(1)} %get-tuple-element.119.refs_0_), channel_id=1, source_target_pairs={{0,3},{1,0},{2,1},{3,2},{4,7},{5,4},{6,5},{7,6},{8,11},{9,8},{10,9... | collective-permute-start | bytes 6152 | tf_op jit(solution)/shard_map/ppermute | solution.py:343
  84.2 0.1 pad.1.clone
  84.3 0.6 copy.15
  84.9 0.9 collective-permute-done.20.refs_1_
  85.8 0.6 collective-permute-done.22.refs_3_
  86.4 1.7 %affine.1 = (f32[512,128]{1,0:T(8,128)}, f32[1,128]{1,0:T(1,128)}) custom-call(s32[4]{0:T(128)S(1)} %pad_add_fusion.place, f32[4,512]{1,0:T(4,128)S(1)} %get-tuple-element.118.latents, f32[4,128]{1,0:T(4,128)S(1)} %get-tuple-element.119.refs_0_, f32[4,128]{1,0:T(4,128)S(1)} %collective-permute-done.20.refs_1_, f32[4,128]{1,0:T(4,128)S(1)} %collective-permute-done.21.refs_2_, ...), custom_call_target="tpu_custom_call" | custom-call | flops 1000000 | bytes 279056 | tf_op jit(solution)/shard_map/affine/pallas_call | solution.py:326
  88.0 0.0 collective-permute-done.19
  88.1 0.1 copy.12
  88.2 0.1 copy.11
  88.4 1.1 %fusion = bf16[1,64,8,512]{3,2,1,0:T(8,128)(2,1)} fusion(f32[1,64,1,512]{3,2,1,0:T(1,128)S(1)} %copy.12, f32[1,64,1,512]{3,2,1,0:T(1,128)S(1)} %copy.11, f32[8]{0:T(128)S(1)} %pad.1.clone, f32[1,64,8,512]{3,2,1,0:T(8,128)S(1)} %bitcast.31), kind=kLoop, calls=%fused_computation.1 | loop fusion | flops 1048576 | bytes 1835040 | tf_op jit(solution)/shard_map/convert_element_type | solution.py:530
  (28 shorter events, 0.2 us)
Async XLA Ops:
  0.6 8.3 %copy-start.10 = (bf16[1,64,8,512]{3,2,1,0:T(8,128)(2,1)S(1)}, bf16[1,64,8,512]{3,2,1,0:T(8,128)(2,1)}, u32[]{:S(2)}) copy-start(bf16[1,64,8,512]{3,2,1,0:T(8,128)(2,1)} %param.7) | copy-start | bytes 1572868
  1.9 11.7 %copy-start.1 = (bf16[8,8,8,512]{3,1,2,0:T(8,128)(2,1)}, bf16[8,8,8,512]{3,1,2,0:T(8,128)(2,1)S(1)}, u32[]{:S(2)}) copy-start(bf16[8,8,8,512]{3,1,2,0:T(8,128)(2,1)S(1)} %copy.13) | copy-start | bytes 1572868
  1.9 22.7 %collective-permute-start.1 = (bf16[64,4096]{1,0:T(8,128)(2,1)S(1)}, bf16[64,4096]{1,0:T(8,128)(2,1)}, u32[]{:S(2)}, u32[]{:S(2)}) collective-permute-start(bf16[64,4096]{1,0:T(8,128)(2,1)S(1)} %bitcast.26), channel_id=1, source_target_pairs={{0,1},{1,2},{2,3},{7,6},{6,5},{5,4},{8,9},{9,10},{10,11},{15,14},{... | collective-permute-start | bytes 1572872 | tf_op jit(solution)/shard_map/ppermute | solution.py:375
  7.7 16.9 %collective-permute-start.2 = (bf16[64,4096]{1,0:T(8,128)(2,1)S(1)}, bf16[64,4096]{1,0:T(8,128)(2,1)}, u32[]{:S(2)}, u32[]{:S(2)}) collective-permute-start(bf16[64,4096]{1,0:T(8,128)(2,1)S(1)} %bitcast.27), channel_id=1, source_target_pairs={{1,0},{2,1},{3,2},{6,7},{5,6},{4,5},{9,8},{10,9},{11,10},{14,15},{... | collective-permute-start | bytes 1572872 | tf_op jit(solution)/shard_map/ppermute | solution.py:375
  9.0 9.3 %copy-start = (f32[4,9,64,128]{3,2,1,0:T(8,128)S(1)}, f32[4,9,64,128]{3,2,1,0:T(8,128)}, u32[]{:S(2)}) copy-start(f32[4,9,64,128]{3,2,1,0:T(8,128)} %bank.1) | copy-start | bytes 3538948
  9.0 9.3 %copy-start.4 = (f32[512,128]{1,0:T(8,128)S(1)}, f32[512,128]{1,0:T(8,128)}, u32[]{:S(2)}) copy-start(f32[512,128]{1,0:T(8,128)} %refs_3_.1) | copy-start | bytes 786436
  9.0 9.3 %copy-start.7 = (f32[1,512]{1,0:T(1,128)S(1)}, f32[1,512]{1,0:T(1,128)}, u32[]{:S(2)}) copy-start(f32[1,512]{1,0:T(1,128)} %refs_1_.1) | copy-start | bytes 6148
  9.0 9.3 %copy-start.8 = (s32[1,4]{1,0:T(1,128)S(1)}, s32[1,4]{1,0:T(1,128)}, u32[]{:S(2)}) copy-start(s32[1,4]{1,0:T(1,128)} %refs_0_.1) | copy-start | bytes 52
  9.0 9.3 %copy-start.9 = (f32[128]{0:T(128)S(1)}, f32[128]{0:T(128)}, u32[]{:S(2)}) copy-start(f32[128]{0:T(128)} %param.13) | copy-start | bytes 1540
  9.2 4.3 %collective-permute-start.5 = (bf16[64,512]{1,0:T(8,128)(2,1)S(1)}, bf16[64,512]{1,0:T(8,128)(2,1)S(1)}, u32[]{:S(2)}, u32[]{:S(2)}) collective-permute-start(bf16[64,512]{1,0:T(8,128)(2,1)S(1)} %slice_select_fusion), channel_id=1, source_target_pairs={{0,16},{16,0},{1,17},{17,1},{2,18},{18,2},{3,19},{19,3},{4,20},{20... | collective-permute-start | bytes 196616 | tf_op jit(solution)/shard_map/ppermute | solution.py:350
  13.6 28.6 %collective-permute-start.6 = (bf16[64,5120]{1,0:T(8,128)(2,1)S(1)}, bf16[64,5120]{1,0:T(8,128)(2,1)S(1)}, u32[]{:S(2)}, u32[]{:S(2)}) collective-permute-start(bf16[64,5120]{1,0:T(8,128)(2,1)S(1)} %feat_rows.1.refs_3_), channel_id=1, source_target_pairs={{0,1},{3,2},{4,5},{7,6},{8,9},{11,10},{12,13},{15,14},{16,17},{19,... | collective-permute-start | bytes 1966088 | tf_op jit(solution)/shard_map/ppermute | solution.py:412
  19.2 4.0 %collective-permute-start = (f32[64,128]{1,0:T(8,128)S(1)}, f32[64,128]{1,0:T(8,128)S(1)}, u32[]{:S(2)}, u32[]{:S(2)}) collective-permute-start(f32[64,128]{1,0:T(8,128)S(1)} %get-tuple-element.65.refs_0_), channel_id=1, source_target_pairs={{0,16},{16,0},{1,17},{17,1},{2,18},{18,2},{3,19},{19,3},{4,20},{20... | collective-permute-start | bytes 98312 | tf_op jit(solution)/shard_map/ppermute | solution.py:343
  24.0 0.6 copy-start.5
  24.6 17.7 %collective-permute-start.3 = (bf16[64,4096]{1,0:T(8,128)(2,1)}, bf16[64,4096]{1,0:T(8,128)(2,1)S(1)}, u32[]{:S(2)}, u32[]{:S(2)}) collective-permute-start(bf16[64,4096]{1,0:T(8,128)(2,1)} %collective-permute-done.1.refs_1_.first), channel_id=1, source_target_pairs={{1,2},{2,3},{6,5},{5,4},{9,10},{10,11},{14,13},{13,12},{17,18},{18... | collective-permute-start | bytes 1572872 | tf_op jit(solution)/shard_map/ppermute | solution.py:375
  25.3 17.0 %collective-permute-start.4 = (bf16[64,4096]{1,0:T(8,128)(2,1)}, bf16[64,4096]{1,0:T(8,128)(2,1)S(1)}, u32[]{:S(2)}, u32[]{:S(2)}) collective-permute-start(bf16[64,4096]{1,0:T(8,128)(2,1)} %collective-permute-done.2.refs_2_.second), channel_id=1, source_target_pairs={{1,0},{2,1},{6,7},{5,6},{9,8},{10,9},{14,15},{13,14},{17,16},{18,1... | collective-permute-start | bytes 1572872 | tf_op jit(solution)/shard_map/ppermute | solution.py:375
  26.6 8.4 %collective-permute-start.7 = (bf16[9,64,128]{2,1,0:T(8,128)(2,1)}, bf16[9,64,128]{2,1,0:T(8,128)(2,1)}, u32[]{:S(2)}, u32[]{:S(2)}) collective-permute-start(bf16[9,64,128]{2,1,0:T(8,128)(2,1)} %get-tuple-element.68.refs_0_), channel_id=1, source_target_pairs={{0,16},{16,0},{1,17},{17,1},{2,18},{18,2},{3,19},{19,3},{4,20},{20... | collective-permute-start | bytes 442376 | tf_op jit(solution)/shard_map/ppermute | solution.py:343
  28.2 1.0 %copy-start.2 = (bf16[8,8,8,512]{3,1,2,0:T(8,128)(2,1)S(1)}, bf16[8,8,8,512]{3,1,2,0:T(8,128)(2,1)}, u32[]{:S(2)}) copy-start(bf16[8,8,8,512]{3,1,2,0:T(8,128)(2,1)} %copy-done.1) | copy-start | bytes 1572868
  33.7 7.8 %collective-permute-start.8 = (bf16[64,576]{1,0:T(8,128)(2,1)S(1)}, bf16[64,576]{1,0:T(8,128)(2,1)S(1)}, u32[]{:S(2)}, u32[]{:S(2)}) collective-permute-start(bf16[64,576]{1,0:T(8,128)(2,1)S(1)} %get-tuple-element.77), channel_id=1, source_target_pairs={{1,0},{2,1},{3,2},{6,7},{5,6},{4,5},{9,8},{10,9},{11,10},{14,15},{... | collective-permute-start | bytes 221192 | tf_op jit(solution)/shard_map/ppermute | solution.py:375
  35.0 7.2 %collective-permute-start.9 = (bf16[64,576]{1,0:T(8,128)(2,1)S(1)}, bf16[64,576]{1,0:T(8,128)(2,1)S(1)}, u32[]{:S(2)}, u32[]{:S(2)}) collective-permute-start(bf16[64,576]{1,0:T(8,128)(2,1)S(1)} %get-tuple-element.78), channel_id=1, source_target_pairs={{0,1},{1,2},{2,3},{7,6},{6,5},{5,4},{8,9},{9,10},{10,11},{15,14},{... | collective-permute-start | bytes 221192 | tf_op jit(solution)/shard_map/ppermute | solution.py:375
  42.3 16.3 %copy-start.6 = (f32[64,128]{1,0:T(8,128)S(1)}, f32[64,128]{1,0:T(8,128)}, u32[]{:S(2)}) copy-start(f32[64,128]{1,0:T(8,128)} %copy-done.5) | copy-start | bytes 98308
  46.9 24.9 %copy-start.3 = (bf16[8,8,8,512]{3,1,2,0:T(8,128)(2,1)S(1)}, bf16[8,8,8,512]{3,1,2,0:T(8,128)(2,1)}, u32[]{:S(2)}) copy-start(bf16[8,8,8,512]{3,1,2,0:T(8,128)(2,1)} %copy-done.1) | copy-start | bytes 1572868
  46.9 24.9 %collective-permute-start.18 = (bf16[64,4096]{1,0:T(8,128)(2,1)S(1)}, bf16[64,4096]{1,0:T(8,128)(2,1)S(1)}, u32[]{:S(2)}, u32[]{:S(2)}) collective-permute-start(bf16[64,4096]{1,0:T(8,128)(2,1)S(1)} %get-tuple-element.101), channel_id=1, source_target_pairs={{1,0},{2,3},{5,4},{6,7},{9,8},{10,11},{13,12},{14,15},{17,16},{18,... | collective-permute-start | bytes 1572872 | tf_op jit(solution)/shard_map/ppermute | solution.py:469
  48.3 10.3 %collective-permute-start.10 = (bf16[128,576]{1,0:T(8,128)(2,1)S(1)}, bf16[128,576]{1,0:T(8,128)(2,1)S(1)}, u32[]{:S(2)}, u32[]{:S(2)}) collective-permute-start(bf16[128,576]{1,0:T(8,128)(2,1)S(1)} %get-tuple-element.87), channel_id=1, source_target_pairs={{0,2},{1,3},{2,0},{3,1},{7,5},{6,4},{5,7},{4,6},{8,10},{9,11},{10,... | collective-permute-start | bytes 442376 | tf_op jit(solution)/shard_map/ppermute | solution.py:375
  59.6 5.5 %collective-permute-start.11 = (bf16[10,64,128]{2,1,0:T(8,128)(2,1)S(1)}, bf16[10,64,128]{2,1,0:T(8,128)(2,1)S(1)}, u32[]{:S(2)}, u32[]{:S(2)}) collective-permute-start(bf16[10,64,128]{2,1,0:T(8,128)(2,1)S(1)} %get-tuple-element.95), channel_id=1, source_target_pairs={{0,16},{16,0},{1,17},{17,1},{2,18},{18,2},{3,19},{19,3},{4,20},{20... | collective-permute-start | bytes 491528 | tf_op jit(solution)/shard_map/ppermute | solution.py:487
  60.2 6.3 %collective-permute-start.15 = (bf16[64,576]{1,0:T(8,128)(2,1)S(1)}, bf16[64,576]{1,0:T(8,128)(2,1)S(1)}, u32[]{:S(2)}, u32[]{:S(2)}) collective-permute-start(bf16[64,576]{1,0:T(8,128)(2,1)S(1)} %get-tuple-element.98), channel_id=1, source_target_pairs={{0,1},{1,2},{2,3},{3,0},{7,6},{6,5},{5,4},{4,7},{8,9},{9,10},{10,1... | collective-permute-start | bytes 221192 | tf_op jit(solution)/shard_map/ppermute | solution.py:375
  60.2 7.8 %collective-permute-start.16 = (bf16[64,576]{1,0:T(8,128)(2,1)S(1)}, bf16[64,576]{1,0:T(8,128)(2,1)S(1)}, u32[]{:S(2)}, u32[]{:S(2)}) collective-permute-start(bf16[64,576]{1,0:T(8,128)(2,1)S(1)} %get-tuple-element.99), channel_id=1, source_target_pairs={{0,2},{1,3},{2,0},{3,1},{7,5},{6,4},{5,7},{4,6},{8,10},{9,11},{10,... | collective-permute-start | bytes 221192 | tf_op jit(solution)/shard_map/ppermute | solution.py:375
  62.2 9.6 %collective-permute-start.17 = (bf16[64,576]{1,0:T(8,128)(2,1)S(1)}, bf16[64,576]{1,0:T(8,128)(2,1)S(1)}, u32[]{:S(2)}, u32[]{:S(2)}) collective-permute-start(bf16[64,576]{1,0:T(8,128)(2,1)S(1)} %get-tuple-element.100), channel_id=1, source_target_pairs={{0,3},{1,0},{2,1},{3,2},{7,4},{6,7},{5,6},{4,5},{8,11},{9,8},{10,9... | collective-permute-start | bytes 221192 | tf_op jit(solution)/shard_map/ppermute | solution.py:375
  65.3 11.6 %collective-permute-start.12 = (bf16[11,64,128]{2,1,0:T(8,128)(2,1)S(1)}, bf16[11,64,128]{2,1,0:T(8,128)(2,1)S(1)}, u32[]{:S(2)}, u32[]{:S(2)}) collective-permute-start(bf16[11,64,128]{2,1,0:T(8,128)(2,1)S(1)} %row_sum.1.refs_0_), channel_id=1, source_target_pairs={{0,4},{4,8},{8,12},{12,0},{1,5},{5,9},{9,13},{13,1},{2,6},{6,10},{... | collective-permute-start | bytes 540680 | tf_op jit(solution)/shard_map/ppermute | solution.py:343
  66.6 10.4 %collective-permute-start.13 = (bf16[11,64,128]{2,1,0:T(8,128)(2,1)S(1)}, bf16[11,64,128]{2,1,0:T(8,128)(2,1)S(1)}, u32[]{:S(2)}, u32[]{:S(2)}) collective-permute-start(bf16[11,64,128]{2,1,0:T(8,128)(2,1)S(1)} %row_sum.1.refs_0_), channel_id=1, source_target_pairs={{0,8},{4,12},{8,0},{12,4},{1,9},{5,13},{9,1},{13,5},{2,10},{6,14},... | collective-permute-start | bytes 540680 | tf_op jit(solution)/shard_map/ppermute | solution.py:343
  68.1 8.9 %collective-permute-start.14 = (bf16[11,64,128]{2,1,0:T(8,128)(2,1)S(1)}, bf16[11,64,128]{2,1,0:T(8,128)(2,1)S(1)}, u32[]{:S(2)}, u32[]{:S(2)}) collective-permute-start(bf16[11,64,128]{2,1,0:T(8,128)(2,1)S(1)} %row_sum.1.refs_0_), channel_id=1, source_target_pairs={{0,12},{4,0},{8,4},{12,8},{1,13},{5,1},{9,5},{13,9},{2,14},{6,2},{... | collective-permute-start | bytes 540680 | tf_op jit(solution)/shard_map/ppermute | solution.py:343
  77.0 11.0 %collective-permute-start.19 = (f32[64,512]{1,0:T(8,128)S(1)}, f32[64,512]{1,0:T(8,128)S(1)}, u32[]{:S(2)}, u32[]{:S(2)}) collective-permute-start(f32[64,512]{1,0:T(8,128)S(1)} %broadcast_select_fusion), channel_id=1, source_target_pairs={{0,16},{16,0},{1,17},{17,1},{2,18},{18,2},{3,19},{19,3},{4,20},{20... | collective-permute-start | bytes 393224 | tf_op jit(solution)/shard_map/ppermute | solution.py:350
  80.4 5.4 %collective-permute-start.20 = (f32[4,128]{1,0:T(4,128)S(1)}, f32[4,128]{1,0:T(4,128)S(1)}, u32[]{:S(2)}, u32[]{:S(2)}) collective-permute-start(f32[4,128]{1,0:T(4,128)S(1)} %get-tuple-element.119.refs_0_), channel_id=1, source_target_pairs={{0,1},{1,2},{2,3},{3,0},{4,5},{5,6},{6,7},{7,4},{8,9},{9,10},{10,1... | collective-permute-start | bytes 6152 | tf_op jit(solution)/shard_map/ppermute | solution.py:343
  80.4 5.4 %collective-permute-start.21 = (f32[4,128]{1,0:T(4,128)S(1)}, f32[4,128]{1,0:T(4,128)S(1)}, u32[]{:S(2)}, u32[]{:S(2)}) collective-permute-start(f32[4,128]{1,0:T(4,128)S(1)} %get-tuple-element.119.refs_0_), channel_id=1, source_target_pairs={{0,2},{1,3},{2,0},{3,1},{4,6},{5,7},{6,4},{7,5},{8,10},{9,11},{10,... | collective-permute-start | bytes 6152 | tf_op jit(solution)/shard_map/ppermute | solution.py:343
  81.5 4.9 %collective-permute-start.22 = (f32[4,128]{1,0:T(4,128)S(1)}, f32[4,128]{1,0:T(4,128)S(1)}, u32[]{:S(2)}, u32[]{:S(2)}) collective-permute-start(f32[4,128]{1,0:T(4,128)S(1)} %get-tuple-element.119.refs_0_), channel_id=1, source_target_pairs={{0,3},{1,0},{2,1},{3,2},{4,7},{5,4},{6,5},{7,6},{8,11},{9,8},{10,9... | collective-permute-start | bytes 6152 | tf_op jit(solution)/shard_map/ppermute | solution.py:343

commit v8 on v7

--- a/solution.py
+++ b/solution.py
@@ -12,6 +12,7 @@
 F32 = jnp.float32
 BF16 = jnp.bfloat16
 VMEM_LIMIT = 16 * 2**20
+COLLECT_FLOPS = 3 * 10**9
 
 
 def params():
@@ -153,22 +154,20 @@
         out[...] = whole[at * ch : (at + 1) * ch]
 
 
-def far_grad_kernel(count, height, width, *refs):
-    first, second, (wide, feat) = refs[:count], refs[count : 2 * count], refs[2 * count : 2 * count + 2]
-    (out, middle, end_block), (wide_end, total, end_total) = refs[2 * count + 2 : -3], refs[-3:]
-    ch = feat.shape[0]
+def middle_grad_kernel(count, height, width, *refs):
+    first, second, wide = refs[:count], refs[count : 2 * count], refs[2 * count]
+    out, middle, end_block, total = refs[2 * count + 1 :]
+    ch = end_block.shape[0]
     for at in range(count):
         middle[at * ch : (at + 1) * ch] = first[at][...] + second[count - 1 - at][...]
     end_block[...] = first[-1][...] + second[-1][...]
+    (out[...],) = tap_products(middle, [wide], [total], height, width)
+
+
+def end_grad_kernel(height, width, end_block, feat, out, wide, total):
     for row in range(height + 2):
-        spread(wide_end, row, feat[:, row * width : (row + 1) * width])
-    if count == 1:
-        whole, end = tap_products(end_block, [wide, wide_end], [total, end_total], height, width)
-    else:
-        (whole,) = tap_products(middle, [wide], [total], height, width)
-        (end,) = tap_products(end_block, [wide_end], [end_total], height, width)
-    out[0 : count * ch] = whole
-    out[count * ch :] = end
+        spread(wide, row, feat[:, row * width : (row + 1) * width])
+    (out[...],) = tap_products(end_block, [wide], [total], height, width)
 
 
 def input_grad_kernel(size, height, width, place, cotan, first, second, middle, far, *refs):
@@ -222,7 +221,7 @@
     return last[:, 3 * n : 3 * n + 1] + last[:, 3 * n + 1 : 3 * n + 2] + last[:, 3 * n + 2 : 3 * n + 3]
 
 
-def collect_kernel(rows, size, place, scale, whole_mod, own, ahead, behind, others, *refs):
+def collect_kernel(rows, size, place, scale, whole_mod, own, ahead, behind, others, end, *refs):
     outs, (by_chan, by_row) = refs[:rows], refs[rows:]
     chan_at, row_at, sign = place[1], place[2], place[3]
     ch = own.shape[0]
@@ -232,7 +231,7 @@
     for d in range(2, size - 1):
         value = others[(d - 2) * ch : (d - 1) * ch].astype(F32)
         by_chan[lax.rem(chan_at + sign * d + size, size)] = value
-    by_chan[jnp.where(chan_at == 0, size - 1, 0)] += others[(size - 3) * ch :].astype(F32)
+    by_chan[jnp.where(chan_at == 0, size - 1, 0)] += end[...].astype(F32)
     in_ch = outs[0].shape[2]
     product = jnp.zeros(whole_mod.shape[1:], F32)
     for tap in range(TAPS):
@@ -409,7 +408,6 @@
     (feat,) = call(
         functools.partial(rows_kernel, height, width), "feat_rows", [extended], feat, feat_before, feat_after
     )
-    feat_end = lax.ppermute(feat, "chan", [(0, 1), (size - 1, size - 2)])
     mod_own, scale = call(
         modulated_kernel,
         "modulated",
@@ -418,6 +416,8 @@
         style,
         *exchange(energy, "rows"),
     )
+    feat, mod_own = lax.optimization_barrier((feat, mod_own))
+    feat_end = lax.ppermute(feat, "chan", [(0, 1), (size - 1, size - 2)])
     message = ((ch, TAPS * ch), BF16)
     whole_mod, *mods = call(
         functools.partial(blocks_kernel, rows, size),
@@ -451,21 +451,26 @@
 
     count = size - 3
     grad_others, middle, end_block = call(
-        functools.partial(far_grad_kernel, count, height, width),
-        "far_grad",
-        [(((count + 1) * ch, TAPS * ch), BF16), ((count * ch, pixels), BF16), ((ch, pixels), BF16)],
+        functools.partial(middle_grad_kernel, count, height, width),
+        "middle_grad",
+        [((count * ch, TAPS * ch), BF16), ((count * ch, pixels), BF16), ((ch, pixels), BF16)],
         *first[1:],
         *second[1:],
         wide,
+        scratch=[((3, count * ch, 3 * ch), F32)],
+        flops=flops // size,
+    )
+    (grad_end,) = call(
+        functools.partial(end_grad_kernel, height, width),
+        "end_grad",
+        [message],
+        end_block,
         feat_end,
-        scratch=[
-            ((3 * ch, (height + 2) * width), BF16),
-            ((3, count * ch, 3 * ch), F32),
-            ((3, ch, 3 * ch), F32),
-        ],
-        flops=flops * 2 // size,
+        scratch=[((3 * ch, (height + 2) * width), BF16), ((3, ch, 3 * ch), F32)],
+        flops=flops // size,
     )
     from_others = along(grad_others, [(i, (i + 2) % size) for i in range(size)])
+    from_end = lax.ppermute(grad_end, "chan", [(1, size - 1), (size - 2, 0)])
     far = lax.ppermute(end_block, "chan", [(1, 0), (size - 2, size - 1)])
     parts = call(
         functools.partial(collect_kernel, rows, size),
@@ -478,8 +483,10 @@
         from_ahead,
         from_behind,
         from_others,
+        from_end,
         scalars=1,
         scratch=[((size, *message[0]), F32), ((rows, TAPS, out_ch, in_ch), BF16)],
+        flops=COLLECT_FLOPS,
     )
     parts, mods = lax.optimization_barrier((parts, mods))
     mods = [mods[0]] + [along(mods[d], [(i, (i + d) % size) for i in range(size)]) for d in range(1, size)]
@@ -528,6 +535,7 @@
         [from_above[:, None], jnp.zeros((ch, height - 2, width), F32), from_below[:, None]], axis=1
     )
     feature_grad = (main.reshape(ch, height, width) + edge).astype(BF16)[None]
+    style_parts, feature_grad = lax.optimization_barrier((style_parts, feature_grad))
     affine_w_grad, affine_b_grad = call(
         functools.partial(affine_kernel, samples, size),
         "affine",

time: 89.9 us -> 89.9 us (level)
  Pallas kernels: 22.9 us -> 25.2 us
  local copies, waits for them, and re-layouts: 4.12 us -> 2.51 us
    ppermute x0 -> x1, waiting for transfers between devices: none -> 4.8 us  [on_device(): from_end = lax.ppermute(grad_end, 'chan', [(1, size - 1), (size - 2, 0)])]
    ppermute x10, waiting for transfers between devices: 6.23 us -> 2.65 us  [along(): return lax.ppermute(x, ('samples', 'chan'), whole)]
    ppermute x2, waiting for transfers between devices: 2.78 us -> 0.01 us  [from_sides(): got = lax.ppermute(jnp.where(at == 0, last, first), axis, [(0, 1), (1, 0)])]
    pallas_call x11 -> x12, Pallas kernels: 22.9 us -> 25.2 us  [call(): pl.pallas_call(kernel, out_shape=outs, in_specs=sspec(scalars) + vspec(le...]
    unnamed x25 -> x19, local copies, waits for them, and re-layouts: 3.76 us -> 2.16 us
    ppermute x0 -> x1, starting transfers between devices: none -> 1.29 us  [on_device(): from_end = lax.ppermute(grad_end, 'chan', [(1, size - 1), (size - 2, 0)])]
    ppermute x1, waiting for transfers between devices: 0.01 us -> 1.03 us  [on_device(): lax.ppermute(parts[r], 'rows', [(i, (i + r) % rows) for i in range(rows)])]
    ppermute x10, starting transfers between devices: 26.3 us -> 25.3 us  [along(): return lax.ppermute(x, ('samples', 'chan'), whole)]
  transfers between devices with their start and end apart: 23 -> 24, of which waited for: 7 -> 7; matrix products, arithmetic and copies ran while one was open for 1% -> 3% of each run, Pallas kernels for 21% -> 22%
where the time goes in v8:
time: 89.9 us; the launch traced here: 89.5 us
  starting transfers between devices  46.6 us (52%)
  Pallas kernels  25.2 us (28%)
  waiting for transfers between devices  13 us (14%)
  local copies, waits for them, and re-layouts  2.51 us (3%)
  other arithmetic  1.25 us (1%)
  between operations  1.01 us (1%)
    ppermute x10, starting transfers between devices, along(): return lax.ppermute(x, ('samples', 'chan'), whole)  25.3 us
    pallas_call x12, Pallas kernels, call(): pl.pallas_call(kernel, out_shape=outs, in_specs=sspec(scalars) + vspec(le...  25.2 us
    ppermute x8, starting transfers between devices, exchange(): lax.ppermute(x, axis, [(i, (i + s) % size) for i in range(size)])  11.4 us
    ppermute x1, waiting for transfers between devices, on_device(): from_end = lax.ppermute(grad_end, 'chan', [(1, size - 1), (size - 2, 0)])  4.8 us
    ppermute x1, starting transfers between devices, on_device(): feat_end = lax.ppermute(feat, 'chan', [(0, 1), (size - 1, size - 2)])  4.56 us
    ppermute x8, waiting for transfers between devices, exchange(): lax.ppermute(x, axis, [(i, (i + s) % size) for i in range(size)])  4.5 us
    ppermute x10, waiting for transfers between devices, along(): return lax.ppermute(x, ('samples', 'chan'), whole)  2.65 us
    ppermute x2, starting transfers between devices, from_sides(): got = lax.ppermute(jnp.where(at == 0, last, first), axis, [(0, 1), (1, 0)])  2.19 us
  transfers between devices with their start and end apart: 24, of which 7 were waited for; matrix products, arithmetic and copies ran while one was open for 3% of the time, Pallas kernels for 22%

profile of v8, /device:TPU:0, one launch (start us, length us, event | category | flops | bytes accessed | tf_op | source)
XLA Modules:
  0.0 89.5 jit_solution(15103227855742735650)
XLA Ops:
  0.7 1.3 %copy.13 = bf16[8,8,8,512]{3,1,2,0:T(8,128)(2,1)S(1)} copy(bf16[8,8,8,512]{3,2,1,0:T(8,128)(2,1)} %bitcast.32) | data formatting | bytes 1048576
  2.0 5.7 %collective-permute-start.1 = (bf16[64,4096]{1,0:T(8,128)(2,1)S(1)}, bf16[64,4096]{1,0:T(8,128)(2,1)}, u32[]{:S(2)}, u32[]{:S(2)}) collective-permute-start(bf16[64,4096]{1,0:T(8,128)(2,1)S(1)} %bitcast.26), channel_id=1, source_target_pairs={{0,1},{1,2},{2,3},{7,6},{6,5},{5,4},{8,9},{9,10},{10,11},{15,14},{... | collective-permute-start | bytes 1572872 | tf_op jit(solution)/shard_map/ppermute | solution.py:374
  7.8 1.3 %collective-permute-start.2 = (bf16[64,4096]{1,0:T(8,128)(2,1)S(1)}, bf16[64,4096]{1,0:T(8,128)(2,1)}, u32[]{:S(2)}, u32[]{:S(2)}) collective-permute-start(bf16[64,4096]{1,0:T(8,128)(2,1)S(1)} %bitcast.27), channel_id=1, source_target_pairs={{1,0},{2,1},{3,2},{6,7},{5,6},{4,5},{9,8},{10,9},{11,10},{14,15},{... | collective-permute-start | bytes 1572872 | tf_op jit(solution)/shard_map/ppermute | solution.py:374
  9.1 0.2 copy.14
  9.3 1.6 %collective-permute-start.3 = (bf16[64,512]{1,0:T(8,128)(2,1)S(1)}, bf16[64,512]{1,0:T(8,128)(2,1)S(1)}, u32[]{:S(2)}, u32[]{:S(2)}) collective-permute-start(bf16[64,512]{1,0:T(8,128)(2,1)S(1)} %slice_select_fusion), channel_id=1, source_target_pairs={{0,16},{16,0},{1,17},{17,1},{2,18},{18,2},{3,19},{19,3},{4,20},{20... | collective-permute-start | bytes 196616 | tf_op jit(solution)/shard_map/ppermute | solution.py:349
  10.9 0.9 %energy.1 = (f32[1,128]{1,0:T(1,128)S(1)}, f32[9,64,128]{2,1,0:T(8,128)S(1)}, f32[64,128]{1,0:T(8,128)S(1)}, f32[8,128]{1,0:T(8,128)S(1)}) custom-call(s32[1,4]{1,0:T(1,128)S(1)} %copy-done.5, f32[1,512]{1,0:T(1,128)S(1)} %copy-done.4, f32[1,128]{1,0:T(1,128)S(1)} %bitcast.30, f32[512,128]{1,0:T(8,128)S(1)} %copy-done.1, f32[4,9,64,128]{3,2,1,0:T(8,128)S(1)} %copy-done), custom_call_target="tpu_custom_call" | custom-call | flops 1000000 | bytes 1776656 | tf_op jit(solution)/shard_map/energy/pallas_call | solution.py:325
  11.8 0.6 collective-permute-start
  12.4 3.4 %collective-permute-done.refs_1_ = f32[64,128]{1,0:T(8,128)S(1)} collective-permute-done((f32[64,128]{1,0:T(8,128)S(1)}, f32[64,128]{1,0:T(8,128)S(1)}, u32[]{:S(2)}, u32[]{:S(2)}) %collective-permute-start) | collective-permute-done | bytes 32800 | tf_op jit(solution)/shard_map/ppermute | solution.py:342
  15.8 0.8 modulated.1
  16.6 0.0 collective-permute-done.3
  16.6 4.6 %collective-permute-start.6 = (bf16[64,5120]{1,0:T(8,128)(2,1)S(1)}, bf16[64,5120]{1,0:T(8,128)(2,1)S(1)}, u32[]{:S(2)}, u32[]{:S(2)}) collective-permute-start(bf16[64,5120]{1,0:T(8,128)(2,1)S(1)} %feat_rows.1.refs_3_), channel_id=1, source_target_pairs={{0,1},{3,2},{4,5},{7,6},{8,9},{11,10},{12,13},{15,14},{16,17},{19,... | collective-permute-start | bytes 1966088 | tf_op jit(solution)/shard_map/ppermute | solution.py:420
  21.2 0.0 collective-permute-done.1.refs_1_.first
  21.2 0.0 collective-permute-done.2.refs_2_.second
  21.2 0.7 collective-permute-start.4
  21.9 1.3 %collective-permute-start.5 = (bf16[64,4096]{1,0:T(8,128)(2,1)}, bf16[64,4096]{1,0:T(8,128)(2,1)}, u32[]{:S(2)}, u32[]{:S(2)}) collective-permute-start(bf16[64,4096]{1,0:T(8,128)(2,1)} %collective-permute-done.2.refs_2_.second), channel_id=1, source_target_pairs={{1,0},{2,1},{6,7},{5,6},{9,8},{10,9},{14,15},{13,14},{17,16},{18,1... | collective-permute-start | bytes 1572872 | tf_op jit(solution)/shard_map/ppermute | solution.py:374
  23.2 0.6 collective-permute-start.7
  23.9 4.5 %near_grad.1 = (bf16[64,576]{1,0:T(8,128)(2,1)S(1)}, bf16[64,576]{1,0:T(8,128)(2,1)S(1)}, bf16[64,576]{1,0:T(8,128)(2,1)S(1)}, bf16[192,5120]{1,0:T(8,128)(2,1)S(1)}) custom-call(bf16[64,4096]{1,0:T(8,128)(2,1)S(1)} %bitcast.28, bf16[64,4096]{1,0:T(8,128)(2,1)} %collective-permute-done.1.refs_1_.first, ...), custom_call_target="tpu_custom_call" | custom-call | flops 905969664 | bytes 4415488 | tf_op jit(solution)/shard_map/near_grad/pallas_call | solution.py:325
  28.4 1.3 %collective-permute-start.8 = (bf16[64,576]{1,0:T(8,128)(2,1)S(1)}, bf16[64,576]{1,0:T(8,128)(2,1)S(1)}, u32[]{:S(2)}, u32[]{:S(2)}) collective-permute-start(bf16[64,576]{1,0:T(8,128)(2,1)S(1)} %get-tuple-element.86), channel_id=1, source_target_pairs={{1,0},{2,1},{3,2},{6,7},{5,6},{4,5},{9,8},{10,9},{11,10},{14,15},{... | collective-permute-start | bytes 221192 | tf_op jit(solution)/shard_map/ppermute | solution.py:374
  29.7 0.0 collective-permute-done.7.refs_1_
  29.7 6.6 %collective-permute-start.9 = (bf16[64,576]{1,0:T(8,128)(2,1)S(1)}, bf16[64,576]{1,0:T(8,128)(2,1)S(1)}, u32[]{:S(2)}, u32[]{:S(2)}) collective-permute-start(bf16[64,576]{1,0:T(8,128)(2,1)S(1)} %get-tuple-element.87), channel_id=1, source_target_pairs={{0,1},{1,2},{2,3},{7,6},{6,5},{5,4},{8,9},{9,10},{10,11},{15,14},{... | collective-permute-start | bytes 221192 | tf_op jit(solution)/shard_map/ppermute | solution.py:374
  36.3 0.1 pad_add_fusion.place
  36.4 1.2 %mod_blocks.1 = (bf16[9,64,256]{2,1,0:T(8,128)(2,1)S(1)}, bf16[64,576]{1,0:T(8,128)(2,1)S(1)}, bf16[64,576]{1,0:T(8,128)(2,1)S(1)}, bf16[64,576]{1,0:T(8,128)(2,1)S(1)}, bf16[64,576]{1,0:T(8,128)(2,1)S(1)}) custom-call(s32[4]{0:T(128)S(1)} %pad_add_fusion.place, bf16[9,64,128]{2,1,0:T(8,128)(2,1)} %get-tuple-element.76.refs_0_, ...), custom_call_target="tpu_custom_call" | custom-call | flops 1000000 | bytes 884752 | tf_op jit(solution)/shard_map/mod_blocks/pallas_call | solution.py:325
  37.6 0.0 collective-permute-done.8.ahead
  37.6 0.7 collective-permute-done.9.behind
  38.3 0.0 collective-permute-done.6.feat
  38.4 0.0 collective-permute-done.4.refs_0_
  38.4 0.0 collective-permute-done.5.refs_1_
  38.4 3.7 %middle_grad.1 = (bf16[64,576]{1,0:T(8,128)(2,1)S(1)}, bf16[64,4096]{1,0:T(8,128)(2,1)S(1)}, bf16[64,4096]{1,0:T(8,128)(2,1)S(1)}) custom-call(bf16[64,4096]{1,0:T(8,128)(2,1)S(1)} %collective-permute-done.4.refs_0_, bf16[64,4096]{1,0:T(8,128)(2,1)} %collective-permute-done.5.refs_1_, bf16[192,5120]{1,0:T(8,128)(2,1)S(1)} %get-tuple-element.94.refs_2_), custom_call_target="tpu_custom_call" | custom-call | flops 301989888 | bytes 4136960 | tf_op jit(solution)/shard_map/middle_grad/pallas_call | solution.py:325
  42.1 0.0 copy-start.3
  42.1 4.6 %collective-permute-start.10 = (bf16[64,576]{1,0:T(8,128)(2,1)S(1)}, bf16[64,576]{1,0:T(8,128)(2,1)S(1)}, u32[]{:S(2)}, u32[]{:S(2)}) collective-permute-start(bf16[64,576]{1,0:T(8,128)(2,1)S(1)} %get-tuple-element.95), channel_id=1, source_target_pairs={{0,2},{1,3},{2,0},{3,1},{7,5},{6,4},{5,7},{4,6},{8,10},{9,11},{10,... | collective-permute-start | bytes 221192 | tf_op jit(solution)/shard_map/ppermute | solution.py:374
  46.7 3.0 %end_grad.1 = bf16[64,576]{1,0:T(8,128)(2,1)S(1)} custom-call(bf16[64,4096]{1,0:T(8,128)(2,1)S(1)} %get-tuple-element.96.end_block, bf16[64,5120]{1,0:T(8,128)(2,1)S(1)} %collective-permute-done.6.feat), custom_call_target="tpu_custom_call" | custom-call | flops 301989888 | bytes 1253376 | tf_op jit(solution)/shard_map/end_grad/pallas_call | solution.py:325
  49.8 1.3 %collective-permute-start.11 = (bf16[64,576]{1,0:T(8,128)(2,1)S(1)}, bf16[64,576]{1,0:T(8,128)(2,1)S(1)}, u32[]{:S(2)}, u32[]{:S(2)}) collective-permute-start(bf16[64,576]{1,0:T(8,128)(2,1)S(1)} %end_grad.1), channel_id=1, source_target_pairs={{1,3},{2,0},{5,7},{6,4},{9,11},{10,8},{13,15},{14,12},{17,19},{18,... | collective-permute-start | bytes 221192 | tf_op jit(solution)/shard_map/ppermute | solution.py:473
  51.1 1.3 %collective-permute-start.19 = (bf16[64,4096]{1,0:T(8,128)(2,1)S(1)}, bf16[64,4096]{1,0:T(8,128)(2,1)S(1)}, u32[]{:S(2)}, u32[]{:S(2)}) collective-permute-start(bf16[64,4096]{1,0:T(8,128)(2,1)S(1)} %get-tuple-element.96.end_block), channel_id=1, source_target_pairs={{1,0},{2,3},{5,4},{6,7},{9,8},{10,11},{13,12},{14,15},{17,16},{18,... | collective-permute-start | bytes 1572872 | tf_op jit(solution)/shard_map/ppermute | solution.py:474
  52.4 0.0 collective-permute-done.10.others
  52.4 4.8 %collective-permute-done.11.end = bf16[64,576]{1,0:T(8,128)(2,1)S(1)} collective-permute-done((bf16[64,576]{1,0:T(8,128)(2,1)S(1)}, bf16[64,576]{1,0:T(8,128)(2,1)S(1)}, u32[]{:S(2)}, u32[]{:S(2)}) %collective-permute-start.11) | collective-permute-done | bytes 73760 | tf_op jit(solution)/shard_map/ppermute | solution.py:473
  57.2 1.1 %collect.1 = (bf16[10,64,128]{2,1,0:T(8,128)(2,1)S(1)}, bf16[10,64,128]{2,1,0:T(8,128)(2,1)S(1)}) custom-call(s32[4]{0:T(128)S(1)} %pad_add_fusion.place, f32[64,128]{1,0:T(8,128)S(1)} %copy-done.3, bf16[9,64,256]{2,1,0:T(8,128)(2,1)S(1)} %get-tuple-element.88.whole_mod, bf16[64,576]{1,0:T(8,128)(2,1)S(1)} %get-tuple-element.89.own, ...), custom_call_target="tpu_custom_call" | custom-call | flops 3000000000 | bytes 1024016 | tf_op jit(solution)/shard_map/collect/pallas_call | solution.py:325
  58.3 0.5 collective-permute-start.12
  58.8 0.0 collective-permute-start.16
  58.8 2.0 %collective-permute-start.17 = (bf16[64,576]{1,0:T(8,128)(2,1)S(1)}, bf16[64,576]{1,0:T(8,128)(2,1)S(1)}, u32[]{:S(2)}, u32[]{:S(2)}) collective-permute-start(bf16[64,576]{1,0:T(8,128)(2,1)S(1)} %get-tuple-element.109), channel_id=1, source_target_pairs={{0,2},{1,3},{2,0},{3,1},{7,5},{6,4},{5,7},{4,6},{8,10},{9,11},{10,... | collective-permute-start | bytes 221192 | tf_op jit(solution)/shard_map/ppermute | solution.py:374
  60.8 1.8 %collective-permute-start.18 = (bf16[64,576]{1,0:T(8,128)(2,1)S(1)}, bf16[64,576]{1,0:T(8,128)(2,1)S(1)}, u32[]{:S(2)}, u32[]{:S(2)}) collective-permute-start(bf16[64,576]{1,0:T(8,128)(2,1)S(1)} %get-tuple-element.110), channel_id=1, source_target_pairs={{0,3},{1,0},{2,1},{3,2},{7,4},{6,7},{5,6},{4,5},{8,11},{9,8},{10,9... | collective-permute-start | bytes 221192 | tf_op jit(solution)/shard_map/ppermute | solution.py:374
  62.6 1.0 %collective-permute-done.12.refs_1_ = bf16[10,64,128]{2,1,0:T(8,128)(2,1)S(1)} collective-permute-done((bf16[10,64,128]{2,1,0:T(8,128)(2,1)S(1)}, bf16[10,64,128]{2,1,0:T(8,128)(2,1)S(1)}, u32[]{:S(2)}, u32[]{:S(2)}) %collective-permute-start.12) | collective-permute-done | bytes 163872 | tf_op jit(solution)/shard_map/ppermute | solution.py:494
  63.6 0.2 row_sum.1.refs_0_
  63.9 0.1 collective-permute-start.13
  63.9 1.2 %collective-permute-done.16.refs_1_ = bf16[64,576]{1,0:T(8,128)(2,1)S(1)} collective-permute-done((bf16[64,576]{1,0:T(8,128)(2,1)S(1)}, bf16[64,576]{1,0:T(8,128)(2,1)S(1)}, u32[]{:S(2)}, u32[]{:S(2)}) %collective-permute-start.16) | collective-permute-done | bytes 73760 | tf_op jit(solution)/shard_map/ppermute | solution.py:374
  65.1 1.5 %collective-permute-start.14 = (bf16[11,64,128]{2,1,0:T(8,128)(2,1)S(1)}, bf16[11,64,128]{2,1,0:T(8,128)(2,1)S(1)}, u32[]{:S(2)}, u32[]{:S(2)}) collective-permute-start(bf16[11,64,128]{2,1,0:T(8,128)(2,1)S(1)} %row_sum.1.refs_0_), channel_id=1, source_target_pairs={{0,8},{4,12},{8,0},{12,4},{1,9},{5,13},{9,1},{13,5},{2,10},{6,14},... | collective-permute-start | bytes 540680 | tf_op jit(solution)/shard_map/ppermute | solution.py:342
  66.6 0.0 collective-permute-done.17.refs_2_
  66.6 4.1 %collective-permute-start.15 = (bf16[11,64,128]{2,1,0:T(8,128)(2,1)S(1)}, bf16[11,64,128]{2,1,0:T(8,128)(2,1)S(1)}, u32[]{:S(2)}, u32[]{:S(2)}) collective-permute-start(bf16[11,64,128]{2,1,0:T(8,128)(2,1)S(1)} %row_sum.1.refs_0_), channel_id=1, source_target_pairs={{0,12},{4,0},{8,4},{12,8},{1,13},{5,1},{9,5},{13,9},{2,14},{6,2},{... | collective-permute-start | bytes 540680 | tf_op jit(solution)/shard_map/ppermute | solution.py:342
  70.8 0.7 collective-permute-done.18.refs_3_
  71.5 5.2 %input_grad.1 = (f32[64,4096]{1,0:T(8,128)S(1)}, f32[64,512]{1,0:T(8,128)S(1)}, f32[64,512]{1,0:T(8,128)S(1)}) custom-call(s32[4]{0:T(128)S(1)} %pad_add_fusion.place, bf16[64,4096]{1,0:T(8,128)(2,1)S(1)} %bitcast.29, bf16[64,4096]{1,0:T(8,128)(2,1)} %collective-permute-done.1.refs_1_.first, bf16[64,4096]{1,0:T(8,128)(2,1)} %collective-permute-done.2.refs_2_.second, ...), custom_call_target="tpu_custom_call" | custom-call | flops 1207959552 | bytes 4227088 | tf_op jit(solution)/shard_map/input_grad/pallas_call | solution.py:325
  76.7 0.0 collective-permute-done.13.refs_1_
  76.7 0.6 collective-permute-start.23
  77.3 0.1 pad.1.clone
  77.4 2.8 %bank_grad.1 = (f32[4,9,64,128]{3,2,1,0:T(8,128)}, f32[4,128]{1,0:T(4,128)S(1)}, f32[4,512]{1,0:T(4,128)S(1)}) custom-call(s32[4]{0:T(128)S(1)} %pad_add_fusion.place, f32[4,9,64,128]{3,2,1,0:T(8,128)S(1)} %copy-done, bf16[11,64,128]{2,1,0:T(8,128)(2,1)S(1)} %row_sum.1.refs_0_, bf16[11,64,128]{2,1,0:T(8,128)(2,1)S(1)} %collective-permute-done.13.refs_1_, ...), custom_call_target="tpu_custom_call" | custom-call | flops 1000000 | bytes 3090448 | tf_op jit(solution)/shard_map/bank_grad/pallas_call | solution.py:325
  80.2 0.0 collective-permute-start.20
  80.2 4.0 %collective-permute-start.21 = (f32[4,128]{1,0:T(4,128)S(1)}, f32[4,128]{1,0:T(4,128)S(1)}, u32[]{:S(2)}, u32[]{:S(2)}) collective-permute-start(f32[4,128]{1,0:T(4,128)S(1)} %get-tuple-element.130.refs_0_), channel_id=1, source_target_pairs={{0,2},{1,3},{2,0},{3,1},{4,6},{5,7},{6,4},{7,5},{8,10},{9,11},{10,... | collective-permute-start | bytes 6152 | tf_op jit(solution)/shard_map/ppermute | solution.py:342
  84.3 0.5 collective-permute-start.22
  84.7 0.6 copy.15
  85.4 0.1 copy.12
  85.5 0.1 copy.11
  85.7 1.1 %fusion = bf16[1,64,8,512]{3,2,1,0:T(8,128)(2,1)} fusion(f32[1,64,1,512]{3,2,1,0:T(1,128)S(1)} %copy.12, f32[1,64,1,512]{3,2,1,0:T(1,128)S(1)} %copy.11, f32[8]{0:T(128)S(1)} %pad.1.clone, f32[1,64,8,512]{3,2,1,0:T(8,128)S(1)} %bitcast.31), kind=kLoop, calls=%fused_computation.1 | loop fusion | flops 1048576 | bytes 1835040 | tf_op jit(solution)/shard_map/convert_element_type | solution.py:537
  86.8 0.0 collective-permute-done.20.refs_1_
  86.8 0.0 collective-permute-done.21.refs_2_
  86.8 1.1 %collective-permute-done.22.refs_3_ = f32[4,128]{1,0:T(4,128)S(1)} collective-permute-done((f32[4,128]{1,0:T(4,128)S(1)}, f32[4,128]{1,0:T(4,128)S(1)}, u32[]{:S(2)}, u32[]{:S(2)}) %collective-permute-start.22) | collective-permute-done | bytes 2080 | tf_op jit(solution)/shard_map/ppermute | solution.py:342
  87.9 1.7 %affine.1 = (f32[512,128]{1,0:T(8,128)}, f32[1,128]{1,0:T(1,128)}) custom-call(s32[4]{0:T(128)S(1)} %pad_add_fusion.place, f32[4,512]{1,0:T(4,128)S(1)} %get-tuple-element.129.latents, f32[4,128]{1,0:T(4,128)S(1)} %get-tuple-element.130.refs_0_, f32[4,128]{1,0:T(4,128)S(1)} %collective-permute-done.20.refs_1_, f32[4,128]{1,0:T(4,128)S(1)} %collective-permute-done.21.refs_2_, ...), custom_call_target="tpu_custom_call" | custom-call | flops 1000000 | bytes 279056 | tf_op jit(solution)/shard_map/affine/pallas_call | solution.py:325
  (25 shorter events, 0.2 us)
Async XLA Ops:
  0.6 8.4 %copy-start.7 = (bf16[1,64,8,512]{3,2,1,0:T(8,128)(2,1)S(1)}, bf16[1,64,8,512]{3,2,1,0:T(8,128)(2,1)}, u32[]{:S(2)}) copy-start(bf16[1,64,8,512]{3,2,1,0:T(8,128)(2,1)} %param.7) | copy-start | bytes 1572868
  0.6 10.2 %copy-start = (f32[4,9,64,128]{3,2,1,0:T(8,128)S(1)}, f32[4,9,64,128]{3,2,1,0:T(8,128)}, u32[]{:S(2)}) copy-start(f32[4,9,64,128]{3,2,1,0:T(8,128)} %bank.1) | copy-start | bytes 3538948
  0.7 10.2 %copy-start.5 = (s32[1,4]{1,0:T(1,128)S(1)}, s32[1,4]{1,0:T(1,128)}, u32[]{:S(2)}) copy-start(s32[1,4]{1,0:T(1,128)} %refs_0_.1) | copy-start | bytes 52
  0.7 10.2 %copy-start.4 = (f32[1,512]{1,0:T(1,128)S(1)}, f32[1,512]{1,0:T(1,128)}, u32[]{:S(2)}) copy-start(f32[1,512]{1,0:T(1,128)} %refs_1_.1) | copy-start | bytes 6148
  0.7 10.2 %copy-start.6 = (f32[128]{0:T(128)S(1)}, f32[128]{0:T(128)}, u32[]{:S(2)}) copy-start(f32[128]{0:T(128)} %param.13) | copy-start | bytes 1540
  0.7 10.2 %copy-start.1 = (f32[512,128]{1,0:T(8,128)S(1)}, f32[512,128]{1,0:T(8,128)}, u32[]{:S(2)}) copy-start(f32[512,128]{1,0:T(8,128)} %refs_3_.1) | copy-start | bytes 786436
  2.0 19.2 %collective-permute-start.1 = (bf16[64,4096]{1,0:T(8,128)(2,1)S(1)}, bf16[64,4096]{1,0:T(8,128)(2,1)}, u32[]{:S(2)}, u32[]{:S(2)}) collective-permute-start(bf16[64,4096]{1,0:T(8,128)(2,1)S(1)} %bitcast.26), channel_id=1, source_target_pairs={{0,1},{1,2},{2,3},{7,6},{6,5},{5,4},{8,9},{9,10},{10,11},{15,14},{... | collective-permute-start | bytes 1572872 | tf_op jit(solution)/shard_map/ppermute | solution.py:374
  7.8 13.5 %collective-permute-start.2 = (bf16[64,4096]{1,0:T(8,128)(2,1)S(1)}, bf16[64,4096]{1,0:T(8,128)(2,1)}, u32[]{:S(2)}, u32[]{:S(2)}) collective-permute-start(bf16[64,4096]{1,0:T(8,128)(2,1)S(1)} %bitcast.27), channel_id=1, source_target_pairs={{1,0},{2,1},{3,2},{6,7},{5,6},{4,5},{9,8},{10,9},{11,10},{14,15},{... | collective-permute-start | bytes 1572872 | tf_op jit(solution)/shard_map/ppermute | solution.py:374
  9.3 7.3 %collective-permute-start.3 = (bf16[64,512]{1,0:T(8,128)(2,1)S(1)}, bf16[64,512]{1,0:T(8,128)(2,1)S(1)}, u32[]{:S(2)}, u32[]{:S(2)}) collective-permute-start(bf16[64,512]{1,0:T(8,128)(2,1)S(1)} %slice_select_fusion), channel_id=1, source_target_pairs={{0,16},{16,0},{1,17},{17,1},{2,18},{18,2},{3,19},{19,3},{4,20},{20... | collective-permute-start | bytes 196616 | tf_op jit(solution)/shard_map/ppermute | solution.py:349
  11.8 4.0 %collective-permute-start = (f32[64,128]{1,0:T(8,128)S(1)}, f32[64,128]{1,0:T(8,128)S(1)}, u32[]{:S(2)}, u32[]{:S(2)}) collective-permute-start(f32[64,128]{1,0:T(8,128)S(1)} %get-tuple-element.72.refs_0_), channel_id=1, source_target_pairs={{0,16},{16,0},{1,17},{17,1},{2,18},{18,2},{3,19},{19,3},{4,20},{20... | collective-permute-start | bytes 98312 | tf_op jit(solution)/shard_map/ppermute | solution.py:342
  16.6 4.7 %copy-start.2 = (f32[64,128]{1,0:T(8,128)}, f32[64,128]{1,0:T(8,128)S(1)}, u32[]{:S(2)}) copy-start(f32[64,128]{1,0:T(8,128)S(1)} %get-tuple-element.73.scale) | copy-start | bytes 98308
  16.6 21.7 %collective-permute-start.6 = (bf16[64,5120]{1,0:T(8,128)(2,1)S(1)}, bf16[64,5120]{1,0:T(8,128)(2,1)S(1)}, u32[]{:S(2)}, u32[]{:S(2)}) collective-permute-start(bf16[64,5120]{1,0:T(8,128)(2,1)S(1)} %feat_rows.1.refs_3_), channel_id=1, source_target_pairs={{0,1},{3,2},{4,5},{7,6},{8,9},{11,10},{12,13},{15,14},{16,17},{19,... | collective-permute-start | bytes 1966088 | tf_op jit(solution)/shard_map/ppermute | solution.py:420
  21.2 17.1 %collective-permute-start.4 = (bf16[64,4096]{1,0:T(8,128)(2,1)}, bf16[64,4096]{1,0:T(8,128)(2,1)S(1)}, u32[]{:S(2)}, u32[]{:S(2)}) collective-permute-start(bf16[64,4096]{1,0:T(8,128)(2,1)} %collective-permute-done.1.refs_1_.first), channel_id=1, source_target_pairs={{1,2},{2,3},{6,5},{5,4},{9,10},{10,11},{14,13},{13,12},{17,18},{18... | collective-permute-start | bytes 1572872 | tf_op jit(solution)/shard_map/ppermute | solution.py:374
  21.9 16.4 %collective-permute-start.5 = (bf16[64,4096]{1,0:T(8,128)(2,1)}, bf16[64,4096]{1,0:T(8,128)(2,1)}, u32[]{:S(2)}, u32[]{:S(2)}) collective-permute-start(bf16[64,4096]{1,0:T(8,128)(2,1)} %collective-permute-done.2.refs_2_.second), channel_id=1, source_target_pairs={{1,0},{2,1},{6,7},{5,6},{9,8},{10,9},{14,15},{13,14},{17,16},{18,1... | collective-permute-start | bytes 1572872 | tf_op jit(solution)/shard_map/ppermute | solution.py:374
  23.2 6.4 %collective-permute-start.7 = (bf16[9,64,128]{2,1,0:T(8,128)(2,1)}, bf16[9,64,128]{2,1,0:T(8,128)(2,1)}, u32[]{:S(2)}, u32[]{:S(2)}) collective-permute-start(bf16[9,64,128]{2,1,0:T(8,128)(2,1)} %get-tuple-element.76.refs_0_), channel_id=1, source_target_pairs={{0,16},{16,0},{1,17},{17,1},{2,18},{18,2},{3,19},{19,3},{4,20},{20... | collective-permute-start | bytes 442376 | tf_op jit(solution)/shard_map/ppermute | solution.py:342
  28.4 9.2 %collective-permute-start.8 = (bf16[64,576]{1,0:T(8,128)(2,1)S(1)}, bf16[64,576]{1,0:T(8,128)(2,1)S(1)}, u32[]{:S(2)}, u32[]{:S(2)}) collective-permute-start(bf16[64,576]{1,0:T(8,128)(2,1)S(1)} %get-tuple-element.86), channel_id=1, source_target_pairs={{1,0},{2,1},{3,2},{6,7},{5,6},{4,5},{9,8},{10,9},{11,10},{14,15},{... | collective-permute-start | bytes 221192 | tf_op jit(solution)/shard_map/ppermute | solution.py:374
  29.7 8.7 %collective-permute-start.9 = (bf16[64,576]{1,0:T(8,128)(2,1)S(1)}, bf16[64,576]{1,0:T(8,128)(2,1)S(1)}, u32[]{:S(2)}, u32[]{:S(2)}) collective-permute-start(bf16[64,576]{1,0:T(8,128)(2,1)S(1)} %get-tuple-element.87), channel_id=1, source_target_pairs={{0,1},{1,2},{2,3},{7,6},{6,5},{5,4},{8,9},{9,10},{10,11},{15,14},{... | collective-permute-start | bytes 221192 | tf_op jit(solution)/shard_map/ppermute | solution.py:374
  42.1 15.1 %copy-start.3 = (f32[64,128]{1,0:T(8,128)S(1)}, f32[64,128]{1,0:T(8,128)}, u32[]{:S(2)}) copy-start(f32[64,128]{1,0:T(8,128)} %copy-done.2) | copy-start | bytes 98308
  42.1 10.3 %collective-permute-start.10 = (bf16[64,576]{1,0:T(8,128)(2,1)S(1)}, bf16[64,576]{1,0:T(8,128)(2,1)S(1)}, u32[]{:S(2)}, u32[]{:S(2)}) collective-permute-start(bf16[64,576]{1,0:T(8,128)(2,1)S(1)} %get-tuple-element.95), channel_id=1, source_target_pairs={{0,2},{1,3},{2,0},{3,1},{7,5},{6,4},{5,7},{4,6},{8,10},{9,11},{10,... | collective-permute-start | bytes 221192 | tf_op jit(solution)/shard_map/ppermute | solution.py:374
  49.8 7.4 %collective-permute-start.11 = (bf16[64,576]{1,0:T(8,128)(2,1)S(1)}, bf16[64,576]{1,0:T(8,128)(2,1)S(1)}, u32[]{:S(2)}, u32[]{:S(2)}) collective-permute-start(bf16[64,576]{1,0:T(8,128)(2,1)S(1)} %end_grad.1), channel_id=1, source_target_pairs={{1,3},{2,0},{5,7},{6,4},{9,11},{10,8},{13,15},{14,12},{17,19},{18,... | collective-permute-start | bytes 221192 | tf_op jit(solution)/shard_map/ppermute | solution.py:473
  51.1 20.4 %collective-permute-start.19 = (bf16[64,4096]{1,0:T(8,128)(2,1)S(1)}, bf16[64,4096]{1,0:T(8,128)(2,1)S(1)}, u32[]{:S(2)}, u32[]{:S(2)}) collective-permute-start(bf16[64,4096]{1,0:T(8,128)(2,1)S(1)} %get-tuple-element.96.end_block), channel_id=1, source_target_pairs={{1,0},{2,3},{5,4},{6,7},{9,8},{10,11},{13,12},{14,15},{17,16},{18,... | collective-permute-start | bytes 1572872 | tf_op jit(solution)/shard_map/ppermute | solution.py:474
  58.3 5.4 %collective-permute-start.12 = (bf16[10,64,128]{2,1,0:T(8,128)(2,1)S(1)}, bf16[10,64,128]{2,1,0:T(8,128)(2,1)S(1)}, u32[]{:S(2)}, u32[]{:S(2)}) collective-permute-start(bf16[10,64,128]{2,1,0:T(8,128)(2,1)S(1)} %get-tuple-element.105), channel_id=1, source_target_pairs={{0,16},{16,0},{1,17},{17,1},{2,18},{18,2},{3,19},{19,3},{4,20},{20... | collective-permute-start | bytes 491528 | tf_op jit(solution)/shard_map/ppermute | solution.py:494
  58.8 6.3 %collective-permute-start.16 = (bf16[64,576]{1,0:T(8,128)(2,1)S(1)}, bf16[64,576]{1,0:T(8,128)(2,1)S(1)}, u32[]{:S(2)}, u32[]{:S(2)}) collective-permute-start(bf16[64,576]{1,0:T(8,128)(2,1)S(1)} %get-tuple-element.108), channel_id=1, source_target_pairs={{0,1},{1,2},{2,3},{3,0},{7,6},{6,5},{5,4},{4,7},{8,9},{9,10},{10,1... | collective-permute-start | bytes 221192 | tf_op jit(solution)/shard_map/ppermute | solution.py:374
  58.8 7.9 %collective-permute-start.17 = (bf16[64,576]{1,0:T(8,128)(2,1)S(1)}, bf16[64,576]{1,0:T(8,128)(2,1)S(1)}, u32[]{:S(2)}, u32[]{:S(2)}) collective-permute-start(bf16[64,576]{1,0:T(8,128)(2,1)S(1)} %get-tuple-element.109), channel_id=1, source_target_pairs={{0,2},{1,3},{2,0},{3,1},{7,5},{6,4},{5,7},{4,6},{8,10},{9,11},{10,... | collective-permute-start | bytes 221192 | tf_op jit(solution)/shard_map/ppermute | solution.py:374
  60.8 10.7 %collective-permute-start.18 = (bf16[64,576]{1,0:T(8,128)(2,1)S(1)}, bf16[64,576]{1,0:T(8,128)(2,1)S(1)}, u32[]{:S(2)}, u32[]{:S(2)}) collective-permute-start(bf16[64,576]{1,0:T(8,128)(2,1)S(1)} %get-tuple-element.110), channel_id=1, source_target_pairs={{0,3},{1,0},{2,1},{3,2},{7,4},{6,7},{5,6},{4,5},{8,11},{9,8},{10,9... | collective-permute-start | bytes 221192 | tf_op jit(solution)/shard_map/ppermute | solution.py:374
  63.9 12.8 %collective-permute-start.13 = (bf16[11,64,128]{2,1,0:T(8,128)(2,1)S(1)}, bf16[11,64,128]{2,1,0:T(8,128)(2,1)S(1)}, u32[]{:S(2)}, u32[]{:S(2)}) collective-permute-start(bf16[11,64,128]{2,1,0:T(8,128)(2,1)S(1)} %row_sum.1.refs_0_), channel_id=1, source_target_pairs={{0,4},{4,8},{8,12},{12,0},{1,5},{5,9},{9,13},{13,1},{2,6},{6,10},{... | collective-permute-start | bytes 540680 | tf_op jit(solution)/shard_map/ppermute | solution.py:342
  65.1 11.6 %collective-permute-start.14 = (bf16[11,64,128]{2,1,0:T(8,128)(2,1)S(1)}, bf16[11,64,128]{2,1,0:T(8,128)(2,1)S(1)}, u32[]{:S(2)}, u32[]{:S(2)}) collective-permute-start(bf16[11,64,128]{2,1,0:T(8,128)(2,1)S(1)} %row_sum.1.refs_0_), channel_id=1, source_target_pairs={{0,8},{4,12},{8,0},{12,4},{1,9},{5,13},{9,1},{13,5},{2,10},{6,14},... | collective-permute-start | bytes 540680 | tf_op jit(solution)/shard_map/ppermute | solution.py:342
  66.6 10.1 %collective-permute-start.15 = (bf16[11,64,128]{2,1,0:T(8,128)(2,1)S(1)}, bf16[11,64,128]{2,1,0:T(8,128)(2,1)S(1)}, u32[]{:S(2)}, u32[]{:S(2)}) collective-permute-start(bf16[11,64,128]{2,1,0:T(8,128)(2,1)S(1)} %row_sum.1.refs_0_), channel_id=1, source_target_pairs={{0,12},{4,0},{8,4},{12,8},{1,13},{5,1},{9,5},{13,9},{2,14},{6,2},{... | collective-permute-start | bytes 540680 | tf_op jit(solution)/shard_map/ppermute | solution.py:342
  76.7 8.6 %collective-permute-start.23 = (f32[64,512]{1,0:T(8,128)S(1)}, f32[64,512]{1,0:T(8,128)S(1)}, u32[]{:S(2)}, u32[]{:S(2)}) collective-permute-start(f32[64,512]{1,0:T(8,128)S(1)} %broadcast_select_fusion), channel_id=1, source_target_pairs={{0,16},{16,0},{1,17},{17,1},{2,18},{18,2},{3,19},{19,3},{4,20},{20... | collective-permute-start | bytes 393224 | tf_op jit(solution)/shard_map/ppermute | solution.py:349
  80.2 6.5 %collective-permute-start.20 = (f32[4,128]{1,0:T(4,128)S(1)}, f32[4,128]{1,0:T(4,128)S(1)}, u32[]{:S(2)}, u32[]{:S(2)}) collective-permute-start(f32[4,128]{1,0:T(4,128)S(1)} %get-tuple-element.130.refs_0_), channel_id=1, source_target_pairs={{0,1},{1,2},{2,3},{3,0},{4,5},{5,6},{6,7},{7,4},{8,9},{9,10},{10,1... | collective-permute-start | bytes 6152 | tf_op jit(solution)/shard_map/ppermute | solution.py:342
  80.2 6.5 %collective-permute-start.21 = (f32[4,128]{1,0:T(4,128)S(1)}, f32[4,128]{1,0:T(4,128)S(1)}, u32[]{:S(2)}, u32[]{:S(2)}) collective-permute-start(f32[4,128]{1,0:T(4,128)S(1)} %get-tuple-element.130.refs_0_), channel_id=1, source_target_pairs={{0,2},{1,3},{2,0},{3,1},{4,6},{5,7},{6,4},{7,5},{8,10},{9,11},{10,... | collective-permute-start | bytes 6152 | tf_op jit(solution)/shard_map/ppermute | solution.py:342
  84.3 3.6 %collective-permute-start.22 = (f32[4,128]{1,0:T(4,128)S(1)}, f32[4,128]{1,0:T(4,128)S(1)}, u32[]{:S(2)}, u32[]{:S(2)}) collective-permute-start(f32[4,128]{1,0:T(4,128)S(1)} %get-tuple-element.130.refs_0_), channel_id=1, source_target_pairs={{0,3},{1,0},{2,1},{3,2},{4,7},{5,4},{6,5},{7,6},{8,11},{9,8},{10,9... | collective-permute-start | bytes 6152 | tf_op jit(solution)/shard_map/ppermute | solution.py:342

commit v9 on v8

--- a/solution.py
+++ b/solution.py
@@ -13,6 +13,7 @@
 BF16 = jnp.bfloat16
 VMEM_LIMIT = 16 * 2**20
 COLLECT_FLOPS = 3 * 10**9
+INPUT_FLOPS = 2 * 10**9
 
 
 def params():
@@ -143,15 +144,18 @@
 
 
 def near_grad_kernel(height, width, *refs):
-    cotans, feat, outs, (wide, gathered, total) = refs[:3], refs[3], refs[4:7], refs[7:]
+    cotans, feat, mods, (own, behind, ahead), (wide, gathered, total) = refs[:3], refs[3], refs[4:6], refs[6:9], refs[9:]
     ch = feat.shape[0]
     for at, cotan in enumerate(cotans):
         gathered[at * ch : (at + 1) * ch] = cotan[...]
     for row in range(height + 2):
         spread(wide, row, feat[:, row * width : (row + 1) * width])
     (whole,) = tap_products(gathered, [wide], [total], height, width)
-    for at, out in enumerate(outs):
-        out[...] = whole[at * ch : (at + 1) * ch]
+    own[...] = whole[0:ch]
+    for at, (out, mod) in enumerate(zip((behind, ahead), mods)):
+        out[0:ch] = whole[(at + 1) * ch : (at + 2) * ch]
+        out[ch : 2 * ch] = mod[...]
+        out[2 * ch :] = mods[1 - at][...]
 
 
 def middle_grad_kernel(count, height, width, *refs):
@@ -164,21 +168,27 @@
     (out[...],) = tap_products(middle, [wide], [total], height, width)
 
 
-def end_grad_kernel(height, width, end_block, feat, out, wide, total):
+def end_grad_kernel(height, width, place, end_block, feat, ahead, behind, out, wide, total):
+    ch = feat.shape[0]
+    second = place[1] == jnp.where(place[3] > 0, 1, place[4] - 2)
+    out[ch:] = jnp.where(second, behind[2 * ch :], ahead[2 * ch :])
     for row in range(height + 2):
         spread(wide, row, feat[:, row * width : (row + 1) * width])
-    (out[...],) = tap_products(end_block, [wide], [total], height, width)
-
-
-def input_grad_kernel(size, height, width, place, cotan, first, second, middle, far, *refs):
-    mods, (main, before, after, gathered, taps_t, total) = refs[:size], refs[size:]
+    (out[0:ch],) = tap_products(end_block, [wide], [total], height, width)
+
+
+def input_grad_kernel(size, height, width, place, cotan, first, second, middle, far, own_mod, behind, ahead, end, *refs):
+    others, (main, before, after, gathered, taps_t, total) = refs[: size - 3], refs[size - 3 :]
     ch = main.shape[0]
     spot = jnp.where(place[3] > 0, place[1], size - 1 - place[1])
     gathered[0:ch] = cotan[...]
     gathered[ch : 2 * ch] = jnp.where(spot == 0, far[...], first[...])
     gathered[2 * ch : (size - 1) * ch] = middle[...]
     gathered[(size - 1) * ch :] = jnp.where(spot == size - 1, far[...], second[...])
-    every = jnp.concatenate([mod[...].astype(F32) for mod in mods], axis=0)
+    mods = [own_mod[...], jnp.where(spot == 0, end[ch:], behind[ch : 2 * ch])]
+    mods += [other[...] for other in others]
+    mods.append(jnp.where(spot == size - 1, end[ch:], ahead[ch : 2 * ch]))
+    every = jnp.concatenate([mod.astype(F32) for mod in mods], axis=0)
     taps_t[...] = every.T.astype(BF16)
     total[...] = jnp.zeros(total.shape, F32)
 
@@ -226,12 +236,12 @@
     chan_at, row_at, sign = place[1], place[2], place[3]
     ch = own.shape[0]
     by_chan[chan_at] = own[...].astype(F32)
-    by_chan[lax.rem(chan_at + sign + size, size)] = ahead[...].astype(F32)
-    by_chan[lax.rem(chan_at - sign + size, size)] = behind[...].astype(F32)
+    by_chan[lax.rem(chan_at + sign + size, size)] = ahead[0:ch].astype(F32)
+    by_chan[lax.rem(chan_at - sign + size, size)] = behind[0:ch].astype(F32)
     for d in range(2, size - 1):
         value = others[(d - 2) * ch : (d - 1) * ch].astype(F32)
         by_chan[lax.rem(chan_at + sign * d + size, size)] = value
-    by_chan[jnp.where(chan_at == 0, size - 1, 0)] += end[...].astype(F32)
+    by_chan[jnp.where(chan_at == 0, size - 1, 0)] += end[0:ch].astype(F32)
     in_ch = outs[0].shape[2]
     product = jnp.zeros(whole_mod.shape[1:], F32)
     for tap in range(TAPS):
@@ -361,7 +371,7 @@
     out_ch, in_ch = bank.shape[2:]
     pixels, all_ch = height * width, ch * size
     sign = 1 - 2 * jnp.remainder(sample_at, 2)
-    place = jnp.stack([sample_at, chan_at, row_at, sign]).astype(jnp.int32)
+    place = jnp.stack([sample_at, chan_at, row_at, sign, size]).astype(jnp.int32)
     flops = 2 * TAPS * ch * ch * size * pixels
 
     def along(x, pairs):
@@ -431,22 +441,24 @@
     first[0], second[0], energy, mod_own = lax.optimization_barrier((first[0], second[0], energy, mod_own))
 
     step(2, first[0], second[0])
-    own_grad, grad_behind, grad_ahead, wide = call(
+    triple, double = ((3 * ch, TAPS * ch), BF16), ((2 * ch, TAPS * ch), BF16)
+    own_grad, to_behind, to_ahead, wide = call(
         functools.partial(near_grad_kernel, height, width),
         "near_grad",
-        [message] * 3 + [((3 * ch, (height + 2) * width), BF16)],
+        [message, triple, triple, ((3 * ch, (height + 2) * width), BF16)],
         cotan,
         first[0],
         second[0],
         feat,
+        mods[size - 1],
+        mods[1],
         scratch=[((3 * ch, pixels), BF16), ((3, 3 * ch, 3 * ch), F32)],
         flops=flops * 3 // size,
     )
-    forth = [(i, i + 1) for i in range(size - 1)]
-    back = [(i + 1, i) for i in range(size - 1)]
-    from_ahead, from_behind = along(grad_behind, back), along(grad_ahead, forth)
-    first[1], second[1], feat_end, wide, mods, whole_mod, from_ahead, from_behind = lax.optimization_barrier(
-        (first[1], second[1], feat_end, wide, mods, whole_mod, from_ahead, from_behind)
+    from_ahead = along(to_behind, [(i + 1, i) for i in range(size - 1)])
+    from_behind = along(to_ahead, [(i, i + 1) for i in range(size - 1)])
+    first[1], second[1], feat_end, wide, whole_mod = lax.optimization_barrier(
+        (first[1], second[1], feat_end, wide, whole_mod)
     )
 
     count = size - 3
@@ -463,13 +475,18 @@
     (grad_end,) = call(
         functools.partial(end_grad_kernel, height, width),
         "end_grad",
-        [message],
+        [double],
+        place,
         end_block,
         feat_end,
+        from_ahead,
+        from_behind,
+        scalars=1,
         scratch=[((3 * ch, (height + 2) * width), BF16), ((3, ch, 3 * ch), F32)],
         flops=flops // size,
     )
     from_others = along(grad_others, [(i, (i + 2) % size) for i in range(size)])
+    from_others, grad_end = lax.optimization_barrier((from_others, grad_end))
     from_end = lax.ppermute(grad_end, "chan", [(1, size - 1), (size - 2, 0)])
     far = lax.ppermute(end_block, "chan", [(1, 0), (size - 2, size - 1)])
     parts = call(
@@ -489,7 +506,7 @@
         flops=COLLECT_FLOPS,
     )
     parts, mods = lax.optimization_barrier((parts, mods))
-    mods = [mods[0]] + [along(mods[d], [(i, (i + d) % size) for i in range(size)]) for d in range(1, size)]
+    others = [along(mods[d], [(i, (i + d) % size) for i in range(size)]) for d in range(2, size - 1)]
     parts = [parts[0]] + [
         lax.ppermute(parts[r], "rows", [(i, (i + r) % rows) for i in range(rows)])
         for r in range(1, rows)
@@ -498,7 +515,7 @@
     (own,) = call(row_sum_kernel, "row_sum", [((slots, out_ch, in_ch), BF16)], scale, small, *parts)
     every = exchange(own, "samples")
 
-    own, mods, far = lax.optimization_barrier((own, mods, far))
+    own, others, far = lax.optimization_barrier((own, others, far))
     main, before, after = call(
         functools.partial(input_grad_kernel, size, height, width),
         "input_grad",
@@ -509,14 +526,18 @@
         second[0],
         middle,
         far,
-        *mods,
+        mods[0],
+        from_behind,
+        from_ahead,
+        from_end,
+        *others,
         scalars=1,
         scratch=[
             ((all_ch, pixels), BF16),
             ((TAPS * ch, all_ch), BF16),
             ((height + 2, 3 * ch, width), F32),
         ],
-        flops=flops,
+        flops=INPUT_FLOPS,
     )
     every, main, before, after = lax.optimization_barrier((every, main, before, after))
     from_above, from_below = from_sides(before, after, "rows")

time: 89.9 us -> 93 us (1.034)
  starting transfers between devices: 46.6 us -> 36.9 us
  waiting for transfers between devices: 13 us -> 21 us
  local copies, waits for them, and re-layouts: 2.51 us -> 5.44 us
  other arithmetic: 1.25 us -> 2.68 us
    ppermute x10 -> x8, starting transfers between devices: 25.3 us -> 19.1 us  [along(): return lax.ppermute(x, ('samples', 'chan'), whole)]
    ppermute x8, waiting for transfers between devices: 4.5 us -> 10.1 us  [exchange(): lax.ppermute(x, axis, [(i, (i + s) % size) for i in range(size)])]
    ppermute x1, waiting for transfers between devices: 1.03 us -> 4.77 us  [on_device(): lax.ppermute(parts[r], 'rows', [(i, (i + r) % rows) for i in range(rows)])]
    ppermute x8, starting transfers between devices: 11.4 us -> 8.06 us  [exchange(): lax.ppermute(x, axis, [(i, (i + s) % size) for i in range(size)])]
    unnamed x19 -> x23, local copies, waits for them, and re-layouts: 2.16 us -> 5 us
    ppermute x10 -> x8, waiting for transfers between devices: 2.65 us -> 0.02 us  [along(): return lax.ppermute(x, ('samples', 'chan'), whole)]
  transfers between devices with their start and end apart: 24 -> 22, of which waited for: 7 -> 7; matrix products, arithmetic and copies ran while one was open for 3% -> 5% of each run, Pallas kernels for 22% -> 26%
where the time goes in v9:
time: 93 us; the launch traced here: 92.4 us
  starting transfers between devices  36.9 us (40%)
  Pallas kernels  25.4 us (27%)
  waiting for transfers between devices  21 us (23%)
  local copies, waits for them, and re-layouts  5.44 us (6%)
  other arithmetic  2.68 us (3%)
  between operations  0.98 us (1%)
    pallas_call x12, Pallas kernels, call(): pl.pallas_call(kernel, out_shape=outs, in_specs=sspec(scalars) + vspec(le...  25.4 us
    ppermute x8, starting transfers between devices, along(): return lax.ppermute(x, ('samples', 'chan'), whole)  19.1 us
    ppermute x8, waiting for transfers between devices, exchange(): lax.ppermute(x, axis, [(i, (i + s) % size) for i in range(size)])  10.1 us
    ppermute x8, starting transfers between devices, exchange(): lax.ppermute(x, axis, [(i, (i + s) % size) for i in range(size)])  8.06 us
    ppermute x1, waiting for transfers between devices, on_device(): from_end = lax.ppermute(grad_end, 'chan', [(1, size - 1), (size - 2, 0)])  5.62 us
    unnamed x23, local copies, waits for them, and re-layouts  5 us
    ppermute x1, waiting for transfers between devices, on_device(): lax.ppermute(parts[r], 'rows', [(i, (i + r) % rows) for i in range(rows)])  4.77 us
    ppermute x1, starting transfers between devices, on_device(): feat_end = lax.ppermute(feat, 'chan', [(0, 1), (size - 1, size - 2)])  4.41 us
  transfers between devices with their start and end apart: 22, of which 7 were waited for; matrix products, arithmetic and copies ran while one was open for 5% of the time, Pallas kernels for 26%

profile of v9, /device:TPU:0, one launch (start us, length us, event | category | flops | bytes accessed | tf_op | source)
XLA Modules:
  0.0 92.4 jit_solution(11310993134946568784)
XLA Ops:
  0.7 1.3 %copy.13 = bf16[8,8,8,512]{3,1,2,0:T(8,128)(2,1)S(1)} copy(bf16[8,8,8,512]{3,2,1,0:T(8,128)(2,1)} %bitcast.32) | data formatting | bytes 1048576
  2.0 5.0 %collective-permute-start.1 = (bf16[64,4096]{1,0:T(8,128)(2,1)S(1)}, bf16[64,4096]{1,0:T(8,128)(2,1)S(1)}, u32[]{:S(2)}, u32[]{:S(2)}) collective-permute-start(bf16[64,4096]{1,0:T(8,128)(2,1)S(1)} %bitcast.26), channel_id=1, source_target_pairs={{0,1},{1,2},{2,3},{7,6},{6,5},{5,4},{8,9},{9,10},{10,11},{15,14},{... | collective-permute-start | bytes 1572872 | tf_op jit(solution)/shard_map/ppermute | solution.py:384
  7.0 1.3 %collective-permute-start.2 = (bf16[64,4096]{1,0:T(8,128)(2,1)S(1)}, bf16[64,4096]{1,0:T(8,128)(2,1)}, u32[]{:S(2)}, u32[]{:S(2)}) collective-permute-start(bf16[64,4096]{1,0:T(8,128)(2,1)S(1)} %bitcast.27), channel_id=1, source_target_pairs={{1,0},{2,1},{3,2},{6,7},{5,6},{4,5},{9,8},{10,9},{11,10},{14,15},{... | collective-permute-start | bytes 1572872 | tf_op jit(solution)/shard_map/ppermute | solution.py:384
  8.3 1.2 %copy.14 = bf16[8,8,8,512]{3,1,2,0:T(8,128)(2,1)S(1)} copy(bf16[8,8,8,512]{3,2,1,0:T(8,128)(2,1)} %bitcast.33) | data formatting | bytes 1048576
  9.5 0.6 slice_select_fusion
  10.1 1.5 %collective-permute-start.3 = (bf16[64,512]{1,0:T(8,128)(2,1)}, bf16[64,512]{1,0:T(8,128)(2,1)}, u32[]{:S(2)}, u32[]{:S(2)}) collective-permute-start(bf16[64,512]{1,0:T(8,128)(2,1)} %slice_select_fusion), channel_id=1, source_target_pairs={{0,16},{16,0},{1,17},{17,1},{2,18},{18,2},{3,19},{19,3},{4,20},{20... | collective-permute-start | bytes 196616 | tf_op jit(solution)/shard_map/ppermute | solution.py:359
  11.7 0.9 %energy.1 = (f32[1,128]{1,0:T(1,128)S(1)}, f32[9,64,128]{2,1,0:T(8,128)S(1)}, f32[64,128]{1,0:T(8,128)S(1)}, f32[8,128]{1,0:T(8,128)S(1)}) custom-call(s32[1,4]{1,0:T(1,128)S(1)} %copy-done.5, f32[1,512]{1,0:T(1,128)S(1)} %copy-done.4, f32[1,128]{1,0:T(1,128)S(1)} %bitcast.30, f32[512,128]{1,0:T(8,128)S(1)} %copy-done.1, f32[4,9,64,128]{3,2,1,0:T(8,128)S(1)} %copy-done), custom_call_target="tpu_custom_call" | custom-call | flops 1000000 | bytes 1776656 | tf_op jit(solution)/shard_map/energy/pallas_call | solution.py:335
  12.6 0.6 collective-permute-start
  13.2 3.6 %collective-permute-done.refs_1_ = f32[64,128]{1,0:T(8,128)S(1)} collective-permute-done((f32[64,128]{1,0:T(8,128)S(1)}, f32[64,128]{1,0:T(8,128)S(1)}, u32[]{:S(2)}, u32[]{:S(2)}) %collective-permute-start) | collective-permute-done | bytes 32800 | tf_op jit(solution)/shard_map/ppermute | solution.py:352
  16.8 0.8 modulated.1
  17.5 0.0 collective-permute-done.3
  17.5 0.9 broadcast_select_fusion.1
  18.5 4.4 %collective-permute-start.6 = (bf16[64,5120]{1,0:T(8,128)(2,1)S(1)}, bf16[64,5120]{1,0:T(8,128)(2,1)S(1)}, u32[]{:S(2)}, u32[]{:S(2)}) collective-permute-start(bf16[64,5120]{1,0:T(8,128)(2,1)S(1)} %feat_rows.1.refs_3_), channel_id=1, source_target_pairs={{0,1},{3,2},{4,5},{7,6},{8,9},{11,10},{12,13},{15,14},{16,17},{19,... | collective-permute-start | bytes 1966088 | tf_op jit(solution)/shard_map/ppermute | solution.py:430
  22.9 0.0 copy-start.7
  22.9 0.8 copy-done.7
  23.7 0.7 collective-permute-start.4
  24.4 1.3 %collective-permute-start.5 = (bf16[64,4096]{1,0:T(8,128)(2,1)}, bf16[64,4096]{1,0:T(8,128)(2,1)}, u32[]{:S(2)}, u32[]{:S(2)}) collective-permute-start(bf16[64,4096]{1,0:T(8,128)(2,1)} %collective-permute-done.2.refs_2_.second), channel_id=1, source_target_pairs={{1,0},{2,1},{6,7},{5,6},{9,8},{10,9},{14,15},{13,14},{17,16},{18,1... | collective-permute-start | bytes 1572872 | tf_op jit(solution)/shard_map/ppermute | solution.py:384
  25.7 0.6 collective-permute-start.7
  26.3 0.1 stack.19.place
  26.4 4.8 %collective-permute-done.7.refs_1_ = bf16[9,64,128]{2,1,0:T(8,128)(2,1)} collective-permute-done((bf16[9,64,128]{2,1,0:T(8,128)(2,1)}, bf16[9,64,128]{2,1,0:T(8,128)(2,1)}, u32[]{:S(2)}, u32[]{:S(2)}) %collective-permute-start.7) | collective-permute-done | bytes 147488 | tf_op jit(solution)/shard_map/ppermute | solution.py:352
  31.2 1.2 %mod_blocks.1 = (bf16[9,64,256]{2,1,0:T(8,128)(2,1)S(1)}, bf16[64,576]{1,0:T(8,128)(2,1)S(1)}, bf16[64,576]{1,0:T(8,128)(2,1)S(1)}, bf16[64,576]{1,0:T(8,128)(2,1)S(1)}, bf16[64,576]{1,0:T(8,128)(2,1)S(1)}) custom-call(s32[5]{0:T(128)S(1)} %stack.19.place, bf16[9,64,128]{2,1,0:T(8,128)(2,1)} %get-tuple-element.67.refs_0_, ...), custom_call_target="tpu_custom_call" | custom-call | flops 1000000 | bytes 884756 | tf_op jit(solution)/shard_map/mod_blocks/pallas_call | solution.py:335
  32.4 0.0 copy-start.8
  32.4 1.0 %copy-done.8 = bf16[64,4096]{1,0:T(8,128)(2,1)S(1)} copy-done((bf16[64,4096]{1,0:T(8,128)(2,1)S(1)}, bf16[64,4096]{1,0:T(8,128)(2,1)}, u32[]{:S(2)}) %copy-start.8) | copy-done | bytes 524312
  33.5 4.4 %near_grad.1 = (bf16[64,576]{1,0:T(8,128)(2,1)S(1)}, bf16[192,576]{1,0:T(8,128)(2,1)S(1)}, bf16[192,576]{1,0:T(8,128)(2,1)S(1)}, bf16[192,5120]{1,0:T(8,128)(2,1)S(1)}) custom-call(bf16[64,4096]{1,0:T(8,128)(2,1)S(1)} %bitcast.28, bf16[64,4096]{1,0:T(8,128)(2,1)S(1)} %copy-done.8, bf16[64,4096]{1,0:T(8,128)(2,1)} %collective-permute-done.2.refs_2_.second, ...), custom_call_target="tpu_custom_call" | custom-call | flops 905969664 | bytes 4857856 | tf_op jit(solution)/shard_map/near_grad/pallas_call | solution.py:335
  37.8 1.3 %collective-permute-start.8 = (bf16[192,576]{1,0:T(8,128)(2,1)S(1)}, bf16[192,576]{1,0:T(8,128)(2,1)S(1)}, u32[]{:S(2)}, u32[]{:S(2)}) collective-permute-start(bf16[192,576]{1,0:T(8,128)(2,1)S(1)} %get-tuple-element.77), channel_id=1, source_target_pairs={{1,0},{2,1},{3,2},{6,7},{5,6},{4,5},{9,8},{10,9},{11,10},{14,15},{... | collective-permute-start | bytes 663560 | tf_op jit(solution)/shard_map/ppermute | solution.py:384
  39.1 5.3 %collective-permute-start.9 = (bf16[192,576]{1,0:T(8,128)(2,1)S(1)}, bf16[192,576]{1,0:T(8,128)(2,1)S(1)}, u32[]{:S(2)}, u32[]{:S(2)}) collective-permute-start(bf16[192,576]{1,0:T(8,128)(2,1)S(1)} %get-tuple-element.78), channel_id=1, source_target_pairs={{0,1},{1,2},{2,3},{7,6},{6,5},{5,4},{8,9},{9,10},{10,11},{15,14},{... | collective-permute-start | bytes 663560 | tf_op jit(solution)/shard_map/ppermute | solution.py:384
  44.5 0.0 collective-permute-done.4.refs_0_
  44.5 0.0 collective-permute-done.5.refs_1_
  44.5 3.7 %middle_grad.1 = (bf16[64,576]{1,0:T(8,128)(2,1)S(1)}, bf16[64,4096]{1,0:T(8,128)(2,1)S(1)}, bf16[64,4096]{1,0:T(8,128)(2,1)S(1)}) custom-call(bf16[64,4096]{1,0:T(8,128)(2,1)S(1)} %collective-permute-done.4.refs_0_, bf16[64,4096]{1,0:T(8,128)(2,1)} %collective-permute-done.5.refs_1_, bf16[192,5120]{1,0:T(8,128)(2,1)S(1)} %get-tuple-element.81.refs_2_), custom_call_target="tpu_custom_call" | custom-call | flops 301989888 | bytes 4136960 | tf_op jit(solution)/shard_map/middle_grad/pallas_call | solution.py:335
  48.2 0.0 copy-start.3
  48.3 4.3 %collective-permute-start.10 = (bf16[64,576]{1,0:T(8,128)(2,1)S(1)}, bf16[64,576]{1,0:T(8,128)(2,1)S(1)}, u32[]{:S(2)}, u32[]{:S(2)}) collective-permute-start(bf16[64,576]{1,0:T(8,128)(2,1)S(1)} %get-tuple-element.82), channel_id=1, source_target_pairs={{0,2},{1,3},{2,0},{3,1},{7,5},{6,4},{5,7},{4,6},{8,10},{9,11},{10,... | collective-permute-start | bytes 221192 | tf_op jit(solution)/shard_map/ppermute | solution.py:384
  52.6 0.0 collective-permute-done.8.ahead
  52.6 3.6 %end_grad.1 = bf16[128,576]{1,0:T(8,128)(2,1)S(1)} custom-call(s32[5]{0:T(128)S(1)} %stack.19.place, bf16[64,4096]{1,0:T(8,128)(2,1)S(1)} %get-tuple-element.83.end_block, bf16[64,5120]{1,0:T(8,128)(2,1)S(1)} %collective-permute-done.6.feat, bf16[192,576]{1,0:T(8,128)(2,1)S(1)} %collective-permute-done.8.ahead, ...), custom_call_target="tpu_custom_call" | custom-call | flops 301989888 | bytes 1769492 | tf_op jit(solution)/shard_map/end_grad/pallas_call | solution.py:335
  56.1 0.0 collective-permute-done.10.others
  56.2 1.3 %collective-permute-start.11 = (bf16[128,576]{1,0:T(8,128)(2,1)S(1)}, bf16[128,576]{1,0:T(8,128)(2,1)S(1)}, u32[]{:S(2)}, u32[]{:S(2)}) collective-permute-start(bf16[128,576]{1,0:T(8,128)(2,1)S(1)} %end_grad.1), channel_id=1, source_target_pairs={{1,3},{2,0},{5,7},{6,4},{9,11},{10,8},{13,15},{14,12},{17,19},{18,... | collective-permute-start | bytes 442376 | tf_op jit(solution)/shard_map/ppermute | solution.py:490
  57.5 1.3 %collective-permute-start.17 = (bf16[64,4096]{1,0:T(8,128)(2,1)S(1)}, bf16[64,4096]{1,0:T(8,128)(2,1)S(1)}, u32[]{:S(2)}, u32[]{:S(2)}) collective-permute-start(bf16[64,4096]{1,0:T(8,128)(2,1)S(1)} %get-tuple-element.83.end_block), channel_id=1, source_target_pairs={{1,0},{2,3},{5,4},{6,7},{9,8},{10,11},{13,12},{14,15},{17,16},{18,... | collective-permute-start | bytes 1572872 | tf_op jit(solution)/shard_map/ppermute | solution.py:491
  58.8 5.6 %collective-permute-done.11.end = bf16[128,576]{1,0:T(8,128)(2,1)S(1)} collective-permute-done((bf16[128,576]{1,0:T(8,128)(2,1)S(1)}, bf16[128,576]{1,0:T(8,128)(2,1)S(1)}, u32[]{:S(2)}, u32[]{:S(2)}) %collective-permute-start.11) | collective-permute-done | bytes 147488 | tf_op jit(solution)/shard_map/ppermute | solution.py:490
  64.4 1.1 %collect.1 = (bf16[10,64,128]{2,1,0:T(8,128)(2,1)S(1)}, bf16[10,64,128]{2,1,0:T(8,128)(2,1)S(1)}) custom-call(s32[5]{0:T(128)S(1)} %stack.19.place, f32[64,128]{1,0:T(8,128)S(1)} %copy-done.3, bf16[9,64,256]{2,1,0:T(8,128)(2,1)S(1)} %get-tuple-element.75.whole_mod, bf16[64,576]{1,0:T(8,128)(2,1)S(1)} %get-tuple-element.76.own, ...), custom_call_target="tpu_custom_call" | custom-call | flops 3000000000 | bytes 1392660 | tf_op jit(solution)/shard_map/collect/pallas_call | solution.py:335
  65.4 0.6 collective-permute-start.12
  66.1 4.8 %collective-permute-done.12.refs_1_ = bf16[10,64,128]{2,1,0:T(8,128)(2,1)S(1)} collective-permute-done((bf16[10,64,128]{2,1,0:T(8,128)(2,1)S(1)}, bf16[10,64,128]{2,1,0:T(8,128)(2,1)S(1)}, u32[]{:S(2)}, u32[]{:S(2)}) %collective-permute-start.12) | collective-permute-done | bytes 163872 | tf_op jit(solution)/shard_map/ppermute | solution.py:511
  70.8 0.2 row_sum.1.refs_0_
  71.0 0.1 collective-permute-start.13
  71.1 1.6 %collective-permute-start.14 = (bf16[11,64,128]{2,1,0:T(8,128)(2,1)S(1)}, bf16[11,64,128]{2,1,0:T(8,128)(2,1)S(1)}, u32[]{:S(2)}, u32[]{:S(2)}) collective-permute-start(bf16[11,64,128]{2,1,0:T(8,128)(2,1)S(1)} %row_sum.1.refs_0_), channel_id=1, source_target_pairs={{0,8},{4,12},{8,0},{12,4},{1,9},{5,13},{9,1},{13,5},{2,10},{6,14},... | collective-permute-start | bytes 540680 | tf_op jit(solution)/shard_map/ppermute | solution.py:352
  72.7 1.4 %collective-permute-start.15 = (bf16[11,64,128]{2,1,0:T(8,128)(2,1)S(1)}, bf16[11,64,128]{2,1,0:T(8,128)(2,1)S(1)}, u32[]{:S(2)}, u32[]{:S(2)}) collective-permute-start(bf16[11,64,128]{2,1,0:T(8,128)(2,1)S(1)} %row_sum.1.refs_0_), channel_id=1, source_target_pairs={{0,12},{4,0},{8,4},{12,8},{1,13},{5,1},{9,5},{13,9},{2,14},{6,2},{... | collective-permute-start | bytes 540680 | tf_op jit(solution)/shard_map/ppermute | solution.py:352
  74.1 0.0 collective-permute-done.16.refs_0_
  74.1 0.5 collective-permute-done.17.far
  74.6 5.0 %input_grad.1 = (f32[64,4096]{1,0:T(8,128)S(1)}, f32[64,512]{1,0:T(8,128)S(1)}, f32[64,512]{1,0:T(8,128)S(1)}) custom-call(s32[5]{0:T(128)S(1)} %stack.19.place, bf16[64,4096]{1,0:T(8,128)(2,1)S(1)} %bitcast.29, bf16[64,4096]{1,0:T(8,128)(2,1)S(1)} %copy-done.9, bf16[64,4096]{1,0:T(8,128)(2,1)} %collective-permute-done.2.refs_2_.second, ...), custom_call_target="tpu_custom_call" | custom-call | flops 2000000000 | bytes 4669460 | tf_op jit(solution)/shard_map/input_grad/pallas_call | solution.py:335
  79.6 0.0 collective-permute-done.13.refs_1_
  79.6 0.0 collective-permute-done.14.refs_2_
  79.6 1.2 %collective-permute-done.15.refs_3_ = bf16[11,64,128]{2,1,0:T(8,128)(2,1)S(1)} collective-permute-done((bf16[11,64,128]{2,1,0:T(8,128)(2,1)S(1)}, bf16[11,64,128]{2,1,0:T(8,128)(2,1)S(1)}, u32[]{:S(2)}, u32[]{:S(2)}) %collective-permute-start.15) | collective-permute-done | bytes 180256 | tf_op jit(solution)/shard_map/ppermute | solution.py:352
  80.9 0.6 collective-permute-start.21
  81.5 0.1 pad.1.clone
  81.5 2.8 %bank_grad.1 = (f32[4,9,64,128]{3,2,1,0:T(8,128)}, f32[4,128]{1,0:T(4,128)S(1)}, f32[4,512]{1,0:T(4,128)S(1)}) custom-call(s32[5]{0:T(128)S(1)} %stack.19.place, f32[4,9,64,128]{3,2,1,0:T(8,128)S(1)} %copy-done, bf16[11,64,128]{2,1,0:T(8,128)(2,1)S(1)} %row_sum.1.refs_0_, bf16[11,64,128]{2,1,0:T(8,128)(2,1)S(1)} %collective-permute-done.13.refs_1_, ...), custom_call_target="tpu_custom_call" | custom-call | flops 1000000 | bytes 3090452 | tf_op jit(solution)/shard_map/bank_grad/pallas_call | solution.py:335
  84.4 0.0 collective-permute-start.18
  84.4 2.8 %collective-permute-start.19 = (f32[4,128]{1,0:T(4,128)S(1)}, f32[4,128]{1,0:T(4,128)S(1)}, u32[]{:S(2)}, u32[]{:S(2)}) collective-permute-start(f32[4,128]{1,0:T(4,128)S(1)} %get-tuple-element.112.refs_0_), channel_id=1, source_target_pairs={{0,2},{1,3},{2,0},{3,1},{4,6},{5,7},{6,4},{7,5},{8,10},{9,11},{10,... | collective-permute-start | bytes 6152 | tf_op jit(solution)/shard_map/ppermute | solution.py:352
  87.1 1.0 %collective-permute-start.20 = (f32[4,128]{1,0:T(4,128)S(1)}, f32[4,128]{1,0:T(4,128)S(1)}, u32[]{:S(2)}, u32[]{:S(2)}) collective-permute-start(f32[4,128]{1,0:T(4,128)S(1)} %get-tuple-element.112.refs_0_), channel_id=1, source_target_pairs={{0,3},{1,0},{2,1},{3,2},{4,7},{5,4},{6,5},{7,6},{8,11},{9,8},{10,9... | collective-permute-start | bytes 6152 | tf_op jit(solution)/shard_map/ppermute | solution.py:352
  88.2 0.6 copy.15
  88.8 0.0 collective-permute-done.21
  88.8 0.1 copy.12
  89.0 0.1 copy.11
  89.1 1.1 %fusion = bf16[1,64,8,512]{3,2,1,0:T(8,128)(2,1)} fusion(f32[1,64,1,512]{3,2,1,0:T(1,128)S(1)} %copy.12, f32[1,64,1,512]{3,2,1,0:T(1,128)S(1)} %copy.11, f32[8]{0:T(128)S(1)} %pad.1.clone, f32[1,64,8,512]{3,2,1,0:T(8,128)S(1)} %bitcast.31), kind=kLoop, calls=%fused_computation.1 | loop fusion | flops 1048576 | bytes 1835040 | tf_op jit(solution)/shard_map/convert_element_type | solution.py:558
  90.3 0.0 collective-permute-done.18.refs_1_
  90.3 0.5 collective-permute-done.20.refs_3_
  90.7 1.7 %affine.1 = (f32[512,128]{1,0:T(8,128)}, f32[1,128]{1,0:T(1,128)}) custom-call(s32[5]{0:T(128)S(1)} %stack.19.place, f32[4,512]{1,0:T(4,128)S(1)} %get-tuple-element.111.latents, f32[4,128]{1,0:T(4,128)S(1)} %get-tuple-element.112.refs_0_, f32[4,128]{1,0:T(4,128)S(1)} %collective-permute-done.18.refs_1_, f32[4,128]{1,0:T(4,128)S(1)} %collective-permute-done.19.refs_2_, ...), custom_call_target="tpu_custom_call" | custom-call | flops 1000000 | bytes 279060 | tf_op jit(solution)/shard_map/affine/pallas_call | solution.py:335
  (25 shorter events, 0.1 us)
Async XLA Ops:
  0.6 11.0 %copy-start = (f32[4,9,64,128]{3,2,1,0:T(8,128)S(1)}, f32[4,9,64,128]{3,2,1,0:T(8,128)}, u32[]{:S(2)}) copy-start(f32[4,9,64,128]{3,2,1,0:T(8,128)} %bank.1) | copy-start | bytes 3538948
  0.6 11.0 %copy-start.5 = (s32[1,4]{1,0:T(1,128)S(1)}, s32[1,4]{1,0:T(1,128)}, u32[]{:S(2)}) copy-start(s32[1,4]{1,0:T(1,128)} %refs_0_.1) | copy-start | bytes 52
  0.7 11.0 %copy-start.4 = (f32[1,512]{1,0:T(1,128)S(1)}, f32[1,512]{1,0:T(1,128)}, u32[]{:S(2)}) copy-start(f32[1,512]{1,0:T(1,128)} %refs_1_.1) | copy-start | bytes 6148
  0.7 11.0 %copy-start.6 = (f32[128]{0:T(128)S(1)}, f32[128]{0:T(128)}, u32[]{:S(2)}) copy-start(f32[128]{0:T(128)} %param.13) | copy-start | bytes 1540
  0.7 11.0 %copy-start.1 = (f32[512,128]{1,0:T(8,128)S(1)}, f32[512,128]{1,0:T(8,128)}, u32[]{:S(2)}) copy-start(f32[512,128]{1,0:T(8,128)} %refs_3_.1) | copy-start | bytes 786436
  2.0 20.9 %collective-permute-start.1 = (bf16[64,4096]{1,0:T(8,128)(2,1)S(1)}, bf16[64,4096]{1,0:T(8,128)(2,1)S(1)}, u32[]{:S(2)}, u32[]{:S(2)}) collective-permute-start(bf16[64,4096]{1,0:T(8,128)(2,1)S(1)} %bitcast.26), channel_id=1, source_target_pairs={{0,1},{1,2},{2,3},{7,6},{6,5},{5,4},{8,9},{9,10},{10,11},{15,14},{... | collective-permute-start | bytes 1572872 | tf_op jit(solution)/shard_map/ppermute | solution.py:384
  7.0 16.7 %collective-permute-start.2 = (bf16[64,4096]{1,0:T(8,128)(2,1)S(1)}, bf16[64,4096]{1,0:T(8,128)(2,1)}, u32[]{:S(2)}, u32[]{:S(2)}) collective-permute-start(bf16[64,4096]{1,0:T(8,128)(2,1)S(1)} %bitcast.27), channel_id=1, source_target_pairs={{1,0},{2,1},{3,2},{6,7},{5,6},{4,5},{9,8},{10,9},{11,10},{14,15},{... | collective-permute-start | bytes 1572872 | tf_op jit(solution)/shard_map/ppermute | solution.py:384
  10.1 7.4 %collective-permute-start.3 = (bf16[64,512]{1,0:T(8,128)(2,1)}, bf16[64,512]{1,0:T(8,128)(2,1)}, u32[]{:S(2)}, u32[]{:S(2)}) collective-permute-start(bf16[64,512]{1,0:T(8,128)(2,1)} %slice_select_fusion), channel_id=1, source_target_pairs={{0,16},{16,0},{1,17},{17,1},{2,18},{18,2},{3,19},{19,3},{4,20},{20... | collective-permute-start | bytes 196616 | tf_op jit(solution)/shard_map/ppermute | solution.py:359
  12.6 4.2 %collective-permute-start = (f32[64,128]{1,0:T(8,128)S(1)}, f32[64,128]{1,0:T(8,128)S(1)}, u32[]{:S(2)}, u32[]{:S(2)}) collective-permute-start(f32[64,128]{1,0:T(8,128)S(1)} %get-tuple-element.63.refs_0_), channel_id=1, source_target_pairs={{0,16},{16,0},{1,17},{17,1},{2,18},{18,2},{3,19},{19,3},{4,20},{20... | collective-permute-start | bytes 98312 | tf_op jit(solution)/shard_map/ppermute | solution.py:352
  17.5 6.2 %copy-start.2 = (f32[64,128]{1,0:T(8,128)}, f32[64,128]{1,0:T(8,128)S(1)}, u32[]{:S(2)}) copy-start(f32[64,128]{1,0:T(8,128)S(1)} %get-tuple-element.64.scale) | copy-start | bytes 98308
  18.5 26.0 %collective-permute-start.6 = (bf16[64,5120]{1,0:T(8,128)(2,1)S(1)}, bf16[64,5120]{1,0:T(8,128)(2,1)S(1)}, u32[]{:S(2)}, u32[]{:S(2)}) collective-permute-start(bf16[64,5120]{1,0:T(8,128)(2,1)S(1)} %feat_rows.1.refs_3_), channel_id=1, source_target_pairs={{0,1},{3,2},{4,5},{7,6},{8,9},{11,10},{12,13},{15,14},{16,17},{19,... | collective-permute-start | bytes 1966088 | tf_op jit(solution)/shard_map/ppermute | solution.py:430
  22.9 0.8 copy-start.7
  23.7 20.8 %collective-permute-start.4 = (bf16[64,4096]{1,0:T(8,128)(2,1)}, bf16[64,4096]{1,0:T(8,128)(2,1)S(1)}, u32[]{:S(2)}, u32[]{:S(2)}) collective-permute-start(bf16[64,4096]{1,0:T(8,128)(2,1)} %copy-done.7), channel_id=1, source_target_pairs={{1,2},{2,3},{6,5},{5,4},{9,10},{10,11},{14,13},{13,12},{17,18},{18... | collective-permute-start | bytes 1572872 | tf_op jit(solution)/shard_map/ppermute | solution.py:384
  24.4 20.1 %collective-permute-start.5 = (bf16[64,4096]{1,0:T(8,128)(2,1)}, bf16[64,4096]{1,0:T(8,128)(2,1)}, u32[]{:S(2)}, u32[]{:S(2)}) collective-permute-start(bf16[64,4096]{1,0:T(8,128)(2,1)} %collective-permute-done.2.refs_2_.second), channel_id=1, source_target_pairs={{1,0},{2,1},{6,7},{5,6},{9,8},{10,9},{14,15},{13,14},{17,16},{18,1... | collective-permute-start | bytes 1572872 | tf_op jit(solution)/shard_map/ppermute | solution.py:384
  25.7 5.5 %collective-permute-start.7 = (bf16[9,64,128]{2,1,0:T(8,128)(2,1)}, bf16[9,64,128]{2,1,0:T(8,128)(2,1)}, u32[]{:S(2)}, u32[]{:S(2)}) collective-permute-start(bf16[9,64,128]{2,1,0:T(8,128)(2,1)} %get-tuple-element.67.refs_0_), channel_id=1, source_target_pairs={{0,16},{16,0},{1,17},{17,1},{2,18},{18,2},{3,19},{19,3},{4,20},{20... | collective-permute-start | bytes 442376 | tf_op jit(solution)/shard_map/ppermute | solution.py:352
  32.4 1.0 %copy-start.8 = (bf16[64,4096]{1,0:T(8,128)(2,1)S(1)}, bf16[64,4096]{1,0:T(8,128)(2,1)}, u32[]{:S(2)}) copy-start(bf16[64,4096]{1,0:T(8,128)(2,1)} %copy-done.7) | copy-start | bytes 1572868
  37.8 14.7 %collective-permute-start.8 = (bf16[192,576]{1,0:T(8,128)(2,1)S(1)}, bf16[192,576]{1,0:T(8,128)(2,1)S(1)}, u32[]{:S(2)}, u32[]{:S(2)}) collective-permute-start(bf16[192,576]{1,0:T(8,128)(2,1)S(1)} %get-tuple-element.77), channel_id=1, source_target_pairs={{1,0},{2,1},{3,2},{6,7},{5,6},{4,5},{9,8},{10,9},{11,10},{14,15},{... | collective-permute-start | bytes 663560 | tf_op jit(solution)/shard_map/ppermute | solution.py:384
  39.1 13.4 %collective-permute-start.9 = (bf16[192,576]{1,0:T(8,128)(2,1)S(1)}, bf16[192,576]{1,0:T(8,128)(2,1)S(1)}, u32[]{:S(2)}, u32[]{:S(2)}) collective-permute-start(bf16[192,576]{1,0:T(8,128)(2,1)S(1)} %get-tuple-element.78), channel_id=1, source_target_pairs={{0,1},{1,2},{2,3},{7,6},{6,5},{5,4},{8,9},{9,10},{10,11},{15,14},{... | collective-permute-start | bytes 663560 | tf_op jit(solution)/shard_map/ppermute | solution.py:384
  48.2 16.1 %copy-start.3 = (f32[64,128]{1,0:T(8,128)S(1)}, f32[64,128]{1,0:T(8,128)}, u32[]{:S(2)}) copy-start(f32[64,128]{1,0:T(8,128)} %copy-done.2) | copy-start | bytes 98308
  48.3 7.9 %collective-permute-start.10 = (bf16[64,576]{1,0:T(8,128)(2,1)S(1)}, bf16[64,576]{1,0:T(8,128)(2,1)S(1)}, u32[]{:S(2)}, u32[]{:S(2)}) collective-permute-start(bf16[64,576]{1,0:T(8,128)(2,1)S(1)} %get-tuple-element.82), channel_id=1, source_target_pairs={{0,2},{1,3},{2,0},{3,1},{7,5},{6,4},{5,7},{4,6},{8,10},{9,11},{10,... | collective-permute-start | bytes 221192 | tf_op jit(solution)/shard_map/ppermute | solution.py:384
  56.2 8.2 %collective-permute-start.11 = (bf16[128,576]{1,0:T(8,128)(2,1)S(1)}, bf16[128,576]{1,0:T(8,128)(2,1)S(1)}, u32[]{:S(2)}, u32[]{:S(2)}) collective-permute-start(bf16[128,576]{1,0:T(8,128)(2,1)S(1)} %end_grad.1), channel_id=1, source_target_pairs={{1,3},{2,0},{5,7},{6,4},{9,11},{10,8},{13,15},{14,12},{17,19},{18,... | collective-permute-start | bytes 442376 | tf_op jit(solution)/shard_map/ppermute | solution.py:490
  57.5 17.2 %collective-permute-start.17 = (bf16[64,4096]{1,0:T(8,128)(2,1)S(1)}, bf16[64,4096]{1,0:T(8,128)(2,1)S(1)}, u32[]{:S(2)}, u32[]{:S(2)}) collective-permute-start(bf16[64,4096]{1,0:T(8,128)(2,1)S(1)} %get-tuple-element.83.end_block), channel_id=1, source_target_pairs={{1,0},{2,3},{5,4},{6,7},{9,8},{10,11},{13,12},{14,15},{17,16},{18,... | collective-permute-start | bytes 1572872 | tf_op jit(solution)/shard_map/ppermute | solution.py:491
  64.4 10.2 %copy-start.9 = (bf16[64,4096]{1,0:T(8,128)(2,1)S(1)}, bf16[64,4096]{1,0:T(8,128)(2,1)}, u32[]{:S(2)}) copy-start(bf16[64,4096]{1,0:T(8,128)(2,1)} %copy-done.7) | copy-start | bytes 1572868
  65.4 5.4 %collective-permute-start.12 = (bf16[10,64,128]{2,1,0:T(8,128)(2,1)S(1)}, bf16[10,64,128]{2,1,0:T(8,128)(2,1)S(1)}, u32[]{:S(2)}, u32[]{:S(2)}) collective-permute-start(bf16[10,64,128]{2,1,0:T(8,128)(2,1)S(1)} %get-tuple-element.92), channel_id=1, source_target_pairs={{0,16},{16,0},{1,17},{17,1},{2,18},{18,2},{3,19},{19,3},{4,20},{20... | collective-permute-start | bytes 491528 | tf_op jit(solution)/shard_map/ppermute | solution.py:511
  66.0 8.0 %collective-permute-start.16 = (bf16[64,576]{1,0:T(8,128)(2,1)S(1)}, bf16[64,576]{1,0:T(8,128)(2,1)S(1)}, u32[]{:S(2)}, u32[]{:S(2)}) collective-permute-start(bf16[64,576]{1,0:T(8,128)(2,1)S(1)} %get-tuple-element.94), channel_id=1, source_target_pairs={{0,2},{1,3},{2,0},{3,1},{7,5},{6,4},{5,7},{4,6},{8,10},{9,11},{10,... | collective-permute-start | bytes 221192 | tf_op jit(solution)/shard_map/ppermute | solution.py:384
  71.0 8.6 %collective-permute-start.13 = (bf16[11,64,128]{2,1,0:T(8,128)(2,1)S(1)}, bf16[11,64,128]{2,1,0:T(8,128)(2,1)S(1)}, u32[]{:S(2)}, u32[]{:S(2)}) collective-permute-start(bf16[11,64,128]{2,1,0:T(8,128)(2,1)S(1)} %row_sum.1.refs_0_), channel_id=1, source_target_pairs={{0,4},{4,8},{8,12},{12,0},{1,5},{5,9},{9,13},{13,1},{2,6},{6,10},{... | collective-permute-start | bytes 540680 | tf_op jit(solution)/shard_map/ppermute | solution.py:352
  71.1 8.5 %collective-permute-start.14 = (bf16[11,64,128]{2,1,0:T(8,128)(2,1)S(1)}, bf16[11,64,128]{2,1,0:T(8,128)(2,1)S(1)}, u32[]{:S(2)}, u32[]{:S(2)}) collective-permute-start(bf16[11,64,128]{2,1,0:T(8,128)(2,1)S(1)} %row_sum.1.refs_0_), channel_id=1, source_target_pairs={{0,8},{4,12},{8,0},{12,4},{1,9},{5,13},{9,1},{13,5},{2,10},{6,14},... | collective-permute-start | bytes 540680 | tf_op jit(solution)/shard_map/ppermute | solution.py:352
  72.7 8.2 %collective-permute-start.15 = (bf16[11,64,128]{2,1,0:T(8,128)(2,1)S(1)}, bf16[11,64,128]{2,1,0:T(8,128)(2,1)S(1)}, u32[]{:S(2)}, u32[]{:S(2)}) collective-permute-start(bf16[11,64,128]{2,1,0:T(8,128)(2,1)S(1)} %row_sum.1.refs_0_), channel_id=1, source_target_pairs={{0,12},{4,0},{8,4},{12,8},{1,13},{5,1},{9,5},{13,9},{2,14},{6,2},{... | collective-permute-start | bytes 540680 | tf_op jit(solution)/shard_map/ppermute | solution.py:352
  80.9 7.9 %collective-permute-start.21 = (f32[64,512]{1,0:T(8,128)S(1)}, f32[64,512]{1,0:T(8,128)S(1)}, u32[]{:S(2)}, u32[]{:S(2)}) collective-permute-start(f32[64,512]{1,0:T(8,128)S(1)} %broadcast_select_fusion), channel_id=1, source_target_pairs={{0,16},{16,0},{1,17},{17,1},{2,18},{18,2},{3,19},{19,3},{4,20},{20... | collective-permute-start | bytes 393224 | tf_op jit(solution)/shard_map/ppermute | solution.py:359
  84.4 5.9 %collective-permute-start.18 = (f32[4,128]{1,0:T(4,128)S(1)}, f32[4,128]{1,0:T(4,128)S(1)}, u32[]{:S(2)}, u32[]{:S(2)}) collective-permute-start(f32[4,128]{1,0:T(4,128)S(1)} %get-tuple-element.112.refs_0_), channel_id=1, source_target_pairs={{0,1},{1,2},{2,3},{3,0},{4,5},{5,6},{6,7},{7,4},{8,9},{9,10},{10,1... | collective-permute-start | bytes 6152 | tf_op jit(solution)/shard_map/ppermute | solution.py:352
  84.4 5.9 %collective-permute-start.19 = (f32[4,128]{1,0:T(4,128)S(1)}, f32[4,128]{1,0:T(4,128)S(1)}, u32[]{:S(2)}, u32[]{:S(2)}) collective-permute-start(f32[4,128]{1,0:T(4,128)S(1)} %get-tuple-element.112.refs_0_), channel_id=1, source_target_pairs={{0,2},{1,3},{2,0},{3,1},{4,6},{5,7},{6,4},{7,5},{8,10},{9,11},{10,... | collective-permute-start | bytes 6152 | tf_op jit(solution)/shard_map/ppermute | solution.py:352
  87.1 3.6 %collective-permute-start.20 = (f32[4,128]{1,0:T(4,128)S(1)}, f32[4,128]{1,0:T(4,128)S(1)}, u32[]{:S(2)}, u32[]{:S(2)}) collective-permute-start(f32[4,128]{1,0:T(4,128)S(1)} %get-tuple-element.112.refs_0_), channel_id=1, source_target_pairs={{0,3},{1,0},{2,1},{3,2},{4,7},{5,4},{6,5},{7,6},{8,11},{9,8},{10,9... | collective-permute-start | bytes 6152 | tf_op jit(solution)/shard_map/ppermute | solution.py:352

commit v10 on v9

--- a/solution.py
+++ b/solution.py
@@ -43,8 +43,8 @@
     return total
 
 
-def energy_kernel(*refs):
-    given, (style_out, kernel_out, energy_out, small), held, sems = refs[:5], refs[5:9], refs[9:14], refs[14]
+def plain_kernel(*refs):
+    given, (plain_out, small), held, sems = refs[:5], refs[5:7], refs[7:12], refs[12]
     copies = [pltpu.make_async_copy(x, y, sems.at[n]) for n, (x, y) in enumerate(zip(given, held))]
     for copy in copies:
         copy.start()
@@ -55,16 +55,14 @@
         jnp.dot(latent[...], affine_w[...], precision=lax.Precision.HIGHEST, preferred_element_type=F32)
         + affine_b[...]
     )
-    style_out[...] = style
     filters, in_ch = bank.shape[0], bank.shape[3]
     weights = [select[0, k].astype(F32) for k in range(filters)]
     total = jnp.zeros(bank.shape[2:], F32)
     for tap in range(TAPS):
-        kernel = mixed(bank, weights, tap)
-        kernel_out[tap] = kernel
-        plain = kernel * style
+        plain = mixed(bank, weights, tap) * style
+        plain_out[tap] = plain
         total = total + plain * plain
-    energy_out[...] = jnp.broadcast_to(jnp.sum(total, axis=1, keepdims=True), energy_out.shape)
+    plain_out[TAPS] = jnp.broadcast_to(jnp.sum(total, axis=1, keepdims=True), total.shape)
     small[...] = jnp.zeros(small.shape, F32)
     last = latent.shape[1] // in_ch
     for n in range(last):
@@ -77,27 +75,20 @@
     small[last + 1 : last + 2] = row
 
 
-def modulated_kernel(kernel, style, *refs):
-    energies, (mod_out, scale_out) = refs[:-2], refs[-2:]
-    energy = energies[0][...]
-    for other in energies[1:]:
-        energy = energy + other[...]
-    scales = lax.rsqrt(energy + EPS)
-    scale_out[...] = scales
-    scale = scales[:, 0:1]
-    for tap in range(TAPS):
-        mod_out[tap] = (kernel[tap] * style[...] * scale).astype(BF16)
-
-
 def blocks_kernel(rows, size, place, *refs):
-    parts, whole, outs, (by_row, by_chan) = refs[:rows], refs[rows], refs[rows + 1 : rows + 1 + size], refs[-2:]
+    parts, (whole, scale_out), outs, (by_row, by_chan) = refs[:rows], refs[rows : rows + 2], refs[rows + 2 : -2], refs[-2:]
     row_at, chan_at, sign = place[2], place[1], place[3]
+    energy = parts[0][TAPS]
+    for part in parts[1:]:
+        energy = energy + part[TAPS]
+    scale = lax.rsqrt(energy[:, 0:1] + EPS)
+    scale_out[...] = jnp.broadcast_to(scale, scale_out.shape)
     for r in range(rows):
-        by_row[lax.rem(row_at - r + rows, rows)] = parts[r][...]
+        by_row[lax.rem(row_at - r + rows, rows)] = parts[r][0:TAPS]
     ch = whole.shape[2] // size
     taps = []
     for tap in range(TAPS):
-        value = beside([by_row[r, tap].astype(F32) for r in range(rows)])
+        value = beside([by_row[r, tap] for r in range(rows)]) * scale
         whole[tap] = value.astype(BF16)
         taps.append(value)
     for z in range(size):
@@ -392,13 +383,11 @@
 
     step(1, cotan, cotan)
 
-    feat = feature[0].reshape(ch, pixels)
-    feat_before, feat_after = from_sides(feat[:, :width], feat[:, pixels - width :], "rows")
     small_rows = -(-(latent.shape[1] // in_ch + 2) // 8) * 8
-    style, kernel, energy, small = call(
-        energy_kernel,
-        "energy",
-        [((1, in_ch), F32), ((TAPS, out_ch, in_ch), F32), ((out_ch, 128), F32), ((small_rows, in_ch), F32)],
+    plain, small = call(
+        plain_kernel,
+        "plain",
+        [((TAPS + 1, out_ch, in_ch), F32), ((small_rows, in_ch), F32)],
         select,
         latent,
         affine_b[None],
@@ -414,31 +403,27 @@
             pltpu.SemaphoreType.DMA((5,)),
         ],
     )
+    plains = exchange(plain, "rows")
+    feature, plain = lax.optimization_barrier((feature, plain))
+    feat = feature[0].reshape(ch, pixels)
+    feat_before, feat_after = from_sides(feat[:, :width], feat[:, pixels - width :], "rows")
     extended = ((ch, (height + 2) * width), BF16)
     (feat,) = call(
         functools.partial(rows_kernel, height, width), "feat_rows", [extended], feat, feat_before, feat_after
     )
-    mod_own, scale = call(
-        modulated_kernel,
-        "modulated",
-        [((TAPS, out_ch, in_ch), BF16), ((out_ch, 128), F32)],
-        kernel,
-        style,
-        *exchange(energy, "rows"),
-    )
-    feat, mod_own = lax.optimization_barrier((feat, mod_own))
+    feat, plains = lax.optimization_barrier((feat, plains))
     feat_end = lax.ppermute(feat, "chan", [(0, 1), (size - 1, size - 2)])
     message = ((ch, TAPS * ch), BF16)
-    whole_mod, *mods = call(
+    whole_mod, scale, *mods = call(
         functools.partial(blocks_kernel, rows, size),
         "mod_blocks",
-        [((TAPS, out_ch, all_ch), BF16)] + [message] * size,
+        [((TAPS, out_ch, all_ch), BF16), ((out_ch, 128), F32)] + [message] * size,
         place,
-        *exchange(mod_own, "rows"),
+        *plains,
         scalars=1,
-        scratch=[((rows, TAPS, out_ch, in_ch), BF16), ((size, *message[0]), BF16)],
-    )
-    first[0], second[0], energy, mod_own = lax.optimization_barrier((first[0], second[0], energy, mod_own))
+        scratch=[((rows, TAPS, out_ch, in_ch), F32), ((size, *message[0]), BF16)],
+    )
+    first[0], second[0], plains = lax.optimization_barrier((first[0], second[0], plains))
 
     step(2, first[0], second[0])
     triple, double = ((3 * ch, TAPS * ch), BF16), ((2 * ch, TAPS * ch), BF16)

time: 93 us -> 91.4 us (0.983)
  Pallas kernels: 25.4 us -> 23.6 us
  other arithmetic: 2.68 us -> 1.17 us
    ppermute x8 -> x7, waiting for transfers between devices: 10.1 us -> 0.86 us  [exchange(): lax.ppermute(x, axis, [(i, (i + s) % size) for i in range(size)])]
    ppermute x2, waiting for transfers between devices: 0.01 us -> 8.93 us  [from_sides(): got = lax.ppermute(jnp.where(at == 0, last, first), axis, [(0, 1), (1, 0)])]
    ppermute x1, waiting for transfers between devices: 0.54 us -> 2.63 us  [on_device(): far = lax.ppermute(end_block, 'chan', [(1, 0), (size - 2, size - 1)])]
    pallas_call x12 -> x11, Pallas kernels: 25.4 us -> 23.6 us  [call(): pl.pallas_call(kernel, out_shape=outs, in_specs=sspec(scalars) + vspec(le...]
    ppermute x1, starting transfers between devices: 4.41 us -> 2.89 us  [on_device(): feat_end = lax.ppermute(feat, 'chan', [(0, 1), (size - 1, size - 2)])]
    ppermute x1, starting transfers between devices: 0.61 us -> 1.56 us  [on_device(): lax.ppermute(parts[r], 'rows', [(i, (i + r) % rows) for i in range(rows)])]
    ppermute x1, waiting for transfers between devices: 4.77 us -> 3.82 us  [on_device(): lax.ppermute(parts[r], 'rows', [(i, (i + r) % rows) for i in range(rows)])]
    ppermute x8 -> x7, starting transfers between devices: 8.06 us -> 8.43 us  [exchange(): lax.ppermute(x, axis, [(i, (i + s) % size) for i in range(size)])]
  transfers between devices with their start and end apart: 22 -> 21, of which waited for: 7 -> 5; matrix products, arithmetic and copies ran while one was open for 5% -> 3% of each run, Pallas kernels for 26% -> 24%
where the time goes in v10:
time: 91.4 us; the launch traced here: 91 us
  starting transfers between devices  37.6 us (41%)
  Pallas kernels  23.6 us (26%)
  waiting for transfers between devices  21.9 us (24%)
  local copies, waits for them, and re-layouts  5.77 us (6%)
  other arithmetic  1.17 us (1%)
  between operations  0.97 us (1%)
    pallas_call x11, Pallas kernels, call(): pl.pallas_call(kernel, out_shape=outs, in_specs=sspec(scalars) + vspec(le...  23.6 us
    ppermute x8, starting transfers between devices, along(): return lax.ppermute(x, ('samples', 'chan'), whole)  20 us
    ppermute x2, waiting for transfers between devices, from_sides(): got = lax.ppermute(jnp.where(at == 0, last, first), axis, [(0, 1), (1, 0)])  8.93 us
    ppermute x7, starting transfers between devices, exchange(): lax.ppermute(x, axis, [(i, (i + s) % size) for i in range(size)])  8.43 us
    ppermute x1, waiting for transfers between devices, on_device(): from_end = lax.ppermute(grad_end, 'chan', [(1, size - 1), (size - 2, 0)])  5.62 us
    unnamed x17, local copies, waits for them, and re-layouts  5.34 us
    ppermute x1, waiting for transfers between devices, on_device(): lax.ppermute(parts[r], 'rows', [(i, (i + r) % rows) for i in range(rows)])  3.82 us
    ppermute x1, starting transfers between devices, on_device(): feat_end = lax.ppermute(feat, 'chan', [(0, 1), (size - 1, size - 2)])  2.89 us
  transfers between devices with their start and end apart: 21, of which 5 were waited for; matrix products, arithmetic and copies ran while one was open for 3% of the time, Pallas kernels for 24%

profile of v10, /device:TPU:0, one launch (start us, length us, event | category | flops | bytes accessed | tf_op | source)
XLA Modules:
  0.0 91.0 jit_solution(12732644560681444049)
XLA Ops:
  0.7 1.3 %copy.14 = bf16[8,8,8,512]{3,1,2,0:T(8,128)(2,1)S(1)} copy(bf16[8,8,8,512]{3,2,1,0:T(8,128)(2,1)} %bitcast.32) | data formatting | bytes 1048576
  1.9 5.7 %collective-permute-start.2 = (bf16[64,4096]{1,0:T(8,128)(2,1)S(1)}, bf16[64,4096]{1,0:T(8,128)(2,1)}, u32[]{:S(2)}, u32[]{:S(2)}) collective-permute-start(bf16[64,4096]{1,0:T(8,128)(2,1)S(1)} %bitcast.26), channel_id=1, source_target_pairs={{0,1},{1,2},{2,3},{7,6},{6,5},{5,4},{8,9},{9,10},{10,11},{15,14},{... | collective-permute-start | bytes 1572872 | tf_op jit(solution)/shard_map/ppermute | solution.py:375
  7.7 1.3 %collective-permute-start.3 = (bf16[64,4096]{1,0:T(8,128)(2,1)S(1)}, bf16[64,4096]{1,0:T(8,128)(2,1)}, u32[]{:S(2)}, u32[]{:S(2)}) collective-permute-start(bf16[64,4096]{1,0:T(8,128)(2,1)S(1)} %bitcast.27), channel_id=1, source_target_pairs={{1,0},{2,1},{3,2},{6,7},{5,6},{4,5},{9,8},{10,9},{11,10},{14,15},{... | collective-permute-start | bytes 1572872 | tf_op jit(solution)/shard_map/ppermute | solution.py:375
  9.0 0.0 copy-start
  9.0 1.3 %copy-done = f32[4,9,64,128]{3,2,1,0:T(8,128)S(1)} copy-done((f32[4,9,64,128]{3,2,1,0:T(8,128)S(1)}, f32[4,9,64,128]{3,2,1,0:T(8,128)}, u32[]{:S(2)}) %copy-start) | copy-done | bytes 1179672
  10.2 0.7 copy-done.3
  10.9 0.7 copy-done.4
  11.6 0.7 copy-done.5
  12.2 1.0 %plain.1 = (f32[10,64,128]{2,1,0:T(8,128)S(1)}, f32[8,128]{1,0:T(8,128)S(1)}) custom-call(s32[1,4]{1,0:T(1,128)S(1)} %copy-done.4, f32[1,512]{1,0:T(1,128)S(1)} %copy-done.3, f32[1,128]{1,0:T(1,128)S(1)} %bitcast.30, f32[512,128]{1,0:T(8,128)S(1)} %copy-done.2, f32[4,9,64,128]{3,2,1,0:T(8,128)S(1)} %copy-done), custom_call_target="tpu_custom_call" | custom-call | flops 1000000 | bytes 1776144 | tf_op jit(solution)/shard_map/plain/pallas_call | solution.py:326
  13.2 1.6 %collective-permute-start.1 = (f32[10,64,128]{2,1,0:T(8,128)S(1)}, f32[10,64,128]{2,1,0:T(8,128)S(1)}, u32[]{:S(2)}, u32[]{:S(2)}) collective-permute-start(f32[10,64,128]{2,1,0:T(8,128)S(1)} %get-tuple-element.62.refs_0_), channel_id=1, source_target_pairs={{0,16},{16,0},{1,17},{17,1},{2,18},{18,2},{3,19},{19,3},{4,20},{20... | collective-permute-start | bytes 983048 | tf_op jit(solution)/shard_map/ppermute | solution.py:343
  14.8 0.2 copy.13
  15.0 0.6 collective-permute-start
  15.6 8.9 %collective-permute-done = bf16[64,512]{1,0:T(8,128)(2,1)S(1)} collective-permute-done((bf16[64,512]{1,0:T(8,128)(2,1)S(1)}, bf16[64,512]{1,0:T(8,128)(2,1)S(1)}, u32[]{:S(2)}, u32[]{:S(2)}) %collective-permute-start) | collective-permute-done | bytes 65568 | tf_op jit(solution)/shard_map/ppermute | solution.py:350
  24.6 0.0 collective-permute-done.1.refs_1_
  24.6 2.9 %collective-permute-start.6 = (bf16[64,5120]{1,0:T(8,128)(2,1)S(1)}, bf16[64,5120]{1,0:T(8,128)(2,1)S(1)}, u32[]{:S(2)}, u32[]{:S(2)}) collective-permute-start(bf16[64,5120]{1,0:T(8,128)(2,1)S(1)} %feat_rows.1.refs_3_), channel_id=1, source_target_pairs={{0,1},{3,2},{4,5},{7,6},{8,9},{11,10},{12,13},{15,14},{16,17},{19,... | collective-permute-start | bytes 1966088 | tf_op jit(solution)/shard_map/ppermute | solution.py:415
  27.5 0.0 collective-permute-done.2.refs_1_.first
  27.5 0.0 collective-permute-done.3.refs_2_.second
  27.5 0.7 collective-permute-start.4
  28.2 1.3 %collective-permute-start.5 = (bf16[64,4096]{1,0:T(8,128)(2,1)}, bf16[64,4096]{1,0:T(8,128)(2,1)S(1)}, u32[]{:S(2)}, u32[]{:S(2)}) collective-permute-start(bf16[64,4096]{1,0:T(8,128)(2,1)} %collective-permute-done.3.refs_2_.second), channel_id=1, source_target_pairs={{1,0},{2,1},{6,7},{5,6},{9,8},{10,9},{14,15},{13,14},{17,16},{18,1... | collective-permute-start | bytes 1572872 | tf_op jit(solution)/shard_map/ppermute | solution.py:375
  29.5 0.1 stack.19.place
  29.6 0.8 mod_blocks.1
  30.4 4.5 %near_grad.1 = (bf16[64,576]{1,0:T(8,128)(2,1)S(1)}, bf16[192,576]{1,0:T(8,128)(2,1)S(1)}, bf16[192,576]{1,0:T(8,128)(2,1)S(1)}, bf16[192,5120]{1,0:T(8,128)(2,1)S(1)}) custom-call(bf16[64,4096]{1,0:T(8,128)(2,1)S(1)} %bitcast.28, bf16[64,4096]{1,0:T(8,128)(2,1)} %collective-permute-done.2.refs_1_.first, ...), custom_call_target="tpu_custom_call" | custom-call | flops 905969664 | bytes 4857856 | tf_op jit(solution)/shard_map/near_grad/pallas_call | solution.py:326
  34.9 1.3 %collective-permute-start.7 = (bf16[192,576]{1,0:T(8,128)(2,1)S(1)}, bf16[192,576]{1,0:T(8,128)(2,1)S(1)}, u32[]{:S(2)}, u32[]{:S(2)}) collective-permute-start(bf16[192,576]{1,0:T(8,128)(2,1)S(1)} %get-tuple-element.75), channel_id=1, source_target_pairs={{1,0},{2,1},{3,2},{6,7},{5,6},{4,5},{9,8},{10,9},{11,10},{14,15},{... | collective-permute-start | bytes 663560 | tf_op jit(solution)/shard_map/ppermute | solution.py:375
  36.2 6.1 %collective-permute-start.8 = (bf16[192,576]{1,0:T(8,128)(2,1)S(1)}, bf16[192,576]{1,0:T(8,128)(2,1)S(1)}, u32[]{:S(2)}, u32[]{:S(2)}) collective-permute-start(bf16[192,576]{1,0:T(8,128)(2,1)S(1)} %get-tuple-element.76), channel_id=1, source_target_pairs={{0,1},{1,2},{2,3},{7,6},{6,5},{5,4},{8,9},{9,10},{10,11},{15,14},{... | collective-permute-start | bytes 663560 | tf_op jit(solution)/shard_map/ppermute | solution.py:375
  42.4 0.0 collective-permute-done.6.feat
  42.4 0.0 collective-permute-done.4.refs_0_
  42.4 0.0 collective-permute-done.5.refs_1_
  42.4 2.7 %middle_grad.1 = (bf16[64,576]{1,0:T(8,128)(2,1)S(1)}, bf16[64,4096]{1,0:T(8,128)(2,1)S(1)}, bf16[64,4096]{1,0:T(8,128)(2,1)S(1)}) custom-call(bf16[64,4096]{1,0:T(8,128)(2,1)S(1)} %collective-permute-done.4.refs_0_, bf16[64,4096]{1,0:T(8,128)(2,1)S(1)} %collective-permute-done.5.refs_1_, bf16[192,5120]{1,0:T(8,128)(2,1)S(1)} %get-tuple-element.79.refs_2_), custom_call_target="tpu_custom_call" | custom-call | flops 301989888 | bytes 4136960 | tf_op jit(solution)/shard_map/middle_grad/pallas_call | solution.py:326
  45.1 3.6 %collective-permute-start.9 = (bf16[64,576]{1,0:T(8,128)(2,1)S(1)}, bf16[64,576]{1,0:T(8,128)(2,1)S(1)}, u32[]{:S(2)}, u32[]{:S(2)}) collective-permute-start(bf16[64,576]{1,0:T(8,128)(2,1)S(1)} %get-tuple-element.80), channel_id=1, source_target_pairs={{0,2},{1,3},{2,0},{3,1},{7,5},{6,4},{5,7},{4,6},{8,10},{9,11},{10,... | collective-permute-start | bytes 221192 | tf_op jit(solution)/shard_map/ppermute | solution.py:375
  48.7 0.0 collective-permute-done.7.ahead
  48.7 0.0 collective-permute-done.8.behind
  48.7 3.6 %end_grad.1 = bf16[128,576]{1,0:T(8,128)(2,1)S(1)} custom-call(s32[5]{0:T(128)S(1)} %stack.19.place, bf16[64,4096]{1,0:T(8,128)(2,1)S(1)} %get-tuple-element.81.end_block, bf16[64,5120]{1,0:T(8,128)(2,1)S(1)} %collective-permute-done.6.feat, bf16[192,576]{1,0:T(8,128)(2,1)S(1)} %collective-permute-done.7.ahead, ...), custom_call_target="tpu_custom_call" | custom-call | flops 301989888 | bytes 1769492 | tf_op jit(solution)/shard_map/end_grad/pallas_call | solution.py:326
  52.3 0.0 collective-permute-done.9.others
  52.3 1.3 %collective-permute-start.10 = (bf16[128,576]{1,0:T(8,128)(2,1)S(1)}, bf16[128,576]{1,0:T(8,128)(2,1)S(1)}, u32[]{:S(2)}, u32[]{:S(2)}) collective-permute-start(bf16[128,576]{1,0:T(8,128)(2,1)S(1)} %end_grad.1), channel_id=1, source_target_pairs={{1,3},{2,0},{5,7},{6,4},{9,11},{10,8},{13,15},{14,12},{17,19},{18,... | collective-permute-start | bytes 442376 | tf_op jit(solution)/shard_map/ppermute | solution.py:475
  53.6 1.3 %collective-permute-start.16 = (bf16[64,4096]{1,0:T(8,128)(2,1)S(1)}, bf16[64,4096]{1,0:T(8,128)(2,1)S(1)}, u32[]{:S(2)}, u32[]{:S(2)}) collective-permute-start(bf16[64,4096]{1,0:T(8,128)(2,1)S(1)} %get-tuple-element.81.end_block), channel_id=1, source_target_pairs={{1,0},{2,3},{5,4},{6,7},{9,8},{10,11},{13,12},{14,15},{17,16},{18,... | collective-permute-start | bytes 1572872 | tf_op jit(solution)/shard_map/ppermute | solution.py:476
  54.9 5.6 %collective-permute-done.10.end = bf16[128,576]{1,0:T(8,128)(2,1)S(1)} collective-permute-done((bf16[128,576]{1,0:T(8,128)(2,1)S(1)}, bf16[128,576]{1,0:T(8,128)(2,1)S(1)}, u32[]{:S(2)}, u32[]{:S(2)}) %collective-permute-start.10) | collective-permute-done | bytes 147488 | tf_op jit(solution)/shard_map/ppermute | solution.py:475
  60.5 1.1 %collect.1 = (bf16[10,64,128]{2,1,0:T(8,128)(2,1)S(1)}, bf16[10,64,128]{2,1,0:T(8,128)(2,1)S(1)}) custom-call(s32[5]{0:T(128)S(1)} %stack.19.place, f32[64,128]{1,0:T(8,128)S(1)} %get-tuple-element.64.scale, bf16[9,64,256]{2,1,0:T(8,128)(2,1)S(1)} %get-tuple-element.73.whole_mod, bf16[64,576]{1,0:T(8,128)(2,1)S(1)} %get-tuple-element.74.own, ...), custom_call_target="tpu_custom_call" | custom-call | flops 3000000000 | bytes 1392660 | tf_op jit(solution)/shard_map/collect/pallas_call | solution.py:326
  61.6 1.6 %collective-permute-start.11 = (bf16[10,64,128]{2,1,0:T(8,128)(2,1)S(1)}, bf16[10,64,128]{2,1,0:T(8,128)(2,1)S(1)}, u32[]{:S(2)}, u32[]{:S(2)}) collective-permute-start(bf16[10,64,128]{2,1,0:T(8,128)(2,1)S(1)} %get-tuple-element.90), channel_id=1, source_target_pairs={{0,16},{16,0},{1,17},{17,1},{2,18},{18,2},{3,19},{19,3},{4,20},{20... | collective-permute-start | bytes 491528 | tf_op jit(solution)/shard_map/ppermute | solution.py:496
  63.1 0.0 collective-permute-start.15
  63.1 3.8 %collective-permute-done.11.refs_1_ = bf16[10,64,128]{2,1,0:T(8,128)(2,1)S(1)} collective-permute-done((bf16[10,64,128]{2,1,0:T(8,128)(2,1)S(1)}, bf16[10,64,128]{2,1,0:T(8,128)(2,1)S(1)}, u32[]{:S(2)}, u32[]{:S(2)}) %collective-permute-start.11) | collective-permute-done | bytes 163872 | tf_op jit(solution)/shard_map/ppermute | solution.py:496
  66.9 0.2 row_sum.1.refs_0_
  67.2 0.1 collective-permute-start.12
  67.2 1.6 %collective-permute-start.13 = (bf16[11,64,128]{2,1,0:T(8,128)(2,1)S(1)}, bf16[11,64,128]{2,1,0:T(8,128)(2,1)S(1)}, u32[]{:S(2)}, u32[]{:S(2)}) collective-permute-start(bf16[11,64,128]{2,1,0:T(8,128)(2,1)S(1)} %row_sum.1.refs_0_), channel_id=1, source_target_pairs={{0,8},{4,12},{8,0},{12,4},{1,9},{5,13},{9,1},{13,5},{2,10},{6,14},... | collective-permute-start | bytes 540680 | tf_op jit(solution)/shard_map/ppermute | solution.py:343
  68.8 1.4 %collective-permute-start.14 = (bf16[11,64,128]{2,1,0:T(8,128)(2,1)S(1)}, bf16[11,64,128]{2,1,0:T(8,128)(2,1)S(1)}, u32[]{:S(2)}, u32[]{:S(2)}) collective-permute-start(bf16[11,64,128]{2,1,0:T(8,128)(2,1)S(1)} %row_sum.1.refs_0_), channel_id=1, source_target_pairs={{0,12},{4,0},{8,4},{12,8},{1,13},{5,1},{9,5},{13,9},{2,14},{6,2},{... | collective-permute-start | bytes 540680 | tf_op jit(solution)/shard_map/ppermute | solution.py:343
  70.2 0.0 collective-permute-done.15.refs_0_
  70.2 2.6 %collective-permute-done.16.far = bf16[64,4096]{1,0:T(8,128)(2,1)S(1)} collective-permute-done((bf16[64,4096]{1,0:T(8,128)(2,1)S(1)}, bf16[64,4096]{1,0:T(8,128)(2,1)S(1)}, u32[]{:S(2)}, u32[]{:S(2)}) %collective-permute-start.16) | collective-permute-done | bytes 524320 | tf_op jit(solution)/shard_map/ppermute | solution.py:476
  72.8 5.2 %input_grad.1 = (f32[64,4096]{1,0:T(8,128)S(1)}, f32[64,512]{1,0:T(8,128)S(1)}, f32[64,512]{1,0:T(8,128)S(1)}) custom-call(s32[5]{0:T(128)S(1)} %stack.19.place, bf16[64,4096]{1,0:T(8,128)(2,1)S(1)} %bitcast.29, bf16[64,4096]{1,0:T(8,128)(2,1)} %collective-permute-done.2.refs_1_.first, bf16[64,4096]{1,0:T(8,128)(2,1)} %collective-permute-done.3.refs_2_.second, ...), custom_call_target="tpu_custom_call" | custom-call | flops 2000000000 | bytes 4669460 | tf_op jit(solution)/shard_map/input_grad/pallas_call | solution.py:326
  78.1 0.0 collective-permute-done.12.refs_1_
  78.1 0.0 collective-permute-done.13.refs_2_
  78.1 0.0 collective-permute-done.14.refs_3_
  78.1 1.6 %collective-permute-start.20 = (f32[64,512]{1,0:T(8,128)S(1)}, f32[64,512]{1,0:T(8,128)S(1)}, u32[]{:S(2)}, u32[]{:S(2)}) collective-permute-start(f32[64,512]{1,0:T(8,128)S(1)} %broadcast_select_fusion), channel_id=1, source_target_pairs={{0,16},{16,0},{1,17},{17,1},{2,18},{18,2},{3,19},{19,3},{4,20},{20... | collective-permute-start | bytes 393224 | tf_op jit(solution)/shard_map/ppermute | solution.py:350
  79.7 0.1 pad.1.clone
  79.7 2.8 %bank_grad.1 = (f32[4,9,64,128]{3,2,1,0:T(8,128)}, f32[4,128]{1,0:T(4,128)S(1)}, f32[4,512]{1,0:T(4,128)S(1)}) custom-call(s32[5]{0:T(128)S(1)} %stack.19.place, f32[4,9,64,128]{3,2,1,0:T(8,128)S(1)} %copy-done.1, bf16[11,64,128]{2,1,0:T(8,128)(2,1)S(1)} %row_sum.1.refs_0_, bf16[11,64,128]{2,1,0:T(8,128)(2,1)S(1)} %collective-permute-done.12.refs_1_, ...), custom_call_target="tpu_custom_call" | custom-call | flops 1000000 | bytes 3090452 | tf_op jit(solution)/shard_map/bank_grad/pallas_call | solution.py:326
  82.6 0.0 collective-permute-start.17
  82.6 3.1 %collective-permute-start.18 = (f32[4,128]{1,0:T(4,128)S(1)}, f32[4,128]{1,0:T(4,128)S(1)}, u32[]{:S(2)}, u32[]{:S(2)}) collective-permute-start(f32[4,128]{1,0:T(4,128)S(1)} %get-tuple-element.110.refs_0_), channel_id=1, source_target_pairs={{0,2},{1,3},{2,0},{3,1},{4,6},{5,7},{6,4},{7,5},{8,10},{9,11},{10,... | collective-permute-start | bytes 6152 | tf_op jit(solution)/shard_map/ppermute | solution.py:343
  85.7 0.7 collective-permute-start.19
  86.4 0.6 copy.15
  87.1 0.1 copy.12
  87.2 0.1 copy.11
  87.3 1.1 %fusion = bf16[1,64,8,512]{3,2,1,0:T(8,128)(2,1)} fusion(f32[1,64,1,512]{3,2,1,0:T(1,128)S(1)} %copy.12, f32[1,64,1,512]{3,2,1,0:T(1,128)S(1)} %copy.11, f32[8]{0:T(128)S(1)} %pad.1.clone, f32[1,64,8,512]{3,2,1,0:T(8,128)S(1)} %bitcast.31), kind=kLoop, calls=%fused_computation.1 | loop fusion | flops 1048576 | bytes 1835040 | tf_op jit(solution)/shard_map/convert_element_type | solution.py:543
  88.4 0.0 collective-permute-done.17.refs_1_
  88.5 0.0 collective-permute-done.18.refs_2_
  88.5 0.8 collective-permute-done.19.refs_3_
  89.3 1.7 %affine.1 = (f32[512,128]{1,0:T(8,128)}, f32[1,128]{1,0:T(1,128)}) custom-call(s32[5]{0:T(128)S(1)} %stack.19.place, f32[4,512]{1,0:T(4,128)S(1)} %get-tuple-element.109.latents, f32[4,128]{1,0:T(4,128)S(1)} %get-tuple-element.110.refs_0_, f32[4,128]{1,0:T(4,128)S(1)} %collective-permute-done.17.refs_1_, f32[4,128]{1,0:T(4,128)S(1)} %collective-permute-done.18.refs_2_, ...), custom_call_target="tpu_custom_call" | custom-call | flops 1000000 | bytes 279060 | tf_op jit(solution)/shard_map/affine/pallas_call | solution.py:326
  (16 shorter events, 0.1 us)
Async XLA Ops:
  0.6 8.3 %copy-start.2 = (f32[512,128]{1,0:T(8,128)S(1)}, f32[512,128]{1,0:T(8,128)}, u32[]{:S(2)}) copy-start(f32[512,128]{1,0:T(8,128)} %refs_3_.1) | copy-start | bytes 786436
  0.6 14.1 %copy-start.6 = (bf16[1,64,8,512]{3,2,1,0:T(8,128)(2,1)S(1)}, bf16[1,64,8,512]{3,2,1,0:T(8,128)(2,1)}, u32[]{:S(2)}) copy-start(bf16[1,64,8,512]{3,2,1,0:T(8,128)(2,1)} %param.7) | copy-start | bytes 1572868
  1.9 25.5 %collective-permute-start.2 = (bf16[64,4096]{1,0:T(8,128)(2,1)S(1)}, bf16[64,4096]{1,0:T(8,128)(2,1)}, u32[]{:S(2)}, u32[]{:S(2)}) collective-permute-start(bf16[64,4096]{1,0:T(8,128)(2,1)S(1)} %bitcast.26), channel_id=1, source_target_pairs={{0,1},{1,2},{2,3},{7,6},{6,5},{5,4},{8,9},{9,10},{10,11},{15,14},{... | collective-permute-start | bytes 1572872 | tf_op jit(solution)/shard_map/ppermute | solution.py:375
  7.7 19.8 %collective-permute-start.3 = (bf16[64,4096]{1,0:T(8,128)(2,1)S(1)}, bf16[64,4096]{1,0:T(8,128)(2,1)}, u32[]{:S(2)}, u32[]{:S(2)}) collective-permute-start(bf16[64,4096]{1,0:T(8,128)(2,1)S(1)} %bitcast.27), channel_id=1, source_target_pairs={{1,0},{2,1},{3,2},{6,7},{5,6},{4,5},{9,8},{10,9},{11,10},{14,15},{... | collective-permute-start | bytes 1572872 | tf_op jit(solution)/shard_map/ppermute | solution.py:375
  9.0 1.3 %copy-start = (f32[4,9,64,128]{3,2,1,0:T(8,128)S(1)}, f32[4,9,64,128]{3,2,1,0:T(8,128)}, u32[]{:S(2)}) copy-start(f32[4,9,64,128]{3,2,1,0:T(8,128)} %bank.1) | copy-start | bytes 3538948
  10.2 0.7 copy-start.3
  10.9 0.7 copy-start.4
  11.6 0.7 copy-start.5
  13.2 11.4 %collective-permute-start.1 = (f32[10,64,128]{2,1,0:T(8,128)S(1)}, f32[10,64,128]{2,1,0:T(8,128)S(1)}, u32[]{:S(2)}, u32[]{:S(2)}) collective-permute-start(f32[10,64,128]{2,1,0:T(8,128)S(1)} %get-tuple-element.62.refs_0_), channel_id=1, source_target_pairs={{0,16},{16,0},{1,17},{17,1},{2,18},{18,2},{3,19},{19,3},{4,20},{20... | collective-permute-start | bytes 983048 | tf_op jit(solution)/shard_map/ppermute | solution.py:343
  15.0 9.5 %collective-permute-start = (bf16[64,512]{1,0:T(8,128)(2,1)S(1)}, bf16[64,512]{1,0:T(8,128)(2,1)S(1)}, u32[]{:S(2)}, u32[]{:S(2)}) collective-permute-start(bf16[64,512]{1,0:T(8,128)(2,1)S(1)} %slice_select_fusion), channel_id=1, source_target_pairs={{0,16},{16,0},{1,17},{17,1},{2,18},{18,2},{3,19},{19,3},{4,20},{20... | collective-permute-start | bytes 196616 | tf_op jit(solution)/shard_map/ppermute | solution.py:350
  24.6 17.8 %collective-permute-start.6 = (bf16[64,5120]{1,0:T(8,128)(2,1)S(1)}, bf16[64,5120]{1,0:T(8,128)(2,1)S(1)}, u32[]{:S(2)}, u32[]{:S(2)}) collective-permute-start(bf16[64,5120]{1,0:T(8,128)(2,1)S(1)} %feat_rows.1.refs_3_), channel_id=1, source_target_pairs={{0,1},{3,2},{4,5},{7,6},{8,9},{11,10},{12,13},{15,14},{16,17},{19,... | collective-permute-start | bytes 1966088 | tf_op jit(solution)/shard_map/ppermute | solution.py:415
  27.5 14.9 %collective-permute-start.4 = (bf16[64,4096]{1,0:T(8,128)(2,1)}, bf16[64,4096]{1,0:T(8,128)(2,1)S(1)}, u32[]{:S(2)}, u32[]{:S(2)}) collective-permute-start(bf16[64,4096]{1,0:T(8,128)(2,1)} %collective-permute-done.2.refs_1_.first), channel_id=1, source_target_pairs={{1,2},{2,3},{6,5},{5,4},{9,10},{10,11},{14,13},{13,12},{17,18},{18... | collective-permute-start | bytes 1572872 | tf_op jit(solution)/shard_map/ppermute | solution.py:375
  28.2 14.2 %collective-permute-start.5 = (bf16[64,4096]{1,0:T(8,128)(2,1)}, bf16[64,4096]{1,0:T(8,128)(2,1)S(1)}, u32[]{:S(2)}, u32[]{:S(2)}) collective-permute-start(bf16[64,4096]{1,0:T(8,128)(2,1)} %collective-permute-done.3.refs_2_.second), channel_id=1, source_target_pairs={{1,0},{2,1},{6,7},{5,6},{9,8},{10,9},{14,15},{13,14},{17,16},{18,1... | collective-permute-start | bytes 1572872 | tf_op jit(solution)/shard_map/ppermute | solution.py:375
  34.9 13.8 %collective-permute-start.7 = (bf16[192,576]{1,0:T(8,128)(2,1)S(1)}, bf16[192,576]{1,0:T(8,128)(2,1)S(1)}, u32[]{:S(2)}, u32[]{:S(2)}) collective-permute-start(bf16[192,576]{1,0:T(8,128)(2,1)S(1)} %get-tuple-element.75), channel_id=1, source_target_pairs={{1,0},{2,1},{3,2},{6,7},{5,6},{4,5},{9,8},{10,9},{11,10},{14,15},{... | collective-permute-start | bytes 663560 | tf_op jit(solution)/shard_map/ppermute | solution.py:375
  36.2 12.5 %collective-permute-start.8 = (bf16[192,576]{1,0:T(8,128)(2,1)S(1)}, bf16[192,576]{1,0:T(8,128)(2,1)S(1)}, u32[]{:S(2)}, u32[]{:S(2)}) collective-permute-start(bf16[192,576]{1,0:T(8,128)(2,1)S(1)} %get-tuple-element.76), channel_id=1, source_target_pairs={{0,1},{1,2},{2,3},{7,6},{6,5},{5,4},{8,9},{9,10},{10,11},{15,14},{... | collective-permute-start | bytes 663560 | tf_op jit(solution)/shard_map/ppermute | solution.py:375
  45.1 7.2 %collective-permute-start.9 = (bf16[64,576]{1,0:T(8,128)(2,1)S(1)}, bf16[64,576]{1,0:T(8,128)(2,1)S(1)}, u32[]{:S(2)}, u32[]{:S(2)}) collective-permute-start(bf16[64,576]{1,0:T(8,128)(2,1)S(1)} %get-tuple-element.80), channel_id=1, source_target_pairs={{0,2},{1,3},{2,0},{3,1},{7,5},{6,4},{5,7},{4,6},{8,10},{9,11},{10,... | collective-permute-start | bytes 221192 | tf_op jit(solution)/shard_map/ppermute | solution.py:375
  52.3 8.2 %collective-permute-start.10 = (bf16[128,576]{1,0:T(8,128)(2,1)S(1)}, bf16[128,576]{1,0:T(8,128)(2,1)S(1)}, u32[]{:S(2)}, u32[]{:S(2)}) collective-permute-start(bf16[128,576]{1,0:T(8,128)(2,1)S(1)} %end_grad.1), channel_id=1, source_target_pairs={{1,3},{2,0},{5,7},{6,4},{9,11},{10,8},{13,15},{14,12},{17,19},{18,... | collective-permute-start | bytes 442376 | tf_op jit(solution)/shard_map/ppermute | solution.py:475
  53.6 19.3 %collective-permute-start.16 = (bf16[64,4096]{1,0:T(8,128)(2,1)S(1)}, bf16[64,4096]{1,0:T(8,128)(2,1)S(1)}, u32[]{:S(2)}, u32[]{:S(2)}) collective-permute-start(bf16[64,4096]{1,0:T(8,128)(2,1)S(1)} %get-tuple-element.81.end_block), channel_id=1, source_target_pairs={{1,0},{2,3},{5,4},{6,7},{9,8},{10,11},{13,12},{14,15},{17,16},{18,... | collective-permute-start | bytes 1572872 | tf_op jit(solution)/shard_map/ppermute | solution.py:476
  61.6 5.4 %collective-permute-start.11 = (bf16[10,64,128]{2,1,0:T(8,128)(2,1)S(1)}, bf16[10,64,128]{2,1,0:T(8,128)(2,1)S(1)}, u32[]{:S(2)}, u32[]{:S(2)}) collective-permute-start(bf16[10,64,128]{2,1,0:T(8,128)(2,1)S(1)} %get-tuple-element.90), channel_id=1, source_target_pairs={{0,16},{16,0},{1,17},{17,1},{2,18},{18,2},{3,19},{19,3},{4,20},{20... | collective-permute-start | bytes 491528 | tf_op jit(solution)/shard_map/ppermute | solution.py:496
  63.1 7.1 %collective-permute-start.15 = (bf16[64,576]{1,0:T(8,128)(2,1)S(1)}, bf16[64,576]{1,0:T(8,128)(2,1)S(1)}, u32[]{:S(2)}, u32[]{:S(2)}) collective-permute-start(bf16[64,576]{1,0:T(8,128)(2,1)S(1)} %get-tuple-element.92), channel_id=1, source_target_pairs={{0,2},{1,3},{2,0},{3,1},{7,5},{6,4},{5,7},{4,6},{8,10},{9,11},{10,... | collective-permute-start | bytes 221192 | tf_op jit(solution)/shard_map/ppermute | solution.py:375
  67.2 10.9 %collective-permute-start.12 = (bf16[11,64,128]{2,1,0:T(8,128)(2,1)S(1)}, bf16[11,64,128]{2,1,0:T(8,128)(2,1)S(1)}, u32[]{:S(2)}, u32[]{:S(2)}) collective-permute-start(bf16[11,64,128]{2,1,0:T(8,128)(2,1)S(1)} %row_sum.1.refs_0_), channel_id=1, source_target_pairs={{0,4},{4,8},{8,12},{12,0},{1,5},{5,9},{9,13},{13,1},{2,6},{6,10},{... | collective-permute-start | bytes 540680 | tf_op jit(solution)/shard_map/ppermute | solution.py:343
  67.2 10.8 %collective-permute-start.13 = (bf16[11,64,128]{2,1,0:T(8,128)(2,1)S(1)}, bf16[11,64,128]{2,1,0:T(8,128)(2,1)S(1)}, u32[]{:S(2)}, u32[]{:S(2)}) collective-permute-start(bf16[11,64,128]{2,1,0:T(8,128)(2,1)S(1)} %row_sum.1.refs_0_), channel_id=1, source_target_pairs={{0,8},{4,12},{8,0},{12,4},{1,9},{5,13},{9,1},{13,5},{2,10},{6,14},... | collective-permute-start | bytes 540680 | tf_op jit(solution)/shard_map/ppermute | solution.py:343
  68.8 9.3 %collective-permute-start.14 = (bf16[11,64,128]{2,1,0:T(8,128)(2,1)S(1)}, bf16[11,64,128]{2,1,0:T(8,128)(2,1)S(1)}, u32[]{:S(2)}, u32[]{:S(2)}) collective-permute-start(bf16[11,64,128]{2,1,0:T(8,128)(2,1)S(1)} %row_sum.1.refs_0_), channel_id=1, source_target_pairs={{0,12},{4,0},{8,4},{12,8},{1,13},{5,1},{9,5},{13,9},{2,14},{6,2},{... | collective-permute-start | bytes 540680 | tf_op jit(solution)/shard_map/ppermute | solution.py:343
  72.8 6.9 %copy-start.1 = (f32[4,9,64,128]{3,2,1,0:T(8,128)S(1)}, f32[4,9,64,128]{3,2,1,0:T(8,128)}, u32[]{:S(2)}) copy-start(f32[4,9,64,128]{3,2,1,0:T(8,128)} %bank.1) | copy-start | bytes 3538948
  78.1 8.9 %collective-permute-start.20 = (f32[64,512]{1,0:T(8,128)S(1)}, f32[64,512]{1,0:T(8,128)S(1)}, u32[]{:S(2)}, u32[]{:S(2)}) collective-permute-start(f32[64,512]{1,0:T(8,128)S(1)} %broadcast_select_fusion), channel_id=1, source_target_pairs={{0,16},{16,0},{1,17},{17,1},{2,18},{18,2},{3,19},{19,3},{4,20},{20... | collective-permute-start | bytes 393224 | tf_op jit(solution)/shard_map/ppermute | solution.py:350
  82.6 5.9 %collective-permute-start.17 = (f32[4,128]{1,0:T(4,128)S(1)}, f32[4,128]{1,0:T(4,128)S(1)}, u32[]{:S(2)}, u32[]{:S(2)}) collective-permute-start(f32[4,128]{1,0:T(4,128)S(1)} %get-tuple-element.110.refs_0_), channel_id=1, source_target_pairs={{0,1},{1,2},{2,3},{3,0},{4,5},{5,6},{6,7},{7,4},{8,9},{9,10},{10,1... | collective-permute-start | bytes 6152 | tf_op jit(solution)/shard_map/ppermute | solution.py:343
  82.6 5.9 %collective-permute-start.18 = (f32[4,128]{1,0:T(4,128)S(1)}, f32[4,128]{1,0:T(4,128)S(1)}, u32[]{:S(2)}, u32[]{:S(2)}) collective-permute-start(f32[4,128]{1,0:T(4,128)S(1)} %get-tuple-element.110.refs_0_), channel_id=1, source_target_pairs={{0,2},{1,3},{2,0},{3,1},{4,6},{5,7},{6,4},{7,5},{8,10},{9,11},{10,... | collective-permute-start | bytes 6152 | tf_op jit(solution)/shard_map/ppermute | solution.py:343
  85.7 3.6 %collective-permute-start.19 = (f32[4,128]{1,0:T(4,128)S(1)}, f32[4,128]{1,0:T(4,128)S(1)}, u32[]{:S(2)}, u32[]{:S(2)}) collective-permute-start(f32[4,128]{1,0:T(4,128)S(1)} %get-tuple-element.110.refs_0_), channel_id=1, source_target_pairs={{0,3},{1,0},{2,1},{3,2},{4,7},{5,4},{6,5},{7,6},{8,11},{9,8},{10,9... | collective-permute-start | bytes 6152 | tf_op jit(solution)/shard_map/ppermute | solution.py:343

commit v11 on v10

--- a/solution.py
+++ b/solution.py
@@ -95,6 +95,7 @@
         by_chan[z] = beside([value[:, z * ch : (z + 1) * ch] for value in taps]).astype(BF16)
     for d in range(size):
         outs[d][...] = by_chan[lax.rem(chan_at + sign * d + size, size)]
+    outs[size][...] = by_chan[size - 1 - chan_at]
 
 
 def shifted(x, by):
@@ -145,8 +146,7 @@
     own[...] = whole[0:ch]
     for at, (out, mod) in enumerate(zip((behind, ahead), mods)):
         out[0:ch] = whole[(at + 1) * ch : (at + 2) * ch]
-        out[ch : 2 * ch] = mod[...]
-        out[2 * ch :] = mods[1 - at][...]
+        out[ch:] = mod[...]
 
 
 def middle_grad_kernel(count, height, width, *refs):
@@ -159,26 +159,24 @@
     (out[...],) = tap_products(middle, [wide], [total], height, width)
 
 
-def end_grad_kernel(height, width, place, end_block, feat, ahead, behind, out, wide, total):
-    ch = feat.shape[0]
-    second = place[1] == jnp.where(place[3] > 0, 1, place[4] - 2)
-    out[ch:] = jnp.where(second, behind[2 * ch :], ahead[2 * ch :])
+def end_grad_kernel(height, width, end_block, feat, out, wide, total):
     for row in range(height + 2):
         spread(wide, row, feat[:, row * width : (row + 1) * width])
-    (out[0:ch],) = tap_products(end_block, [wide], [total], height, width)
-
-
-def input_grad_kernel(size, height, width, place, cotan, first, second, middle, far, own_mod, behind, ahead, end, *refs):
-    others, (main, before, after, gathered, taps_t, total) = refs[: size - 3], refs[size - 3 :]
+    (out[...],) = tap_products(end_block, [wide], [total], height, width)
+
+
+def input_grad_kernel(size, height, width, place, cotan, first, second, middle, far, own_mod, behind, ahead, *refs):
+    others, (main, before, after, gathered, taps_t, total) = refs[: size - 2], refs[size - 2 :]
     ch = main.shape[0]
     spot = jnp.where(place[3] > 0, place[1], size - 1 - place[1])
     gathered[0:ch] = cotan[...]
     gathered[ch : 2 * ch] = jnp.where(spot == 0, far[...], first[...])
     gathered[2 * ch : (size - 1) * ch] = middle[...]
     gathered[(size - 1) * ch :] = jnp.where(spot == size - 1, far[...], second[...])
-    mods = [own_mod[...], jnp.where(spot == 0, end[ch:], behind[ch : 2 * ch])]
-    mods += [other[...] for other in others]
-    mods.append(jnp.where(spot == size - 1, end[ch:], ahead[ch : 2 * ch]))
+    end_mod = others[-1][...]
+    mods = [own_mod[...], jnp.where(spot == 0, end_mod, behind[ch:])]
+    mods += [other[...] for other in others[:-1]]
+    mods.append(jnp.where(spot == size - 1, end_mod, ahead[ch:]))
     every = jnp.concatenate([mod.astype(F32) for mod in mods], axis=0)
     taps_t[...] = every.T.astype(BF16)
     total[...] = jnp.zeros(total.shape, F32)
@@ -232,7 +230,7 @@
     for d in range(2, size - 1):
         value = others[(d - 2) * ch : (d - 1) * ch].astype(F32)
         by_chan[lax.rem(chan_at + sign * d + size, size)] = value
-    by_chan[jnp.where(chan_at == 0, size - 1, 0)] += end[0:ch].astype(F32)
+    by_chan[jnp.where(chan_at == 0, size - 1, 0)] += end[...].astype(F32)
     in_ch = outs[0].shape[2]
     product = jnp.zeros(whole_mod.shape[1:], F32)
     for tap in range(TAPS):
@@ -362,7 +360,7 @@
     out_ch, in_ch = bank.shape[2:]
     pixels, all_ch = height * width, ch * size
     sign = 1 - 2 * jnp.remainder(sample_at, 2)
-    place = jnp.stack([sample_at, chan_at, row_at, sign, size]).astype(jnp.int32)
+    place = jnp.stack([sample_at, chan_at, row_at, sign]).astype(jnp.int32)
     flops = 2 * TAPS * ch * ch * size * pixels
 
     def along(x, pairs):
@@ -404,20 +402,20 @@
         ],
     )
     plains = exchange(plain, "rows")
-    feature, plain = lax.optimization_barrier((feature, plain))
+    feature, cotan = lax.optimization_barrier((feature, cotan))
     feat = feature[0].reshape(ch, pixels)
     feat_before, feat_after = from_sides(feat[:, :width], feat[:, pixels - width :], "rows")
     extended = ((ch, (height + 2) * width), BF16)
     (feat,) = call(
         functools.partial(rows_kernel, height, width), "feat_rows", [extended], feat, feat_before, feat_after
     )
-    feat, plains = lax.optimization_barrier((feat, plains))
+    feat, plain = lax.optimization_barrier((feat, plain))
     feat_end = lax.ppermute(feat, "chan", [(0, 1), (size - 1, size - 2)])
     message = ((ch, TAPS * ch), BF16)
     whole_mod, scale, *mods = call(
         functools.partial(blocks_kernel, rows, size),
         "mod_blocks",
-        [((TAPS, out_ch, all_ch), BF16), ((out_ch, 128), F32)] + [message] * size,
+        [((TAPS, out_ch, all_ch), BF16), ((out_ch, 128), F32)] + [message] * (size + 1),
         place,
         *plains,
         scalars=1,
@@ -426,11 +424,11 @@
     first[0], second[0], plains = lax.optimization_barrier((first[0], second[0], plains))
 
     step(2, first[0], second[0])
-    triple, double = ((3 * ch, TAPS * ch), BF16), ((2 * ch, TAPS * ch), BF16)
+    double = ((2 * ch, TAPS * ch), BF16)
     own_grad, to_behind, to_ahead, wide = call(
         functools.partial(near_grad_kernel, height, width),
         "near_grad",
-        [message, triple, triple, ((3 * ch, (height + 2) * width), BF16)],
+        [message, double, double, ((3 * ch, (height + 2) * width), BF16)],
         cotan,
         first[0],
         second[0],
@@ -460,18 +458,13 @@
     (grad_end,) = call(
         functools.partial(end_grad_kernel, height, width),
         "end_grad",
-        [double],
-        place,
+        [message],
         end_block,
         feat_end,
-        from_ahead,
-        from_behind,
-        scalars=1,
         scratch=[((3 * ch, (height + 2) * width), BF16), ((3, ch, 3 * ch), F32)],
         flops=flops // size,
     )
     from_others = along(grad_others, [(i, (i + 2) % size) for i in range(size)])
-    from_others, grad_end = lax.optimization_barrier((from_others, grad_end))
     from_end = lax.ppermute(grad_end, "chan", [(1, size - 1), (size - 2, 0)])
     far = lax.ppermute(end_block, "chan", [(1, 0), (size - 2, size - 1)])
     parts = call(
@@ -492,6 +485,7 @@
     )
     parts, mods = lax.optimization_barrier((parts, mods))
     others = [along(mods[d], [(i, (i + d) % size) for i in range(size)]) for d in range(2, size - 1)]
+    others.append(lax.ppermute(mods[size], "chan", [(0, size - 1), (size - 1, 0)]))
     parts = [parts[0]] + [
         lax.ppermute(parts[r], "rows", [(i, (i + r) % rows) for i in range(rows)])
         for r in range(1, rows)
@@ -514,7 +508,6 @@
         mods[0],
         from_behind,
         from_ahead,
-        from_end,
         *others,
         scalars=1,
         scratch=[

time: 91.4 us -> 87.6 us (0.958)
  waiting for transfers between devices: 21.9 us -> 12.7 us
  starting transfers between devices: 37.6 us -> 44.2 us
  local copies, waits for them, and re-layouts: 5.77 us -> 3.49 us
    ppermute x2, waiting for transfers between devices: 8.93 us -> 1.17 us  [from_sides(): got = lax.ppermute(jnp.where(at == 0, last, first), axis, [(0, 1), (1, 0)])]
    ppermute x0 -> x1, starting transfers between devices: none -> 3.39 us  [on_device(): lax.ppermute(mods[size], 'chan', [(0, size - 1), (size - 1, 0)])]
    ppermute x7, waiting for transfers between devices: 0.86 us -> 4.03 us  [exchange(): lax.ppermute(x, axis, [(i, (i + s) % size) for i in range(size)])]
    ppermute x1, waiting for transfers between devices: 3.82 us -> 1.08 us  [on_device(): lax.ppermute(parts[r], 'rows', [(i, (i + r) % rows) for i in range(rows)])]
    ppermute x1, waiting for transfers between devices: 2.63 us -> 0.01 us  [on_device(): far = lax.ppermute(end_block, 'chan', [(1, 0), (size - 2, size - 1)])]
    ppermute x1, starting transfers between devices: 2.89 us -> 5.29 us  [on_device(): feat_end = lax.ppermute(feat, 'chan', [(0, 1), (size - 1, size - 2)])]
    unnamed x17 -> x19, local copies, waits for them, and re-layouts: 5.34 us -> 3.13 us
    ppermute x8, starting transfers between devices: 20 us -> 22.1 us  [along(): return lax.ppermute(x, ('samples', 'chan'), whole)]
  transfers between devices with their start and end apart: 21 -> 22, of which waited for: 5 -> 7; matrix products, arithmetic and copies ran while one was open for 3% -> 3% of each run, Pallas kernels for 24% -> 26%
where the time goes in v11:
time: 87.6 us; the launch traced here: 87.1 us
  starting transfers between devices  44.2 us (50%)
  Pallas kernels  24.4 us (28%)
  waiting for transfers between devices  12.7 us (14%)
  local copies, waits for them, and re-layouts  3.49 us (4%)
  other arithmetic  1.26 us (1%)
  between operations  1.01 us (1%)
    pallas_call x11, Pallas kernels, call(): pl.pallas_call(kernel, out_shape=outs, in_specs=sspec(scalars) + vspec(le...  24.4 us
    ppermute x8, starting transfers between devices, along(): return lax.ppermute(x, ('samples', 'chan'), whole)  22.1 us
    ppermute x7, starting transfers between devices, exchange(): lax.ppermute(x, axis, [(i, (i + s) % size) for i in range(size)])  7.44 us
    ppermute x1, waiting for transfers between devices, on_device(): from_end = lax.ppermute(grad_end, 'chan', [(1, size - 1), (size - 2, 0)])  6.01 us
    ppermute x1, starting transfers between devices, on_device(): feat_end = lax.ppermute(feat, 'chan', [(0, 1), (size - 1, size - 2)])  5.29 us
    ppermute x7, waiting for transfers between devices, exchange(): lax.ppermute(x, axis, [(i, (i + s) % size) for i in range(size)])  4.03 us
    ppermute x1, starting transfers between devices, on_device(): lax.ppermute(mods[size], 'chan', [(0, size - 1), (size - 1, 0)])  3.39 us
    unnamed x19, local copies, waits for them, and re-layouts  3.13 us
  transfers between devices with their start and end apart: 22, of which 7 were waited for; matrix products, arithmetic and copies ran while one was open for 3% of the time, Pallas kernels for 26%

profile of v11, /device:TPU:0, one launch (start us, length us, event | category | flops | bytes accessed | tf_op | source)
XLA Modules:
  0.0 87.1 jit_solution(4922426851882717460)
XLA Ops:
  0.7 1.3 %copy.13 = bf16[8,8,8,512]{3,1,2,0:T(8,128)(2,1)S(1)} copy(bf16[8,8,8,512]{3,2,1,0:T(8,128)(2,1)} %bitcast.32) | data formatting | bytes 1048576
  2.0 5.7 %collective-permute-start.1 = (bf16[64,4096]{1,0:T(8,128)(2,1)S(1)}, bf16[64,4096]{1,0:T(8,128)(2,1)}, u32[]{:S(2)}, u32[]{:S(2)}) collective-permute-start(bf16[64,4096]{1,0:T(8,128)(2,1)S(1)} %bitcast.26), channel_id=1, source_target_pairs={{0,1},{1,2},{2,3},{7,6},{6,5},{5,4},{8,9},{9,10},{10,11},{15,14},{... | collective-permute-start | bytes 1572872 | tf_op jit(solution)/shard_map/ppermute | solution.py:373
  7.8 1.3 %collective-permute-start.2 = (bf16[64,4096]{1,0:T(8,128)(2,1)S(1)}, bf16[64,4096]{1,0:T(8,128)(2,1)}, u32[]{:S(2)}, u32[]{:S(2)}) collective-permute-start(bf16[64,4096]{1,0:T(8,128)(2,1)S(1)} %bitcast.27), channel_id=1, source_target_pairs={{1,0},{2,1},{3,2},{6,7},{5,6},{4,5},{9,8},{10,9},{11,10},{14,15},{... | collective-permute-start | bytes 1572872 | tf_op jit(solution)/shard_map/ppermute | solution.py:373
  9.1 0.2 copy.14
  9.3 1.6 %collective-permute-start.5 = (bf16[64,512]{1,0:T(8,128)(2,1)S(1)}, bf16[64,512]{1,0:T(8,128)(2,1)S(1)}, u32[]{:S(2)}, u32[]{:S(2)}) collective-permute-start(bf16[64,512]{1,0:T(8,128)(2,1)S(1)} %slice_select_fusion), channel_id=1, source_target_pairs={{0,16},{16,0},{1,17},{17,1},{2,18},{18,2},{3,19},{19,3},{4,20},{20... | collective-permute-start | bytes 196616 | tf_op jit(solution)/shard_map/ppermute | solution.py:348
  10.9 1.0 %plain.1 = (f32[10,64,128]{2,1,0:T(8,128)S(1)}, f32[8,128]{1,0:T(8,128)S(1)}) custom-call(s32[1,4]{1,0:T(1,128)S(1)} %copy-done.5, f32[1,512]{1,0:T(1,128)S(1)} %copy-done.4, f32[1,128]{1,0:T(1,128)S(1)} %bitcast.30, f32[512,128]{1,0:T(8,128)S(1)} %copy-done.3, f32[4,9,64,128]{3,2,1,0:T(8,128)S(1)} %copy-done), custom_call_target="tpu_custom_call" | custom-call | flops 1000000 | bytes 1776144 | tf_op jit(solution)/shard_map/plain/pallas_call | solution.py:324
  11.8 0.0 copy-start.1
  11.8 0.6 collective-permute-start
  12.4 1.2 %collective-permute-done.5 = bf16[64,512]{1,0:T(8,128)(2,1)S(1)} collective-permute-done((bf16[64,512]{1,0:T(8,128)(2,1)S(1)}, bf16[64,512]{1,0:T(8,128)(2,1)S(1)}, u32[]{:S(2)}, u32[]{:S(2)}) %collective-permute-start.5) | collective-permute-done | bytes 65568 | tf_op jit(solution)/shard_map/ppermute | solution.py:348
  13.7 5.3 %collective-permute-start.6 = (bf16[64,5120]{1,0:T(8,128)(2,1)S(1)}, bf16[64,5120]{1,0:T(8,128)(2,1)S(1)}, u32[]{:S(2)}, u32[]{:S(2)}) collective-permute-start(bf16[64,5120]{1,0:T(8,128)(2,1)S(1)} %feat_rows.1.refs_3_), channel_id=1, source_target_pairs={{0,1},{3,2},{4,5},{7,6},{8,9},{11,10},{12,13},{15,14},{16,17},{19,... | collective-permute-start | bytes 1966088 | tf_op jit(solution)/shard_map/ppermute | solution.py:413
  19.0 2.7 %collective-permute-done.refs_1_ = f32[10,64,128]{2,1,0:T(8,128)} collective-permute-done((f32[10,64,128]{2,1,0:T(8,128)S(1)}, f32[10,64,128]{2,1,0:T(8,128)}, u32[]{:S(2)}, u32[]{:S(2)}) %collective-permute-start) | collective-permute-done | bytes 327712 | tf_op jit(solution)/shard_map/ppermute | solution.py:341
  21.7 0.0 collective-permute-done.1.refs_1_.first
  21.7 0.0 collective-permute-done.2.refs_2_.second
  21.7 0.7 collective-permute-start.3
  22.4 1.3 %collective-permute-start.4 = (bf16[64,4096]{1,0:T(8,128)(2,1)}, bf16[64,4096]{1,0:T(8,128)(2,1)}, u32[]{:S(2)}, u32[]{:S(2)}) collective-permute-start(bf16[64,4096]{1,0:T(8,128)(2,1)} %collective-permute-done.2.refs_2_.second), channel_id=1, source_target_pairs={{1,0},{2,1},{6,7},{5,6},{9,8},{10,9},{14,15},{13,14},{17,16},{18,1... | collective-permute-start | bytes 1572872 | tf_op jit(solution)/shard_map/ppermute | solution.py:373
  23.7 0.1 pad_add_fusion.place
  23.8 1.0 %copy-done.2 = f32[10,64,128]{2,1,0:T(8,128)S(1)} copy-done((f32[10,64,128]{2,1,0:T(8,128)S(1)}, f32[10,64,128]{2,1,0:T(8,128)}, u32[]{:S(2)}) %copy-start.2) | copy-done | bytes 327704
  24.8 1.3 %mod_blocks.1 = (bf16[9,64,256]{2,1,0:T(8,128)(2,1)S(1)}, f32[64,128]{1,0:T(8,128)S(1)}, bf16[64,576]{1,0:T(8,128)(2,1)S(1)}, bf16[64,576]{1,0:T(8,128)(2,1)S(1)...) custom-call(s32[4]{0:T(128)S(1)} %pad_add_fusion.place, ...), custom_call_target="tpu_custom_call" | custom-call | flops 1000000 | bytes 1351696 | tf_op jit(solution)/shard_map/mod_blocks/pallas_call | solution.py:324
  26.0 4.5 %near_grad.1 = (bf16[64,576]{1,0:T(8,128)(2,1)S(1)}, bf16[128,576]{1,0:T(8,128)(2,1)S(1)}, bf16[128,576]{1,0:T(8,128)(2,1)S(1)}, bf16[192,5120]{1,0:T(8,128)(2,1)S(1)}) custom-call(bf16[64,4096]{1,0:T(8,128)(2,1)S(1)} %bitcast.28, bf16[64,4096]{1,0:T(8,128)(2,1)} %collective-permute-done.1.refs_1_.first, ...), custom_call_target="tpu_custom_call" | custom-call | flops 905969664 | bytes 4710400 | tf_op jit(solution)/shard_map/near_grad/pallas_call | solution.py:324
  30.6 1.3 %collective-permute-start.7 = (bf16[128,576]{1,0:T(8,128)(2,1)S(1)}, bf16[128,576]{1,0:T(8,128)(2,1)S(1)}, u32[]{:S(2)}, u32[]{:S(2)}) collective-permute-start(bf16[128,576]{1,0:T(8,128)(2,1)S(1)} %get-tuple-element.74), channel_id=1, source_target_pairs={{1,0},{2,1},{3,2},{6,7},{5,6},{4,5},{9,8},{10,9},{11,10},{14,15},{... | collective-permute-start | bytes 442376 | tf_op jit(solution)/shard_map/ppermute | solution.py:373
  31.9 7.5 %collective-permute-start.8 = (bf16[128,576]{1,0:T(8,128)(2,1)S(1)}, bf16[128,576]{1,0:T(8,128)(2,1)S(1)}, u32[]{:S(2)}, u32[]{:S(2)}) collective-permute-start(bf16[128,576]{1,0:T(8,128)(2,1)S(1)} %get-tuple-element.75), channel_id=1, source_target_pairs={{0,1},{1,2},{2,3},{7,6},{6,5},{5,4},{8,9},{9,10},{10,11},{15,14},{... | collective-permute-start | bytes 442376 | tf_op jit(solution)/shard_map/ppermute | solution.py:373
  39.4 0.0 collective-permute-done.6.feat
  39.4 0.0 collective-permute-done.3.refs_0_
  39.5 0.0 collective-permute-done.4.refs_1_
  39.5 3.7 %middle_grad.1 = (bf16[64,576]{1,0:T(8,128)(2,1)S(1)}, bf16[64,4096]{1,0:T(8,128)(2,1)S(1)}, bf16[64,4096]{1,0:T(8,128)(2,1)S(1)}) custom-call(bf16[64,4096]{1,0:T(8,128)(2,1)S(1)} %collective-permute-done.3.refs_0_, bf16[64,4096]{1,0:T(8,128)(2,1)} %collective-permute-done.4.refs_1_, bf16[192,5120]{1,0:T(8,128)(2,1)S(1)} %get-tuple-element.78.refs_2_), custom_call_target="tpu_custom_call" | custom-call | flops 301989888 | bytes 4136960 | tf_op jit(solution)/shard_map/middle_grad/pallas_call | solution.py:324
  43.2 4.3 %collective-permute-start.9 = (bf16[64,576]{1,0:T(8,128)(2,1)S(1)}, bf16[64,576]{1,0:T(8,128)(2,1)S(1)}, u32[]{:S(2)}, u32[]{:S(2)}) collective-permute-start(bf16[64,576]{1,0:T(8,128)(2,1)S(1)} %get-tuple-element.79), channel_id=1, source_target_pairs={{0,2},{1,3},{2,0},{3,1},{7,5},{6,4},{5,7},{4,6},{8,10},{9,11},{10,... | collective-permute-start | bytes 221192 | tf_op jit(solution)/shard_map/ppermute | solution.py:373
  47.5 1.3 %collective-permute-start.17 = (bf16[64,4096]{1,0:T(8,128)(2,1)S(1)}, bf16[64,4096]{1,0:T(8,128)(2,1)S(1)}, u32[]{:S(2)}, u32[]{:S(2)}) collective-permute-start(bf16[64,4096]{1,0:T(8,128)(2,1)S(1)} %get-tuple-element.80.end_block), channel_id=1, source_target_pairs={{1,0},{2,3},{5,4},{6,7},{9,8},{10,11},{13,12},{14,15},{17,16},{18,... | collective-permute-start | bytes 1572872 | tf_op jit(solution)/shard_map/ppermute | solution.py:469
  48.8 3.0 %end_grad.1 = bf16[64,576]{1,0:T(8,128)(2,1)S(1)} custom-call(bf16[64,4096]{1,0:T(8,128)(2,1)S(1)} %get-tuple-element.80.end_block, bf16[64,5120]{1,0:T(8,128)(2,1)S(1)} %collective-permute-done.6.feat), custom_call_target="tpu_custom_call" | custom-call | flops 301989888 | bytes 1253376 | tf_op jit(solution)/shard_map/end_grad/pallas_call | solution.py:324
  51.8 1.3 %collective-permute-start.10 = (bf16[64,576]{1,0:T(8,128)(2,1)S(1)}, bf16[64,576]{1,0:T(8,128)(2,1)S(1)}, u32[]{:S(2)}, u32[]{:S(2)}) collective-permute-start(bf16[64,576]{1,0:T(8,128)(2,1)S(1)} %end_grad.1), channel_id=1, source_target_pairs={{1,3},{2,0},{5,7},{6,4},{9,11},{10,8},{13,15},{14,12},{17,19},{18,... | collective-permute-start | bytes 221192 | tf_op jit(solution)/shard_map/ppermute | solution.py:468
  53.1 0.0 collective-permute-done.7.ahead
  53.1 0.0 collective-permute-done.8.behind
  53.2 0.0 collective-permute-done.9.others
  53.2 6.0 %collective-permute-done.10.end = bf16[64,576]{1,0:T(8,128)(2,1)S(1)} collective-permute-done((bf16[64,576]{1,0:T(8,128)(2,1)S(1)}, bf16[64,576]{1,0:T(8,128)(2,1)S(1)}, u32[]{:S(2)}, u32[]{:S(2)}) %collective-permute-start.10) | collective-permute-done | bytes 73760 | tf_op jit(solution)/shard_map/ppermute | solution.py:468
  59.2 1.1 %collect.1 = (bf16[10,64,128]{2,1,0:T(8,128)(2,1)S(1)}, bf16[10,64,128]{2,1,0:T(8,128)(2,1)S(1)}) custom-call(s32[4]{0:T(128)S(1)} %pad_add_fusion.place, f32[64,128]{1,0:T(8,128)S(1)} %get-tuple-element.61.scale, bf16[9,64,256]{2,1,0:T(8,128)(2,1)S(1)} %get-tuple-element.72.whole_mod, bf16[64,576]{1,0:T(8,128)(2,1)S(1)} %get-tuple-element.73.own, ...), custom_call_target="tpu_custom_call" | custom-call | flops 3000000000 | bytes 1171472 | tf_op jit(solution)/shard_map/collect/pallas_call | solution.py:324
  60.2 0.9 %collective-permute-start.11 = (bf16[10,64,128]{2,1,0:T(8,128)(2,1)S(1)}, bf16[10,64,128]{2,1,0:T(8,128)(2,1)S(1)}, u32[]{:S(2)}, u32[]{:S(2)}) collective-permute-start(bf16[10,64,128]{2,1,0:T(8,128)(2,1)S(1)} %get-tuple-element.88), channel_id=1, source_target_pairs={{0,16},{16,0},{1,17},{17,1},{2,18},{18,2},{3,19},{19,3},{4,20},{20... | collective-permute-start | bytes 491528 | tf_op jit(solution)/shard_map/ppermute | solution.py:490
  61.1 0.0 collective-permute-start.15
  61.1 3.4 %collective-permute-start.16 = (bf16[64,576]{1,0:T(8,128)(2,1)S(1)}, bf16[64,576]{1,0:T(8,128)(2,1)S(1)}, u32[]{:S(2)}, u32[]{:S(2)}) collective-permute-start(bf16[64,576]{1,0:T(8,128)(2,1)S(1)} %get-tuple-element.91), channel_id=1, source_target_pairs={{0,3},{3,0},{4,7},{7,4},{8,11},{11,8},{12,15},{15,12},{16,19},{19,... | collective-permute-start | bytes 221192 | tf_op jit(solution)/shard_map/ppermute | solution.py:488
  64.5 1.1 %collective-permute-done.11.refs_1_ = bf16[10,64,128]{2,1,0:T(8,128)(2,1)S(1)} collective-permute-done((bf16[10,64,128]{2,1,0:T(8,128)(2,1)S(1)}, bf16[10,64,128]{2,1,0:T(8,128)(2,1)S(1)}, u32[]{:S(2)}, u32[]{:S(2)}) %collective-permute-start.11) | collective-permute-done | bytes 163872 | tf_op jit(solution)/shard_map/ppermute | solution.py:490
  65.6 0.2 row_sum.1.refs_0_
  65.8 0.1 collective-permute-start.12
  65.9 1.6 %collective-permute-start.13 = (bf16[11,64,128]{2,1,0:T(8,128)(2,1)S(1)}, bf16[11,64,128]{2,1,0:T(8,128)(2,1)S(1)}, u32[]{:S(2)}, u32[]{:S(2)}) collective-permute-start(bf16[11,64,128]{2,1,0:T(8,128)(2,1)S(1)} %row_sum.1.refs_0_), channel_id=1, source_target_pairs={{0,8},{4,12},{8,0},{12,4},{1,9},{5,13},{9,1},{13,5},{2,10},{6,14},... | collective-permute-start | bytes 540680 | tf_op jit(solution)/shard_map/ppermute | solution.py:341
  67.5 0.0 collective-permute-done.15.refs_0_
  67.5 1.4 %collective-permute-start.14 = (bf16[11,64,128]{2,1,0:T(8,128)(2,1)S(1)}, bf16[11,64,128]{2,1,0:T(8,128)(2,1)S(1)}, u32[]{:S(2)}, u32[]{:S(2)}) collective-permute-start(bf16[11,64,128]{2,1,0:T(8,128)(2,1)S(1)} %row_sum.1.refs_0_), channel_id=1, source_target_pairs={{0,12},{4,0},{8,4},{12,8},{1,13},{5,1},{9,5},{13,9},{2,14},{6,2},{... | collective-permute-start | bytes 540680 | tf_op jit(solution)/shard_map/ppermute | solution.py:341
  68.9 0.4 collective-permute-done.16.refs_1_
  69.3 0.0 collective-permute-done.17.far
  69.3 5.1 %input_grad.1 = (f32[64,4096]{1,0:T(8,128)S(1)}, f32[64,512]{1,0:T(8,128)S(1)}, f32[64,512]{1,0:T(8,128)S(1)}) custom-call(s32[4]{0:T(128)S(1)} %pad_add_fusion.place, bf16[64,4096]{1,0:T(8,128)(2,1)S(1)} %bitcast.29, bf16[64,4096]{1,0:T(8,128)(2,1)} %collective-permute-done.1.refs_1_.first, bf16[64,4096]{1,0:T(8,128)(2,1)} %collective-permute-done.2.refs_2_.second, ...), custom_call_target="tpu_custom_call" | custom-call | flops 2000000000 | bytes 4448272 | tf_op jit(solution)/shard_map/input_grad/pallas_call | solution.py:324
  74.4 0.0 collective-permute-done.12.refs_1_
  74.4 0.0 collective-permute-done.13.refs_2_
  74.4 1.2 %collective-permute-done.14.refs_3_ = bf16[11,64,128]{2,1,0:T(8,128)(2,1)S(1)} collective-permute-done((bf16[11,64,128]{2,1,0:T(8,128)(2,1)S(1)}, bf16[11,64,128]{2,1,0:T(8,128)(2,1)S(1)}, u32[]{:S(2)}, u32[]{:S(2)}) %collective-permute-start.14) | collective-permute-done | bytes 180256 | tf_op jit(solution)/shard_map/ppermute | solution.py:341
  75.7 0.9 %collective-permute-start.21 = (f32[64,512]{1,0:T(8,128)S(1)}, f32[64,512]{1,0:T(8,128)S(1)}, u32[]{:S(2)}, u32[]{:S(2)}) collective-permute-start(f32[64,512]{1,0:T(8,128)S(1)} %broadcast_select_fusion), channel_id=1, source_target_pairs={{0,16},{16,0},{1,17},{17,1},{2,18},{18,2},{3,19},{19,3},{4,20},{20... | collective-permute-start | bytes 393224 | tf_op jit(solution)/shard_map/ppermute | solution.py:348
  76.6 0.1 pad.1.clone
  76.6 2.8 %bank_grad.1 = (f32[4,9,64,128]{3,2,1,0:T(8,128)}, f32[4,128]{1,0:T(4,128)S(1)}, f32[4,512]{1,0:T(4,128)S(1)}) custom-call(s32[4]{0:T(128)S(1)} %pad_add_fusion.place, f32[4,9,64,128]{3,2,1,0:T(8,128)S(1)} %copy-done, bf16[11,64,128]{2,1,0:T(8,128)(2,1)S(1)} %row_sum.1.refs_0_, bf16[11,64,128]{2,1,0:T(8,128)(2,1)S(1)} %collective-permute-done.12.refs_1_, ...), custom_call_target="tpu_custom_call" | custom-call | flops 1000000 | bytes 3090448 | tf_op jit(solution)/shard_map/bank_grad/pallas_call | solution.py:324
  79.4 0.0 collective-permute-start.18
  79.4 2.2 %collective-permute-start.19 = (f32[4,128]{1,0:T(4,128)S(1)}, f32[4,128]{1,0:T(4,128)S(1)}, u32[]{:S(2)}, u32[]{:S(2)}) collective-permute-start(f32[4,128]{1,0:T(4,128)S(1)} %get-tuple-element.110.refs_0_), channel_id=1, source_target_pairs={{0,2},{1,3},{2,0},{3,1},{4,6},{5,7},{6,4},{7,5},{8,10},{9,11},{10,... | collective-permute-start | bytes 6152 | tf_op jit(solution)/shard_map/ppermute | solution.py:341
  81.6 1.6 %collective-permute-start.20 = (f32[4,128]{1,0:T(4,128)S(1)}, f32[4,128]{1,0:T(4,128)S(1)}, u32[]{:S(2)}, u32[]{:S(2)}) collective-permute-start(f32[4,128]{1,0:T(4,128)S(1)} %get-tuple-element.110.refs_0_), channel_id=1, source_target_pairs={{0,3},{1,0},{2,1},{3,2},{4,7},{5,4},{6,5},{7,6},{8,11},{9,8},{10,9... | collective-permute-start | bytes 6152 | tf_op jit(solution)/shard_map/ppermute | solution.py:341
  83.3 0.6 copy.15
  83.9 0.0 collective-permute-done.21
  83.9 0.1 copy.12
  84.1 0.1 copy.11
  84.2 1.1 %fusion = bf16[1,64,8,512]{3,2,1,0:T(8,128)(2,1)} fusion(f32[1,64,1,512]{3,2,1,0:T(1,128)S(1)} %copy.12, f32[1,64,1,512]{3,2,1,0:T(1,128)S(1)} %copy.11, f32[8]{0:T(128)S(1)} %pad.1.clone, f32[1,64,8,512]{3,2,1,0:T(8,128)S(1)} %bitcast.31), kind=kLoop, calls=%fused_computation.1 | loop fusion | flops 1048576 | bytes 1835040 | tf_op jit(solution)/shard_map/convert_element_type | solution.py:536
  85.3 0.0 collective-permute-done.18.refs_1_
  85.3 0.0 collective-permute-done.19.refs_2_
  85.3 0.1 collective-permute-done.20.refs_3_
  85.4 1.7 %affine.1 = (f32[512,128]{1,0:T(8,128)}, f32[1,128]{1,0:T(1,128)}) custom-call(s32[4]{0:T(128)S(1)} %pad_add_fusion.place, f32[4,512]{1,0:T(4,128)S(1)} %get-tuple-element.109.latents, f32[4,128]{1,0:T(4,128)S(1)} %get-tuple-element.110.refs_0_, f32[4,128]{1,0:T(4,128)S(1)} %collective-permute-done.18.refs_1_, f32[4,128]{1,0:T(4,128)S(1)} %collective-permute-done.19.refs_2_, ...), custom_call_target="tpu_custom_call" | custom-call | flops 1000000 | bytes 279056 | tf_op jit(solution)/shard_map/affine/pallas_call | solution.py:324
  (20 shorter events, 0.1 us)
Async XLA Ops:
  0.6 8.4 %copy-start.7 = (bf16[1,64,8,512]{3,2,1,0:T(8,128)(2,1)S(1)}, bf16[1,64,8,512]{3,2,1,0:T(8,128)(2,1)}, u32[]{:S(2)}) copy-start(bf16[1,64,8,512]{3,2,1,0:T(8,128)(2,1)} %param.7) | copy-start | bytes 1572868
  0.6 10.2 %copy-start = (f32[4,9,64,128]{3,2,1,0:T(8,128)S(1)}, f32[4,9,64,128]{3,2,1,0:T(8,128)}, u32[]{:S(2)}) copy-start(f32[4,9,64,128]{3,2,1,0:T(8,128)} %bank.1) | copy-start | bytes 3538948
  0.7 10.2 %copy-start.5 = (s32[1,4]{1,0:T(1,128)S(1)}, s32[1,4]{1,0:T(1,128)}, u32[]{:S(2)}) copy-start(s32[1,4]{1,0:T(1,128)} %refs_0_.1) | copy-start | bytes 52
  0.7 10.2 %copy-start.4 = (f32[1,512]{1,0:T(1,128)S(1)}, f32[1,512]{1,0:T(1,128)}, u32[]{:S(2)}) copy-start(f32[1,512]{1,0:T(1,128)} %refs_1_.1) | copy-start | bytes 6148
  0.7 10.2 %copy-start.6 = (f32[128]{0:T(128)S(1)}, f32[128]{0:T(128)}, u32[]{:S(2)}) copy-start(f32[128]{0:T(128)} %param.13) | copy-start | bytes 1540
  0.7 10.2 %copy-start.3 = (f32[512,128]{1,0:T(8,128)S(1)}, f32[512,128]{1,0:T(8,128)}, u32[]{:S(2)}) copy-start(f32[512,128]{1,0:T(8,128)} %refs_3_.1) | copy-start | bytes 786436
  2.0 19.7 %collective-permute-start.1 = (bf16[64,4096]{1,0:T(8,128)(2,1)S(1)}, bf16[64,4096]{1,0:T(8,128)(2,1)}, u32[]{:S(2)}, u32[]{:S(2)}) collective-permute-start(bf16[64,4096]{1,0:T(8,128)(2,1)S(1)} %bitcast.26), channel_id=1, source_target_pairs={{0,1},{1,2},{2,3},{7,6},{6,5},{5,4},{8,9},{9,10},{10,11},{15,14},{... | collective-permute-start | bytes 1572872 | tf_op jit(solution)/shard_map/ppermute | solution.py:373
  7.8 13.9 %collective-permute-start.2 = (bf16[64,4096]{1,0:T(8,128)(2,1)S(1)}, bf16[64,4096]{1,0:T(8,128)(2,1)}, u32[]{:S(2)}, u32[]{:S(2)}) collective-permute-start(bf16[64,4096]{1,0:T(8,128)(2,1)S(1)} %bitcast.27), channel_id=1, source_target_pairs={{1,0},{2,1},{3,2},{6,7},{5,6},{4,5},{9,8},{10,9},{11,10},{14,15},{... | collective-permute-start | bytes 1572872 | tf_op jit(solution)/shard_map/ppermute | solution.py:373
  9.3 4.3 %collective-permute-start.5 = (bf16[64,512]{1,0:T(8,128)(2,1)S(1)}, bf16[64,512]{1,0:T(8,128)(2,1)S(1)}, u32[]{:S(2)}, u32[]{:S(2)}) collective-permute-start(bf16[64,512]{1,0:T(8,128)(2,1)S(1)} %slice_select_fusion), channel_id=1, source_target_pairs={{0,16},{16,0},{1,17},{17,1},{2,18},{18,2},{3,19},{19,3},{4,20},{20... | collective-permute-start | bytes 196616 | tf_op jit(solution)/shard_map/ppermute | solution.py:348
  11.8 9.9 %copy-start.1 = (f32[10,64,128]{2,1,0:T(8,128)}, f32[10,64,128]{2,1,0:T(8,128)S(1)}, u32[]{:S(2)}) copy-start(f32[10,64,128]{2,1,0:T(8,128)S(1)} %get-tuple-element.60.refs_0_) | copy-start | bytes 983044
  11.8 9.9 %collective-permute-start = (f32[10,64,128]{2,1,0:T(8,128)S(1)}, f32[10,64,128]{2,1,0:T(8,128)}, u32[]{:S(2)}, u32[]{:S(2)}) collective-permute-start(f32[10,64,128]{2,1,0:T(8,128)S(1)} %get-tuple-element.60.refs_0_), channel_id=1, source_target_pairs={{0,16},{16,0},{1,17},{17,1},{2,18},{18,2},{3,19},{19,3},{4,20},{20... | collective-permute-start | bytes 983048 | tf_op jit(solution)/shard_map/ppermute | solution.py:341
  13.7 25.8 %collective-permute-start.6 = (bf16[64,5120]{1,0:T(8,128)(2,1)S(1)}, bf16[64,5120]{1,0:T(8,128)(2,1)S(1)}, u32[]{:S(2)}, u32[]{:S(2)}) collective-permute-start(bf16[64,5120]{1,0:T(8,128)(2,1)S(1)} %feat_rows.1.refs_3_), channel_id=1, source_target_pairs={{0,1},{3,2},{4,5},{7,6},{8,9},{11,10},{12,13},{15,14},{16,17},{19,... | collective-permute-start | bytes 1966088 | tf_op jit(solution)/shard_map/ppermute | solution.py:413
  21.7 17.7 %collective-permute-start.3 = (bf16[64,4096]{1,0:T(8,128)(2,1)}, bf16[64,4096]{1,0:T(8,128)(2,1)S(1)}, u32[]{:S(2)}, u32[]{:S(2)}) collective-permute-start(bf16[64,4096]{1,0:T(8,128)(2,1)} %collective-permute-done.1.refs_1_.first), channel_id=1, source_target_pairs={{1,2},{2,3},{6,5},{5,4},{9,10},{10,11},{14,13},{13,12},{17,18},{18... | collective-permute-start | bytes 1572872 | tf_op jit(solution)/shard_map/ppermute | solution.py:373
  22.4 17.0 %collective-permute-start.4 = (bf16[64,4096]{1,0:T(8,128)(2,1)}, bf16[64,4096]{1,0:T(8,128)(2,1)}, u32[]{:S(2)}, u32[]{:S(2)}) collective-permute-start(bf16[64,4096]{1,0:T(8,128)(2,1)} %collective-permute-done.2.refs_2_.second), channel_id=1, source_target_pairs={{1,0},{2,1},{6,7},{5,6},{9,8},{10,9},{14,15},{13,14},{17,16},{18,1... | collective-permute-start | bytes 1572872 | tf_op jit(solution)/shard_map/ppermute | solution.py:373
  23.8 1.0 %copy-start.2 = (f32[10,64,128]{2,1,0:T(8,128)S(1)}, f32[10,64,128]{2,1,0:T(8,128)}, u32[]{:S(2)}) copy-start(f32[10,64,128]{2,1,0:T(8,128)} %copy-done.1) | copy-start | bytes 983044
  30.6 22.6 %collective-permute-start.7 = (bf16[128,576]{1,0:T(8,128)(2,1)S(1)}, bf16[128,576]{1,0:T(8,128)(2,1)S(1)}, u32[]{:S(2)}, u32[]{:S(2)}) collective-permute-start(bf16[128,576]{1,0:T(8,128)(2,1)S(1)} %get-tuple-element.74), channel_id=1, source_target_pairs={{1,0},{2,1},{3,2},{6,7},{5,6},{4,5},{9,8},{10,9},{11,10},{14,15},{... | collective-permute-start | bytes 442376 | tf_op jit(solution)/shard_map/ppermute | solution.py:373
  31.9 21.3 %collective-permute-start.8 = (bf16[128,576]{1,0:T(8,128)(2,1)S(1)}, bf16[128,576]{1,0:T(8,128)(2,1)S(1)}, u32[]{:S(2)}, u32[]{:S(2)}) collective-permute-start(bf16[128,576]{1,0:T(8,128)(2,1)S(1)} %get-tuple-element.75), channel_id=1, source_target_pairs={{0,1},{1,2},{2,3},{7,6},{6,5},{5,4},{8,9},{9,10},{10,11},{15,14},{... | collective-permute-start | bytes 442376 | tf_op jit(solution)/shard_map/ppermute | solution.py:373
  43.2 10.0 %collective-permute-start.9 = (bf16[64,576]{1,0:T(8,128)(2,1)S(1)}, bf16[64,576]{1,0:T(8,128)(2,1)S(1)}, u32[]{:S(2)}, u32[]{:S(2)}) collective-permute-start(bf16[64,576]{1,0:T(8,128)(2,1)S(1)} %get-tuple-element.79), channel_id=1, source_target_pairs={{0,2},{1,3},{2,0},{3,1},{7,5},{6,4},{5,7},{4,6},{8,10},{9,11},{10,... | collective-permute-start | bytes 221192 | tf_op jit(solution)/shard_map/ppermute | solution.py:373
  47.5 21.7 %collective-permute-start.17 = (bf16[64,4096]{1,0:T(8,128)(2,1)S(1)}, bf16[64,4096]{1,0:T(8,128)(2,1)S(1)}, u32[]{:S(2)}, u32[]{:S(2)}) collective-permute-start(bf16[64,4096]{1,0:T(8,128)(2,1)S(1)} %get-tuple-element.80.end_block), channel_id=1, source_target_pairs={{1,0},{2,3},{5,4},{6,7},{9,8},{10,11},{13,12},{14,15},{17,16},{18,... | collective-permute-start | bytes 1572872 | tf_op jit(solution)/shard_map/ppermute | solution.py:469
  51.8 7.3 %collective-permute-start.10 = (bf16[64,576]{1,0:T(8,128)(2,1)S(1)}, bf16[64,576]{1,0:T(8,128)(2,1)S(1)}, u32[]{:S(2)}, u32[]{:S(2)}) collective-permute-start(bf16[64,576]{1,0:T(8,128)(2,1)S(1)} %end_grad.1), channel_id=1, source_target_pairs={{1,3},{2,0},{5,7},{6,4},{9,11},{10,8},{13,15},{14,12},{17,19},{18,... | collective-permute-start | bytes 221192 | tf_op jit(solution)/shard_map/ppermute | solution.py:468
  60.2 5.4 %collective-permute-start.11 = (bf16[10,64,128]{2,1,0:T(8,128)(2,1)S(1)}, bf16[10,64,128]{2,1,0:T(8,128)(2,1)S(1)}, u32[]{:S(2)}, u32[]{:S(2)}) collective-permute-start(bf16[10,64,128]{2,1,0:T(8,128)(2,1)S(1)} %get-tuple-element.88), channel_id=1, source_target_pairs={{0,16},{16,0},{1,17},{17,1},{2,18},{18,2},{3,19},{19,3},{4,20},{20... | collective-permute-start | bytes 491528 | tf_op jit(solution)/shard_map/ppermute | solution.py:490
  61.1 6.4 %collective-permute-start.15 = (bf16[64,576]{1,0:T(8,128)(2,1)S(1)}, bf16[64,576]{1,0:T(8,128)(2,1)S(1)}, u32[]{:S(2)}, u32[]{:S(2)}) collective-permute-start(bf16[64,576]{1,0:T(8,128)(2,1)S(1)} %get-tuple-element.90), channel_id=1, source_target_pairs={{0,2},{1,3},{2,0},{3,1},{7,5},{6,4},{5,7},{4,6},{8,10},{9,11},{10,... | collective-permute-start | bytes 221192 | tf_op jit(solution)/shard_map/ppermute | solution.py:373
  61.1 8.1 %collective-permute-start.16 = (bf16[64,576]{1,0:T(8,128)(2,1)S(1)}, bf16[64,576]{1,0:T(8,128)(2,1)S(1)}, u32[]{:S(2)}, u32[]{:S(2)}) collective-permute-start(bf16[64,576]{1,0:T(8,128)(2,1)S(1)} %get-tuple-element.91), channel_id=1, source_target_pairs={{0,3},{3,0},{4,7},{7,4},{8,11},{11,8},{12,15},{15,12},{16,19},{19,... | collective-permute-start | bytes 221192 | tf_op jit(solution)/shard_map/ppermute | solution.py:488
  65.8 8.5 %collective-permute-start.12 = (bf16[11,64,128]{2,1,0:T(8,128)(2,1)S(1)}, bf16[11,64,128]{2,1,0:T(8,128)(2,1)S(1)}, u32[]{:S(2)}, u32[]{:S(2)}) collective-permute-start(bf16[11,64,128]{2,1,0:T(8,128)(2,1)S(1)} %row_sum.1.refs_0_), channel_id=1, source_target_pairs={{0,4},{4,8},{8,12},{12,0},{1,5},{5,9},{9,13},{13,1},{2,6},{6,10},{... | collective-permute-start | bytes 540680 | tf_op jit(solution)/shard_map/ppermute | solution.py:341
  65.9 8.5 %collective-permute-start.13 = (bf16[11,64,128]{2,1,0:T(8,128)(2,1)S(1)}, bf16[11,64,128]{2,1,0:T(8,128)(2,1)S(1)}, u32[]{:S(2)}, u32[]{:S(2)}) collective-permute-start(bf16[11,64,128]{2,1,0:T(8,128)(2,1)S(1)} %row_sum.1.refs_0_), channel_id=1, source_target_pairs={{0,8},{4,12},{8,0},{12,4},{1,9},{5,13},{9,1},{13,5},{2,10},{6,14},... | collective-permute-start | bytes 540680 | tf_op jit(solution)/shard_map/ppermute | solution.py:341
  67.5 8.1 %collective-permute-start.14 = (bf16[11,64,128]{2,1,0:T(8,128)(2,1)S(1)}, bf16[11,64,128]{2,1,0:T(8,128)(2,1)S(1)}, u32[]{:S(2)}, u32[]{:S(2)}) collective-permute-start(bf16[11,64,128]{2,1,0:T(8,128)(2,1)S(1)} %row_sum.1.refs_0_), channel_id=1, source_target_pairs={{0,12},{4,0},{8,4},{12,8},{1,13},{5,1},{9,5},{13,9},{2,14},{6,2},{... | collective-permute-start | bytes 540680 | tf_op jit(solution)/shard_map/ppermute | solution.py:341
  75.7 8.2 %collective-permute-start.21 = (f32[64,512]{1,0:T(8,128)S(1)}, f32[64,512]{1,0:T(8,128)S(1)}, u32[]{:S(2)}, u32[]{:S(2)}) collective-permute-start(f32[64,512]{1,0:T(8,128)S(1)} %broadcast_select_fusion), channel_id=1, source_target_pairs={{0,16},{16,0},{1,17},{17,1},{2,18},{18,2},{3,19},{19,3},{4,20},{20... | collective-permute-start | bytes 393224 | tf_op jit(solution)/shard_map/ppermute | solution.py:348
  79.4 5.9 %collective-permute-start.18 = (f32[4,128]{1,0:T(4,128)S(1)}, f32[4,128]{1,0:T(4,128)S(1)}, u32[]{:S(2)}, u32[]{:S(2)}) collective-permute-start(f32[4,128]{1,0:T(4,128)S(1)} %get-tuple-element.110.refs_0_), channel_id=1, source_target_pairs={{0,1},{1,2},{2,3},{3,0},{4,5},{5,6},{6,7},{7,4},{8,9},{9,10},{10,1... | collective-permute-start | bytes 6152 | tf_op jit(solution)/shard_map/ppermute | solution.py:341
  79.4 5.9 %collective-permute-start.19 = (f32[4,128]{1,0:T(4,128)S(1)}, f32[4,128]{1,0:T(4,128)S(1)}, u32[]{:S(2)}, u32[]{:S(2)}) collective-permute-start(f32[4,128]{1,0:T(4,128)S(1)} %get-tuple-element.110.refs_0_), channel_id=1, source_target_pairs={{0,2},{1,3},{2,0},{3,1},{4,6},{5,7},{6,4},{7,5},{8,10},{9,11},{10,... | collective-permute-start | bytes 6152 | tf_op jit(solution)/shard_map/ppermute | solution.py:341
  81.6 3.8 %collective-permute-start.20 = (f32[4,128]{1,0:T(4,128)S(1)}, f32[4,128]{1,0:T(4,128)S(1)}, u32[]{:S(2)}, u32[]{:S(2)}) collective-permute-start(f32[4,128]{1,0:T(4,128)S(1)} %get-tuple-element.110.refs_0_), channel_id=1, source_target_pairs={{0,3},{1,0},{2,1},{3,2},{4,7},{5,4},{6,5},{7,6},{8,11},{9,8},{10,9... | collective-permute-start | bytes 6152 | tf_op jit(solution)/shard_map/ppermute | solution.py:341

commit v12 on v11

--- a/solution.py
+++ b/solution.py
@@ -12,7 +12,7 @@
 F32 = jnp.float32
 BF16 = jnp.bfloat16
 VMEM_LIMIT = 16 * 2**20
-COLLECT_FLOPS = 3 * 10**9
+COLLECT_FLOPS = 6 * 10**9
 INPUT_FLOPS = 2 * 10**9
 
 
@@ -466,6 +466,7 @@
     )
     from_others = along(grad_others, [(i, (i + 2) % size) for i in range(size)])
     from_end = lax.ppermute(grad_end, "chan", [(1, size - 1), (size - 2, 0)])
+    end_block, grad_end = lax.optimization_barrier((end_block, grad_end))
     far = lax.ppermute(end_block, "chan", [(1, 0), (size - 2, size - 1)])
     parts = call(
         functools.partial(collect_kernel, rows, size),

time: 87.6 us -> 87 us (level)
    ppermute x1, waiting for transfers between devices: 0.01 us -> 1.34 us  [on_device(): far = lax.ppermute(end_block, 'chan', [(1, 0), (size - 2, size - 1)])]
    ppermute x1, waiting for transfers between devices: 6.01 us -> 4.71 us  [on_device(): from_end = lax.ppermute(grad_end, 'chan', [(1, size - 1), (size - 2, 0)])]
    ppermute x7, waiting for transfers between devices: 4.03 us -> 2.91 us  [exchange(): lax.ppermute(x, axis, [(i, (i + s) % size) for i in range(size)])]
where the time goes in v12:
time: 87 us; the launch traced here: 86.5 us
  starting transfers between devices  44 us (51%)
  Pallas kernels  24.4 us (28%)
  waiting for transfers between devices  12.3 us (14%)
  local copies, waits for them, and re-layouts  3.49 us (4%)
  other arithmetic  1.27 us (1%)
  between operations  1.02 us (1%)
    pallas_call x11, Pallas kernels, call(): pl.pallas_call(kernel, out_shape=outs, in_specs=sspec(scalars) + vspec(le...  24.4 us
    ppermute x8, starting transfers between devices, along(): return lax.ppermute(x, ('samples', 'chan'), whole)  22.1 us
    ppermute x7, starting transfers between devices, exchange(): lax.ppermute(x, axis, [(i, (i + s) % size) for i in range(size)])  7.44 us
    ppermute x1, starting transfers between devices, on_device(): feat_end = lax.ppermute(feat, 'chan', [(0, 1), (size - 1, size - 2)])  5.29 us
    ppermute x1, waiting for transfers between devices, on_device(): from_end = lax.ppermute(grad_end, 'chan', [(1, size - 1), (size - 2, 0)])  4.71 us
    unnamed x19, local copies, waits for them, and re-layouts  3.13 us
    ppermute x7, waiting for transfers between devices, exchange(): lax.ppermute(x, axis, [(i, (i + s) % size) for i in range(size)])  2.91 us
    ppermute x2, starting transfers between devices, from_sides(): got = lax.ppermute(jnp.where(at == 0, last, first), axis, [(0, 1), (1, 0)])  2.84 us
  transfers between devices with their start and end apart: 22, of which 7 were waited for; matrix products, arithmetic and copies ran while one was open for 3% of the time, Pallas kernels for 26%

profile of v12, /device:TPU:0, one launch (start us, length us, event | category | flops | bytes accessed | tf_op | source)
XLA Modules:
  0.0 86.5 jit_solution(2957141609497888303)
XLA Ops:
  0.7 1.3 %copy.13 = bf16[8,8,8,512]{3,1,2,0:T(8,128)(2,1)S(1)} copy(bf16[8,8,8,512]{3,2,1,0:T(8,128)(2,1)} %bitcast.32) | data formatting | bytes 1048576
  2.0 5.7 %collective-permute-start.1 = (bf16[64,4096]{1,0:T(8,128)(2,1)S(1)}, bf16[64,4096]{1,0:T(8,128)(2,1)}, u32[]{:S(2)}, u32[]{:S(2)}) collective-permute-start(bf16[64,4096]{1,0:T(8,128)(2,1)S(1)} %bitcast.26), channel_id=1, source_target_pairs={{0,1},{1,2},{2,3},{7,6},{6,5},{5,4},{8,9},{9,10},{10,11},{15,14},{... | collective-permute-start | bytes 1572872 | tf_op jit(solution)/shard_map/ppermute | solution.py:373
  7.8 1.3 %collective-permute-start.2 = (bf16[64,4096]{1,0:T(8,128)(2,1)S(1)}, bf16[64,4096]{1,0:T(8,128)(2,1)}, u32[]{:S(2)}, u32[]{:S(2)}) collective-permute-start(bf16[64,4096]{1,0:T(8,128)(2,1)S(1)} %bitcast.27), channel_id=1, source_target_pairs={{1,0},{2,1},{3,2},{6,7},{5,6},{4,5},{9,8},{10,9},{11,10},{14,15},{... | collective-permute-start | bytes 1572872 | tf_op jit(solution)/shard_map/ppermute | solution.py:373
  9.1 0.2 copy.14
  9.3 1.6 %collective-permute-start.5 = (bf16[64,512]{1,0:T(8,128)(2,1)S(1)}, bf16[64,512]{1,0:T(8,128)(2,1)S(1)}, u32[]{:S(2)}, u32[]{:S(2)}) collective-permute-start(bf16[64,512]{1,0:T(8,128)(2,1)S(1)} %slice_select_fusion), channel_id=1, source_target_pairs={{0,16},{16,0},{1,17},{17,1},{2,18},{18,2},{3,19},{19,3},{4,20},{20... | collective-permute-start | bytes 196616 | tf_op jit(solution)/shard_map/ppermute | solution.py:348
  10.9 1.0 %plain.1 = (f32[10,64,128]{2,1,0:T(8,128)S(1)}, f32[8,128]{1,0:T(8,128)S(1)}) custom-call(s32[1,4]{1,0:T(1,128)S(1)} %copy-done.5, f32[1,512]{1,0:T(1,128)S(1)} %copy-done.4, f32[1,128]{1,0:T(1,128)S(1)} %bitcast.30, f32[512,128]{1,0:T(8,128)S(1)} %copy-done.3, f32[4,9,64,128]{3,2,1,0:T(8,128)S(1)} %copy-done), custom_call_target="tpu_custom_call" | custom-call | flops 1000000 | bytes 1776144 | tf_op jit(solution)/shard_map/plain/pallas_call | solution.py:324
  11.8 0.0 copy-start.1
  11.8 0.6 collective-permute-start
  12.4 1.2 %collective-permute-done.5 = bf16[64,512]{1,0:T(8,128)(2,1)S(1)} collective-permute-done((bf16[64,512]{1,0:T(8,128)(2,1)S(1)}, bf16[64,512]{1,0:T(8,128)(2,1)S(1)}, u32[]{:S(2)}, u32[]{:S(2)}) %collective-permute-start.5) | collective-permute-done | bytes 65568 | tf_op jit(solution)/shard_map/ppermute | solution.py:348
  13.7 5.3 %collective-permute-start.6 = (bf16[64,5120]{1,0:T(8,128)(2,1)S(1)}, bf16[64,5120]{1,0:T(8,128)(2,1)S(1)}, u32[]{:S(2)}, u32[]{:S(2)}) collective-permute-start(bf16[64,5120]{1,0:T(8,128)(2,1)S(1)} %feat_rows.1.refs_3_), channel_id=1, source_target_pairs={{0,1},{3,2},{4,5},{7,6},{8,9},{11,10},{12,13},{15,14},{16,17},{19,... | collective-permute-start | bytes 1966088 | tf_op jit(solution)/shard_map/ppermute | solution.py:413
  19.0 2.7 %collective-permute-done.refs_1_ = f32[10,64,128]{2,1,0:T(8,128)} collective-permute-done((f32[10,64,128]{2,1,0:T(8,128)S(1)}, f32[10,64,128]{2,1,0:T(8,128)}, u32[]{:S(2)}, u32[]{:S(2)}) %collective-permute-start) | collective-permute-done | bytes 327712 | tf_op jit(solution)/shard_map/ppermute | solution.py:341
  21.7 0.0 collective-permute-done.1.refs_1_.first
  21.7 0.0 collective-permute-done.2.refs_2_.second
  21.7 0.7 collective-permute-start.3
  22.4 1.3 %collective-permute-start.4 = (bf16[64,4096]{1,0:T(8,128)(2,1)}, bf16[64,4096]{1,0:T(8,128)(2,1)}, u32[]{:S(2)}, u32[]{:S(2)}) collective-permute-start(bf16[64,4096]{1,0:T(8,128)(2,1)} %collective-permute-done.2.refs_2_.second), channel_id=1, source_target_pairs={{1,0},{2,1},{6,7},{5,6},{9,8},{10,9},{14,15},{13,14},{17,16},{18,1... | collective-permute-start | bytes 1572872 | tf_op jit(solution)/shard_map/ppermute | solution.py:373
  23.7 0.1 pad_add_fusion.place
  23.8 1.0 %copy-done.2 = f32[10,64,128]{2,1,0:T(8,128)S(1)} copy-done((f32[10,64,128]{2,1,0:T(8,128)S(1)}, f32[10,64,128]{2,1,0:T(8,128)}, u32[]{:S(2)}) %copy-start.2) | copy-done | bytes 327704
  24.8 1.3 %mod_blocks.1 = (bf16[9,64,256]{2,1,0:T(8,128)(2,1)S(1)}, f32[64,128]{1,0:T(8,128)S(1)}, bf16[64,576]{1,0:T(8,128)(2,1)S(1)}, bf16[64,576]{1,0:T(8,128)(2,1)S(1)...) custom-call(s32[4]{0:T(128)S(1)} %pad_add_fusion.place, ...), custom_call_target="tpu_custom_call" | custom-call | flops 1000000 | bytes 1351696 | tf_op jit(solution)/shard_map/mod_blocks/pallas_call | solution.py:324
  26.0 4.5 %near_grad.1 = (bf16[64,576]{1,0:T(8,128)(2,1)S(1)}, bf16[128,576]{1,0:T(8,128)(2,1)S(1)}, bf16[128,576]{1,0:T(8,128)(2,1)S(1)}, bf16[192,5120]{1,0:T(8,128)(2,1)S(1)}) custom-call(bf16[64,4096]{1,0:T(8,128)(2,1)S(1)} %bitcast.28, bf16[64,4096]{1,0:T(8,128)(2,1)} %collective-permute-done.1.refs_1_.first, ...), custom_call_target="tpu_custom_call" | custom-call | flops 905969664 | bytes 4710400 | tf_op jit(solution)/shard_map/near_grad/pallas_call | solution.py:324
  30.6 1.3 %collective-permute-start.7 = (bf16[128,576]{1,0:T(8,128)(2,1)S(1)}, bf16[128,576]{1,0:T(8,128)(2,1)S(1)}, u32[]{:S(2)}, u32[]{:S(2)}) collective-permute-start(bf16[128,576]{1,0:T(8,128)(2,1)S(1)} %get-tuple-element.75), channel_id=1, source_target_pairs={{1,0},{2,1},{3,2},{6,7},{5,6},{4,5},{9,8},{10,9},{11,10},{14,15},{... | collective-permute-start | bytes 442376 | tf_op jit(solution)/shard_map/ppermute | solution.py:373
  31.9 7.5 %collective-permute-start.8 = (bf16[128,576]{1,0:T(8,128)(2,1)S(1)}, bf16[128,576]{1,0:T(8,128)(2,1)S(1)}, u32[]{:S(2)}, u32[]{:S(2)}) collective-permute-start(bf16[128,576]{1,0:T(8,128)(2,1)S(1)} %get-tuple-element.76), channel_id=1, source_target_pairs={{0,1},{1,2},{2,3},{7,6},{6,5},{5,4},{8,9},{9,10},{10,11},{15,14},{... | collective-permute-start | bytes 442376 | tf_op jit(solution)/shard_map/ppermute | solution.py:373
  39.4 0.0 collective-permute-done.6.feat
  39.4 0.0 collective-permute-done.3.refs_0_
  39.5 0.0 collective-permute-done.4.refs_1_
  39.5 3.7 %middle_grad.1 = (bf16[64,576]{1,0:T(8,128)(2,1)S(1)}, bf16[64,4096]{1,0:T(8,128)(2,1)S(1)}, bf16[64,4096]{1,0:T(8,128)(2,1)S(1)}) custom-call(bf16[64,4096]{1,0:T(8,128)(2,1)S(1)} %collective-permute-done.3.refs_0_, bf16[64,4096]{1,0:T(8,128)(2,1)} %collective-permute-done.4.refs_1_, bf16[192,5120]{1,0:T(8,128)(2,1)S(1)} %get-tuple-element.79.refs_2_), custom_call_target="tpu_custom_call" | custom-call | flops 301989888 | bytes 4136960 | tf_op jit(solution)/shard_map/middle_grad/pallas_call | solution.py:324
  43.2 4.3 %collective-permute-start.9 = (bf16[64,576]{1,0:T(8,128)(2,1)S(1)}, bf16[64,576]{1,0:T(8,128)(2,1)S(1)}, u32[]{:S(2)}, u32[]{:S(2)}) collective-permute-start(bf16[64,576]{1,0:T(8,128)(2,1)S(1)} %get-tuple-element.80), channel_id=1, source_target_pairs={{0,2},{1,3},{2,0},{3,1},{7,5},{6,4},{5,7},{4,6},{8,10},{9,11},{10,... | collective-permute-start | bytes 221192 | tf_op jit(solution)/shard_map/ppermute | solution.py:373
  47.5 3.0 %end_grad.1 = bf16[64,576]{1,0:T(8,128)(2,1)S(1)} custom-call(bf16[64,4096]{1,0:T(8,128)(2,1)S(1)} %get-tuple-element.93.end_block, bf16[64,5120]{1,0:T(8,128)(2,1)S(1)} %collective-permute-done.6.feat), custom_call_target="tpu_custom_call" | custom-call | flops 301989888 | bytes 1253376 | tf_op jit(solution)/shard_map/end_grad/pallas_call | solution.py:324
  50.5 1.3 %collective-permute-start.10 = (bf16[64,576]{1,0:T(8,128)(2,1)S(1)}, bf16[64,576]{1,0:T(8,128)(2,1)S(1)}, u32[]{:S(2)}, u32[]{:S(2)}) collective-permute-start(bf16[64,576]{1,0:T(8,128)(2,1)S(1)} %end_grad.1), channel_id=1, source_target_pairs={{1,3},{2,0},{5,7},{6,4},{9,11},{10,8},{13,15},{14,12},{17,19},{18,... | collective-permute-start | bytes 221192 | tf_op jit(solution)/shard_map/ppermute | solution.py:468
  51.8 1.3 %collective-permute-start.17 = (bf16[64,4096]{1,0:T(8,128)(2,1)S(1)}, bf16[64,4096]{1,0:T(8,128)(2,1)S(1)}, u32[]{:S(2)}, u32[]{:S(2)}) collective-permute-start(bf16[64,4096]{1,0:T(8,128)(2,1)S(1)} %get-tuple-element.93.end_block), channel_id=1, source_target_pairs={{1,0},{2,3},{5,4},{6,7},{9,8},{10,11},{13,12},{14,15},{17,16},{18,... | collective-permute-start | bytes 1572872 | tf_op jit(solution)/shard_map/ppermute | solution.py:470
  53.1 0.0 collective-permute-done.7.ahead
  53.2 0.0 collective-permute-done.8.behind
  53.2 0.0 collective-permute-done.9.others
  53.2 4.7 %collective-permute-done.10.end = bf16[64,576]{1,0:T(8,128)(2,1)S(1)} collective-permute-done((bf16[64,576]{1,0:T(8,128)(2,1)S(1)}, bf16[64,576]{1,0:T(8,128)(2,1)S(1)}, u32[]{:S(2)}, u32[]{:S(2)}) %collective-permute-start.10) | collective-permute-done | bytes 73760 | tf_op jit(solution)/shard_map/ppermute | solution.py:468
  57.9 1.1 %collect.1 = (bf16[10,64,128]{2,1,0:T(8,128)(2,1)S(1)}, bf16[10,64,128]{2,1,0:T(8,128)(2,1)S(1)}) custom-call(s32[4]{0:T(128)S(1)} %pad_add_fusion.place, f32[64,128]{1,0:T(8,128)S(1)} %get-tuple-element.62.scale, bf16[9,64,256]{2,1,0:T(8,128)(2,1)S(1)} %get-tuple-element.73.whole_mod, bf16[64,576]{1,0:T(8,128)(2,1)S(1)} %get-tuple-element.74.own, ...), custom_call_target="tpu_custom_call" | custom-call | flops 6000000000 | bytes 1171472 | tf_op jit(solution)/shard_map/collect/pallas_call | solution.py:324
  58.9 0.9 %collective-permute-start.11 = (bf16[10,64,128]{2,1,0:T(8,128)(2,1)S(1)}, bf16[10,64,128]{2,1,0:T(8,128)(2,1)S(1)}, u32[]{:S(2)}, u32[]{:S(2)}) collective-permute-start(bf16[10,64,128]{2,1,0:T(8,128)(2,1)S(1)} %get-tuple-element.89), channel_id=1, source_target_pairs={{0,16},{16,0},{1,17},{17,1},{2,18},{18,2},{3,19},{19,3},{4,20},{20... | collective-permute-start | bytes 491528 | tf_op jit(solution)/shard_map/ppermute | solution.py:491
  59.9 0.0 collective-permute-start.15
  59.9 2.8 %collective-permute-start.16 = (bf16[64,576]{1,0:T(8,128)(2,1)S(1)}, bf16[64,576]{1,0:T(8,128)(2,1)S(1)}, u32[]{:S(2)}, u32[]{:S(2)}) collective-permute-start(bf16[64,576]{1,0:T(8,128)(2,1)S(1)} %get-tuple-element.92), channel_id=1, source_target_pairs={{0,3},{3,0},{4,7},{7,4},{8,11},{11,8},{12,15},{15,12},{16,19},{19,... | collective-permute-start | bytes 221192 | tf_op jit(solution)/shard_map/ppermute | solution.py:489
  62.7 1.7 %collective-permute-done.11.refs_1_ = bf16[10,64,128]{2,1,0:T(8,128)(2,1)S(1)} collective-permute-done((bf16[10,64,128]{2,1,0:T(8,128)(2,1)S(1)}, bf16[10,64,128]{2,1,0:T(8,128)(2,1)S(1)}, u32[]{:S(2)}, u32[]{:S(2)}) %collective-permute-start.11) | collective-permute-done | bytes 163872 | tf_op jit(solution)/shard_map/ppermute | solution.py:491
  64.3 0.2 row_sum.1.refs_0_
  64.5 0.1 collective-permute-start.12
  64.6 1.6 %collective-permute-start.13 = (bf16[11,64,128]{2,1,0:T(8,128)(2,1)S(1)}, bf16[11,64,128]{2,1,0:T(8,128)(2,1)S(1)}, u32[]{:S(2)}, u32[]{:S(2)}) collective-permute-start(bf16[11,64,128]{2,1,0:T(8,128)(2,1)S(1)} %row_sum.1.refs_0_), channel_id=1, source_target_pairs={{0,8},{4,12},{8,0},{12,4},{1,9},{5,13},{9,1},{13,5},{2,10},{6,14},... | collective-permute-start | bytes 540680 | tf_op jit(solution)/shard_map/ppermute | solution.py:341
  66.2 0.0 collective-permute-done.15.refs_0_
  66.2 1.4 %collective-permute-start.14 = (bf16[11,64,128]{2,1,0:T(8,128)(2,1)S(1)}, bf16[11,64,128]{2,1,0:T(8,128)(2,1)S(1)}, u32[]{:S(2)}, u32[]{:S(2)}) collective-permute-start(bf16[11,64,128]{2,1,0:T(8,128)(2,1)S(1)} %row_sum.1.refs_0_), channel_id=1, source_target_pairs={{0,12},{4,0},{8,4},{12,8},{1,13},{5,1},{9,5},{13,9},{2,14},{6,2},{... | collective-permute-start | bytes 540680 | tf_op jit(solution)/shard_map/ppermute | solution.py:341
  67.6 0.5 collective-permute-done.16.refs_1_
  68.1 1.3 %collective-permute-done.17.far = bf16[64,4096]{1,0:T(8,128)(2,1)S(1)} collective-permute-done((bf16[64,4096]{1,0:T(8,128)(2,1)S(1)}, bf16[64,4096]{1,0:T(8,128)(2,1)S(1)}, u32[]{:S(2)}, u32[]{:S(2)}) %collective-permute-start.17) | collective-permute-done | bytes 524320 | tf_op jit(solution)/shard_map/ppermute | solution.py:470
  69.4 5.1 %input_grad.1 = (f32[64,4096]{1,0:T(8,128)S(1)}, f32[64,512]{1,0:T(8,128)S(1)}, f32[64,512]{1,0:T(8,128)S(1)}) custom-call(s32[4]{0:T(128)S(1)} %pad_add_fusion.place, bf16[64,4096]{1,0:T(8,128)(2,1)S(1)} %bitcast.29, bf16[64,4096]{1,0:T(8,128)(2,1)} %collective-permute-done.1.refs_1_.first, bf16[64,4096]{1,0:T(8,128)(2,1)} %collective-permute-done.2.refs_2_.second, ...), custom_call_target="tpu_custom_call" | custom-call | flops 2000000000 | bytes 4448272 | tf_op jit(solution)/shard_map/input_grad/pallas_call | solution.py:324
  74.6 0.0 collective-permute-done.12.refs_1_
  74.6 0.0 collective-permute-done.13.refs_2_
  74.6 0.0 collective-permute-done.14.refs_3_
  74.6 1.3 %collective-permute-start.21 = (f32[64,512]{1,0:T(8,128)S(1)}, f32[64,512]{1,0:T(8,128)S(1)}, u32[]{:S(2)}, u32[]{:S(2)}) collective-permute-start(f32[64,512]{1,0:T(8,128)S(1)} %broadcast_select_fusion), channel_id=1, source_target_pairs={{0,16},{16,0},{1,17},{17,1},{2,18},{18,2},{3,19},{19,3},{4,20},{20... | collective-permute-start | bytes 393224 | tf_op jit(solution)/shard_map/ppermute | solution.py:348
  75.9 0.1 pad.1.clone
  76.0 2.8 %bank_grad.1 = (f32[4,9,64,128]{3,2,1,0:T(8,128)}, f32[4,128]{1,0:T(4,128)S(1)}, f32[4,512]{1,0:T(4,128)S(1)}) custom-call(s32[4]{0:T(128)S(1)} %pad_add_fusion.place, f32[4,9,64,128]{3,2,1,0:T(8,128)S(1)} %copy-done, bf16[11,64,128]{2,1,0:T(8,128)(2,1)S(1)} %row_sum.1.refs_0_, bf16[11,64,128]{2,1,0:T(8,128)(2,1)S(1)} %collective-permute-done.12.refs_1_, ...), custom_call_target="tpu_custom_call" | custom-call | flops 1000000 | bytes 3090448 | tf_op jit(solution)/shard_map/bank_grad/pallas_call | solution.py:324
  78.8 0.0 collective-permute-start.18
  78.8 2.5 %collective-permute-start.19 = (f32[4,128]{1,0:T(4,128)S(1)}, f32[4,128]{1,0:T(4,128)S(1)}, u32[]{:S(2)}, u32[]{:S(2)}) collective-permute-start(f32[4,128]{1,0:T(4,128)S(1)} %get-tuple-element.112.refs_0_), channel_id=1, source_target_pairs={{0,2},{1,3},{2,0},{3,1},{4,6},{5,7},{6,4},{7,5},{8,10},{9,11},{10,... | collective-permute-start | bytes 6152 | tf_op jit(solution)/shard_map/ppermute | solution.py:341
  81.3 1.4 %collective-permute-start.20 = (f32[4,128]{1,0:T(4,128)S(1)}, f32[4,128]{1,0:T(4,128)S(1)}, u32[]{:S(2)}, u32[]{:S(2)}) collective-permute-start(f32[4,128]{1,0:T(4,128)S(1)} %get-tuple-element.112.refs_0_), channel_id=1, source_target_pairs={{0,3},{1,0},{2,1},{3,2},{4,7},{5,4},{6,5},{7,6},{8,11},{9,8},{10,9... | collective-permute-start | bytes 6152 | tf_op jit(solution)/shard_map/ppermute | solution.py:341
  82.6 0.6 copy.15
  83.2 0.0 collective-permute-done.21
  83.3 0.1 copy.12
  83.4 0.1 copy.11
  83.6 1.1 %fusion = bf16[1,64,8,512]{3,2,1,0:T(8,128)(2,1)} fusion(f32[1,64,1,512]{3,2,1,0:T(1,128)S(1)} %copy.12, f32[1,64,1,512]{3,2,1,0:T(1,128)S(1)} %copy.11, f32[8]{0:T(128)S(1)} %pad.1.clone, f32[1,64,8,512]{3,2,1,0:T(8,128)S(1)} %bitcast.31), kind=kLoop, calls=%fused_computation.1 | loop fusion | flops 1048576 | bytes 1835040 | tf_op jit(solution)/shard_map/convert_element_type | solution.py:537
  84.7 0.0 collective-permute-done.18.refs_1_
  84.7 0.0 collective-permute-done.19.refs_2_
  84.7 0.2 collective-permute-done.20.refs_3_
  84.8 1.7 %affine.1 = (f32[512,128]{1,0:T(8,128)}, f32[1,128]{1,0:T(1,128)}) custom-call(s32[4]{0:T(128)S(1)} %pad_add_fusion.place, f32[4,512]{1,0:T(4,128)S(1)} %get-tuple-element.111.latents, f32[4,128]{1,0:T(4,128)S(1)} %get-tuple-element.112.refs_0_, f32[4,128]{1,0:T(4,128)S(1)} %collective-permute-done.18.refs_1_, f32[4,128]{1,0:T(4,128)S(1)} %collective-permute-done.19.refs_2_, ...), custom_call_target="tpu_custom_call" | custom-call | flops 1000000 | bytes 279056 | tf_op jit(solution)/shard_map/affine/pallas_call | solution.py:324
  (20 shorter events, 0.1 us)
Async XLA Ops:
  0.6 8.4 %copy-start.7 = (bf16[1,64,8,512]{3,2,1,0:T(8,128)(2,1)S(1)}, bf16[1,64,8,512]{3,2,1,0:T(8,128)(2,1)}, u32[]{:S(2)}) copy-start(bf16[1,64,8,512]{3,2,1,0:T(8,128)(2,1)} %param.7) | copy-start | bytes 1572868
  0.6 10.2 %copy-start = (f32[4,9,64,128]{3,2,1,0:T(8,128)S(1)}, f32[4,9,64,128]{3,2,1,0:T(8,128)}, u32[]{:S(2)}) copy-start(f32[4,9,64,128]{3,2,1,0:T(8,128)} %bank.1) | copy-start | bytes 3538948
  0.7 10.2 %copy-start.5 = (s32[1,4]{1,0:T(1,128)S(1)}, s32[1,4]{1,0:T(1,128)}, u32[]{:S(2)}) copy-start(s32[1,4]{1,0:T(1,128)} %refs_0_.1) | copy-start | bytes 52
  0.7 10.2 %copy-start.4 = (f32[1,512]{1,0:T(1,128)S(1)}, f32[1,512]{1,0:T(1,128)}, u32[]{:S(2)}) copy-start(f32[1,512]{1,0:T(1,128)} %refs_1_.1) | copy-start | bytes 6148
  0.7 10.2 %copy-start.6 = (f32[128]{0:T(128)S(1)}, f32[128]{0:T(128)}, u32[]{:S(2)}) copy-start(f32[128]{0:T(128)} %param.13) | copy-start | bytes 1540
  0.7 10.2 %copy-start.3 = (f32[512,128]{1,0:T(8,128)S(1)}, f32[512,128]{1,0:T(8,128)}, u32[]{:S(2)}) copy-start(f32[512,128]{1,0:T(8,128)} %refs_3_.1) | copy-start | bytes 786436
  2.0 19.7 %collective-permute-start.1 = (bf16[64,4096]{1,0:T(8,128)(2,1)S(1)}, bf16[64,4096]{1,0:T(8,128)(2,1)}, u32[]{:S(2)}, u32[]{:S(2)}) collective-permute-start(bf16[64,4096]{1,0:T(8,128)(2,1)S(1)} %bitcast.26), channel_id=1, source_target_pairs={{0,1},{1,2},{2,3},{7,6},{6,5},{5,4},{8,9},{9,10},{10,11},{15,14},{... | collective-permute-start | bytes 1572872 | tf_op jit(solution)/shard_map/ppermute | solution.py:373
  7.8 13.9 %collective-permute-start.2 = (bf16[64,4096]{1,0:T(8,128)(2,1)S(1)}, bf16[64,4096]{1,0:T(8,128)(2,1)}, u32[]{:S(2)}, u32[]{:S(2)}) collective-permute-start(bf16[64,4096]{1,0:T(8,128)(2,1)S(1)} %bitcast.27), channel_id=1, source_target_pairs={{1,0},{2,1},{3,2},{6,7},{5,6},{4,5},{9,8},{10,9},{11,10},{14,15},{... | collective-permute-start | bytes 1572872 | tf_op jit(solution)/shard_map/ppermute | solution.py:373
  9.3 4.3 %collective-permute-start.5 = (bf16[64,512]{1,0:T(8,128)(2,1)S(1)}, bf16[64,512]{1,0:T(8,128)(2,1)S(1)}, u32[]{:S(2)}, u32[]{:S(2)}) collective-permute-start(bf16[64,512]{1,0:T(8,128)(2,1)S(1)} %slice_select_fusion), channel_id=1, source_target_pairs={{0,16},{16,0},{1,17},{17,1},{2,18},{18,2},{3,19},{19,3},{4,20},{20... | collective-permute-start | bytes 196616 | tf_op jit(solution)/shard_map/ppermute | solution.py:348
  11.8 9.9 %copy-start.1 = (f32[10,64,128]{2,1,0:T(8,128)}, f32[10,64,128]{2,1,0:T(8,128)S(1)}, u32[]{:S(2)}) copy-start(f32[10,64,128]{2,1,0:T(8,128)S(1)} %get-tuple-element.61.refs_0_) | copy-start | bytes 983044
  11.8 9.9 %collective-permute-start = (f32[10,64,128]{2,1,0:T(8,128)S(1)}, f32[10,64,128]{2,1,0:T(8,128)}, u32[]{:S(2)}, u32[]{:S(2)}) collective-permute-start(f32[10,64,128]{2,1,0:T(8,128)S(1)} %get-tuple-element.61.refs_0_), channel_id=1, source_target_pairs={{0,16},{16,0},{1,17},{17,1},{2,18},{18,2},{3,19},{19,3},{4,20},{20... | collective-permute-start | bytes 983048 | tf_op jit(solution)/shard_map/ppermute | solution.py:341
  13.7 25.8 %collective-permute-start.6 = (bf16[64,5120]{1,0:T(8,128)(2,1)S(1)}, bf16[64,5120]{1,0:T(8,128)(2,1)S(1)}, u32[]{:S(2)}, u32[]{:S(2)}) collective-permute-start(bf16[64,5120]{1,0:T(8,128)(2,1)S(1)} %feat_rows.1.refs_3_), channel_id=1, source_target_pairs={{0,1},{3,2},{4,5},{7,6},{8,9},{11,10},{12,13},{15,14},{16,17},{19,... | collective-permute-start | bytes 1966088 | tf_op jit(solution)/shard_map/ppermute | solution.py:413
  21.7 17.7 %collective-permute-start.3 = (bf16[64,4096]{1,0:T(8,128)(2,1)}, bf16[64,4096]{1,0:T(8,128)(2,1)S(1)}, u32[]{:S(2)}, u32[]{:S(2)}) collective-permute-start(bf16[64,4096]{1,0:T(8,128)(2,1)} %collective-permute-done.1.refs_1_.first), channel_id=1, source_target_pairs={{1,2},{2,3},{6,5},{5,4},{9,10},{10,11},{14,13},{13,12},{17,18},{18... | collective-permute-start | bytes 1572872 | tf_op jit(solution)/shard_map/ppermute | solution.py:373
  22.4 17.0 %collective-permute-start.4 = (bf16[64,4096]{1,0:T(8,128)(2,1)}, bf16[64,4096]{1,0:T(8,128)(2,1)}, u32[]{:S(2)}, u32[]{:S(2)}) collective-permute-start(bf16[64,4096]{1,0:T(8,128)(2,1)} %collective-permute-done.2.refs_2_.second), channel_id=1, source_target_pairs={{1,0},{2,1},{6,7},{5,6},{9,8},{10,9},{14,15},{13,14},{17,16},{18,1... | collective-permute-start | bytes 1572872 | tf_op jit(solution)/shard_map/ppermute | solution.py:373
  23.8 1.0 %copy-start.2 = (f32[10,64,128]{2,1,0:T(8,128)S(1)}, f32[10,64,128]{2,1,0:T(8,128)}, u32[]{:S(2)}) copy-start(f32[10,64,128]{2,1,0:T(8,128)} %copy-done.1) | copy-start | bytes 983044
  30.6 22.6 %collective-permute-start.7 = (bf16[128,576]{1,0:T(8,128)(2,1)S(1)}, bf16[128,576]{1,0:T(8,128)(2,1)S(1)}, u32[]{:S(2)}, u32[]{:S(2)}) collective-permute-start(bf16[128,576]{1,0:T(8,128)(2,1)S(1)} %get-tuple-element.75), channel_id=1, source_target_pairs={{1,0},{2,1},{3,2},{6,7},{5,6},{4,5},{9,8},{10,9},{11,10},{14,15},{... | collective-permute-start | bytes 442376 | tf_op jit(solution)/shard_map/ppermute | solution.py:373
  31.9 21.3 %collective-permute-start.8 = (bf16[128,576]{1,0:T(8,128)(2,1)S(1)}, bf16[128,576]{1,0:T(8,128)(2,1)S(1)}, u32[]{:S(2)}, u32[]{:S(2)}) collective-permute-start(bf16[128,576]{1,0:T(8,128)(2,1)S(1)} %get-tuple-element.76), channel_id=1, source_target_pairs={{0,1},{1,2},{2,3},{7,6},{6,5},{5,4},{8,9},{9,10},{10,11},{15,14},{... | collective-permute-start | bytes 442376 | tf_op jit(solution)/shard_map/ppermute | solution.py:373
  43.2 10.0 %collective-permute-start.9 = (bf16[64,576]{1,0:T(8,128)(2,1)S(1)}, bf16[64,576]{1,0:T(8,128)(2,1)S(1)}, u32[]{:S(2)}, u32[]{:S(2)}) collective-permute-start(bf16[64,576]{1,0:T(8,128)(2,1)S(1)} %get-tuple-element.80), channel_id=1, source_target_pairs={{0,2},{1,3},{2,0},{3,1},{7,5},{6,4},{5,7},{4,6},{8,10},{9,11},{10,... | collective-permute-start | bytes 221192 | tf_op jit(solution)/shard_map/ppermute | solution.py:373
  50.5 7.3 %collective-permute-start.10 = (bf16[64,576]{1,0:T(8,128)(2,1)S(1)}, bf16[64,576]{1,0:T(8,128)(2,1)S(1)}, u32[]{:S(2)}, u32[]{:S(2)}) collective-permute-start(bf16[64,576]{1,0:T(8,128)(2,1)S(1)} %end_grad.1), channel_id=1, source_target_pairs={{1,3},{2,0},{5,7},{6,4},{9,11},{10,8},{13,15},{14,12},{17,19},{18,... | collective-permute-start | bytes 221192 | tf_op jit(solution)/shard_map/ppermute | solution.py:468
  51.8 17.6 %collective-permute-start.17 = (bf16[64,4096]{1,0:T(8,128)(2,1)S(1)}, bf16[64,4096]{1,0:T(8,128)(2,1)S(1)}, u32[]{:S(2)}, u32[]{:S(2)}) collective-permute-start(bf16[64,4096]{1,0:T(8,128)(2,1)S(1)} %get-tuple-element.93.end_block), channel_id=1, source_target_pairs={{1,0},{2,3},{5,4},{6,7},{9,8},{10,11},{13,12},{14,15},{17,16},{18,... | collective-permute-start | bytes 1572872 | tf_op jit(solution)/shard_map/ppermute | solution.py:470
  58.9 5.4 %collective-permute-start.11 = (bf16[10,64,128]{2,1,0:T(8,128)(2,1)S(1)}, bf16[10,64,128]{2,1,0:T(8,128)(2,1)S(1)}, u32[]{:S(2)}, u32[]{:S(2)}) collective-permute-start(bf16[10,64,128]{2,1,0:T(8,128)(2,1)S(1)} %get-tuple-element.89), channel_id=1, source_target_pairs={{0,16},{16,0},{1,17},{17,1},{2,18},{18,2},{3,19},{19,3},{4,20},{20... | collective-permute-start | bytes 491528 | tf_op jit(solution)/shard_map/ppermute | solution.py:491
  59.9 6.3 %collective-permute-start.15 = (bf16[64,576]{1,0:T(8,128)(2,1)S(1)}, bf16[64,576]{1,0:T(8,128)(2,1)S(1)}, u32[]{:S(2)}, u32[]{:S(2)}) collective-permute-start(bf16[64,576]{1,0:T(8,128)(2,1)S(1)} %get-tuple-element.91), channel_id=1, source_target_pairs={{0,2},{1,3},{2,0},{3,1},{7,5},{6,4},{5,7},{4,6},{8,10},{9,11},{10,... | collective-permute-start | bytes 221192 | tf_op jit(solution)/shard_map/ppermute | solution.py:373
  59.9 8.2 %collective-permute-start.16 = (bf16[64,576]{1,0:T(8,128)(2,1)S(1)}, bf16[64,576]{1,0:T(8,128)(2,1)S(1)}, u32[]{:S(2)}, u32[]{:S(2)}) collective-permute-start(bf16[64,576]{1,0:T(8,128)(2,1)S(1)} %get-tuple-element.92), channel_id=1, source_target_pairs={{0,3},{3,0},{4,7},{7,4},{8,11},{11,8},{12,15},{15,12},{16,19},{19,... | collective-permute-start | bytes 221192 | tf_op jit(solution)/shard_map/ppermute | solution.py:489
  64.5 10.0 %collective-permute-start.12 = (bf16[11,64,128]{2,1,0:T(8,128)(2,1)S(1)}, bf16[11,64,128]{2,1,0:T(8,128)(2,1)S(1)}, u32[]{:S(2)}, u32[]{:S(2)}) collective-permute-start(bf16[11,64,128]{2,1,0:T(8,128)(2,1)S(1)} %row_sum.1.refs_0_), channel_id=1, source_target_pairs={{0,4},{4,8},{8,12},{12,0},{1,5},{5,9},{9,13},{13,1},{2,6},{6,10},{... | collective-permute-start | bytes 540680 | tf_op jit(solution)/shard_map/ppermute | solution.py:341
  64.6 10.0 %collective-permute-start.13 = (bf16[11,64,128]{2,1,0:T(8,128)(2,1)S(1)}, bf16[11,64,128]{2,1,0:T(8,128)(2,1)S(1)}, u32[]{:S(2)}, u32[]{:S(2)}) collective-permute-start(bf16[11,64,128]{2,1,0:T(8,128)(2,1)S(1)} %row_sum.1.refs_0_), channel_id=1, source_target_pairs={{0,8},{4,12},{8,0},{12,4},{1,9},{5,13},{9,1},{13,5},{2,10},{6,14},... | collective-permute-start | bytes 540680 | tf_op jit(solution)/shard_map/ppermute | solution.py:341
  66.2 8.4 %collective-permute-start.14 = (bf16[11,64,128]{2,1,0:T(8,128)(2,1)S(1)}, bf16[11,64,128]{2,1,0:T(8,128)(2,1)S(1)}, u32[]{:S(2)}, u32[]{:S(2)}) collective-permute-start(bf16[11,64,128]{2,1,0:T(8,128)(2,1)S(1)} %row_sum.1.refs_0_), channel_id=1, source_target_pairs={{0,12},{4,0},{8,4},{12,8},{1,13},{5,1},{9,5},{13,9},{2,14},{6,2},{... | collective-permute-start | bytes 540680 | tf_op jit(solution)/shard_map/ppermute | solution.py:341
  74.6 8.6 %collective-permute-start.21 = (f32[64,512]{1,0:T(8,128)S(1)}, f32[64,512]{1,0:T(8,128)S(1)}, u32[]{:S(2)}, u32[]{:S(2)}) collective-permute-start(f32[64,512]{1,0:T(8,128)S(1)} %broadcast_select_fusion), channel_id=1, source_target_pairs={{0,16},{16,0},{1,17},{17,1},{2,18},{18,2},{3,19},{19,3},{4,20},{20... | collective-permute-start | bytes 393224 | tf_op jit(solution)/shard_map/ppermute | solution.py:348
  78.8 5.9 %collective-permute-start.18 = (f32[4,128]{1,0:T(4,128)S(1)}, f32[4,128]{1,0:T(4,128)S(1)}, u32[]{:S(2)}, u32[]{:S(2)}) collective-permute-start(f32[4,128]{1,0:T(4,128)S(1)} %get-tuple-element.112.refs_0_), channel_id=1, source_target_pairs={{0,1},{1,2},{2,3},{3,0},{4,5},{5,6},{6,7},{7,4},{8,9},{9,10},{10,1... | collective-permute-start | bytes 6152 | tf_op jit(solution)/shard_map/ppermute | solution.py:341
  78.8 5.9 %collective-permute-start.19 = (f32[4,128]{1,0:T(4,128)S(1)}, f32[4,128]{1,0:T(4,128)S(1)}, u32[]{:S(2)}, u32[]{:S(2)}) collective-permute-start(f32[4,128]{1,0:T(4,128)S(1)} %get-tuple-element.112.refs_0_), channel_id=1, source_target_pairs={{0,2},{1,3},{2,0},{3,1},{4,6},{5,7},{6,4},{7,5},{8,10},{9,11},{10,... | collective-permute-start | bytes 6152 | tf_op jit(solution)/shard_map/ppermute | solution.py:341
  81.3 3.6 %collective-permute-start.20 = (f32[4,128]{1,0:T(4,128)S(1)}, f32[4,128]{1,0:T(4,128)S(1)}, u32[]{:S(2)}, u32[]{:S(2)}) collective-permute-start(f32[4,128]{1,0:T(4,128)S(1)} %get-tuple-element.112.refs_0_), channel_id=1, source_target_pairs={{0,3},{1,0},{2,1},{3,2},{4,7},{5,4},{6,5},{7,6},{8,11},{9,8},{10,9... | collective-permute-start | bytes 6152 | tf_op jit(solution)/shard_map/ppermute | solution.py:341

commit v13 on v12

--- a/solution.py
+++ b/solution.py
@@ -135,17 +135,20 @@
     return [jnp.concatenate([total[kh] for kh in range(3)], axis=1).astype(BF16) for total in totals]
 
 
+def own_grad_kernel(height, width, cotan, feat, out, wide, total):
+    for row in range(height + 2):
+        spread(wide, row, feat[:, row * width : (row + 1) * width])
+    (out[...],) = tap_products(cotan, [wide], [total], height, width)
+
+
 def near_grad_kernel(height, width, *refs):
-    cotans, feat, mods, (own, behind, ahead), (wide, gathered, total) = refs[:3], refs[3], refs[4:6], refs[6:9], refs[9:]
-    ch = feat.shape[0]
+    cotans, wide, mods, outs, (gathered, total) = refs[:2], refs[2], refs[3:5], refs[5:7], refs[7:]
+    ch = cotans[0].shape[0]
     for at, cotan in enumerate(cotans):
         gathered[at * ch : (at + 1) * ch] = cotan[...]
-    for row in range(height + 2):
-        spread(wide, row, feat[:, row * width : (row + 1) * width])
     (whole,) = tap_products(gathered, [wide], [total], height, width)
-    own[...] = whole[0:ch]
-    for at, (out, mod) in enumerate(zip((behind, ahead), mods)):
-        out[0:ch] = whole[(at + 1) * ch : (at + 2) * ch]
+    for at, (out, mod) in enumerate(zip(outs, mods)):
+        out[0:ch] = whole[at * ch : (at + 1) * ch]
         out[ch:] = mod[...]
 
 
@@ -421,27 +424,36 @@
         scalars=1,
         scratch=[((rows, TAPS, out_ch, in_ch), F32), ((size, *message[0]), BF16)],
     )
-    first[0], second[0], plains = lax.optimization_barrier((first[0], second[0], plains))
+    own_grad, wide = call(
+        functools.partial(own_grad_kernel, height, width),
+        "own_grad",
+        [message, ((3 * ch, (height + 2) * width), BF16)],
+        cotan,
+        feat,
+        scratch=[((3, ch, 3 * ch), F32)],
+        flops=flops // size,
+    )
+    first[0], second[0], plains, own_grad, wide = lax.optimization_barrier(
+        (first[0], second[0], plains, own_grad, wide)
+    )
 
     step(2, first[0], second[0])
     double = ((2 * ch, TAPS * ch), BF16)
-    own_grad, to_behind, to_ahead, wide = call(
+    to_behind, to_ahead = call(
         functools.partial(near_grad_kernel, height, width),
         "near_grad",
-        [message, double, double, ((3 * ch, (height + 2) * width), BF16)],
-        cotan,
+        [double, double],
         first[0],
         second[0],
-        feat,
+        wide,
         mods[size - 1],
         mods[1],
-        scratch=[((3 * ch, pixels), BF16), ((3, 3 * ch, 3 * ch), F32)],
-        flops=flops * 3 // size,
+        scratch=[((2 * ch, pixels), BF16), ((3, 2 * ch, 3 * ch), F32)],
+        flops=flops * 2 // size,
     )
     from_ahead = along(to_behind, [(i + 1, i) for i in range(size - 1)])
-    from_behind = along(to_ahead, [(i, i + 1) for i in range(size - 1)])
-    first[1], second[1], feat_end, wide, whole_mod = lax.optimization_barrier(
-        (first[1], second[1], feat_end, wide, whole_mod)
+    first[1], second[1], feat_end, to_ahead, whole_mod = lax.optimization_barrier(
+        (first[1], second[1], feat_end, to_ahead, whole_mod)
     )
 
     count = size - 3
@@ -464,6 +476,8 @@
         scratch=[((3 * ch, (height + 2) * width), BF16), ((3, ch, 3 * ch), F32)],
         flops=flops // size,
     )
+    to_ahead, grad_others = lax.optimization_barrier((to_ahead, grad_others))
+    from_behind = along(to_ahead, [(i, i + 1) for i in range(size - 1)])
     from_others = along(grad_others, [(i, (i + 2) % size) for i in range(size)])
     from_end = lax.ppermute(grad_end, "chan", [(1, size - 1), (size - 2, 0)])
     end_block, grad_end = lax.optimization_barrier((end_block, grad_end))

time: 87 us -> 93 us (1.069)
  Pallas kernels: 24.4 us -> 30.5 us
  starting transfers between devices: 44 us -> 42.3 us
  waiting for transfers between devices: 12.3 us -> 13.5 us
    pallas_call x11 -> x12, Pallas kernels: 24.4 us -> 30.5 us  [call(): pl.pallas_call(kernel, out_shape=outs, in_specs=sspec(scalars) + vspec(le...]
    ppermute x8, waiting for transfers between devices: 0.02 us -> 3.36 us  [along(): return lax.ppermute(x, ('samples', 'chan'), whole)]
    ppermute x8, starting transfers between devices: 22.1 us -> 19.3 us  [along(): return lax.ppermute(x, ('samples', 'chan'), whole)]
    ppermute x7, waiting for transfers between devices: 2.91 us -> 0.31 us  [exchange(): lax.ppermute(x, axis, [(i, (i + s) % size) for i in range(size)])]
    ppermute x1, waiting for transfers between devices: 1.34 us -> 0.01 us  [on_device(): far = lax.ppermute(end_block, 'chan', [(1, 0), (size - 2, size - 1)])]
    ppermute x1, waiting for transfers between devices: 4.71 us -> 5.7 us  [on_device(): from_end = lax.ppermute(grad_end, 'chan', [(1, size - 1), (size - 2, 0)])]
  transfers between devices with their start and end apart: 22 -> 22, of which waited for: 7 -> 7; matrix products, arithmetic and copies ran while one was open for 3% -> 3% of each run, Pallas kernels for 26% -> 31%
where the time goes in v13:
time: 93 us; the launch traced here: 92.5 us
  starting transfers between devices  42.3 us (45%)
  Pallas kernels  30.5 us (33%)
  waiting for transfers between devices  13.5 us (15%)
  local copies, waits for them, and re-layouts  3.93 us (4%)
  other arithmetic  1.25 us (1%)
  between operations  0.98 us (1%)
    pallas_call x12, Pallas kernels, call(): pl.pallas_call(kernel, out_shape=outs, in_specs=sspec(scalars) + vspec(le...  30.5 us
    ppermute x8, starting transfers between devices, along(): return lax.ppermute(x, ('samples', 'chan'), whole)  19.3 us
    ppermute x7, starting transfers between devices, exchange(): lax.ppermute(x, axis, [(i, (i + s) % size) for i in range(size)])  7.46 us
    ppermute x1, starting transfers between devices, on_device(): feat_end = lax.ppermute(feat, 'chan', [(0, 1), (size - 1, size - 2)])  6.1 us
    ppermute x1, waiting for transfers between devices, on_device(): from_end = lax.ppermute(grad_end, 'chan', [(1, size - 1), (size - 2, 0)])  5.7 us
    unnamed x19, local copies, waits for them, and re-layouts  3.58 us
    ppermute x8, waiting for transfers between devices, along(): return lax.ppermute(x, ('samples', 'chan'), whole)  3.36 us
    ppermute x2, starting transfers between devices, from_sides(): got = lax.ppermute(jnp.where(at == 0, last, first), axis, [(0, 1), (1, 0)])  3.24 us
  transfers between devices with their start and end apart: 22, of which 7 were waited for; matrix products, arithmetic and copies ran while one was open for 3% of the time, Pallas kernels for 31%

profile of v13, /device:TPU:0, one launch (start us, length us, event | category | flops | bytes accessed | tf_op | source)
XLA Modules:
  0.0 92.5 jit_solution(12225598580367780209)
XLA Ops:
  0.7 2.1 %copy.13 = bf16[8,8,8,512]{3,1,2,0:T(8,128)(2,1)} copy(bf16[8,8,8,512]{3,2,1,0:T(8,128)(2,1)} %bitcast.28) | data formatting | bytes 1048576
  2.8 5.7 %collective-permute-start.1 = (bf16[64,4096]{1,0:T(8,128)(2,1)}, bf16[64,4096]{1,0:T(8,128)(2,1)}, u32[]{:S(2)}, u32[]{:S(2)}) collective-permute-start(bf16[64,4096]{1,0:T(8,128)(2,1)} %bitcast.10.cotan), channel_id=1, source_target_pairs={{0,1},{1,2},{2,3},{7,6},{6,5},{5,4},{8,9},{9,10},{10,11},{15,14},{... | collective-permute-start | bytes 1572872 | tf_op jit(solution)/shard_map/ppermute | solution.py:376
  8.6 1.3 %collective-permute-start.2 = (bf16[64,4096]{1,0:T(8,128)(2,1)}, bf16[64,4096]{1,0:T(8,128)(2,1)}, u32[]{:S(2)}, u32[]{:S(2)}) collective-permute-start(bf16[64,4096]{1,0:T(8,128)(2,1)} %bitcast.10.cotan), channel_id=1, source_target_pairs={{1,0},{2,1},{3,2},{6,7},{5,6},{4,5},{9,8},{10,9},{11,10},{14,15},{... | collective-permute-start | bytes 1572872 | tf_op jit(solution)/shard_map/ppermute | solution.py:376
  9.9 0.2 copy.14
  10.1 1.6 %collective-permute-start.3 = (bf16[64,512]{1,0:T(8,128)(2,1)S(1)}, bf16[64,512]{1,0:T(8,128)(2,1)S(1)}, u32[]{:S(2)}, u32[]{:S(2)}) collective-permute-start(bf16[64,512]{1,0:T(8,128)(2,1)S(1)} %slice_select_fusion), channel_id=1, source_target_pairs={{0,16},{16,0},{1,17},{17,1},{2,18},{18,2},{3,19},{19,3},{4,20},{20... | collective-permute-start | bytes 196616 | tf_op jit(solution)/shard_map/ppermute | solution.py:351
  11.7 1.0 %plain.1 = (f32[10,64,128]{2,1,0:T(8,128)S(1)}, f32[8,128]{1,0:T(8,128)S(1)}) custom-call(s32[1,4]{1,0:T(1,128)S(1)} %copy-done.3, f32[1,512]{1,0:T(1,128)S(1)} %copy-done.2, f32[1,128]{1,0:T(1,128)S(1)} %bitcast.26, f32[512,128]{1,0:T(8,128)S(1)} %copy-done.1, f32[4,9,64,128]{3,2,1,0:T(8,128)S(1)} %copy-done), custom_call_target="tpu_custom_call" | custom-call | flops 1000000 | bytes 1776144 | tf_op jit(solution)/shard_map/plain/pallas_call | solution.py:327
  12.6 0.6 collective-permute-start
  13.2 1.2 %collective-permute-done.3 = bf16[64,512]{1,0:T(8,128)(2,1)S(1)} collective-permute-done((bf16[64,512]{1,0:T(8,128)(2,1)S(1)}, bf16[64,512]{1,0:T(8,128)(2,1)S(1)}, u32[]{:S(2)}, u32[]{:S(2)}) %collective-permute-start.3) | collective-permute-done | bytes 65568 | tf_op jit(solution)/shard_map/ppermute | solution.py:351
  14.4 0.9 feat_rows.1.feat
  15.3 6.1 %collective-permute-start.6 = (bf16[64,5120]{1,0:T(8,128)(2,1)}, bf16[64,5120]{1,0:T(8,128)(2,1)}, u32[]{:S(2)}, u32[]{:S(2)}) collective-permute-start(bf16[64,5120]{1,0:T(8,128)(2,1)} %feat_rows.1.feat), channel_id=1, source_target_pairs={{0,1},{3,2},{4,5},{7,6},{8,9},{11,10},{12,13},{15,14},{16,17},{19,... | collective-permute-start | bytes 1966088 | tf_op jit(solution)/shard_map/ppermute | solution.py:416
  21.4 4.3 %own_grad.1 = (bf16[64,576]{1,0:T(8,128)(2,1)S(1)}, bf16[192,5120]{1,0:T(8,128)(2,1)S(1)}) custom-call(bf16[64,4096]{1,0:T(8,128)(2,1)} %bitcast.10.cotan, bf16[64,5120]{1,0:T(8,128)(2,1)} %feat_rows.1.feat), custom_call_target="tpu_custom_call" | custom-call | flops 301989888 | bytes 3219456 | tf_op jit(solution)/shard_map/own_grad/pallas_call | solution.py:327
  25.7 0.0 copy-start.5
  25.7 0.6 copy-done.5
  26.3 0.0 collective-permute-done.refs_1_
  26.3 0.0 collective-permute-done.1.refs_0_.first
  26.3 0.0 collective-permute-done.2.refs_1_.second
  26.4 1.5 %collective-permute-start.4 = (bf16[64,4096]{1,0:T(8,128)(2,1)}, bf16[64,4096]{1,0:T(8,128)(2,1)}, u32[]{:S(2)}, u32[]{:S(2)}) collective-permute-start(bf16[64,4096]{1,0:T(8,128)(2,1)} %collective-permute-done.1.refs_0_.first), channel_id=1, source_target_pairs={{1,2},{2,3},{6,5},{5,4},{9,10},{10,11},{14,13},{13,12},{17,18},{18... | collective-permute-start | bytes 1572872 | tf_op jit(solution)/shard_map/ppermute | solution.py:376
  27.8 1.3 %collective-permute-start.5 = (bf16[64,4096]{1,0:T(8,128)(2,1)}, bf16[64,4096]{1,0:T(8,128)(2,1)}, u32[]{:S(2)}, u32[]{:S(2)}) collective-permute-start(bf16[64,4096]{1,0:T(8,128)(2,1)} %collective-permute-done.2.refs_1_.second), channel_id=1, source_target_pairs={{1,0},{2,1},{6,7},{5,6},{9,8},{10,9},{14,15},{13,14},{17,16},{18,1... | collective-permute-start | bytes 1572872 | tf_op jit(solution)/shard_map/ppermute | solution.py:376
  29.1 0.1 pad_add_fusion.place
  29.2 1.3 %mod_blocks.1 = (bf16[9,64,256]{2,1,0:T(8,128)(2,1)S(1)}, f32[64,128]{1,0:T(8,128)S(1)}, bf16[64,576]{1,0:T(8,128)(2,1)S(1)}, bf16[64,576]{1,0:T(8,128)(2,1)S(1)...) custom-call(s32[4]{0:T(128)S(1)} %pad_add_fusion.place, ...), custom_call_target="tpu_custom_call" | custom-call | flops 1000000 | bytes 1351696 | tf_op jit(solution)/shard_map/mod_blocks/pallas_call | solution.py:327
  30.5 4.1 %near_grad.1 = (bf16[128,576]{1,0:T(8,128)(2,1)S(1)}, bf16[128,576]{1,0:T(8,128)(2,1)S(1)}) custom-call(bf16[64,4096]{1,0:T(8,128)(2,1)} %collective-permute-done.1.refs_0_.first, bf16[64,4096]{1,0:T(8,128)(2,1)} %collective-permute-done.2.refs_1_.second, bf16[192,5120]{1,0:T(8,128)(2,1)S(1)} %get-tuple-element.75.refs_2_, ...), custom_call_target="tpu_custom_call" | custom-call | flops 603979776 | bytes 3457024 | tf_op jit(solution)/shard_map/near_grad/pallas_call | solution.py:327
  34.6 1.3 %collective-permute-start.7 = (bf16[128,576]{1,0:T(8,128)(2,1)S(1)}, bf16[128,576]{1,0:T(8,128)(2,1)S(1)}, u32[]{:S(2)}, u32[]{:S(2)}) collective-permute-start(bf16[128,576]{1,0:T(8,128)(2,1)S(1)} %get-tuple-element.82), channel_id=1, source_target_pairs={{1,0},{2,1},{3,2},{6,7},{5,6},{4,5},{9,8},{10,9},{11,10},{14,15},{... | collective-permute-start | bytes 442376 | tf_op jit(solution)/shard_map/ppermute | solution.py:376
  35.9 0.0 collective-permute-done.6.feat
  35.9 0.0 collective-permute-done.4.refs_0_
  35.9 3.3 %collective-permute-done.5.refs_1_ = bf16[64,4096]{1,0:T(8,128)(2,1)} collective-permute-done((bf16[64,4096]{1,0:T(8,128)(2,1)}, bf16[64,4096]{1,0:T(8,128)(2,1)}, u32[]{:S(2)}, u32[]{:S(2)}) %collective-permute-start.5) | collective-permute-done | bytes 524320 | tf_op jit(solution)/shard_map/ppermute | solution.py:376
  39.2 3.9 %middle_grad.1 = (bf16[64,576]{1,0:T(8,128)(2,1)S(1)}, bf16[64,4096]{1,0:T(8,128)(2,1)S(1)}, bf16[64,4096]{1,0:T(8,128)(2,1)S(1)}) custom-call(bf16[64,4096]{1,0:T(8,128)(2,1)} %collective-permute-done.4.refs_0_, bf16[64,4096]{1,0:T(8,128)(2,1)} %collective-permute-done.5.refs_1_, bf16[192,5120]{1,0:T(8,128)(2,1)S(1)} %get-tuple-element.75.refs_2_), custom_call_target="tpu_custom_call" | custom-call | flops 301989888 | bytes 4136960 | tf_op jit(solution)/shard_map/middle_grad/pallas_call | solution.py:327
  43.1 0.0 copy-start.6
  43.1 2.6 %collective-permute-start.8 = (bf16[128,576]{1,0:T(8,128)(2,1)S(1)}, bf16[128,576]{1,0:T(8,128)(2,1)S(1)}, u32[]{:S(2)}, u32[]{:S(2)}) collective-permute-start(bf16[128,576]{1,0:T(8,128)(2,1)S(1)} %get-tuple-element.87), channel_id=1, source_target_pairs={{0,1},{1,2},{2,3},{7,6},{6,5},{5,4},{8,9},{9,10},{10,11},{15,14},{... | collective-permute-start | bytes 442376 | tf_op jit(solution)/shard_map/ppermute | solution.py:376
  45.7 5.7 %collective-permute-start.9 = (bf16[64,576]{1,0:T(8,128)(2,1)S(1)}, bf16[64,576]{1,0:T(8,128)(2,1)S(1)}, u32[]{:S(2)}, u32[]{:S(2)}) collective-permute-start(bf16[64,576]{1,0:T(8,128)(2,1)S(1)} %get-tuple-element.88), channel_id=1, source_target_pairs={{0,2},{1,3},{2,0},{3,1},{7,5},{6,4},{5,7},{4,6},{8,10},{9,11},{10,... | collective-permute-start | bytes 221192 | tf_op jit(solution)/shard_map/ppermute | solution.py:376
  51.4 4.1 %end_grad.1 = bf16[64,576]{1,0:T(8,128)(2,1)S(1)} custom-call(bf16[64,4096]{1,0:T(8,128)(2,1)S(1)} %get-tuple-element.101.end_block, bf16[64,5120]{1,0:T(8,128)(2,1)} %collective-permute-done.6.feat), custom_call_target="tpu_custom_call" | custom-call | flops 301989888 | bytes 1253376 | tf_op jit(solution)/shard_map/end_grad/pallas_call | solution.py:327
  55.5 1.3 %collective-permute-start.10 = (bf16[64,576]{1,0:T(8,128)(2,1)S(1)}, bf16[64,576]{1,0:T(8,128)(2,1)S(1)}, u32[]{:S(2)}, u32[]{:S(2)}) collective-permute-start(bf16[64,576]{1,0:T(8,128)(2,1)S(1)} %end_grad.1), channel_id=1, source_target_pairs={{1,3},{2,0},{5,7},{6,4},{9,11},{10,8},{13,15},{14,12},{17,19},{18,... | collective-permute-start | bytes 221192 | tf_op jit(solution)/shard_map/ppermute | solution.py:482
  56.8 1.3 %collective-permute-start.17 = (bf16[64,4096]{1,0:T(8,128)(2,1)S(1)}, bf16[64,4096]{1,0:T(8,128)(2,1)S(1)}, u32[]{:S(2)}, u32[]{:S(2)}) collective-permute-start(bf16[64,4096]{1,0:T(8,128)(2,1)S(1)} %get-tuple-element.101.end_block), channel_id=1, source_target_pairs={{1,0},{2,3},{5,4},{6,7},{9,8},{10,11},{13,12},{14,15},{17,16},{18,... | collective-permute-start | bytes 1572872 | tf_op jit(solution)/shard_map/ppermute | solution.py:484
  58.1 0.0 collective-permute-done.7.ahead
  58.1 0.0 collective-permute-done.9.others
  58.1 5.7 %collective-permute-done.10.end = bf16[64,576]{1,0:T(8,128)(2,1)S(1)} collective-permute-done((bf16[64,576]{1,0:T(8,128)(2,1)S(1)}, bf16[64,576]{1,0:T(8,128)(2,1)S(1)}, u32[]{:S(2)}, u32[]{:S(2)}) %collective-permute-start.10) | collective-permute-done | bytes 73760 | tf_op jit(solution)/shard_map/ppermute | solution.py:482
  63.8 0.0 collective-permute-done.8.behind
  63.8 1.1 %collect.1 = (bf16[10,64,128]{2,1,0:T(8,128)(2,1)S(1)}, bf16[10,64,128]{2,1,0:T(8,128)(2,1)S(1)}) custom-call(s32[4]{0:T(128)S(1)} %pad_add_fusion.place, f32[64,128]{1,0:T(8,128)S(1)} %get-tuple-element.66.scale, bf16[9,64,256]{2,1,0:T(8,128)(2,1)S(1)} %get-tuple-element.80.whole_mod, bf16[64,576]{1,0:T(8,128)(2,1)S(1)} %copy-done.6, ...), custom_call_target="tpu_custom_call" | custom-call | flops 6000000000 | bytes 1171472 | tf_op jit(solution)/shard_map/collect/pallas_call | solution.py:327
  64.9 1.7 %collective-permute-start.11 = (bf16[10,64,128]{2,1,0:T(8,128)(2,1)S(1)}, bf16[10,64,128]{2,1,0:T(8,128)(2,1)S(1)}, u32[]{:S(2)}, u32[]{:S(2)}) collective-permute-start(bf16[10,64,128]{2,1,0:T(8,128)(2,1)S(1)} %get-tuple-element.97), channel_id=1, source_target_pairs={{0,16},{16,0},{1,17},{17,1},{2,18},{18,2},{3,19},{19,3},{4,20},{20... | collective-permute-start | bytes 491528 | tf_op jit(solution)/shard_map/ppermute | solution.py:505
  66.6 0.0 collective-permute-start.15
  66.6 1.9 %collective-permute-start.16 = (bf16[64,576]{1,0:T(8,128)(2,1)S(1)}, bf16[64,576]{1,0:T(8,128)(2,1)S(1)}, u32[]{:S(2)}, u32[]{:S(2)}) collective-permute-start(bf16[64,576]{1,0:T(8,128)(2,1)S(1)} %get-tuple-element.100), channel_id=1, source_target_pairs={{0,3},{3,0},{4,7},{7,4},{8,11},{11,8},{12,15},{15,12},{16,19},{19,... | collective-permute-start | bytes 221192 | tf_op jit(solution)/shard_map/ppermute | solution.py:503
  68.5 1.8 %collective-permute-done.11.refs_1_ = bf16[10,64,128]{2,1,0:T(8,128)(2,1)S(1)} collective-permute-done((bf16[10,64,128]{2,1,0:T(8,128)(2,1)S(1)}, bf16[10,64,128]{2,1,0:T(8,128)(2,1)S(1)}, u32[]{:S(2)}, u32[]{:S(2)}) %collective-permute-start.11) | collective-permute-done | bytes 163872 | tf_op jit(solution)/shard_map/ppermute | solution.py:505
  70.3 0.2 row_sum.1.refs_0_
  70.5 0.1 collective-permute-start.12
  70.6 1.6 %collective-permute-start.13 = (bf16[11,64,128]{2,1,0:T(8,128)(2,1)S(1)}, bf16[11,64,128]{2,1,0:T(8,128)(2,1)S(1)}, u32[]{:S(2)}, u32[]{:S(2)}) collective-permute-start(bf16[11,64,128]{2,1,0:T(8,128)(2,1)S(1)} %row_sum.1.refs_0_), channel_id=1, source_target_pairs={{0,8},{4,12},{8,0},{12,4},{1,9},{5,13},{9,1},{13,5},{2,10},{6,14},... | collective-permute-start | bytes 540680 | tf_op jit(solution)/shard_map/ppermute | solution.py:344
  72.1 0.0 collective-permute-done.15.refs_0_
  72.1 1.4 %collective-permute-start.14 = (bf16[11,64,128]{2,1,0:T(8,128)(2,1)S(1)}, bf16[11,64,128]{2,1,0:T(8,128)(2,1)S(1)}, u32[]{:S(2)}, u32[]{:S(2)}) collective-permute-start(bf16[11,64,128]{2,1,0:T(8,128)(2,1)S(1)} %row_sum.1.refs_0_), channel_id=1, source_target_pairs={{0,12},{4,0},{8,4},{12,8},{1,13},{5,1},{9,5},{13,9},{2,14},{6,2},{... | collective-permute-start | bytes 540680 | tf_op jit(solution)/shard_map/ppermute | solution.py:344
  73.5 1.2 %collective-permute-done.16.refs_1_ = bf16[64,576]{1,0:T(8,128)(2,1)S(1)} collective-permute-done((bf16[64,576]{1,0:T(8,128)(2,1)S(1)}, bf16[64,576]{1,0:T(8,128)(2,1)S(1)}, u32[]{:S(2)}, u32[]{:S(2)}) %collective-permute-start.16) | collective-permute-done | bytes 73760 | tf_op jit(solution)/shard_map/ppermute | solution.py:503
  74.7 0.0 collective-permute-done.17.far
  74.7 5.3 %input_grad.1 = (f32[64,4096]{1,0:T(8,128)S(1)}, f32[64,512]{1,0:T(8,128)S(1)}, f32[64,512]{1,0:T(8,128)S(1)}) custom-call(s32[4]{0:T(128)S(1)} %pad_add_fusion.place, bf16[64,4096]{1,0:T(8,128)(2,1)} %bitcast.10.cotan, bf16[64,4096]{1,0:T(8,128)(2,1)} %collective-permute-done.1.refs_0_.first, bf16[64,4096]{1,0:T(8,128)(2,1)} %collective-permute-done.2.refs_1_.second, ...), custom_call_target="tpu_custom_call" | custom-call | flops 2000000000 | bytes 4448272 | tf_op jit(solution)/shard_map/input_grad/pallas_call | solution.py:327
  80.1 0.0 collective-permute-done.13.refs_2_
  80.1 0.2 collective-permute-done.14.refs_3_
  80.3 1.7 %collective-permute-start.21 = (f32[64,512]{1,0:T(8,128)S(1)}, f32[64,512]{1,0:T(8,128)S(1)}, u32[]{:S(2)}, u32[]{:S(2)}) collective-permute-start(f32[64,512]{1,0:T(8,128)S(1)} %broadcast_select_fusion), channel_id=1, source_target_pairs={{0,16},{16,0},{1,17},{17,1},{2,18},{18,2},{3,19},{19,3},{4,20},{20... | collective-permute-start | bytes 393224 | tf_op jit(solution)/shard_map/ppermute | solution.py:351
  82.0 0.1 pad.1.clone
  82.1 2.8 %bank_grad.1 = (f32[4,9,64,128]{3,2,1,0:T(8,128)}, f32[4,128]{1,0:T(4,128)S(1)}, f32[4,512]{1,0:T(4,128)S(1)}) custom-call(s32[4]{0:T(128)S(1)} %pad_add_fusion.place, f32[4,9,64,128]{3,2,1,0:T(8,128)S(1)} %copy-done, bf16[11,64,128]{2,1,0:T(8,128)(2,1)S(1)} %row_sum.1.refs_0_, bf16[11,64,128]{2,1,0:T(8,128)(2,1)S(1)} %collective-permute-done.12.refs_1_, ...), custom_call_target="tpu_custom_call" | custom-call | flops 1000000 | bytes 3090448 | tf_op jit(solution)/shard_map/bank_grad/pallas_call | solution.py:327
  84.9 1.4 %collective-permute-start.19 = (f32[4,128]{1,0:T(4,128)S(1)}, f32[4,128]{1,0:T(4,128)S(1)}, u32[]{:S(2)}, u32[]{:S(2)}) collective-permute-start(f32[4,128]{1,0:T(4,128)S(1)} %get-tuple-element.120.refs_0_), channel_id=1, source_target_pairs={{0,2},{1,3},{2,0},{3,1},{4,6},{5,7},{6,4},{7,5},{8,10},{9,11},{10,... | collective-permute-start | bytes 6152 | tf_op jit(solution)/shard_map/ppermute | solution.py:344
  86.3 2.4 %collective-permute-start.20 = (f32[4,128]{1,0:T(4,128)S(1)}, f32[4,128]{1,0:T(4,128)S(1)}, u32[]{:S(2)}, u32[]{:S(2)}) collective-permute-start(f32[4,128]{1,0:T(4,128)S(1)} %get-tuple-element.120.refs_0_), channel_id=1, source_target_pairs={{0,3},{1,0},{2,1},{3,2},{4,7},{5,4},{6,5},{7,6},{8,11},{9,8},{10,9... | collective-permute-start | bytes 6152 | tf_op jit(solution)/shard_map/ppermute | solution.py:344
  88.7 0.6 copy.15
  89.4 0.1 copy.12
  89.5 0.1 copy.11
  89.6 1.1 %fusion = bf16[1,64,8,512]{3,2,1,0:T(8,128)(2,1)} fusion(f32[1,64,1,512]{3,2,1,0:T(1,128)S(1)} %copy.12, f32[1,64,1,512]{3,2,1,0:T(1,128)S(1)} %copy.11, f32[8]{0:T(128)S(1)} %pad.1.clone, f32[1,64,8,512]{3,2,1,0:T(8,128)S(1)} %bitcast.27), kind=kLoop, calls=%fused_computation.1 | loop fusion | flops 1048576 | bytes 1835040 | tf_op jit(solution)/shard_map/convert_element_type | solution.py:551
  90.8 0.0 collective-permute-done.18.refs_1_
  90.8 0.0 collective-permute-done.19.refs_2_
  90.8 0.1 collective-permute-done.20.refs_3_
  90.8 1.7 %affine.1 = (f32[512,128]{1,0:T(8,128)}, f32[1,128]{1,0:T(1,128)}) custom-call(s32[4]{0:T(128)S(1)} %pad_add_fusion.place, f32[4,512]{1,0:T(4,128)S(1)} %get-tuple-element.119.latents, f32[4,128]{1,0:T(4,128)S(1)} %get-tuple-element.120.refs_0_, f32[4,128]{1,0:T(4,128)S(1)} %collective-permute-done.18.refs_1_, f32[4,128]{1,0:T(4,128)S(1)} %collective-permute-done.19.refs_2_, ...), custom_call_target="tpu_custom_call" | custom-call | flops 1000000 | bytes 279056 | tf_op jit(solution)/shard_map/affine/pallas_call | solution.py:327
  (21 shorter events, 0.1 us)
Async XLA Ops:
  0.6 9.2 %copy-start.7 = (bf16[1,64,8,512]{3,2,1,0:T(8,128)(2,1)S(1)}, bf16[1,64,8,512]{3,2,1,0:T(8,128)(2,1)}, u32[]{:S(2)}) copy-start(bf16[1,64,8,512]{3,2,1,0:T(8,128)(2,1)} %param.7) | copy-start | bytes 1572868
  0.6 11.0 %copy-start = (f32[4,9,64,128]{3,2,1,0:T(8,128)S(1)}, f32[4,9,64,128]{3,2,1,0:T(8,128)}, u32[]{:S(2)}) copy-start(f32[4,9,64,128]{3,2,1,0:T(8,128)} %bank.1) | copy-start | bytes 3538948
  0.7 11.0 %copy-start.3 = (s32[1,4]{1,0:T(1,128)S(1)}, s32[1,4]{1,0:T(1,128)}, u32[]{:S(2)}) copy-start(s32[1,4]{1,0:T(1,128)} %refs_0_.1) | copy-start | bytes 52
  0.7 11.0 %copy-start.2 = (f32[1,512]{1,0:T(1,128)S(1)}, f32[1,512]{1,0:T(1,128)}, u32[]{:S(2)}) copy-start(f32[1,512]{1,0:T(1,128)} %refs_1_.1) | copy-start | bytes 6148
  0.7 11.0 %copy-start.4 = (f32[128]{0:T(128)S(1)}, f32[128]{0:T(128)}, u32[]{:S(2)}) copy-start(f32[128]{0:T(128)} %param.13) | copy-start | bytes 1540
  0.7 11.0 %copy-start.1 = (f32[512,128]{1,0:T(8,128)S(1)}, f32[512,128]{1,0:T(8,128)}, u32[]{:S(2)}) copy-start(f32[512,128]{1,0:T(8,128)} %refs_3_.1) | copy-start | bytes 786436
  2.8 23.5 %collective-permute-start.1 = (bf16[64,4096]{1,0:T(8,128)(2,1)}, bf16[64,4096]{1,0:T(8,128)(2,1)}, u32[]{:S(2)}, u32[]{:S(2)}) collective-permute-start(bf16[64,4096]{1,0:T(8,128)(2,1)} %bitcast.10.cotan), channel_id=1, source_target_pairs={{0,1},{1,2},{2,3},{7,6},{6,5},{5,4},{8,9},{9,10},{10,11},{15,14},{... | collective-permute-start | bytes 1572872 | tf_op jit(solution)/shard_map/ppermute | solution.py:376
  8.6 17.8 %collective-permute-start.2 = (bf16[64,4096]{1,0:T(8,128)(2,1)}, bf16[64,4096]{1,0:T(8,128)(2,1)}, u32[]{:S(2)}, u32[]{:S(2)}) collective-permute-start(bf16[64,4096]{1,0:T(8,128)(2,1)} %bitcast.10.cotan), channel_id=1, source_target_pairs={{1,0},{2,1},{3,2},{6,7},{5,6},{4,5},{9,8},{10,9},{11,10},{14,15},{... | collective-permute-start | bytes 1572872 | tf_op jit(solution)/shard_map/ppermute | solution.py:376
  10.1 4.3 %collective-permute-start.3 = (bf16[64,512]{1,0:T(8,128)(2,1)S(1)}, bf16[64,512]{1,0:T(8,128)(2,1)S(1)}, u32[]{:S(2)}, u32[]{:S(2)}) collective-permute-start(bf16[64,512]{1,0:T(8,128)(2,1)S(1)} %slice_select_fusion), channel_id=1, source_target_pairs={{0,16},{16,0},{1,17},{17,1},{2,18},{18,2},{3,19},{19,3},{4,20},{20... | collective-permute-start | bytes 196616 | tf_op jit(solution)/shard_map/ppermute | solution.py:351
  12.6 13.7 %collective-permute-start = (f32[10,64,128]{2,1,0:T(8,128)S(1)}, f32[10,64,128]{2,1,0:T(8,128)}, u32[]{:S(2)}, u32[]{:S(2)}) collective-permute-start(f32[10,64,128]{2,1,0:T(8,128)S(1)} %get-tuple-element.65.refs_0_), channel_id=1, source_target_pairs={{0,16},{16,0},{1,17},{17,1},{2,18},{18,2},{3,19},{19,3},{4,20},{20... | collective-permute-start | bytes 983048 | tf_op jit(solution)/shard_map/ppermute | solution.py:344
  15.3 20.5 %collective-permute-start.6 = (bf16[64,5120]{1,0:T(8,128)(2,1)}, bf16[64,5120]{1,0:T(8,128)(2,1)}, u32[]{:S(2)}, u32[]{:S(2)}) collective-permute-start(bf16[64,5120]{1,0:T(8,128)(2,1)} %feat_rows.1.feat), channel_id=1, source_target_pairs={{0,1},{3,2},{4,5},{7,6},{8,9},{11,10},{12,13},{15,14},{16,17},{19,... | collective-permute-start | bytes 1966088 | tf_op jit(solution)/shard_map/ppermute | solution.py:416
  25.7 0.6 copy-start.5
  26.4 9.5 %collective-permute-start.4 = (bf16[64,4096]{1,0:T(8,128)(2,1)}, bf16[64,4096]{1,0:T(8,128)(2,1)}, u32[]{:S(2)}, u32[]{:S(2)}) collective-permute-start(bf16[64,4096]{1,0:T(8,128)(2,1)} %collective-permute-done.1.refs_0_.first), channel_id=1, source_target_pairs={{1,2},{2,3},{6,5},{5,4},{9,10},{10,11},{14,13},{13,12},{17,18},{18... | collective-permute-start | bytes 1572872 | tf_op jit(solution)/shard_map/ppermute | solution.py:376
  27.8 11.4 %collective-permute-start.5 = (bf16[64,4096]{1,0:T(8,128)(2,1)}, bf16[64,4096]{1,0:T(8,128)(2,1)}, u32[]{:S(2)}, u32[]{:S(2)}) collective-permute-start(bf16[64,4096]{1,0:T(8,128)(2,1)} %collective-permute-done.2.refs_1_.second), channel_id=1, source_target_pairs={{1,0},{2,1},{6,7},{5,6},{9,8},{10,9},{14,15},{13,14},{17,16},{18,1... | collective-permute-start | bytes 1572872 | tf_op jit(solution)/shard_map/ppermute | solution.py:376
  34.6 23.5 %collective-permute-start.7 = (bf16[128,576]{1,0:T(8,128)(2,1)S(1)}, bf16[128,576]{1,0:T(8,128)(2,1)S(1)}, u32[]{:S(2)}, u32[]{:S(2)}) collective-permute-start(bf16[128,576]{1,0:T(8,128)(2,1)S(1)} %get-tuple-element.82), channel_id=1, source_target_pairs={{1,0},{2,1},{3,2},{6,7},{5,6},{4,5},{9,8},{10,9},{11,10},{14,15},{... | collective-permute-start | bytes 442376 | tf_op jit(solution)/shard_map/ppermute | solution.py:376
  43.1 20.7 %copy-start.6 = (bf16[64,576]{1,0:T(8,128)(2,1)S(1)}, bf16[64,576]{1,0:T(8,128)(2,1)}, u32[]{:S(2)}) copy-start(bf16[64,576]{1,0:T(8,128)(2,1)} %copy-done.5) | copy-start | bytes 221188
  43.1 20.7 %collective-permute-start.8 = (bf16[128,576]{1,0:T(8,128)(2,1)S(1)}, bf16[128,576]{1,0:T(8,128)(2,1)S(1)}, u32[]{:S(2)}, u32[]{:S(2)}) collective-permute-start(bf16[128,576]{1,0:T(8,128)(2,1)S(1)} %get-tuple-element.87), channel_id=1, source_target_pairs={{0,1},{1,2},{2,3},{7,6},{6,5},{5,4},{8,9},{9,10},{10,11},{15,14},{... | collective-permute-start | bytes 442376 | tf_op jit(solution)/shard_map/ppermute | solution.py:376
  45.7 12.4 %collective-permute-start.9 = (bf16[64,576]{1,0:T(8,128)(2,1)S(1)}, bf16[64,576]{1,0:T(8,128)(2,1)S(1)}, u32[]{:S(2)}, u32[]{:S(2)}) collective-permute-start(bf16[64,576]{1,0:T(8,128)(2,1)S(1)} %get-tuple-element.88), channel_id=1, source_target_pairs={{0,2},{1,3},{2,0},{3,1},{7,5},{6,4},{5,7},{4,6},{8,10},{9,11},{10,... | collective-permute-start | bytes 221192 | tf_op jit(solution)/shard_map/ppermute | solution.py:376
  55.5 8.3 %collective-permute-start.10 = (bf16[64,576]{1,0:T(8,128)(2,1)S(1)}, bf16[64,576]{1,0:T(8,128)(2,1)S(1)}, u32[]{:S(2)}, u32[]{:S(2)}) collective-permute-start(bf16[64,576]{1,0:T(8,128)(2,1)S(1)} %end_grad.1), channel_id=1, source_target_pairs={{1,3},{2,0},{5,7},{6,4},{9,11},{10,8},{13,15},{14,12},{17,19},{18,... | collective-permute-start | bytes 221192 | tf_op jit(solution)/shard_map/ppermute | solution.py:482
  56.8 17.9 %collective-permute-start.17 = (bf16[64,4096]{1,0:T(8,128)(2,1)S(1)}, bf16[64,4096]{1,0:T(8,128)(2,1)S(1)}, u32[]{:S(2)}, u32[]{:S(2)}) collective-permute-start(bf16[64,4096]{1,0:T(8,128)(2,1)S(1)} %get-tuple-element.101.end_block), channel_id=1, source_target_pairs={{1,0},{2,3},{5,4},{6,7},{9,8},{10,11},{13,12},{14,15},{17,16},{18,... | collective-permute-start | bytes 1572872 | tf_op jit(solution)/shard_map/ppermute | solution.py:484
  64.9 5.4 %collective-permute-start.11 = (bf16[10,64,128]{2,1,0:T(8,128)(2,1)S(1)}, bf16[10,64,128]{2,1,0:T(8,128)(2,1)S(1)}, u32[]{:S(2)}, u32[]{:S(2)}) collective-permute-start(bf16[10,64,128]{2,1,0:T(8,128)(2,1)S(1)} %get-tuple-element.97), channel_id=1, source_target_pairs={{0,16},{16,0},{1,17},{17,1},{2,18},{18,2},{3,19},{19,3},{4,20},{20... | collective-permute-start | bytes 491528 | tf_op jit(solution)/shard_map/ppermute | solution.py:505
  66.6 5.6 %collective-permute-start.15 = (bf16[64,576]{1,0:T(8,128)(2,1)S(1)}, bf16[64,576]{1,0:T(8,128)(2,1)S(1)}, u32[]{:S(2)}, u32[]{:S(2)}) collective-permute-start(bf16[64,576]{1,0:T(8,128)(2,1)S(1)} %get-tuple-element.99), channel_id=1, source_target_pairs={{0,2},{1,3},{2,0},{3,1},{7,5},{6,4},{5,7},{4,6},{8,10},{9,11},{10,... | collective-permute-start | bytes 221192 | tf_op jit(solution)/shard_map/ppermute | solution.py:376
  66.6 8.1 %collective-permute-start.16 = (bf16[64,576]{1,0:T(8,128)(2,1)S(1)}, bf16[64,576]{1,0:T(8,128)(2,1)S(1)}, u32[]{:S(2)}, u32[]{:S(2)}) collective-permute-start(bf16[64,576]{1,0:T(8,128)(2,1)S(1)} %get-tuple-element.100), channel_id=1, source_target_pairs={{0,3},{3,0},{4,7},{7,4},{8,11},{11,8},{12,15},{15,12},{16,19},{19,... | collective-permute-start | bytes 221192 | tf_op jit(solution)/shard_map/ppermute | solution.py:503
  70.5 9.6 %collective-permute-start.12 = (bf16[11,64,128]{2,1,0:T(8,128)(2,1)S(1)}, bf16[11,64,128]{2,1,0:T(8,128)(2,1)S(1)}, u32[]{:S(2)}, u32[]{:S(2)}) collective-permute-start(bf16[11,64,128]{2,1,0:T(8,128)(2,1)S(1)} %row_sum.1.refs_0_), channel_id=1, source_target_pairs={{0,4},{4,8},{8,12},{12,0},{1,5},{5,9},{9,13},{13,1},{2,6},{6,10},{... | collective-permute-start | bytes 540680 | tf_op jit(solution)/shard_map/ppermute | solution.py:344
  70.6 9.5 %collective-permute-start.13 = (bf16[11,64,128]{2,1,0:T(8,128)(2,1)S(1)}, bf16[11,64,128]{2,1,0:T(8,128)(2,1)S(1)}, u32[]{:S(2)}, u32[]{:S(2)}) collective-permute-start(bf16[11,64,128]{2,1,0:T(8,128)(2,1)S(1)} %row_sum.1.refs_0_), channel_id=1, source_target_pairs={{0,8},{4,12},{8,0},{12,4},{1,9},{5,13},{9,1},{13,5},{2,10},{6,14},... | collective-permute-start | bytes 540680 | tf_op jit(solution)/shard_map/ppermute | solution.py:344
  72.1 8.1 %collective-permute-start.14 = (bf16[11,64,128]{2,1,0:T(8,128)(2,1)S(1)}, bf16[11,64,128]{2,1,0:T(8,128)(2,1)S(1)}, u32[]{:S(2)}, u32[]{:S(2)}) collective-permute-start(bf16[11,64,128]{2,1,0:T(8,128)(2,1)S(1)} %row_sum.1.refs_0_), channel_id=1, source_target_pairs={{0,12},{4,0},{8,4},{12,8},{1,13},{5,1},{9,5},{13,9},{2,14},{6,2},{... | collective-permute-start | bytes 540680 | tf_op jit(solution)/shard_map/ppermute | solution.py:344
  80.3 9.0 %collective-permute-start.21 = (f32[64,512]{1,0:T(8,128)S(1)}, f32[64,512]{1,0:T(8,128)S(1)}, u32[]{:S(2)}, u32[]{:S(2)}) collective-permute-start(f32[64,512]{1,0:T(8,128)S(1)} %broadcast_select_fusion), channel_id=1, source_target_pairs={{0,16},{16,0},{1,17},{17,1},{2,18},{18,2},{3,19},{19,3},{4,20},{20... | collective-permute-start | bytes 393224 | tf_op jit(solution)/shard_map/ppermute | solution.py:351
  84.9 5.9 %collective-permute-start.18 = (f32[4,128]{1,0:T(4,128)S(1)}, f32[4,128]{1,0:T(4,128)S(1)}, u32[]{:S(2)}, u32[]{:S(2)}) collective-permute-start(f32[4,128]{1,0:T(4,128)S(1)} %get-tuple-element.120.refs_0_), channel_id=1, source_target_pairs={{0,1},{1,2},{2,3},{3,0},{4,5},{5,6},{6,7},{7,4},{8,9},{9,10},{10,1... | collective-permute-start | bytes 6152 | tf_op jit(solution)/shard_map/ppermute | solution.py:344
  84.9 5.9 %collective-permute-start.19 = (f32[4,128]{1,0:T(4,128)S(1)}, f32[4,128]{1,0:T(4,128)S(1)}, u32[]{:S(2)}, u32[]{:S(2)}) collective-permute-start(f32[4,128]{1,0:T(4,128)S(1)} %get-tuple-element.120.refs_0_), channel_id=1, source_target_pairs={{0,2},{1,3},{2,0},{3,1},{4,6},{5,7},{6,4},{7,5},{8,10},{9,11},{10,... | collective-permute-start | bytes 6152 | tf_op jit(solution)/shard_map/ppermute | solution.py:344
  86.3 4.6 %collective-permute-start.20 = (f32[4,128]{1,0:T(4,128)S(1)}, f32[4,128]{1,0:T(4,128)S(1)}, u32[]{:S(2)}, u32[]{:S(2)}) collective-permute-start(f32[4,128]{1,0:T(4,128)S(1)} %get-tuple-element.120.refs_0_), channel_id=1, source_target_pairs={{0,3},{1,0},{2,1},{3,2},{4,7},{5,4},{6,5},{7,6},{8,11},{9,8},{10,9... | collective-permute-start | bytes 6152 | tf_op jit(solution)/shard_map/ppermute | solution.py:344

commit v14 on v12

--- a/solution.py
+++ b/solution.py
@@ -165,7 +165,7 @@
     (out[...],) = tap_products(end_block, [wide], [total], height, width)
 
 
-def input_grad_kernel(size, height, width, place, cotan, first, second, middle, far, own_mod, behind, ahead, *refs):
+def input_grad_kernel(rows, size, height, width, place, cotan, first, second, middle, far, own_mod, behind, ahead, *refs):
     others, (main, before, after, gathered, taps_t, total) = refs[: size - 2], refs[size - 2 :]
     ch = main.shape[0]
     spot = jnp.where(place[3] > 0, place[1], size - 1 - place[1])
@@ -195,7 +195,7 @@
         if row == 0:
             before[...] = value
         elif row == height + 1:
-            after[...] = value
+            after[...] = jnp.where(place[2] == 1, before[...], value) if rows == 2 else value
         else:
             main[:, (row - 1) * width : row * width] = value
 
@@ -266,9 +266,10 @@
 
 
 def bank_grad_kernel(samples, small_rows, place, bank, *refs):
-    parts, (bank_grad, style_grad, latents, held) = refs[:samples], refs[samples:]
+    parts, (bank_out, style_grad, latents, held, bank_grad, sems) = refs[:samples], refs[samples:]
+    copies = [pltpu.make_async_copy(bank_grad.at[:, tap], bank_out.at[:, tap], sems.at[tap]) for tap in range(TAPS)]
     for s in range(samples):
-        held[lax.rem(place[0] - s + samples, samples)] = parts[s][...]
+        held[partner(place[0], s, samples)] = parts[s][...]
     filters, in_ch = bank.shape[0], bank.shape[3]
     last = latents.shape[1] // in_ch
     sel, styles, scales, falls = [], [], [], []
@@ -293,9 +294,12 @@
                 totals[k] = term if totals[k] is None else totals[k] + term
         for k in range(filters):
             bank_grad[k, tap] = totals[k]
+        copies[tap].start()
     for b in range(samples):
         value = jnp.sum(sums[b], axis=0, keepdims=True)
         style_grad[b : b + 1] = value
+    for copy in copies:
+        copy.wait()
 
 
 def affine_kernel(samples, size, place, latents, *refs):
@@ -305,11 +309,12 @@
     style_grad = held[0]
     for z in range(1, size):
         style_grad = style_grad + held[z]
+    high, mid, low = split3(latents[...])
+    top, middle, bottom = split3(style_grad)
     w_grad[...] = lax.dot_general(
-        latents[...],
-        style_grad,
+        jnp.concatenate([high, high, mid, high, mid, low], axis=0).astype(BF16),
+        jnp.concatenate([top, middle, top, bottom, middle, top], axis=0).astype(BF16),
         (((0,), (0,)), ((), ())),
-        precision=lax.Precision.HIGHEST,
         preferred_element_type=F32,
     )
     bias = style_grad[0:1]
@@ -318,7 +323,7 @@
     b_grad[...] = bias
 
 
-def call(kernel, name, outs, *operands, scalars=0, fetched=0, scratch=(), flops=10**6):
+def call(kernel, name, outs, *operands, scalars=0, fetched=0, kept=0, scratch=(), flops=10**6):
     outs = tuple(jax.ShapeDtypeStruct(*o) for o in outs)
     moved = sum(o.size * o.dtype.itemsize for o in (*outs, *operands))
     return pl.pallas_call(
@@ -327,7 +332,7 @@
         in_specs=sspec(scalars)
         + vspec(len(operands) - scalars - fetched)
         + [pl.BlockSpec(memory_space=pltpu.HBM)] * fetched,
-        out_specs=tuple(vspec(len(outs))),
+        out_specs=tuple([pl.BlockSpec(memory_space=pltpu.HBM)] * kept + vspec(len(outs) - kept)),
         scratch_shapes=[pltpu.VMEM(*s) if isinstance(s, tuple) else s for s in scratch],
         compiler_params=params(),
         cost_estimate=cost(flops, moved),
@@ -335,6 +340,18 @@
     )(*operands)
 
 
+def partner(at, step, size):
+    return at ^ step if size & (size - 1) == 0 else (at - step + size) % size
+
+
+def exchange_pairs(x, axis):
+    size = lax.axis_size(axis)
+    got = {0: x}
+    for step in sorted(range(1, size), key=lambda n: (n < 2, n)):
+        got[step] = lax.ppermute(x, axis, [(partner(i, step, size), i) for i in range(size)])
+    return [got[step] for step in range(size)]
+
+
 def exchange(x, axis):
     size = lax.axis_size(axis)
     return [x] + [
@@ -345,7 +362,8 @@
 def from_sides(first, last, axis):
     size, at = lax.axis_size(axis), lax.axis_index(axis)
     if size == 2:
-        got = lax.ppermute(jnp.where(at == 0, last, first), axis, [(0, 1), (1, 0)])
+        edge = last if first is None else jnp.where(at == 0, last, first)
+        got = lax.ppermute(edge, axis, [(0, 1), (1, 0)])
         nothing = jnp.zeros_like(got)
         return jnp.where(at == 1, got, nothing), jnp.where(at == 0, got, nothing)
     up = [(i, i + 1) for i in range(size - 1)]
@@ -493,11 +511,11 @@
     ]
     slots = TAPS + 1 - (-3 * small_rows // out_ch)
     (own,) = call(row_sum_kernel, "row_sum", [((slots, out_ch, in_ch), BF16)], scale, small, *parts)
-    every = exchange(own, "samples")
+    every = exchange_pairs(own, "samples")
 
     own, others, far = lax.optimization_barrier((own, others, far))
     main, before, after = call(
-        functools.partial(input_grad_kernel, size, height, width),
+        functools.partial(input_grad_kernel, rows, size, height, width),
         "input_grad",
         [((ch, pixels), F32), ((ch, width), F32), ((ch, width), F32)],
         place,
@@ -519,7 +537,7 @@
         flops=INPUT_FLOPS,
     )
     every, main, before, after = lax.optimization_barrier((every, main, before, after))
-    from_above, from_below = from_sides(before, after, "rows")
+    from_above, from_below = from_sides(None if rows == 2 else before, after, "rows")
     bank_grad, style_part, latents = call(
         functools.partial(bank_grad_kernel, samples, small_rows),
         "bank_grad",
@@ -528,7 +546,8 @@
         bank,
         *every,
         scalars=1,
-        scratch=[((samples, slots, out_ch, in_ch), BF16)],
+        scratch=[((samples, slots, out_ch, in_ch), BF16), (bank.shape, F32), pltpu.SemaphoreType.DMA((TAPS,))],
+        kept=1,
     )
     style_parts = exchange(style_part, "chan")
     edge = jnp.concatenate(

time: 87 us -> 86.8 us (level)
  waiting for transfers between devices: 12.3 us -> 13.8 us
  starting transfers between devices: 44 us -> 42.6 us
    ppermute x7 -> x4, starting transfers between devices: 7.44 us -> 4.46 us  [exchange(): lax.ppermute(x, axis, [(i, (i + s) % size) for i in range(size)])]
    ppermute x2 -> x5, starting transfers between devices: 2.84 us -> 4.41 us  [the longest x2 2.47 us: from_sides(): got = lax.ppermute(edge, axis, [(0, 1), (1, 0)])]
    ppermute x1, waiting for transfers between devices: 0.5 us -> 1.59 us  [on_device(): lax.ppermute(mods[size], 'chan', [(0, size - 1), (size - 1, 0)])]
    ppermute x7 -> x4, waiting for transfers between devices: 2.91 us -> 2.92 us  [exchange(): lax.ppermute(x, axis, [(i, (i + s) % size) for i in range(size)])]
  transfers between devices with their start and end apart: 22 -> 22, of which waited for: 7 -> 8; matrix products, arithmetic and copies ran while one was open for 3% -> 3% of each run, Pallas kernels for 26% -> 26%
where the time goes in v14:
time: 86.8 us; the launch traced here: 86.3 us
  starting transfers between devices  42.6 us (49%)
  Pallas kernels  24.2 us (28%)
  waiting for transfers between devices  13.8 us (16%)
  local copies, waits for them, and re-layouts  3.49 us (4%)
  other arithmetic  1.25 us (1%)
  between operations  1 us (1%)
    pallas_call x11, Pallas kernels, call(): pl.pallas_call(kernel, out_shape=outs, in_specs=sspec(scalars) + vspec(le...  24.2 us
    ppermute x8, starting transfers between devices, along(): return lax.ppermute(x, ('samples', 'chan'), whole)  22.1 us
    ppermute x1, starting transfers between devices, on_device(): feat_end = lax.ppermute(feat, 'chan', [(0, 1), (size - 1, size - 2)])  5.29 us
    ppermute x1, waiting for transfers between devices, on_device(): from_end = lax.ppermute(grad_end, 'chan', [(1, size - 1), (size - 2, 0)])  4.71 us
    ppermute x4, starting transfers between devices, exchange(): lax.ppermute(x, axis, [(i, (i + s) % size) for i in range(size)])  4.46 us
    unnamed x19, local copies, waits for them, and re-layouts  3.13 us
    ppermute x4, waiting for transfers between devices, exchange(): lax.ppermute(x, axis, [(i, (i + s) % size) for i in range(size)])  2.92 us
    ppermute x1, starting transfers between devices, on_device(): lax.ppermute(mods[size], 'chan', [(0, size - 1), (size - 1, 0)])  2.8 us
  transfers between devices with their start and end apart: 22, of which 8 were waited for; matrix products, arithmetic and copies ran while one was open for 3% of the time, Pallas kernels for 26%

profile of v14, /device:TPU:0, one launch (start us, length us, event | category | flops | bytes accessed | tf_op | source)
XLA Modules:
  0.0 86.3 jit_solution(7128781584466056376)
XLA Ops:
  0.7 1.3 %copy.13 = bf16[8,8,8,512]{3,1,2,0:T(8,128)(2,1)S(1)} copy(bf16[8,8,8,512]{3,2,1,0:T(8,128)(2,1)} %bitcast.32) | data formatting | bytes 1048576
  2.0 5.7 %collective-permute-start.1 = (bf16[64,4096]{1,0:T(8,128)(2,1)S(1)}, bf16[64,4096]{1,0:T(8,128)(2,1)}, u32[]{:S(2)}, u32[]{:S(2)}) collective-permute-start(bf16[64,4096]{1,0:T(8,128)(2,1)S(1)} %bitcast.26), channel_id=1, source_target_pairs={{0,1},{1,2},{2,3},{7,6},{6,5},{5,4},{8,9},{9,10},{10,11},{15,14},{... | collective-permute-start | bytes 1572872 | tf_op jit(solution)/shard_map/ppermute | solution.py:391
  7.8 1.3 %collective-permute-start.2 = (bf16[64,4096]{1,0:T(8,128)(2,1)S(1)}, bf16[64,4096]{1,0:T(8,128)(2,1)}, u32[]{:S(2)}, u32[]{:S(2)}) collective-permute-start(bf16[64,4096]{1,0:T(8,128)(2,1)S(1)} %bitcast.27), channel_id=1, source_target_pairs={{1,0},{2,1},{3,2},{6,7},{5,6},{4,5},{9,8},{10,9},{11,10},{14,15},{... | collective-permute-start | bytes 1572872 | tf_op jit(solution)/shard_map/ppermute | solution.py:391
  9.1 0.2 copy.14
  9.3 1.6 %collective-permute-start.5 = (bf16[64,512]{1,0:T(8,128)(2,1)S(1)}, bf16[64,512]{1,0:T(8,128)(2,1)S(1)}, u32[]{:S(2)}, u32[]{:S(2)}) collective-permute-start(bf16[64,512]{1,0:T(8,128)(2,1)S(1)} %slice_select_fusion), channel_id=1, source_target_pairs={{0,16},{16,0},{1,17},{17,1},{2,18},{18,2},{3,19},{19,3},{4,20},{20... | collective-permute-start | bytes 196616 | tf_op jit(solution)/shard_map/ppermute | solution.py:366
  10.9 1.0 %plain.1 = (f32[10,64,128]{2,1,0:T(8,128)S(1)}, f32[8,128]{1,0:T(8,128)S(1)}) custom-call(s32[1,4]{1,0:T(1,128)S(1)} %copy-done.5, f32[1,512]{1,0:T(1,128)S(1)} %copy-done.4, f32[1,128]{1,0:T(1,128)S(1)} %bitcast.30, f32[512,128]{1,0:T(8,128)S(1)} %copy-done.3, f32[4,9,64,128]{3,2,1,0:T(8,128)S(1)} %copy-done), custom_call_target="tpu_custom_call" | custom-call | flops 1000000 | bytes 1776144 | tf_op jit(solution)/shard_map/plain/pallas_call | solution.py:329
  11.8 0.0 copy-start.1
  11.8 0.6 collective-permute-start
  12.4 1.2 %collective-permute-done.5 = bf16[64,512]{1,0:T(8,128)(2,1)S(1)} collective-permute-done((bf16[64,512]{1,0:T(8,128)(2,1)S(1)}, bf16[64,512]{1,0:T(8,128)(2,1)S(1)}, u32[]{:S(2)}, u32[]{:S(2)}) %collective-permute-start.5) | collective-permute-done | bytes 65568 | tf_op jit(solution)/shard_map/ppermute | solution.py:366
  13.7 5.3 %collective-permute-start.6 = (bf16[64,5120]{1,0:T(8,128)(2,1)S(1)}, bf16[64,5120]{1,0:T(8,128)(2,1)S(1)}, u32[]{:S(2)}, u32[]{:S(2)}) collective-permute-start(bf16[64,5120]{1,0:T(8,128)(2,1)S(1)} %feat_rows.1.refs_3_), channel_id=1, source_target_pairs={{0,1},{3,2},{4,5},{7,6},{8,9},{11,10},{12,13},{15,14},{16,17},{19,... | collective-permute-start | bytes 1966088 | tf_op jit(solution)/shard_map/ppermute | solution.py:431
  19.0 2.7 %collective-permute-done.refs_1_ = f32[10,64,128]{2,1,0:T(8,128)} collective-permute-done((f32[10,64,128]{2,1,0:T(8,128)S(1)}, f32[10,64,128]{2,1,0:T(8,128)}, u32[]{:S(2)}, u32[]{:S(2)}) %collective-permute-start) | collective-permute-done | bytes 327712 | tf_op jit(solution)/shard_map/ppermute | solution.py:358
  21.7 0.0 collective-permute-done.1.refs_1_.first
  21.7 0.0 collective-permute-done.2.refs_2_.second
  21.7 0.7 collective-permute-start.3
  22.4 1.3 %collective-permute-start.4 = (bf16[64,4096]{1,0:T(8,128)(2,1)}, bf16[64,4096]{1,0:T(8,128)(2,1)}, u32[]{:S(2)}, u32[]{:S(2)}) collective-permute-start(bf16[64,4096]{1,0:T(8,128)(2,1)} %collective-permute-done.2.refs_2_.second), channel_id=1, source_target_pairs={{1,0},{2,1},{6,7},{5,6},{9,8},{10,9},{14,15},{13,14},{17,16},{18,1... | collective-permute-start | bytes 1572872 | tf_op jit(solution)/shard_map/ppermute | solution.py:391
  23.7 0.1 pad_add_fusion.place
  23.8 1.0 %copy-done.2 = f32[10,64,128]{2,1,0:T(8,128)S(1)} copy-done((f32[10,64,128]{2,1,0:T(8,128)S(1)}, f32[10,64,128]{2,1,0:T(8,128)}, u32[]{:S(2)}) %copy-start.2) | copy-done | bytes 327704
  24.8 1.3 %mod_blocks.1 = (bf16[9,64,256]{2,1,0:T(8,128)(2,1)S(1)}, f32[64,128]{1,0:T(8,128)S(1)}, bf16[64,576]{1,0:T(8,128)(2,1)S(1)}, bf16[64,576]{1,0:T(8,128)(2,1)S(1)...) custom-call(s32[4]{0:T(128)S(1)} %pad_add_fusion.place, ...), custom_call_target="tpu_custom_call" | custom-call | flops 1000000 | bytes 1351696 | tf_op jit(solution)/shard_map/mod_blocks/pallas_call | solution.py:329
  26.0 4.5 %near_grad.1 = (bf16[64,576]{1,0:T(8,128)(2,1)S(1)}, bf16[128,576]{1,0:T(8,128)(2,1)S(1)}, bf16[128,576]{1,0:T(8,128)(2,1)S(1)}, bf16[192,5120]{1,0:T(8,128)(2,1)S(1)}) custom-call(bf16[64,4096]{1,0:T(8,128)(2,1)S(1)} %bitcast.28, bf16[64,4096]{1,0:T(8,128)(2,1)} %collective-permute-done.1.refs_1_.first, ...), custom_call_target="tpu_custom_call" | custom-call | flops 905969664 | bytes 4710400 | tf_op jit(solution)/shard_map/near_grad/pallas_call | solution.py:329
  30.6 1.3 %collective-permute-start.7 = (bf16[128,576]{1,0:T(8,128)(2,1)S(1)}, bf16[128,576]{1,0:T(8,128)(2,1)S(1)}, u32[]{:S(2)}, u32[]{:S(2)}) collective-permute-start(bf16[128,576]{1,0:T(8,128)(2,1)S(1)} %get-tuple-element.73), channel_id=1, source_target_pairs={{1,0},{2,1},{3,2},{6,7},{5,6},{4,5},{9,8},{10,9},{11,10},{14,15},{... | collective-permute-start | bytes 442376 | tf_op jit(solution)/shard_map/ppermute | solution.py:391
  31.9 7.5 %collective-permute-start.8 = (bf16[128,576]{1,0:T(8,128)(2,1)S(1)}, bf16[128,576]{1,0:T(8,128)(2,1)S(1)}, u32[]{:S(2)}, u32[]{:S(2)}) collective-permute-start(bf16[128,576]{1,0:T(8,128)(2,1)S(1)} %get-tuple-element.74), channel_id=1, source_target_pairs={{0,1},{1,2},{2,3},{7,6},{6,5},{5,4},{8,9},{9,10},{10,11},{15,14},{... | collective-permute-start | bytes 442376 | tf_op jit(solution)/shard_map/ppermute | solution.py:391
  39.4 0.0 collective-permute-done.6.feat
  39.4 0.0 collective-permute-done.3.refs_0_
  39.5 0.0 collective-permute-done.4.refs_1_
  39.5 3.7 %middle_grad.1 = (bf16[64,576]{1,0:T(8,128)(2,1)S(1)}, bf16[64,4096]{1,0:T(8,128)(2,1)S(1)}, bf16[64,4096]{1,0:T(8,128)(2,1)S(1)}) custom-call(bf16[64,4096]{1,0:T(8,128)(2,1)S(1)} %collective-permute-done.3.refs_0_, bf16[64,4096]{1,0:T(8,128)(2,1)} %collective-permute-done.4.refs_1_, bf16[192,5120]{1,0:T(8,128)(2,1)S(1)} %get-tuple-element.77.refs_2_), custom_call_target="tpu_custom_call" | custom-call | flops 301989888 | bytes 4136960 | tf_op jit(solution)/shard_map/middle_grad/pallas_call | solution.py:329
  43.2 4.3 %collective-permute-start.9 = (bf16[64,576]{1,0:T(8,128)(2,1)S(1)}, bf16[64,576]{1,0:T(8,128)(2,1)S(1)}, u32[]{:S(2)}, u32[]{:S(2)}) collective-permute-start(bf16[64,576]{1,0:T(8,128)(2,1)S(1)} %get-tuple-element.78), channel_id=1, source_target_pairs={{0,2},{1,3},{2,0},{3,1},{7,5},{6,4},{5,7},{4,6},{8,10},{9,11},{10,... | collective-permute-start | bytes 221192 | tf_op jit(solution)/shard_map/ppermute | solution.py:391
  47.5 3.0 %end_grad.1 = bf16[64,576]{1,0:T(8,128)(2,1)S(1)} custom-call(bf16[64,4096]{1,0:T(8,128)(2,1)S(1)} %get-tuple-element.91.end_block, bf16[64,5120]{1,0:T(8,128)(2,1)S(1)} %collective-permute-done.6.feat), custom_call_target="tpu_custom_call" | custom-call | flops 301989888 | bytes 1253376 | tf_op jit(solution)/shard_map/end_grad/pallas_call | solution.py:329
  50.5 1.3 %collective-permute-start.10 = (bf16[64,576]{1,0:T(8,128)(2,1)S(1)}, bf16[64,576]{1,0:T(8,128)(2,1)S(1)}, u32[]{:S(2)}, u32[]{:S(2)}) collective-permute-start(bf16[64,576]{1,0:T(8,128)(2,1)S(1)} %end_grad.1), channel_id=1, source_target_pairs={{1,3},{2,0},{5,7},{6,4},{9,11},{10,8},{13,15},{14,12},{17,19},{18,... | collective-permute-start | bytes 221192 | tf_op jit(solution)/shard_map/ppermute | solution.py:486
  51.8 1.3 %collective-permute-start.17 = (bf16[64,4096]{1,0:T(8,128)(2,1)S(1)}, bf16[64,4096]{1,0:T(8,128)(2,1)S(1)}, u32[]{:S(2)}, u32[]{:S(2)}) collective-permute-start(bf16[64,4096]{1,0:T(8,128)(2,1)S(1)} %get-tuple-element.91.end_block), channel_id=1, source_target_pairs={{1,0},{2,3},{5,4},{6,7},{9,8},{10,11},{13,12},{14,15},{17,16},{18,... | collective-permute-start | bytes 1572872 | tf_op jit(solution)/shard_map/ppermute | solution.py:488
  53.1 0.0 collective-permute-done.7.ahead
  53.2 0.0 collective-permute-done.8.behind
  53.2 0.0 collective-permute-done.9.others
  53.2 4.7 %collective-permute-done.10.end = bf16[64,576]{1,0:T(8,128)(2,1)S(1)} collective-permute-done((bf16[64,576]{1,0:T(8,128)(2,1)S(1)}, bf16[64,576]{1,0:T(8,128)(2,1)S(1)}, u32[]{:S(2)}, u32[]{:S(2)}) %collective-permute-start.10) | collective-permute-done | bytes 73760 | tf_op jit(solution)/shard_map/ppermute | solution.py:486
  57.9 1.1 %collect.1 = (bf16[10,64,128]{2,1,0:T(8,128)(2,1)S(1)}, bf16[10,64,128]{2,1,0:T(8,128)(2,1)S(1)}) custom-call(s32[4]{0:T(128)S(1)} %pad_add_fusion.place, f32[64,128]{1,0:T(8,128)S(1)} %get-tuple-element.60.scale, bf16[9,64,256]{2,1,0:T(8,128)(2,1)S(1)} %get-tuple-element.71.whole_mod, bf16[64,576]{1,0:T(8,128)(2,1)S(1)} %get-tuple-element.72.own, ...), custom_call_target="tpu_custom_call" | custom-call | flops 6000000000 | bytes 1171472 | tf_op jit(solution)/shard_map/collect/pallas_call | solution.py:329
  58.9 0.9 %collective-permute-start.11 = (bf16[10,64,128]{2,1,0:T(8,128)(2,1)S(1)}, bf16[10,64,128]{2,1,0:T(8,128)(2,1)S(1)}, u32[]{:S(2)}, u32[]{:S(2)}) collective-permute-start(bf16[10,64,128]{2,1,0:T(8,128)(2,1)S(1)} %get-tuple-element.87), channel_id=1, source_target_pairs={{0,16},{16,0},{1,17},{17,1},{2,18},{18,2},{3,19},{19,3},{4,20},{20... | collective-permute-start | bytes 491528 | tf_op jit(solution)/shard_map/ppermute | solution.py:509
  59.9 0.0 collective-permute-start.15
  59.9 2.8 %collective-permute-start.16 = (bf16[64,576]{1,0:T(8,128)(2,1)S(1)}, bf16[64,576]{1,0:T(8,128)(2,1)S(1)}, u32[]{:S(2)}, u32[]{:S(2)}) collective-permute-start(bf16[64,576]{1,0:T(8,128)(2,1)S(1)} %get-tuple-element.90), channel_id=1, source_target_pairs={{0,3},{3,0},{4,7},{7,4},{8,11},{11,8},{12,15},{15,12},{16,19},{19,... | collective-permute-start | bytes 221192 | tf_op jit(solution)/shard_map/ppermute | solution.py:507
  62.7 1.7 %collective-permute-done.11.refs_1_ = bf16[10,64,128]{2,1,0:T(8,128)(2,1)S(1)} collective-permute-done((bf16[10,64,128]{2,1,0:T(8,128)(2,1)S(1)}, bf16[10,64,128]{2,1,0:T(8,128)(2,1)S(1)}, u32[]{:S(2)}, u32[]{:S(2)}) %collective-permute-start.11) | collective-permute-done | bytes 163872 | tf_op jit(solution)/shard_map/ppermute | solution.py:509
  64.3 0.2 row_sum.1.refs_0_
  64.5 0.1 collective-permute-start.12
  64.6 1.6 %collective-permute-start.13 = (bf16[11,64,128]{2,1,0:T(8,128)(2,1)S(1)}, bf16[11,64,128]{2,1,0:T(8,128)(2,1)S(1)}, u32[]{:S(2)}, u32[]{:S(2)}) collective-permute-start(bf16[11,64,128]{2,1,0:T(8,128)(2,1)S(1)} %row_sum.1.refs_0_), channel_id=1, source_target_pairs={{8,0},{12,4},{0,8},{4,12},{9,1},{13,5},{1,9},{5,13},{10,2},{14,6},... | collective-permute-start | bytes 540680 | tf_op jit(solution)/shard_map/ppermute | solution.py:351
  66.2 0.0 collective-permute-done.15.refs_0_
  66.2 0.3 collective-permute-start.14
  66.5 1.6 %collective-permute-done.16.refs_1_ = bf16[64,576]{1,0:T(8,128)(2,1)S(1)} collective-permute-done((bf16[64,576]{1,0:T(8,128)(2,1)S(1)}, bf16[64,576]{1,0:T(8,128)(2,1)S(1)}, u32[]{:S(2)}, u32[]{:S(2)}) %collective-permute-start.16) | collective-permute-done | bytes 73760 | tf_op jit(solution)/shard_map/ppermute | solution.py:507
  68.1 1.3 %collective-permute-done.17.far = bf16[64,4096]{1,0:T(8,128)(2,1)S(1)} collective-permute-done((bf16[64,4096]{1,0:T(8,128)(2,1)S(1)}, bf16[64,4096]{1,0:T(8,128)(2,1)S(1)}, u32[]{:S(2)}, u32[]{:S(2)}) %collective-permute-start.17) | collective-permute-done | bytes 524320 | tf_op jit(solution)/shard_map/ppermute | solution.py:488
  69.4 5.2 %input_grad.1 = (f32[64,4096]{1,0:T(8,128)S(1)}, f32[64,512]{1,0:T(8,128)}, f32[64,512]{1,0:T(8,128)S(1)}) custom-call(s32[4]{0:T(128)S(1)} %pad_add_fusion.place, bf16[64,4096]{1,0:T(8,128)(2,1)S(1)} %bitcast.29, bf16[64,4096]{1,0:T(8,128)(2,1)} %collective-permute-done.1.refs_1_.first, bf16[64,4096]{1,0:T(8,128)(2,1)} %collective-permute-done.2.refs_2_.second, ...), custom_call_target="tpu_custom_call" | custom-call | flops 2000000000 | bytes 4448272 | tf_op jit(solution)/shard_map/input_grad/pallas_call | solution.py:329
  74.6 0.0 collective-permute-done.12.refs_1_
  74.6 0.0 collective-permute-done.13.refs_2_
  74.6 0.4 collective-permute-done.14.refs_3_
  75.0 0.9 %collective-permute-start.21 = (f32[64,512]{1,0:T(8,128)S(1)}, f32[64,512]{1,0:T(8,128)S(1)}, u32[]{:S(2)}, u32[]{:S(2)}) collective-permute-start(f32[64,512]{1,0:T(8,128)S(1)} %get-tuple-element.104), channel_id=1, source_target_pairs={{0,16},{16,0},{1,17},{17,1},{2,18},{18,2},{3,19},{19,3},{4,20},{20... | collective-permute-start | bytes 393224 | tf_op jit(solution)/shard_map/ppermute | solution.py:366
  75.9 0.1 pad.1.clone
  76.0 2.7 %bank_grad.1 = (f32[4,9,64,128]{3,2,1,0:T(8,128)}, f32[4,128]{1,0:T(4,128)S(1)}, f32[4,512]{1,0:T(4,128)S(1)}) custom-call(s32[4]{0:T(128)S(1)} %pad_add_fusion.place, f32[4,9,64,128]{3,2,1,0:T(8,128)S(1)} %copy-done, bf16[11,64,128]{2,1,0:T(8,128)(2,1)S(1)} %row_sum.1.refs_0_, bf16[11,64,128]{2,1,0:T(8,128)(2,1)S(1)} %collective-permute-done.12.refs_1_, ...), custom_call_target="tpu_custom_call" | custom-call | flops 1000000 | bytes 3090448 | tf_op jit(solution)/shard_map/bank_grad/pallas_call | solution.py:329
  78.7 0.1 collective-permute-start.18
  78.8 2.5 %collective-permute-start.19 = (f32[4,128]{1,0:T(4,128)S(1)}, f32[4,128]{1,0:T(4,128)S(1)}, u32[]{:S(2)}, u32[]{:S(2)}) collective-permute-start(f32[4,128]{1,0:T(4,128)S(1)} %get-tuple-element.108.refs_0_), channel_id=1, source_target_pairs={{0,2},{1,3},{2,0},{3,1},{4,6},{5,7},{6,4},{7,5},{8,10},{9,11},{10,... | collective-permute-start | bytes 6152 | tf_op jit(solution)/shard_map/ppermute | solution.py:358
  81.2 1.3 %collective-permute-start.20 = (f32[4,128]{1,0:T(4,128)S(1)}, f32[4,128]{1,0:T(4,128)S(1)}, u32[]{:S(2)}, u32[]{:S(2)}) collective-permute-start(f32[4,128]{1,0:T(4,128)S(1)} %get-tuple-element.108.refs_0_), channel_id=1, source_target_pairs={{0,3},{1,0},{2,1},{3,2},{4,7},{5,4},{6,5},{7,6},{8,11},{9,8},{10,9... | collective-permute-start | bytes 6152 | tf_op jit(solution)/shard_map/ppermute | solution.py:358
  82.6 0.6 copy.15
  83.2 0.0 collective-permute-done.21
  83.2 0.1 copy.12
  83.4 0.1 copy.11
  83.5 1.1 %fusion = bf16[1,64,8,512]{3,2,1,0:T(8,128)(2,1)} fusion(f32[1,64,1,512]{3,2,1,0:T(1,128)S(1)} %copy.12, f32[1,64,1,512]{3,2,1,0:T(1,128)S(1)} %copy.11, f32[8]{0:T(128)S(1)} %pad.1.clone, f32[1,64,8,512]{3,2,1,0:T(8,128)S(1)} %bitcast.31), kind=kLoop, calls=%fused_computation.1 | loop fusion | flops 1048576 | bytes 1835040 | tf_op jit(solution)/shard_map/convert_element_type | solution.py:556
  84.6 0.0 collective-permute-done.18.refs_1_
  84.6 0.0 collective-permute-done.19.refs_2_
  84.6 0.2 collective-permute-done.20.refs_3_
  84.8 1.5 %affine.1 = (f32[512,128]{1,0:T(8,128)}, f32[1,128]{1,0:T(1,128)}) custom-call(s32[4]{0:T(128)S(1)} %pad_add_fusion.place, f32[4,512]{1,0:T(4,128)S(1)} %get-tuple-element.107.latents, f32[4,128]{1,0:T(4,128)S(1)} %get-tuple-element.108.refs_0_, f32[4,128]{1,0:T(4,128)S(1)} %collective-permute-done.18.refs_1_, f32[4,128]{1,0:T(4,128)S(1)} %collective-permute-done.19.refs_2_, ...), custom_call_target="tpu_custom_call" | custom-call | flops 1000000 | bytes 279056 | tf_op jit(solution)/shard_map/affine/pallas_call | solution.py:329
  (19 shorter events, 0.1 us)
Async XLA Ops:
  0.6 8.4 %copy-start.7 = (bf16[1,64,8,512]{3,2,1,0:T(8,128)(2,1)S(1)}, bf16[1,64,8,512]{3,2,1,0:T(8,128)(2,1)}, u32[]{:S(2)}) copy-start(bf16[1,64,8,512]{3,2,1,0:T(8,128)(2,1)} %param.7) | copy-start | bytes 1572868
  0.6 10.2 %copy-start = (f32[4,9,64,128]{3,2,1,0:T(8,128)S(1)}, f32[4,9,64,128]{3,2,1,0:T(8,128)}, u32[]{:S(2)}) copy-start(f32[4,9,64,128]{3,2,1,0:T(8,128)} %bank.1) | copy-start | bytes 3538948
  0.7 10.2 %copy-start.5 = (s32[1,4]{1,0:T(1,128)S(1)}, s32[1,4]{1,0:T(1,128)}, u32[]{:S(2)}) copy-start(s32[1,4]{1,0:T(1,128)} %refs_0_.1) | copy-start | bytes 52
  0.7 10.2 %copy-start.4 = (f32[1,512]{1,0:T(1,128)S(1)}, f32[1,512]{1,0:T(1,128)}, u32[]{:S(2)}) copy-start(f32[1,512]{1,0:T(1,128)} %refs_1_.1) | copy-start | bytes 6148
  0.7 10.2 %copy-start.6 = (f32[128]{0:T(128)S(1)}, f32[128]{0:T(128)}, u32[]{:S(2)}) copy-start(f32[128]{0:T(128)} %param.13) | copy-start | bytes 1540
  0.7 10.2 %copy-start.3 = (f32[512,128]{1,0:T(8,128)S(1)}, f32[512,128]{1,0:T(8,128)}, u32[]{:S(2)}) copy-start(f32[512,128]{1,0:T(8,128)} %refs_3_.1) | copy-start | bytes 786436
  2.0 19.7 %collective-permute-start.1 = (bf16[64,4096]{1,0:T(8,128)(2,1)S(1)}, bf16[64,4096]{1,0:T(8,128)(2,1)}, u32[]{:S(2)}, u32[]{:S(2)}) collective-permute-start(bf16[64,4096]{1,0:T(8,128)(2,1)S(1)} %bitcast.26), channel_id=1, source_target_pairs={{0,1},{1,2},{2,3},{7,6},{6,5},{5,4},{8,9},{9,10},{10,11},{15,14},{... | collective-permute-start | bytes 1572872 | tf_op jit(solution)/shard_map/ppermute | solution.py:391
  7.8 13.9 %collective-permute-start.2 = (bf16[64,4096]{1,0:T(8,128)(2,1)S(1)}, bf16[64,4096]{1,0:T(8,128)(2,1)}, u32[]{:S(2)}, u32[]{:S(2)}) collective-permute-start(bf16[64,4096]{1,0:T(8,128)(2,1)S(1)} %bitcast.27), channel_id=1, source_target_pairs={{1,0},{2,1},{3,2},{6,7},{5,6},{4,5},{9,8},{10,9},{11,10},{14,15},{... | collective-permute-start | bytes 1572872 | tf_op jit(solution)/shard_map/ppermute | solution.py:391
  9.3 4.3 %collective-permute-start.5 = (bf16[64,512]{1,0:T(8,128)(2,1)S(1)}, bf16[64,512]{1,0:T(8,128)(2,1)S(1)}, u32[]{:S(2)}, u32[]{:S(2)}) collective-permute-start(bf16[64,512]{1,0:T(8,128)(2,1)S(1)} %slice_select_fusion), channel_id=1, source_target_pairs={{0,16},{16,0},{1,17},{17,1},{2,18},{18,2},{3,19},{19,3},{4,20},{20... | collective-permute-start | bytes 196616 | tf_op jit(solution)/shard_map/ppermute | solution.py:366
  11.8 9.9 %copy-start.1 = (f32[10,64,128]{2,1,0:T(8,128)}, f32[10,64,128]{2,1,0:T(8,128)S(1)}, u32[]{:S(2)}) copy-start(f32[10,64,128]{2,1,0:T(8,128)S(1)} %get-tuple-element.59.refs_0_) | copy-start | bytes 983044
  11.8 9.8 %collective-permute-start = (f32[10,64,128]{2,1,0:T(8,128)S(1)}, f32[10,64,128]{2,1,0:T(8,128)}, u32[]{:S(2)}, u32[]{:S(2)}) collective-permute-start(f32[10,64,128]{2,1,0:T(8,128)S(1)} %get-tuple-element.59.refs_0_), channel_id=1, source_target_pairs={{0,16},{16,0},{1,17},{17,1},{2,18},{18,2},{3,19},{19,3},{4,20},{20... | collective-permute-start | bytes 983048 | tf_op jit(solution)/shard_map/ppermute | solution.py:358
  13.7 25.8 %collective-permute-start.6 = (bf16[64,5120]{1,0:T(8,128)(2,1)S(1)}, bf16[64,5120]{1,0:T(8,128)(2,1)S(1)}, u32[]{:S(2)}, u32[]{:S(2)}) collective-permute-start(bf16[64,5120]{1,0:T(8,128)(2,1)S(1)} %feat_rows.1.refs_3_), channel_id=1, source_target_pairs={{0,1},{3,2},{4,5},{7,6},{8,9},{11,10},{12,13},{15,14},{16,17},{19,... | collective-permute-start | bytes 1966088 | tf_op jit(solution)/shard_map/ppermute | solution.py:431
  21.7 17.7 %collective-permute-start.3 = (bf16[64,4096]{1,0:T(8,128)(2,1)}, bf16[64,4096]{1,0:T(8,128)(2,1)S(1)}, u32[]{:S(2)}, u32[]{:S(2)}) collective-permute-start(bf16[64,4096]{1,0:T(8,128)(2,1)} %collective-permute-done.1.refs_1_.first), channel_id=1, source_target_pairs={{1,2},{2,3},{6,5},{5,4},{9,10},{10,11},{14,13},{13,12},{17,18},{18... | collective-permute-start | bytes 1572872 | tf_op jit(solution)/shard_map/ppermute | solution.py:391
  22.4 17.0 %collective-permute-start.4 = (bf16[64,4096]{1,0:T(8,128)(2,1)}, bf16[64,4096]{1,0:T(8,128)(2,1)}, u32[]{:S(2)}, u32[]{:S(2)}) collective-permute-start(bf16[64,4096]{1,0:T(8,128)(2,1)} %collective-permute-done.2.refs_2_.second), channel_id=1, source_target_pairs={{1,0},{2,1},{6,7},{5,6},{9,8},{10,9},{14,15},{13,14},{17,16},{18,1... | collective-permute-start | bytes 1572872 | tf_op jit(solution)/shard_map/ppermute | solution.py:391
  23.8 1.0 %copy-start.2 = (f32[10,64,128]{2,1,0:T(8,128)S(1)}, f32[10,64,128]{2,1,0:T(8,128)}, u32[]{:S(2)}) copy-start(f32[10,64,128]{2,1,0:T(8,128)} %copy-done.1) | copy-start | bytes 983044
  30.6 22.6 %collective-permute-start.7 = (bf16[128,576]{1,0:T(8,128)(2,1)S(1)}, bf16[128,576]{1,0:T(8,128)(2,1)S(1)}, u32[]{:S(2)}, u32[]{:S(2)}) collective-permute-start(bf16[128,576]{1,0:T(8,128)(2,1)S(1)} %get-tuple-element.73), channel_id=1, source_target_pairs={{1,0},{2,1},{3,2},{6,7},{5,6},{4,5},{9,8},{10,9},{11,10},{14,15},{... | collective-permute-start | bytes 442376 | tf_op jit(solution)/shard_map/ppermute | solution.py:391
  31.9 21.3 %collective-permute-start.8 = (bf16[128,576]{1,0:T(8,128)(2,1)S(1)}, bf16[128,576]{1,0:T(8,128)(2,1)S(1)}, u32[]{:S(2)}, u32[]{:S(2)}) collective-permute-start(bf16[128,576]{1,0:T(8,128)(2,1)S(1)} %get-tuple-element.74), channel_id=1, source_target_pairs={{0,1},{1,2},{2,3},{7,6},{6,5},{5,4},{8,9},{9,10},{10,11},{15,14},{... | collective-permute-start | bytes 442376 | tf_op jit(solution)/shard_map/ppermute | solution.py:391
  43.2 10.0 %collective-permute-start.9 = (bf16[64,576]{1,0:T(8,128)(2,1)S(1)}, bf16[64,576]{1,0:T(8,128)(2,1)S(1)}, u32[]{:S(2)}, u32[]{:S(2)}) collective-permute-start(bf16[64,576]{1,0:T(8,128)(2,1)S(1)} %get-tuple-element.78), channel_id=1, source_target_pairs={{0,2},{1,3},{2,0},{3,1},{7,5},{6,4},{5,7},{4,6},{8,10},{9,11},{10,... | collective-permute-start | bytes 221192 | tf_op jit(solution)/shard_map/ppermute | solution.py:391
  50.5 7.3 %collective-permute-start.10 = (bf16[64,576]{1,0:T(8,128)(2,1)S(1)}, bf16[64,576]{1,0:T(8,128)(2,1)S(1)}, u32[]{:S(2)}, u32[]{:S(2)}) collective-permute-start(bf16[64,576]{1,0:T(8,128)(2,1)S(1)} %end_grad.1), channel_id=1, source_target_pairs={{1,3},{2,0},{5,7},{6,4},{9,11},{10,8},{13,15},{14,12},{17,19},{18,... | collective-permute-start | bytes 221192 | tf_op jit(solution)/shard_map/ppermute | solution.py:486
  51.8 17.6 %collective-permute-start.17 = (bf16[64,4096]{1,0:T(8,128)(2,1)S(1)}, bf16[64,4096]{1,0:T(8,128)(2,1)S(1)}, u32[]{:S(2)}, u32[]{:S(2)}) collective-permute-start(bf16[64,4096]{1,0:T(8,128)(2,1)S(1)} %get-tuple-element.91.end_block), channel_id=1, source_target_pairs={{1,0},{2,3},{5,4},{6,7},{9,8},{10,11},{13,12},{14,15},{17,16},{18,... | collective-permute-start | bytes 1572872 | tf_op jit(solution)/shard_map/ppermute | solution.py:488
  58.9 5.4 %collective-permute-start.11 = (bf16[10,64,128]{2,1,0:T(8,128)(2,1)S(1)}, bf16[10,64,128]{2,1,0:T(8,128)(2,1)S(1)}, u32[]{:S(2)}, u32[]{:S(2)}) collective-permute-start(bf16[10,64,128]{2,1,0:T(8,128)(2,1)S(1)} %get-tuple-element.87), channel_id=1, source_target_pairs={{0,16},{16,0},{1,17},{17,1},{2,18},{18,2},{3,19},{19,3},{4,20},{20... | collective-permute-start | bytes 491528 | tf_op jit(solution)/shard_map/ppermute | solution.py:509
  59.9 6.4 %collective-permute-start.15 = (bf16[64,576]{1,0:T(8,128)(2,1)S(1)}, bf16[64,576]{1,0:T(8,128)(2,1)S(1)}, u32[]{:S(2)}, u32[]{:S(2)}) collective-permute-start(bf16[64,576]{1,0:T(8,128)(2,1)S(1)} %get-tuple-element.89), channel_id=1, source_target_pairs={{0,2},{1,3},{2,0},{3,1},{7,5},{6,4},{5,7},{4,6},{8,10},{9,11},{10,... | collective-permute-start | bytes 221192 | tf_op jit(solution)/shard_map/ppermute | solution.py:391
  59.9 8.2 %collective-permute-start.16 = (bf16[64,576]{1,0:T(8,128)(2,1)S(1)}, bf16[64,576]{1,0:T(8,128)(2,1)S(1)}, u32[]{:S(2)}, u32[]{:S(2)}) collective-permute-start(bf16[64,576]{1,0:T(8,128)(2,1)S(1)} %get-tuple-element.90), channel_id=1, source_target_pairs={{0,3},{3,0},{4,7},{7,4},{8,11},{11,8},{12,15},{15,12},{16,19},{19,... | collective-permute-start | bytes 221192 | tf_op jit(solution)/shard_map/ppermute | solution.py:507
  64.5 10.1 %collective-permute-start.12 = (bf16[11,64,128]{2,1,0:T(8,128)(2,1)S(1)}, bf16[11,64,128]{2,1,0:T(8,128)(2,1)S(1)}, u32[]{:S(2)}, u32[]{:S(2)}) collective-permute-start(bf16[11,64,128]{2,1,0:T(8,128)(2,1)S(1)} %row_sum.1.refs_0_), channel_id=1, source_target_pairs={{4,0},{0,4},{12,8},{8,12},{5,1},{1,5},{13,9},{9,13},{6,2},{2,6},{1... | collective-permute-start | bytes 540680 | tf_op jit(solution)/shard_map/ppermute | solution.py:351
  64.6 10.0 %collective-permute-start.13 = (bf16[11,64,128]{2,1,0:T(8,128)(2,1)S(1)}, bf16[11,64,128]{2,1,0:T(8,128)(2,1)S(1)}, u32[]{:S(2)}, u32[]{:S(2)}) collective-permute-start(bf16[11,64,128]{2,1,0:T(8,128)(2,1)S(1)} %row_sum.1.refs_0_), channel_id=1, source_target_pairs={{8,0},{12,4},{0,8},{4,12},{9,1},{13,5},{1,9},{5,13},{10,2},{14,6},... | collective-permute-start | bytes 540680 | tf_op jit(solution)/shard_map/ppermute | solution.py:351
  66.2 8.8 %collective-permute-start.14 = (bf16[11,64,128]{2,1,0:T(8,128)(2,1)S(1)}, bf16[11,64,128]{2,1,0:T(8,128)(2,1)S(1)}, u32[]{:S(2)}, u32[]{:S(2)}) collective-permute-start(bf16[11,64,128]{2,1,0:T(8,128)(2,1)S(1)} %row_sum.1.refs_0_), channel_id=1, source_target_pairs={{12,0},{8,4},{4,8},{0,12},{13,1},{9,5},{5,9},{1,13},{14,2},{10,6},... | collective-permute-start | bytes 540680 | tf_op jit(solution)/shard_map/ppermute | solution.py:351
  75.0 8.2 %collective-permute-start.21 = (f32[64,512]{1,0:T(8,128)S(1)}, f32[64,512]{1,0:T(8,128)S(1)}, u32[]{:S(2)}, u32[]{:S(2)}) collective-permute-start(f32[64,512]{1,0:T(8,128)S(1)} %get-tuple-element.104), channel_id=1, source_target_pairs={{0,16},{16,0},{1,17},{17,1},{2,18},{18,2},{3,19},{19,3},{4,20},{20... | collective-permute-start | bytes 393224 | tf_op jit(solution)/shard_map/ppermute | solution.py:366
  78.7 5.9 %collective-permute-start.18 = (f32[4,128]{1,0:T(4,128)S(1)}, f32[4,128]{1,0:T(4,128)S(1)}, u32[]{:S(2)}, u32[]{:S(2)}) collective-permute-start(f32[4,128]{1,0:T(4,128)S(1)} %get-tuple-element.108.refs_0_), channel_id=1, source_target_pairs={{0,1},{1,2},{2,3},{3,0},{4,5},{5,6},{6,7},{7,4},{8,9},{9,10},{10,1... | collective-permute-start | bytes 6152 | tf_op jit(solution)/shard_map/ppermute | solution.py:358
  78.8 5.9 %collective-permute-start.19 = (f32[4,128]{1,0:T(4,128)S(1)}, f32[4,128]{1,0:T(4,128)S(1)}, u32[]{:S(2)}, u32[]{:S(2)}) collective-permute-start(f32[4,128]{1,0:T(4,128)S(1)} %get-tuple-element.108.refs_0_), channel_id=1, source_target_pairs={{0,2},{1,3},{2,0},{3,1},{4,6},{5,7},{6,4},{7,5},{8,10},{9,11},{10,... | collective-permute-start | bytes 6152 | tf_op jit(solution)/shard_map/ppermute | solution.py:358
  81.2 3.6 %collective-permute-start.20 = (f32[4,128]{1,0:T(4,128)S(1)}, f32[4,128]{1,0:T(4,128)S(1)}, u32[]{:S(2)}, u32[]{:S(2)}) collective-permute-start(f32[4,128]{1,0:T(4,128)S(1)} %get-tuple-element.108.refs_0_), channel_id=1, source_target_pairs={{0,3},{1,0},{2,1},{3,2},{4,7},{5,4},{6,5},{7,6},{8,11},{9,8},{10,9... | collective-permute-start | bytes 6152 | tf_op jit(solution)/shard_map/ppermute | solution.py:358

commit v15 on v14

--- a/solution.py
+++ b/solution.py
@@ -268,8 +268,8 @@
 def bank_grad_kernel(samples, small_rows, place, bank, *refs):
     parts, (bank_out, style_grad, latents, held, bank_grad, sems) = refs[:samples], refs[samples:]
     copies = [pltpu.make_async_copy(bank_grad.at[:, tap], bank_out.at[:, tap], sems.at[tap]) for tap in range(TAPS)]
-    for s in range(samples):
-        held[partner(place[0], s, samples)] = parts[s][...]
+    for part, step in zip(parts, steps_of(samples)):
+        held[partner(place[0], step, samples)] = part[...]
     filters, in_ch = bank.shape[0], bank.shape[3]
     last = latents.shape[1] // in_ch
     sel, styles, scales, falls = [], [], [], []
@@ -302,13 +302,11 @@
         copy.wait()
 
 
-def affine_kernel(samples, size, place, latents, *refs):
-    parts, (w_grad, b_grad, held) = refs[:size], refs[size:]
-    for d in range(size):
-        held[lax.rem(place[1] - d + size, size)] = parts[d][...]
-    style_grad = held[0]
-    for z in range(1, size):
-        style_grad = style_grad + held[z]
+def affine_kernel(samples, latents, *refs):
+    parts, (w_grad, b_grad) = refs[:-2], refs[-2:]
+    style_grad = parts[0][...]
+    for part in parts[1:]:
+        style_grad = style_grad + part[...]
     high, mid, low = split3(latents[...])
     top, middle, bottom = split3(style_grad)
     w_grad[...] = lax.dot_general(
@@ -344,12 +342,15 @@
     return at ^ step if size & (size - 1) == 0 else (at - step + size) % size
 
 
+def steps_of(size):
+    return [0] + sorted(range(1, size), key=lambda n: (n < 2, n))
+
+
 def exchange_pairs(x, axis):
     size = lax.axis_size(axis)
-    got = {0: x}
-    for step in sorted(range(1, size), key=lambda n: (n < 2, n)):
-        got[step] = lax.ppermute(x, axis, [(partner(i, step, size), i) for i in range(size)])
-    return [got[step] for step in range(size)]
+    return [x] + [
+        lax.ppermute(x, axis, [(partner(i, step, size), i) for i in range(size)]) for step in steps_of(size)[1:]
+    ]
 
 
 def exchange(x, axis):
@@ -357,6 +358,18 @@
     return [x] + [
         lax.ppermute(x, axis, [(i, (i + s) % size) for i in range(size)]) for s in range(1, size)
     ]
+
+
+def halves_of_sum(x, axis):
+    size = lax.axis_size(axis)
+    if size & (size - 1):
+        return [lax.psum(x, axis)]
+    step, parts = 1, [x]
+    while step < size:
+        x = sum(parts[1:], parts[0])
+        parts = [x, lax.ppermute(x, axis, [(i, i ^ step) for i in range(size)])]
+        step *= 2
+    return parts
 
 
 def from_sides(first, last, axis):
@@ -549,21 +562,18 @@
         scratch=[((samples, slots, out_ch, in_ch), BF16), (bank.shape, F32), pltpu.SemaphoreType.DMA((TAPS,))],
         kept=1,
     )
-    style_parts = exchange(style_part, "chan")
+    style_parts = halves_of_sum(style_part, "chan")
     edge = jnp.concatenate(
         [from_above[:, None], jnp.zeros((ch, height - 2, width), F32), from_below[:, None]], axis=1
     )
     feature_grad = (main.reshape(ch, height, width) + edge).astype(BF16)[None]
     style_parts, feature_grad = lax.optimization_barrier((style_parts, feature_grad))
     affine_w_grad, affine_b_grad = call(
-        functools.partial(affine_kernel, samples, size),
+        functools.partial(affine_kernel, samples),
         "affine",
         [(affine_w.shape, F32), ((1, in_ch), F32)],
-        place,
         latents,
         *style_parts,
-        scalars=1,
-        scratch=[((size, samples, in_ch), F32)],
     )
     return (feature_grad, bank_grad, affine_w_grad, affine_b_grad[0])
 

time: 86.8 us -> 88.1 us (1.015)
  waiting for transfers between devices: 13.8 us -> 18.4 us
  starting transfers between devices: 42.6 us -> 40 us
    ppermute x0 -> x2, waiting for transfers between devices: none -> 5.42 us  [halves_of_sum(): parts = [x, lax.ppermute(x, axis, [(i, i ^ step) for i in range(size)])]]
    ppermute x4 -> x1, starting transfers between devices: 4.46 us -> 0.6 us  [exchange(): lax.ppermute(x, axis, [(i, (i + s) % size) for i in range(size)])]
    ppermute x4 -> x1, waiting for transfers between devices: 2.92 us -> 2.71 us  [exchange(): lax.ppermute(x, axis, [(i, (i + s) % size) for i in range(size)])]
  transfers between devices with their start and end apart: 22 -> 21, of which waited for: 8 -> 8; matrix products, arithmetic and copies ran while one was open for 3% -> 3% of each run, Pallas kernels for 26% -> 26%
where the time goes in v15:
time: 88.1 us; the launch traced here: 87.7 us
  starting transfers between devices  40 us (45%)
  Pallas kernels  23.6 us (27%)
  waiting for transfers between devices  18.4 us (21%)
  local copies, waits for them, and re-layouts  3.48 us (4%)
  other arithmetic  1.23 us (1%)
  between operations  1 us (1%)
    pallas_call x11, Pallas kernels, call(): pl.pallas_call(kernel, out_shape=outs, in_specs=sspec(scalars) + vspec(le...  23.6 us
    ppermute x8, starting transfers between devices, along(): return lax.ppermute(x, ('samples', 'chan'), whole)  22.2 us
    ppermute x2, waiting for transfers between devices, halves_of_sum(): parts = [x, lax.ppermute(x, axis, [(i, i ^ step) for i in range(size)])]  5.42 us
    ppermute x1, starting transfers between devices, on_device(): feat_end = lax.ppermute(feat, 'chan', [(0, 1), (size - 1, size - 2)])  5.29 us
    ppermute x1, waiting for transfers between devices, on_device(): from_end = lax.ppermute(grad_end, 'chan', [(1, size - 1), (size - 2, 0)])  4.71 us
    unnamed x19, local copies, waits for them, and re-layouts  3.13 us
    ppermute x2, starting transfers between devices, from_sides(): got = lax.ppermute(edge, axis, [(0, 1), (1, 0)])  2.82 us
    ppermute x1, starting transfers between devices, on_device(): lax.ppermute(mods[size], 'chan', [(0, size - 1), (size - 1, 0)])  2.81 us
  transfers between devices with their start and end apart: 21, of which 8 were waited for; matrix products, arithmetic and copies ran while one was open for 3% of the time, Pallas kernels for 26%

profile of v15, /device:TPU:0, one launch (start us, length us, event | category | flops | bytes accessed | tf_op | source)
XLA Modules:
  0.0 87.7 jit_solution(17209115550377070407)
XLA Ops:
  0.6 0.0 copy-start.7
  0.6 0.0 copy-start
  0.7 1.3 %copy.13 = bf16[8,8,8,512]{3,1,2,0:T(8,128)(2,1)S(1)} copy(bf16[8,8,8,512]{3,2,1,0:T(8,128)(2,1)} %bitcast.32) | data formatting | bytes 1048576
  2.0 5.7 %collective-permute-start.1 = (bf16[64,4096]{1,0:T(8,128)(2,1)S(1)}, bf16[64,4096]{1,0:T(8,128)(2,1)}, u32[]{:S(2)}, u32[]{:S(2)}) collective-permute-start(bf16[64,4096]{1,0:T(8,128)(2,1)S(1)} %bitcast.26), channel_id=1, source_target_pairs={{0,1},{1,2},{2,3},{7,6},{6,5},{5,4},{8,9},{9,10},{10,11},{15,14},{... | collective-permute-start | bytes 1572872 | tf_op jit(solution)/shard_map/ppermute | solution.py:404
  7.8 1.3 %collective-permute-start.2 = (bf16[64,4096]{1,0:T(8,128)(2,1)S(1)}, bf16[64,4096]{1,0:T(8,128)(2,1)}, u32[]{:S(2)}, u32[]{:S(2)}) collective-permute-start(bf16[64,4096]{1,0:T(8,128)(2,1)S(1)} %bitcast.27), channel_id=1, source_target_pairs={{1,0},{2,1},{3,2},{6,7},{5,6},{4,5},{9,8},{10,9},{11,10},{14,15},{... | collective-permute-start | bytes 1572872 | tf_op jit(solution)/shard_map/ppermute | solution.py:404
  9.1 0.2 copy.14
  9.3 1.6 %collective-permute-start.5 = (bf16[64,512]{1,0:T(8,128)(2,1)S(1)}, bf16[64,512]{1,0:T(8,128)(2,1)S(1)}, u32[]{:S(2)}, u32[]{:S(2)}) collective-permute-start(bf16[64,512]{1,0:T(8,128)(2,1)S(1)} %slice_select_fusion), channel_id=1, source_target_pairs={{0,16},{16,0},{1,17},{17,1},{2,18},{18,2},{3,19},{19,3},{4,20},{20... | collective-permute-start | bytes 196616 | tf_op jit(solution)/shard_map/ppermute | solution.py:379
  10.9 1.0 %plain.1 = (f32[10,64,128]{2,1,0:T(8,128)S(1)}, f32[8,128]{1,0:T(8,128)S(1)}) custom-call(s32[1,4]{1,0:T(1,128)S(1)} %copy-done.5, f32[1,512]{1,0:T(1,128)S(1)} %copy-done.4, f32[1,128]{1,0:T(1,128)S(1)} %bitcast.30, f32[512,128]{1,0:T(8,128)S(1)} %copy-done.3, f32[4,9,64,128]{3,2,1,0:T(8,128)S(1)} %copy-done), custom_call_target="tpu_custom_call" | custom-call | flops 1000000 | bytes 1776144 | tf_op jit(solution)/shard_map/plain/pallas_call | solution.py:327
  11.8 0.0 copy-start.1
  11.8 0.6 collective-permute-start
  12.4 1.2 %collective-permute-done.5 = bf16[64,512]{1,0:T(8,128)(2,1)S(1)} collective-permute-done((bf16[64,512]{1,0:T(8,128)(2,1)S(1)}, bf16[64,512]{1,0:T(8,128)(2,1)S(1)}, u32[]{:S(2)}, u32[]{:S(2)}) %collective-permute-start.5) | collective-permute-done | bytes 65568 | tf_op jit(solution)/shard_map/ppermute | solution.py:379
  13.7 5.3 %collective-permute-start.6 = (bf16[64,5120]{1,0:T(8,128)(2,1)S(1)}, bf16[64,5120]{1,0:T(8,128)(2,1)S(1)}, u32[]{:S(2)}, u32[]{:S(2)}) collective-permute-start(bf16[64,5120]{1,0:T(8,128)(2,1)S(1)} %feat_rows.1.refs_3_), channel_id=1, source_target_pairs={{0,1},{3,2},{4,5},{7,6},{8,9},{11,10},{12,13},{15,14},{16,17},{19,... | collective-permute-start | bytes 1966088 | tf_op jit(solution)/shard_map/ppermute | solution.py:444
  19.0 2.7 %collective-permute-done.refs_1_ = f32[10,64,128]{2,1,0:T(8,128)} collective-permute-done((f32[10,64,128]{2,1,0:T(8,128)S(1)}, f32[10,64,128]{2,1,0:T(8,128)}, u32[]{:S(2)}, u32[]{:S(2)}) %collective-permute-start) | collective-permute-done | bytes 327712 | tf_op jit(solution)/shard_map/ppermute | solution.py:359
  21.7 0.0 collective-permute-done.1.refs_1_.first
  21.7 0.0 collective-permute-done.2.refs_2_.second
  21.7 0.7 collective-permute-start.3
  22.4 1.3 %collective-permute-start.4 = (bf16[64,4096]{1,0:T(8,128)(2,1)}, bf16[64,4096]{1,0:T(8,128)(2,1)}, u32[]{:S(2)}, u32[]{:S(2)}) collective-permute-start(bf16[64,4096]{1,0:T(8,128)(2,1)} %collective-permute-done.2.refs_2_.second), channel_id=1, source_target_pairs={{1,0},{2,1},{6,7},{5,6},{9,8},{10,9},{14,15},{13,14},{17,16},{18,1... | collective-permute-start | bytes 1572872 | tf_op jit(solution)/shard_map/ppermute | solution.py:404
  23.7 0.1 pad_add_fusion.place
  23.8 1.0 %copy-done.2 = f32[10,64,128]{2,1,0:T(8,128)S(1)} copy-done((f32[10,64,128]{2,1,0:T(8,128)S(1)}, f32[10,64,128]{2,1,0:T(8,128)}, u32[]{:S(2)}) %copy-start.2) | copy-done | bytes 327704
  24.8 1.3 %mod_blocks.1 = (bf16[9,64,256]{2,1,0:T(8,128)(2,1)S(1)}, f32[64,128]{1,0:T(8,128)S(1)}, bf16[64,576]{1,0:T(8,128)(2,1)S(1)}, bf16[64,576]{1,0:T(8,128)(2,1)S(1)...) custom-call(s32[4]{0:T(128)S(1)} %pad_add_fusion.place, ...), custom_call_target="tpu_custom_call" | custom-call | flops 1000000 | bytes 1351696 | tf_op jit(solution)/shard_map/mod_blocks/pallas_call | solution.py:327
  26.0 4.5 %near_grad.1 = (bf16[64,576]{1,0:T(8,128)(2,1)S(1)}, bf16[128,576]{1,0:T(8,128)(2,1)S(1)}, bf16[128,576]{1,0:T(8,128)(2,1)S(1)}, bf16[192,5120]{1,0:T(8,128)(2,1)S(1)}) custom-call(bf16[64,4096]{1,0:T(8,128)(2,1)S(1)} %bitcast.28, bf16[64,4096]{1,0:T(8,128)(2,1)} %collective-permute-done.1.refs_1_.first, ...), custom_call_target="tpu_custom_call" | custom-call | flops 905969664 | bytes 4710400 | tf_op jit(solution)/shard_map/near_grad/pallas_call | solution.py:327
  30.6 1.3 %collective-permute-start.7 = (bf16[128,576]{1,0:T(8,128)(2,1)S(1)}, bf16[128,576]{1,0:T(8,128)(2,1)S(1)}, u32[]{:S(2)}, u32[]{:S(2)}) collective-permute-start(bf16[128,576]{1,0:T(8,128)(2,1)S(1)} %get-tuple-element.71), channel_id=1, source_target_pairs={{1,0},{2,1},{3,2},{6,7},{5,6},{4,5},{9,8},{10,9},{11,10},{14,15},{... | collective-permute-start | bytes 442376 | tf_op jit(solution)/shard_map/ppermute | solution.py:404
  31.9 7.6 %collective-permute-start.8 = (bf16[128,576]{1,0:T(8,128)(2,1)S(1)}, bf16[128,576]{1,0:T(8,128)(2,1)S(1)}, u32[]{:S(2)}, u32[]{:S(2)}) collective-permute-start(bf16[128,576]{1,0:T(8,128)(2,1)S(1)} %get-tuple-element.72), channel_id=1, source_target_pairs={{0,1},{1,2},{2,3},{7,6},{6,5},{5,4},{8,9},{9,10},{10,11},{15,14},{... | collective-permute-start | bytes 442376 | tf_op jit(solution)/shard_map/ppermute | solution.py:404
  39.4 0.0 collective-permute-done.6.feat
  39.5 0.0 collective-permute-done.3.refs_0_
  39.5 0.0 collective-permute-done.4.refs_1_
  39.5 3.7 %middle_grad.1 = (bf16[64,576]{1,0:T(8,128)(2,1)S(1)}, bf16[64,4096]{1,0:T(8,128)(2,1)S(1)}, bf16[64,4096]{1,0:T(8,128)(2,1)S(1)}) custom-call(bf16[64,4096]{1,0:T(8,128)(2,1)S(1)} %collective-permute-done.3.refs_0_, bf16[64,4096]{1,0:T(8,128)(2,1)} %collective-permute-done.4.refs_1_, bf16[192,5120]{1,0:T(8,128)(2,1)S(1)} %get-tuple-element.75.refs_2_), custom_call_target="tpu_custom_call" | custom-call | flops 301989888 | bytes 4136960 | tf_op jit(solution)/shard_map/middle_grad/pallas_call | solution.py:327
  43.2 4.3 %collective-permute-start.9 = (bf16[64,576]{1,0:T(8,128)(2,1)S(1)}, bf16[64,576]{1,0:T(8,128)(2,1)S(1)}, u32[]{:S(2)}, u32[]{:S(2)}) collective-permute-start(bf16[64,576]{1,0:T(8,128)(2,1)S(1)} %get-tuple-element.76), channel_id=1, source_target_pairs={{0,2},{1,3},{2,0},{3,1},{7,5},{6,4},{5,7},{4,6},{8,10},{9,11},{10,... | collective-permute-start | bytes 221192 | tf_op jit(solution)/shard_map/ppermute | solution.py:404
  47.5 3.0 %end_grad.1 = bf16[64,576]{1,0:T(8,128)(2,1)S(1)} custom-call(bf16[64,4096]{1,0:T(8,128)(2,1)S(1)} %get-tuple-element.89.end_block, bf16[64,5120]{1,0:T(8,128)(2,1)S(1)} %collective-permute-done.6.feat), custom_call_target="tpu_custom_call" | custom-call | flops 301989888 | bytes 1253376 | tf_op jit(solution)/shard_map/end_grad/pallas_call | solution.py:327
  50.6 1.3 %collective-permute-start.10 = (bf16[64,576]{1,0:T(8,128)(2,1)S(1)}, bf16[64,576]{1,0:T(8,128)(2,1)S(1)}, u32[]{:S(2)}, u32[]{:S(2)}) collective-permute-start(bf16[64,576]{1,0:T(8,128)(2,1)S(1)} %end_grad.1), channel_id=1, source_target_pairs={{1,3},{2,0},{5,7},{6,4},{9,11},{10,8},{13,15},{14,12},{17,19},{18,... | collective-permute-start | bytes 221192 | tf_op jit(solution)/shard_map/ppermute | solution.py:499
  51.9 1.3 %collective-permute-start.17 = (bf16[64,4096]{1,0:T(8,128)(2,1)S(1)}, bf16[64,4096]{1,0:T(8,128)(2,1)S(1)}, u32[]{:S(2)}, u32[]{:S(2)}) collective-permute-start(bf16[64,4096]{1,0:T(8,128)(2,1)S(1)} %get-tuple-element.89.end_block), channel_id=1, source_target_pairs={{1,0},{2,3},{5,4},{6,7},{9,8},{10,11},{13,12},{14,15},{17,16},{18,... | collective-permute-start | bytes 1572872 | tf_op jit(solution)/shard_map/ppermute | solution.py:501
  53.2 0.0 collective-permute-done.7.ahead
  53.2 0.0 collective-permute-done.8.behind
  53.2 0.0 collective-permute-done.9.others
  53.2 4.7 %collective-permute-done.10.end = bf16[64,576]{1,0:T(8,128)(2,1)S(1)} collective-permute-done((bf16[64,576]{1,0:T(8,128)(2,1)S(1)}, bf16[64,576]{1,0:T(8,128)(2,1)S(1)}, u32[]{:S(2)}, u32[]{:S(2)}) %collective-permute-start.10) | collective-permute-done | bytes 73760 | tf_op jit(solution)/shard_map/ppermute | solution.py:499
  57.9 1.1 %collect.1 = (bf16[10,64,128]{2,1,0:T(8,128)(2,1)S(1)}, bf16[10,64,128]{2,1,0:T(8,128)(2,1)S(1)}) custom-call(s32[4]{0:T(128)S(1)} %pad_add_fusion.place, f32[64,128]{1,0:T(8,128)S(1)} %get-tuple-element.58.scale, bf16[9,64,256]{2,1,0:T(8,128)(2,1)S(1)} %get-tuple-element.69.whole_mod, bf16[64,576]{1,0:T(8,128)(2,1)S(1)} %get-tuple-element.70.own, ...), custom_call_target="tpu_custom_call" | custom-call | flops 6000000000 | bytes 1171472 | tf_op jit(solution)/shard_map/collect/pallas_call | solution.py:327
  59.0 0.9 %collective-permute-start.11 = (bf16[10,64,128]{2,1,0:T(8,128)(2,1)S(1)}, bf16[10,64,128]{2,1,0:T(8,128)(2,1)S(1)}, u32[]{:S(2)}, u32[]{:S(2)}) collective-permute-start(bf16[10,64,128]{2,1,0:T(8,128)(2,1)S(1)} %get-tuple-element.85), channel_id=1, source_target_pairs={{0,16},{16,0},{1,17},{17,1},{2,18},{18,2},{3,19},{19,3},{4,20},{20... | collective-permute-start | bytes 491528 | tf_op jit(solution)/shard_map/ppermute | solution.py:522
  59.9 0.0 collective-permute-start.15
  59.9 2.8 %collective-permute-start.16 = (bf16[64,576]{1,0:T(8,128)(2,1)S(1)}, bf16[64,576]{1,0:T(8,128)(2,1)S(1)}, u32[]{:S(2)}, u32[]{:S(2)}) collective-permute-start(bf16[64,576]{1,0:T(8,128)(2,1)S(1)} %get-tuple-element.88), channel_id=1, source_target_pairs={{0,3},{3,0},{4,7},{7,4},{8,11},{11,8},{12,15},{15,12},{16,19},{19,... | collective-permute-start | bytes 221192 | tf_op jit(solution)/shard_map/ppermute | solution.py:520
  62.7 1.7 %collective-permute-done.11.refs_1_ = bf16[10,64,128]{2,1,0:T(8,128)(2,1)S(1)} collective-permute-done((bf16[10,64,128]{2,1,0:T(8,128)(2,1)S(1)}, bf16[10,64,128]{2,1,0:T(8,128)(2,1)S(1)}, u32[]{:S(2)}, u32[]{:S(2)}) %collective-permute-start.11) | collective-permute-done | bytes 163872 | tf_op jit(solution)/shard_map/ppermute | solution.py:522
  64.3 0.2 row_sum.1.refs_0_
  64.6 1.6 %collective-permute-start.12 = (bf16[11,64,128]{2,1,0:T(8,128)(2,1)S(1)}, bf16[11,64,128]{2,1,0:T(8,128)(2,1)S(1)}, u32[]{:S(2)}, u32[]{:S(2)}) collective-permute-start(bf16[11,64,128]{2,1,0:T(8,128)(2,1)S(1)} %row_sum.1.refs_0_), channel_id=1, source_target_pairs={{8,0},{12,4},{0,8},{4,12},{9,1},{13,5},{1,9},{5,13},{10,2},{14,6},... | collective-permute-start | bytes 540680 | tf_op jit(solution)/shard_map/ppermute | solution.py:352
  66.1 0.0 collective-permute-start.13
  66.1 0.0 collective-permute-done.15.refs_0_
  66.1 0.6 collective-permute-start.14
  66.8 1.3 %collective-permute-done.16.refs_1_ = bf16[64,576]{1,0:T(8,128)(2,1)S(1)} collective-permute-done((bf16[64,576]{1,0:T(8,128)(2,1)S(1)}, bf16[64,576]{1,0:T(8,128)(2,1)S(1)}, u32[]{:S(2)}, u32[]{:S(2)}) %collective-permute-start.16) | collective-permute-done | bytes 73760 | tf_op jit(solution)/shard_map/ppermute | solution.py:520
  68.1 1.3 %collective-permute-done.17.far = bf16[64,4096]{1,0:T(8,128)(2,1)S(1)} collective-permute-done((bf16[64,4096]{1,0:T(8,128)(2,1)S(1)}, bf16[64,4096]{1,0:T(8,128)(2,1)S(1)}, u32[]{:S(2)}, u32[]{:S(2)}) %collective-permute-start.17) | collective-permute-done | bytes 524320 | tf_op jit(solution)/shard_map/ppermute | solution.py:501
  69.4 5.2 %input_grad.1 = (f32[64,4096]{1,0:T(8,128)S(1)}, f32[64,512]{1,0:T(8,128)}, f32[64,512]{1,0:T(8,128)S(1)}) custom-call(s32[4]{0:T(128)S(1)} %pad_add_fusion.place, bf16[64,4096]{1,0:T(8,128)(2,1)S(1)} %bitcast.29, bf16[64,4096]{1,0:T(8,128)(2,1)} %collective-permute-done.1.refs_1_.first, bf16[64,4096]{1,0:T(8,128)(2,1)} %collective-permute-done.2.refs_2_.second, ...), custom_call_target="tpu_custom_call" | custom-call | flops 2000000000 | bytes 4448272 | tf_op jit(solution)/shard_map/input_grad/pallas_call | solution.py:327
  74.6 0.0 collective-permute-done.12.refs_1_
  74.6 0.0 collective-permute-done.13.refs_2_
  74.6 0.0 collective-permute-done.14.refs_3_
  74.6 1.3 %collective-permute-start.20 = (f32[64,512]{1,0:T(8,128)S(1)}, f32[64,512]{1,0:T(8,128)S(1)}, u32[]{:S(2)}, u32[]{:S(2)}) collective-permute-start(f32[64,512]{1,0:T(8,128)S(1)} %get-tuple-element.102), channel_id=1, source_target_pairs={{0,16},{16,0},{1,17},{17,1},{2,18},{18,2},{3,19},{19,3},{4,20},{20... | collective-permute-start | bytes 393224 | tf_op jit(solution)/shard_map/ppermute | solution.py:379
  75.9 2.7 %bank_grad.1 = (f32[4,9,64,128]{3,2,1,0:T(8,128)}, f32[4,128]{1,0:T(4,128)S(1)}, f32[4,512]{1,0:T(4,128)S(1)}) custom-call(s32[4]{0:T(128)S(1)} %pad_add_fusion.place, f32[4,9,64,128]{3,2,1,0:T(8,128)S(1)} %copy-done, bf16[11,64,128]{2,1,0:T(8,128)(2,1)S(1)} %row_sum.1.refs_0_, bf16[11,64,128]{2,1,0:T(8,128)(2,1)S(1)} %collective-permute-done.12.refs_1_, ...), custom_call_target="tpu_custom_call" | custom-call | flops 1000000 | bytes 3090448 | tf_op jit(solution)/shard_map/bank_grad/pallas_call | solution.py:327
  78.6 0.1 collective-permute-start.18
  78.7 0.1 pad.1.clone
  78.8 0.6 copy.15
  79.4 2.9 %collective-permute-done.18 = f32[4,128]{1,0:T(4,128)S(1)} collective-permute-done((f32[4,128]{1,0:T(4,128)S(1)}, f32[4,128]{1,0:T(4,128)S(1)}, u32[]{:S(2)}, u32[]{:S(2)}) %collective-permute-start.18) | collective-permute-done | bytes 2080 | tf_op jit(solution)/shard_map/ppermute | solution.py:370
  82.2 0.5 collective-permute-start.19
  82.8 0.0 collective-permute-done.20
  82.8 0.1 copy.12
  82.9 0.1 copy.11
  83.1 1.1 %fusion = bf16[1,64,8,512]{3,2,1,0:T(8,128)(2,1)} fusion(f32[1,64,1,512]{3,2,1,0:T(1,128)S(1)} %copy.12, f32[1,64,1,512]{3,2,1,0:T(1,128)S(1)} %copy.11, f32[8]{0:T(128)S(1)} %pad.1.clone, f32[1,64,8,512]{3,2,1,0:T(8,128)S(1)} %bitcast.31), kind=kLoop, calls=%fused_computation.1 | loop fusion | flops 1048576 | bytes 1835040 | tf_op jit(solution)/shard_map/convert_element_type | solution.py:569
  84.2 2.5 %collective-permute-done.19.refs_1_ = f32[4,128]{1,0:T(4,128)S(1)} collective-permute-done((f32[4,128]{1,0:T(4,128)S(1)}, f32[4,128]{1,0:T(4,128)S(1)}, u32[]{:S(2)}, u32[]{:S(2)}) %collective-permute-start.19) | collective-permute-done | bytes 2080 | tf_op jit(solution)/shard_map/ppermute | solution.py:370
  86.7 0.9 %affine.1 = (f32[512,128]{1,0:T(8,128)}, f32[1,128]{1,0:T(1,128)}) custom-call(f32[4,512]{1,0:T(4,128)S(1)} %get-tuple-element.105.latents, f32[4,128]{1,0:T(4,128)S(1)} %add.18.refs_0_, f32[4,128]{1,0:T(4,128)S(1)} %collective-permute-done.19.refs_1_), custom_call_target="tpu_custom_call" | custom-call | flops 1000000 | bytes 274944 | tf_op jit(solution)/shard_map/affine/pallas_call | solution.py:327
  (18 shorter events, 0.1 us)
Async XLA Ops:
  0.6 8.4 %copy-start.7 = (bf16[1,64,8,512]{3,2,1,0:T(8,128)(2,1)S(1)}, bf16[1,64,8,512]{3,2,1,0:T(8,128)(2,1)}, u32[]{:S(2)}) copy-start(bf16[1,64,8,512]{3,2,1,0:T(8,128)(2,1)} %param.7) | copy-start | bytes 1572868
  0.6 10.2 %copy-start = (f32[4,9,64,128]{3,2,1,0:T(8,128)S(1)}, f32[4,9,64,128]{3,2,1,0:T(8,128)}, u32[]{:S(2)}) copy-start(f32[4,9,64,128]{3,2,1,0:T(8,128)} %bank.1) | copy-start | bytes 3538948
  0.7 10.2 %copy-start.5 = (s32[1,4]{1,0:T(1,128)S(1)}, s32[1,4]{1,0:T(1,128)}, u32[]{:S(2)}) copy-start(s32[1,4]{1,0:T(1,128)} %refs_0_.1) | copy-start | bytes 52
  0.7 10.2 %copy-start.4 = (f32[1,512]{1,0:T(1,128)S(1)}, f32[1,512]{1,0:T(1,128)}, u32[]{:S(2)}) copy-start(f32[1,512]{1,0:T(1,128)} %refs_1_.1) | copy-start | bytes 6148
  0.7 10.2 %copy-start.6 = (f32[128]{0:T(128)S(1)}, f32[128]{0:T(128)}, u32[]{:S(2)}) copy-start(f32[128]{0:T(128)} %param.13) | copy-start | bytes 1540
  0.7 10.2 %copy-start.3 = (f32[512,128]{1,0:T(8,128)S(1)}, f32[512,128]{1,0:T(8,128)}, u32[]{:S(2)}) copy-start(f32[512,128]{1,0:T(8,128)} %refs_3_.1) | copy-start | bytes 786436
  2.0 19.7 %collective-permute-start.1 = (bf16[64,4096]{1,0:T(8,128)(2,1)S(1)}, bf16[64,4096]{1,0:T(8,128)(2,1)}, u32[]{:S(2)}, u32[]{:S(2)}) collective-permute-start(bf16[64,4096]{1,0:T(8,128)(2,1)S(1)} %bitcast.26), channel_id=1, source_target_pairs={{0,1},{1,2},{2,3},{7,6},{6,5},{5,4},{8,9},{9,10},{10,11},{15,14},{... | collective-permute-start | bytes 1572872 | tf_op jit(solution)/shard_map/ppermute | solution.py:404
  7.8 13.9 %collective-permute-start.2 = (bf16[64,4096]{1,0:T(8,128)(2,1)S(1)}, bf16[64,4096]{1,0:T(8,128)(2,1)}, u32[]{:S(2)}, u32[]{:S(2)}) collective-permute-start(bf16[64,4096]{1,0:T(8,128)(2,1)S(1)} %bitcast.27), channel_id=1, source_target_pairs={{1,0},{2,1},{3,2},{6,7},{5,6},{4,5},{9,8},{10,9},{11,10},{14,15},{... | collective-permute-start | bytes 1572872 | tf_op jit(solution)/shard_map/ppermute | solution.py:404
  9.3 4.3 %collective-permute-start.5 = (bf16[64,512]{1,0:T(8,128)(2,1)S(1)}, bf16[64,512]{1,0:T(8,128)(2,1)S(1)}, u32[]{:S(2)}, u32[]{:S(2)}) collective-permute-start(bf16[64,512]{1,0:T(8,128)(2,1)S(1)} %slice_select_fusion), channel_id=1, source_target_pairs={{0,16},{16,0},{1,17},{17,1},{2,18},{18,2},{3,19},{19,3},{4,20},{20... | collective-permute-start | bytes 196616 | tf_op jit(solution)/shard_map/ppermute | solution.py:379
  11.8 9.9 %copy-start.1 = (f32[10,64,128]{2,1,0:T(8,128)}, f32[10,64,128]{2,1,0:T(8,128)S(1)}, u32[]{:S(2)}) copy-start(f32[10,64,128]{2,1,0:T(8,128)S(1)} %get-tuple-element.57.refs_0_) | copy-start | bytes 983044
  11.8 9.8 %collective-permute-start = (f32[10,64,128]{2,1,0:T(8,128)S(1)}, f32[10,64,128]{2,1,0:T(8,128)}, u32[]{:S(2)}, u32[]{:S(2)}) collective-permute-start(f32[10,64,128]{2,1,0:T(8,128)S(1)} %get-tuple-element.57.refs_0_), channel_id=1, source_target_pairs={{0,16},{16,0},{1,17},{17,1},{2,18},{18,2},{3,19},{19,3},{4,20},{20... | collective-permute-start | bytes 983048 | tf_op jit(solution)/shard_map/ppermute | solution.py:359
  13.7 25.8 %collective-permute-start.6 = (bf16[64,5120]{1,0:T(8,128)(2,1)S(1)}, bf16[64,5120]{1,0:T(8,128)(2,1)S(1)}, u32[]{:S(2)}, u32[]{:S(2)}) collective-permute-start(bf16[64,5120]{1,0:T(8,128)(2,1)S(1)} %feat_rows.1.refs_3_), channel_id=1, source_target_pairs={{0,1},{3,2},{4,5},{7,6},{8,9},{11,10},{12,13},{15,14},{16,17},{19,... | collective-permute-start | bytes 1966088 | tf_op jit(solution)/shard_map/ppermute | solution.py:444
  21.7 17.8 %collective-permute-start.3 = (bf16[64,4096]{1,0:T(8,128)(2,1)}, bf16[64,4096]{1,0:T(8,128)(2,1)S(1)}, u32[]{:S(2)}, u32[]{:S(2)}) collective-permute-start(bf16[64,4096]{1,0:T(8,128)(2,1)} %collective-permute-done.1.refs_1_.first), channel_id=1, source_target_pairs={{1,2},{2,3},{6,5},{5,4},{9,10},{10,11},{14,13},{13,12},{17,18},{18... | collective-permute-start | bytes 1572872 | tf_op jit(solution)/shard_map/ppermute | solution.py:404
  22.4 17.1 %collective-permute-start.4 = (bf16[64,4096]{1,0:T(8,128)(2,1)}, bf16[64,4096]{1,0:T(8,128)(2,1)}, u32[]{:S(2)}, u32[]{:S(2)}) collective-permute-start(bf16[64,4096]{1,0:T(8,128)(2,1)} %collective-permute-done.2.refs_2_.second), channel_id=1, source_target_pairs={{1,0},{2,1},{6,7},{5,6},{9,8},{10,9},{14,15},{13,14},{17,16},{18,1... | collective-permute-start | bytes 1572872 | tf_op jit(solution)/shard_map/ppermute | solution.py:404
  23.8 1.0 %copy-start.2 = (f32[10,64,128]{2,1,0:T(8,128)S(1)}, f32[10,64,128]{2,1,0:T(8,128)}, u32[]{:S(2)}) copy-start(f32[10,64,128]{2,1,0:T(8,128)} %copy-done.1) | copy-start | bytes 983044
  30.6 22.6 %collective-permute-start.7 = (bf16[128,576]{1,0:T(8,128)(2,1)S(1)}, bf16[128,576]{1,0:T(8,128)(2,1)S(1)}, u32[]{:S(2)}, u32[]{:S(2)}) collective-permute-start(bf16[128,576]{1,0:T(8,128)(2,1)S(1)} %get-tuple-element.71), channel_id=1, source_target_pairs={{1,0},{2,1},{3,2},{6,7},{5,6},{4,5},{9,8},{10,9},{11,10},{14,15},{... | collective-permute-start | bytes 442376 | tf_op jit(solution)/shard_map/ppermute | solution.py:404
  31.9 21.3 %collective-permute-start.8 = (bf16[128,576]{1,0:T(8,128)(2,1)S(1)}, bf16[128,576]{1,0:T(8,128)(2,1)S(1)}, u32[]{:S(2)}, u32[]{:S(2)}) collective-permute-start(bf16[128,576]{1,0:T(8,128)(2,1)S(1)} %get-tuple-element.72), channel_id=1, source_target_pairs={{0,1},{1,2},{2,3},{7,6},{6,5},{5,4},{8,9},{9,10},{10,11},{15,14},{... | collective-permute-start | bytes 442376 | tf_op jit(solution)/shard_map/ppermute | solution.py:404
  43.2 10.0 %collective-permute-start.9 = (bf16[64,576]{1,0:T(8,128)(2,1)S(1)}, bf16[64,576]{1,0:T(8,128)(2,1)S(1)}, u32[]{:S(2)}, u32[]{:S(2)}) collective-permute-start(bf16[64,576]{1,0:T(8,128)(2,1)S(1)} %get-tuple-element.76), channel_id=1, source_target_pairs={{0,2},{1,3},{2,0},{3,1},{7,5},{6,4},{5,7},{4,6},{8,10},{9,11},{10,... | collective-permute-start | bytes 221192 | tf_op jit(solution)/shard_map/ppermute | solution.py:404
  50.6 7.3 %collective-permute-start.10 = (bf16[64,576]{1,0:T(8,128)(2,1)S(1)}, bf16[64,576]{1,0:T(8,128)(2,1)S(1)}, u32[]{:S(2)}, u32[]{:S(2)}) collective-permute-start(bf16[64,576]{1,0:T(8,128)(2,1)S(1)} %end_grad.1), channel_id=1, source_target_pairs={{1,3},{2,0},{5,7},{6,4},{9,11},{10,8},{13,15},{14,12},{17,19},{18,... | collective-permute-start | bytes 221192 | tf_op jit(solution)/shard_map/ppermute | solution.py:499
  51.9 17.6 %collective-permute-start.17 = (bf16[64,4096]{1,0:T(8,128)(2,1)S(1)}, bf16[64,4096]{1,0:T(8,128)(2,1)S(1)}, u32[]{:S(2)}, u32[]{:S(2)}) collective-permute-start(bf16[64,4096]{1,0:T(8,128)(2,1)S(1)} %get-tuple-element.89.end_block), channel_id=1, source_target_pairs={{1,0},{2,3},{5,4},{6,7},{9,8},{10,11},{13,12},{14,15},{17,16},{18,... | collective-permute-start | bytes 1572872 | tf_op jit(solution)/shard_map/ppermute | solution.py:501
  59.0 5.4 %collective-permute-start.11 = (bf16[10,64,128]{2,1,0:T(8,128)(2,1)S(1)}, bf16[10,64,128]{2,1,0:T(8,128)(2,1)S(1)}, u32[]{:S(2)}, u32[]{:S(2)}) collective-permute-start(bf16[10,64,128]{2,1,0:T(8,128)(2,1)S(1)} %get-tuple-element.85), channel_id=1, source_target_pairs={{0,16},{16,0},{1,17},{17,1},{2,18},{18,2},{3,19},{19,3},{4,20},{20... | collective-permute-start | bytes 491528 | tf_op jit(solution)/shard_map/ppermute | solution.py:522
  59.9 6.3 %collective-permute-start.15 = (bf16[64,576]{1,0:T(8,128)(2,1)S(1)}, bf16[64,576]{1,0:T(8,128)(2,1)S(1)}, u32[]{:S(2)}, u32[]{:S(2)}) collective-permute-start(bf16[64,576]{1,0:T(8,128)(2,1)S(1)} %get-tuple-element.87), channel_id=1, source_target_pairs={{0,2},{1,3},{2,0},{3,1},{7,5},{6,4},{5,7},{4,6},{8,10},{9,11},{10,... | collective-permute-start | bytes 221192 | tf_op jit(solution)/shard_map/ppermute | solution.py:404
  59.9 8.2 %collective-permute-start.16 = (bf16[64,576]{1,0:T(8,128)(2,1)S(1)}, bf16[64,576]{1,0:T(8,128)(2,1)S(1)}, u32[]{:S(2)}, u32[]{:S(2)}) collective-permute-start(bf16[64,576]{1,0:T(8,128)(2,1)S(1)} %get-tuple-element.88), channel_id=1, source_target_pairs={{0,3},{3,0},{4,7},{7,4},{8,11},{11,8},{12,15},{15,12},{16,19},{19,... | collective-permute-start | bytes 221192 | tf_op jit(solution)/shard_map/ppermute | solution.py:520
  64.6 10.1 %collective-permute-start.12 = (bf16[11,64,128]{2,1,0:T(8,128)(2,1)S(1)}, bf16[11,64,128]{2,1,0:T(8,128)(2,1)S(1)}, u32[]{:S(2)}, u32[]{:S(2)}) collective-permute-start(bf16[11,64,128]{2,1,0:T(8,128)(2,1)S(1)} %row_sum.1.refs_0_), channel_id=1, source_target_pairs={{8,0},{12,4},{0,8},{4,12},{9,1},{13,5},{1,9},{5,13},{10,2},{14,6},... | collective-permute-start | bytes 540680 | tf_op jit(solution)/shard_map/ppermute | solution.py:352
  66.1 8.5 %collective-permute-start.13 = (bf16[11,64,128]{2,1,0:T(8,128)(2,1)S(1)}, bf16[11,64,128]{2,1,0:T(8,128)(2,1)S(1)}, u32[]{:S(2)}, u32[]{:S(2)}) collective-permute-start(bf16[11,64,128]{2,1,0:T(8,128)(2,1)S(1)} %row_sum.1.refs_0_), channel_id=1, source_target_pairs={{12,0},{8,4},{4,8},{0,12},{13,1},{9,5},{5,9},{1,13},{14,2},{10,6},... | collective-permute-start | bytes 540680 | tf_op jit(solution)/shard_map/ppermute | solution.py:352
  66.1 8.5 %collective-permute-start.14 = (bf16[11,64,128]{2,1,0:T(8,128)(2,1)S(1)}, bf16[11,64,128]{2,1,0:T(8,128)(2,1)S(1)}, u32[]{:S(2)}, u32[]{:S(2)}) collective-permute-start(bf16[11,64,128]{2,1,0:T(8,128)(2,1)S(1)} %row_sum.1.refs_0_), channel_id=1, source_target_pairs={{4,0},{0,4},{12,8},{8,12},{5,1},{1,5},{13,9},{9,13},{6,2},{2,6},{1... | collective-permute-start | bytes 540680 | tf_op jit(solution)/shard_map/ppermute | solution.py:352
  74.6 8.1 %collective-permute-start.20 = (f32[64,512]{1,0:T(8,128)S(1)}, f32[64,512]{1,0:T(8,128)S(1)}, u32[]{:S(2)}, u32[]{:S(2)}) collective-permute-start(f32[64,512]{1,0:T(8,128)S(1)} %get-tuple-element.102), channel_id=1, source_target_pairs={{0,16},{16,0},{1,17},{17,1},{2,18},{18,2},{3,19},{19,3},{4,20},{20... | collective-permute-start | bytes 393224 | tf_op jit(solution)/shard_map/ppermute | solution.py:379
  78.6 3.7 %collective-permute-start.18 = (f32[4,128]{1,0:T(4,128)S(1)}, f32[4,128]{1,0:T(4,128)S(1)}, u32[]{:S(2)}, u32[]{:S(2)}) collective-permute-start(f32[4,128]{1,0:T(4,128)S(1)} %get-tuple-element.100), channel_id=1, source_target_pairs={{0,1},{1,0},{2,3},{3,2},{4,5},{5,4},{6,7},{7,6},{8,9},{9,8},{10,11... | collective-permute-start | bytes 6152 | tf_op jit(solution)/shard_map/ppermute | solution.py:370
  82.2 4.5 %collective-permute-start.19 = (f32[4,128]{1,0:T(4,128)S(1)}, f32[4,128]{1,0:T(4,128)S(1)}, u32[]{:S(2)}, u32[]{:S(2)}) collective-permute-start(f32[4,128]{1,0:T(4,128)S(1)} %add.18.refs_0_), channel_id=1, source_target_pairs={{0,2},{1,3},{2,0},{3,1},{4,6},{5,7},{6,4},{7,5},{8,10},{9,11},{10,... | collective-permute-start | bytes 6152 | tf_op jit(solution)/shard_map/ppermute | solution.py:370

commit v16 on v15

--- a/solution.py
+++ b/solution.py
@@ -150,13 +150,15 @@
 
 
 def middle_grad_kernel(count, height, width, *refs):
-    first, second, wide = refs[:count], refs[count : 2 * count], refs[2 * count]
-    out, middle, end_block, total = refs[2 * count + 1 :]
+    first, second, wide, mods = refs[:count], refs[count : 2 * count], refs[2 * count], refs[2 * count + 1 : 3 * count + 1]
+    out, middle, end_block, total = refs[3 * count + 1 :]
     ch = end_block.shape[0]
     for at in range(count):
         middle[at * ch : (at + 1) * ch] = first[at][...] + second[count - 1 - at][...]
     end_block[...] = first[-1][...] + second[-1][...]
-    (out[...],) = tap_products(middle, [wide], [total], height, width)
+    (out[0 : count * ch],) = tap_products(middle, [wide], [total], height, width)
+    for at, mod in enumerate(mods):
+        out[(count + at) * ch : (count + at + 1) * ch] = mod[...]
 
 
 def end_grad_kernel(height, width, end_block, feat, out, wide, total):
@@ -165,18 +167,17 @@
     (out[...],) = tap_products(end_block, [wide], [total], height, width)
 
 
-def input_grad_kernel(rows, size, height, width, place, cotan, first, second, middle, far, own_mod, behind, ahead, *refs):
-    others, (main, before, after, gathered, taps_t, total) = refs[: size - 2], refs[size - 2 :]
+def input_grad_kernel(rows, size, height, width, place, cotan, first, second, middle, far, own_mod, behind, ahead, others, end_mod, *refs):
+    main, before, after, gathered, taps_t, total = refs
     ch = main.shape[0]
     spot = jnp.where(place[3] > 0, place[1], size - 1 - place[1])
     gathered[0:ch] = cotan[...]
     gathered[ch : 2 * ch] = jnp.where(spot == 0, far[...], first[...])
     gathered[2 * ch : (size - 1) * ch] = middle[...]
     gathered[(size - 1) * ch :] = jnp.where(spot == size - 1, far[...], second[...])
-    end_mod = others[-1][...]
-    mods = [own_mod[...], jnp.where(spot == 0, end_mod, behind[ch:])]
-    mods += [other[...] for other in others[:-1]]
-    mods.append(jnp.where(spot == size - 1, end_mod, ahead[ch:]))
+    mods = [own_mod[...], jnp.where(spot == 0, end_mod[...], behind[ch:])]
+    mods.append(others[(size - 3) * ch :])
+    mods.append(jnp.where(spot == size - 1, end_mod[...], ahead[ch:]))
     every = jnp.concatenate([mod.astype(F32) for mod in mods], axis=0)
     taps_t[...] = every.T.astype(BF16)
     total[...] = jnp.zeros(total.shape, F32)
@@ -302,11 +303,15 @@
         copy.wait()
 
 
+def pair_sum(parts):
+    while len(parts) > 1:
+        parts = [x + y for x, y in zip(parts[::2], parts[1::2])]
+    return parts[0]
+
+
 def affine_kernel(samples, latents, *refs):
     parts, (w_grad, b_grad) = refs[:-2], refs[-2:]
-    style_grad = parts[0][...]
-    for part in parts[1:]:
-        style_grad = style_grad + part[...]
+    style_grad = pair_sum([part[...] for part in parts])
     high, mid, low = split3(latents[...])
     top, middle, bottom = split3(style_grad)
     w_grad[...] = lax.dot_general(
@@ -360,16 +365,11 @@
     ]
 
 
-def halves_of_sum(x, axis):
+def terms_of_sum(x, axis):
     size = lax.axis_size(axis)
     if size & (size - 1):
         return [lax.psum(x, axis)]
-    step, parts = 1, [x]
-    while step < size:
-        x = sum(parts[1:], parts[0])
-        parts = [x, lax.ppermute(x, axis, [(i, i ^ step) for i in range(size)])]
-        step *= 2
-    return parts
+    return [x] + [lax.ppermute(x, axis, [(i, i ^ step) for i in range(size)]) for step in range(1, size)]
 
 
 def from_sides(first, last, axis):
@@ -479,10 +479,11 @@
     grad_others, middle, end_block = call(
         functools.partial(middle_grad_kernel, count, height, width),
         "middle_grad",
-        [((count * ch, TAPS * ch), BF16), ((count * ch, pixels), BF16), ((ch, pixels), BF16)],
+        [((2 * count * ch, TAPS * ch), BF16), ((count * ch, pixels), BF16), ((ch, pixels), BF16)],
         *first[1:],
         *second[1:],
         wide,
+        *mods[2 : size - 1],
         scratch=[((3, count * ch, 3 * ch), F32)],
         flops=flops // size,
     )
@@ -516,8 +517,7 @@
         flops=COLLECT_FLOPS,
     )
     parts, mods = lax.optimization_barrier((parts, mods))
-    others = [along(mods[d], [(i, (i + d) % size) for i in range(size)]) for d in range(2, size - 1)]
-    others.append(lax.ppermute(mods[size], "chan", [(0, size - 1), (size - 1, 0)]))
+    end_mod = lax.ppermute(mods[size], "chan", [(0, size - 1), (size - 1, 0)])
     parts = [parts[0]] + [
         lax.ppermute(parts[r], "rows", [(i, (i + r) % rows) for i in range(rows)])
         for r in range(1, rows)
@@ -526,7 +526,7 @@
     (own,) = call(row_sum_kernel, "row_sum", [((slots, out_ch, in_ch), BF16)], scale, small, *parts)
     every = exchange_pairs(own, "samples")
 
-    own, others, far = lax.optimization_barrier((own, others, far))
+    own, end_mod, far = lax.optimization_barrier((own, end_mod, far))
     main, before, after = call(
         functools.partial(input_grad_kernel, rows, size, height, width),
         "input_grad",
@@ -540,7 +540,8 @@
         mods[0],
         from_behind,
         from_ahead,
-        *others,
+        from_others,
+        end_mod,
         scalars=1,
         scratch=[
             ((all_ch, pixels), BF16),
@@ -562,7 +563,7 @@
         scratch=[((samples, slots, out_ch, in_ch), BF16), (bank.shape, F32), pltpu.SemaphoreType.DMA((TAPS,))],
         kept=1,
     )
-    style_parts = halves_of_sum(style_part, "chan")
+    style_parts = terms_of_sum(style_part, "chan")
     edge = jnp.concatenate(
         [from_above[:, None], jnp.zeros((ch, height - 2, width), F32), from_below[:, None]], axis=1
     )

time: 88.1 us -> 86.3 us (0.980)
  waiting for transfers between devices: 18.4 us -> 12.6 us
  starting transfers between devices: 40 us -> 43.8 us
    ppermute x3 -> x4, waiting for transfers between devices: 6.74 us -> 2.33 us  [the longest x1 1.21 us: on_device(): end_mod = lax.ppermute(mods[size], 'chan', [(0, size - 1), (size - 1, 0)])]
    ppermute x3 -> x4, starting transfers between devices: 3.39 us -> 7.25 us  [the longest x3 4.44 us: terms_of_sum(): lax.ppermute(x, axis, [(i, i ^ step) for i in range(size)])]
    ppermute x1, waiting for transfers between devices: 1.33 us -> 0.01 us  [on_device(): far = lax.ppermute(end_block, 'chan', [(1, 0), (size - 2, size - 1)])]
    ppermute x8 -> x7, starting transfers between devices: 22.2 us -> 22.2 us  [along(): return lax.ppermute(x, ('samples', 'chan'), whole)]
  transfers between devices with their start and end apart: 21 -> 21, of which waited for: 8 -> 6; matrix products, arithmetic and copies ran while one was open for 3% -> 3% of each run, Pallas kernels for 26% -> 26%
where the time goes in v16:
time: 86.3 us; the launch traced here: 85.8 us
  starting transfers between devices  43.8 us (51%)
  Pallas kernels  23.6 us (27%)
  waiting for transfers between devices  12.6 us (15%)
  local copies, waits for them, and re-layouts  3.49 us (4%)
  other arithmetic  1.23 us (1%)
  between operations  0.99 us (1%)
    pallas_call x11, Pallas kernels, call(): pl.pallas_call(kernel, out_shape=outs, in_specs=sspec(scalars) + vspec(le...  23.6 us
    ppermute x7, starting transfers between devices, along(): return lax.ppermute(x, ('samples', 'chan'), whole)  22.2 us
    ppermute x1, starting transfers between devices, on_device(): feat_end = lax.ppermute(feat, 'chan', [(0, 1), (size - 1, size - 2)])  5.29 us
    ppermute x1, waiting for transfers between devices, on_device(): from_end = lax.ppermute(grad_end, 'chan', [(1, size - 1), (size - 2, 0)])  4.72 us
    ppermute x3, starting transfers between devices, terms_of_sum(): lax.ppermute(x, axis, [(i, i ^ step) for i in range(size)])  4.44 us
    unnamed x19, local copies, waits for them, and re-layouts  3.13 us
    ppermute x2, starting transfers between devices, from_sides(): got = lax.ppermute(edge, axis, [(0, 1), (1, 0)])  2.82 us
    ppermute x1, starting transfers between devices, on_device(): end_mod = lax.ppermute(mods[size], 'chan', [(0, size - 1), (size - 1, 0)])  2.8 us
  transfers between devices with their start and end apart: 21, of which 6 were waited for; matrix products, arithmetic and copies ran while one was open for 3% of the time, Pallas kernels for 26%

profile of v16, /device:TPU:0, one launch (start us, length us, event | category | flops | bytes accessed | tf_op | source)
XLA Modules:
  0.0 85.8 jit_solution(12279317658611634528)
XLA Ops:
  0.7 1.3 %copy.13 = bf16[8,8,8,512]{3,1,2,0:T(8,128)(2,1)S(1)} copy(bf16[8,8,8,512]{3,2,1,0:T(8,128)(2,1)} %bitcast.32) | data formatting | bytes 1048576
  2.0 5.7 %collective-permute-start.1 = (bf16[64,4096]{1,0:T(8,128)(2,1)S(1)}, bf16[64,4096]{1,0:T(8,128)(2,1)}, u32[]{:S(2)}, u32[]{:S(2)}) collective-permute-start(bf16[64,4096]{1,0:T(8,128)(2,1)S(1)} %bitcast.26), channel_id=1, source_target_pairs={{0,1},{1,2},{2,3},{7,6},{6,5},{5,4},{8,9},{9,10},{10,11},{15,14},{... | collective-permute-start | bytes 1572872 | tf_op jit(solution)/shard_map/ppermute | solution.py:404
  7.8 1.3 %collective-permute-start.2 = (bf16[64,4096]{1,0:T(8,128)(2,1)S(1)}, bf16[64,4096]{1,0:T(8,128)(2,1)}, u32[]{:S(2)}, u32[]{:S(2)}) collective-permute-start(bf16[64,4096]{1,0:T(8,128)(2,1)S(1)} %bitcast.27), channel_id=1, source_target_pairs={{1,0},{2,1},{3,2},{6,7},{5,6},{4,5},{9,8},{10,9},{11,10},{14,15},{... | collective-permute-start | bytes 1572872 | tf_op jit(solution)/shard_map/ppermute | solution.py:404
  9.1 0.2 copy.14
  9.3 1.6 %collective-permute-start.5 = (bf16[64,512]{1,0:T(8,128)(2,1)S(1)}, bf16[64,512]{1,0:T(8,128)(2,1)S(1)}, u32[]{:S(2)}, u32[]{:S(2)}) collective-permute-start(bf16[64,512]{1,0:T(8,128)(2,1)S(1)} %slice_select_fusion), channel_id=1, source_target_pairs={{0,16},{16,0},{1,17},{17,1},{2,18},{18,2},{3,19},{19,3},{4,20},{20... | collective-permute-start | bytes 196616 | tf_op jit(solution)/shard_map/ppermute | solution.py:379
  10.8 0.0 copy-done.6
  10.9 0.0 copy-done.3
  10.9 1.0 %plain.1 = (f32[10,64,128]{2,1,0:T(8,128)S(1)}, f32[8,128]{1,0:T(8,128)S(1)}) custom-call(s32[1,4]{1,0:T(1,128)S(1)} %copy-done.5, f32[1,512]{1,0:T(1,128)S(1)} %copy-done.4, f32[1,128]{1,0:T(1,128)S(1)} %bitcast.30, f32[512,128]{1,0:T(8,128)S(1)} %copy-done.3, f32[4,9,64,128]{3,2,1,0:T(8,128)S(1)} %copy-done), custom_call_target="tpu_custom_call" | custom-call | flops 1000000 | bytes 1776144 | tf_op jit(solution)/shard_map/plain/pallas_call | solution.py:332
  11.8 0.0 copy-start.1
  11.8 0.6 collective-permute-start
  12.4 1.2 %collective-permute-done.5 = bf16[64,512]{1,0:T(8,128)(2,1)S(1)} collective-permute-done((bf16[64,512]{1,0:T(8,128)(2,1)S(1)}, bf16[64,512]{1,0:T(8,128)(2,1)S(1)}, u32[]{:S(2)}, u32[]{:S(2)}) %collective-permute-start.5) | collective-permute-done | bytes 65568 | tf_op jit(solution)/shard_map/ppermute | solution.py:379
  13.7 5.3 %collective-permute-start.6 = (bf16[64,5120]{1,0:T(8,128)(2,1)S(1)}, bf16[64,5120]{1,0:T(8,128)(2,1)S(1)}, u32[]{:S(2)}, u32[]{:S(2)}) collective-permute-start(bf16[64,5120]{1,0:T(8,128)(2,1)S(1)} %feat_rows.1.refs_3_), channel_id=1, source_target_pairs={{0,1},{3,2},{4,5},{7,6},{8,9},{11,10},{12,13},{15,14},{16,17},{19,... | collective-permute-start | bytes 1966088 | tf_op jit(solution)/shard_map/ppermute | solution.py:444
  19.0 2.7 %collective-permute-done.refs_1_ = f32[10,64,128]{2,1,0:T(8,128)} collective-permute-done((f32[10,64,128]{2,1,0:T(8,128)S(1)}, f32[10,64,128]{2,1,0:T(8,128)}, u32[]{:S(2)}, u32[]{:S(2)}) %collective-permute-start) | collective-permute-done | bytes 327712 | tf_op jit(solution)/shard_map/ppermute | solution.py:364
  21.7 0.0 collective-permute-done.1.refs_1_.first
  21.7 0.0 collective-permute-done.2.refs_2_.second
  21.7 0.7 collective-permute-start.3
  22.4 1.3 %collective-permute-start.4 = (bf16[64,4096]{1,0:T(8,128)(2,1)}, bf16[64,4096]{1,0:T(8,128)(2,1)}, u32[]{:S(2)}, u32[]{:S(2)}) collective-permute-start(bf16[64,4096]{1,0:T(8,128)(2,1)} %collective-permute-done.2.refs_2_.second), channel_id=1, source_target_pairs={{1,0},{2,1},{6,7},{5,6},{9,8},{10,9},{14,15},{13,14},{17,16},{18,1... | collective-permute-start | bytes 1572872 | tf_op jit(solution)/shard_map/ppermute | solution.py:404
  23.7 0.1 pad_add_fusion.place
  23.8 1.0 %copy-done.2 = f32[10,64,128]{2,1,0:T(8,128)S(1)} copy-done((f32[10,64,128]{2,1,0:T(8,128)S(1)}, f32[10,64,128]{2,1,0:T(8,128)}, u32[]{:S(2)}) %copy-start.2) | copy-done | bytes 327704
  24.8 1.3 %mod_blocks.1 = (bf16[9,64,256]{2,1,0:T(8,128)(2,1)S(1)}, f32[64,128]{1,0:T(8,128)S(1)}, bf16[64,576]{1,0:T(8,128)(2,1)S(1)}, bf16[64,576]{1,0:T(8,128)(2,1)S(1)...) custom-call(s32[4]{0:T(128)S(1)} %pad_add_fusion.place, ...), custom_call_target="tpu_custom_call" | custom-call | flops 1000000 | bytes 1351696 | tf_op jit(solution)/shard_map/mod_blocks/pallas_call | solution.py:332
  26.0 4.5 %near_grad.1 = (bf16[64,576]{1,0:T(8,128)(2,1)S(1)}, bf16[128,576]{1,0:T(8,128)(2,1)S(1)}, bf16[128,576]{1,0:T(8,128)(2,1)S(1)}, bf16[192,5120]{1,0:T(8,128)(2,1)S(1)}) custom-call(bf16[64,4096]{1,0:T(8,128)(2,1)S(1)} %bitcast.28, bf16[64,4096]{1,0:T(8,128)(2,1)} %collective-permute-done.1.refs_1_.first, ...), custom_call_target="tpu_custom_call" | custom-call | flops 905969664 | bytes 4710400 | tf_op jit(solution)/shard_map/near_grad/pallas_call | solution.py:332
  30.6 1.3 %collective-permute-start.7 = (bf16[128,576]{1,0:T(8,128)(2,1)S(1)}, bf16[128,576]{1,0:T(8,128)(2,1)S(1)}, u32[]{:S(2)}, u32[]{:S(2)}) collective-permute-start(bf16[128,576]{1,0:T(8,128)(2,1)S(1)} %get-tuple-element.71), channel_id=1, source_target_pairs={{1,0},{2,1},{3,2},{6,7},{5,6},{4,5},{9,8},{10,9},{11,10},{14,15},{... | collective-permute-start | bytes 442376 | tf_op jit(solution)/shard_map/ppermute | solution.py:404
  31.9 7.6 %collective-permute-start.8 = (bf16[128,576]{1,0:T(8,128)(2,1)S(1)}, bf16[128,576]{1,0:T(8,128)(2,1)S(1)}, u32[]{:S(2)}, u32[]{:S(2)}) collective-permute-start(bf16[128,576]{1,0:T(8,128)(2,1)S(1)} %get-tuple-element.72), channel_id=1, source_target_pairs={{0,1},{1,2},{2,3},{7,6},{6,5},{5,4},{8,9},{9,10},{10,11},{15,14},{... | collective-permute-start | bytes 442376 | tf_op jit(solution)/shard_map/ppermute | solution.py:404
  39.4 0.0 collective-permute-done.6.feat
  39.5 0.0 collective-permute-done.3.refs_0_
  39.5 0.0 collective-permute-done.4.refs_1_
  39.5 3.7 %middle_grad.1 = (bf16[128,576]{1,0:T(8,128)(2,1)S(1)}, bf16[64,4096]{1,0:T(8,128)(2,1)S(1)}, bf16[64,4096]{1,0:T(8,128)(2,1)S(1)}) custom-call(bf16[64,4096]{1,0:T(8,128)(2,1)S(1)} %collective-permute-done.3.refs_0_, bf16[64,4096]{1,0:T(8,128)(2,1)} %collective-permute-done.4.refs_1_, bf16[192,5120]{1,0:T(8,128)(2,1)S(1)} %get-tuple-element.75.refs_2_, ...), custom_call_target="tpu_custom_call" | custom-call | flops 301989888 | bytes 4284416 | tf_op jit(solution)/shard_map/middle_grad/pallas_call | solution.py:332
  43.2 4.3 %collective-permute-start.9 = (bf16[128,576]{1,0:T(8,128)(2,1)S(1)}, bf16[128,576]{1,0:T(8,128)(2,1)S(1)}, u32[]{:S(2)}, u32[]{:S(2)}) collective-permute-start(bf16[128,576]{1,0:T(8,128)(2,1)S(1)} %get-tuple-element.77), channel_id=1, source_target_pairs={{0,2},{1,3},{2,0},{3,1},{7,5},{6,4},{5,7},{4,6},{8,10},{9,11},{10,... | collective-permute-start | bytes 442376 | tf_op jit(solution)/shard_map/ppermute | solution.py:404
  47.5 3.0 %end_grad.1 = bf16[64,576]{1,0:T(8,128)(2,1)S(1)} custom-call(bf16[64,4096]{1,0:T(8,128)(2,1)S(1)} %get-tuple-element.88.end_block, bf16[64,5120]{1,0:T(8,128)(2,1)S(1)} %collective-permute-done.6.feat), custom_call_target="tpu_custom_call" | custom-call | flops 301989888 | bytes 1253376 | tf_op jit(solution)/shard_map/end_grad/pallas_call | solution.py:332
  50.6 1.3 %collective-permute-start.10 = (bf16[64,576]{1,0:T(8,128)(2,1)S(1)}, bf16[64,576]{1,0:T(8,128)(2,1)S(1)}, u32[]{:S(2)}, u32[]{:S(2)}) collective-permute-start(bf16[64,576]{1,0:T(8,128)(2,1)S(1)} %end_grad.1), channel_id=1, source_target_pairs={{1,3},{2,0},{5,7},{6,4},{9,11},{10,8},{13,15},{14,12},{17,19},{18,... | collective-permute-start | bytes 221192 | tf_op jit(solution)/shard_map/ppermute | solution.py:500
  51.9 1.3 %collective-permute-start.16 = (bf16[64,4096]{1,0:T(8,128)(2,1)S(1)}, bf16[64,4096]{1,0:T(8,128)(2,1)S(1)}, u32[]{:S(2)}, u32[]{:S(2)}) collective-permute-start(bf16[64,4096]{1,0:T(8,128)(2,1)S(1)} %get-tuple-element.88.end_block), channel_id=1, source_target_pairs={{1,0},{2,3},{5,4},{6,7},{9,8},{10,11},{13,12},{14,15},{17,16},{18,... | collective-permute-start | bytes 1572872 | tf_op jit(solution)/shard_map/ppermute | solution.py:502
  53.2 0.0 collective-permute-done.7.ahead
  53.2 0.0 collective-permute-done.8.behind
  53.2 4.7 %collective-permute-done.10.end = bf16[64,576]{1,0:T(8,128)(2,1)S(1)} collective-permute-done((bf16[64,576]{1,0:T(8,128)(2,1)S(1)}, bf16[64,576]{1,0:T(8,128)(2,1)S(1)}, u32[]{:S(2)}, u32[]{:S(2)}) %collective-permute-start.10) | collective-permute-done | bytes 73760 | tf_op jit(solution)/shard_map/ppermute | solution.py:500
  57.9 0.0 collective-permute-done.9.others
  57.9 1.1 %collect.1 = (bf16[10,64,128]{2,1,0:T(8,128)(2,1)S(1)}, bf16[10,64,128]{2,1,0:T(8,128)(2,1)S(1)}) custom-call(s32[4]{0:T(128)S(1)} %pad_add_fusion.place, f32[64,128]{1,0:T(8,128)S(1)} %get-tuple-element.58.scale, bf16[9,64,256]{2,1,0:T(8,128)(2,1)S(1)} %get-tuple-element.69.whole_mod, bf16[64,576]{1,0:T(8,128)(2,1)S(1)} %get-tuple-element.70.own, ...), custom_call_target="tpu_custom_call" | custom-call | flops 6000000000 | bytes 1245200 | tf_op jit(solution)/shard_map/collect/pallas_call | solution.py:332
  59.0 0.9 %collective-permute-start.11 = (bf16[10,64,128]{2,1,0:T(8,128)(2,1)S(1)}, bf16[10,64,128]{2,1,0:T(8,128)(2,1)S(1)}, u32[]{:S(2)}, u32[]{:S(2)}) collective-permute-start(bf16[10,64,128]{2,1,0:T(8,128)(2,1)S(1)} %get-tuple-element.85), channel_id=1, source_target_pairs={{0,16},{16,0},{1,17},{17,1},{2,18},{18,2},{3,19},{19,3},{4,20},{20... | collective-permute-start | bytes 491528 | tf_op jit(solution)/shard_map/ppermute | solution.py:522
  59.9 2.8 %collective-permute-start.15 = (bf16[64,576]{1,0:T(8,128)(2,1)S(1)}, bf16[64,576]{1,0:T(8,128)(2,1)S(1)}, u32[]{:S(2)}, u32[]{:S(2)}) collective-permute-start(bf16[64,576]{1,0:T(8,128)(2,1)S(1)} %get-tuple-element.87), channel_id=1, source_target_pairs={{0,3},{3,0},{4,7},{7,4},{8,11},{11,8},{12,15},{15,12},{16,19},{19,... | collective-permute-start | bytes 221192 | tf_op jit(solution)/shard_map/ppermute | solution.py:520
  62.7 1.7 %collective-permute-done.11.refs_1_ = bf16[10,64,128]{2,1,0:T(8,128)(2,1)S(1)} collective-permute-done((bf16[10,64,128]{2,1,0:T(8,128)(2,1)S(1)}, bf16[10,64,128]{2,1,0:T(8,128)(2,1)S(1)}, u32[]{:S(2)}, u32[]{:S(2)}) %collective-permute-start.11) | collective-permute-done | bytes 163872 | tf_op jit(solution)/shard_map/ppermute | solution.py:522
  64.3 0.2 row_sum.1.refs_0_
  64.6 1.6 %collective-permute-start.12 = (bf16[11,64,128]{2,1,0:T(8,128)(2,1)S(1)}, bf16[11,64,128]{2,1,0:T(8,128)(2,1)S(1)}, u32[]{:S(2)}, u32[]{:S(2)}) collective-permute-start(bf16[11,64,128]{2,1,0:T(8,128)(2,1)S(1)} %row_sum.1.refs_0_), channel_id=1, source_target_pairs={{8,0},{12,4},{0,8},{4,12},{9,1},{13,5},{1,9},{5,13},{10,2},{14,6},... | collective-permute-start | bytes 540680 | tf_op jit(solution)/shard_map/ppermute | solution.py:357
  66.1 0.0 collective-permute-start.13
  66.1 0.6 collective-permute-start.14
  66.8 1.2 %collective-permute-done.15.end_mod = bf16[64,576]{1,0:T(8,128)(2,1)S(1)} collective-permute-done((bf16[64,576]{1,0:T(8,128)(2,1)S(1)}, bf16[64,576]{1,0:T(8,128)(2,1)S(1)}, u32[]{:S(2)}, u32[]{:S(2)}) %collective-permute-start.15) | collective-permute-done | bytes 73760 | tf_op jit(solution)/shard_map/ppermute | solution.py:520
  68.0 0.0 collective-permute-done.16.far
  68.0 5.2 %input_grad.1 = (f32[64,4096]{1,0:T(8,128)S(1)}, f32[64,512]{1,0:T(8,128)}, f32[64,512]{1,0:T(8,128)S(1)}) custom-call(s32[4]{0:T(128)S(1)} %pad_add_fusion.place, bf16[64,4096]{1,0:T(8,128)(2,1)S(1)} %bitcast.29, bf16[64,4096]{1,0:T(8,128)(2,1)} %collective-permute-done.1.refs_1_.first, bf16[64,4096]{1,0:T(8,128)(2,1)} %collective-permute-done.2.refs_2_.second, ...), custom_call_target="tpu_custom_call" | custom-call | flops 2000000000 | bytes 4522000 | tf_op jit(solution)/shard_map/input_grad/pallas_call | solution.py:332
  73.2 0.0 collective-permute-done.12.refs_1_
  73.2 0.0 collective-permute-done.13.refs_2_
  73.2 0.0 collective-permute-done.14.refs_3_
  73.2 1.3 %collective-permute-start.20 = (f32[64,512]{1,0:T(8,128)S(1)}, f32[64,512]{1,0:T(8,128)S(1)}, u32[]{:S(2)}, u32[]{:S(2)}) collective-permute-start(f32[64,512]{1,0:T(8,128)S(1)} %get-tuple-element.100), channel_id=1, source_target_pairs={{0,16},{16,0},{1,17},{17,1},{2,18},{18,2},{3,19},{19,3},{4,20},{20... | collective-permute-start | bytes 393224 | tf_op jit(solution)/shard_map/ppermute | solution.py:379
  74.5 0.1 pad.1.clone
  74.5 2.7 %bank_grad.1 = (f32[4,9,64,128]{3,2,1,0:T(8,128)}, f32[4,128]{1,0:T(4,128)S(1)}, f32[4,512]{1,0:T(4,128)S(1)}) custom-call(s32[4]{0:T(128)S(1)} %pad_add_fusion.place, f32[4,9,64,128]{3,2,1,0:T(8,128)S(1)} %copy-done, bf16[11,64,128]{2,1,0:T(8,128)(2,1)S(1)} %row_sum.1.refs_0_, bf16[11,64,128]{2,1,0:T(8,128)(2,1)S(1)} %collective-permute-done.12.refs_1_, ...), custom_call_target="tpu_custom_call" | custom-call | flops 1000000 | bytes 3090448 | tf_op jit(solution)/shard_map/bank_grad/pallas_call | solution.py:332
  77.2 0.1 collective-permute-start.17
  77.3 2.2 %collective-permute-start.18 = (f32[4,128]{1,0:T(4,128)S(1)}, f32[4,128]{1,0:T(4,128)S(1)}, u32[]{:S(2)}, u32[]{:S(2)}) collective-permute-start(f32[4,128]{1,0:T(4,128)S(1)} %get-tuple-element.104.refs_0_), channel_id=1, source_target_pairs={{0,2},{1,3},{2,0},{3,1},{4,6},{5,7},{6,4},{7,5},{8,10},{9,11},{10,... | collective-permute-start | bytes 6152 | tf_op jit(solution)/shard_map/ppermute | solution.py:372
  79.5 2.2 %collective-permute-start.19 = (f32[4,128]{1,0:T(4,128)S(1)}, f32[4,128]{1,0:T(4,128)S(1)}, u32[]{:S(2)}, u32[]{:S(2)}) collective-permute-start(f32[4,128]{1,0:T(4,128)S(1)} %get-tuple-element.104.refs_0_), channel_id=1, source_target_pairs={{0,3},{1,2},{2,1},{3,0},{4,7},{5,6},{6,5},{7,4},{8,11},{9,10},{10,... | collective-permute-start | bytes 6152 | tf_op jit(solution)/shard_map/ppermute | solution.py:372
  81.7 0.6 copy.15
  82.3 0.0 collective-permute-done.20
  82.3 0.1 copy.12
  82.5 0.1 copy.11
  82.6 1.1 %fusion = bf16[1,64,8,512]{3,2,1,0:T(8,128)(2,1)} fusion(f32[1,64,1,512]{3,2,1,0:T(1,128)S(1)} %copy.12, f32[1,64,1,512]{3,2,1,0:T(1,128)S(1)} %copy.11, f32[8]{0:T(128)S(1)} %pad.1.clone, f32[1,64,8,512]{3,2,1,0:T(8,128)S(1)} %bitcast.31), kind=kLoop, calls=%fused_computation.1 | loop fusion | flops 1048576 | bytes 1835040 | tf_op jit(solution)/shard_map/convert_element_type | solution.py:570
  83.7 0.0 collective-permute-done.17.refs_1_
  83.7 0.0 collective-permute-done.18.refs_2_
  83.7 1.1 %collective-permute-done.19.refs_3_ = f32[4,128]{1,0:T(4,128)S(1)} collective-permute-done((f32[4,128]{1,0:T(4,128)S(1)}, f32[4,128]{1,0:T(4,128)S(1)}, u32[]{:S(2)}, u32[]{:S(2)}) %collective-permute-start.19) | collective-permute-done | bytes 2080 | tf_op jit(solution)/shard_map/ppermute | solution.py:372
  84.9 0.9 %affine.1 = (f32[512,128]{1,0:T(8,128)}, f32[1,128]{1,0:T(1,128)}) custom-call(f32[4,512]{1,0:T(4,128)S(1)} %get-tuple-element.103.latents, f32[4,128]{1,0:T(4,128)S(1)} %get-tuple-element.104.refs_0_, f32[4,128]{1,0:T(4,128)S(1)} %collective-permute-done.17.refs_1_, f32[4,128]{1,0:T(4,128)S(1)} %collective-permute-done.18.refs_2_, ...), custom_call_target="tpu_custom_call" | custom-call | flops 1000000 | bytes 279040 | tf_op jit(solution)/shard_map/affine/pallas_call | solution.py:332
  (17 shorter events, 0.1 us)
Async XLA Ops:
  0.6 8.4 %copy-start.7 = (bf16[1,64,8,512]{3,2,1,0:T(8,128)(2,1)S(1)}, bf16[1,64,8,512]{3,2,1,0:T(8,128)(2,1)}, u32[]{:S(2)}) copy-start(bf16[1,64,8,512]{3,2,1,0:T(8,128)(2,1)} %param.7) | copy-start | bytes 1572868
  0.6 10.2 %copy-start = (f32[4,9,64,128]{3,2,1,0:T(8,128)S(1)}, f32[4,9,64,128]{3,2,1,0:T(8,128)}, u32[]{:S(2)}) copy-start(f32[4,9,64,128]{3,2,1,0:T(8,128)} %bank.1) | copy-start | bytes 3538948
  0.7 10.2 %copy-start.5 = (s32[1,4]{1,0:T(1,128)S(1)}, s32[1,4]{1,0:T(1,128)}, u32[]{:S(2)}) copy-start(s32[1,4]{1,0:T(1,128)} %refs_0_.1) | copy-start | bytes 52
  0.7 10.2 %copy-start.4 = (f32[1,512]{1,0:T(1,128)S(1)}, f32[1,512]{1,0:T(1,128)}, u32[]{:S(2)}) copy-start(f32[1,512]{1,0:T(1,128)} %refs_1_.1) | copy-start | bytes 6148
  0.7 10.2 %copy-start.6 = (f32[128]{0:T(128)S(1)}, f32[128]{0:T(128)}, u32[]{:S(2)}) copy-start(f32[128]{0:T(128)} %param.13) | copy-start | bytes 1540
  0.7 10.2 %copy-start.3 = (f32[512,128]{1,0:T(8,128)S(1)}, f32[512,128]{1,0:T(8,128)}, u32[]{:S(2)}) copy-start(f32[512,128]{1,0:T(8,128)} %refs_3_.1) | copy-start | bytes 786436
  2.0 19.7 %collective-permute-start.1 = (bf16[64,4096]{1,0:T(8,128)(2,1)S(1)}, bf16[64,4096]{1,0:T(8,128)(2,1)}, u32[]{:S(2)}, u32[]{:S(2)}) collective-permute-start(bf16[64,4096]{1,0:T(8,128)(2,1)S(1)} %bitcast.26), channel_id=1, source_target_pairs={{0,1},{1,2},{2,3},{7,6},{6,5},{5,4},{8,9},{9,10},{10,11},{15,14},{... | collective-permute-start | bytes 1572872 | tf_op jit(solution)/shard_map/ppermute | solution.py:404
  7.8 13.9 %collective-permute-start.2 = (bf16[64,4096]{1,0:T(8,128)(2,1)S(1)}, bf16[64,4096]{1,0:T(8,128)(2,1)}, u32[]{:S(2)}, u32[]{:S(2)}) collective-permute-start(bf16[64,4096]{1,0:T(8,128)(2,1)S(1)} %bitcast.27), channel_id=1, source_target_pairs={{1,0},{2,1},{3,2},{6,7},{5,6},{4,5},{9,8},{10,9},{11,10},{14,15},{... | collective-permute-start | bytes 1572872 | tf_op jit(solution)/shard_map/ppermute | solution.py:404
  9.3 4.3 %collective-permute-start.5 = (bf16[64,512]{1,0:T(8,128)(2,1)S(1)}, bf16[64,512]{1,0:T(8,128)(2,1)S(1)}, u32[]{:S(2)}, u32[]{:S(2)}) collective-permute-start(bf16[64,512]{1,0:T(8,128)(2,1)S(1)} %slice_select_fusion), channel_id=1, source_target_pairs={{0,16},{16,0},{1,17},{17,1},{2,18},{18,2},{3,19},{19,3},{4,20},{20... | collective-permute-start | bytes 196616 | tf_op jit(solution)/shard_map/ppermute | solution.py:379
  11.8 9.9 %copy-start.1 = (f32[10,64,128]{2,1,0:T(8,128)}, f32[10,64,128]{2,1,0:T(8,128)S(1)}, u32[]{:S(2)}) copy-start(f32[10,64,128]{2,1,0:T(8,128)S(1)} %get-tuple-element.57.refs_0_) | copy-start | bytes 983044
  11.8 9.8 %collective-permute-start = (f32[10,64,128]{2,1,0:T(8,128)S(1)}, f32[10,64,128]{2,1,0:T(8,128)}, u32[]{:S(2)}, u32[]{:S(2)}) collective-permute-start(f32[10,64,128]{2,1,0:T(8,128)S(1)} %get-tuple-element.57.refs_0_), channel_id=1, source_target_pairs={{0,16},{16,0},{1,17},{17,1},{2,18},{18,2},{3,19},{19,3},{4,20},{20... | collective-permute-start | bytes 983048 | tf_op jit(solution)/shard_map/ppermute | solution.py:364
  13.7 25.8 %collective-permute-start.6 = (bf16[64,5120]{1,0:T(8,128)(2,1)S(1)}, bf16[64,5120]{1,0:T(8,128)(2,1)S(1)}, u32[]{:S(2)}, u32[]{:S(2)}) collective-permute-start(bf16[64,5120]{1,0:T(8,128)(2,1)S(1)} %feat_rows.1.refs_3_), channel_id=1, source_target_pairs={{0,1},{3,2},{4,5},{7,6},{8,9},{11,10},{12,13},{15,14},{16,17},{19,... | collective-permute-start | bytes 1966088 | tf_op jit(solution)/shard_map/ppermute | solution.py:444
  21.7 17.8 %collective-permute-start.3 = (bf16[64,4096]{1,0:T(8,128)(2,1)}, bf16[64,4096]{1,0:T(8,128)(2,1)S(1)}, u32[]{:S(2)}, u32[]{:S(2)}) collective-permute-start(bf16[64,4096]{1,0:T(8,128)(2,1)} %collective-permute-done.1.refs_1_.first), channel_id=1, source_target_pairs={{1,2},{2,3},{6,5},{5,4},{9,10},{10,11},{14,13},{13,12},{17,18},{18... | collective-permute-start | bytes 1572872 | tf_op jit(solution)/shard_map/ppermute | solution.py:404
  22.4 17.1 %collective-permute-start.4 = (bf16[64,4096]{1,0:T(8,128)(2,1)}, bf16[64,4096]{1,0:T(8,128)(2,1)}, u32[]{:S(2)}, u32[]{:S(2)}) collective-permute-start(bf16[64,4096]{1,0:T(8,128)(2,1)} %collective-permute-done.2.refs_2_.second), channel_id=1, source_target_pairs={{1,0},{2,1},{6,7},{5,6},{9,8},{10,9},{14,15},{13,14},{17,16},{18,1... | collective-permute-start | bytes 1572872 | tf_op jit(solution)/shard_map/ppermute | solution.py:404
  23.8 1.0 %copy-start.2 = (f32[10,64,128]{2,1,0:T(8,128)S(1)}, f32[10,64,128]{2,1,0:T(8,128)}, u32[]{:S(2)}) copy-start(f32[10,64,128]{2,1,0:T(8,128)} %copy-done.1) | copy-start | bytes 983044
  30.6 22.6 %collective-permute-start.7 = (bf16[128,576]{1,0:T(8,128)(2,1)S(1)}, bf16[128,576]{1,0:T(8,128)(2,1)S(1)}, u32[]{:S(2)}, u32[]{:S(2)}) collective-permute-start(bf16[128,576]{1,0:T(8,128)(2,1)S(1)} %get-tuple-element.71), channel_id=1, source_target_pairs={{1,0},{2,1},{3,2},{6,7},{5,6},{4,5},{9,8},{10,9},{11,10},{14,15},{... | collective-permute-start | bytes 442376 | tf_op jit(solution)/shard_map/ppermute | solution.py:404
  31.9 21.3 %collective-permute-start.8 = (bf16[128,576]{1,0:T(8,128)(2,1)S(1)}, bf16[128,576]{1,0:T(8,128)(2,1)S(1)}, u32[]{:S(2)}, u32[]{:S(2)}) collective-permute-start(bf16[128,576]{1,0:T(8,128)(2,1)S(1)} %get-tuple-element.72), channel_id=1, source_target_pairs={{0,1},{1,2},{2,3},{7,6},{6,5},{5,4},{8,9},{9,10},{10,11},{15,14},{... | collective-permute-start | bytes 442376 | tf_op jit(solution)/shard_map/ppermute | solution.py:404
  43.2 14.7 %collective-permute-start.9 = (bf16[128,576]{1,0:T(8,128)(2,1)S(1)}, bf16[128,576]{1,0:T(8,128)(2,1)S(1)}, u32[]{:S(2)}, u32[]{:S(2)}) collective-permute-start(bf16[128,576]{1,0:T(8,128)(2,1)S(1)} %get-tuple-element.77), channel_id=1, source_target_pairs={{0,2},{1,3},{2,0},{3,1},{7,5},{6,4},{5,7},{4,6},{8,10},{9,11},{10,... | collective-permute-start | bytes 442376 | tf_op jit(solution)/shard_map/ppermute | solution.py:404
  50.6 7.3 %collective-permute-start.10 = (bf16[64,576]{1,0:T(8,128)(2,1)S(1)}, bf16[64,576]{1,0:T(8,128)(2,1)S(1)}, u32[]{:S(2)}, u32[]{:S(2)}) collective-permute-start(bf16[64,576]{1,0:T(8,128)(2,1)S(1)} %end_grad.1), channel_id=1, source_target_pairs={{1,3},{2,0},{5,7},{6,4},{9,11},{10,8},{13,15},{14,12},{17,19},{18,... | collective-permute-start | bytes 221192 | tf_op jit(solution)/shard_map/ppermute | solution.py:500
  51.9 16.1 %collective-permute-start.16 = (bf16[64,4096]{1,0:T(8,128)(2,1)S(1)}, bf16[64,4096]{1,0:T(8,128)(2,1)S(1)}, u32[]{:S(2)}, u32[]{:S(2)}) collective-permute-start(bf16[64,4096]{1,0:T(8,128)(2,1)S(1)} %get-tuple-element.88.end_block), channel_id=1, source_target_pairs={{1,0},{2,3},{5,4},{6,7},{9,8},{10,11},{13,12},{14,15},{17,16},{18,... | collective-permute-start | bytes 1572872 | tf_op jit(solution)/shard_map/ppermute | solution.py:502
  59.0 5.4 %collective-permute-start.11 = (bf16[10,64,128]{2,1,0:T(8,128)(2,1)S(1)}, bf16[10,64,128]{2,1,0:T(8,128)(2,1)S(1)}, u32[]{:S(2)}, u32[]{:S(2)}) collective-permute-start(bf16[10,64,128]{2,1,0:T(8,128)(2,1)S(1)} %get-tuple-element.85), channel_id=1, source_target_pairs={{0,16},{16,0},{1,17},{17,1},{2,18},{18,2},{3,19},{19,3},{4,20},{20... | collective-permute-start | bytes 491528 | tf_op jit(solution)/shard_map/ppermute | solution.py:522
  59.9 8.1 %collective-permute-start.15 = (bf16[64,576]{1,0:T(8,128)(2,1)S(1)}, bf16[64,576]{1,0:T(8,128)(2,1)S(1)}, u32[]{:S(2)}, u32[]{:S(2)}) collective-permute-start(bf16[64,576]{1,0:T(8,128)(2,1)S(1)} %get-tuple-element.87), channel_id=1, source_target_pairs={{0,3},{3,0},{4,7},{7,4},{8,11},{11,8},{12,15},{15,12},{16,19},{19,... | collective-permute-start | bytes 221192 | tf_op jit(solution)/shard_map/ppermute | solution.py:520
  64.6 8.6 %collective-permute-start.12 = (bf16[11,64,128]{2,1,0:T(8,128)(2,1)S(1)}, bf16[11,64,128]{2,1,0:T(8,128)(2,1)S(1)}, u32[]{:S(2)}, u32[]{:S(2)}) collective-permute-start(bf16[11,64,128]{2,1,0:T(8,128)(2,1)S(1)} %row_sum.1.refs_0_), channel_id=1, source_target_pairs={{8,0},{12,4},{0,8},{4,12},{9,1},{13,5},{1,9},{5,13},{10,2},{14,6},... | collective-permute-start | bytes 540680 | tf_op jit(solution)/shard_map/ppermute | solution.py:357
  66.1 7.0 %collective-permute-start.13 = (bf16[11,64,128]{2,1,0:T(8,128)(2,1)S(1)}, bf16[11,64,128]{2,1,0:T(8,128)(2,1)S(1)}, u32[]{:S(2)}, u32[]{:S(2)}) collective-permute-start(bf16[11,64,128]{2,1,0:T(8,128)(2,1)S(1)} %row_sum.1.refs_0_), channel_id=1, source_target_pairs={{12,0},{8,4},{4,8},{0,12},{13,1},{9,5},{5,9},{1,13},{14,2},{10,6},... | collective-permute-start | bytes 540680 | tf_op jit(solution)/shard_map/ppermute | solution.py:357
  66.1 7.0 %collective-permute-start.14 = (bf16[11,64,128]{2,1,0:T(8,128)(2,1)S(1)}, bf16[11,64,128]{2,1,0:T(8,128)(2,1)S(1)}, u32[]{:S(2)}, u32[]{:S(2)}) collective-permute-start(bf16[11,64,128]{2,1,0:T(8,128)(2,1)S(1)} %row_sum.1.refs_0_), channel_id=1, source_target_pairs={{4,0},{0,4},{12,8},{8,12},{5,1},{1,5},{13,9},{9,13},{6,2},{2,6},{1... | collective-permute-start | bytes 540680 | tf_op jit(solution)/shard_map/ppermute | solution.py:357
  73.2 9.1 %collective-permute-start.20 = (f32[64,512]{1,0:T(8,128)S(1)}, f32[64,512]{1,0:T(8,128)S(1)}, u32[]{:S(2)}, u32[]{:S(2)}) collective-permute-start(f32[64,512]{1,0:T(8,128)S(1)} %get-tuple-element.100), channel_id=1, source_target_pairs={{0,16},{16,0},{1,17},{17,1},{2,18},{18,2},{3,19},{19,3},{4,20},{20... | collective-permute-start | bytes 393224 | tf_op jit(solution)/shard_map/ppermute | solution.py:379
  77.2 6.5 %collective-permute-start.17 = (f32[4,128]{1,0:T(4,128)S(1)}, f32[4,128]{1,0:T(4,128)S(1)}, u32[]{:S(2)}, u32[]{:S(2)}) collective-permute-start(f32[4,128]{1,0:T(4,128)S(1)} %get-tuple-element.104.refs_0_), channel_id=1, source_target_pairs={{0,1},{1,0},{2,3},{3,2},{4,5},{5,4},{6,7},{7,6},{8,9},{9,8},{10,11... | collective-permute-start | bytes 6152 | tf_op jit(solution)/shard_map/ppermute | solution.py:372
  77.3 6.4 %collective-permute-start.18 = (f32[4,128]{1,0:T(4,128)S(1)}, f32[4,128]{1,0:T(4,128)S(1)}, u32[]{:S(2)}, u32[]{:S(2)}) collective-permute-start(f32[4,128]{1,0:T(4,128)S(1)} %get-tuple-element.104.refs_0_), channel_id=1, source_target_pairs={{0,2},{1,3},{2,0},{3,1},{4,6},{5,7},{6,4},{7,5},{8,10},{9,11},{10,... | collective-permute-start | bytes 6152 | tf_op jit(solution)/shard_map/ppermute | solution.py:372
  79.5 5.4 %collective-permute-start.19 = (f32[4,128]{1,0:T(4,128)S(1)}, f32[4,128]{1,0:T(4,128)S(1)}, u32[]{:S(2)}, u32[]{:S(2)}) collective-permute-start(f32[4,128]{1,0:T(4,128)S(1)} %get-tuple-element.104.refs_0_), channel_id=1, source_target_pairs={{0,3},{1,2},{2,1},{3,0},{4,7},{5,6},{6,5},{7,4},{8,11},{9,10},{10,... | collective-permute-start | bytes 6152 | tf_op jit(solution)/shard_map/ppermute | solution.py:372

commit v17 on v16

--- a/solution.py
+++ b/solution.py
@@ -44,7 +44,7 @@
 
 
 def plain_kernel(*refs):
-    given, (plain_out, small), held, sems = refs[:5], refs[5:7], refs[7:12], refs[12]
+    given, (plain_out, message, small), held, sems = refs[:5], refs[5:8], refs[8:13], refs[13]
     copies = [pltpu.make_async_copy(x, y, sems.at[n]) for n, (x, y) in enumerate(zip(given, held))]
     for copy in copies:
         copy.start()
@@ -61,8 +61,11 @@
     for tap in range(TAPS):
         plain = mixed(bank, weights, tap) * style
         plain_out[tap] = plain
+        message[tap] = plain.astype(BF16)
         total = total + plain * plain
-    plain_out[TAPS] = jnp.broadcast_to(jnp.sum(total, axis=1, keepdims=True), total.shape)
+    energy = jnp.sum(total, axis=1, keepdims=True)
+    plain_out[TAPS] = jnp.broadcast_to(energy, total.shape)
+    put_columns(message, [energy])
     small[...] = jnp.zeros(small.shape, F32)
     last = latent.shape[1] // in_ch
     for n in range(last):
@@ -78,13 +81,13 @@
 def blocks_kernel(rows, size, place, *refs):
     parts, (whole, scale_out), outs, (by_row, by_chan) = refs[:rows], refs[rows : rows + 2], refs[rows + 2 : -2], refs[-2:]
     row_at, chan_at, sign = place[2], place[1], place[3]
-    energy = parts[0][TAPS]
+    energy = parts[0][TAPS][:, 0:1]
     for part in parts[1:]:
-        energy = energy + part[TAPS]
-    scale = lax.rsqrt(energy[:, 0:1] + EPS)
+        energy = energy + get_column(part[TAPS])
+    scale = lax.rsqrt(energy + EPS)
     scale_out[...] = jnp.broadcast_to(scale, scale_out.shape)
     for r in range(rows):
-        by_row[lax.rem(row_at - r + rows, rows)] = parts[r][0:TAPS]
+        by_row[lax.rem(row_at - r + rows, rows)] = parts[r][0:TAPS].astype(F32)
     ch = whole.shape[2] // size
     taps = []
     for tap in range(TAPS):
@@ -413,10 +416,10 @@
     step(1, cotan, cotan)
 
     small_rows = -(-(latent.shape[1] // in_ch + 2) // 8) * 8
-    plain, small = call(
+    plain, plain_message, small = call(
         plain_kernel,
         "plain",
-        [((TAPS + 1, out_ch, in_ch), F32), ((small_rows, in_ch), F32)],
+        [((TAPS + 1, out_ch, in_ch), F32), ((TAPS + 1, out_ch, in_ch), BF16), ((small_rows, in_ch), F32)],
         select,
         latent,
         affine_b[None],
@@ -432,7 +435,7 @@
             pltpu.SemaphoreType.DMA((5,)),
         ],
     )
-    plains = exchange(plain, "rows")
+    plains = [plain] + exchange(plain_message, "rows")[1:]
     feature, cotan = lax.optimization_barrier((feature, cotan))
     feat = feature[0].reshape(ch, pixels)
     feat_before, feat_after = from_sides(feat[:, :width], feat[:, pixels - width :], "rows")

time: 86.3 us -> 86.6 us (level)
  waiting for transfers between devices: 12.6 us -> 9.75 us
  local copies, waits for them, and re-layouts: 3.49 us -> 5.78 us
  starting transfers between devices: 43.8 us -> 45 us
    ppermute x1, waiting for transfers between devices: 2.71 us -> 0.15 us  [exchange(): lax.ppermute(x, axis, [(i, (i + s) % size) for i in range(size)])]
    unnamed x19 -> x23, local copies, waits for them, and re-layouts: 3.13 us -> 5.43 us
    ppermute x7, starting transfers between devices: 22.2 us -> 23.1 us  [along(): return lax.ppermute(x, ('samples', 'chan'), whole)]
where the time goes in v17:
time: 86.6 us; the launch traced here: 86.1 us
  starting transfers between devices  45 us (52%)
  Pallas kernels  23.3 us (27%)
  waiting for transfers between devices  9.75 us (11%)
  local copies, waits for them, and re-layouts  5.78 us (7%)
  other arithmetic  1.23 us (1%)
  between operations  0.99 us (1%)
    pallas_call x11, Pallas kernels, call(): pl.pallas_call(kernel, out_shape=outs, in_specs=sspec(scalars) + vspec(le...  23.3 us
    ppermute x7, starting transfers between devices, along(): return lax.ppermute(x, ('samples', 'chan'), whole)  23.1 us
    unnamed x23, local copies, waits for them, and re-layouts  5.43 us
    ppermute x1, starting transfers between devices, on_device(): feat_end = lax.ppermute(feat, 'chan', [(0, 1), (size - 1, size - 2)])  4.9 us
    ppermute x1, waiting for transfers between devices, on_device(): from_end = lax.ppermute(grad_end, 'chan', [(1, size - 1), (size - 2, 0)])  4.72 us
    ppermute x3, starting transfers between devices, terms_of_sum(): lax.ppermute(x, axis, [(i, i ^ step) for i in range(size)])  4.44 us
    ppermute x2, starting transfers between devices, from_sides(): got = lax.ppermute(edge, axis, [(0, 1), (1, 0)])  2.91 us
    ppermute x1, starting transfers between devices, on_device(): end_mod = lax.ppermute(mods[size], 'chan', [(0, size - 1), (size - 1, 0)])  2.8 us
  transfers between devices with their start and end apart: 21, of which 6 were waited for; matrix products, arithmetic and copies ran while one was open for 3% of the time, Pallas kernels for 26%

profile of v17, /device:TPU:0, one launch (start us, length us, event | category | flops | bytes accessed | tf_op | source)
XLA Modules:
  0.0 86.1 jit_solution(12170103111182201051)
XLA Ops:
  0.7 1.3 %copy.13 = bf16[8,8,8,512]{3,1,2,0:T(8,128)(2,1)S(1)} copy(bf16[8,8,8,512]{3,2,1,0:T(8,128)(2,1)} %bitcast.32) | data formatting | bytes 1048576
  2.0 5.7 %collective-permute-start.1 = (bf16[64,4096]{1,0:T(8,128)(2,1)S(1)}, bf16[64,4096]{1,0:T(8,128)(2,1)}, u32[]{:S(2)}, u32[]{:S(2)}) collective-permute-start(bf16[64,4096]{1,0:T(8,128)(2,1)S(1)} %bitcast.26), channel_id=1, source_target_pairs={{0,1},{1,2},{2,3},{7,6},{6,5},{5,4},{8,9},{9,10},{10,11},{15,14},{... | collective-permute-start | bytes 1572872 | tf_op jit(solution)/shard_map/ppermute | solution.py:407
  7.8 1.3 %collective-permute-start.2 = (bf16[64,4096]{1,0:T(8,128)(2,1)S(1)}, bf16[64,4096]{1,0:T(8,128)(2,1)}, u32[]{:S(2)}, u32[]{:S(2)}) collective-permute-start(bf16[64,4096]{1,0:T(8,128)(2,1)S(1)} %bitcast.27), channel_id=1, source_target_pairs={{1,0},{2,1},{3,2},{6,7},{5,6},{4,5},{9,8},{10,9},{11,10},{14,15},{... | collective-permute-start | bytes 1572872 | tf_op jit(solution)/shard_map/ppermute | solution.py:407
  9.1 0.2 copy.14
  9.3 1.6 %collective-permute-start.5 = (bf16[64,512]{1,0:T(8,128)(2,1)S(1)}, bf16[64,512]{1,0:T(8,128)(2,1)S(1)}, u32[]{:S(2)}, u32[]{:S(2)}) collective-permute-start(bf16[64,512]{1,0:T(8,128)(2,1)S(1)} %slice_select_fusion), channel_id=1, source_target_pairs={{0,16},{16,0},{1,17},{17,1},{2,18},{18,2},{3,19},{19,3},{4,20},{20... | collective-permute-start | bytes 196616 | tf_op jit(solution)/shard_map/ppermute | solution.py:382
  10.9 1.0 %plain.1 = (f32[10,64,128]{2,1,0:T(8,128)S(1)}, bf16[10,64,128]{2,1,0:T(8,128)(2,1)S(1)}, f32[8,128]{1,0:T(8,128)S(1)}) custom-call(s32[1,4]{1,0:T(1,128)S(1)} %copy-done.7, f32[1,512]{1,0:T(1,128)S(1)} %copy-done.6, f32[1,128]{1,0:T(1,128)S(1)} %bitcast.30, f32[512,128]{1,0:T(8,128)S(1)} %copy-done.3, f32[4,9,64,128]{3,2,1,0:T(8,128)S(1)} %copy-done), custom_call_target="tpu_custom_call" | custom-call | flops 1000000 | bytes 1939984 | tf_op jit(solution)/shard_map/plain/pallas_call | solution.py:335
  11.8 0.0 copy-start.1
  11.9 0.7 copy-done.1
  12.6 0.5 collective-permute-start
  13.1 0.5 collective-permute-done.5
  13.7 4.9 %collective-permute-start.6 = (bf16[64,5120]{1,0:T(8,128)(2,1)S(1)}, bf16[64,5120]{1,0:T(8,128)(2,1)S(1)}, u32[]{:S(2)}, u32[]{:S(2)}) collective-permute-start(bf16[64,5120]{1,0:T(8,128)(2,1)S(1)} %feat_rows.1.refs_3_), channel_id=1, source_target_pairs={{0,1},{3,2},{4,5},{7,6},{8,9},{11,10},{12,13},{15,14},{16,17},{19,... | collective-permute-start | bytes 1966088 | tf_op jit(solution)/shard_map/ppermute | solution.py:447
  18.6 0.1 collective-permute-done.refs_1_
  18.7 0.7 copy-done.4
  19.4 0.0 collective-permute-done.1.refs_1_.first
  19.4 0.0 collective-permute-done.2.refs_2_.second
  19.4 0.7 collective-permute-start.3
  20.1 1.3 %collective-permute-start.4 = (bf16[64,4096]{1,0:T(8,128)(2,1)}, bf16[64,4096]{1,0:T(8,128)(2,1)}, u32[]{:S(2)}, u32[]{:S(2)}) collective-permute-start(bf16[64,4096]{1,0:T(8,128)(2,1)} %collective-permute-done.2.refs_2_.second), channel_id=1, source_target_pairs={{1,0},{2,1},{6,7},{5,6},{9,8},{10,9},{14,15},{13,14},{17,16},{18,1... | collective-permute-start | bytes 1572872 | tf_op jit(solution)/shard_map/ppermute | solution.py:407
  21.4 0.1 pad_add_fusion.place
  21.5 1.0 %copy-done.2 = f32[10,64,128]{2,1,0:T(8,128)S(1)} copy-done((f32[10,64,128]{2,1,0:T(8,128)S(1)}, f32[10,64,128]{2,1,0:T(8,128)}, u32[]{:S(2)}) %copy-start.2) | copy-done | bytes 327704
  22.5 0.9 %copy-done.5 = bf16[10,64,128]{2,1,0:T(8,128)(2,1)S(1)} copy-done((bf16[10,64,128]{2,1,0:T(8,128)(2,1)S(1)}, bf16[10,64,128]{2,1,0:T(8,128)(2,1)}, u32[]{:S(2)}) %copy-start.5) | copy-done | bytes 163864
  23.4 0.9 %mod_blocks.1 = (bf16[9,64,256]{2,1,0:T(8,128)(2,1)S(1)}, f32[64,128]{1,0:T(8,128)S(1)}, bf16[64,576]{1,0:T(8,128)(2,1)S(1)}, bf16[64,576]{1,0:T(8,128)(2,1)S(1)...) custom-call(s32[4]{0:T(128)S(1)} %pad_add_fusion.place, ...), custom_call_target="tpu_custom_call" | custom-call | flops 1000000 | bytes 1187856 | tf_op jit(solution)/shard_map/mod_blocks/pallas_call | solution.py:335
  24.3 4.5 %near_grad.1 = (bf16[64,576]{1,0:T(8,128)(2,1)S(1)}, bf16[128,576]{1,0:T(8,128)(2,1)S(1)}, bf16[128,576]{1,0:T(8,128)(2,1)S(1)}, bf16[192,5120]{1,0:T(8,128)(2,1)S(1)}) custom-call(bf16[64,4096]{1,0:T(8,128)(2,1)S(1)} %bitcast.28, bf16[64,4096]{1,0:T(8,128)(2,1)} %collective-permute-done.1.refs_1_.first, ...), custom_call_target="tpu_custom_call" | custom-call | flops 905969664 | bytes 4710400 | tf_op jit(solution)/shard_map/near_grad/pallas_call | solution.py:335
  28.8 1.3 %collective-permute-start.7 = (bf16[128,576]{1,0:T(8,128)(2,1)S(1)}, bf16[128,576]{1,0:T(8,128)(2,1)S(1)}, u32[]{:S(2)}, u32[]{:S(2)}) collective-permute-start(bf16[128,576]{1,0:T(8,128)(2,1)S(1)} %get-tuple-element.73), channel_id=1, source_target_pairs={{1,0},{2,1},{3,2},{6,7},{5,6},{4,5},{9,8},{10,9},{11,10},{14,15},{... | collective-permute-start | bytes 442376 | tf_op jit(solution)/shard_map/ppermute | solution.py:407
  30.1 8.5 %collective-permute-start.8 = (bf16[128,576]{1,0:T(8,128)(2,1)S(1)}, bf16[128,576]{1,0:T(8,128)(2,1)S(1)}, u32[]{:S(2)}, u32[]{:S(2)}) collective-permute-start(bf16[128,576]{1,0:T(8,128)(2,1)S(1)} %get-tuple-element.74), channel_id=1, source_target_pairs={{0,1},{1,2},{2,3},{7,6},{6,5},{5,4},{8,9},{9,10},{10,11},{15,14},{... | collective-permute-start | bytes 442376 | tf_op jit(solution)/shard_map/ppermute | solution.py:407
  38.6 0.0 collective-permute-done.6.feat
  38.7 0.0 collective-permute-done.3.refs_0_
  38.7 0.0 collective-permute-done.4.refs_1_
  38.7 3.7 %middle_grad.1 = (bf16[128,576]{1,0:T(8,128)(2,1)S(1)}, bf16[64,4096]{1,0:T(8,128)(2,1)S(1)}, bf16[64,4096]{1,0:T(8,128)(2,1)S(1)}) custom-call(bf16[64,4096]{1,0:T(8,128)(2,1)S(1)} %collective-permute-done.3.refs_0_, bf16[64,4096]{1,0:T(8,128)(2,1)} %collective-permute-done.4.refs_1_, bf16[192,5120]{1,0:T(8,128)(2,1)S(1)} %get-tuple-element.77.refs_2_, ...), custom_call_target="tpu_custom_call" | custom-call | flops 301989888 | bytes 4284416 | tf_op jit(solution)/shard_map/middle_grad/pallas_call | solution.py:335
  42.4 4.3 %collective-permute-start.9 = (bf16[128,576]{1,0:T(8,128)(2,1)S(1)}, bf16[128,576]{1,0:T(8,128)(2,1)S(1)}, u32[]{:S(2)}, u32[]{:S(2)}) collective-permute-start(bf16[128,576]{1,0:T(8,128)(2,1)S(1)} %get-tuple-element.79), channel_id=1, source_target_pairs={{0,2},{1,3},{2,0},{3,1},{7,5},{6,4},{5,7},{4,6},{8,10},{9,11},{10,... | collective-permute-start | bytes 442376 | tf_op jit(solution)/shard_map/ppermute | solution.py:407
  46.7 3.0 %end_grad.1 = bf16[64,576]{1,0:T(8,128)(2,1)S(1)} custom-call(bf16[64,4096]{1,0:T(8,128)(2,1)S(1)} %get-tuple-element.90.end_block, bf16[64,5120]{1,0:T(8,128)(2,1)S(1)} %collective-permute-done.6.feat), custom_call_target="tpu_custom_call" | custom-call | flops 301989888 | bytes 1253376 | tf_op jit(solution)/shard_map/end_grad/pallas_call | solution.py:335
  49.8 1.3 %collective-permute-start.10 = (bf16[64,576]{1,0:T(8,128)(2,1)S(1)}, bf16[64,576]{1,0:T(8,128)(2,1)S(1)}, u32[]{:S(2)}, u32[]{:S(2)}) collective-permute-start(bf16[64,576]{1,0:T(8,128)(2,1)S(1)} %end_grad.1), channel_id=1, source_target_pairs={{1,3},{2,0},{5,7},{6,4},{9,11},{10,8},{13,15},{14,12},{17,19},{18,... | collective-permute-start | bytes 221192 | tf_op jit(solution)/shard_map/ppermute | solution.py:503
  51.1 1.3 %collective-permute-start.16 = (bf16[64,4096]{1,0:T(8,128)(2,1)S(1)}, bf16[64,4096]{1,0:T(8,128)(2,1)S(1)}, u32[]{:S(2)}, u32[]{:S(2)}) collective-permute-start(bf16[64,4096]{1,0:T(8,128)(2,1)S(1)} %get-tuple-element.90.end_block), channel_id=1, source_target_pairs={{1,0},{2,3},{5,4},{6,7},{9,8},{10,11},{13,12},{14,15},{17,16},{18,... | collective-permute-start | bytes 1572872 | tf_op jit(solution)/shard_map/ppermute | solution.py:505
  52.4 0.0 collective-permute-done.7.ahead
  52.4 0.0 collective-permute-done.8.behind
  52.4 4.7 %collective-permute-done.10.end = bf16[64,576]{1,0:T(8,128)(2,1)S(1)} collective-permute-done((bf16[64,576]{1,0:T(8,128)(2,1)S(1)}, bf16[64,576]{1,0:T(8,128)(2,1)S(1)}, u32[]{:S(2)}, u32[]{:S(2)}) %collective-permute-start.10) | collective-permute-done | bytes 73760 | tf_op jit(solution)/shard_map/ppermute | solution.py:503
  57.1 0.0 collective-permute-done.9.others
  57.1 1.1 %collect.1 = (bf16[10,64,128]{2,1,0:T(8,128)(2,1)S(1)}, bf16[10,64,128]{2,1,0:T(8,128)(2,1)S(1)}) custom-call(s32[4]{0:T(128)S(1)} %pad_add_fusion.place, f32[64,128]{1,0:T(8,128)S(1)} %get-tuple-element.60.scale, bf16[9,64,256]{2,1,0:T(8,128)(2,1)S(1)} %get-tuple-element.71.whole_mod, bf16[64,576]{1,0:T(8,128)(2,1)S(1)} %get-tuple-element.72.own, ...), custom_call_target="tpu_custom_call" | custom-call | flops 6000000000 | bytes 1245200 | tf_op jit(solution)/shard_map/collect/pallas_call | solution.py:335
  58.2 1.6 %collective-permute-start.11 = (bf16[10,64,128]{2,1,0:T(8,128)(2,1)S(1)}, bf16[10,64,128]{2,1,0:T(8,128)(2,1)S(1)}, u32[]{:S(2)}, u32[]{:S(2)}) collective-permute-start(bf16[10,64,128]{2,1,0:T(8,128)(2,1)S(1)} %get-tuple-element.87), channel_id=1, source_target_pairs={{0,16},{16,0},{1,17},{17,1},{2,18},{18,2},{3,19},{19,3},{4,20},{20... | collective-permute-start | bytes 491528 | tf_op jit(solution)/shard_map/ppermute | solution.py:525
  59.7 2.8 %collective-permute-start.15 = (bf16[64,576]{1,0:T(8,128)(2,1)S(1)}, bf16[64,576]{1,0:T(8,128)(2,1)S(1)}, u32[]{:S(2)}, u32[]{:S(2)}) collective-permute-start(bf16[64,576]{1,0:T(8,128)(2,1)S(1)} %get-tuple-element.89), channel_id=1, source_target_pairs={{0,3},{3,0},{4,7},{7,4},{8,11},{11,8},{12,15},{15,12},{16,19},{19,... | collective-permute-start | bytes 221192 | tf_op jit(solution)/shard_map/ppermute | solution.py:523
  62.5 1.0 %collective-permute-done.11.refs_1_ = bf16[10,64,128]{2,1,0:T(8,128)(2,1)S(1)} collective-permute-done((bf16[10,64,128]{2,1,0:T(8,128)(2,1)S(1)}, bf16[10,64,128]{2,1,0:T(8,128)(2,1)S(1)}, u32[]{:S(2)}, u32[]{:S(2)}) %collective-permute-start.11) | collective-permute-done | bytes 163872 | tf_op jit(solution)/shard_map/ppermute | solution.py:525
  63.5 0.2 row_sum.1.refs_0_
  63.8 1.6 %collective-permute-start.12 = (bf16[11,64,128]{2,1,0:T(8,128)(2,1)S(1)}, bf16[11,64,128]{2,1,0:T(8,128)(2,1)S(1)}, u32[]{:S(2)}, u32[]{:S(2)}) collective-permute-start(bf16[11,64,128]{2,1,0:T(8,128)(2,1)S(1)} %row_sum.1.refs_0_), channel_id=1, source_target_pairs={{8,0},{12,4},{0,8},{4,12},{9,1},{13,5},{1,9},{5,13},{10,2},{14,6},... | collective-permute-start | bytes 540680 | tf_op jit(solution)/shard_map/ppermute | solution.py:360
  65.3 0.0 collective-permute-start.13
  65.3 0.6 collective-permute-start.14
  66.0 1.9 %collective-permute-done.15.end_mod = bf16[64,576]{1,0:T(8,128)(2,1)S(1)} collective-permute-done((bf16[64,576]{1,0:T(8,128)(2,1)S(1)}, bf16[64,576]{1,0:T(8,128)(2,1)S(1)}, u32[]{:S(2)}, u32[]{:S(2)}) %collective-permute-start.15) | collective-permute-done | bytes 73760 | tf_op jit(solution)/shard_map/ppermute | solution.py:523
  67.8 0.0 collective-permute-done.16.far
  67.8 5.2 %input_grad.1 = (f32[64,4096]{1,0:T(8,128)S(1)}, f32[64,512]{1,0:T(8,128)}, f32[64,512]{1,0:T(8,128)S(1)}) custom-call(s32[4]{0:T(128)S(1)} %pad_add_fusion.place, bf16[64,4096]{1,0:T(8,128)(2,1)S(1)} %bitcast.29, bf16[64,4096]{1,0:T(8,128)(2,1)} %collective-permute-done.1.refs_1_.first, bf16[64,4096]{1,0:T(8,128)(2,1)} %collective-permute-done.2.refs_2_.second, ...), custom_call_target="tpu_custom_call" | custom-call | flops 2000000000 | bytes 4522000 | tf_op jit(solution)/shard_map/input_grad/pallas_call | solution.py:335
  73.0 0.0 collective-permute-done.12.refs_1_
  73.0 0.0 collective-permute-done.13.refs_2_
  73.1 0.0 collective-permute-done.14.refs_3_
  73.1 1.4 %collective-permute-start.20 = (f32[64,512]{1,0:T(8,128)S(1)}, f32[64,512]{1,0:T(8,128)S(1)}, u32[]{:S(2)}, u32[]{:S(2)}) collective-permute-start(f32[64,512]{1,0:T(8,128)S(1)} %get-tuple-element.102), channel_id=1, source_target_pairs={{0,16},{16,0},{1,17},{17,1},{2,18},{18,2},{3,19},{19,3},{4,20},{20... | collective-permute-start | bytes 393224 | tf_op jit(solution)/shard_map/ppermute | solution.py:382
  74.4 0.1 pad.1.clone
  74.5 2.7 %bank_grad.1 = (f32[4,9,64,128]{3,2,1,0:T(8,128)}, f32[4,128]{1,0:T(4,128)S(1)}, f32[4,512]{1,0:T(4,128)S(1)}) custom-call(s32[4]{0:T(128)S(1)} %pad_add_fusion.place, f32[4,9,64,128]{3,2,1,0:T(8,128)S(1)} %copy-done, bf16[11,64,128]{2,1,0:T(8,128)(2,1)S(1)} %row_sum.1.refs_0_, bf16[11,64,128]{2,1,0:T(8,128)(2,1)S(1)} %collective-permute-done.12.refs_1_, ...), custom_call_target="tpu_custom_call" | custom-call | flops 1000000 | bytes 3090448 | tf_op jit(solution)/shard_map/bank_grad/pallas_call | solution.py:335
  77.2 0.1 collective-permute-start.17
  77.3 2.5 %collective-permute-start.18 = (f32[4,128]{1,0:T(4,128)S(1)}, f32[4,128]{1,0:T(4,128)S(1)}, u32[]{:S(2)}, u32[]{:S(2)}) collective-permute-start(f32[4,128]{1,0:T(4,128)S(1)} %get-tuple-element.106.refs_0_), channel_id=1, source_target_pairs={{0,2},{1,3},{2,0},{3,1},{4,6},{5,7},{6,4},{7,5},{8,10},{9,11},{10,... | collective-permute-start | bytes 6152 | tf_op jit(solution)/shard_map/ppermute | solution.py:375
  79.8 1.9 %collective-permute-start.19 = (f32[4,128]{1,0:T(4,128)S(1)}, f32[4,128]{1,0:T(4,128)S(1)}, u32[]{:S(2)}, u32[]{:S(2)}) collective-permute-start(f32[4,128]{1,0:T(4,128)S(1)} %get-tuple-element.106.refs_0_), channel_id=1, source_target_pairs={{0,3},{1,2},{2,1},{3,0},{4,7},{5,6},{6,5},{7,4},{8,11},{9,10},{10,... | collective-permute-start | bytes 6152 | tf_op jit(solution)/shard_map/ppermute | solution.py:375
  81.7 0.6 copy.15
  82.3 0.0 collective-permute-done.20
  82.3 0.1 copy.12
  82.4 0.1 copy.11
  82.6 1.1 %fusion = bf16[1,64,8,512]{3,2,1,0:T(8,128)(2,1)} fusion(f32[1,64,1,512]{3,2,1,0:T(1,128)S(1)} %copy.12, f32[1,64,1,512]{3,2,1,0:T(1,128)S(1)} %copy.11, f32[8]{0:T(128)S(1)} %pad.1.clone, f32[1,64,8,512]{3,2,1,0:T(8,128)S(1)} %bitcast.31), kind=kLoop, calls=%fused_computation.1 | loop fusion | flops 1048576 | bytes 1835040 | tf_op jit(solution)/shard_map/convert_element_type | solution.py:573
  83.7 0.0 collective-permute-done.17.refs_1_
  83.7 1.4 %collective-permute-done.19.refs_3_ = f32[4,128]{1,0:T(4,128)S(1)} collective-permute-done((f32[4,128]{1,0:T(4,128)S(1)}, f32[4,128]{1,0:T(4,128)S(1)}, u32[]{:S(2)}, u32[]{:S(2)}) %collective-permute-start.19) | collective-permute-done | bytes 2080 | tf_op jit(solution)/shard_map/ppermute | solution.py:375
  85.2 0.9 %affine.1 = (f32[512,128]{1,0:T(8,128)}, f32[1,128]{1,0:T(1,128)}) custom-call(f32[4,512]{1,0:T(4,128)S(1)} %get-tuple-element.105.latents, f32[4,128]{1,0:T(4,128)S(1)} %get-tuple-element.106.refs_0_, f32[4,128]{1,0:T(4,128)S(1)} %collective-permute-done.17.refs_1_, f32[4,128]{1,0:T(4,128)S(1)} %collective-permute-done.18.refs_2_, ...), custom_call_target="tpu_custom_call" | custom-call | flops 1000000 | bytes 279040 | tf_op jit(solution)/shard_map/affine/pallas_call | solution.py:335
  (21 shorter events, 0.1 us)
Async XLA Ops:
  0.6 8.4 %copy-start.9 = (bf16[1,64,8,512]{3,2,1,0:T(8,128)(2,1)S(1)}, bf16[1,64,8,512]{3,2,1,0:T(8,128)(2,1)}, u32[]{:S(2)}) copy-start(bf16[1,64,8,512]{3,2,1,0:T(8,128)(2,1)} %param.7) | copy-start | bytes 1572868
  0.6 10.2 %copy-start = (f32[4,9,64,128]{3,2,1,0:T(8,128)S(1)}, f32[4,9,64,128]{3,2,1,0:T(8,128)}, u32[]{:S(2)}) copy-start(f32[4,9,64,128]{3,2,1,0:T(8,128)} %bank.1) | copy-start | bytes 3538948
  0.7 10.2 %copy-start.7 = (s32[1,4]{1,0:T(1,128)S(1)}, s32[1,4]{1,0:T(1,128)}, u32[]{:S(2)}) copy-start(s32[1,4]{1,0:T(1,128)} %refs_0_.1) | copy-start | bytes 52
  0.7 10.2 %copy-start.6 = (f32[1,512]{1,0:T(1,128)S(1)}, f32[1,512]{1,0:T(1,128)}, u32[]{:S(2)}) copy-start(f32[1,512]{1,0:T(1,128)} %refs_1_.1) | copy-start | bytes 6148
  0.7 10.2 %copy-start.8 = (f32[128]{0:T(128)S(1)}, f32[128]{0:T(128)}, u32[]{:S(2)}) copy-start(f32[128]{0:T(128)} %param.13) | copy-start | bytes 1540
  0.7 10.2 %copy-start.3 = (f32[512,128]{1,0:T(8,128)S(1)}, f32[512,128]{1,0:T(8,128)}, u32[]{:S(2)}) copy-start(f32[512,128]{1,0:T(8,128)} %refs_3_.1) | copy-start | bytes 786436
  2.0 17.4 %collective-permute-start.1 = (bf16[64,4096]{1,0:T(8,128)(2,1)S(1)}, bf16[64,4096]{1,0:T(8,128)(2,1)}, u32[]{:S(2)}, u32[]{:S(2)}) collective-permute-start(bf16[64,4096]{1,0:T(8,128)(2,1)S(1)} %bitcast.26), channel_id=1, source_target_pairs={{0,1},{1,2},{2,3},{7,6},{6,5},{5,4},{8,9},{9,10},{10,11},{15,14},{... | collective-permute-start | bytes 1572872 | tf_op jit(solution)/shard_map/ppermute | solution.py:407
  7.8 11.6 %collective-permute-start.2 = (bf16[64,4096]{1,0:T(8,128)(2,1)S(1)}, bf16[64,4096]{1,0:T(8,128)(2,1)}, u32[]{:S(2)}, u32[]{:S(2)}) collective-permute-start(bf16[64,4096]{1,0:T(8,128)(2,1)S(1)} %bitcast.27), channel_id=1, source_target_pairs={{1,0},{2,1},{3,2},{6,7},{5,6},{4,5},{9,8},{10,9},{11,10},{14,15},{... | collective-permute-start | bytes 1572872 | tf_op jit(solution)/shard_map/ppermute | solution.py:407
  9.3 4.3 %collective-permute-start.5 = (bf16[64,512]{1,0:T(8,128)(2,1)S(1)}, bf16[64,512]{1,0:T(8,128)(2,1)S(1)}, u32[]{:S(2)}, u32[]{:S(2)}) collective-permute-start(bf16[64,512]{1,0:T(8,128)(2,1)S(1)} %slice_select_fusion), channel_id=1, source_target_pairs={{0,16},{16,0},{1,17},{17,1},{2,18},{18,2},{3,19},{19,3},{4,20},{20... | collective-permute-start | bytes 196616 | tf_op jit(solution)/shard_map/ppermute | solution.py:382
  11.8 0.7 copy-start.1
  12.6 6.2 %collective-permute-start = (bf16[10,64,128]{2,1,0:T(8,128)(2,1)S(1)}, bf16[10,64,128]{2,1,0:T(8,128)(2,1)S(1)}, u32[]{:S(2)}, u32[]{:S(2)}) collective-permute-start(bf16[10,64,128]{2,1,0:T(8,128)(2,1)S(1)} %get-tuple-element.59), channel_id=1, source_target_pairs={{0,16},{16,0},{1,17},{17,1},{2,18},{18,2},{3,19},{19,3},{4,20},{20... | collective-permute-start | bytes 491528 | tf_op jit(solution)/shard_map/ppermute | solution.py:367
  13.7 25.0 %collective-permute-start.6 = (bf16[64,5120]{1,0:T(8,128)(2,1)S(1)}, bf16[64,5120]{1,0:T(8,128)(2,1)S(1)}, u32[]{:S(2)}, u32[]{:S(2)}) collective-permute-start(bf16[64,5120]{1,0:T(8,128)(2,1)S(1)} %feat_rows.1.refs_3_), channel_id=1, source_target_pairs={{0,1},{3,2},{4,5},{7,6},{8,9},{11,10},{12,13},{15,14},{16,17},{19,... | collective-permute-start | bytes 1966088 | tf_op jit(solution)/shard_map/ppermute | solution.py:447
  18.7 0.7 copy-start.4
  19.4 19.2 %collective-permute-start.3 = (bf16[64,4096]{1,0:T(8,128)(2,1)}, bf16[64,4096]{1,0:T(8,128)(2,1)S(1)}, u32[]{:S(2)}, u32[]{:S(2)}) collective-permute-start(bf16[64,4096]{1,0:T(8,128)(2,1)} %collective-permute-done.1.refs_1_.first), channel_id=1, source_target_pairs={{1,2},{2,3},{6,5},{5,4},{9,10},{10,11},{14,13},{13,12},{17,18},{18... | collective-permute-start | bytes 1572872 | tf_op jit(solution)/shard_map/ppermute | solution.py:407
  20.1 18.6 %collective-permute-start.4 = (bf16[64,4096]{1,0:T(8,128)(2,1)}, bf16[64,4096]{1,0:T(8,128)(2,1)}, u32[]{:S(2)}, u32[]{:S(2)}) collective-permute-start(bf16[64,4096]{1,0:T(8,128)(2,1)} %collective-permute-done.2.refs_2_.second), channel_id=1, source_target_pairs={{1,0},{2,1},{6,7},{5,6},{9,8},{10,9},{14,15},{13,14},{17,16},{18,1... | collective-permute-start | bytes 1572872 | tf_op jit(solution)/shard_map/ppermute | solution.py:407
  21.5 1.0 %copy-start.2 = (f32[10,64,128]{2,1,0:T(8,128)S(1)}, f32[10,64,128]{2,1,0:T(8,128)}, u32[]{:S(2)}) copy-start(f32[10,64,128]{2,1,0:T(8,128)} %copy-done.1) | copy-start | bytes 983044
  22.5 0.9 %copy-start.5 = (bf16[10,64,128]{2,1,0:T(8,128)(2,1)S(1)}, bf16[10,64,128]{2,1,0:T(8,128)(2,1)}, u32[]{:S(2)}) copy-start(bf16[10,64,128]{2,1,0:T(8,128)(2,1)} %copy-done.4) | copy-start | bytes 491524
  28.8 23.5 %collective-permute-start.7 = (bf16[128,576]{1,0:T(8,128)(2,1)S(1)}, bf16[128,576]{1,0:T(8,128)(2,1)S(1)}, u32[]{:S(2)}, u32[]{:S(2)}) collective-permute-start(bf16[128,576]{1,0:T(8,128)(2,1)S(1)} %get-tuple-element.73), channel_id=1, source_target_pairs={{1,0},{2,1},{3,2},{6,7},{5,6},{4,5},{9,8},{10,9},{11,10},{14,15},{... | collective-permute-start | bytes 442376 | tf_op jit(solution)/shard_map/ppermute | solution.py:407
  30.1 22.2 %collective-permute-start.8 = (bf16[128,576]{1,0:T(8,128)(2,1)S(1)}, bf16[128,576]{1,0:T(8,128)(2,1)S(1)}, u32[]{:S(2)}, u32[]{:S(2)}) collective-permute-start(bf16[128,576]{1,0:T(8,128)(2,1)S(1)} %get-tuple-element.74), channel_id=1, source_target_pairs={{0,1},{1,2},{2,3},{7,6},{6,5},{5,4},{8,9},{9,10},{10,11},{15,14},{... | collective-permute-start | bytes 442376 | tf_op jit(solution)/shard_map/ppermute | solution.py:407
  42.4 14.7 %collective-permute-start.9 = (bf16[128,576]{1,0:T(8,128)(2,1)S(1)}, bf16[128,576]{1,0:T(8,128)(2,1)S(1)}, u32[]{:S(2)}, u32[]{:S(2)}) collective-permute-start(bf16[128,576]{1,0:T(8,128)(2,1)S(1)} %get-tuple-element.79), channel_id=1, source_target_pairs={{0,2},{1,3},{2,0},{3,1},{7,5},{6,4},{5,7},{4,6},{8,10},{9,11},{10,... | collective-permute-start | bytes 442376 | tf_op jit(solution)/shard_map/ppermute | solution.py:407
  49.8 7.3 %collective-permute-start.10 = (bf16[64,576]{1,0:T(8,128)(2,1)S(1)}, bf16[64,576]{1,0:T(8,128)(2,1)S(1)}, u32[]{:S(2)}, u32[]{:S(2)}) collective-permute-start(bf16[64,576]{1,0:T(8,128)(2,1)S(1)} %end_grad.1), channel_id=1, source_target_pairs={{1,3},{2,0},{5,7},{6,4},{9,11},{10,8},{13,15},{14,12},{17,19},{18,... | collective-permute-start | bytes 221192 | tf_op jit(solution)/shard_map/ppermute | solution.py:503
  51.1 16.8 %collective-permute-start.16 = (bf16[64,4096]{1,0:T(8,128)(2,1)S(1)}, bf16[64,4096]{1,0:T(8,128)(2,1)S(1)}, u32[]{:S(2)}, u32[]{:S(2)}) collective-permute-start(bf16[64,4096]{1,0:T(8,128)(2,1)S(1)} %get-tuple-element.90.end_block), channel_id=1, source_target_pairs={{1,0},{2,3},{5,4},{6,7},{9,8},{10,11},{13,12},{14,15},{17,16},{18,... | collective-permute-start | bytes 1572872 | tf_op jit(solution)/shard_map/ppermute | solution.py:505
  58.2 5.4 %collective-permute-start.11 = (bf16[10,64,128]{2,1,0:T(8,128)(2,1)S(1)}, bf16[10,64,128]{2,1,0:T(8,128)(2,1)S(1)}, u32[]{:S(2)}, u32[]{:S(2)}) collective-permute-start(bf16[10,64,128]{2,1,0:T(8,128)(2,1)S(1)} %get-tuple-element.87), channel_id=1, source_target_pairs={{0,16},{16,0},{1,17},{17,1},{2,18},{18,2},{3,19},{19,3},{4,20},{20... | collective-permute-start | bytes 491528 | tf_op jit(solution)/shard_map/ppermute | solution.py:525
  59.7 8.1 %collective-permute-start.15 = (bf16[64,576]{1,0:T(8,128)(2,1)S(1)}, bf16[64,576]{1,0:T(8,128)(2,1)S(1)}, u32[]{:S(2)}, u32[]{:S(2)}) collective-permute-start(bf16[64,576]{1,0:T(8,128)(2,1)S(1)} %get-tuple-element.89), channel_id=1, source_target_pairs={{0,3},{3,0},{4,7},{7,4},{8,11},{11,8},{12,15},{15,12},{16,19},{19,... | collective-permute-start | bytes 221192 | tf_op jit(solution)/shard_map/ppermute | solution.py:523
  63.8 9.3 %collective-permute-start.12 = (bf16[11,64,128]{2,1,0:T(8,128)(2,1)S(1)}, bf16[11,64,128]{2,1,0:T(8,128)(2,1)S(1)}, u32[]{:S(2)}, u32[]{:S(2)}) collective-permute-start(bf16[11,64,128]{2,1,0:T(8,128)(2,1)S(1)} %row_sum.1.refs_0_), channel_id=1, source_target_pairs={{8,0},{12,4},{0,8},{4,12},{9,1},{13,5},{1,9},{5,13},{10,2},{14,6},... | collective-permute-start | bytes 540680 | tf_op jit(solution)/shard_map/ppermute | solution.py:360
  65.3 7.7 %collective-permute-start.13 = (bf16[11,64,128]{2,1,0:T(8,128)(2,1)S(1)}, bf16[11,64,128]{2,1,0:T(8,128)(2,1)S(1)}, u32[]{:S(2)}, u32[]{:S(2)}) collective-permute-start(bf16[11,64,128]{2,1,0:T(8,128)(2,1)S(1)} %row_sum.1.refs_0_), channel_id=1, source_target_pairs={{12,0},{8,4},{4,8},{0,12},{13,1},{9,5},{5,9},{1,13},{14,2},{10,6},... | collective-permute-start | bytes 540680 | tf_op jit(solution)/shard_map/ppermute | solution.py:360
  65.3 7.7 %collective-permute-start.14 = (bf16[11,64,128]{2,1,0:T(8,128)(2,1)S(1)}, bf16[11,64,128]{2,1,0:T(8,128)(2,1)S(1)}, u32[]{:S(2)}, u32[]{:S(2)}) collective-permute-start(bf16[11,64,128]{2,1,0:T(8,128)(2,1)S(1)} %row_sum.1.refs_0_), channel_id=1, source_target_pairs={{4,0},{0,4},{12,8},{8,12},{5,1},{1,5},{13,9},{9,13},{6,2},{2,6},{1... | collective-permute-start | bytes 540680 | tf_op jit(solution)/shard_map/ppermute | solution.py:360
  73.1 9.2 %collective-permute-start.20 = (f32[64,512]{1,0:T(8,128)S(1)}, f32[64,512]{1,0:T(8,128)S(1)}, u32[]{:S(2)}, u32[]{:S(2)}) collective-permute-start(f32[64,512]{1,0:T(8,128)S(1)} %get-tuple-element.102), channel_id=1, source_target_pairs={{0,16},{16,0},{1,17},{17,1},{2,18},{18,2},{3,19},{19,3},{4,20},{20... | collective-permute-start | bytes 393224 | tf_op jit(solution)/shard_map/ppermute | solution.py:382
  77.2 6.5 %collective-permute-start.17 = (f32[4,128]{1,0:T(4,128)S(1)}, f32[4,128]{1,0:T(4,128)S(1)}, u32[]{:S(2)}, u32[]{:S(2)}) collective-permute-start(f32[4,128]{1,0:T(4,128)S(1)} %get-tuple-element.106.refs_0_), channel_id=1, source_target_pairs={{0,1},{1,0},{2,3},{3,2},{4,5},{5,4},{6,7},{7,6},{8,9},{9,8},{10,11... | collective-permute-start | bytes 6152 | tf_op jit(solution)/shard_map/ppermute | solution.py:375
  77.3 6.4 %collective-permute-start.18 = (f32[4,128]{1,0:T(4,128)S(1)}, f32[4,128]{1,0:T(4,128)S(1)}, u32[]{:S(2)}, u32[]{:S(2)}) collective-permute-start(f32[4,128]{1,0:T(4,128)S(1)} %get-tuple-element.106.refs_0_), channel_id=1, source_target_pairs={{0,2},{1,3},{2,0},{3,1},{4,6},{5,7},{6,4},{7,5},{8,10},{9,11},{10,... | collective-permute-start | bytes 6152 | tf_op jit(solution)/shard_map/ppermute | solution.py:375
  79.8 5.4 %collective-permute-start.19 = (f32[4,128]{1,0:T(4,128)S(1)}, f32[4,128]{1,0:T(4,128)S(1)}, u32[]{:S(2)}, u32[]{:S(2)}) collective-permute-start(f32[4,128]{1,0:T(4,128)S(1)} %get-tuple-element.106.refs_0_), channel_id=1, source_target_pairs={{0,3},{1,2},{2,1},{3,0},{4,7},{5,6},{6,5},{7,4},{8,11},{9,10},{10,... | collective-permute-start | bytes 6152 | tf_op jit(solution)/shard_map/ppermute | solution.py:375

commit v18 on v16

--- a/solution.py
+++ b/solution.py
@@ -11,7 +11,7 @@
 TAPS = 9
 F32 = jnp.float32
 BF16 = jnp.bfloat16
-VMEM_LIMIT = 16 * 2**20
+VMEM_LIMIT = 10 * 2**20
 COLLECT_FLOPS = 6 * 10**9
 INPUT_FLOPS = 2 * 10**9
 

time: 86.3 us -> 86.3 us (level)
  no operation moved by 1% of the time
where the time goes in v18:
time: 86.3 us; the launch traced here: 85.8 us
  starting transfers between devices  43.8 us (51%)
  Pallas kernels  23.6 us (27%)
  waiting for transfers between devices  12.6 us (15%)
  local copies, waits for them, and re-layouts  3.49 us (4%)
  other arithmetic  1.28 us (1%)
  between operations  0.99 us (1%)
    pallas_call x11, Pallas kernels, call(): pl.pallas_call(kernel, out_shape=outs, in_specs=sspec(scalars) + vspec(le...  23.6 us
    ppermute x7, starting transfers between devices, along(): return lax.ppermute(x, ('samples', 'chan'), whole)  22.2 us
    ppermute x1, starting transfers between devices, on_device(): feat_end = lax.ppermute(feat, 'chan', [(0, 1), (size - 1, size - 2)])  5.29 us
    ppermute x1, waiting for transfers between devices, on_device(): from_end = lax.ppermute(grad_end, 'chan', [(1, size - 1), (size - 2, 0)])  4.72 us
    ppermute x3, starting transfers between devices, terms_of_sum(): lax.ppermute(x, axis, [(i, i ^ step) for i in range(size)])  4.44 us
    unnamed x19, local copies, waits for them, and re-layouts  3.13 us
    ppermute x2, starting transfers between devices, from_sides(): got = lax.ppermute(edge, axis, [(0, 1), (1, 0)])  2.82 us
    ppermute x1, starting transfers between devices, on_device(): end_mod = lax.ppermute(mods[size], 'chan', [(0, size - 1), (size - 1, 0)])  2.8 us
  transfers between devices with their start and end apart: 21, of which 6 were waited for; matrix products, arithmetic and copies ran while one was open for 3% of the time, Pallas kernels for 26%

profile of v18, /device:TPU:0, one launch (start us, length us, event | category | flops | bytes accessed | tf_op | source)
XLA Modules:
  0.0 85.8 jit_solution(18028199518191788614)
XLA Ops:
  0.7 1.3 %copy.13 = bf16[8,8,8,512]{3,1,2,0:T(8,128)(2,1)S(1)} copy(bf16[8,8,8,512]{3,2,1,0:T(8,128)(2,1)} %bitcast.32) | data formatting | bytes 1048576
  2.0 5.7 %collective-permute-start.1 = (bf16[64,4096]{1,0:T(8,128)(2,1)S(1)}, bf16[64,4096]{1,0:T(8,128)(2,1)}, u32[]{:S(2)}, u32[]{:S(2)}) collective-permute-start(bf16[64,4096]{1,0:T(8,128)(2,1)S(1)} %bitcast.26), channel_id=1, source_target_pairs={{0,1},{1,2},{2,3},{7,6},{6,5},{5,4},{8,9},{9,10},{10,11},{15,14},{... | collective-permute-start | bytes 1572872 | tf_op jit(solution)/shard_map/ppermute | solution.py:404
  7.8 1.3 %collective-permute-start.2 = (bf16[64,4096]{1,0:T(8,128)(2,1)S(1)}, bf16[64,4096]{1,0:T(8,128)(2,1)}, u32[]{:S(2)}, u32[]{:S(2)}) collective-permute-start(bf16[64,4096]{1,0:T(8,128)(2,1)S(1)} %bitcast.27), channel_id=1, source_target_pairs={{1,0},{2,1},{3,2},{6,7},{5,6},{4,5},{9,8},{10,9},{11,10},{14,15},{... | collective-permute-start | bytes 1572872 | tf_op jit(solution)/shard_map/ppermute | solution.py:404
  9.1 0.2 copy.14
  9.3 1.6 %collective-permute-start.5 = (bf16[64,512]{1,0:T(8,128)(2,1)S(1)}, bf16[64,512]{1,0:T(8,128)(2,1)S(1)}, u32[]{:S(2)}, u32[]{:S(2)}) collective-permute-start(bf16[64,512]{1,0:T(8,128)(2,1)S(1)} %slice_select_fusion), channel_id=1, source_target_pairs={{0,16},{16,0},{1,17},{17,1},{2,18},{18,2},{3,19},{19,3},{4,20},{20... | collective-permute-start | bytes 196616 | tf_op jit(solution)/shard_map/ppermute | solution.py:379
  10.8 0.0 copy-done.6
  10.9 0.0 copy-done.3
  10.9 1.0 %plain.1 = (f32[10,64,128]{2,1,0:T(8,128)S(1)}, f32[8,128]{1,0:T(8,128)S(1)}) custom-call(s32[1,4]{1,0:T(1,128)S(1)} %copy-done.5, f32[1,512]{1,0:T(1,128)S(1)} %copy-done.4, f32[1,128]{1,0:T(1,128)S(1)} %bitcast.30, f32[512,128]{1,0:T(8,128)S(1)} %copy-done.3, f32[4,9,64,128]{3,2,1,0:T(8,128)S(1)} %copy-done), custom_call_target="tpu_custom_call" | custom-call | flops 1000000 | bytes 1776144 | tf_op jit(solution)/shard_map/plain/pallas_call | solution.py:332
  11.8 0.0 copy-start.1
  11.8 0.6 collective-permute-start
  12.4 1.2 %collective-permute-done.5 = bf16[64,512]{1,0:T(8,128)(2,1)S(1)} collective-permute-done((bf16[64,512]{1,0:T(8,128)(2,1)S(1)}, bf16[64,512]{1,0:T(8,128)(2,1)S(1)}, u32[]{:S(2)}, u32[]{:S(2)}) %collective-permute-start.5) | collective-permute-done | bytes 65568 | tf_op jit(solution)/shard_map/ppermute | solution.py:379
  13.7 5.3 %collective-permute-start.6 = (bf16[64,5120]{1,0:T(8,128)(2,1)S(1)}, bf16[64,5120]{1,0:T(8,128)(2,1)S(1)}, u32[]{:S(2)}, u32[]{:S(2)}) collective-permute-start(bf16[64,5120]{1,0:T(8,128)(2,1)S(1)} %feat_rows.1.refs_3_), channel_id=1, source_target_pairs={{0,1},{3,2},{4,5},{7,6},{8,9},{11,10},{12,13},{15,14},{16,17},{19,... | collective-permute-start | bytes 1966088 | tf_op jit(solution)/shard_map/ppermute | solution.py:444
  19.0 2.7 %collective-permute-done.refs_1_ = f32[10,64,128]{2,1,0:T(8,128)} collective-permute-done((f32[10,64,128]{2,1,0:T(8,128)S(1)}, f32[10,64,128]{2,1,0:T(8,128)}, u32[]{:S(2)}, u32[]{:S(2)}) %collective-permute-start) | collective-permute-done | bytes 327712 | tf_op jit(solution)/shard_map/ppermute | solution.py:364
  21.7 0.0 collective-permute-done.1.refs_1_.first
  21.7 0.0 collective-permute-done.2.refs_2_.second
  21.7 0.7 collective-permute-start.3
  22.4 1.3 %collective-permute-start.4 = (bf16[64,4096]{1,0:T(8,128)(2,1)}, bf16[64,4096]{1,0:T(8,128)(2,1)}, u32[]{:S(2)}, u32[]{:S(2)}) collective-permute-start(bf16[64,4096]{1,0:T(8,128)(2,1)} %collective-permute-done.2.refs_2_.second), channel_id=1, source_target_pairs={{1,0},{2,1},{6,7},{5,6},{9,8},{10,9},{14,15},{13,14},{17,16},{18,1... | collective-permute-start | bytes 1572872 | tf_op jit(solution)/shard_map/ppermute | solution.py:404
  23.7 0.1 pad_add_fusion.place
  23.8 1.0 %copy-done.2 = f32[10,64,128]{2,1,0:T(8,128)S(1)} copy-done((f32[10,64,128]{2,1,0:T(8,128)S(1)}, f32[10,64,128]{2,1,0:T(8,128)}, u32[]{:S(2)}) %copy-start.2) | copy-done | bytes 327704
  24.8 1.3 %mod_blocks.1 = (bf16[9,64,256]{2,1,0:T(8,128)(2,1)S(1)}, f32[64,128]{1,0:T(8,128)S(1)}, bf16[64,576]{1,0:T(8,128)(2,1)S(1)}, bf16[64,576]{1,0:T(8,128)(2,1)S(1)...) custom-call(s32[4]{0:T(128)S(1)} %pad_add_fusion.place, ...), custom_call_target="tpu_custom_call" | custom-call | flops 1000000 | bytes 1351696 | tf_op jit(solution)/shard_map/mod_blocks/pallas_call | solution.py:332
  26.0 4.5 %near_grad.1 = (bf16[64,576]{1,0:T(8,128)(2,1)S(1)}, bf16[128,576]{1,0:T(8,128)(2,1)S(1)}, bf16[128,576]{1,0:T(8,128)(2,1)S(1)}, bf16[192,5120]{1,0:T(8,128)(2,1)S(1)}) custom-call(bf16[64,4096]{1,0:T(8,128)(2,1)S(1)} %bitcast.28, bf16[64,4096]{1,0:T(8,128)(2,1)} %collective-permute-done.1.refs_1_.first, ...), custom_call_target="tpu_custom_call" | custom-call | flops 905969664 | bytes 4710400 | tf_op jit(solution)/shard_map/near_grad/pallas_call | solution.py:332
  30.6 1.3 %collective-permute-start.7 = (bf16[128,576]{1,0:T(8,128)(2,1)S(1)}, bf16[128,576]{1,0:T(8,128)(2,1)S(1)}, u32[]{:S(2)}, u32[]{:S(2)}) collective-permute-start(bf16[128,576]{1,0:T(8,128)(2,1)S(1)} %get-tuple-element.71), channel_id=1, source_target_pairs={{1,0},{2,1},{3,2},{6,7},{5,6},{4,5},{9,8},{10,9},{11,10},{14,15},{... | collective-permute-start | bytes 442376 | tf_op jit(solution)/shard_map/ppermute | solution.py:404
  31.9 7.6 %collective-permute-start.8 = (bf16[128,576]{1,0:T(8,128)(2,1)S(1)}, bf16[128,576]{1,0:T(8,128)(2,1)S(1)}, u32[]{:S(2)}, u32[]{:S(2)}) collective-permute-start(bf16[128,576]{1,0:T(8,128)(2,1)S(1)} %get-tuple-element.72), channel_id=1, source_target_pairs={{0,1},{1,2},{2,3},{7,6},{6,5},{5,4},{8,9},{9,10},{10,11},{15,14},{... | collective-permute-start | bytes 442376 | tf_op jit(solution)/shard_map/ppermute | solution.py:404
  39.4 0.0 collective-permute-done.6.feat
  39.5 0.0 collective-permute-done.3.refs_0_
  39.5 0.0 collective-permute-done.4.refs_1_
  39.5 3.7 %middle_grad.1 = (bf16[128,576]{1,0:T(8,128)(2,1)S(1)}, bf16[64,4096]{1,0:T(8,128)(2,1)S(1)}, bf16[64,4096]{1,0:T(8,128)(2,1)S(1)}) custom-call(bf16[64,4096]{1,0:T(8,128)(2,1)S(1)} %collective-permute-done.3.refs_0_, bf16[64,4096]{1,0:T(8,128)(2,1)} %collective-permute-done.4.refs_1_, bf16[192,5120]{1,0:T(8,128)(2,1)S(1)} %get-tuple-element.75.refs_2_, ...), custom_call_target="tpu_custom_call" | custom-call | flops 301989888 | bytes 4284416 | tf_op jit(solution)/shard_map/middle_grad/pallas_call | solution.py:332
  43.2 4.3 %collective-permute-start.9 = (bf16[128,576]{1,0:T(8,128)(2,1)S(1)}, bf16[128,576]{1,0:T(8,128)(2,1)S(1)}, u32[]{:S(2)}, u32[]{:S(2)}) collective-permute-start(bf16[128,576]{1,0:T(8,128)(2,1)S(1)} %get-tuple-element.77), channel_id=1, source_target_pairs={{0,2},{1,3},{2,0},{3,1},{7,5},{6,4},{5,7},{4,6},{8,10},{9,11},{10,... | collective-permute-start | bytes 442376 | tf_op jit(solution)/shard_map/ppermute | solution.py:404
  47.5 3.0 %end_grad.1 = bf16[64,576]{1,0:T(8,128)(2,1)S(1)} custom-call(bf16[64,4096]{1,0:T(8,128)(2,1)S(1)} %get-tuple-element.88.end_block, bf16[64,5120]{1,0:T(8,128)(2,1)S(1)} %collective-permute-done.6.feat), custom_call_target="tpu_custom_call" | custom-call | flops 301989888 | bytes 1253376 | tf_op jit(solution)/shard_map/end_grad/pallas_call | solution.py:332
  50.6 1.3 %collective-permute-start.10 = (bf16[64,576]{1,0:T(8,128)(2,1)S(1)}, bf16[64,576]{1,0:T(8,128)(2,1)S(1)}, u32[]{:S(2)}, u32[]{:S(2)}) collective-permute-start(bf16[64,576]{1,0:T(8,128)(2,1)S(1)} %end_grad.1), channel_id=1, source_target_pairs={{1,3},{2,0},{5,7},{6,4},{9,11},{10,8},{13,15},{14,12},{17,19},{18,... | collective-permute-start | bytes 221192 | tf_op jit(solution)/shard_map/ppermute | solution.py:500
  51.9 1.3 %collective-permute-start.16 = (bf16[64,4096]{1,0:T(8,128)(2,1)S(1)}, bf16[64,4096]{1,0:T(8,128)(2,1)S(1)}, u32[]{:S(2)}, u32[]{:S(2)}) collective-permute-start(bf16[64,4096]{1,0:T(8,128)(2,1)S(1)} %get-tuple-element.88.end_block), channel_id=1, source_target_pairs={{1,0},{2,3},{5,4},{6,7},{9,8},{10,11},{13,12},{14,15},{17,16},{18,... | collective-permute-start | bytes 1572872 | tf_op jit(solution)/shard_map/ppermute | solution.py:502
  53.2 0.0 collective-permute-done.7.ahead
  53.2 0.0 collective-permute-done.8.behind
  53.2 4.7 %collective-permute-done.10.end = bf16[64,576]{1,0:T(8,128)(2,1)S(1)} collective-permute-done((bf16[64,576]{1,0:T(8,128)(2,1)S(1)}, bf16[64,576]{1,0:T(8,128)(2,1)S(1)}, u32[]{:S(2)}, u32[]{:S(2)}) %collective-permute-start.10) | collective-permute-done | bytes 73760 | tf_op jit(solution)/shard_map/ppermute | solution.py:500
  57.9 0.0 collective-permute-done.9.others
  57.9 1.1 %collect.1 = (bf16[10,64,128]{2,1,0:T(8,128)(2,1)S(1)}, bf16[10,64,128]{2,1,0:T(8,128)(2,1)S(1)}) custom-call(s32[4]{0:T(128)S(1)} %pad_add_fusion.place, f32[64,128]{1,0:T(8,128)S(1)} %get-tuple-element.58.scale, bf16[9,64,256]{2,1,0:T(8,128)(2,1)S(1)} %get-tuple-element.69.whole_mod, bf16[64,576]{1,0:T(8,128)(2,1)S(1)} %get-tuple-element.70.own, ...), custom_call_target="tpu_custom_call" | custom-call | flops 6000000000 | bytes 1245200 | tf_op jit(solution)/shard_map/collect/pallas_call | solution.py:332
  59.0 0.9 %collective-permute-start.11 = (bf16[10,64,128]{2,1,0:T(8,128)(2,1)S(1)}, bf16[10,64,128]{2,1,0:T(8,128)(2,1)S(1)}, u32[]{:S(2)}, u32[]{:S(2)}) collective-permute-start(bf16[10,64,128]{2,1,0:T(8,128)(2,1)S(1)} %get-tuple-element.85), channel_id=1, source_target_pairs={{0,16},{16,0},{1,17},{17,1},{2,18},{18,2},{3,19},{19,3},{4,20},{20... | collective-permute-start | bytes 491528 | tf_op jit(solution)/shard_map/ppermute | solution.py:522
  59.9 2.8 %collective-permute-start.15 = (bf16[64,576]{1,0:T(8,128)(2,1)S(1)}, bf16[64,576]{1,0:T(8,128)(2,1)S(1)}, u32[]{:S(2)}, u32[]{:S(2)}) collective-permute-start(bf16[64,576]{1,0:T(8,128)(2,1)S(1)} %get-tuple-element.87), channel_id=1, source_target_pairs={{0,3},{3,0},{4,7},{7,4},{8,11},{11,8},{12,15},{15,12},{16,19},{19,... | collective-permute-start | bytes 221192 | tf_op jit(solution)/shard_map/ppermute | solution.py:520
  62.7 1.7 %collective-permute-done.11.refs_1_ = bf16[10,64,128]{2,1,0:T(8,128)(2,1)S(1)} collective-permute-done((bf16[10,64,128]{2,1,0:T(8,128)(2,1)S(1)}, bf16[10,64,128]{2,1,0:T(8,128)(2,1)S(1)}, u32[]{:S(2)}, u32[]{:S(2)}) %collective-permute-start.11) | collective-permute-done | bytes 163872 | tf_op jit(solution)/shard_map/ppermute | solution.py:522
  64.3 0.2 row_sum.1.refs_0_
  64.6 1.6 %collective-permute-start.12 = (bf16[11,64,128]{2,1,0:T(8,128)(2,1)S(1)}, bf16[11,64,128]{2,1,0:T(8,128)(2,1)S(1)}, u32[]{:S(2)}, u32[]{:S(2)}) collective-permute-start(bf16[11,64,128]{2,1,0:T(8,128)(2,1)S(1)} %row_sum.1.refs_0_), channel_id=1, source_target_pairs={{8,0},{12,4},{0,8},{4,12},{9,1},{13,5},{1,9},{5,13},{10,2},{14,6},... | collective-permute-start | bytes 540680 | tf_op jit(solution)/shard_map/ppermute | solution.py:357
  66.1 0.0 collective-permute-start.13
  66.1 0.6 collective-permute-start.14
  66.8 1.2 %collective-permute-done.15.end_mod = bf16[64,576]{1,0:T(8,128)(2,1)S(1)} collective-permute-done((bf16[64,576]{1,0:T(8,128)(2,1)S(1)}, bf16[64,576]{1,0:T(8,128)(2,1)S(1)}, u32[]{:S(2)}, u32[]{:S(2)}) %collective-permute-start.15) | collective-permute-done | bytes 73760 | tf_op jit(solution)/shard_map/ppermute | solution.py:520
  68.0 0.0 collective-permute-done.16.far
  68.0 5.2 %input_grad.1 = (f32[64,4096]{1,0:T(8,128)S(1)}, f32[64,512]{1,0:T(8,128)}, f32[64,512]{1,0:T(8,128)S(1)}) custom-call(s32[4]{0:T(128)S(1)} %pad_add_fusion.place, bf16[64,4096]{1,0:T(8,128)(2,1)S(1)} %bitcast.29, bf16[64,4096]{1,0:T(8,128)(2,1)} %collective-permute-done.1.refs_1_.first, bf16[64,4096]{1,0:T(8,128)(2,1)} %collective-permute-done.2.refs_2_.second, ...), custom_call_target="tpu_custom_call" | custom-call | flops 2000000000 | bytes 4522000 | tf_op jit(solution)/shard_map/input_grad/pallas_call | solution.py:332
  73.2 0.0 collective-permute-done.12.refs_1_
  73.2 0.0 collective-permute-done.13.refs_2_
  73.2 0.0 collective-permute-done.14.refs_3_
  73.2 1.3 %collective-permute-start.20 = (f32[64,512]{1,0:T(8,128)S(1)}, f32[64,512]{1,0:T(8,128)S(1)}, u32[]{:S(2)}, u32[]{:S(2)}) collective-permute-start(f32[64,512]{1,0:T(8,128)S(1)} %get-tuple-element.100), channel_id=1, source_target_pairs={{0,16},{16,0},{1,17},{17,1},{2,18},{18,2},{3,19},{19,3},{4,20},{20... | collective-permute-start | bytes 393224 | tf_op jit(solution)/shard_map/ppermute | solution.py:379
  74.5 0.1 pad.1.clone
  74.5 2.7 %bank_grad.1 = (f32[4,9,64,128]{3,2,1,0:T(8,128)}, f32[4,128]{1,0:T(4,128)S(1)}, f32[4,512]{1,0:T(4,128)S(1)}) custom-call(s32[4]{0:T(128)S(1)} %pad_add_fusion.place, f32[4,9,64,128]{3,2,1,0:T(8,128)S(1)} %copy-done, bf16[11,64,128]{2,1,0:T(8,128)(2,1)S(1)} %row_sum.1.refs_0_, bf16[11,64,128]{2,1,0:T(8,128)(2,1)S(1)} %collective-permute-done.12.refs_1_, ...), custom_call_target="tpu_custom_call" | custom-call | flops 1000000 | bytes 3090448 | tf_op jit(solution)/shard_map/bank_grad/pallas_call | solution.py:332
  77.2 0.1 collective-permute-start.17
  77.3 2.2 %collective-permute-start.18 = (f32[4,128]{1,0:T(4,128)S(1)}, f32[4,128]{1,0:T(4,128)S(1)}, u32[]{:S(2)}, u32[]{:S(2)}) collective-permute-start(f32[4,128]{1,0:T(4,128)S(1)} %get-tuple-element.104.refs_0_), channel_id=1, source_target_pairs={{0,2},{1,3},{2,0},{3,1},{4,6},{5,7},{6,4},{7,5},{8,10},{9,11},{10,... | collective-permute-start | bytes 6152 | tf_op jit(solution)/shard_map/ppermute | solution.py:372
  79.5 2.2 %collective-permute-start.19 = (f32[4,128]{1,0:T(4,128)S(1)}, f32[4,128]{1,0:T(4,128)S(1)}, u32[]{:S(2)}, u32[]{:S(2)}) collective-permute-start(f32[4,128]{1,0:T(4,128)S(1)} %get-tuple-element.104.refs_0_), channel_id=1, source_target_pairs={{0,3},{1,2},{2,1},{3,0},{4,7},{5,6},{6,5},{7,4},{8,11},{9,10},{10,... | collective-permute-start | bytes 6152 | tf_op jit(solution)/shard_map/ppermute | solution.py:372
  81.7 0.6 copy.15
  82.3 0.0 collective-permute-done.20
  82.3 0.1 copy.12
  82.5 0.1 copy.11
  82.6 1.2 %fusion = bf16[1,64,8,512]{3,2,1,0:T(8,128)(2,1)} fusion(f32[1,64,1,512]{3,2,1,0:T(1,128)S(1)} %copy.12, f32[1,64,1,512]{3,2,1,0:T(1,128)S(1)} %copy.11, f32[8]{0:T(128)S(1)} %pad.1.clone, f32[1,64,8,512]{3,2,1,0:T(8,128)S(1)} %bitcast.31), kind=kLoop, calls=%fused_computation.1 | loop fusion | flops 1048576 | bytes 1835040 | tf_op jit(solution)/shard_map/convert_element_type | solution.py:570
  83.8 0.0 collective-permute-done.17.refs_1_
  83.8 0.0 collective-permute-done.18.refs_2_
  83.8 1.1 %collective-permute-done.19.refs_3_ = f32[4,128]{1,0:T(4,128)S(1)} collective-permute-done((f32[4,128]{1,0:T(4,128)S(1)}, f32[4,128]{1,0:T(4,128)S(1)}, u32[]{:S(2)}, u32[]{:S(2)}) %collective-permute-start.19) | collective-permute-done | bytes 2080 | tf_op jit(solution)/shard_map/ppermute | solution.py:372
  84.9 0.9 %affine.1 = (f32[512,128]{1,0:T(8,128)}, f32[1,128]{1,0:T(1,128)}) custom-call(f32[4,512]{1,0:T(4,128)S(1)} %get-tuple-element.103.latents, f32[4,128]{1,0:T(4,128)S(1)} %get-tuple-element.104.refs_0_, f32[4,128]{1,0:T(4,128)S(1)} %collective-permute-done.17.refs_1_, f32[4,128]{1,0:T(4,128)S(1)} %collective-permute-done.18.refs_2_, ...), custom_call_target="tpu_custom_call" | custom-call | flops 1000000 | bytes 279040 | tf_op jit(solution)/shard_map/affine/pallas_call | solution.py:332
  (17 shorter events, 0.1 us)
Async XLA Ops:
  0.6 8.4 %copy-start.7 = (bf16[1,64,8,512]{3,2,1,0:T(8,128)(2,1)S(1)}, bf16[1,64,8,512]{3,2,1,0:T(8,128)(2,1)}, u32[]{:S(2)}) copy-start(bf16[1,64,8,512]{3,2,1,0:T(8,128)(2,1)} %param.7) | copy-start | bytes 1572868
  0.6 10.2 %copy-start = (f32[4,9,64,128]{3,2,1,0:T(8,128)S(1)}, f32[4,9,64,128]{3,2,1,0:T(8,128)}, u32[]{:S(2)}) copy-start(f32[4,9,64,128]{3,2,1,0:T(8,128)} %bank.1) | copy-start | bytes 3538948
  0.7 10.2 %copy-start.5 = (s32[1,4]{1,0:T(1,128)S(1)}, s32[1,4]{1,0:T(1,128)}, u32[]{:S(2)}) copy-start(s32[1,4]{1,0:T(1,128)} %refs_0_.1) | copy-start | bytes 52
  0.7 10.2 %copy-start.4 = (f32[1,512]{1,0:T(1,128)S(1)}, f32[1,512]{1,0:T(1,128)}, u32[]{:S(2)}) copy-start(f32[1,512]{1,0:T(1,128)} %refs_1_.1) | copy-start | bytes 6148
  0.7 10.2 %copy-start.6 = (f32[128]{0:T(128)S(1)}, f32[128]{0:T(128)}, u32[]{:S(2)}) copy-start(f32[128]{0:T(128)} %param.13) | copy-start | bytes 1540
  0.7 10.2 %copy-start.3 = (f32[512,128]{1,0:T(8,128)S(1)}, f32[512,128]{1,0:T(8,128)}, u32[]{:S(2)}) copy-start(f32[512,128]{1,0:T(8,128)} %refs_3_.1) | copy-start | bytes 786436
  2.0 19.7 %collective-permute-start.1 = (bf16[64,4096]{1,0:T(8,128)(2,1)S(1)}, bf16[64,4096]{1,0:T(8,128)(2,1)}, u32[]{:S(2)}, u32[]{:S(2)}) collective-permute-start(bf16[64,4096]{1,0:T(8,128)(2,1)S(1)} %bitcast.26), channel_id=1, source_target_pairs={{0,1},{1,2},{2,3},{7,6},{6,5},{5,4},{8,9},{9,10},{10,11},{15,14},{... | collective-permute-start | bytes 1572872 | tf_op jit(solution)/shard_map/ppermute | solution.py:404
  7.8 13.9 %collective-permute-start.2 = (bf16[64,4096]{1,0:T(8,128)(2,1)S(1)}, bf16[64,4096]{1,0:T(8,128)(2,1)}, u32[]{:S(2)}, u32[]{:S(2)}) collective-permute-start(bf16[64,4096]{1,0:T(8,128)(2,1)S(1)} %bitcast.27), channel_id=1, source_target_pairs={{1,0},{2,1},{3,2},{6,7},{5,6},{4,5},{9,8},{10,9},{11,10},{14,15},{... | collective-permute-start | bytes 1572872 | tf_op jit(solution)/shard_map/ppermute | solution.py:404
  9.3 4.3 %collective-permute-start.5 = (bf16[64,512]{1,0:T(8,128)(2,1)S(1)}, bf16[64,512]{1,0:T(8,128)(2,1)S(1)}, u32[]{:S(2)}, u32[]{:S(2)}) collective-permute-start(bf16[64,512]{1,0:T(8,128)(2,1)S(1)} %slice_select_fusion), channel_id=1, source_target_pairs={{0,16},{16,0},{1,17},{17,1},{2,18},{18,2},{3,19},{19,3},{4,20},{20... | collective-permute-start | bytes 196616 | tf_op jit(solution)/shard_map/ppermute | solution.py:379
  11.8 9.9 %copy-start.1 = (f32[10,64,128]{2,1,0:T(8,128)}, f32[10,64,128]{2,1,0:T(8,128)S(1)}, u32[]{:S(2)}) copy-start(f32[10,64,128]{2,1,0:T(8,128)S(1)} %get-tuple-element.57.refs_0_) | copy-start | bytes 983044
  11.8 9.8 %collective-permute-start = (f32[10,64,128]{2,1,0:T(8,128)S(1)}, f32[10,64,128]{2,1,0:T(8,128)}, u32[]{:S(2)}, u32[]{:S(2)}) collective-permute-start(f32[10,64,128]{2,1,0:T(8,128)S(1)} %get-tuple-element.57.refs_0_), channel_id=1, source_target_pairs={{0,16},{16,0},{1,17},{17,1},{2,18},{18,2},{3,19},{19,3},{4,20},{20... | collective-permute-start | bytes 983048 | tf_op jit(solution)/shard_map/ppermute | solution.py:364
  13.7 25.8 %collective-permute-start.6 = (bf16[64,5120]{1,0:T(8,128)(2,1)S(1)}, bf16[64,5120]{1,0:T(8,128)(2,1)S(1)}, u32[]{:S(2)}, u32[]{:S(2)}) collective-permute-start(bf16[64,5120]{1,0:T(8,128)(2,1)S(1)} %feat_rows.1.refs_3_), channel_id=1, source_target_pairs={{0,1},{3,2},{4,5},{7,6},{8,9},{11,10},{12,13},{15,14},{16,17},{19,... | collective-permute-start | bytes 1966088 | tf_op jit(solution)/shard_map/ppermute | solution.py:444
  21.7 17.8 %collective-permute-start.3 = (bf16[64,4096]{1,0:T(8,128)(2,1)}, bf16[64,4096]{1,0:T(8,128)(2,1)S(1)}, u32[]{:S(2)}, u32[]{:S(2)}) collective-permute-start(bf16[64,4096]{1,0:T(8,128)(2,1)} %collective-permute-done.1.refs_1_.first), channel_id=1, source_target_pairs={{1,2},{2,3},{6,5},{5,4},{9,10},{10,11},{14,13},{13,12},{17,18},{18... | collective-permute-start | bytes 1572872 | tf_op jit(solution)/shard_map/ppermute | solution.py:404
  22.4 17.1 %collective-permute-start.4 = (bf16[64,4096]{1,0:T(8,128)(2,1)}, bf16[64,4096]{1,0:T(8,128)(2,1)}, u32[]{:S(2)}, u32[]{:S(2)}) collective-permute-start(bf16[64,4096]{1,0:T(8,128)(2,1)} %collective-permute-done.2.refs_2_.second), channel_id=1, source_target_pairs={{1,0},{2,1},{6,7},{5,6},{9,8},{10,9},{14,15},{13,14},{17,16},{18,1... | collective-permute-start | bytes 1572872 | tf_op jit(solution)/shard_map/ppermute | solution.py:404
  23.8 1.0 %copy-start.2 = (f32[10,64,128]{2,1,0:T(8,128)S(1)}, f32[10,64,128]{2,1,0:T(8,128)}, u32[]{:S(2)}) copy-start(f32[10,64,128]{2,1,0:T(8,128)} %copy-done.1) | copy-start | bytes 983044
  30.6 22.6 %collective-permute-start.7 = (bf16[128,576]{1,0:T(8,128)(2,1)S(1)}, bf16[128,576]{1,0:T(8,128)(2,1)S(1)}, u32[]{:S(2)}, u32[]{:S(2)}) collective-permute-start(bf16[128,576]{1,0:T(8,128)(2,1)S(1)} %get-tuple-element.71), channel_id=1, source_target_pairs={{1,0},{2,1},{3,2},{6,7},{5,6},{4,5},{9,8},{10,9},{11,10},{14,15},{... | collective-permute-start | bytes 442376 | tf_op jit(solution)/shard_map/ppermute | solution.py:404
  31.9 21.3 %collective-permute-start.8 = (bf16[128,576]{1,0:T(8,128)(2,1)S(1)}, bf16[128,576]{1,0:T(8,128)(2,1)S(1)}, u32[]{:S(2)}, u32[]{:S(2)}) collective-permute-start(bf16[128,576]{1,0:T(8,128)(2,1)S(1)} %get-tuple-element.72), channel_id=1, source_target_pairs={{0,1},{1,2},{2,3},{7,6},{6,5},{5,4},{8,9},{9,10},{10,11},{15,14},{... | collective-permute-start | bytes 442376 | tf_op jit(solution)/shard_map/ppermute | solution.py:404
  43.2 14.7 %collective-permute-start.9 = (bf16[128,576]{1,0:T(8,128)(2,1)S(1)}, bf16[128,576]{1,0:T(8,128)(2,1)S(1)}, u32[]{:S(2)}, u32[]{:S(2)}) collective-permute-start(bf16[128,576]{1,0:T(8,128)(2,1)S(1)} %get-tuple-element.77), channel_id=1, source_target_pairs={{0,2},{1,3},{2,0},{3,1},{7,5},{6,4},{5,7},{4,6},{8,10},{9,11},{10,... | collective-permute-start | bytes 442376 | tf_op jit(solution)/shard_map/ppermute | solution.py:404
  50.6 7.3 %collective-permute-start.10 = (bf16[64,576]{1,0:T(8,128)(2,1)S(1)}, bf16[64,576]{1,0:T(8,128)(2,1)S(1)}, u32[]{:S(2)}, u32[]{:S(2)}) collective-permute-start(bf16[64,576]{1,0:T(8,128)(2,1)S(1)} %end_grad.1), channel_id=1, source_target_pairs={{1,3},{2,0},{5,7},{6,4},{9,11},{10,8},{13,15},{14,12},{17,19},{18,... | collective-permute-start | bytes 221192 | tf_op jit(solution)/shard_map/ppermute | solution.py:500
  51.9 16.1 %collective-permute-start.16 = (bf16[64,4096]{1,0:T(8,128)(2,1)S(1)}, bf16[64,4096]{1,0:T(8,128)(2,1)S(1)}, u32[]{:S(2)}, u32[]{:S(2)}) collective-permute-start(bf16[64,4096]{1,0:T(8,128)(2,1)S(1)} %get-tuple-element.88.end_block), channel_id=1, source_target_pairs={{1,0},{2,3},{5,4},{6,7},{9,8},{10,11},{13,12},{14,15},{17,16},{18,... | collective-permute-start | bytes 1572872 | tf_op jit(solution)/shard_map/ppermute | solution.py:502
  59.0 5.4 %collective-permute-start.11 = (bf16[10,64,128]{2,1,0:T(8,128)(2,1)S(1)}, bf16[10,64,128]{2,1,0:T(8,128)(2,1)S(1)}, u32[]{:S(2)}, u32[]{:S(2)}) collective-permute-start(bf16[10,64,128]{2,1,0:T(8,128)(2,1)S(1)} %get-tuple-element.85), channel_id=1, source_target_pairs={{0,16},{16,0},{1,17},{17,1},{2,18},{18,2},{3,19},{19,3},{4,20},{20... | collective-permute-start | bytes 491528 | tf_op jit(solution)/shard_map/ppermute | solution.py:522
  59.9 8.1 %collective-permute-start.15 = (bf16[64,576]{1,0:T(8,128)(2,1)S(1)}, bf16[64,576]{1,0:T(8,128)(2,1)S(1)}, u32[]{:S(2)}, u32[]{:S(2)}) collective-permute-start(bf16[64,576]{1,0:T(8,128)(2,1)S(1)} %get-tuple-element.87), channel_id=1, source_target_pairs={{0,3},{3,0},{4,7},{7,4},{8,11},{11,8},{12,15},{15,12},{16,19},{19,... | collective-permute-start | bytes 221192 | tf_op jit(solution)/shard_map/ppermute | solution.py:520
  64.6 8.6 %collective-permute-start.12 = (bf16[11,64,128]{2,1,0:T(8,128)(2,1)S(1)}, bf16[11,64,128]{2,1,0:T(8,128)(2,1)S(1)}, u32[]{:S(2)}, u32[]{:S(2)}) collective-permute-start(bf16[11,64,128]{2,1,0:T(8,128)(2,1)S(1)} %row_sum.1.refs_0_), channel_id=1, source_target_pairs={{8,0},{12,4},{0,8},{4,12},{9,1},{13,5},{1,9},{5,13},{10,2},{14,6},... | collective-permute-start | bytes 540680 | tf_op jit(solution)/shard_map/ppermute | solution.py:357
  66.1 7.0 %collective-permute-start.13 = (bf16[11,64,128]{2,1,0:T(8,128)(2,1)S(1)}, bf16[11,64,128]{2,1,0:T(8,128)(2,1)S(1)}, u32[]{:S(2)}, u32[]{:S(2)}) collective-permute-start(bf16[11,64,128]{2,1,0:T(8,128)(2,1)S(1)} %row_sum.1.refs_0_), channel_id=1, source_target_pairs={{12,0},{8,4},{4,8},{0,12},{13,1},{9,5},{5,9},{1,13},{14,2},{10,6},... | collective-permute-start | bytes 540680 | tf_op jit(solution)/shard_map/ppermute | solution.py:357
  66.1 7.0 %collective-permute-start.14 = (bf16[11,64,128]{2,1,0:T(8,128)(2,1)S(1)}, bf16[11,64,128]{2,1,0:T(8,128)(2,1)S(1)}, u32[]{:S(2)}, u32[]{:S(2)}) collective-permute-start(bf16[11,64,128]{2,1,0:T(8,128)(2,1)S(1)} %row_sum.1.refs_0_), channel_id=1, source_target_pairs={{4,0},{0,4},{12,8},{8,12},{5,1},{1,5},{13,9},{9,13},{6,2},{2,6},{1... | collective-permute-start | bytes 540680 | tf_op jit(solution)/shard_map/ppermute | solution.py:357
  73.2 9.1 %collective-permute-start.20 = (f32[64,512]{1,0:T(8,128)S(1)}, f32[64,512]{1,0:T(8,128)S(1)}, u32[]{:S(2)}, u32[]{:S(2)}) collective-permute-start(f32[64,512]{1,0:T(8,128)S(1)} %get-tuple-element.100), channel_id=1, source_target_pairs={{0,16},{16,0},{1,17},{17,1},{2,18},{18,2},{3,19},{19,3},{4,20},{20... | collective-permute-start | bytes 393224 | tf_op jit(solution)/shard_map/ppermute | solution.py:379
  77.2 6.5 %collective-permute-start.17 = (f32[4,128]{1,0:T(4,128)S(1)}, f32[4,128]{1,0:T(4,128)S(1)}, u32[]{:S(2)}, u32[]{:S(2)}) collective-permute-start(f32[4,128]{1,0:T(4,128)S(1)} %get-tuple-element.104.refs_0_), channel_id=1, source_target_pairs={{0,1},{1,0},{2,3},{3,2},{4,5},{5,4},{6,7},{7,6},{8,9},{9,8},{10,11... | collective-permute-start | bytes 6152 | tf_op jit(solution)/shard_map/ppermute | solution.py:372
  77.3 6.5 %collective-permute-start.18 = (f32[4,128]{1,0:T(4,128)S(1)}, f32[4,128]{1,0:T(4,128)S(1)}, u32[]{:S(2)}, u32[]{:S(2)}) collective-permute-start(f32[4,128]{1,0:T(4,128)S(1)} %get-tuple-element.104.refs_0_), channel_id=1, source_target_pairs={{0,2},{1,3},{2,0},{3,1},{4,6},{5,7},{6,4},{7,5},{8,10},{9,11},{10,... | collective-permute-start | bytes 6152 | tf_op jit(solution)/shard_map/ppermute | solution.py:372
  79.5 5.4 %collective-permute-start.19 = (f32[4,128]{1,0:T(4,128)S(1)}, f32[4,128]{1,0:T(4,128)S(1)}, u32[]{:S(2)}, u32[]{:S(2)}) collective-permute-start(f32[4,128]{1,0:T(4,128)S(1)} %get-tuple-element.104.refs_0_), channel_id=1, source_target_pairs={{0,3},{1,2},{2,1},{3,0},{4,7},{5,6},{6,5},{7,4},{8,11},{9,10},{10,... | collective-permute-start | bytes 6152 | tf_op jit(solution)/shard_map/ppermute | solution.py:372

commit v19 on v18

--- a/solution.py
+++ b/solution.py
@@ -168,7 +168,7 @@
 
 
 def input_grad_kernel(rows, size, height, width, place, cotan, first, second, middle, far, own_mod, behind, ahead, others, end_mod, *refs):
-    main, before, after, gathered, taps_t, total = refs
+    main, before, after, gathered, taps_t = refs
     ch = main.shape[0]
     spot = jnp.where(place[3] > 0, place[1], size - 1 - place[1])
     gathered[0:ch] = cotan[...]
@@ -180,19 +180,15 @@
     mods.append(jnp.where(spot == size - 1, end_mod[...], ahead[ch:]))
     every = jnp.concatenate([mod.astype(F32) for mod in mods], axis=0)
     taps_t[...] = every.T.astype(BF16)
-    total[...] = jnp.zeros(total.shape, F32)
-
-    def body(row, _):
-        g = gathered[:, pl.ds(pl.multiple_of(row * width, width), width)]
+    for row in range(height + 2):
+        total = None
         for kh in range(3):
-            y = jnp.dot(taps_t[kh * 3 * ch : (kh + 1) * 3 * ch], g, preferred_element_type=F32)
-            total[row + kh] += y
-        return 0
-
-    lax.fori_loop(0, height, body, 0)
-    for row in range(height + 2):
-        value = total[row, ch : 2 * ch]
-        value = value + shifted(total[row, 0:ch], -1) + shifted(total[row, 2 * ch : 3 * ch], 1)
+            if 0 <= row - kh < height:
+                g = gathered[:, (row - kh) * width : (row - kh + 1) * width]
+                y = jnp.dot(taps_t[kh * 3 * ch : (kh + 1) * 3 * ch], g, preferred_element_type=F32)
+                total = y if total is None else total + y
+        value = total[ch : 2 * ch]
+        value = value + shifted(total[0:ch], -1) + shifted(total[2 * ch : 3 * ch], 1)
         if row == 0:
             before[...] = value
         elif row == height + 1:
@@ -546,7 +542,6 @@
         scratch=[
             ((all_ch, pixels), BF16),
             ((TAPS * ch, all_ch), BF16),
-            ((height + 2, 3 * ch, width), F32),
         ],
         flops=INPUT_FLOPS,
     )

time: 86.3 us -> 85.7 us (level)
  Pallas kernels: 23.6 us -> 21.8 us
  waiting for transfers between devices: 12.6 us -> 14.2 us
    pallas_call x11, Pallas kernels: 23.6 us -> 21.8 us  [call(): pl.pallas_call(kernel, out_shape=outs, in_specs=sspec(scalars) + vspec(le...]
    ppermute x3, waiting for transfers between devices: 0.01 us -> 1.64 us  [exchange_pairs(): lax.ppermute(x, axis, [(partner(i, step, size), i) for i in range(size)])]
  transfers between devices with their start and end apart: 21 -> 21, of which waited for: 6 -> 7; matrix products, arithmetic and copies ran while one was open for 3% -> 3% of each run, Pallas kernels for 26% -> 25%
where the time goes in v19:
time: 85.7 us; the launch traced here: 85.2 us
  starting transfers between devices  43.4 us (51%)
  Pallas kernels  21.8 us (25%)
  waiting for transfers between devices  14.2 us (17%)
  local copies, waits for them, and re-layouts  3.49 us (4%)
  other arithmetic  1.28 us (1%)
  between operations  0.98 us (1%)
    ppermute x7, starting transfers between devices, along(): return lax.ppermute(x, ('samples', 'chan'), whole)  22.2 us
    pallas_call x11, Pallas kernels, call(): pl.pallas_call(kernel, out_shape=outs, in_specs=sspec(scalars) + vspec(le...  21.8 us
    ppermute x1, starting transfers between devices, on_device(): feat_end = lax.ppermute(feat, 'chan', [(0, 1), (size - 1, size - 2)])  5.29 us
    ppermute x1, waiting for transfers between devices, on_device(): from_end = lax.ppermute(grad_end, 'chan', [(1, size - 1), (size - 2, 0)])  4.72 us
    ppermute x3, starting transfers between devices, terms_of_sum(): lax.ppermute(x, axis, [(i, i ^ step) for i in range(size)])  4.44 us
    unnamed x19, local copies, waits for them, and re-layouts  3.13 us
    ppermute x1, starting transfers between devices, on_device(): end_mod = lax.ppermute(mods[size], 'chan', [(0, size - 1), (size - 1, 0)])  2.8 us
    ppermute x1, waiting for transfers between devices, exchange(): lax.ppermute(x, axis, [(i, (i + s) % size) for i in range(size)])  2.71 us
  transfers between devices with their start and end apart: 21, of which 7 were waited for; matrix products, arithmetic and copies ran while one was open for 3% of the time, Pallas kernels for 25%

profile of v19, /device:TPU:0, one launch (start us, length us, event | category | flops | bytes accessed | tf_op | source)
XLA Modules:
  0.0 85.2 jit_solution(2613374207304499905)
XLA Ops:
  0.6 0.0 copy-start.7
  0.6 0.0 copy-start
  0.7 1.3 %copy.13 = bf16[8,8,8,512]{3,1,2,0:T(8,128)(2,1)S(1)} copy(bf16[8,8,8,512]{3,2,1,0:T(8,128)(2,1)} %bitcast.32) | data formatting | bytes 1048576
  2.0 5.7 %collective-permute-start.1 = (bf16[64,4096]{1,0:T(8,128)(2,1)S(1)}, bf16[64,4096]{1,0:T(8,128)(2,1)}, u32[]{:S(2)}, u32[]{:S(2)}) collective-permute-start(bf16[64,4096]{1,0:T(8,128)(2,1)S(1)} %bitcast.26), channel_id=1, source_target_pairs={{0,1},{1,2},{2,3},{7,6},{6,5},{5,4},{8,9},{9,10},{10,11},{15,14},{... | collective-permute-start | bytes 1572872 | tf_op jit(solution)/shard_map/ppermute | solution.py:400
  7.8 1.3 %collective-permute-start.2 = (bf16[64,4096]{1,0:T(8,128)(2,1)S(1)}, bf16[64,4096]{1,0:T(8,128)(2,1)}, u32[]{:S(2)}, u32[]{:S(2)}) collective-permute-start(bf16[64,4096]{1,0:T(8,128)(2,1)S(1)} %bitcast.27), channel_id=1, source_target_pairs={{1,0},{2,1},{3,2},{6,7},{5,6},{4,5},{9,8},{10,9},{11,10},{14,15},{... | collective-permute-start | bytes 1572872 | tf_op jit(solution)/shard_map/ppermute | solution.py:400
  9.1 0.2 copy.14
  9.3 1.6 %collective-permute-start.5 = (bf16[64,512]{1,0:T(8,128)(2,1)S(1)}, bf16[64,512]{1,0:T(8,128)(2,1)S(1)}, u32[]{:S(2)}, u32[]{:S(2)}) collective-permute-start(bf16[64,512]{1,0:T(8,128)(2,1)S(1)} %slice_select_fusion), channel_id=1, source_target_pairs={{0,16},{16,0},{1,17},{17,1},{2,18},{18,2},{3,19},{19,3},{4,20},{20... | collective-permute-start | bytes 196616 | tf_op jit(solution)/shard_map/ppermute | solution.py:375
  10.9 1.0 %plain.1 = (f32[10,64,128]{2,1,0:T(8,128)S(1)}, f32[8,128]{1,0:T(8,128)S(1)}) custom-call(s32[1,4]{1,0:T(1,128)S(1)} %copy-done.5, f32[1,512]{1,0:T(1,128)S(1)} %copy-done.4, f32[1,128]{1,0:T(1,128)S(1)} %bitcast.30, f32[512,128]{1,0:T(8,128)S(1)} %copy-done.3, f32[4,9,64,128]{3,2,1,0:T(8,128)S(1)} %copy-done), custom_call_target="tpu_custom_call" | custom-call | flops 1000000 | bytes 1776144 | tf_op jit(solution)/shard_map/plain/pallas_call | solution.py:328
  11.8 0.0 copy-start.1
  11.8 0.6 collective-permute-start
  12.4 1.2 %collective-permute-done.5 = bf16[64,512]{1,0:T(8,128)(2,1)S(1)} collective-permute-done((bf16[64,512]{1,0:T(8,128)(2,1)S(1)}, bf16[64,512]{1,0:T(8,128)(2,1)S(1)}, u32[]{:S(2)}, u32[]{:S(2)}) %collective-permute-start.5) | collective-permute-done | bytes 65568 | tf_op jit(solution)/shard_map/ppermute | solution.py:375
  13.7 5.3 %collective-permute-start.6 = (bf16[64,5120]{1,0:T(8,128)(2,1)S(1)}, bf16[64,5120]{1,0:T(8,128)(2,1)S(1)}, u32[]{:S(2)}, u32[]{:S(2)}) collective-permute-start(bf16[64,5120]{1,0:T(8,128)(2,1)S(1)} %feat_rows.1.refs_3_), channel_id=1, source_target_pairs={{0,1},{3,2},{4,5},{7,6},{8,9},{11,10},{12,13},{15,14},{16,17},{19,... | collective-permute-start | bytes 1966088 | tf_op jit(solution)/shard_map/ppermute | solution.py:440
  19.0 2.7 %collective-permute-done.refs_1_ = f32[10,64,128]{2,1,0:T(8,128)} collective-permute-done((f32[10,64,128]{2,1,0:T(8,128)S(1)}, f32[10,64,128]{2,1,0:T(8,128)}, u32[]{:S(2)}, u32[]{:S(2)}) %collective-permute-start) | collective-permute-done | bytes 327712 | tf_op jit(solution)/shard_map/ppermute | solution.py:360
  21.7 0.0 collective-permute-done.1.refs_1_.first
  21.7 0.0 collective-permute-done.2.refs_2_.second
  21.7 0.7 collective-permute-start.3
  22.4 1.3 %collective-permute-start.4 = (bf16[64,4096]{1,0:T(8,128)(2,1)}, bf16[64,4096]{1,0:T(8,128)(2,1)}, u32[]{:S(2)}, u32[]{:S(2)}) collective-permute-start(bf16[64,4096]{1,0:T(8,128)(2,1)} %collective-permute-done.2.refs_2_.second), channel_id=1, source_target_pairs={{1,0},{2,1},{6,7},{5,6},{9,8},{10,9},{14,15},{13,14},{17,16},{18,1... | collective-permute-start | bytes 1572872 | tf_op jit(solution)/shard_map/ppermute | solution.py:400
  23.7 0.1 pad_add_fusion.place
  23.8 1.0 %copy-done.2 = f32[10,64,128]{2,1,0:T(8,128)S(1)} copy-done((f32[10,64,128]{2,1,0:T(8,128)S(1)}, f32[10,64,128]{2,1,0:T(8,128)}, u32[]{:S(2)}) %copy-start.2) | copy-done | bytes 327704
  24.8 1.3 %mod_blocks.1 = (bf16[9,64,256]{2,1,0:T(8,128)(2,1)S(1)}, f32[64,128]{1,0:T(8,128)S(1)}, bf16[64,576]{1,0:T(8,128)(2,1)S(1)}, bf16[64,576]{1,0:T(8,128)(2,1)S(1)...) custom-call(s32[4]{0:T(128)S(1)} %pad_add_fusion.place, ...), custom_call_target="tpu_custom_call" | custom-call | flops 1000000 | bytes 1351696 | tf_op jit(solution)/shard_map/mod_blocks/pallas_call | solution.py:328
  26.0 4.5 %near_grad.1 = (bf16[64,576]{1,0:T(8,128)(2,1)S(1)}, bf16[128,576]{1,0:T(8,128)(2,1)S(1)}, bf16[128,576]{1,0:T(8,128)(2,1)S(1)}, bf16[192,5120]{1,0:T(8,128)(2,1)S(1)}) custom-call(bf16[64,4096]{1,0:T(8,128)(2,1)S(1)} %bitcast.28, bf16[64,4096]{1,0:T(8,128)(2,1)} %collective-permute-done.1.refs_1_.first, ...), custom_call_target="tpu_custom_call" | custom-call | flops 905969664 | bytes 4710400 | tf_op jit(solution)/shard_map/near_grad/pallas_call | solution.py:328
  30.6 1.3 %collective-permute-start.7 = (bf16[128,576]{1,0:T(8,128)(2,1)S(1)}, bf16[128,576]{1,0:T(8,128)(2,1)S(1)}, u32[]{:S(2)}, u32[]{:S(2)}) collective-permute-start(bf16[128,576]{1,0:T(8,128)(2,1)S(1)} %get-tuple-element.71), channel_id=1, source_target_pairs={{1,0},{2,1},{3,2},{6,7},{5,6},{4,5},{9,8},{10,9},{11,10},{14,15},{... | collective-permute-start | bytes 442376 | tf_op jit(solution)/shard_map/ppermute | solution.py:400
  31.9 7.6 %collective-permute-start.8 = (bf16[128,576]{1,0:T(8,128)(2,1)S(1)}, bf16[128,576]{1,0:T(8,128)(2,1)S(1)}, u32[]{:S(2)}, u32[]{:S(2)}) collective-permute-start(bf16[128,576]{1,0:T(8,128)(2,1)S(1)} %get-tuple-element.72), channel_id=1, source_target_pairs={{0,1},{1,2},{2,3},{7,6},{6,5},{5,4},{8,9},{9,10},{10,11},{15,14},{... | collective-permute-start | bytes 442376 | tf_op jit(solution)/shard_map/ppermute | solution.py:400
  39.4 0.0 collective-permute-done.6.feat
  39.5 0.0 collective-permute-done.3.refs_0_
  39.5 0.0 collective-permute-done.4.refs_1_
  39.5 3.7 %middle_grad.1 = (bf16[128,576]{1,0:T(8,128)(2,1)S(1)}, bf16[64,4096]{1,0:T(8,128)(2,1)S(1)}, bf16[64,4096]{1,0:T(8,128)(2,1)S(1)}) custom-call(bf16[64,4096]{1,0:T(8,128)(2,1)S(1)} %collective-permute-done.3.refs_0_, bf16[64,4096]{1,0:T(8,128)(2,1)} %collective-permute-done.4.refs_1_, bf16[192,5120]{1,0:T(8,128)(2,1)S(1)} %get-tuple-element.75.refs_2_, ...), custom_call_target="tpu_custom_call" | custom-call | flops 301989888 | bytes 4284416 | tf_op jit(solution)/shard_map/middle_grad/pallas_call | solution.py:328
  43.2 4.3 %collective-permute-start.9 = (bf16[128,576]{1,0:T(8,128)(2,1)S(1)}, bf16[128,576]{1,0:T(8,128)(2,1)S(1)}, u32[]{:S(2)}, u32[]{:S(2)}) collective-permute-start(bf16[128,576]{1,0:T(8,128)(2,1)S(1)} %get-tuple-element.77), channel_id=1, source_target_pairs={{0,2},{1,3},{2,0},{3,1},{7,5},{6,4},{5,7},{4,6},{8,10},{9,11},{10,... | collective-permute-start | bytes 442376 | tf_op jit(solution)/shard_map/ppermute | solution.py:400
  47.5 3.0 %end_grad.1 = bf16[64,576]{1,0:T(8,128)(2,1)S(1)} custom-call(bf16[64,4096]{1,0:T(8,128)(2,1)S(1)} %get-tuple-element.88.end_block, bf16[64,5120]{1,0:T(8,128)(2,1)S(1)} %collective-permute-done.6.feat), custom_call_target="tpu_custom_call" | custom-call | flops 301989888 | bytes 1253376 | tf_op jit(solution)/shard_map/end_grad/pallas_call | solution.py:328
  50.6 1.3 %collective-permute-start.10 = (bf16[64,576]{1,0:T(8,128)(2,1)S(1)}, bf16[64,576]{1,0:T(8,128)(2,1)S(1)}, u32[]{:S(2)}, u32[]{:S(2)}) collective-permute-start(bf16[64,576]{1,0:T(8,128)(2,1)S(1)} %end_grad.1), channel_id=1, source_target_pairs={{1,3},{2,0},{5,7},{6,4},{9,11},{10,8},{13,15},{14,12},{17,19},{18,... | collective-permute-start | bytes 221192 | tf_op jit(solution)/shard_map/ppermute | solution.py:496
  51.9 1.3 %collective-permute-start.16 = (bf16[64,4096]{1,0:T(8,128)(2,1)S(1)}, bf16[64,4096]{1,0:T(8,128)(2,1)S(1)}, u32[]{:S(2)}, u32[]{:S(2)}) collective-permute-start(bf16[64,4096]{1,0:T(8,128)(2,1)S(1)} %get-tuple-element.88.end_block), channel_id=1, source_target_pairs={{1,0},{2,3},{5,4},{6,7},{9,8},{10,11},{13,12},{14,15},{17,16},{18,... | collective-permute-start | bytes 1572872 | tf_op jit(solution)/shard_map/ppermute | solution.py:498
  53.2 0.0 collective-permute-done.7.ahead
  53.2 0.0 collective-permute-done.8.behind
  53.2 4.7 %collective-permute-done.10.end = bf16[64,576]{1,0:T(8,128)(2,1)S(1)} collective-permute-done((bf16[64,576]{1,0:T(8,128)(2,1)S(1)}, bf16[64,576]{1,0:T(8,128)(2,1)S(1)}, u32[]{:S(2)}, u32[]{:S(2)}) %collective-permute-start.10) | collective-permute-done | bytes 73760 | tf_op jit(solution)/shard_map/ppermute | solution.py:496
  57.9 0.0 collective-permute-done.9.others
  57.9 1.1 %collect.1 = (bf16[10,64,128]{2,1,0:T(8,128)(2,1)S(1)}, bf16[10,64,128]{2,1,0:T(8,128)(2,1)S(1)}) custom-call(s32[4]{0:T(128)S(1)} %pad_add_fusion.place, f32[64,128]{1,0:T(8,128)S(1)} %get-tuple-element.58.scale, bf16[9,64,256]{2,1,0:T(8,128)(2,1)S(1)} %get-tuple-element.69.whole_mod, bf16[64,576]{1,0:T(8,128)(2,1)S(1)} %get-tuple-element.70.own, ...), custom_call_target="tpu_custom_call" | custom-call | flops 6000000000 | bytes 1245200 | tf_op jit(solution)/shard_map/collect/pallas_call | solution.py:328
  59.0 0.9 %collective-permute-start.11 = (bf16[10,64,128]{2,1,0:T(8,128)(2,1)S(1)}, bf16[10,64,128]{2,1,0:T(8,128)(2,1)S(1)}, u32[]{:S(2)}, u32[]{:S(2)}) collective-permute-start(bf16[10,64,128]{2,1,0:T(8,128)(2,1)S(1)} %get-tuple-element.85), channel_id=1, source_target_pairs={{0,16},{16,0},{1,17},{17,1},{2,18},{18,2},{3,19},{19,3},{4,20},{20... | collective-permute-start | bytes 491528 | tf_op jit(solution)/shard_map/ppermute | solution.py:518
  59.9 2.8 %collective-permute-start.15 = (bf16[64,576]{1,0:T(8,128)(2,1)S(1)}, bf16[64,576]{1,0:T(8,128)(2,1)S(1)}, u32[]{:S(2)}, u32[]{:S(2)}) collective-permute-start(bf16[64,576]{1,0:T(8,128)(2,1)S(1)} %get-tuple-element.87), channel_id=1, source_target_pairs={{0,3},{3,0},{4,7},{7,4},{8,11},{11,8},{12,15},{15,12},{16,19},{19,... | collective-permute-start | bytes 221192 | tf_op jit(solution)/shard_map/ppermute | solution.py:516
  62.7 1.7 %collective-permute-done.11.refs_1_ = bf16[10,64,128]{2,1,0:T(8,128)(2,1)S(1)} collective-permute-done((bf16[10,64,128]{2,1,0:T(8,128)(2,1)S(1)}, bf16[10,64,128]{2,1,0:T(8,128)(2,1)S(1)}, u32[]{:S(2)}, u32[]{:S(2)}) %collective-permute-start.11) | collective-permute-done | bytes 163872 | tf_op jit(solution)/shard_map/ppermute | solution.py:518
  64.3 0.2 row_sum.1.refs_0_
  64.6 1.6 %collective-permute-start.12 = (bf16[11,64,128]{2,1,0:T(8,128)(2,1)S(1)}, bf16[11,64,128]{2,1,0:T(8,128)(2,1)S(1)}, u32[]{:S(2)}, u32[]{:S(2)}) collective-permute-start(bf16[11,64,128]{2,1,0:T(8,128)(2,1)S(1)} %row_sum.1.refs_0_), channel_id=1, source_target_pairs={{8,0},{12,4},{0,8},{4,12},{9,1},{13,5},{1,9},{5,13},{10,2},{14,6},... | collective-permute-start | bytes 540680 | tf_op jit(solution)/shard_map/ppermute | solution.py:353
  66.1 0.0 collective-permute-start.13
  66.1 0.6 collective-permute-start.14
  66.8 1.2 %collective-permute-done.15.end_mod = bf16[64,576]{1,0:T(8,128)(2,1)S(1)} collective-permute-done((bf16[64,576]{1,0:T(8,128)(2,1)S(1)}, bf16[64,576]{1,0:T(8,128)(2,1)S(1)}, u32[]{:S(2)}, u32[]{:S(2)}) %collective-permute-start.15) | collective-permute-done | bytes 73760 | tf_op jit(solution)/shard_map/ppermute | solution.py:516
  68.0 0.0 collective-permute-done.16.far
  68.0 3.4 %input_grad.1 = (f32[64,4096]{1,0:T(8,128)S(1)}, f32[64,512]{1,0:T(8,128)}, f32[64,512]{1,0:T(8,128)S(1)}) custom-call(s32[4]{0:T(128)S(1)} %pad_add_fusion.place, bf16[64,4096]{1,0:T(8,128)(2,1)S(1)} %bitcast.29, bf16[64,4096]{1,0:T(8,128)(2,1)} %collective-permute-done.1.refs_1_.first, bf16[64,4096]{1,0:T(8,128)(2,1)} %collective-permute-done.2.refs_2_.second, ...), custom_call_target="tpu_custom_call" | custom-call | flops 2000000000 | bytes 4522000 | tf_op jit(solution)/shard_map/input_grad/pallas_call | solution.py:328
  71.3 0.0 collective-permute-done.12.refs_1_
  71.4 1.6 %collective-permute-done.13.refs_2_ = bf16[11,64,128]{2,1,0:T(8,128)(2,1)S(1)} collective-permute-done((bf16[11,64,128]{2,1,0:T(8,128)(2,1)S(1)}, bf16[11,64,128]{2,1,0:T(8,128)(2,1)S(1)}, u32[]{:S(2)}, u32[]{:S(2)}) %collective-permute-start.13) | collective-permute-done | bytes 180256 | tf_op jit(solution)/shard_map/ppermute | solution.py:353
  73.0 0.0 collective-permute-done.14.refs_3_
  73.0 0.8 collective-permute-start.20
  73.8 0.1 pad.1.clone
  73.9 2.7 %bank_grad.1 = (f32[4,9,64,128]{3,2,1,0:T(8,128)}, f32[4,128]{1,0:T(4,128)S(1)}, f32[4,512]{1,0:T(4,128)S(1)}) custom-call(s32[4]{0:T(128)S(1)} %pad_add_fusion.place, f32[4,9,64,128]{3,2,1,0:T(8,128)S(1)} %copy-done, bf16[11,64,128]{2,1,0:T(8,128)(2,1)S(1)} %row_sum.1.refs_0_, bf16[11,64,128]{2,1,0:T(8,128)(2,1)S(1)} %collective-permute-done.12.refs_1_, ...), custom_call_target="tpu_custom_call" | custom-call | flops 1000000 | bytes 3090448 | tf_op jit(solution)/shard_map/bank_grad/pallas_call | solution.py:328
  76.6 0.1 collective-permute-start.17
  76.7 2.2 %collective-permute-start.18 = (f32[4,128]{1,0:T(4,128)S(1)}, f32[4,128]{1,0:T(4,128)S(1)}, u32[]{:S(2)}, u32[]{:S(2)}) collective-permute-start(f32[4,128]{1,0:T(4,128)S(1)} %get-tuple-element.104.refs_0_), channel_id=1, source_target_pairs={{0,2},{1,3},{2,0},{3,1},{4,6},{5,7},{6,4},{7,5},{8,10},{9,11},{10,... | collective-permute-start | bytes 6152 | tf_op jit(solution)/shard_map/ppermute | solution.py:368
  78.9 2.2 %collective-permute-start.19 = (f32[4,128]{1,0:T(4,128)S(1)}, f32[4,128]{1,0:T(4,128)S(1)}, u32[]{:S(2)}, u32[]{:S(2)}) collective-permute-start(f32[4,128]{1,0:T(4,128)S(1)} %get-tuple-element.104.refs_0_), channel_id=1, source_target_pairs={{0,3},{1,2},{2,1},{3,0},{4,7},{5,6},{6,5},{7,4},{8,11},{9,10},{10,... | collective-permute-start | bytes 6152 | tf_op jit(solution)/shard_map/ppermute | solution.py:368
  81.1 0.6 copy.15
  81.7 0.0 collective-permute-done.20
  81.7 0.1 copy.12
  81.9 0.1 copy.11
  82.0 1.2 %fusion = bf16[1,64,8,512]{3,2,1,0:T(8,128)(2,1)} fusion(f32[1,64,1,512]{3,2,1,0:T(1,128)S(1)} %copy.12, f32[1,64,1,512]{3,2,1,0:T(1,128)S(1)} %copy.11, f32[8]{0:T(128)S(1)} %pad.1.clone, f32[1,64,8,512]{3,2,1,0:T(8,128)S(1)} %bitcast.31), kind=kLoop, calls=%fused_computation.1 | loop fusion | flops 1048576 | bytes 1835040 | tf_op jit(solution)/shard_map/convert_element_type | solution.py:565
  83.2 0.0 collective-permute-done.17.refs_1_
  83.2 0.0 collective-permute-done.18.refs_2_
  83.2 1.1 %collective-permute-done.19.refs_3_ = f32[4,128]{1,0:T(4,128)S(1)} collective-permute-done((f32[4,128]{1,0:T(4,128)S(1)}, f32[4,128]{1,0:T(4,128)S(1)}, u32[]{:S(2)}, u32[]{:S(2)}) %collective-permute-start.19) | collective-permute-done | bytes 2080 | tf_op jit(solution)/shard_map/ppermute | solution.py:368
  84.2 0.9 %affine.1 = (f32[512,128]{1,0:T(8,128)}, f32[1,128]{1,0:T(1,128)}) custom-call(f32[4,512]{1,0:T(4,128)S(1)} %get-tuple-element.103.latents, f32[4,128]{1,0:T(4,128)S(1)} %get-tuple-element.104.refs_0_, f32[4,128]{1,0:T(4,128)S(1)} %collective-permute-done.17.refs_1_, f32[4,128]{1,0:T(4,128)S(1)} %collective-permute-done.18.refs_2_, ...), custom_call_target="tpu_custom_call" | custom-call | flops 1000000 | bytes 279040 | tf_op jit(solution)/shard_map/affine/pallas_call | solution.py:328
  (17 shorter events, 0.1 us)
Async XLA Ops:
  0.6 8.4 %copy-start.7 = (bf16[1,64,8,512]{3,2,1,0:T(8,128)(2,1)S(1)}, bf16[1,64,8,512]{3,2,1,0:T(8,128)(2,1)}, u32[]{:S(2)}) copy-start(bf16[1,64,8,512]{3,2,1,0:T(8,128)(2,1)} %param.7) | copy-start | bytes 1572868
  0.6 10.2 %copy-start = (f32[4,9,64,128]{3,2,1,0:T(8,128)S(1)}, f32[4,9,64,128]{3,2,1,0:T(8,128)}, u32[]{:S(2)}) copy-start(f32[4,9,64,128]{3,2,1,0:T(8,128)} %bank.1) | copy-start | bytes 3538948
  0.7 10.2 %copy-start.5 = (s32[1,4]{1,0:T(1,128)S(1)}, s32[1,4]{1,0:T(1,128)}, u32[]{:S(2)}) copy-start(s32[1,4]{1,0:T(1,128)} %refs_0_.1) | copy-start | bytes 52
  0.7 10.2 %copy-start.4 = (f32[1,512]{1,0:T(1,128)S(1)}, f32[1,512]{1,0:T(1,128)}, u32[]{:S(2)}) copy-start(f32[1,512]{1,0:T(1,128)} %refs_1_.1) | copy-start | bytes 6148
  0.7 10.2 %copy-start.6 = (f32[128]{0:T(128)S(1)}, f32[128]{0:T(128)}, u32[]{:S(2)}) copy-start(f32[128]{0:T(128)} %param.13) | copy-start | bytes 1540
  0.7 10.2 %copy-start.3 = (f32[512,128]{1,0:T(8,128)S(1)}, f32[512,128]{1,0:T(8,128)}, u32[]{:S(2)}) copy-start(f32[512,128]{1,0:T(8,128)} %refs_3_.1) | copy-start | bytes 786436
  2.0 19.7 %collective-permute-start.1 = (bf16[64,4096]{1,0:T(8,128)(2,1)S(1)}, bf16[64,4096]{1,0:T(8,128)(2,1)}, u32[]{:S(2)}, u32[]{:S(2)}) collective-permute-start(bf16[64,4096]{1,0:T(8,128)(2,1)S(1)} %bitcast.26), channel_id=1, source_target_pairs={{0,1},{1,2},{2,3},{7,6},{6,5},{5,4},{8,9},{9,10},{10,11},{15,14},{... | collective-permute-start | bytes 1572872 | tf_op jit(solution)/shard_map/ppermute | solution.py:400
  7.8 13.9 %collective-permute-start.2 = (bf16[64,4096]{1,0:T(8,128)(2,1)S(1)}, bf16[64,4096]{1,0:T(8,128)(2,1)}, u32[]{:S(2)}, u32[]{:S(2)}) collective-permute-start(bf16[64,4096]{1,0:T(8,128)(2,1)S(1)} %bitcast.27), channel_id=1, source_target_pairs={{1,0},{2,1},{3,2},{6,7},{5,6},{4,5},{9,8},{10,9},{11,10},{14,15},{... | collective-permute-start | bytes 1572872 | tf_op jit(solution)/shard_map/ppermute | solution.py:400
  9.3 4.3 %collective-permute-start.5 = (bf16[64,512]{1,0:T(8,128)(2,1)S(1)}, bf16[64,512]{1,0:T(8,128)(2,1)S(1)}, u32[]{:S(2)}, u32[]{:S(2)}) collective-permute-start(bf16[64,512]{1,0:T(8,128)(2,1)S(1)} %slice_select_fusion), channel_id=1, source_target_pairs={{0,16},{16,0},{1,17},{17,1},{2,18},{18,2},{3,19},{19,3},{4,20},{20... | collective-permute-start | bytes 196616 | tf_op jit(solution)/shard_map/ppermute | solution.py:375
  11.8 9.9 %copy-start.1 = (f32[10,64,128]{2,1,0:T(8,128)}, f32[10,64,128]{2,1,0:T(8,128)S(1)}, u32[]{:S(2)}) copy-start(f32[10,64,128]{2,1,0:T(8,128)S(1)} %get-tuple-element.57.refs_0_) | copy-start | bytes 983044
  11.8 9.8 %collective-permute-start = (f32[10,64,128]{2,1,0:T(8,128)S(1)}, f32[10,64,128]{2,1,0:T(8,128)}, u32[]{:S(2)}, u32[]{:S(2)}) collective-permute-start(f32[10,64,128]{2,1,0:T(8,128)S(1)} %get-tuple-element.57.refs_0_), channel_id=1, source_target_pairs={{0,16},{16,0},{1,17},{17,1},{2,18},{18,2},{3,19},{19,3},{4,20},{20... | collective-permute-start | bytes 983048 | tf_op jit(solution)/shard_map/ppermute | solution.py:360
  13.7 25.8 %collective-permute-start.6 = (bf16[64,5120]{1,0:T(8,128)(2,1)S(1)}, bf16[64,5120]{1,0:T(8,128)(2,1)S(1)}, u32[]{:S(2)}, u32[]{:S(2)}) collective-permute-start(bf16[64,5120]{1,0:T(8,128)(2,1)S(1)} %feat_rows.1.refs_3_), channel_id=1, source_target_pairs={{0,1},{3,2},{4,5},{7,6},{8,9},{11,10},{12,13},{15,14},{16,17},{19,... | collective-permute-start | bytes 1966088 | tf_op jit(solution)/shard_map/ppermute | solution.py:440
  21.7 17.8 %collective-permute-start.3 = (bf16[64,4096]{1,0:T(8,128)(2,1)}, bf16[64,4096]{1,0:T(8,128)(2,1)S(1)}, u32[]{:S(2)}, u32[]{:S(2)}) collective-permute-start(bf16[64,4096]{1,0:T(8,128)(2,1)} %collective-permute-done.1.refs_1_.first), channel_id=1, source_target_pairs={{1,2},{2,3},{6,5},{5,4},{9,10},{10,11},{14,13},{13,12},{17,18},{18... | collective-permute-start | bytes 1572872 | tf_op jit(solution)/shard_map/ppermute | solution.py:400
  22.4 17.1 %collective-permute-start.4 = (bf16[64,4096]{1,0:T(8,128)(2,1)}, bf16[64,4096]{1,0:T(8,128)(2,1)}, u32[]{:S(2)}, u32[]{:S(2)}) collective-permute-start(bf16[64,4096]{1,0:T(8,128)(2,1)} %collective-permute-done.2.refs_2_.second), channel_id=1, source_target_pairs={{1,0},{2,1},{6,7},{5,6},{9,8},{10,9},{14,15},{13,14},{17,16},{18,1... | collective-permute-start | bytes 1572872 | tf_op jit(solution)/shard_map/ppermute | solution.py:400
  23.8 1.0 %copy-start.2 = (f32[10,64,128]{2,1,0:T(8,128)S(1)}, f32[10,64,128]{2,1,0:T(8,128)}, u32[]{:S(2)}) copy-start(f32[10,64,128]{2,1,0:T(8,128)} %copy-done.1) | copy-start | bytes 983044
  30.6 22.6 %collective-permute-start.7 = (bf16[128,576]{1,0:T(8,128)(2,1)S(1)}, bf16[128,576]{1,0:T(8,128)(2,1)S(1)}, u32[]{:S(2)}, u32[]{:S(2)}) collective-permute-start(bf16[128,576]{1,0:T(8,128)(2,1)S(1)} %get-tuple-element.71), channel_id=1, source_target_pairs={{1,0},{2,1},{3,2},{6,7},{5,6},{4,5},{9,8},{10,9},{11,10},{14,15},{... | collective-permute-start | bytes 442376 | tf_op jit(solution)/shard_map/ppermute | solution.py:400
  31.9 21.3 %collective-permute-start.8 = (bf16[128,576]{1,0:T(8,128)(2,1)S(1)}, bf16[128,576]{1,0:T(8,128)(2,1)S(1)}, u32[]{:S(2)}, u32[]{:S(2)}) collective-permute-start(bf16[128,576]{1,0:T(8,128)(2,1)S(1)} %get-tuple-element.72), channel_id=1, source_target_pairs={{0,1},{1,2},{2,3},{7,6},{6,5},{5,4},{8,9},{9,10},{10,11},{15,14},{... | collective-permute-start | bytes 442376 | tf_op jit(solution)/shard_map/ppermute | solution.py:400
  43.2 14.7 %collective-permute-start.9 = (bf16[128,576]{1,0:T(8,128)(2,1)S(1)}, bf16[128,576]{1,0:T(8,128)(2,1)S(1)}, u32[]{:S(2)}, u32[]{:S(2)}) collective-permute-start(bf16[128,576]{1,0:T(8,128)(2,1)S(1)} %get-tuple-element.77), channel_id=1, source_target_pairs={{0,2},{1,3},{2,0},{3,1},{7,5},{6,4},{5,7},{4,6},{8,10},{9,11},{10,... | collective-permute-start | bytes 442376 | tf_op jit(solution)/shard_map/ppermute | solution.py:400
  50.6 7.3 %collective-permute-start.10 = (bf16[64,576]{1,0:T(8,128)(2,1)S(1)}, bf16[64,576]{1,0:T(8,128)(2,1)S(1)}, u32[]{:S(2)}, u32[]{:S(2)}) collective-permute-start(bf16[64,576]{1,0:T(8,128)(2,1)S(1)} %end_grad.1), channel_id=1, source_target_pairs={{1,3},{2,0},{5,7},{6,4},{9,11},{10,8},{13,15},{14,12},{17,19},{18,... | collective-permute-start | bytes 221192 | tf_op jit(solution)/shard_map/ppermute | solution.py:496
  51.9 16.1 %collective-permute-start.16 = (bf16[64,4096]{1,0:T(8,128)(2,1)S(1)}, bf16[64,4096]{1,0:T(8,128)(2,1)S(1)}, u32[]{:S(2)}, u32[]{:S(2)}) collective-permute-start(bf16[64,4096]{1,0:T(8,128)(2,1)S(1)} %get-tuple-element.88.end_block), channel_id=1, source_target_pairs={{1,0},{2,3},{5,4},{6,7},{9,8},{10,11},{13,12},{14,15},{17,16},{18,... | collective-permute-start | bytes 1572872 | tf_op jit(solution)/shard_map/ppermute | solution.py:498
  59.0 5.4 %collective-permute-start.11 = (bf16[10,64,128]{2,1,0:T(8,128)(2,1)S(1)}, bf16[10,64,128]{2,1,0:T(8,128)(2,1)S(1)}, u32[]{:S(2)}, u32[]{:S(2)}) collective-permute-start(bf16[10,64,128]{2,1,0:T(8,128)(2,1)S(1)} %get-tuple-element.85), channel_id=1, source_target_pairs={{0,16},{16,0},{1,17},{17,1},{2,18},{18,2},{3,19},{19,3},{4,20},{20... | collective-permute-start | bytes 491528 | tf_op jit(solution)/shard_map/ppermute | solution.py:518
  59.9 8.1 %collective-permute-start.15 = (bf16[64,576]{1,0:T(8,128)(2,1)S(1)}, bf16[64,576]{1,0:T(8,128)(2,1)S(1)}, u32[]{:S(2)}, u32[]{:S(2)}) collective-permute-start(bf16[64,576]{1,0:T(8,128)(2,1)S(1)} %get-tuple-element.87), channel_id=1, source_target_pairs={{0,3},{3,0},{4,7},{7,4},{8,11},{11,8},{12,15},{15,12},{16,19},{19,... | collective-permute-start | bytes 221192 | tf_op jit(solution)/shard_map/ppermute | solution.py:516
  64.6 6.8 %collective-permute-start.12 = (bf16[11,64,128]{2,1,0:T(8,128)(2,1)S(1)}, bf16[11,64,128]{2,1,0:T(8,128)(2,1)S(1)}, u32[]{:S(2)}, u32[]{:S(2)}) collective-permute-start(bf16[11,64,128]{2,1,0:T(8,128)(2,1)S(1)} %row_sum.1.refs_0_), channel_id=1, source_target_pairs={{8,0},{12,4},{0,8},{4,12},{9,1},{13,5},{1,9},{5,13},{10,2},{14,6},... | collective-permute-start | bytes 540680 | tf_op jit(solution)/shard_map/ppermute | solution.py:353
  66.1 6.8 %collective-permute-start.13 = (bf16[11,64,128]{2,1,0:T(8,128)(2,1)S(1)}, bf16[11,64,128]{2,1,0:T(8,128)(2,1)S(1)}, u32[]{:S(2)}, u32[]{:S(2)}) collective-permute-start(bf16[11,64,128]{2,1,0:T(8,128)(2,1)S(1)} %row_sum.1.refs_0_), channel_id=1, source_target_pairs={{12,0},{8,4},{4,8},{0,12},{13,1},{9,5},{5,9},{1,13},{14,2},{10,6},... | collective-permute-start | bytes 540680 | tf_op jit(solution)/shard_map/ppermute | solution.py:353
  66.1 6.8 %collective-permute-start.14 = (bf16[11,64,128]{2,1,0:T(8,128)(2,1)S(1)}, bf16[11,64,128]{2,1,0:T(8,128)(2,1)S(1)}, u32[]{:S(2)}, u32[]{:S(2)}) collective-permute-start(bf16[11,64,128]{2,1,0:T(8,128)(2,1)S(1)} %row_sum.1.refs_0_), channel_id=1, source_target_pairs={{4,0},{0,4},{12,8},{8,12},{5,1},{1,5},{13,9},{9,13},{6,2},{2,6},{1... | collective-permute-start | bytes 540680 | tf_op jit(solution)/shard_map/ppermute | solution.py:353
  73.0 8.7 %collective-permute-start.20 = (f32[64,512]{1,0:T(8,128)S(1)}, f32[64,512]{1,0:T(8,128)S(1)}, u32[]{:S(2)}, u32[]{:S(2)}) collective-permute-start(f32[64,512]{1,0:T(8,128)S(1)} %get-tuple-element.100), channel_id=1, source_target_pairs={{0,16},{16,0},{1,17},{17,1},{2,18},{18,2},{3,19},{19,3},{4,20},{20... | collective-permute-start | bytes 393224 | tf_op jit(solution)/shard_map/ppermute | solution.py:375
  76.6 6.5 %collective-permute-start.17 = (f32[4,128]{1,0:T(4,128)S(1)}, f32[4,128]{1,0:T(4,128)S(1)}, u32[]{:S(2)}, u32[]{:S(2)}) collective-permute-start(f32[4,128]{1,0:T(4,128)S(1)} %get-tuple-element.104.refs_0_), channel_id=1, source_target_pairs={{0,1},{1,0},{2,3},{3,2},{4,5},{5,4},{6,7},{7,6},{8,9},{9,8},{10,11... | collective-permute-start | bytes 6152 | tf_op jit(solution)/shard_map/ppermute | solution.py:368
  76.7 6.5 %collective-permute-start.18 = (f32[4,128]{1,0:T(4,128)S(1)}, f32[4,128]{1,0:T(4,128)S(1)}, u32[]{:S(2)}, u32[]{:S(2)}) collective-permute-start(f32[4,128]{1,0:T(4,128)S(1)} %get-tuple-element.104.refs_0_), channel_id=1, source_target_pairs={{0,2},{1,3},{2,0},{3,1},{4,6},{5,7},{6,4},{7,5},{8,10},{9,11},{10,... | collective-permute-start | bytes 6152 | tf_op jit(solution)/shard_map/ppermute | solution.py:368
  78.9 5.4 %collective-permute-start.19 = (f32[4,128]{1,0:T(4,128)S(1)}, f32[4,128]{1,0:T(4,128)S(1)}, u32[]{:S(2)}, u32[]{:S(2)}) collective-permute-start(f32[4,128]{1,0:T(4,128)S(1)} %get-tuple-element.104.refs_0_), channel_id=1, source_target_pairs={{0,3},{1,2},{2,1},{3,0},{4,7},{5,6},{6,5},{7,4},{8,11},{9,10},{10,... | collective-permute-start | bytes 6152 | tf_op jit(solution)/shard_map/ppermute | solution.py:368

commit v20 on v19

--- a/solution.py
+++ b/solution.py
@@ -120,19 +120,14 @@
 
 
 def tap_products(g_ref, wides, totals, height, width):
-    for total in totals:
-        total[...] = jnp.zeros(total.shape, F32)
-
-    def body(row, _):
-        g = g_ref[:, pl.ds(pl.multiple_of(row * width, width), width)]
-        for wide, total in zip(wides, totals):
-            for kh in range(3):
-                x = wide[:, pl.ds(pl.multiple_of((row + kh) * width, width), width)]
-                total[kh] += lax.dot_general(g, x, (((1,), (1,)), ((), ())), preferred_element_type=F32)
-        return 0
-
-    lax.fori_loop(0, height, body, 0)
-    return [jnp.concatenate([total[kh] for kh in range(3)], axis=1).astype(BF16) for total in totals]
+    g = g_ref[...]
+    contract = (((1,), (1,)), ((), ()))
+    out = []
+    for wide in wides:
+        rows = [wide[:, kh * width : (kh + height) * width] for kh in range(3)]
+        parts = [lax.dot_general(g, x, contract, preferred_element_type=F32) for x in rows]
+        out.append(jnp.concatenate(parts, axis=1).astype(BF16))
+    return out
 
 
 def near_grad_kernel(height, width, *refs):

time: 85.7 us -> 83.2 us (0.971)
  Pallas kernels: 21.8 us -> 17.6 us
  starting transfers between devices: 43.4 us -> 44.9 us
    pallas_call x11, Pallas kernels: 21.8 us -> 17.6 us  [call(): pl.pallas_call(kernel, out_shape=outs, in_specs=sspec(scalars) + vspec(le...]
    ppermute x1, waiting for transfers between devices: 0.01 us -> 2.56 us  [on_device(): far = lax.ppermute(end_block, 'chan', [(1, 0), (size - 2, size - 1)])]
    ppermute x3, waiting for transfers between devices: 1.64 us -> 0.01 us  [exchange_pairs(): lax.ppermute(x, axis, [(partner(i, step, size), i) for i in range(size)])]
    ppermute x1, waiting for transfers between devices: 1.68 us -> 0.37 us  [on_device(): lax.ppermute(parts[r], 'rows', [(i, (i + r) % rows) for i in range(rows)])]
    ppermute x1, starting transfers between devices: 2.8 us -> 4.04 us  [on_device(): end_mod = lax.ppermute(mods[size], 'chan', [(0, size - 1), (size - 1, 0)])]
  transfers between devices with their start and end apart: 21 -> 21, of which waited for: 7 -> 7; matrix products, arithmetic and copies ran while one was open for 3% -> 3% of each run, Pallas kernels for 25% -> 20%
where the time goes in v20:
time: 83.2 us; the launch traced here: 82.7 us
  starting transfers between devices  44.9 us (54%)
  Pallas kernels  17.6 us (21%)
  waiting for transfers between devices  14.5 us (17%)
  local copies, waits for them, and re-layouts  3.49 us (4%)
  other arithmetic  1.28 us (2%)
  between operations  0.99 us (1%)
    ppermute x7, starting transfers between devices, along(): return lax.ppermute(x, ('samples', 'chan'), whole)  22.2 us
    pallas_call x11, Pallas kernels, call(): pl.pallas_call(kernel, out_shape=outs, in_specs=sspec(scalars) + vspec(le...  17.6 us
    ppermute x1, starting transfers between devices, on_device(): feat_end = lax.ppermute(feat, 'chan', [(0, 1), (size - 1, size - 2)])  5.29 us
    ppermute x1, waiting for transfers between devices, on_device(): from_end = lax.ppermute(grad_end, 'chan', [(1, size - 1), (size - 2, 0)])  4.67 us
    ppermute x3, starting transfers between devices, terms_of_sum(): lax.ppermute(x, axis, [(i, i ^ step) for i in range(size)])  4.44 us
    ppermute x1, starting transfers between devices, on_device(): end_mod = lax.ppermute(mods[size], 'chan', [(0, size - 1), (size - 1, 0)])  4.04 us
    unnamed x19, local copies, waits for them, and re-layouts  3.13 us
    ppermute x1, waiting for transfers between devices, exchange(): lax.ppermute(x, axis, [(i, (i + s) % size) for i in range(size)])  2.71 us
  transfers between devices with their start and end apart: 21, of which 7 were waited for; matrix products, arithmetic and copies ran while one was open for 3% of the time, Pallas kernels for 20%

profile of v20, /device:TPU:0, one launch (start us, length us, event | category | flops | bytes accessed | tf_op | source)
XLA Modules:
  0.0 82.7 jit_solution(4476828432490241888)
XLA Ops:
  0.6 0.0 copy-start.7
  0.6 0.0 copy-start
  0.7 1.3 %copy.13 = bf16[8,8,8,512]{3,1,2,0:T(8,128)(2,1)S(1)} copy(bf16[8,8,8,512]{3,2,1,0:T(8,128)(2,1)} %bitcast.32) | data formatting | bytes 1048576
  2.0 5.7 %collective-permute-start.1 = (bf16[64,4096]{1,0:T(8,128)(2,1)S(1)}, bf16[64,4096]{1,0:T(8,128)(2,1)}, u32[]{:S(2)}, u32[]{:S(2)}) collective-permute-start(bf16[64,4096]{1,0:T(8,128)(2,1)S(1)} %bitcast.26), channel_id=1, source_target_pairs={{0,1},{1,2},{2,3},{7,6},{6,5},{5,4},{8,9},{9,10},{10,11},{15,14},{... | collective-permute-start | bytes 1572872 | tf_op jit(solution)/shard_map/ppermute | solution.py:395
  7.8 1.3 %collective-permute-start.2 = (bf16[64,4096]{1,0:T(8,128)(2,1)S(1)}, bf16[64,4096]{1,0:T(8,128)(2,1)}, u32[]{:S(2)}, u32[]{:S(2)}) collective-permute-start(bf16[64,4096]{1,0:T(8,128)(2,1)S(1)} %bitcast.27), channel_id=1, source_target_pairs={{1,0},{2,1},{3,2},{6,7},{5,6},{4,5},{9,8},{10,9},{11,10},{14,15},{... | collective-permute-start | bytes 1572872 | tf_op jit(solution)/shard_map/ppermute | solution.py:395
  9.1 0.2 copy.14
  9.3 1.6 %collective-permute-start.5 = (bf16[64,512]{1,0:T(8,128)(2,1)S(1)}, bf16[64,512]{1,0:T(8,128)(2,1)S(1)}, u32[]{:S(2)}, u32[]{:S(2)}) collective-permute-start(bf16[64,512]{1,0:T(8,128)(2,1)S(1)} %slice_select_fusion), channel_id=1, source_target_pairs={{0,16},{16,0},{1,17},{17,1},{2,18},{18,2},{3,19},{19,3},{4,20},{20... | collective-permute-start | bytes 196616 | tf_op jit(solution)/shard_map/ppermute | solution.py:370
  10.9 1.0 %plain.1 = (f32[10,64,128]{2,1,0:T(8,128)S(1)}, f32[8,128]{1,0:T(8,128)S(1)}) custom-call(s32[1,4]{1,0:T(1,128)S(1)} %copy-done.5, f32[1,512]{1,0:T(1,128)S(1)} %copy-done.4, f32[1,128]{1,0:T(1,128)S(1)} %bitcast.30, f32[512,128]{1,0:T(8,128)S(1)} %copy-done.3, f32[4,9,64,128]{3,2,1,0:T(8,128)S(1)} %copy-done), custom_call_target="tpu_custom_call" | custom-call | flops 1000000 | bytes 1776144 | tf_op jit(solution)/shard_map/plain/pallas_call | solution.py:323
  11.8 0.0 copy-start.1
  11.8 0.6 collective-permute-start
  12.4 1.2 %collective-permute-done.5 = bf16[64,512]{1,0:T(8,128)(2,1)S(1)} collective-permute-done((bf16[64,512]{1,0:T(8,128)(2,1)S(1)}, bf16[64,512]{1,0:T(8,128)(2,1)S(1)}, u32[]{:S(2)}, u32[]{:S(2)}) %collective-permute-start.5) | collective-permute-done | bytes 65568 | tf_op jit(solution)/shard_map/ppermute | solution.py:370
  13.7 5.3 %collective-permute-start.6 = (bf16[64,5120]{1,0:T(8,128)(2,1)S(1)}, bf16[64,5120]{1,0:T(8,128)(2,1)S(1)}, u32[]{:S(2)}, u32[]{:S(2)}) collective-permute-start(bf16[64,5120]{1,0:T(8,128)(2,1)S(1)} %feat_rows.1.refs_3_), channel_id=1, source_target_pairs={{0,1},{3,2},{4,5},{7,6},{8,9},{11,10},{12,13},{15,14},{16,17},{19,... | collective-permute-start | bytes 1966088 | tf_op jit(solution)/shard_map/ppermute | solution.py:435
  19.0 2.7 %collective-permute-done.refs_1_ = f32[10,64,128]{2,1,0:T(8,128)} collective-permute-done((f32[10,64,128]{2,1,0:T(8,128)S(1)}, f32[10,64,128]{2,1,0:T(8,128)}, u32[]{:S(2)}, u32[]{:S(2)}) %collective-permute-start) | collective-permute-done | bytes 327712 | tf_op jit(solution)/shard_map/ppermute | solution.py:355
  21.7 0.0 collective-permute-done.1.refs_1_.first
  21.7 0.0 collective-permute-done.2.refs_2_.second
  21.7 0.7 collective-permute-start.3
  22.4 1.3 %collective-permute-start.4 = (bf16[64,4096]{1,0:T(8,128)(2,1)}, bf16[64,4096]{1,0:T(8,128)(2,1)}, u32[]{:S(2)}, u32[]{:S(2)}) collective-permute-start(bf16[64,4096]{1,0:T(8,128)(2,1)} %collective-permute-done.2.refs_2_.second), channel_id=1, source_target_pairs={{1,0},{2,1},{6,7},{5,6},{9,8},{10,9},{14,15},{13,14},{17,16},{18,1... | collective-permute-start | bytes 1572872 | tf_op jit(solution)/shard_map/ppermute | solution.py:395
  23.7 0.1 pad_add_fusion.place
  23.8 1.0 %copy-done.2 = f32[10,64,128]{2,1,0:T(8,128)S(1)} copy-done((f32[10,64,128]{2,1,0:T(8,128)S(1)}, f32[10,64,128]{2,1,0:T(8,128)}, u32[]{:S(2)}) %copy-start.2) | copy-done | bytes 327704
  24.8 1.3 %mod_blocks.1 = (bf16[9,64,256]{2,1,0:T(8,128)(2,1)S(1)}, f32[64,128]{1,0:T(8,128)S(1)}, bf16[64,576]{1,0:T(8,128)(2,1)S(1)}, bf16[64,576]{1,0:T(8,128)(2,1)S(1)...) custom-call(s32[4]{0:T(128)S(1)} %pad_add_fusion.place, ...), custom_call_target="tpu_custom_call" | custom-call | flops 1000000 | bytes 1351696 | tf_op jit(solution)/shard_map/mod_blocks/pallas_call | solution.py:323
  26.0 2.8 %near_grad.1 = (bf16[64,576]{1,0:T(8,128)(2,1)S(1)}, bf16[128,576]{1,0:T(8,128)(2,1)S(1)}, bf16[128,576]{1,0:T(8,128)(2,1)S(1)}, bf16[192,5120]{1,0:T(8,128)(2,1)S(1)}) custom-call(bf16[64,4096]{1,0:T(8,128)(2,1)S(1)} %bitcast.28, bf16[64,4096]{1,0:T(8,128)(2,1)} %collective-permute-done.1.refs_1_.first, ...), custom_call_target="tpu_custom_call" | custom-call | flops 905969664 | bytes 4710400 | tf_op jit(solution)/shard_map/near_grad/pallas_call | solution.py:323
  28.8 1.3 %collective-permute-start.7 = (bf16[128,576]{1,0:T(8,128)(2,1)S(1)}, bf16[128,576]{1,0:T(8,128)(2,1)S(1)}, u32[]{:S(2)}, u32[]{:S(2)}) collective-permute-start(bf16[128,576]{1,0:T(8,128)(2,1)S(1)} %get-tuple-element.71), channel_id=1, source_target_pairs={{1,0},{2,1},{3,2},{6,7},{5,6},{4,5},{9,8},{10,9},{11,10},{14,15},{... | collective-permute-start | bytes 442376 | tf_op jit(solution)/shard_map/ppermute | solution.py:395
  30.1 7.6 %collective-permute-start.8 = (bf16[128,576]{1,0:T(8,128)(2,1)S(1)}, bf16[128,576]{1,0:T(8,128)(2,1)S(1)}, u32[]{:S(2)}, u32[]{:S(2)}) collective-permute-start(bf16[128,576]{1,0:T(8,128)(2,1)S(1)} %get-tuple-element.72), channel_id=1, source_target_pairs={{0,1},{1,2},{2,3},{7,6},{6,5},{5,4},{8,9},{9,10},{10,11},{15,14},{... | collective-permute-start | bytes 442376 | tf_op jit(solution)/shard_map/ppermute | solution.py:395
  37.7 0.0 collective-permute-done.6.feat
  37.7 0.0 collective-permute-done.3.refs_0_
  37.7 0.0 collective-permute-done.4.refs_1_
  37.7 2.8 %middle_grad.1 = (bf16[128,576]{1,0:T(8,128)(2,1)S(1)}, bf16[64,4096]{1,0:T(8,128)(2,1)S(1)}, bf16[64,4096]{1,0:T(8,128)(2,1)S(1)}) custom-call(bf16[64,4096]{1,0:T(8,128)(2,1)S(1)} %collective-permute-done.3.refs_0_, bf16[64,4096]{1,0:T(8,128)(2,1)} %collective-permute-done.4.refs_1_, bf16[192,5120]{1,0:T(8,128)(2,1)S(1)} %get-tuple-element.75.refs_2_, ...), custom_call_target="tpu_custom_call" | custom-call | flops 301989888 | bytes 4284416 | tf_op jit(solution)/shard_map/middle_grad/pallas_call | solution.py:323
  40.5 4.3 %collective-permute-start.9 = (bf16[128,576]{1,0:T(8,128)(2,1)S(1)}, bf16[128,576]{1,0:T(8,128)(2,1)S(1)}, u32[]{:S(2)}, u32[]{:S(2)}) collective-permute-start(bf16[128,576]{1,0:T(8,128)(2,1)S(1)} %get-tuple-element.77), channel_id=1, source_target_pairs={{0,2},{1,3},{2,0},{3,1},{7,5},{6,4},{5,7},{4,6},{8,10},{9,11},{10,... | collective-permute-start | bytes 442376 | tf_op jit(solution)/shard_map/ppermute | solution.py:395
  44.8 1.5 %end_grad.1 = bf16[64,576]{1,0:T(8,128)(2,1)S(1)} custom-call(bf16[64,4096]{1,0:T(8,128)(2,1)S(1)} %get-tuple-element.88.end_block, bf16[64,5120]{1,0:T(8,128)(2,1)S(1)} %collective-permute-done.6.feat), custom_call_target="tpu_custom_call" | custom-call | flops 301989888 | bytes 1253376 | tf_op jit(solution)/shard_map/end_grad/pallas_call | solution.py:323
  46.3 1.3 %collective-permute-start.10 = (bf16[64,576]{1,0:T(8,128)(2,1)S(1)}, bf16[64,576]{1,0:T(8,128)(2,1)S(1)}, u32[]{:S(2)}, u32[]{:S(2)}) collective-permute-start(bf16[64,576]{1,0:T(8,128)(2,1)S(1)} %end_grad.1), channel_id=1, source_target_pairs={{1,3},{2,0},{5,7},{6,4},{9,11},{10,8},{13,15},{14,12},{17,19},{18,... | collective-permute-start | bytes 221192 | tf_op jit(solution)/shard_map/ppermute | solution.py:491
  47.6 1.3 %collective-permute-start.16 = (bf16[64,4096]{1,0:T(8,128)(2,1)S(1)}, bf16[64,4096]{1,0:T(8,128)(2,1)S(1)}, u32[]{:S(2)}, u32[]{:S(2)}) collective-permute-start(bf16[64,4096]{1,0:T(8,128)(2,1)S(1)} %get-tuple-element.88.end_block), channel_id=1, source_target_pairs={{1,0},{2,3},{5,4},{6,7},{9,8},{10,11},{13,12},{14,15},{17,16},{18,... | collective-permute-start | bytes 1572872 | tf_op jit(solution)/shard_map/ppermute | solution.py:493
  48.9 0.0 collective-permute-done.7.ahead
  48.9 0.0 collective-permute-done.8.behind
  49.0 4.7 %collective-permute-done.10.end = bf16[64,576]{1,0:T(8,128)(2,1)S(1)} collective-permute-done((bf16[64,576]{1,0:T(8,128)(2,1)S(1)}, bf16[64,576]{1,0:T(8,128)(2,1)S(1)}, u32[]{:S(2)}, u32[]{:S(2)}) %collective-permute-start.10) | collective-permute-done | bytes 73760 | tf_op jit(solution)/shard_map/ppermute | solution.py:491
  53.6 0.0 collective-permute-done.9.others
  53.6 1.1 %collect.1 = (bf16[10,64,128]{2,1,0:T(8,128)(2,1)S(1)}, bf16[10,64,128]{2,1,0:T(8,128)(2,1)S(1)}) custom-call(s32[4]{0:T(128)S(1)} %pad_add_fusion.place, f32[64,128]{1,0:T(8,128)S(1)} %get-tuple-element.58.scale, bf16[9,64,256]{2,1,0:T(8,128)(2,1)S(1)} %get-tuple-element.69.whole_mod, bf16[64,576]{1,0:T(8,128)(2,1)S(1)} %get-tuple-element.70.own, ...), custom_call_target="tpu_custom_call" | custom-call | flops 6000000000 | bytes 1245200 | tf_op jit(solution)/shard_map/collect/pallas_call | solution.py:323
  54.7 1.0 %collective-permute-start.11 = (bf16[10,64,128]{2,1,0:T(8,128)(2,1)S(1)}, bf16[10,64,128]{2,1,0:T(8,128)(2,1)S(1)}, u32[]{:S(2)}, u32[]{:S(2)}) collective-permute-start(bf16[10,64,128]{2,1,0:T(8,128)(2,1)S(1)} %get-tuple-element.85), channel_id=1, source_target_pairs={{0,16},{16,0},{1,17},{17,1},{2,18},{18,2},{3,19},{19,3},{4,20},{20... | collective-permute-start | bytes 491528 | tf_op jit(solution)/shard_map/ppermute | solution.py:513
  55.7 4.0 %collective-permute-start.15 = (bf16[64,576]{1,0:T(8,128)(2,1)S(1)}, bf16[64,576]{1,0:T(8,128)(2,1)S(1)}, u32[]{:S(2)}, u32[]{:S(2)}) collective-permute-start(bf16[64,576]{1,0:T(8,128)(2,1)S(1)} %get-tuple-element.87), channel_id=1, source_target_pairs={{0,3},{3,0},{4,7},{7,4},{8,11},{11,8},{12,15},{15,12},{16,19},{19,... | collective-permute-start | bytes 221192 | tf_op jit(solution)/shard_map/ppermute | solution.py:511
  59.7 0.4 collective-permute-done.11.refs_1_
  60.1 0.2 row_sum.1.refs_0_
  60.3 1.6 %collective-permute-start.12 = (bf16[11,64,128]{2,1,0:T(8,128)(2,1)S(1)}, bf16[11,64,128]{2,1,0:T(8,128)(2,1)S(1)}, u32[]{:S(2)}, u32[]{:S(2)}) collective-permute-start(bf16[11,64,128]{2,1,0:T(8,128)(2,1)S(1)} %row_sum.1.refs_0_), channel_id=1, source_target_pairs={{8,0},{12,4},{0,8},{4,12},{9,1},{13,5},{1,9},{5,13},{10,2},{14,6},... | collective-permute-start | bytes 540680 | tf_op jit(solution)/shard_map/ppermute | solution.py:348
  61.9 0.0 collective-permute-start.13
  61.9 0.6 collective-permute-start.14
  62.5 1.4 %collective-permute-done.15.end_mod = bf16[64,576]{1,0:T(8,128)(2,1)S(1)} collective-permute-done((bf16[64,576]{1,0:T(8,128)(2,1)S(1)}, bf16[64,576]{1,0:T(8,128)(2,1)S(1)}, u32[]{:S(2)}, u32[]{:S(2)}) %collective-permute-start.15) | collective-permute-done | bytes 73760 | tf_op jit(solution)/shard_map/ppermute | solution.py:511
  63.9 2.6 %collective-permute-done.16.far = bf16[64,4096]{1,0:T(8,128)(2,1)S(1)} collective-permute-done((bf16[64,4096]{1,0:T(8,128)(2,1)S(1)}, bf16[64,4096]{1,0:T(8,128)(2,1)S(1)}, u32[]{:S(2)}, u32[]{:S(2)}) %collective-permute-start.16) | collective-permute-done | bytes 524320 | tf_op jit(solution)/shard_map/ppermute | solution.py:493
  66.4 3.4 %input_grad.1 = (f32[64,4096]{1,0:T(8,128)S(1)}, f32[64,512]{1,0:T(8,128)}, f32[64,512]{1,0:T(8,128)S(1)}) custom-call(s32[4]{0:T(128)S(1)} %pad_add_fusion.place, bf16[64,4096]{1,0:T(8,128)(2,1)S(1)} %bitcast.29, bf16[64,4096]{1,0:T(8,128)(2,1)} %collective-permute-done.1.refs_1_.first, bf16[64,4096]{1,0:T(8,128)(2,1)} %collective-permute-done.2.refs_2_.second, ...), custom_call_target="tpu_custom_call" | custom-call | flops 2000000000 | bytes 4522000 | tf_op jit(solution)/shard_map/input_grad/pallas_call | solution.py:323
  69.8 0.0 collective-permute-done.12.refs_1_
  69.8 0.0 collective-permute-done.13.refs_2_
  69.8 0.0 collective-permute-done.14.refs_3_
  69.8 1.0 %collective-permute-start.20 = (f32[64,512]{1,0:T(8,128)S(1)}, f32[64,512]{1,0:T(8,128)S(1)}, u32[]{:S(2)}, u32[]{:S(2)}) collective-permute-start(f32[64,512]{1,0:T(8,128)S(1)} %get-tuple-element.100), channel_id=1, source_target_pairs={{0,16},{16,0},{1,17},{17,1},{2,18},{18,2},{3,19},{19,3},{4,20},{20... | collective-permute-start | bytes 393224 | tf_op jit(solution)/shard_map/ppermute | solution.py:370
  70.9 0.1 pad.1.clone
  70.9 2.7 %bank_grad.1 = (f32[4,9,64,128]{3,2,1,0:T(8,128)}, f32[4,128]{1,0:T(4,128)S(1)}, f32[4,512]{1,0:T(4,128)S(1)}) custom-call(s32[4]{0:T(128)S(1)} %pad_add_fusion.place, f32[4,9,64,128]{3,2,1,0:T(8,128)S(1)} %copy-done, bf16[11,64,128]{2,1,0:T(8,128)(2,1)S(1)} %row_sum.1.refs_0_, bf16[11,64,128]{2,1,0:T(8,128)(2,1)S(1)} %collective-permute-done.12.refs_1_, ...), custom_call_target="tpu_custom_call" | custom-call | flops 1000000 | bytes 3090448 | tf_op jit(solution)/shard_map/bank_grad/pallas_call | solution.py:323
  73.6 0.1 collective-permute-start.17
  73.7 2.7 %collective-permute-start.18 = (f32[4,128]{1,0:T(4,128)S(1)}, f32[4,128]{1,0:T(4,128)S(1)}, u32[]{:S(2)}, u32[]{:S(2)}) collective-permute-start(f32[4,128]{1,0:T(4,128)S(1)} %get-tuple-element.104.refs_0_), channel_id=1, source_target_pairs={{0,2},{1,3},{2,0},{3,1},{4,6},{5,7},{6,4},{7,5},{8,10},{9,11},{10,... | collective-permute-start | bytes 6152 | tf_op jit(solution)/shard_map/ppermute | solution.py:363
  76.4 1.7 %collective-permute-start.19 = (f32[4,128]{1,0:T(4,128)S(1)}, f32[4,128]{1,0:T(4,128)S(1)}, u32[]{:S(2)}, u32[]{:S(2)}) collective-permute-start(f32[4,128]{1,0:T(4,128)S(1)} %get-tuple-element.104.refs_0_), channel_id=1, source_target_pairs={{0,3},{1,2},{2,1},{3,0},{4,7},{5,6},{6,5},{7,4},{8,11},{9,10},{10,... | collective-permute-start | bytes 6152 | tf_op jit(solution)/shard_map/ppermute | solution.py:363
  78.1 0.6 copy.15
  78.7 0.0 collective-permute-done.20
  78.8 0.1 copy.12
  78.9 0.1 copy.11
  79.0 1.2 %fusion = bf16[1,64,8,512]{3,2,1,0:T(8,128)(2,1)} fusion(f32[1,64,1,512]{3,2,1,0:T(1,128)S(1)} %copy.12, f32[1,64,1,512]{3,2,1,0:T(1,128)S(1)} %copy.11, f32[8]{0:T(128)S(1)} %pad.1.clone, f32[1,64,8,512]{3,2,1,0:T(8,128)S(1)} %bitcast.31), kind=kLoop, calls=%fused_computation.1 | loop fusion | flops 1048576 | bytes 1835040 | tf_op jit(solution)/shard_map/convert_element_type | solution.py:560
  80.2 0.0 collective-permute-done.17.refs_1_
  80.2 0.0 collective-permute-done.18.refs_2_
  80.2 1.6 %collective-permute-done.19.refs_3_ = f32[4,128]{1,0:T(4,128)S(1)} collective-permute-done((f32[4,128]{1,0:T(4,128)S(1)}, f32[4,128]{1,0:T(4,128)S(1)}, u32[]{:S(2)}, u32[]{:S(2)}) %collective-permute-start.19) | collective-permute-done | bytes 2080 | tf_op jit(solution)/shard_map/ppermute | solution.py:363
  81.8 0.9 %affine.1 = (f32[512,128]{1,0:T(8,128)}, f32[1,128]{1,0:T(1,128)}) custom-call(f32[4,512]{1,0:T(4,128)S(1)} %get-tuple-element.103.latents, f32[4,128]{1,0:T(4,128)S(1)} %get-tuple-element.104.refs_0_, f32[4,128]{1,0:T(4,128)S(1)} %collective-permute-done.17.refs_1_, f32[4,128]{1,0:T(4,128)S(1)} %collective-permute-done.18.refs_2_, ...), custom_call_target="tpu_custom_call" | custom-call | flops 1000000 | bytes 279040 | tf_op jit(solution)/shard_map/affine/pallas_call | solution.py:323
  (17 shorter events, 0.1 us)
Async XLA Ops:
  0.6 8.4 %copy-start.7 = (bf16[1,64,8,512]{3,2,1,0:T(8,128)(2,1)S(1)}, bf16[1,64,8,512]{3,2,1,0:T(8,128)(2,1)}, u32[]{:S(2)}) copy-start(bf16[1,64,8,512]{3,2,1,0:T(8,128)(2,1)} %param.7) | copy-start | bytes 1572868
  0.6 10.2 %copy-start = (f32[4,9,64,128]{3,2,1,0:T(8,128)S(1)}, f32[4,9,64,128]{3,2,1,0:T(8,128)}, u32[]{:S(2)}) copy-start(f32[4,9,64,128]{3,2,1,0:T(8,128)} %bank.1) | copy-start | bytes 3538948
  0.7 10.2 %copy-start.5 = (s32[1,4]{1,0:T(1,128)S(1)}, s32[1,4]{1,0:T(1,128)}, u32[]{:S(2)}) copy-start(s32[1,4]{1,0:T(1,128)} %refs_0_.1) | copy-start | bytes 52
  0.7 10.2 %copy-start.4 = (f32[1,512]{1,0:T(1,128)S(1)}, f32[1,512]{1,0:T(1,128)}, u32[]{:S(2)}) copy-start(f32[1,512]{1,0:T(1,128)} %refs_1_.1) | copy-start | bytes 6148
  0.7 10.2 %copy-start.6 = (f32[128]{0:T(128)S(1)}, f32[128]{0:T(128)}, u32[]{:S(2)}) copy-start(f32[128]{0:T(128)} %param.13) | copy-start | bytes 1540
  0.7 10.2 %copy-start.3 = (f32[512,128]{1,0:T(8,128)S(1)}, f32[512,128]{1,0:T(8,128)}, u32[]{:S(2)}) copy-start(f32[512,128]{1,0:T(8,128)} %refs_3_.1) | copy-start | bytes 786436
  2.0 19.7 %collective-permute-start.1 = (bf16[64,4096]{1,0:T(8,128)(2,1)S(1)}, bf16[64,4096]{1,0:T(8,128)(2,1)}, u32[]{:S(2)}, u32[]{:S(2)}) collective-permute-start(bf16[64,4096]{1,0:T(8,128)(2,1)S(1)} %bitcast.26), channel_id=1, source_target_pairs={{0,1},{1,2},{2,3},{7,6},{6,5},{5,4},{8,9},{9,10},{10,11},{15,14},{... | collective-permute-start | bytes 1572872 | tf_op jit(solution)/shard_map/ppermute | solution.py:395
  7.8 13.9 %collective-permute-start.2 = (bf16[64,4096]{1,0:T(8,128)(2,1)S(1)}, bf16[64,4096]{1,0:T(8,128)(2,1)}, u32[]{:S(2)}, u32[]{:S(2)}) collective-permute-start(bf16[64,4096]{1,0:T(8,128)(2,1)S(1)} %bitcast.27), channel_id=1, source_target_pairs={{1,0},{2,1},{3,2},{6,7},{5,6},{4,5},{9,8},{10,9},{11,10},{14,15},{... | collective-permute-start | bytes 1572872 | tf_op jit(solution)/shard_map/ppermute | solution.py:395
  9.3 4.3 %collective-permute-start.5 = (bf16[64,512]{1,0:T(8,128)(2,1)S(1)}, bf16[64,512]{1,0:T(8,128)(2,1)S(1)}, u32[]{:S(2)}, u32[]{:S(2)}) collective-permute-start(bf16[64,512]{1,0:T(8,128)(2,1)S(1)} %slice_select_fusion), channel_id=1, source_target_pairs={{0,16},{16,0},{1,17},{17,1},{2,18},{18,2},{3,19},{19,3},{4,20},{20... | collective-permute-start | bytes 196616 | tf_op jit(solution)/shard_map/ppermute | solution.py:370
  11.8 9.9 %copy-start.1 = (f32[10,64,128]{2,1,0:T(8,128)}, f32[10,64,128]{2,1,0:T(8,128)S(1)}, u32[]{:S(2)}) copy-start(f32[10,64,128]{2,1,0:T(8,128)S(1)} %get-tuple-element.57.refs_0_) | copy-start | bytes 983044
  11.8 9.8 %collective-permute-start = (f32[10,64,128]{2,1,0:T(8,128)S(1)}, f32[10,64,128]{2,1,0:T(8,128)}, u32[]{:S(2)}, u32[]{:S(2)}) collective-permute-start(f32[10,64,128]{2,1,0:T(8,128)S(1)} %get-tuple-element.57.refs_0_), channel_id=1, source_target_pairs={{0,16},{16,0},{1,17},{17,1},{2,18},{18,2},{3,19},{19,3},{4,20},{20... | collective-permute-start | bytes 983048 | tf_op jit(solution)/shard_map/ppermute | solution.py:355
  13.7 24.0 %collective-permute-start.6 = (bf16[64,5120]{1,0:T(8,128)(2,1)S(1)}, bf16[64,5120]{1,0:T(8,128)(2,1)S(1)}, u32[]{:S(2)}, u32[]{:S(2)}) collective-permute-start(bf16[64,5120]{1,0:T(8,128)(2,1)S(1)} %feat_rows.1.refs_3_), channel_id=1, source_target_pairs={{0,1},{3,2},{4,5},{7,6},{8,9},{11,10},{12,13},{15,14},{16,17},{19,... | collective-permute-start | bytes 1966088 | tf_op jit(solution)/shard_map/ppermute | solution.py:435
  21.7 16.0 %collective-permute-start.3 = (bf16[64,4096]{1,0:T(8,128)(2,1)}, bf16[64,4096]{1,0:T(8,128)(2,1)S(1)}, u32[]{:S(2)}, u32[]{:S(2)}) collective-permute-start(bf16[64,4096]{1,0:T(8,128)(2,1)} %collective-permute-done.1.refs_1_.first), channel_id=1, source_target_pairs={{1,2},{2,3},{6,5},{5,4},{9,10},{10,11},{14,13},{13,12},{17,18},{18... | collective-permute-start | bytes 1572872 | tf_op jit(solution)/shard_map/ppermute | solution.py:395
  22.4 15.3 %collective-permute-start.4 = (bf16[64,4096]{1,0:T(8,128)(2,1)}, bf16[64,4096]{1,0:T(8,128)(2,1)}, u32[]{:S(2)}, u32[]{:S(2)}) collective-permute-start(bf16[64,4096]{1,0:T(8,128)(2,1)} %collective-permute-done.2.refs_2_.second), channel_id=1, source_target_pairs={{1,0},{2,1},{6,7},{5,6},{9,8},{10,9},{14,15},{13,14},{17,16},{18,1... | collective-permute-start | bytes 1572872 | tf_op jit(solution)/shard_map/ppermute | solution.py:395
  23.8 1.0 %copy-start.2 = (f32[10,64,128]{2,1,0:T(8,128)S(1)}, f32[10,64,128]{2,1,0:T(8,128)}, u32[]{:S(2)}) copy-start(f32[10,64,128]{2,1,0:T(8,128)} %copy-done.1) | copy-start | bytes 983044
  28.8 20.1 %collective-permute-start.7 = (bf16[128,576]{1,0:T(8,128)(2,1)S(1)}, bf16[128,576]{1,0:T(8,128)(2,1)S(1)}, u32[]{:S(2)}, u32[]{:S(2)}) collective-permute-start(bf16[128,576]{1,0:T(8,128)(2,1)S(1)} %get-tuple-element.71), channel_id=1, source_target_pairs={{1,0},{2,1},{3,2},{6,7},{5,6},{4,5},{9,8},{10,9},{11,10},{14,15},{... | collective-permute-start | bytes 442376 | tf_op jit(solution)/shard_map/ppermute | solution.py:395
  30.1 18.8 %collective-permute-start.8 = (bf16[128,576]{1,0:T(8,128)(2,1)S(1)}, bf16[128,576]{1,0:T(8,128)(2,1)S(1)}, u32[]{:S(2)}, u32[]{:S(2)}) collective-permute-start(bf16[128,576]{1,0:T(8,128)(2,1)S(1)} %get-tuple-element.72), channel_id=1, source_target_pairs={{0,1},{1,2},{2,3},{7,6},{6,5},{5,4},{8,9},{9,10},{10,11},{15,14},{... | collective-permute-start | bytes 442376 | tf_op jit(solution)/shard_map/ppermute | solution.py:395
  40.5 13.1 %collective-permute-start.9 = (bf16[128,576]{1,0:T(8,128)(2,1)S(1)}, bf16[128,576]{1,0:T(8,128)(2,1)S(1)}, u32[]{:S(2)}, u32[]{:S(2)}) collective-permute-start(bf16[128,576]{1,0:T(8,128)(2,1)S(1)} %get-tuple-element.77), channel_id=1, source_target_pairs={{0,2},{1,3},{2,0},{3,1},{7,5},{6,4},{5,7},{4,6},{8,10},{9,11},{10,... | collective-permute-start | bytes 442376 | tf_op jit(solution)/shard_map/ppermute | solution.py:395
  46.3 7.3 %collective-permute-start.10 = (bf16[64,576]{1,0:T(8,128)(2,1)S(1)}, bf16[64,576]{1,0:T(8,128)(2,1)S(1)}, u32[]{:S(2)}, u32[]{:S(2)}) collective-permute-start(bf16[64,576]{1,0:T(8,128)(2,1)S(1)} %end_grad.1), channel_id=1, source_target_pairs={{1,3},{2,0},{5,7},{6,4},{9,11},{10,8},{13,15},{14,12},{17,19},{18,... | collective-permute-start | bytes 221192 | tf_op jit(solution)/shard_map/ppermute | solution.py:491
  47.6 18.8 %collective-permute-start.16 = (bf16[64,4096]{1,0:T(8,128)(2,1)S(1)}, bf16[64,4096]{1,0:T(8,128)(2,1)S(1)}, u32[]{:S(2)}, u32[]{:S(2)}) collective-permute-start(bf16[64,4096]{1,0:T(8,128)(2,1)S(1)} %get-tuple-element.88.end_block), channel_id=1, source_target_pairs={{1,0},{2,3},{5,4},{6,7},{9,8},{10,11},{13,12},{14,15},{17,16},{18,... | collective-permute-start | bytes 1572872 | tf_op jit(solution)/shard_map/ppermute | solution.py:493
  54.7 5.4 %collective-permute-start.11 = (bf16[10,64,128]{2,1,0:T(8,128)(2,1)S(1)}, bf16[10,64,128]{2,1,0:T(8,128)(2,1)S(1)}, u32[]{:S(2)}, u32[]{:S(2)}) collective-permute-start(bf16[10,64,128]{2,1,0:T(8,128)(2,1)S(1)} %get-tuple-element.85), channel_id=1, source_target_pairs={{0,16},{16,0},{1,17},{17,1},{2,18},{18,2},{3,19},{19,3},{4,20},{20... | collective-permute-start | bytes 491528 | tf_op jit(solution)/shard_map/ppermute | solution.py:513
  55.7 8.2 %collective-permute-start.15 = (bf16[64,576]{1,0:T(8,128)(2,1)S(1)}, bf16[64,576]{1,0:T(8,128)(2,1)S(1)}, u32[]{:S(2)}, u32[]{:S(2)}) collective-permute-start(bf16[64,576]{1,0:T(8,128)(2,1)S(1)} %get-tuple-element.87), channel_id=1, source_target_pairs={{0,3},{3,0},{4,7},{7,4},{8,11},{11,8},{12,15},{15,12},{16,19},{19,... | collective-permute-start | bytes 221192 | tf_op jit(solution)/shard_map/ppermute | solution.py:511
  60.3 9.5 %collective-permute-start.12 = (bf16[11,64,128]{2,1,0:T(8,128)(2,1)S(1)}, bf16[11,64,128]{2,1,0:T(8,128)(2,1)S(1)}, u32[]{:S(2)}, u32[]{:S(2)}) collective-permute-start(bf16[11,64,128]{2,1,0:T(8,128)(2,1)S(1)} %row_sum.1.refs_0_), channel_id=1, source_target_pairs={{8,0},{12,4},{0,8},{4,12},{9,1},{13,5},{1,9},{5,13},{10,2},{14,6},... | collective-permute-start | bytes 540680 | tf_op jit(solution)/shard_map/ppermute | solution.py:348
  61.9 7.9 %collective-permute-start.13 = (bf16[11,64,128]{2,1,0:T(8,128)(2,1)S(1)}, bf16[11,64,128]{2,1,0:T(8,128)(2,1)S(1)}, u32[]{:S(2)}, u32[]{:S(2)}) collective-permute-start(bf16[11,64,128]{2,1,0:T(8,128)(2,1)S(1)} %row_sum.1.refs_0_), channel_id=1, source_target_pairs={{12,0},{8,4},{4,8},{0,12},{13,1},{9,5},{5,9},{1,13},{14,2},{10,6},... | collective-permute-start | bytes 540680 | tf_op jit(solution)/shard_map/ppermute | solution.py:348
  61.9 7.9 %collective-permute-start.14 = (bf16[11,64,128]{2,1,0:T(8,128)(2,1)S(1)}, bf16[11,64,128]{2,1,0:T(8,128)(2,1)S(1)}, u32[]{:S(2)}, u32[]{:S(2)}) collective-permute-start(bf16[11,64,128]{2,1,0:T(8,128)(2,1)S(1)} %row_sum.1.refs_0_), channel_id=1, source_target_pairs={{4,0},{0,4},{12,8},{8,12},{5,1},{1,5},{13,9},{9,13},{6,2},{2,6},{1... | collective-permute-start | bytes 540680 | tf_op jit(solution)/shard_map/ppermute | solution.py:348
  69.8 8.9 %collective-permute-start.20 = (f32[64,512]{1,0:T(8,128)S(1)}, f32[64,512]{1,0:T(8,128)S(1)}, u32[]{:S(2)}, u32[]{:S(2)}) collective-permute-start(f32[64,512]{1,0:T(8,128)S(1)} %get-tuple-element.100), channel_id=1, source_target_pairs={{0,16},{16,0},{1,17},{17,1},{2,18},{18,2},{3,19},{19,3},{4,20},{20... | collective-permute-start | bytes 393224 | tf_op jit(solution)/shard_map/ppermute | solution.py:370
  73.6 6.5 %collective-permute-start.17 = (f32[4,128]{1,0:T(4,128)S(1)}, f32[4,128]{1,0:T(4,128)S(1)}, u32[]{:S(2)}, u32[]{:S(2)}) collective-permute-start(f32[4,128]{1,0:T(4,128)S(1)} %get-tuple-element.104.refs_0_), channel_id=1, source_target_pairs={{0,1},{1,0},{2,3},{3,2},{4,5},{5,4},{6,7},{7,6},{8,9},{9,8},{10,11... | collective-permute-start | bytes 6152 | tf_op jit(solution)/shard_map/ppermute | solution.py:363
  73.7 6.5 %collective-permute-start.18 = (f32[4,128]{1,0:T(4,128)S(1)}, f32[4,128]{1,0:T(4,128)S(1)}, u32[]{:S(2)}, u32[]{:S(2)}) collective-permute-start(f32[4,128]{1,0:T(4,128)S(1)} %get-tuple-element.104.refs_0_), channel_id=1, source_target_pairs={{0,2},{1,3},{2,0},{3,1},{4,6},{5,7},{6,4},{7,5},{8,10},{9,11},{10,... | collective-permute-start | bytes 6152 | tf_op jit(solution)/shard_map/ppermute | solution.py:363
  76.4 5.4 %collective-permute-start.19 = (f32[4,128]{1,0:T(4,128)S(1)}, f32[4,128]{1,0:T(4,128)S(1)}, u32[]{:S(2)}, u32[]{:S(2)}) collective-permute-start(f32[4,128]{1,0:T(4,128)S(1)} %get-tuple-element.104.refs_0_), channel_id=1, source_target_pairs={{0,3},{1,2},{2,1},{3,0},{4,7},{5,6},{6,5},{7,4},{8,11},{9,10},{10,... | collective-permute-start | bytes 6152 | tf_op jit(solution)/shard_map/ppermute | solution.py:363
